TPU v7x, 32 devices: a whole 2x2x4 slice. The times are simulated.
32 devices in a mesh: dp: 2 (over x), ctx: 16 (over z, y, core).
Axes of the slice: x: 2, y: 2, z: 4, core: 2. Of those that a mesh axis runs over, the one named last changes fastest.
Arguments:
- positions: int32 [2, 2048], P('dp', 'ctx'), may hold values from 0 to 2047, as said below
- queries: bfloat16 [2, 2048, 2, 576], P('dp', 'ctx'), may hold values from -12 to 12
- latent: bfloat16 [2, 2048, 576], P('dp', 'ctx'), may hold values from -6 to 6
- out_grad: bfloat16 [2, 2048, 2, 128], P('dp', 'ctx'), may hold values from -6 to 6
- attn_out: bfloat16 [2, 2048, 2, 512], P('dp', 'ctx'), may hold values from -2 to 2
- wuv: bfloat16 [2, 512, 128], replicated, may hold values from -0.25 to 0.25
Outputs:
- grad_queries: bfloat16 [2, 2048, 2, 576], P('dp', 'ctx')
- grad_latent: bfloat16 [2, 2048, 576], P('dp', 'ctx')
- grad_wuv: float32 [2, 512, 128], replicated
Inputs may be any that keep to these rules, and one draw needn't show every extreme that they name: Each sequence's rows hold every position 0 to 2047 once. The rows of one index of ctx are 16 blocks of 8 consecutive positions in rising order; block s lies in positions s * 128 to (s + 1) * 128 - 1.
All inputs are finite; a program needn't handle non-finite values.
Results may differ from a plain program's by a relative error of at most 0.0085.
Values may be sent and summed in bfloat16 or wider, within the bound.
No kernel may reach another device: no remote copies, remote signals or barrier semaphores. Data moves between devices by JAX's collectives and lax.ppermute only.
A program may use at most 256 MiB of HBM per device.

v0:
```python
import math

import jax
import jax.numpy as jnp
from jax import lax
from jax.sharding import PartitionSpec as P

ROPE = 64
HEAD_DIM = 128
STRIPES = 16


def masked_scores(query_rows, key_rows, key_pos, query_pos, factor):
    scores = factor * jnp.dot(query_rows, key_rows.T, preferred_element_type=jnp.float32)
    return jnp.where(key_pos[None, :] <= query_pos[:, None], scores, -1e30)


def body(positions, queries, latent, out_grad, attn_out, wuv):
    tok_count = queries.shape[1]
    heads = queries.shape[2]
    width = queries.shape[3]
    lat_width = attn_out.shape[3]
    parts = lax.axis_size("ctx")
    stretch = tok_count // STRIPES
    rows = stretch * heads
    span = parts * stretch
    factor = (HEAD_DIM + ROPE) ** (-0.5)
    grad_context = jnp.einsum(
        "thd,hld->thl", out_grad[0], wuv, preferred_element_type=jnp.float32
    ).astype(jnp.bfloat16)
    delta = jnp.sum(grad_context.astype(jnp.float32) * attn_out[0].astype(jnp.float32), axis=-1)
    q_rows = queries[0].reshape(STRIPES, rows, width)
    g_rows = grad_context.reshape(STRIPES, rows, lat_width)
    d_rows = delta.reshape(STRIPES, rows)
    p_rows = jnp.repeat(positions[0].reshape(STRIPES, stretch), heads, axis=1)
    own = (latent[0].reshape(STRIPES, stretch, width), positions[0].reshape(STRIPES, stretch))
    keys, key_pos = (
        lax.all_gather(own[0], "ctx", axis=1, tiled=True),
        lax.all_gather(own[1], "ctx", axis=1, tiled=True),
    )
    lse_list = []
    for stripe in range(STRIPES):
        scores = masked_scores(
            q_rows[stripe],
            keys[: stripe + 1].reshape(-1, width),
            key_pos[: stripe + 1].reshape(-1),
            p_rows[stripe],
            factor,
        )
        top = jnp.max(scores, axis=1)
        lse_list.append(top + jnp.log(jnp.sum(jnp.exp(scores - top[:, None]), axis=1)))
    lse_rows = jnp.stack(lse_list)
    score_blocks = []
    prob_blocks = []
    grads = []
    for stripe in range(STRIPES):
        key_rows = keys[: stripe + 1].reshape(-1, width)
        scores = masked_scores(
            q_rows[stripe], key_rows, key_pos[: stripe + 1].reshape(-1), p_rows[stripe], factor
        )
        prob = jnp.exp(scores - lse_rows[stripe][:, None])
        grad_prob = jnp.dot(
            g_rows[stripe], key_rows[:, :lat_width].T, preferred_element_type=jnp.float32
        )
        grad_score = (prob * (grad_prob - d_rows[stripe][:, None])).astype(jnp.bfloat16)
        grads.append(
            (factor * jnp.dot(grad_score, key_rows, preferred_element_type=jnp.float32)).astype(
                jnp.bfloat16
            )
        )
        score_blocks.append(grad_score)
        prob_blocks.append(prob.astype(jnp.bfloat16))
    key_terms = []
    for block in range(STRIPES):
        score_cat = jnp.concatenate(
            [score_blocks[s][:, block * span : (block + 1) * span] for s in range(block, STRIPES)],
            axis=0,
        )
        prob_cat = jnp.concatenate(
            [prob_blocks[s][:, block * span : (block + 1) * span] for s in range(block, STRIPES)],
            axis=0,
        )
        query_cat = q_rows[block:].reshape(-1, width)
        context_cat = g_rows[block:].reshape(-1, lat_width)
        along_query = factor * jnp.dot(score_cat.T, query_cat, preferred_element_type=jnp.float32)
        along_value = jnp.dot(prob_cat.T, context_cat, preferred_element_type=jnp.float32)
        term = jnp.concatenate(
            [along_query[:, :lat_width] + along_value, along_query[:, lat_width:]], axis=1
        )
        key_terms.append(term.astype(jnp.bfloat16))
    partial_value = jnp.stack(key_terms)
    returned = lax.all_to_all(partial_value, "ctx", split_axis=1, concat_axis=1, tiled=True)
    grad_lat = jnp.sum(returned.reshape(STRIPES, parts, stretch, width).astype(jnp.float32), axis=1)
    grad_lat = grad_lat.reshape(1, tok_count, width).astype(jnp.bfloat16)
    grad_q = jnp.stack(grads).reshape(1, tok_count, heads, width)
    everyone = tok_count * parts * lax.axis_size("dp")
    weight_term = jnp.einsum(
        "thl,thd->hld", attn_out[0], out_grad[0], preferred_element_type=jnp.float32
    ) * (1.0 / math.sqrt(everyone))
    grad_w = lax.psum(weight_term, ("dp", "ctx"))
    return (grad_q, grad_lat, grad_w)


def solution(mesh):
    placed = (
        P("dp", "ctx"),
        P("dp", "ctx", None, None),
        P("dp", "ctx", None),
        P("dp", "ctx", None, None),
        P("dp", "ctx", None, None),
        P(),
    )
    return jax.shard_map(
        body,
        mesh=mesh,
        in_specs=placed,
        out_specs=(P("dp", "ctx", None, None), P("dp", "ctx", None), P()),
        check_vma=False,
    )
```

profile of v0, /device:TPU:0, one launch (start us, length us, event | category | flops | bytes accessed | tf_op | source)
XLA Modules:
  0.0 394.0 jit_solution(2795079057572154454)
XLA Ops:
  8.1 1.8 copy.230
  9.9 1.4 copy.299
  11.3 1.9 slice.1729
  13.1 1.3 multiply_reduce_fusion
  14.4 1.0 copy.300
  16.2 0.9 slice.1762
  17.1 0.9 slice.1793
  18.7 0.9 slice.1822
  21.8 0.9 slice.1874
  23.3 0.9 slice.1897
  24.9 0.9 slice.1918
  26.4 0.9 slice.1937
  27.9 0.9 slice.1954
  28.8 0.9 slice.1969
  30.3 0.9 slice.1982
  31.8 0.9 slice.1993
  33.3 0.9 slice.2002
  37.6 2.7 fusion.223
  40.3 1.1 copy.229
  45.6 1.1 copy.237
  48.0 23.4 %all_gather.6 = s32[16,128]{0,1:T(8,128)S(1)} all-gather(s32[16,8]{0,1:T(8,128)S(1)} %copy.228), channel_id=1, replica_groups=mesh['dp'=2,'ctx'=16] {'ctx'}, dimensions={1}, use_global_device_ids=true | all-gather | bytes 8704 | tf_op jit(solution)/shard_map/all_gather | solution.py:39
  73.5 1.1 copy.241
  78.0 1.1 copy.245
  82.5 1.1 copy.249
  87.6 1.1 copy.253
  93.3 1.1 copy.257
  134.2 1.0 reshape_reshape_squeeze.3
  135.2 1.8 reshape_reshape.3
  137.0 1.2 copy.302
  138.2 1.0 reshape.1083
  140.4 0.9 reshape.1085
  142.6 0.9 reshape.1087
  144.7 0.9 reshape.1089
  146.8 0.9 reshape.1091
  164.4 1.1 slice.2013
  166.3 1.2 fusion.234
  167.7 1.0 slice.2017
  169.3 1.1 slice.2021
  184.2 0.9 fusion.248
  185.4 0.9 fusion.249
  217.2 4.9 %copy.345 = bf16[16,128,576]{2,0,1:T(8,128)(2,1)} copy(bf16[16,128,576]{1,2,0:T(8,128)(2,1)} %constant_dynamic-update-slice_fusion.252) | data formatting | bytes 4718592 | tf_op jit(solution)/shard_map/stack | solution.py:91
  222.1 4.5 %all-to-all-start = ((bf16[16,128,576]{2,0,1:T(8,128)(2,1)}), bf16[16,128,576]{2,0,1:T(8,128)(2,1)}, u32[]{:S(2)}, u32[]{:S(2)}) async-start(bf16[16,128,576]{2,0,1:T(8,128)(2,1)} %copy.345), calls=%async_computation | async-start | bytes 5242880 | tf_op jit(solution)/shard_map/all_to_all | solution.py:92
  226.6 2.0 convolution_multiply_fusion.8
  228.7 1.6 fusion.123
  230.3 1.9 fusion.129
  232.2 1.8 fusion.127
  234.0 1.9 fusion.121
  235.9 1.7 fusion.119
  238.5 0.9 fusion.115
  239.4 0.9 fusion.101
  240.3 0.9 fusion.99
  241.2 1.0 fusion.113
  242.2 1.0 fusion.111
  243.1 1.0 fusion.109
  244.1 1.0 fusion.107
  245.1 1.0 fusion.105
  246.2 1.1 fusion.125
  247.2 1.1 fusion.103
  248.3 1.1 reshape.1082
  249.4 1.1 copy.349
  250.5 28.4 %all-to-all-done = bf16[16,128,576]{2,0,1:T(8,128)(2,1)} async-done(((bf16[16,128,576]{2,0,1:T(8,128)(2,1)}), bf16[16,128,576]{2,0,1:T(8,128)(2,1)}, u32[]{:S(2)}, u32[]{:S(2)}) %all-to-all-start) | async-done | bytes 2359328 | tf_op jit(solution)/shard_map/all_to_all | solution.py:92
  278.9 2.1 reduce.1
  281.9 102.4 %all-reduce.2.cloned.1.call-done = f32[2,512,128]{2,1,0:T(8,128)} async-done(((f32[2,512,128]{2,1,0:T(8,128)}), f32[2,512,128]{2,1,0:T(8,128)}) %all-reduce.2.cloned.1.call-update) | async-done | bytes 524304 | tf_op jit(solution)/shard_map/psum | solution.py:100
  384.3 1.9 copy.649
  (789 shorter events, 141.6 us)
Async XLA Ops:
  8.0 8.2 %copy-start.2 = (bf16[1,128,2,576]{1,3,2,0:T(8,128)(2,1)S(1)}, bf16[1,128,2,576]{1,3,2,0:T(8,128)(2,1)}, u32[]{:S(2)}) copy-start(bf16[1,128,2,576]{1,3,2,0:T(8,128)(2,1)} %param.7) | copy-start | bytes 884740
  8.0 156.4 %all-gather.2.cloned.1.call-start = ((), (), s32[]{:S(2)}) async-start(), calls=%async_computation.1 | async-start | bytes 2785280 | tf_op jit(solution)/shard_map/all_gather | solution.py:38
  37.6 35.3 %copy-start.142 = (bf16[8,2,512]{2,0,1:T(8,128)(2,1)S(1)}, bf16[8,2,512]{2,0,1:T(8,128)(2,1)}, u32[]{:S(2)}) copy-start(bf16[8,2,512]{2,0,1:T(8,128)(2,1)} %get-tuple-element.44) | copy-start | bytes 49156
  37.6 39.8 %copy-start.141 = (bf16[8,2,512]{2,0,1:T(8,128)(2,1)S(1)}, bf16[8,2,512]{2,0,1:T(8,128)(2,1)}, u32[]{:S(2)}) copy-start(bf16[8,2,512]{2,0,1:T(8,128)(2,1)} %get-tuple-element.43) | copy-start | bytes 49156
  37.6 43.5 %copy-start.155 = (f32[8,2]{0,1:T(2,128)S(1)}, f32[8,2]{0,1:T(2,128)}, u32[]{:S(2)}) copy-start(f32[8,2]{0,1:T(2,128)} %get-tuple-element.325) | copy-start | bytes 196
  37.6 44.3 %copy-start.140 = (bf16[8,2,512]{2,0,1:T(8,128)(2,1)S(1)}, bf16[8,2,512]{2,0,1:T(8,128)(2,1)}, u32[]{:S(2)}) copy-start(bf16[8,2,512]{2,0,1:T(8,128)(2,1)} %get-tuple-element.42) | copy-start | bytes 49156
  40.3 45.3 %copy-start.154 = (f32[8,2]{0,1:T(2,128)S(1)}, f32[8,2]{0,1:T(2,128)}, u32[]{:S(2)}) copy-start(f32[8,2]{0,1:T(2,128)} %get-tuple-element.324) | copy-start | bytes 196
  40.3 58.8 %copy-start.30 = (bf16[1,8,2,576]{1,3,2,0:T(8,128)(2,1)S(1)}, bf16[1,8,2,576]{1,3,2,0:T(8,128)(2,1)}, u32[]{:S(2)}) copy-start(bf16[1,8,2,576]{1,3,2,0:T(8,128)(2,1)} %get-tuple-element.23) | copy-start | bytes 55300
  40.3 62.2 %copy-start.139 = (bf16[8,2,512]{2,0,1:T(8,128)(2,1)S(1)}, bf16[8,2,512]{2,0,1:T(8,128)(2,1)}, u32[]{:S(2)}) copy-start(bf16[8,2,512]{2,0,1:T(8,128)(2,1)} %get-tuple-element.38) | copy-start | bytes 49156
  40.3 62.8 %copy-start.29 = (bf16[1,8,2,576]{1,3,2,0:T(8,128)(2,1)S(1)}, bf16[1,8,2,576]{1,3,2,0:T(8,128)(2,1)}, u32[]{:S(2)}) copy-start(bf16[1,8,2,576]{1,3,2,0:T(8,128)(2,1)} %get-tuple-element.22) | copy-start | bytes 55300
  40.3 66.3 %copy-start.138 = (bf16[8,2,512]{2,0,1:T(8,128)(2,1)S(1)}, bf16[8,2,512]{2,0,1:T(8,128)(2,1)}, u32[]{:S(2)}) copy-start(bf16[8,2,512]{2,0,1:T(8,128)(2,1)} %get-tuple-element.37) | copy-start | bytes 49156
  41.5 69.2 %copy-start.137 = (bf16[8,2,512]{2,0,1:T(8,128)(2,1)S(1)}, bf16[8,2,512]{2,0,1:T(8,128)(2,1)}, u32[]{:S(2)}) copy-start(bf16[8,2,512]{2,0,1:T(8,128)(2,1)} %get-tuple-element.36) | copy-start | bytes 49156
  46.7 68.2 %copy-start.136 = (bf16[8,2,512]{2,0,1:T(8,128)(2,1)S(1)}, bf16[8,2,512]{2,0,1:T(8,128)(2,1)}, u32[]{:S(2)}) copy-start(bf16[8,2,512]{2,0,1:T(8,128)(2,1)} %get-tuple-element.35) | copy-start | bytes 49156
  72.9 46.1 %copy-start.135 = (bf16[8,2,512]{2,0,1:T(8,128)(2,1)S(1)}, bf16[8,2,512]{2,0,1:T(8,128)(2,1)}, u32[]{:S(2)}) copy-start(bf16[8,2,512]{2,0,1:T(8,128)(2,1)} %get-tuple-element.34) | copy-start | bytes 49156
  76.7 46.5 %copy-start.134 = (bf16[8,2,512]{2,0,1:T(8,128)(2,1)S(1)}, bf16[8,2,512]{2,0,1:T(8,128)(2,1)}, u32[]{:S(2)}) copy-start(bf16[8,2,512]{2,0,1:T(8,128)(2,1)} %get-tuple-element.33) | copy-start | bytes 49156
  79.8 47.4 %copy-start.133 = (bf16[8,2,512]{2,0,1:T(8,128)(2,1)S(1)}, bf16[8,2,512]{2,0,1:T(8,128)(2,1)}, u32[]{:S(2)}) copy-start(bf16[8,2,512]{2,0,1:T(8,128)(2,1)} %get-tuple-element.32) | copy-start | bytes 49156
  83.6 46.4 %copy-start.153 = (f32[8,2]{0,1:T(2,128)S(1)}, f32[8,2]{0,1:T(2,128)}, u32[]{:S(2)}) copy-start(f32[8,2]{0,1:T(2,128)} %get-tuple-element.314) | copy-start | bytes 196
  83.6 47.1 %copy-start.132 = (bf16[8,2,512]{2,0,1:T(8,128)(2,1)S(1)}, bf16[8,2,512]{2,0,1:T(8,128)(2,1)}, u32[]{:S(2)}) copy-start(bf16[8,2,512]{2,0,1:T(8,128)(2,1)} %get-tuple-element.31) | copy-start | bytes 49156
  88.7 44.8 %copy-start.152 = (f32[8,2]{0,1:T(2,128)S(1)}, f32[8,2]{0,1:T(2,128)}, u32[]{:S(2)}) copy-start(f32[8,2]{0,1:T(2,128)} %get-tuple-element.313) | copy-start | bytes 196
  115.5 23.6 %copy-start.48 = (bf16[120,2,512]{2,0,1:T(8,128)(2,1)S(1)}, bf16[120,2,512]{2,0,1:T(8,128)(2,1)}, u32[]{:S(2)}) copy-start(bf16[120,2,512]{2,0,1:T(8,128)(2,1)} %slice.2137) | copy-start | bytes 737284
  123.8 16.4 %copy-start.39 = (bf16[1,112,2,576]{1,3,2,0:T(8,128)(2,1)S(1)}, bf16[1,112,2,576]{1,3,2,0:T(8,128)(2,1)}, u32[]{:S(2)}) copy-start(bf16[1,112,2,576]{1,3,2,0:T(8,128)(2,1)} %slice.1762) | copy-start | bytes 774148
  135.2 7.2 %copy-start.38 = (bf16[1,104,2,576]{1,3,2,0:T(8,128)(2,1)S(1)}, bf16[1,104,2,576]{1,3,2,0:T(8,128)(2,1)}, u32[]{:S(2)}) copy-start(bf16[1,104,2,576]{1,3,2,0:T(8,128)(2,1)} %slice.1793) | copy-start | bytes 718852
  150.7 7.1 %copy-start.34 = (bf16[1,40,2,576]{1,3,2,0:T(8,128)(2,1)S(1)}, bf16[1,40,2,576]{1,3,2,0:T(8,128)(2,1)}, u32[]{:S(2)}) copy-start(bf16[1,40,2,576]{1,3,2,0:T(8,128)(2,1)} %slice.1969) | copy-start | bytes 276484
  151.7 7.0 %copy-start.85 = (bf16[40,2,512]{2,0,1:T(8,128)(2,1)S(1)}, bf16[40,2,512]{2,0,1:T(8,128)(2,1)}, u32[]{:S(2)}) copy-start(bf16[40,2,512]{2,0,1:T(8,128)(2,1)} %slice.2357) | copy-start | bytes 245764
  152.4 7.1 %copy-start.33 = (bf16[1,32,2,576]{1,3,2,0:T(8,128)(2,1)S(1)}, bf16[1,32,2,576]{1,3,2,0:T(8,128)(2,1)}, u32[]{:S(2)}) copy-start(bf16[1,32,2,576]{1,3,2,0:T(8,128)(2,1)} %slice.1982) | copy-start | bytes 221188
  152.6 7.7 %copy-start.90 = (bf16[32,2,512]{2,0,1:T(8,128)(2,1)S(1)}, bf16[32,2,512]{2,0,1:T(8,128)(2,1)}, u32[]{:S(2)}) copy-start(bf16[32,2,512]{2,0,1:T(8,128)(2,1)} %slice.2368) | copy-start | bytes 196612
  153.4 7.7 %copy-start.32 = (bf16[1,24,2,576]{1,3,2,0:T(8,128)(2,1)S(1)}, bf16[1,24,2,576]{1,3,2,0:T(8,128)(2,1)}, u32[]{:S(2)}) copy-start(bf16[1,24,2,576]{1,3,2,0:T(8,128)(2,1)} %slice.1993) | copy-start | bytes 165892
  153.6 8.4 %copy-start.98 = (bf16[24,2,512]{2,0,1:T(8,128)(2,1)S(1)}, bf16[24,2,512]{2,0,1:T(8,128)(2,1)}, u32[]{:S(2)}) copy-start(bf16[24,2,512]{2,0,1:T(8,128)(2,1)} %slice.2377) | copy-start | bytes 147460
  154.3 8.3 %copy-start.31 = (bf16[1,16,2,576]{1,3,2,0:T(8,128)(2,1)S(1)}, bf16[1,16,2,576]{1,3,2,0:T(8,128)(2,1)}, u32[]{:S(2)}) copy-start(bf16[1,16,2,576]{1,3,2,0:T(8,128)(2,1)} %slice.2002) | copy-start | bytes 110596
  154.5 9.0 %copy-start.103 = (bf16[16,2,512]{2,0,1:T(8,128)(2,1)S(1)}, bf16[16,2,512]{2,0,1:T(8,128)(2,1)}, u32[]{:S(2)}) copy-start(bf16[16,2,512]{2,0,1:T(8,128)(2,1)} %slice.2384) | copy-start | bytes 98308
  156.3 10.0 %copy-start.145 = (bf16[16,576]{1,0:T(8,128)(2,1)S(1)}, bf16[16,576]{1,0:T(8,128)(2,1)}, u32[]{:S(2)}) copy-start(bf16[16,576]{1,0:T(8,128)(2,1)} %squeeze.120) | copy-start | bytes 55300
  156.3 10.0 %copy-start.187 = (s32[16]{0:T(128)S(1)}, s32[16]{0:T(128)}, u32[]{:S(2)}) copy-start(s32[16]{0:T(128)} %broadcast_in_dim.162) | copy-start | bytes 196
  157.8 10.9 %copy-start.110 = (bf16[16,576]{1,0:T(8,128)(2,1)S(1)}, bf16[16,576]{1,0:T(8,128)(2,1)}, u32[]{:S(2)}) copy-start(bf16[16,576]{1,0:T(8,128)(2,1)} %squeeze.124) | copy-start | bytes 55300
  157.8 10.9 %copy-start.151 = (s32[2,128]{1,0:T(2,128)S(1)}, s32[2,128]{1,0:T(2,128)}, u32[]{:S(2)}) copy-start(s32[2,128]{1,0:T(2,128)} %copy.236) | copy-start | bytes 3076
  157.8 10.9 %copy-start.165 = (s32[16]{0:T(128)S(1)}, s32[16]{0:T(128)}, u32[]{:S(2)}) copy-start(s32[16]{0:T(128)} %broadcast_in_dim.165) | copy-start | bytes 196
  160.4 10.0 %copy-start.111 = (bf16[16,576]{1,0:T(8,128)(2,1)S(1)}, bf16[16,576]{1,0:T(8,128)(2,1)}, u32[]{:S(2)}) copy-start(bf16[16,576]{1,0:T(8,128)(2,1)} %squeeze.126) | copy-start | bytes 55300
  160.4 10.0 %copy-start.176 = (s32[16]{0:T(128)S(1)}, s32[16]{0:T(128)}, u32[]{:S(2)}) copy-start(s32[16]{0:T(128)} %broadcast_in_dim.168) | copy-start | bytes 196
  168.7 20.3 %copy-start.26 = (bf16[2,128,576]{2,1,0:T(8,128)(2,1)}, bf16[2,128,576]{2,1,0:T(8,128)(2,1)S(1)}, u32[]{:S(2)}) copy-start(bf16[2,128,576]{2,1,0:T(8,128)(2,1)S(1)} %slice.2017) | copy-start | bytes 884740
  170.4 18.8 %copy-start.25 = (bf16[3,128,576]{2,1,0:T(8,128)(2,1)}, bf16[3,128,576]{2,1,0:T(8,128)(2,1)S(1)}, u32[]{:S(2)}) copy-start(bf16[3,128,576]{2,1,0:T(8,128)(2,1)S(1)} %slice.2021) | copy-start | bytes 1327108
  171.1 18.4 %copy-start.24 = (bf16[4,128,576]{2,1,0:T(8,128)(2,1)}, bf16[4,128,576]{2,1,0:T(8,128)(2,1)S(1)}, u32[]{:S(2)}) copy-start(bf16[4,128,576]{2,1,0:T(8,128)(2,1)S(1)} %slice.2025) | copy-start | bytes 1769476
  172.8 17.3 %copy-start.22 = (bf16[6,128,576]{2,1,0:T(8,128)(2,1)}, bf16[6,128,576]{2,1,0:T(8,128)(2,1)S(1)}, u32[]{:S(2)}) copy-start(bf16[6,128,576]{2,1,0:T(8,128)(2,1)S(1)} %slice.2033) | copy-start | bytes 2654212
  173.7 16.8 %copy-start.20 = (bf16[7,128,576]{2,1,0:T(8,128)(2,1)}, bf16[7,128,576]{2,1,0:T(8,128)(2,1)S(1)}, u32[]{:S(2)}) copy-start(bf16[7,128,576]{2,1,0:T(8,128)(2,1)S(1)} %slice.2037) | copy-start | bytes 3096580
  174.6 16.3 %copy-start.18 = (bf16[8,128,576]{2,1,0:T(8,128)(2,1)}, bf16[8,128,576]{2,1,0:T(8,128)(2,1)S(1)}, u32[]{:S(2)}) copy-start(bf16[8,128,576]{2,1,0:T(8,128)(2,1)S(1)} %slice.2041) | copy-start | bytes 3538948
  175.6 15.8 %copy-start.16 = (bf16[9,128,576]{2,1,0:T(8,128)(2,1)}, bf16[9,128,576]{2,1,0:T(8,128)(2,1)S(1)}, u32[]{:S(2)}) copy-start(bf16[9,128,576]{2,1,0:T(8,128)(2,1)S(1)} %slice.2045) | copy-start | bytes 3981316
  176.6 15.2 %copy-start.14 = (bf16[10,128,576]{2,1,0:T(8,128)(2,1)}, bf16[10,128,576]{2,1,0:T(8,128)(2,1)S(1)}, u32[]{:S(2)}) copy-start(bf16[10,128,576]{2,1,0:T(8,128)(2,1)S(1)} %slice.2049) | copy-start | bytes 4423684
  177.8 14.6 %copy-start.12 = (bf16[11,128,576]{2,1,0:T(8,128)(2,1)}, bf16[11,128,576]{2,1,0:T(8,128)(2,1)S(1)}, u32[]{:S(2)}) copy-start(bf16[11,128,576]{2,1,0:T(8,128)(2,1)S(1)} %slice.2053) | copy-start | bytes 4866052
  178.9 14.0 %copy-start.10 = (bf16[12,128,576]{2,1,0:T(8,128)(2,1)}, bf16[12,128,576]{2,1,0:T(8,128)(2,1)S(1)}, u32[]{:S(2)}) copy-start(bf16[12,128,576]{2,1,0:T(8,128)(2,1)S(1)} %slice.2057) | copy-start | bytes 5308420
  180.4 13.1 %copy-start.8 = (bf16[13,128,576]{2,1,0:T(8,128)(2,1)}, bf16[13,128,576]{2,1,0:T(8,128)(2,1)S(1)}, u32[]{:S(2)}) copy-start(bf16[13,128,576]{2,1,0:T(8,128)(2,1)S(1)} %slice.2061) | copy-start | bytes 5750788
  181.9 12.1 %copy-start.6 = (bf16[14,128,576]{2,1,0:T(8,128)(2,1)}, bf16[14,128,576]{2,1,0:T(8,128)(2,1)S(1)}, u32[]{:S(2)}) copy-start(bf16[14,128,576]{2,1,0:T(8,128)(2,1)S(1)} %slice.2065) | copy-start | bytes 6193156
  183.7 11.0 %copy-start.4 = (bf16[15,128,576]{2,1,0:T(8,128)(2,1)}, bf16[15,128,576]{2,1,0:T(8,128)(2,1)S(1)}, u32[]{:S(2)}) copy-start(bf16[15,128,576]{2,1,0:T(8,128)(2,1)S(1)} %slice.2069) | copy-start | bytes 6635524
  189.2 7.0 %copy-start.144 = (bf16[16,256]{1,0:T(8,128)(2,1)}, bf16[16,256]{1,0:T(8,128)(2,1)S(1)}, u32[]{:S(2)}) copy-start(bf16[16,256]{1,0:T(8,128)(2,1)S(1)} %fusion.133) | copy-start | bytes 24580
  189.5 6.7 %copy-start.143 = (bf16[16,384]{1,0:T(8,128)(2,1)}, bf16[16,384]{1,0:T(8,128)(2,1)S(1)}, u32[]{:S(2)}) copy-start(bf16[16,384]{1,0:T(8,128)(2,1)S(1)} %fusion.130) | copy-start | bytes 36868
  205.6 8.2 %copy-start.91 = (bf16[64,512]{1,0:T(8,128)(2,1)S(1)}, bf16[64,512]{1,0:T(8,128)(2,1)}, u32[]{:S(2)}) copy-start(bf16[64,512]{1,0:T(8,128)(2,1)} %reshape.1106) | copy-start | bytes 196612
  206.1 8.6 %copy-start.97 = (bf16[48,512]{1,0:T(8,128)(2,1)S(1)}, bf16[48,512]{1,0:T(8,128)(2,1)}, u32[]{:S(2)}) copy-start(bf16[48,512]{1,0:T(8,128)(2,1)} %reshape.1108) | copy-start | bytes 147460
  207.1 8.5 %copy-start.105 = (bf16[32,512]{1,0:T(8,128)(2,1)S(1)}, bf16[32,512]{1,0:T(8,128)(2,1)}, u32[]{:S(2)}) copy-start(bf16[32,512]{1,0:T(8,128)(2,1)} %reshape.1110) | copy-start | bytes 98308
  222.1 56.8 %all-to-all-start = ((bf16[16,128,576]{2,0,1:T(8,128)(2,1)}), bf16[16,128,576]{2,0,1:T(8,128)(2,1)}, u32[]{:S(2)}, u32[]{:S(2)}) async-start(bf16[16,128,576]{2,0,1:T(8,128)(2,1)} %copy.345), calls=%async_computation | async-start | bytes 5242880 | tf_op jit(solution)/shard_map/all_to_all | solution.py:92
  226.6 157.7 %all-reduce.2.cloned.1.call-start = ((), (), s32[]{:S(2)}) async-start(), calls=%async_computation.2 | async-start | bytes 1048576 | tf_op jit(solution)/shard_map/psum | solution.py:100
  228.7 8.9 %copy-start.23 = (bf16[6,128,576]{2,1,0:T(8,128)(2,1)S(1)}, bf16[6,128,576]{2,1,0:T(8,128)(2,1)}, u32[]{:S(2)}) copy-start(bf16[6,128,576]{2,1,0:T(8,128)(2,1)} %copy-done.22) | copy-start | bytes 2654212
  228.7 8.9 %copy-start.96 = (bf16[16,768]{1,0:T(8,128)(2,1)S(1)}, bf16[16,768]{1,0:T(8,128)(2,1)}, u32[]{:S(2)}) copy-start(bf16[16,768]{1,0:T(8,128)(2,1)} %copy-done.95) | copy-start | bytes 73732
  228.7 9.8 %copy-start.21 = (bf16[7,128,576]{2,1,0:T(8,128)(2,1)S(1)}, bf16[7,128,576]{2,1,0:T(8,128)(2,1)}, u32[]{:S(2)}) copy-start(bf16[7,128,576]{2,1,0:T(8,128)(2,1)} %copy-done.20) | copy-start | bytes 3096580
  228.7 9.8 %copy-start.93 = (bf16[16,896]{1,0:T(8,128)(2,1)S(1)}, bf16[16,896]{1,0:T(8,128)(2,1)}, u32[]{:S(2)}) copy-start(bf16[16,896]{1,0:T(8,128)(2,1)} %copy-done.92) | copy-start | bytes 86020
  230.3 9.1 %copy-start.19 = (bf16[8,128,576]{2,1,0:T(8,128)(2,1)S(1)}, bf16[8,128,576]{2,1,0:T(8,128)(2,1)}, u32[]{:S(2)}) copy-start(bf16[8,128,576]{2,1,0:T(8,128)(2,1)} %copy-done.18) | copy-start | bytes 3538948
  230.3 9.1 %copy-start.89 = (bf16[16,1024]{1,0:T(8,128)(2,1)S(1)}, bf16[16,1024]{1,0:T(8,128)(2,1)}, u32[]{:S(2)}) copy-start(bf16[16,1024]{1,0:T(8,128)(2,1)} %copy-done.88) | copy-start | bytes 98308
  249.4 136.8 %copy-start.1 = (bf16[2,512,128]{2,1,0:T(8,128)(2,1)S(1)}, bf16[2,512,128]{2,1,0:T(8,128)(2,1)}, u32[]{:S(2)}) copy-start(bf16[2,512,128]{2,1,0:T(8,128)(2,1)} %param.11) | copy-start | bytes 786436
  (127 other events, 350.3 us)
Sparse Core Ops, SparseCore 0:
  11.0 46.2 all-gather.1
Sparse Core Ops, SparseCore 1:
  232.9 151.3 all-reduce.1
where the time goes:
time: 400 us; the launch traced here: 394 us
  local copies, waits for them, and re-layouts  149 us (37%)
  waiting for transfers between devices  131 us (33%)
  matrix products  48.9 us (12%)
  blocking collectives  23.4 us (6%)
  between operations  19.2 us (5%)
  other arithmetic  18.6 us (5%)
  starting transfers between devices  4.55 us (1%)
    psum x1, waiting for transfers between devices, body(): grad_w = lax.psum(weight_term, ('dp', 'ctx'))  102 us
    all_to_all x1, waiting for transfers between devices, body(): lax.all_to_all(partial_value, 'ctx', split_axis=1, concat_axis=1, tiled=T...  28.4 us
    all_gather x1, blocking collectives, body(): lax.all_gather(own[1], 'ctx', axis=1, tiled=True)  23.4 us
    broadcast_in_dim x32, local copies, waits for them, and re-layouts, body(): p_rows = jnp.repeat(positions[0].reshape(STRIPES, stretch), heads, axis=1)  19.8 us
    dot_general x16, matrix products, body(): jnp.dot(grad_score, key_rows, preferred_element_type=jnp.float32)  19.5 us
    slice x28, local copies, waits for them, and re-layouts, body(): query_cat = q_rows[block:].reshape(-1, width)  16.9 us
    unnamed x18, other arithmetic  13 us
    slice x17, local copies, waits for them, and re-layouts, body(): q_rows[stripe]  11.6 us
  transfers between devices with their start and end apart: 3, of which 2 were waited for; matrix products, arithmetic and copies ran while one was open for 40% of the time, Pallas kernels for 0%

commit v1 on v0

v1 whole, which is shorter than its diff:
```python
import functools
import math

import jax
import jax.numpy as jnp
from jax import lax
from jax.experimental import pallas as pl
from jax.experimental.pallas import tpu as pltpu
from jax.sharding import PartitionSpec as P

ROPE = 64
HEAD_DIM = 128
GROUP = 4
EXTRA = 16
F32 = jnp.float32
BF16 = jnp.bfloat16
VMEM_LIMIT = 56 * 1024 * 1024


def mm(a, b):
    return jnp.dot(a, b, preferred_element_type=F32)


def mm_t(a, b):
    return lax.dot_general(a, b, (((1,), (1,)), ((), ())), preferred_element_type=F32)


def call(kernel, outs, args, scratch=(), flops=0, nbytes=0, name=None, smem=()):
    specs = [
        pl.BlockSpec(memory_space=pltpu.SMEM if i in smem else pltpu.VMEM) for i in range(len(args))
    ]
    return pl.pallas_call(
        kernel,
        out_shape=[jax.ShapeDtypeStruct(s, d) for s, d in outs],
        in_specs=specs,
        out_specs=[pl.BlockSpec(memory_space=pltpu.VMEM) for _ in outs],
        scratch_shapes=list(scratch),
        compiler_params=pltpu.CompilerParams(vmem_limit_bytes=VMEM_LIMIT),
        cost_estimate=pl.CostEstimate(flops=flops, bytes_accessed=nbytes, transcendentals=0),
        name=name,
    )(*args)


def own_kernel(idx_ref, attn_ref, og_ref, wuv_ref, delta_ref, *rest):
    chunks, term = rest[:GROUP], rest[GROUP]
    heads, lat, tok = attn_ref.shape
    delta_ref[...] = jnp.zeros_like(delta_ref)
    for h in range(heads):
        g = mm(wuv_ref[h], og_ref[h]).astype(BF16).astype(F32)
        delta_ref[h : h + 1, :] = jnp.sum(g * attn_ref[h].astype(F32), axis=0, keepdims=True)
        term[h] = mm_t(attn_ref[h], og_ref[h])
    step = lat // GROUP
    me = lax.rem(idx_ref[0], GROUP)
    for k in range(GROUP):
        at = pl.multiple_of(jnp.bitwise_xor(me, k) * step, step)
        chunks[k][...] = term[:, pl.ds(at, step), :].astype(BF16)


def score_kernel(factor, nkey, width, heads, *refs):
    lat_refs = refs[:nkey]
    q_refs = refs[nkey : nkey + GROUP]
    delta_ref = refs[nkey + GROUP]
    s_ref, k_ref, stat_ref, kt, qt = refs[nkey + GROUP + 1 :]
    wide = kt.shape[0]
    tok = lat_refs[0].shape[1]
    rows = heads * tok
    for a in range(nkey):
        kt[: width + EXTRA, a * tok : (a + 1) * tok] = lat_refs[a][...]
    kt[width + EXTRA :, :] = jnp.zeros((wide - width - EXTRA, nkey * tok), BF16)
    k_ref[...] = kt[...].T
    pos = k_ref[:, width : width + 128 - width % 128].astype(F32)
    key_pos = pos[:, 0:1] * 64.0 + pos[:, 1:2]
    qt[width:, :] = jnp.zeros((wide - width, rows), BF16)
    stat_ref[...] = jnp.zeros_like(stat_ref)
    stat_ref[GROUP * heads : GROUP * heads + heads, :] = delta_ref[:heads, :]
    for j in range(GROUP):
        q_ref = q_refs[j]
        for h in range(heads):
            qt[:width, h * tok : (h + 1) * tok] = q_ref[h * width : (h + 1) * width, :]
        base = q_ref.shape[0] - EXTRA
        qp = q_ref[base:, :].astype(F32)
        one = qp[0:1, :] * 64.0 + qp[1:2, :]
        row_pos = jnp.concatenate([one] * heads, axis=1)
        s = mm(k_ref[...], qt[...]) * factor
        s = jnp.where(key_pos <= row_pos, s, -1e30)
        s_ref[:, j * rows : (j + 1) * rows] = s
        top = jnp.max(s, axis=0, keepdims=True)
        lse = top + jnp.log(jnp.sum(jnp.exp(s - top), axis=0, keepdims=True))
        for h in range(heads):
            stat_ref[j * heads + h : j * heads + h + 1, :] = lse[:, h * tok : (h + 1) * tok]


def context_kernel(width, heads, *refs):
    q_refs = refs[:GROUP]
    k_ref, wuv_ref, g_ref, gp_ref = refs[GROUP:]
    lat = wuv_ref.shape[1]
    tok = q_refs[0].shape[1]
    rows = heads * tok
    for j in range(GROUP):
        for h in range(heads):
            at = heads * width + h * HEAD_DIM
            og = q_refs[j][at : at + HEAD_DIM, :]
            g_ref[:, j * rows + h * tok : j * rows + (h + 1) * tok] = mm(wuv_ref[h], og).astype(BF16)
        cols = slice(j * rows, (j + 1) * rows)
        gp_ref[:, cols] = mm(k_ref[:, :lat], g_ref[:, cols])


def grad_kernel(factor, nkey, width, heads, *refs):
    lat_refs = refs[:nkey]
    q_refs = refs[nkey : nkey + GROUP]
    stats = refs[nkey + GROUP : nkey + 2 * GROUP]
    s_ref, gp_ref, g_ref = refs[nkey + 2 * GROUP : nkey + 2 * GROUP + 3]
    rest = refs[nkey + 2 * GROUP + 3 :]
    gq_refs = rest[:GROUP]
    part_refs = rest[GROUP : GROUP + nkey]
    kt, qt, gs_all, p_all = rest[GROUP + nkey :]
    tok = lat_refs[0].shape[1]
    rows = heads * tok
    lat = g_ref.shape[0]
    for a in range(nkey):
        kt[:, a * tok : (a + 1) * tok] = lat_refs[a][:width, :]
    for j in range(GROUP):
        cols = slice(j * rows, (j + 1) * rows)
        lse_parts = []
        for k in range(GROUP):
            at = (j ^ k) * heads
            lse_parts.append(
                jnp.concatenate([stats[k][at + h : at + h + 1, :] for h in range(heads)], axis=1)
            )
        top = functools.reduce(jnp.maximum, lse_parts)
        lse = top + jnp.log(sum(jnp.exp(part - top) for part in lse_parts))
        at = GROUP * heads
        delta = jnp.concatenate([stats[j][at + h : at + h + 1, :] for h in range(heads)], axis=1)
        p = jnp.exp(s_ref[:, cols] - lse)
        gs = (p * (gp_ref[:, cols] - delta)).astype(BF16)
        p_all[:, cols] = p.astype(BF16)
        gs_all[:, cols] = gs
        gq = (mm(kt[...], gs) * factor).astype(BF16)
        for h in range(heads):
            head_cols = slice(j * rows + h * tok, j * rows + (h + 1) * tok)
            qt[:, head_cols] = q_refs[j][h * width : (h + 1) * width, :]
            gq_refs[j][h] = gq[:, h * tok : (h + 1) * tok]
    for a in range(nkey):
        at = slice(a * tok, (a + 1) * tok)
        gs = gs_all[at, :]
        along = mm_t(qt[...], gs) * factor
        value = mm_t(g_ref[...], p_all[at, :])
        part_refs[a][:lat, :] = (along[:lat] + value).astype(BF16)
        part_refs[a][lat:, :] = along[lat:].astype(BF16)


def spread_kernel(idx_ref, *refs):
    chunks, out_ref = refs[:GROUP], refs[GROUP]
    step = chunks[0].shape[1]
    me = lax.rem(idx_ref[0], GROUP)
    for k in range(GROUP):
        at = pl.multiple_of(jnp.bitwise_xor(me, k) * step, step)
        out_ref[:, pl.ds(at, step), :] = chunks[k][...].astype(F32)


def body(n_ctx, n_dp, positions, queries, latent, out_grad, attn_out, wuv):
    tok, heads, width = queries.shape[1:]
    lat = attn_out.shape[3]
    lines = n_ctx // GROUP
    rows = heads * tok
    all_rows = GROUP * rows
    keys = lines * tok
    wide = -(-(width + EXTRA) // 128) * 128
    factor = (HEAD_DIM + ROPE) ** (-0.5)

    def swap(x, mask):
        return lax.ppermute(x, "ctx", [(i, i ^ mask) for i in range(n_ctx)])

    idx = lax.axis_index("ctx").reshape(1)
    pos = positions
    pos_rows = jnp.concatenate(
        [pos // 64, pos % 64, jnp.zeros((EXTRA - 2, tok), pos.dtype)], axis=0
    ).astype(BF16)
    q_t = jnp.transpose(queries[0], (1, 2, 0))
    og_t = jnp.transpose(out_grad[0], (1, 2, 0))
    attn_t = jnp.transpose(attn_out[0], (1, 2, 0))
    lat_msg = jnp.concatenate([latent[0].T, pos_rows], axis=0)
    q_msg = jnp.concatenate(
        [q_t.reshape(heads * width, tok), og_t.reshape(heads * HEAD_DIM, tok), pos_rows], axis=0
    )
    lats = [lat_msg] + [swap(lat_msg, GROUP * k) for k in range(1, lines)]
    qs = [q_msg] + [swap(q_msg, k) for k in range(1, GROUP)]

    step = lat // GROUP
    delta, *chunks = call(
        own_kernel,
        [((8, tok), F32)] + [((heads, step, HEAD_DIM), BF16)] * GROUP,
        [idx, attn_t, og_t, wuv],
        [pltpu.VMEM((heads, lat, HEAD_DIM), F32)],
        flops=4 * rows * lat * HEAD_DIM,
        nbytes=2 * (attn_t.size + og_t.size + 2 * wuv.size),
        name="own_rows",
        smem=(0,),
    )
    got = [chunks[0]] + [swap(chunks[k], k) for k in range(1, GROUP)]
    scale = 1.0 / math.sqrt(tok * n_ctx * n_dp)
    mine = (sum(c.astype(F32) for c in got) * scale).astype(BF16)
    for bit in range((lines - 1).bit_length()):
        mine = (mine.astype(F32) + swap(mine, GROUP << bit).astype(F32)).astype(BF16)
    for bit in range((n_dp - 1).bit_length()):
        other = lax.ppermute(mine, "dp", [(i, i ^ (1 << bit)) for i in range(n_dp)])
        mine = (mine.astype(F32) + other.astype(F32)).astype(BF16)

    s, k_nat, stat = call(
        functools.partial(score_kernel, factor, lines, width, heads),
        [((keys, all_rows), F32), ((keys, wide), BF16), ((EXTRA, tok), F32)],
        lats + qs + [delta],
        [pltpu.VMEM((wide, keys), BF16), pltpu.VMEM((wide, rows), BF16)],
        flops=2 * keys * all_rows * wide,
        nbytes=4 * keys * all_rows + 2 * keys * wide * 2 + 2 * all_rows * wide,
        name="scores",
    )
    stats = [stat] + [swap(stat, k) for k in range(1, GROUP)]
    g, gp = call(
        functools.partial(context_kernel, width, heads),
        [((lat, all_rows), BF16), ((keys, all_rows), F32)],
        qs + [k_nat, wuv],
        flops=2 * keys * all_rows * lat + 2 * all_rows * lat * HEAD_DIM,
        nbytes=4 * keys * all_rows + 2 * keys * wide + 2 * all_rows * (wide + lat),
        name="context_grads",
    )
    outs = call(
        functools.partial(grad_kernel, factor, lines, width, heads),
        [((heads, width, tok), BF16)] * GROUP + [((width, tok), BF16)] * lines,
        lats + qs + stats + [s, gp, g],
        [
            pltpu.VMEM((width, keys), BF16),
            pltpu.VMEM((width, all_rows), BF16),
            pltpu.VMEM((keys, all_rows), BF16),
            pltpu.VMEM((keys, all_rows), BF16),
        ],
        flops=2 * keys * all_rows * (2 * width + lat),
        nbytes=8 * keys * all_rows + 2 * all_rows * (2 * width + lat) + 4 * keys * width,
        name="gradients",
    )
    gqs, parts = outs[:GROUP], outs[GROUP:]
    parts = [parts[0]] + [swap(parts[k], GROUP * k) for k in range(1, lines)]
    gqs = [gqs[0]] + [swap(gqs[k], k) for k in range(1, GROUP)]
    grad_lat = sum(p.astype(F32) for p in parts).astype(BF16)
    grad_q = sum(p.astype(F32) for p in gqs).astype(BF16)
    pieces = [mine] + [swap(mine, k) for k in range(1, GROUP)]
    (grad_w,) = call(
        spread_kernel, [((heads, lat, HEAD_DIM), F32)], [idx] + pieces, name="spread", smem=(0,)
    )
    return (jnp.transpose(grad_q, (2, 0, 1))[None], grad_lat.T[None], grad_w)


def solution(mesh):
    placed = (
        P("dp", "ctx"),
        P("dp", "ctx", None, None),
        P("dp", "ctx", None),
        P("dp", "ctx", None, None),
        P("dp", "ctx", None, None),
        P(),
    )
    return jax.shard_map(
        functools.partial(body, mesh.shape["ctx"], mesh.shape["dp"]),
        mesh=mesh,
        in_specs=placed,
        out_specs=(P("dp", "ctx", None, None), P("dp", "ctx", None), P()),
        check_vma=False,
    )
```

time: 400 us -> 85.4 us (0.21); the launches traced: 394 us -> 84.9 us
  local copies, waits for them, and re-layouts: 149 us -> 7.88 us
  waiting for transfers between devices: 131 us -> 24.7 us
  matrix products: 48.9 us -> 0 us
  blocking collectives: 23.4 us -> 0 us
  starting transfers between devices: 4.55 us -> 26.9 us
  Pallas kernels: 0 us -> 19.5 us
  between operations: 19.2 us -> 0.84 us
  other arithmetic: 18.6 us -> 5.11 us
    psum x1 -> x0, waiting for transfers between devices: 102 us -> none  [body(): grad_w = lax.psum(weight_term, ('dp', 'ctx'))]
    slice x136 -> x0, local copies, waits for them, and re-layouts: 56.8 us -> none  [the longest x28 16.9 us: body(): query_cat = q_rows[block:].reshape(-1, width)]
    dot_general x82 -> x0, matrix products: 48.9 us -> none  [the longest x16 19.5 us: body(): jnp.dot(grad_score, key_rows, preferred_element_type=jnp.float32)]
    all_to_all x1 -> x0, waiting for transfers between devices: 28.4 us -> none  [body(): lax.all_to_all(partial_value, 'ctx', split_axis=1, concat_axis=1, tiled=T...]
    ppermute x0 -> x24, starting transfers between devices: none -> 26.9 us  [the longest x23 25.4 us: swap(): return lax.ppermute(x, 'ctx', [(i, i ^ mask) for i in range(n_ctx)])]
    ppermute x0 -> x24, waiting for transfers between devices: none -> 24.7 us  [the longest x23 24.7 us: swap(): return lax.ppermute(x, 'ctx', [(i, i ^ mask) for i in range(n_ctx)])]
    all_gather x1 -> x0, blocking collectives: 23.4 us -> none  [body(): lax.all_gather(own[1], 'ctx', axis=1, tiled=True)]
    reshape x29 -> x0, local copies, waits for them, and re-layouts: 22.3 us -> none  [the longest x14 11.2 us: body(): query_cat = q_rows[block:].reshape(-1, width)]
  transfers between devices with their start and end apart: 3 -> 24, of which waited for: 2 -> 7; matrix products, arithmetic and copies ran while one was open for 40% -> 7% of each run, Pallas kernels for 0% -> 20%
where the time goes in v1:
time: 85.4 us; the launch traced here: 84.9 us
  starting transfers between devices  26.9 us (31%)
  waiting for transfers between devices  24.7 us (29%)
  Pallas kernels  19.5 us (23%)
  local copies, waits for them, and re-layouts  7.88 us (9%)
  other arithmetic  5.11 us (6%)
    ppermute x23, starting transfers between devices, swap(): return lax.ppermute(x, 'ctx', [(i, i ^ mask) for i in range(n_ctx)])  25.4 us
    ppermute x23, waiting for transfers between devices, swap(): return lax.ppermute(x, 'ctx', [(i, i ^ mask) for i in range(n_ctx)])  24.7 us
    pallas_call x5, Pallas kernels, call(): pl.pallas_call(kernel, out_shape=[jax.ShapeDtypeStruct(s, d) for s, d in...  19.5 us
    unnamed x34, local copies, waits for them, and re-layouts  5.05 us
    broadcast_in_dim x2, other arithmetic, body(): return (jnp.transpose(grad_q, (2, 0, 1))[None], grad_lat.T[None], grad_w)  3.48 us
    concatenate x1, local copies, waits for them, and re-layouts, body(): jnp.concatenate([q_t.reshape(heads * width, tok), og_t.reshape(heads * HE...  2.83 us
  transfers between devices with their start and end apart: 24, of which 7 were waited for; matrix products, arithmetic and copies ran while one was open for 7% of the time, Pallas kernels for 20%

profile of v1, /device:TPU:0, one launch (start us, length us, event | category | flops | bytes accessed | tf_op | source)
XLA Modules:
  0.0 84.9 jit_solution(5122164890923414834)
XLA Ops:
  0.6 1.6 %copy.9 = bf16[1,128,2,128]{1,3,2,0:T(8,128)(2,1)} copy(bf16[1,128,2,128]{3,2,1,0:T(2,128)(2,1)} %param.9) | data formatting | bytes 131072 | tf_op args[3]
  2.3 1.8 %copy.10 = bf16[1,128,2,512]{1,3,2,0:T(8,128)(2,1)} copy(bf16[1,128,2,512]{3,2,1,0:T(2,128)(2,1)} %param.10) | data formatting | bytes 524288 | tf_op args[4]
  4.1 2.1 %own_rows.1 = (f32[8,128]{1,0:T(8,128)}, bf16[2,128,128]{2,1,0:T(8,128)(2,1)}, bf16[2,128,128]{2,1,0:T(8,128)(2,1)}, bf16[2,128,128]{2,1,0:T(8,128)(2,1)}, bf16[2,128,128]{2,1,0:T(8,128)(2,1)}) custom-call(s32[1]{0:T(128)} %bitcast.8.idx_ref, bf16[2,512,128]{2,1,0:T(8,128)(2,1)} %bitcast.25, bf16[2,128,128]{2,1,0:T(8,128)(2,1)} %bitcast.26, ...), custom_call_target="tpu_custom_call" | custom-call | flops 67108864 | bytes 851968 | tf_op jit(solution)/shard_map/own_rows/pallas_call | solution.py:32
  6.2 2.4 %collective-permute-start.17 = (bf16[2,128,128]{2,1,0:T(8,128)(2,1)}, bf16[2,128,128]{2,1,0:T(8,128)(2,1)S(1)}, u32[]{:S(2)}, u32[]{:S(2)}) collective-permute-start(bf16[2,128,128]{2,1,0:T(8,128)(2,1)} %get-tuple-element.38), channel_id=1, source_target_pairs={{0,3},{1,2},{2,1},{3,0},{4,7},{5,6},{6,5},{7,4},{8,11},{9,10},{10,... | collective-permute-start | bytes 196616 | tf_op jit(solution)/shard_map/ppermute | solution.py:172
  8.6 0.6 collective-permute-start.16
  9.2 0.1 collective-permute-start.15
  9.3 0.7 fusion.3
  9.9 2.8 %concatenate.11.refs_4_.refs_0_ = bf16[1424,128]{1,0:T(8,128)(2,1)S(1)} concatenate(bf16[1152,128]{1,0:T(8,128)(2,1)} %bitcast.28, bf16[256,128]{1,0:T(8,128)(2,1)} %bitcast.27, bf16[1,128]{1,0:T(2,128)(2,1)S(1)} %get-tuple-element.39, bf16[1,128]{1,0:T(2,128)(2,1)S(1)} %get-tuple-element.40, bf16[14,128]{1,0:T(8,128)(2,1)S(1)} %broadcast_in_dim.9), dimensions={0} | concatenate | bytes 729088 | tf_op jit(solution)/shard_map/concatenate | solution.py:183
  12.8 0.0 copy-start
  12.8 0.5 collective-permute-start.3
  13.3 1.5 %collective-permute-start.4 = (bf16[1424,128]{1,0:T(8,128)(2,1)S(1)}, bf16[1424,128]{1,0:T(8,128)(2,1)S(1)}, u32[]{:S(2)}, u32[]{:S(2)}) collective-permute-start(bf16[1424,128]{1,0:T(8,128)(2,1)S(1)} %concatenate.11.refs_4_.refs_0_), channel_id=1, source_target_pairs={{0,2},{1,3},{2,0},{3,1},{4,6},{5,7},{6,4},{7,5},{8,10},{9,11},{10,... | collective-permute-start | bytes 1093640 | tf_op jit(solution)/shard_map/ppermute | solution.py:172
  14.7 0.0 collective-permute-done.17
  14.7 0.0 collective-permute-start.5
  14.8 0.0 collective-permute-done.16
  14.8 0.0 collective-permute-done.15
  14.8 0.9 %multiply_convert_fusion = bf16[2,128,128]{2,1,0:T(8,128)(2,1)S(1)} fusion(bf16[2,128,128]{2,1,0:T(8,128)(2,1)S(1)} %collective-permute-done.17, bf16[2,128,128]{2,1,0:T(8,128)(2,1)S(1)} %collective-permute-done.16, bf16[2,128,128]{2,1,0:T(8,128)(2,1)S(1)} %collective-permute-done.15, bf16[2,128,128]{2,1,0:T(8,128)(2,1)} %get-tuple-element.35), kind=kLoop, calls=%fused_computation.8 | loop fusion | flops 294912 | bytes 327680 | tf_op jit(solution)/shard_map/convert_element_type | solution.py:202
  15.7 1.8 %collective-permute-start.18 = (bf16[2,128,128]{2,1,0:T(8,128)(2,1)S(1)}, bf16[2,128,128]{2,1,0:T(8,128)(2,1)S(1)}, u32[]{:S(2)}, u32[]{:S(2)}) collective-permute-start(bf16[2,128,128]{2,1,0:T(8,128)(2,1)S(1)} %multiply_convert_fusion), channel_id=1, source_target_pairs={{0,4},{1,5},{2,6},{3,7},{4,0},{5,1},{6,2},{7,3},{8,12},{9,13},{10,... | collective-permute-start | bytes 196616 | tf_op jit(solution)/shard_map/ppermute | solution.py:172
  17.5 0.4 collective-permute-start
  17.9 2.5 %collective-permute-done.18 = bf16[2,128,128]{2,1,0:T(8,128)(2,1)S(1)} collective-permute-done((bf16[2,128,128]{2,1,0:T(8,128)(2,1)S(1)}, bf16[2,128,128]{2,1,0:T(8,128)(2,1)S(1)}, u32[]{:S(2)}, u32[]{:S(2)}) %collective-permute-start.18) | collective-permute-done | bytes 65568 | tf_op jit(solution)/shard_map/ppermute | solution.py:172
  20.4 2.7 %collective-permute-start.19 = (bf16[2,128,128]{2,1,0:T(8,128)(2,1)S(1)}, bf16[2,128,128]{2,1,0:T(8,128)(2,1)S(1)}, u32[]{:S(2)}, u32[]{:S(2)}) collective-permute-start(bf16[2,128,128]{2,1,0:T(8,128)(2,1)S(1)} %add_convert_fusion.4), channel_id=1, source_target_pairs={{0,8},{1,9},{2,10},{3,11},{4,12},{5,13},{6,14},{7,15},{8,0},{9,1},... | collective-permute-start | bytes 196616 | tf_op jit(solution)/shard_map/ppermute | solution.py:172
  23.1 0.5 collective-permute-done.refs_1_
  23.6 3.3 %collective-permute-start.1 = (bf16[592,128]{1,0:T(8,128)(2,1)S(1)}, bf16[592,128]{1,0:T(8,128)(2,1)S(1)}, u32[]{:S(2)}, u32[]{:S(2)}) collective-permute-start(bf16[592,128]{1,0:T(8,128)(2,1)S(1)} %pad_maximum_fusion.refs_0_), channel_id=1, source_target_pairs={{0,8},{1,9},{2,10},{3,11},{4,12},{5,13},{6,14},{7,15},{8,0},{9,1},... | collective-permute-start | bytes 454664 | tf_op jit(solution)/shard_map/ppermute | solution.py:172
  26.9 0.0 collective-permute-done.19
  26.9 3.0 %collective-permute-start.2 = (bf16[592,128]{1,0:T(8,128)(2,1)S(1)}, bf16[592,128]{1,0:T(8,128)(2,1)S(1)}, u32[]{:S(2)}, u32[]{:S(2)}) collective-permute-start(bf16[592,128]{1,0:T(8,128)(2,1)S(1)} %pad_maximum_fusion.refs_0_), channel_id=1, source_target_pairs={{0,12},{1,13},{2,14},{3,15},{4,8},{5,9},{6,10},{7,11},{8,4},{9,5},... | collective-permute-start | bytes 454664 | tf_op jit(solution)/shard_map/ppermute | solution.py:172
  30.0 7.7 %collective-permute-done.1.refs_2_ = bf16[592,128]{1,0:T(8,128)(2,1)S(1)} collective-permute-done((bf16[592,128]{1,0:T(8,128)(2,1)S(1)}, bf16[592,128]{1,0:T(8,128)(2,1)S(1)}, u32[]{:S(2)}, u32[]{:S(2)}) %collective-permute-start.1) | collective-permute-done | bytes 151584 | tf_op jit(solution)/shard_map/ppermute | solution.py:172
  37.7 1.5 %collective-permute-start.20 = (bf16[2,128,128]{2,1,0:T(8,128)(2,1)S(1)}, bf16[2,128,128]{2,1,0:T(8,128)(2,1)S(1)}, u32[]{:S(2)}, u32[]{:S(2)}) collective-permute-start(bf16[2,128,128]{2,1,0:T(8,128)(2,1)S(1)} %add_convert_fusion.3), channel_id=1, source_target_pairs={{0,16},{16,0},{1,17},{17,1},{2,18},{18,2},{3,19},{19,3},{4,20},{20... | collective-permute-start | bytes 196616 | tf_op jit(solution)/shard_map/ppermute | solution.py:206
  39.2 0.0 collective-permute-done.2.refs_3_
  39.2 0.0 collective-permute-done.3.refs_5_.refs_1_
  39.2 0.0 collective-permute-done.4.refs_6_.refs_2_
  39.3 0.0 collective-permute-done.5.refs_7_.refs_3_
  39.3 0.6 copy-done.8
  39.9 0.2 copy-done.2
  40.1 0.1 copy-done.3
  40.2 0.1 copy-done.4
  40.3 4.4 %scores.1 = (f32[512,1024]{1,0:T(8,128)}, bf16[512,640]{1,0:T(8,128)(2,1)}, f32[16,128]{1,0:T(8,128)}) custom-call(bf16[592,128]{1,0:T(8,128)(2,1)} %copy-done.1, bf16[592,128]{1,0:T(8,128)(2,1)} %copy-done.6, bf16[592,128]{1,0:T(8,128)(2,1)} %copy-done.7, bf16[592,128]{1,0:T(8,128)(2,1)} %copy-done.8, bf16[1424,128]{1,0:T(8,128)(2,1)} %copy-done, ...), custom_call_target="tpu_custom_call" | custom-call | flops 671088640 | bytes 4718592 | tf_op jit(solution)/shard_map/scores/pallas_call | solution.py:32
  44.7 0.0 collective-permute-start.6
  44.7 1.4 %collective-permute-start.7 = (f32[16,128]{1,0:T(8,128)}, f32[16,128]{1,0:T(8,128)S(1)}, u32[]{:S(2)}, u32[]{:S(2)}) collective-permute-start(f32[16,128]{1,0:T(8,128)} %get-tuple-element.22.refs_8_), channel_id=1, source_target_pairs={{0,2},{1,3},{2,0},{3,1},{4,6},{5,7},{6,4},{7,5},{8,10},{9,11},{10,... | collective-permute-start | bytes 24584 | tf_op jit(solution)/shard_map/ppermute | solution.py:172
  46.1 0.4 collective-permute-start.8
  46.5 4.1 %context_grads.1 = (bf16[512,1024]{1,0:T(8,128)(2,1)}, f32[512,1024]{1,0:T(8,128)}) custom-call(bf16[1424,128]{1,0:T(8,128)(2,1)} %copy-done, bf16[1424,128]{1,0:T(8,128)(2,1)} %copy-done.2, bf16[1424,128]{1,0:T(8,128)(2,1)} %copy-done.3, bf16[1424,128]{1,0:T(8,128)(2,1)} %copy-done.4, bf16[512,640]{1,0:T(8,128)(2,1)} %get-tuple-element.24.refs_4_, ...), custom_call_target="tpu_custom_call" | custom-call | flops 671088640 | bytes 5111808 | tf_op jit(solution)/shard_map/context_grads/pallas_call | solution.py:32
  50.7 0.0 collective-permute-done.6.refs_9_
  50.7 0.0 collective-permute-done.7.refs_10_
  50.7 0.6 copy-done.13
  51.3 0.0 copy-done.14
  51.3 0.0 copy-done.15
  51.3 7.1 %gradients.1 = (bf16[2,576,128]{2,1,0:T(8,128)(2,1)}, bf16[2,576,128]{2,1,0:T(8,128)(2,1)}, bf16[2,576,128]{2,1,0:T(8,128)(2,1)}, bf16[2,576,128]{2,1,0:T(8,128)...) custom-call(bf16[592,128]{1,0:T(8,128)(2,1)} %copy-done.1, ...), custom_call_target="tpu_custom_call" | custom-call | flops 1744830464 | bytes 8781824 | tf_op jit(solution)/shard_map/gradients/pallas_call | solution.py:32
  58.4 2.1 %collective-permute-start.14 = (bf16[576,128]{1,0:T(8,128)(2,1)}, bf16[576,128]{1,0:T(8,128)(2,1)S(1)}, u32[]{:S(2)}, u32[]{:S(2)}) collective-permute-start(bf16[576,128]{1,0:T(8,128)(2,1)} %get-tuple-element.34), channel_id=1, source_target_pairs={{0,12},{1,13},{2,14},{3,15},{4,8},{5,9},{6,10},{7,11},{8,4},{9,5},... | collective-permute-start | bytes 442376 | tf_op jit(solution)/shard_map/ppermute | solution.py:172
  60.5 0.0 collective-permute-done.20
  60.5 0.1 collective-permute-start.21
  60.6 1.1 %collective-permute-start.13 = (bf16[576,128]{1,0:T(8,128)(2,1)}, bf16[576,128]{1,0:T(8,128)(2,1)S(1)}, u32[]{:S(2)}, u32[]{:S(2)}) collective-permute-start(bf16[576,128]{1,0:T(8,128)(2,1)} %get-tuple-element.33), channel_id=1, source_target_pairs={{0,8},{1,9},{2,10},{3,11},{4,12},{5,13},{6,14},{7,15},{8,0},{9,1},... | collective-permute-start | bytes 442376 | tf_op jit(solution)/shard_map/ppermute | solution.py:172
  61.7 1.3 %collective-permute-start.12 = (bf16[576,128]{1,0:T(8,128)(2,1)}, bf16[576,128]{1,0:T(8,128)(2,1)S(1)}, u32[]{:S(2)}, u32[]{:S(2)}) collective-permute-start(bf16[576,128]{1,0:T(8,128)(2,1)} %get-tuple-element.32), channel_id=1, source_target_pairs={{0,4},{1,5},{2,6},{3,7},{4,0},{5,1},{6,2},{7,3},{8,12},{9,13},{10,... | collective-permute-start | bytes 442376 | tf_op jit(solution)/shard_map/ppermute | solution.py:172
  63.0 1.4 %collective-permute-start.22 = (bf16[2,128,128]{2,1,0:T(8,128)(2,1)S(1)}, bf16[2,128,128]{2,1,0:T(8,128)(2,1)S(1)}, u32[]{:S(2)}, u32[]{:S(2)}) collective-permute-start(bf16[2,128,128]{2,1,0:T(8,128)(2,1)S(1)} %add_convert_fusion.2.refs_0_), channel_id=1, source_target_pairs={{0,2},{1,3},{2,0},{3,1},{4,6},{5,7},{6,4},{7,5},{8,10},{9,11},{10,... | collective-permute-start | bytes 196616 | tf_op jit(solution)/shard_map/ppermute | solution.py:172
  64.4 0.0 collective-permute-start.23
  64.4 2.8 %collective-permute-done.22.refs_2_ = bf16[2,128,128]{2,1,0:T(8,128)(2,1)S(1)} collective-permute-done((bf16[2,128,128]{2,1,0:T(8,128)(2,1)S(1)}, bf16[2,128,128]{2,1,0:T(8,128)(2,1)S(1)}, u32[]{:S(2)}, u32[]{:S(2)}) %collective-permute-start.22) | collective-permute-done | bytes 65568 | tf_op jit(solution)/shard_map/ppermute | solution.py:172
  67.2 0.1 collective-permute-start.11
  67.3 1.3 %collective-permute-done.23.refs_3_ = bf16[2,128,128]{2,1,0:T(8,128)(2,1)S(1)} collective-permute-done((bf16[2,128,128]{2,1,0:T(8,128)(2,1)S(1)}, bf16[2,128,128]{2,1,0:T(8,128)(2,1)S(1)}, u32[]{:S(2)}, u32[]{:S(2)}) %collective-permute-start.23) | collective-permute-done | bytes 65568 | tf_op jit(solution)/shard_map/ppermute | solution.py:172
  68.6 0.8 collective-permute-start.10
  69.4 0.0 collective-permute-done.14
  69.4 0.5 collective-permute-start.9
  69.9 1.8 %spread.1 = f32[2,512,128]{2,1,0:T(8,128)} custom-call(s32[1]{0:T(128)} %bitcast.8.idx_ref, bf16[2,128,128]{2,1,0:T(8,128)(2,1)} %copy-done.5, bf16[2,128,128]{2,1,0:T(8,128)(2,1)} %copy-done.10, bf16[2,128,128]{2,1,0:T(8,128)(2,1)} %copy-done.11, bf16[2,128,128]{2,1,0:T(8,128)(2,1)} %copy-done.12), custom_call_target="tpu_custom_call" | custom-call | tf_op jit(solution)/shard_map/spread/pallas_call | solution.py:32
  71.7 3.6 %collective-permute-done.13 = bf16[576,128]{1,0:T(8,128)(2,1)S(1)} collective-permute-done((bf16[576,128]{1,0:T(8,128)(2,1)}, bf16[576,128]{1,0:T(8,128)(2,1)S(1)}, u32[]{:S(2)}, u32[]{:S(2)}) %collective-permute-start.13) | collective-permute-done | bytes 147488 | tf_op jit(solution)/shard_map/ppermute | solution.py:172
  75.3 0.0 collective-permute-done.12
  75.3 1.7 %fusion.1 = bf16[1,128,576]{1,2,0:T(8,128)(2,1)} fusion(bf16[576,128]{1,0:T(8,128)(2,1)S(1)} %collective-permute-done.14, bf16[576,128]{1,0:T(8,128)(2,1)S(1)} %collective-permute-done.13, bf16[576,128]{1,0:T(8,128)(2,1)S(1)} %collective-permute-done.12, bf16[576,128]{1,0:T(8,128)(2,1)} %get-tuple-element.31), kind=kLoop, calls=%fused_computation.4 | loop fusion | flops 589824 | bytes 737280 | tf_op jit(solution)/shard_map/broadcast_in_dim | solution.py:250
  76.9 6.2 %collective-permute-done.10 = bf16[2,576,128]{2,1,0:T(8,128)(2,1)S(1)} collective-permute-done((bf16[2,576,128]{2,1,0:T(8,128)(2,1)}, bf16[2,576,128]{2,1,0:T(8,128)(2,1)S(1)}, u32[]{:S(2)}, u32[]{:S(2)}) %collective-permute-start.10) | collective-permute-done | bytes 294944 | tf_op jit(solution)/shard_map/ppermute | solution.py:172
  83.1 1.8 %fusion = bf16[1,128,2,576]{1,3,2,0:T(8,128)(2,1)} fusion(bf16[2,576,128]{2,1,0:T(8,128)(2,1)S(1)} %collective-permute-done.11, bf16[2,576,128]{2,1,0:T(8,128)(2,1)S(1)} %collective-permute-done.10, bf16[2,576,128]{2,1,0:T(8,128)(2,1)S(1)} %collective-permute-done.9, bf16[2,576,128]{2,1,0:T(8,128)(2,1)} %get-tuple-element.27), kind=kLoop, calls=%fused_computation.1 | loop fusion | flops 1179648 | bytes 1474560 | tf_op jit(solution)/shard_map/broadcast_in_dim | solution.py:250
  (33 shorter events, 0.1 us)
Async XLA Ops:
  0.6 16.8 %copy-start.9 = (bf16[1,128,576]{1,2,0:T(8,128)(2,1)S(1)}, bf16[1,128,576]{1,2,0:T(8,128)(2,1)}, u32[]{:S(2)}) copy-start(bf16[1,128,576]{1,2,0:T(8,128)(2,1)} %param.8) | copy-start | bytes 442372
  6.2 8.6 %collective-permute-start.17 = (bf16[2,128,128]{2,1,0:T(8,128)(2,1)}, bf16[2,128,128]{2,1,0:T(8,128)(2,1)S(1)}, u32[]{:S(2)}, u32[]{:S(2)}) collective-permute-start(bf16[2,128,128]{2,1,0:T(8,128)(2,1)} %get-tuple-element.38), channel_id=1, source_target_pairs={{0,3},{1,2},{2,1},{3,0},{4,7},{5,6},{6,5},{7,4},{8,11},{9,10},{10,... | collective-permute-start | bytes 196616 | tf_op jit(solution)/shard_map/ppermute | solution.py:172
  8.6 6.2 %collective-permute-start.16 = (bf16[2,128,128]{2,1,0:T(8,128)(2,1)}, bf16[2,128,128]{2,1,0:T(8,128)(2,1)S(1)}, u32[]{:S(2)}, u32[]{:S(2)}) collective-permute-start(bf16[2,128,128]{2,1,0:T(8,128)(2,1)} %get-tuple-element.37), channel_id=1, source_target_pairs={{0,2},{1,3},{2,0},{3,1},{4,6},{5,7},{6,4},{7,5},{8,10},{9,11},{10,... | collective-permute-start | bytes 196616 | tf_op jit(solution)/shard_map/ppermute | solution.py:172
  9.2 5.6 %collective-permute-start.15 = (bf16[2,128,128]{2,1,0:T(8,128)(2,1)}, bf16[2,128,128]{2,1,0:T(8,128)(2,1)S(1)}, u32[]{:S(2)}, u32[]{:S(2)}) collective-permute-start(bf16[2,128,128]{2,1,0:T(8,128)(2,1)} %get-tuple-element.36), channel_id=1, source_target_pairs={{0,1},{1,0},{2,3},{3,2},{4,5},{5,4},{6,7},{7,6},{8,9},{9,8},{10,11... | collective-permute-start | bytes 196616 | tf_op jit(solution)/shard_map/ppermute | solution.py:172
  12.8 26.5 %copy-start = (bf16[1424,128]{1,0:T(8,128)(2,1)}, bf16[1424,128]{1,0:T(8,128)(2,1)S(1)}, u32[]{:S(2)}) copy-start(bf16[1424,128]{1,0:T(8,128)(2,1)S(1)} %concatenate.11.refs_4_.refs_0_) | copy-start | bytes 1093636
  12.8 26.4 %collective-permute-start.3 = (bf16[1424,128]{1,0:T(8,128)(2,1)S(1)}, bf16[1424,128]{1,0:T(8,128)(2,1)S(1)}, u32[]{:S(2)}, u32[]{:S(2)}) collective-permute-start(bf16[1424,128]{1,0:T(8,128)(2,1)S(1)} %concatenate.11.refs_4_.refs_0_), channel_id=1, source_target_pairs={{0,1},{1,0},{2,3},{3,2},{4,5},{5,4},{6,7},{7,6},{8,9},{9,8},{10,11... | collective-permute-start | bytes 1093640 | tf_op jit(solution)/shard_map/ppermute | solution.py:172
  13.3 26.0 %collective-permute-start.4 = (bf16[1424,128]{1,0:T(8,128)(2,1)S(1)}, bf16[1424,128]{1,0:T(8,128)(2,1)S(1)}, u32[]{:S(2)}, u32[]{:S(2)}) collective-permute-start(bf16[1424,128]{1,0:T(8,128)(2,1)S(1)} %concatenate.11.refs_4_.refs_0_), channel_id=1, source_target_pairs={{0,2},{1,3},{2,0},{3,1},{4,6},{5,7},{6,4},{7,5},{8,10},{9,11},{10,... | collective-permute-start | bytes 1093640 | tf_op jit(solution)/shard_map/ppermute | solution.py:172
  14.7 24.5 %collective-permute-start.5 = (bf16[1424,128]{1,0:T(8,128)(2,1)S(1)}, bf16[1424,128]{1,0:T(8,128)(2,1)S(1)}, u32[]{:S(2)}, u32[]{:S(2)}) collective-permute-start(bf16[1424,128]{1,0:T(8,128)(2,1)S(1)} %concatenate.11.refs_4_.refs_0_), channel_id=1, source_target_pairs={{0,3},{1,2},{2,1},{3,0},{4,7},{5,6},{6,5},{7,4},{8,11},{9,10},{10,... | collective-permute-start | bytes 1093640 | tf_op jit(solution)/shard_map/ppermute | solution.py:172
  15.7 4.7 %collective-permute-start.18 = (bf16[2,128,128]{2,1,0:T(8,128)(2,1)S(1)}, bf16[2,128,128]{2,1,0:T(8,128)(2,1)S(1)}, u32[]{:S(2)}, u32[]{:S(2)}) collective-permute-start(bf16[2,128,128]{2,1,0:T(8,128)(2,1)S(1)} %multiply_convert_fusion), channel_id=1, source_target_pairs={{0,4},{1,5},{2,6},{3,7},{4,0},{5,1},{6,2},{7,3},{8,12},{9,13},{10,... | collective-permute-start | bytes 196616 | tf_op jit(solution)/shard_map/ppermute | solution.py:172
  17.5 21.8 %copy-start.1 = (bf16[592,128]{1,0:T(8,128)(2,1)}, bf16[592,128]{1,0:T(8,128)(2,1)S(1)}, u32[]{:S(2)}) copy-start(bf16[592,128]{1,0:T(8,128)(2,1)S(1)} %pad_maximum_fusion.refs_0_) | copy-start | bytes 454660
  17.5 6.1 %collective-permute-start = (bf16[592,128]{1,0:T(8,128)(2,1)S(1)}, bf16[592,128]{1,0:T(8,128)(2,1)S(1)}, u32[]{:S(2)}, u32[]{:S(2)}) collective-permute-start(bf16[592,128]{1,0:T(8,128)(2,1)S(1)} %pad_maximum_fusion.refs_0_), channel_id=1, source_target_pairs={{0,4},{1,5},{2,6},{3,7},{4,0},{5,1},{6,2},{7,3},{8,12},{9,13},{10,... | collective-permute-start | bytes 454664 | tf_op jit(solution)/shard_map/ppermute | solution.py:172
  20.4 6.5 %collective-permute-start.19 = (bf16[2,128,128]{2,1,0:T(8,128)(2,1)S(1)}, bf16[2,128,128]{2,1,0:T(8,128)(2,1)S(1)}, u32[]{:S(2)}, u32[]{:S(2)}) collective-permute-start(bf16[2,128,128]{2,1,0:T(8,128)(2,1)S(1)} %add_convert_fusion.4), channel_id=1, source_target_pairs={{0,8},{1,9},{2,10},{3,11},{4,12},{5,13},{6,14},{7,15},{8,0},{9,1},... | collective-permute-start | bytes 196616 | tf_op jit(solution)/shard_map/ppermute | solution.py:172
  23.6 15.7 %copy-start.6 = (bf16[592,128]{1,0:T(8,128)(2,1)}, bf16[592,128]{1,0:T(8,128)(2,1)S(1)}, u32[]{:S(2)}) copy-start(bf16[592,128]{1,0:T(8,128)(2,1)S(1)} %collective-permute-done.refs_1_) | copy-start | bytes 454660
  23.6 14.1 %collective-permute-start.1 = (bf16[592,128]{1,0:T(8,128)(2,1)S(1)}, bf16[592,128]{1,0:T(8,128)(2,1)S(1)}, u32[]{:S(2)}, u32[]{:S(2)}) collective-permute-start(bf16[592,128]{1,0:T(8,128)(2,1)S(1)} %pad_maximum_fusion.refs_0_), channel_id=1, source_target_pairs={{0,8},{1,9},{2,10},{3,11},{4,12},{5,13},{6,14},{7,15},{8,0},{9,1},... | collective-permute-start | bytes 454664 | tf_op jit(solution)/shard_map/ppermute | solution.py:172
  26.9 12.3 %collective-permute-start.2 = (bf16[592,128]{1,0:T(8,128)(2,1)S(1)}, bf16[592,128]{1,0:T(8,128)(2,1)S(1)}, u32[]{:S(2)}, u32[]{:S(2)}) collective-permute-start(bf16[592,128]{1,0:T(8,128)(2,1)S(1)} %pad_maximum_fusion.refs_0_), channel_id=1, source_target_pairs={{0,12},{1,13},{2,14},{3,15},{4,8},{5,9},{6,10},{7,11},{8,4},{9,5},... | collective-permute-start | bytes 454664 | tf_op jit(solution)/shard_map/ppermute | solution.py:172
  37.7 1.6 %copy-start.7 = (bf16[592,128]{1,0:T(8,128)(2,1)}, bf16[592,128]{1,0:T(8,128)(2,1)S(1)}, u32[]{:S(2)}) copy-start(bf16[592,128]{1,0:T(8,128)(2,1)S(1)} %collective-permute-done.1.refs_2_) | copy-start | bytes 454660
  37.7 22.8 %collective-permute-start.20 = (bf16[2,128,128]{2,1,0:T(8,128)(2,1)S(1)}, bf16[2,128,128]{2,1,0:T(8,128)(2,1)S(1)}, u32[]{:S(2)}, u32[]{:S(2)}) collective-permute-start(bf16[2,128,128]{2,1,0:T(8,128)(2,1)S(1)} %add_convert_fusion.3), channel_id=1, source_target_pairs={{0,16},{16,0},{1,17},{17,1},{2,18},{18,2},{3,19},{19,3},{4,20},{20... | collective-permute-start | bytes 196616 | tf_op jit(solution)/shard_map/ppermute | solution.py:206
  39.2 0.7 copy-start.8
  39.2 0.8 copy-start.2
  39.3 0.9 %copy-start.3 = (bf16[1424,128]{1,0:T(8,128)(2,1)}, bf16[1424,128]{1,0:T(8,128)(2,1)S(1)}, u32[]{:S(2)}) copy-start(bf16[1424,128]{1,0:T(8,128)(2,1)S(1)} %collective-permute-done.4.refs_6_.refs_2_) | copy-start | bytes 1093636
  39.3 1.0 %copy-start.4 = (bf16[1424,128]{1,0:T(8,128)(2,1)}, bf16[1424,128]{1,0:T(8,128)(2,1)S(1)}, u32[]{:S(2)}) copy-start(bf16[1424,128]{1,0:T(8,128)(2,1)S(1)} %collective-permute-done.5.refs_7_.refs_3_) | copy-start | bytes 1093636
  44.7 6.0 %collective-permute-start.6 = (f32[16,128]{1,0:T(8,128)}, f32[16,128]{1,0:T(8,128)S(1)}, u32[]{:S(2)}, u32[]{:S(2)}) collective-permute-start(f32[16,128]{1,0:T(8,128)} %get-tuple-element.22.refs_8_), channel_id=1, source_target_pairs={{0,1},{1,0},{2,3},{3,2},{4,5},{5,4},{6,7},{7,6},{8,9},{9,8},{10,11... | collective-permute-start | bytes 24584 | tf_op jit(solution)/shard_map/ppermute | solution.py:172
  44.7 6.0 %collective-permute-start.7 = (f32[16,128]{1,0:T(8,128)}, f32[16,128]{1,0:T(8,128)S(1)}, u32[]{:S(2)}, u32[]{:S(2)}) collective-permute-start(f32[16,128]{1,0:T(8,128)} %get-tuple-element.22.refs_8_), channel_id=1, source_target_pairs={{0,2},{1,3},{2,0},{3,1},{4,6},{5,7},{6,4},{7,5},{8,10},{9,11},{10,... | collective-permute-start | bytes 24584 | tf_op jit(solution)/shard_map/ppermute | solution.py:172
  46.1 4.6 %collective-permute-start.8 = (f32[16,128]{1,0:T(8,128)}, f32[16,128]{1,0:T(8,128)S(1)}, u32[]{:S(2)}, u32[]{:S(2)}) collective-permute-start(f32[16,128]{1,0:T(8,128)} %get-tuple-element.22.refs_8_), channel_id=1, source_target_pairs={{0,3},{1,2},{2,1},{3,0},{4,7},{5,6},{6,5},{7,4},{8,11},{9,10},{10,... | collective-permute-start | bytes 24584 | tf_op jit(solution)/shard_map/ppermute | solution.py:172
  50.7 0.6 copy-start.13
  50.7 0.6 copy-start.14
  50.7 0.6 copy-start.15
  58.4 11.0 %collective-permute-start.14 = (bf16[576,128]{1,0:T(8,128)(2,1)}, bf16[576,128]{1,0:T(8,128)(2,1)S(1)}, u32[]{:S(2)}, u32[]{:S(2)}) collective-permute-start(bf16[576,128]{1,0:T(8,128)(2,1)} %get-tuple-element.34), channel_id=1, source_target_pairs={{0,12},{1,13},{2,14},{3,15},{4,8},{5,9},{6,10},{7,11},{8,4},{9,5},... | collective-permute-start | bytes 442376 | tf_op jit(solution)/shard_map/ppermute | solution.py:172
  60.5 9.4 %copy-start.5 = (bf16[2,128,128]{2,1,0:T(8,128)(2,1)}, bf16[2,128,128]{2,1,0:T(8,128)(2,1)S(1)}, u32[]{:S(2)}) copy-start(bf16[2,128,128]{2,1,0:T(8,128)(2,1)S(1)} %add_convert_fusion.2.refs_0_) | copy-start | bytes 196612
  60.5 3.9 %collective-permute-start.21 = (bf16[2,128,128]{2,1,0:T(8,128)(2,1)S(1)}, bf16[2,128,128]{2,1,0:T(8,128)(2,1)S(1)}, u32[]{:S(2)}, u32[]{:S(2)}) collective-permute-start(bf16[2,128,128]{2,1,0:T(8,128)(2,1)S(1)} %add_convert_fusion.2.refs_0_), channel_id=1, source_target_pairs={{0,1},{1,0},{2,3},{3,2},{4,5},{5,4},{6,7},{7,6},{8,9},{9,8},{10,11... | collective-permute-start | bytes 196616 | tf_op jit(solution)/shard_map/ppermute | solution.py:172
  60.6 14.6 %collective-permute-start.13 = (bf16[576,128]{1,0:T(8,128)(2,1)}, bf16[576,128]{1,0:T(8,128)(2,1)S(1)}, u32[]{:S(2)}, u32[]{:S(2)}) collective-permute-start(bf16[576,128]{1,0:T(8,128)(2,1)} %get-tuple-element.33), channel_id=1, source_target_pairs={{0,8},{1,9},{2,10},{3,11},{4,12},{5,13},{6,14},{7,15},{8,0},{9,1},... | collective-permute-start | bytes 442376 | tf_op jit(solution)/shard_map/ppermute | solution.py:172
  61.7 13.6 %collective-permute-start.12 = (bf16[576,128]{1,0:T(8,128)(2,1)}, bf16[576,128]{1,0:T(8,128)(2,1)S(1)}, u32[]{:S(2)}, u32[]{:S(2)}) collective-permute-start(bf16[576,128]{1,0:T(8,128)(2,1)} %get-tuple-element.32), channel_id=1, source_target_pairs={{0,4},{1,5},{2,6},{3,7},{4,0},{5,1},{6,2},{7,3},{8,12},{9,13},{10,... | collective-permute-start | bytes 442376 | tf_op jit(solution)/shard_map/ppermute | solution.py:172
  63.0 4.3 %collective-permute-start.22 = (bf16[2,128,128]{2,1,0:T(8,128)(2,1)S(1)}, bf16[2,128,128]{2,1,0:T(8,128)(2,1)S(1)}, u32[]{:S(2)}, u32[]{:S(2)}) collective-permute-start(bf16[2,128,128]{2,1,0:T(8,128)(2,1)S(1)} %add_convert_fusion.2.refs_0_), channel_id=1, source_target_pairs={{0,2},{1,3},{2,0},{3,1},{4,6},{5,7},{6,4},{7,5},{8,10},{9,11},{10,... | collective-permute-start | bytes 196616 | tf_op jit(solution)/shard_map/ppermute | solution.py:172
  64.4 5.5 %copy-start.10 = (bf16[2,128,128]{2,1,0:T(8,128)(2,1)}, bf16[2,128,128]{2,1,0:T(8,128)(2,1)S(1)}, u32[]{:S(2)}) copy-start(bf16[2,128,128]{2,1,0:T(8,128)(2,1)S(1)} %collective-permute-done.21.refs_1_) | copy-start | bytes 196612
  64.4 4.2 %collective-permute-start.23 = (bf16[2,128,128]{2,1,0:T(8,128)(2,1)S(1)}, bf16[2,128,128]{2,1,0:T(8,128)(2,1)S(1)}, u32[]{:S(2)}, u32[]{:S(2)}) collective-permute-start(bf16[2,128,128]{2,1,0:T(8,128)(2,1)S(1)} %add_convert_fusion.2.refs_0_), channel_id=1, source_target_pairs={{0,3},{1,2},{2,1},{3,0},{4,7},{5,6},{6,5},{7,4},{8,11},{9,10},{10,... | collective-permute-start | bytes 196616 | tf_op jit(solution)/shard_map/ppermute | solution.py:172
  67.2 2.7 %copy-start.11 = (bf16[2,128,128]{2,1,0:T(8,128)(2,1)}, bf16[2,128,128]{2,1,0:T(8,128)(2,1)S(1)}, u32[]{:S(2)}) copy-start(bf16[2,128,128]{2,1,0:T(8,128)(2,1)S(1)} %collective-permute-done.22.refs_2_) | copy-start | bytes 196612
  67.2 9.7 %collective-permute-start.11 = (bf16[2,576,128]{2,1,0:T(8,128)(2,1)}, bf16[2,576,128]{2,1,0:T(8,128)(2,1)S(1)}, u32[]{:S(2)}, u32[]{:S(2)}) collective-permute-start(bf16[2,576,128]{2,1,0:T(8,128)(2,1)} %get-tuple-element.30), channel_id=1, source_target_pairs={{0,3},{1,2},{2,1},{3,0},{4,7},{5,6},{6,5},{7,4},{8,11},{9,10},{10,... | collective-permute-start | bytes 884744 | tf_op jit(solution)/shard_map/ppermute | solution.py:172
  68.6 1.3 %copy-start.12 = (bf16[2,128,128]{2,1,0:T(8,128)(2,1)}, bf16[2,128,128]{2,1,0:T(8,128)(2,1)S(1)}, u32[]{:S(2)}) copy-start(bf16[2,128,128]{2,1,0:T(8,128)(2,1)S(1)} %collective-permute-done.23.refs_3_) | copy-start | bytes 196612
  68.6 14.4 %collective-permute-start.10 = (bf16[2,576,128]{2,1,0:T(8,128)(2,1)}, bf16[2,576,128]{2,1,0:T(8,128)(2,1)S(1)}, u32[]{:S(2)}, u32[]{:S(2)}) collective-permute-start(bf16[2,576,128]{2,1,0:T(8,128)(2,1)} %get-tuple-element.29), channel_id=1, source_target_pairs={{0,2},{1,3},{2,0},{3,1},{4,6},{5,7},{6,4},{7,5},{8,10},{9,11},{10,... | collective-permute-start | bytes 884744 | tf_op jit(solution)/shard_map/ppermute | solution.py:172
  69.4 13.6 %collective-permute-start.9 = (bf16[2,576,128]{2,1,0:T(8,128)(2,1)}, bf16[2,576,128]{2,1,0:T(8,128)(2,1)S(1)}, u32[]{:S(2)}, u32[]{:S(2)}) collective-permute-start(bf16[2,576,128]{2,1,0:T(8,128)(2,1)} %get-tuple-element.28), channel_id=1, source_target_pairs={{0,1},{1,0},{2,3},{3,2},{4,5},{5,4},{6,7},{7,6},{8,9},{9,8},{10,11... | collective-permute-start | bytes 884744 | tf_op jit(solution)/shard_map/ppermute | solution.py:172

commit v2 on v1

v2 whole, which is shorter than its diff:
```python
import functools
import math

import jax
import jax.numpy as jnp
from jax import lax
from jax.experimental import pallas as pl
from jax.experimental.pallas import tpu as pltpu
from jax.sharding import PartitionSpec as P

ROPE = 64
HEAD_DIM = 128
GROUP = 4
EXTRA = 16
F32 = jnp.float32
BF16 = jnp.bfloat16


def mm(a, b):
    return jnp.dot(a, b, preferred_element_type=F32)


def mm_t(a, b):
    return lax.dot_general(a, b, (((1,), (1,)), ((), ())), preferred_element_type=F32)


def size_of(shape, dtype):
    return math.prod(shape) * jnp.dtype(dtype).itemsize


def call(kernel, name, outs, args, scratch=(), flops=0, smem=()):
    specs = [
        pl.BlockSpec(memory_space=pltpu.SMEM if i in smem else pltpu.VMEM) for i in range(len(args))
    ]
    moved = sum(size_of(a.shape, a.dtype) for a in args) + sum(size_of(*o) for o in outs)
    held = moved + sum(size_of(*s) for s in scratch)
    return pl.pallas_call(
        kernel,
        out_shape=[jax.ShapeDtypeStruct(s, d) for s, d in outs],
        in_specs=specs,
        out_specs=[pl.BlockSpec(memory_space=pltpu.VMEM) for _ in outs],
        scratch_shapes=[pltpu.VMEM(s, d) for s, d in scratch],
        compiler_params=pltpu.CompilerParams(vmem_limit_bytes=int(1.2 * held) + (8 << 20)),
        cost_estimate=pl.CostEstimate(flops=flops, bytes_accessed=moved, transcendentals=0),
        name=name,
    )(*args)


def pack_kernel(pos_ref, q_ref, og_ref, lat_ref, lat_msg_ref, msg_ref):
    heads, width, tok = q_ref.shape
    lat_msg_ref[:width, :] = lat_ref[...]
    lat_msg_ref[width:, :] = pos_ref[...]
    for h in range(heads):
        msg_ref[h * width : (h + 1) * width, :] = q_ref[h]
        at = heads * width + h * HEAD_DIM
        msg_ref[at : at + HEAD_DIM, :] = og_ref[:, h, :].T
    msg_ref[heads * (width + HEAD_DIM) :, :] = pos_ref[...]


def own_kernel(width, idx_ref, attn_ref, msg_ref, wuv_ref, delta_ref, *rest):
    chunks, term = rest[:GROUP], rest[GROUP]
    heads, lat, _ = wuv_ref.shape
    delta_ref[...] = jnp.zeros_like(delta_ref)
    for h in range(heads):
        at = heads * width + h * HEAD_DIM
        og = msg_ref[at : at + HEAD_DIM, :]
        attn = attn_ref[:, h, :].T
        g = mm(wuv_ref[h], og).astype(BF16).astype(F32)
        delta_ref[h : h + 1, :] = jnp.sum(g * attn.astype(F32), axis=0, keepdims=True)
        term[h] = mm_t(attn, og)
    step = lat // GROUP
    me = lax.rem(idx_ref[0], GROUP)
    for k in range(GROUP):
        at = pl.multiple_of(jnp.bitwise_xor(me, k) * step, step)
        chunks[k][...] = term[:, pl.ds(at, step), :].astype(BF16)


def score_kernel(factor, nkey, width, heads, *refs):
    lat_refs = refs[:nkey]
    q_refs = refs[nkey : nkey + GROUP]
    delta_ref, s_ref, k_ref, stat_ref, kt, qt = refs[nkey + GROUP :]
    wide = kt.shape[0]
    tok = lat_refs[0].shape[1]
    rows = heads * tok
    for a in range(nkey):
        kt[: width + EXTRA, a * tok : (a + 1) * tok] = lat_refs[a][...]
    kt[width + EXTRA :, :] = jnp.zeros((wide - width - EXTRA, nkey * tok), BF16)
    k_ref[...] = kt[...].T
    pos = k_ref[:, wide - 128 :].astype(F32)
    at = width - (wide - 128)
    key_pos = pos[:, at : at + 1] * 64.0 + pos[:, at + 1 : at + 2]
    qt[width:, :] = jnp.zeros((wide - width, rows), BF16)
    stat_ref[...] = jnp.zeros_like(stat_ref)
    stat_ref[GROUP * heads : GROUP * heads + heads, :] = delta_ref[:heads, :]
    for j in range(GROUP):
        q_ref = q_refs[j]
        for h in range(heads):
            qt[:width, h * tok : (h + 1) * tok] = q_ref[h * width : (h + 1) * width, :]
        base = q_ref.shape[0] - EXTRA
        qp = q_ref[base:, :].astype(F32)
        one = qp[0:1, :] * 64.0 + qp[1:2, :]
        row_pos = jnp.concatenate([one] * heads, axis=1)
        s = mm(k_ref[...], qt[...]) * factor
        s = jnp.where(key_pos <= row_pos, s, -1e30)
        s_ref[:, j * rows : (j + 1) * rows] = s
        top = jnp.max(s, axis=0, keepdims=True)
        lse = top + jnp.log(jnp.sum(jnp.exp(s - top), axis=0, keepdims=True))
        for h in range(heads):
            at = j * heads + h
            stat_ref[at : at + 1, :] = lse[:, h * tok : (h + 1) * tok]


def context_kernel(width, heads, *refs):
    q_refs = refs[:GROUP]
    wuv_ref, k_ref, g_ref, gp_ref = refs[GROUP:]
    lat, all_rows = g_ref.shape
    tok = q_refs[0].shape[1]
    rows = heads * tok
    for j in range(GROUP):
        for h in range(heads):
            at = heads * width + h * HEAD_DIM
            og = q_refs[j][at : at + HEAD_DIM, :]
            col = j * rows + h * tok
            g_ref[:, col : col + tok] = mm(wuv_ref[h], og).astype(BF16)
        cols = slice(j * rows, (j + 1) * rows)
        gp_ref[:, cols] = mm(k_ref[:, :lat], g_ref[:, cols])


def grad_kernel(factor, nkey, width, heads, *refs):
    lat_refs, refs = refs[:nkey], refs[nkey:]
    q_refs, refs = refs[:GROUP], refs[GROUP:]
    stats, refs = refs[:GROUP], refs[GROUP:]
    (s_ref, gp_ref, g_ref), refs = refs[:3], refs[3:]
    part_refs, refs = refs[:nkey], refs[nkey:]
    own_ref, core_ref, across_ref, kt, qt, gs_all, p_all = refs
    tok = q_refs[0].shape[1]
    rows = heads * tok
    lat = g_ref.shape[0]
    for a in range(nkey):
        kt[:, a * tok : (a + 1) * tok] = lat_refs[a][:width, :]
    for j in range(GROUP):
        cols = slice(j * rows, (j + 1) * rows)
        lse_parts = []
        for k in range(GROUP):
            at = (j ^ k) * heads
            lse_parts.append(
                jnp.concatenate([stats[k][at + h : at + h + 1, :] for h in range(heads)], axis=1)
            )
        top = functools.reduce(jnp.maximum, lse_parts)
        lse = top + jnp.log(sum(jnp.exp(part - top) for part in lse_parts))
        at = GROUP * heads
        delta = jnp.concatenate([stats[j][at + h : at + h + 1, :] for h in range(heads)], axis=1)
        p = jnp.exp(s_ref[:, cols] - lse)
        gs = (p * (gp_ref[:, cols] - delta)).astype(BF16)
        gs_all[:, cols] = gs
        p_all[:, cols] = p.astype(BF16)
        gq = (mm(kt[...], gs) * factor).astype(BF16)
        for h in range(heads):
            head_cols = slice(j * rows + h * tok, j * rows + (h + 1) * tok)
            qt[:, head_cols] = q_refs[j][h * width : (h + 1) * width, :]
            part = gq[:, h * tok : (h + 1) * tok]
            if j == 0:
                own_ref[h] = part
            elif j == 2:
                across_ref[h] = part
            else:
                core_ref[j // 2 * heads + h] = part
    for a in range(nkey):
        at = slice(a * tok, (a + 1) * tok)
        along = mm_t(qt[...], gs_all[at, :]) * factor
        value = mm_t(g_ref[...], p_all[at, :])
        part_refs[a][:lat, :] = (along[:lat] + value).astype(BF16)
        part_refs[a][lat:, :] = along[lat:].astype(BF16)


def spread_kernel(idx_ref, *refs):
    chunks, out_ref = refs[:GROUP], refs[GROUP]
    step = chunks[0].shape[1]
    me = lax.rem(idx_ref[0], GROUP)
    for k in range(GROUP):
        at = pl.multiple_of(jnp.bitwise_xor(me, k) * step, step)
        out_ref[:, pl.ds(at, step), :] = chunks[k][...].astype(F32)


def body(n_ctx, n_dp, positions, queries, latent, out_grad, attn_out, wuv):
    tok, heads, width = queries.shape[1:]
    lat = attn_out.shape[3]
    lines = n_ctx // GROUP
    line_bits = (lines - 1).bit_length()
    rows = heads * tok
    all_rows = GROUP * rows
    keys = lines * tok
    wide = -(-(width + EXTRA) // 128) * 128
    factor = (HEAD_DIM + ROPE) ** (-0.5)

    def swap(x, mask):
        return lax.ppermute(x, "ctx", [(i, i ^ mask) for i in range(n_ctx)])

    def after(x, *done):
        return lax.optimization_barrier((x, done))[0]

    idx = lax.axis_index("ctx").reshape(1)
    pos_rows = jnp.concatenate(
        [positions // 64, positions % 64, jnp.zeros((EXTRA - 2, tok), positions.dtype)], axis=0
    ).astype(BF16)
    lat_msg, q_msg = call(
        pack_kernel,
        "pack",
        [((width + EXTRA, tok), BF16), ((heads * (width + HEAD_DIM) + EXTRA, tok), BF16)],
        [pos_rows, jnp.transpose(queries[0], (1, 2, 0)), out_grad[0], latent[0].T],
    )
    held, firsts = {0: lat_msg}, []
    for bit in reversed(range(line_bits)):
        first = swap(lat_msg, GROUP << bit)
        ahead = {m: after(x, first) for m, x in held.items() if m}
        held.update({m | 1 << bit: swap(x, GROUP << bit) for m, x in ahead.items()})
        held[1 << bit] = first
        firsts.append(first)
    lats = [held[m] for m in range(lines)]
    q_across = swap(q_msg, 2)
    q_core = swap(q_msg, 1)
    q_far = swap(after(q_across, q_core), 1)
    qs = [q_msg, q_core, q_across, q_far]

    step = lat // GROUP
    delta, *chunks = call(
        functools.partial(own_kernel, width),
        "own_rows",
        [((8, tok), F32)] + [((heads, step, HEAD_DIM), BF16)] * GROUP,
        [idx, attn_out[0], q_msg, wuv],
        [((heads, lat, HEAD_DIM), F32)],
        flops=4 * rows * lat * HEAD_DIM,
        smem=(0,),
    )
    chunks = after(chunks, *firsts, q_core, q_across)
    got = [chunks[0]] + [swap(chunks[k], k) for k in range(1, GROUP)]
    scale = 1.0 / math.sqrt(tok * n_ctx * n_dp)
    mine = (sum(c.astype(F32) for c in got) * scale).astype(BF16)
    hops = [("ctx", n_ctx, GROUP << bit) for bit in range(line_bits)]
    hops += [("dp", n_dp, 1 << bit) for bit in range((n_dp - 1).bit_length())]

    def climb(total, steps, *done):
        for axis, size, mask in steps:
            other = lax.ppermute(total, axis, [(i, i ^ mask) for i in range(size)])
            other = after(other, *done)
            total = (total.astype(F32) + other.astype(F32)).astype(BF16)
        return total

    s, k_nat, stat = call(
        functools.partial(score_kernel, factor, lines, width, heads),
        "scores",
        [((keys, all_rows), F32), ((keys, wide), BF16), ((EXTRA, tok), F32)],
        lats + qs + [after(delta, mine)],
        [((wide, keys), BF16), ((wide, rows), BF16)],
        flops=2 * keys * all_rows * wide,
    )
    stats = [stat] + [swap(stat, k) for k in range(1, GROUP)]
    mine = climb(mine, hops[:1], stat)
    g, gp = call(
        functools.partial(context_kernel, width, heads),
        "context",
        [((lat, all_rows), BF16), ((keys, all_rows), F32)],
        qs + [wuv, after(k_nat, mine)],
        flops=2 * keys * all_rows * lat + 2 * all_rows * lat * HEAD_DIM,
    )
    mine = climb(mine, hops[1:-1], gp)
    outs = call(
        functools.partial(grad_kernel, factor, lines, width, heads),
        "gradients",
        [((width, tok), BF16)] * lines
        + [((heads, width, tok), BF16), ((2 * heads, width, tok), BF16), ((heads, width, tok), BF16)],
        lats + qs + [after(stats[0], mine)] + stats[1:] + [s, gp, g],
        [
            ((width, keys), BF16),
            ((width, all_rows), BF16),
            ((keys, all_rows), BF16),
            ((keys, all_rows), BF16),
        ],
        flops=2 * keys * all_rows * (2 * width + lat),
    )
    parts, (gq_own, gq_core, gq_across) = list(outs[:lines]), outs[lines:]
    mine = climb(mine, hops[-1:], gq_own)
    kept = [parts[0]]
    for bit in range(line_bits):
        for m in reversed(range(1 << bit, lines, 2 << bit)):
            got_part = swap(parts[m], GROUP << bit)
            target = m ^ 1 << bit
            if target:
                parts[target] = (parts[target].astype(F32) + got_part.astype(F32)).astype(BF16)
            else:
                kept.append(got_part)
    gq_got = swap(gq_core, 1)
    gq_sum = (gq_across.astype(F32) + gq_got[heads:].astype(F32)).astype(BF16)
    gq_last = swap(gq_sum, 2)
    grad_lat = sum(p.astype(F32) for p in kept).astype(BF16)
    grad_q = sum(p.astype(F32) for p in (gq_own, gq_got[:heads], gq_last)).astype(BF16)
    pieces = [mine] + [swap(mine, k) for k in range(1, GROUP)]
    (grad_w,) = call(
        spread_kernel, "spread", [((heads, lat, HEAD_DIM), F32)], [idx] + pieces, smem=(0,)
    )
    return (jnp.transpose(grad_q, (2, 0, 1))[None], grad_lat.T[None], grad_w)


def solution(mesh):
    placed = (
        P("dp", "ctx"),
        P("dp", "ctx", None, None),
        P("dp", "ctx", None),
        P("dp", "ctx", None, None),
        P("dp", "ctx", None, None),
        P(),
    )
    return jax.shard_map(
        functools.partial(body, mesh.shape["ctx"], mesh.shape["dp"]),
        mesh=mesh,
        in_specs=placed,
        out_specs=(P("dp", "ctx", None, None), P("dp", "ctx", None), P()),
        check_vma=False,
    )
```

time: 85.4 us -> 62.8 us (0.74)
  Pallas kernels: 19.5 us -> 8.04 us
  waiting for transfers between devices: 24.7 us -> 21 us
  local copies, waits for them, and re-layouts: 7.88 us -> 4.69 us
  other arithmetic: 5.11 us -> 2.53 us
  starting transfers between devices: 26.9 us -> 25.5 us
    pallas_call x5 -> x6, Pallas kernels: 19.5 us -> 8.04 us  [call(): pl.pallas_call(kernel, out_shape=[jax.ShapeDtypeStruct(s, d) for s, d in...]
    ppermute x23 -> x20, starting transfers between devices: 25.4 us -> 19.7 us  [swap(): return lax.ppermute(x, 'ctx', [(i, i ^ mask) for i in range(n_ctx)])]
    ppermute x23 -> x20, waiting for transfers between devices: 24.7 us -> 19.2 us  [swap(): return lax.ppermute(x, 'ctx', [(i, i ^ mask) for i in range(n_ctx)])]
    ppermute x1 -> x3, starting transfers between devices: 1.49 us -> 5.85 us  [climb(): other = lax.ppermute(total, axis, [(i, i ^ mask) for i in range(size)])]
    concatenate x1, local copies, waits for them, and re-layouts: 2.83 us -> 0.08 us  [body(): jnp.concatenate([positions // 64, positions % 64, jnp.zeros((EXTRA - 2, t...]
    broadcast_in_dim x2, other arithmetic: 3.48 us -> 1.55 us  [body(): return (jnp.transpose(grad_q, (2, 0, 1))[None], grad_lat.T[None], grad_w)]
    ppermute x1 -> x3, waiting for transfers between devices: 0.01 us -> 1.78 us  [climb(): other = lax.ppermute(total, axis, [(i, i ^ mask) for i in range(size)])]
    unnamed x34 -> x12, local copies, waits for them, and re-layouts: 5.05 us -> 4.61 us
  transfers between devices with their start and end apart: 24 -> 23, of which waited for: 7 -> 9; matrix products, arithmetic and copies ran while one was open for 7% -> 1% of each run, Pallas kernels for 20% -> 7%
where the time goes in v2:
time: 62.8 us; the launch traced here: 62.5 us
  starting transfers between devices  25.5 us (41%)
  waiting for transfers between devices  21 us (33%)
  Pallas kernels  8.04 us (13%)
  local copies, waits for them, and re-layouts  4.69 us (7%)
  other arithmetic  2.53 us (4%)
  between operations  0.76 us (1%)
    ppermute x20, starting transfers between devices, swap(): return lax.ppermute(x, 'ctx', [(i, i ^ mask) for i in range(n_ctx)])  19.7 us
    ppermute x20, waiting for transfers between devices, swap(): return lax.ppermute(x, 'ctx', [(i, i ^ mask) for i in range(n_ctx)])  19.2 us
    pallas_call x6, Pallas kernels, call(): pl.pallas_call(kernel, out_shape=[jax.ShapeDtypeStruct(s, d) for s, d in...  8.04 us
    ppermute x3, starting transfers between devices, climb(): other = lax.ppermute(total, axis, [(i, i ^ mask) for i in range(size)])  5.85 us
    unnamed x12, local copies, waits for them, and re-layouts  4.61 us
    ppermute x3, waiting for transfers between devices, climb(): other = lax.ppermute(total, axis, [(i, i ^ mask) for i in range(size)])  1.78 us
    broadcast_in_dim x2, other arithmetic, body(): return (jnp.transpose(grad_q, (2, 0, 1))[None], grad_lat.T[None], grad_w)  1.55 us
  transfers between devices with their start and end apart: 23, of which 9 were waited for; matrix products, arithmetic and copies ran while one was open for 1% of the time, Pallas kernels for 7%

profile of v2, /device:TPU:0, one launch (start us, length us, event | category | flops | bytes accessed | tf_op | source)
XLA Modules:
  0.0 62.5 jit_solution(6017953310467784896)
XLA Ops:
  0.6 0.7 %fusion.3 = (bf16[1,128]{1,0:T(2,128)(2,1)S(1)}, bf16[1,128]{1,0:T(2,128)(2,1)S(1)}) fusion(s32[1,128]{1,0:T(1,128)} %param.6), kind=kLoop, calls=%fused_computation.17 | loop fusion | flops 2688 | bytes 1024 | tf_op jit(solution)/shard_map/convert
  1.3 0.1 pad.2.clone
  1.4 0.1 maximum_maximum_fusion.pos_ref
  1.5 1.0 %copy-done = bf16[1,128,2,576]{1,3,2,0:T(8,128)(2,1)S(1)} copy-done((bf16[1,128,2,576]{1,3,2,0:T(8,128)(2,1)S(1)}, bf16[1,128,2,576]{1,3,2,0:T(8,128)(2,1)}, u32[]{:S(2)}) %copy-start) | copy-done | bytes 294936
  2.4 0.9 %copy-done.4 = bf16[1,128,576]{1,2,0:T(8,128)(2,1)S(1)} copy-done((bf16[1,128,576]{1,2,0:T(8,128)(2,1)S(1)}, bf16[1,128,576]{1,2,0:T(8,128)(2,1)}, u32[]{:S(2)}) %copy-start.4) | copy-done | bytes 147480
  3.3 0.8 %copy-done.5 = bf16[1,128,2,128]{3,2,1,0:T(2,128)(2,1)S(1)} copy-done((bf16[1,128,2,128]{3,2,1,0:T(2,128)(2,1)S(1)}, bf16[1,128,2,128]{3,2,1,0:T(2,128)(2,1)}, u32[]{:S(2)}) %copy-start.5) | copy-done | bytes 65560
  4.2 0.2 pack.1
  4.4 3.0 %collective-permute-start.4 = (bf16[1424,128]{1,0:T(8,128)(2,1)S(1)}, bf16[1424,128]{1,0:T(8,128)(2,1)S(1)}, u32[]{:S(2)}, u32[]{:S(2)}) collective-permute-start(bf16[1424,128]{1,0:T(8,128)(2,1)S(1)} %get-tuple-element.36.msg_ref.refs_4_.refs_0_), channel_id=1, source_target_pairs={{0,2},{1,3},{2,0},{3,1},{4,6},{5,7},{6,4},{7,5},{8,10},{9,11},{10,... | collective-permute-start | bytes 1093640 | tf_op jit(solution)/shard_map/ppermute | solution.py:197
  7.4 0.0 collective-permute-start.3
  7.4 2.6 %collective-permute-start.1 = (bf16[592,128]{1,0:T(8,128)(2,1)S(1)}, bf16[592,128]{1,0:T(8,128)(2,1)S(1)}, u32[]{:S(2)}, u32[]{:S(2)}) collective-permute-start(bf16[592,128]{1,0:T(8,128)(2,1)S(1)} %get-tuple-element.34.refs_0_), channel_id=1, source_target_pairs={{0,8},{1,9},{2,10},{3,11},{4,12},{5,13},{6,14},{7,15},{8,0},{9,1},... | collective-permute-start | bytes 454664 | tf_op jit(solution)/shard_map/ppermute | solution.py:197
  10.0 1.6 %collective-permute-start = (bf16[592,128]{1,0:T(8,128)(2,1)S(1)}, bf16[592,128]{1,0:T(8,128)(2,1)S(1)}, u32[]{:S(2)}, u32[]{:S(2)}) collective-permute-start(bf16[592,128]{1,0:T(8,128)(2,1)S(1)} %get-tuple-element.34.refs_0_), channel_id=1, source_target_pairs={{0,4},{1,5},{2,6},{3,7},{4,0},{5,1},{6,2},{7,3},{8,12},{9,13},{10,... | collective-permute-start | bytes 454664 | tf_op jit(solution)/shard_map/ppermute | solution.py:197
  11.6 4.3 %collective-permute-done.4.refs_6_.refs_2_ = bf16[1424,128]{1,0:T(8,128)(2,1)S(1)} collective-permute-done((bf16[1424,128]{1,0:T(8,128)(2,1)S(1)}, bf16[1424,128]{1,0:T(8,128)(2,1)S(1)}, u32[]{:S(2)}, u32[]{:S(2)}) %collective-permute-start.4) | collective-permute-done | bytes 364576 | tf_op jit(solution)/shard_map/ppermute | solution.py:197
  15.9 0.0 collective-permute-done.3.refs_5_.refs_1_
  15.9 0.0 collective-permute-start.5
  15.9 0.9 %copy-done.1 = bf16[1,128,2,512]{3,2,1,0:T(2,128)(2,1)S(1)} copy-done((bf16[1,128,2,512]{3,2,1,0:T(2,128)(2,1)S(1)}, bf16[1,128,2,512]{3,2,1,0:T(2,128)(2,1)}, u32[]{:S(2)}) %copy-start.1) | copy-done | bytes 262168
  16.9 0.9 %copy-done.2 = bf16[2,512,128]{2,1,0:T(8,128)(2,1)S(1)} copy-done((bf16[2,512,128]{2,1,0:T(8,128)(2,1)S(1)}, bf16[2,512,128]{2,1,0:T(8,128)(2,1)}, u32[]{:S(2)}) %copy-start.2) | copy-done | bytes 262168
  17.8 0.8 %own_rows.1 = (f32[8,128]{1,0:T(8,128)S(1)}, bf16[2,128,128]{2,1,0:T(8,128)(2,1)S(1)}, bf16[2,128,128]{2,1,0:T(8,128)(2,1)S(1)}, bf16[2,128,128]{2,1,0:T(8,128)(2,1)S(1)}, bf16[2,128,128]{2,1,0:T(8,128)(2,1)S(1)}) custom-call(s32[1]{0:T(128)} %bitcast.5.idx_ref, bf16[128,2,512]{2,1,0:T(2,128)(2,1)S(1)} %bitcast.18, ...), custom_call_target="tpu_custom_call" | custom-call | flops 67108864 | bytes 1155076 | tf_op jit(solution)/shard_map/own_rows/pallas_call | solution.py:37
  18.7 0.0 collective-permute-done.1.refs_2_
  18.7 0.0 collective-permute-done.refs_1_
  18.7 0.6 collective-permute-start.6
  19.3 1.7 %collective-permute-start.7 = (bf16[2,128,128]{2,1,0:T(8,128)(2,1)S(1)}, bf16[2,128,128]{2,1,0:T(8,128)(2,1)S(1)}, u32[]{:S(2)}, u32[]{:S(2)}) collective-permute-start(bf16[2,128,128]{2,1,0:T(8,128)(2,1)S(1)} %get-tuple-element.45), channel_id=1, source_target_pairs={{0,2},{1,3},{2,0},{3,1},{4,6},{5,7},{6,4},{7,5},{8,10},{9,11},{10,... | collective-permute-start | bytes 196616 | tf_op jit(solution)/shard_map/ppermute | solution.py:197
  21.0 0.0 collective-permute-start.8
  21.0 1.6 %collective-permute-start.2 = (bf16[592,128]{1,0:T(8,128)(2,1)S(1)}, bf16[592,128]{1,0:T(8,128)(2,1)S(1)}, u32[]{:S(2)}, u32[]{:S(2)}) collective-permute-start(bf16[592,128]{1,0:T(8,128)(2,1)S(1)} %collective-permute-done.1.refs_2_), channel_id=1, source_target_pairs={{0,4},{1,5},{2,6},{3,7},{4,0},{5,1},{6,2},{7,3},{8,12},{9,13},{10,... | collective-permute-start | bytes 454664 | tf_op jit(solution)/shard_map/ppermute | solution.py:197
  22.6 0.0 collective-permute-done.6
  22.6 0.9 %collective-permute-done.7 = bf16[2,128,128]{2,1,0:T(8,128)(2,1)S(1)} collective-permute-done((bf16[2,128,128]{2,1,0:T(8,128)(2,1)S(1)}, bf16[2,128,128]{2,1,0:T(8,128)(2,1)S(1)}, u32[]{:S(2)}, u32[]{:S(2)}) %collective-permute-start.7) | collective-permute-done | bytes 65568 | tf_op jit(solution)/shard_map/ppermute | solution.py:197
  23.5 1.9 %collective-permute-done.8 = bf16[2,128,128]{2,1,0:T(8,128)(2,1)S(1)} collective-permute-done((bf16[2,128,128]{2,1,0:T(8,128)(2,1)S(1)}, bf16[2,128,128]{2,1,0:T(8,128)(2,1)S(1)}, u32[]{:S(2)}, u32[]{:S(2)}) %collective-permute-start.8) | collective-permute-done | bytes 65568 | tf_op jit(solution)/shard_map/ppermute | solution.py:197
  25.4 1.6 %collective-permute-start.9 = (bf16[2,128,128]{2,1,0:T(8,128)(2,1)S(1)}, bf16[2,128,128]{2,1,0:T(8,128)(2,1)S(1)}, u32[]{:S(2)}, u32[]{:S(2)}) collective-permute-start(bf16[2,128,128]{2,1,0:T(8,128)(2,1)S(1)} %multiply_convert_fusion), channel_id=1, source_target_pairs={{0,4},{1,5},{2,6},{3,7},{4,0},{5,1},{6,2},{7,3},{8,12},{9,13},{10,... | collective-permute-start | bytes 196616 | tf_op jit(solution)/shard_map/ppermute | solution.py:244
  27.1 0.2 collective-permute-done.2.refs_3_
  27.3 0.0 collective-permute-done.5.refs_7_.refs_3_
  27.3 1.6 %scores.1 = (f32[512,1024]{1,0:T(8,128)S(1)}, bf16[512,640]{1,0:T(8,128)(2,1)S(1)}, f32[16,128]{1,0:T(8,128)S(1)}) custom-call(bf16[592,128]{1,0:T(8,128)(2,1)S(1)} %get-tuple-element.34.refs_0_, bf16[592,128]{1,0:T(8,128)(2,1)S(1)} %collective-permute-done.refs_1_, bf16[592,128]{1,0:T(8,128)(2,1)S(1)} %collective-permute-done.1.refs_2_, ...), custom_call_target="tpu_custom_call" | custom-call | flops 671088640 | bytes 4829184 | tf_op jit(solution)/shard_map/scores/pallas_call | solution.py:37
  28.9 0.9 %collective-permute-done.9 = bf16[2,128,128]{2,1,0:T(8,128)(2,1)S(1)} collective-permute-done((bf16[2,128,128]{2,1,0:T(8,128)(2,1)S(1)}, bf16[2,128,128]{2,1,0:T(8,128)(2,1)S(1)}, u32[]{:S(2)}, u32[]{:S(2)}) %collective-permute-start.9) | collective-permute-done | bytes 65568 | tf_op jit(solution)/shard_map/ppermute | solution.py:244
  29.8 2.7 %collective-permute-start.10 = (bf16[2,128,128]{2,1,0:T(8,128)(2,1)S(1)}, bf16[2,128,128]{2,1,0:T(8,128)(2,1)S(1)}, u32[]{:S(2)}, u32[]{:S(2)}) collective-permute-start(bf16[2,128,128]{2,1,0:T(8,128)(2,1)S(1)} %add_convert_fusion.6), channel_id=1, source_target_pairs={{0,8},{1,9},{2,10},{3,11},{4,12},{5,13},{6,14},{7,15},{8,0},{9,1},... | collective-permute-start | bytes 196616 | tf_op jit(solution)/shard_map/ppermute | solution.py:244
  32.5 0.3 collective-permute-start.13
  32.8 0.8 %collective-permute-start.12 = (f32[16,128]{1,0:T(8,128)S(1)}, f32[16,128]{1,0:T(8,128)S(1)}, u32[]{:S(2)}, u32[]{:S(2)}) collective-permute-start(f32[16,128]{1,0:T(8,128)S(1)} %get-tuple-element.54.refs_8_), channel_id=1, source_target_pairs={{0,2},{1,3},{2,0},{3,1},{4,6},{5,7},{6,4},{7,5},{8,10},{9,11},{10,... | collective-permute-start | bytes 24584 | tf_op jit(solution)/shard_map/ppermute | solution.py:197
  33.6 0.8 %collective-permute-start.11 = (f32[16,128]{1,0:T(8,128)S(1)}, f32[16,128]{1,0:T(8,128)S(1)}, u32[]{:S(2)}, u32[]{:S(2)}) collective-permute-start(f32[16,128]{1,0:T(8,128)S(1)} %get-tuple-element.54.refs_8_), channel_id=1, source_target_pairs={{0,1},{1,0},{2,3},{3,2},{4,5},{5,4},{6,7},{7,6},{8,9},{9,8},{10,11... | collective-permute-start | bytes 24584 | tf_op jit(solution)/shard_map/ppermute | solution.py:197
  34.3 0.0 copy-done.3
  34.3 1.2 %context.1 = (bf16[512,1024]{1,0:T(8,128)(2,1)S(1)}, f32[512,1024]{1,0:T(8,128)S(1)}) custom-call(bf16[1424,128]{1,0:T(8,128)(2,1)S(1)} %get-tuple-element.36.msg_ref.refs_4_.refs_0_, bf16[1424,128]{1,0:T(8,128)(2,1)S(1)} %collective-permute-done.3.refs_5_.refs_1_, bf16[1424,128]{1,0:T(8,128)(2,1)S(1)} %collective-permute-done.4.refs_6_.refs_2_, ...), custom_call_target="tpu_custom_call" | custom-call | flops 671088640 | bytes 5521408 | tf_op jit(solution)/shard_map/context/pallas_call | solution.py:37
  35.6 0.0 collective-permute-done.10
  35.6 0.0 collective-permute-done.13.refs_11_
  35.6 0.8 %collective-permute-done.12.refs_10_ = f32[16,128]{1,0:T(8,128)S(1)} collective-permute-done((f32[16,128]{1,0:T(8,128)S(1)}, f32[16,128]{1,0:T(8,128)S(1)}, u32[]{:S(2)}, u32[]{:S(2)}) %collective-permute-start.12) | collective-permute-done | bytes 8224 | tf_op jit(solution)/shard_map/ppermute | solution.py:197
  36.5 0.0 collective-permute-done.11.refs_9_
  36.5 3.3 %gradients.1 = (bf16[576,128]{1,0:T(8,128)(2,1)S(1)}, bf16[576,128]{1,0:T(8,128)(2,1)S(1)}, bf16[576,128]{1,0:T(8,128)(2,1)S(1)}, bf16[576,128]{1,0:T(8,128)(2,1...) custom-call(bf16[592,128]{1,0:T(8,128)(2,1)S(1)} %get-tuple-element.34.r, ...), custom_call_target="tpu_custom_call" | custom-call | flops 1744830464 | bytes 9109504 | tf_op jit(solution)/shard_map/gradients/pallas_call | solution.py:37
  39.8 0.1 collective-permute-start.14
  39.9 1.6 %collective-permute-start.19 = (bf16[2,128,128]{2,1,0:T(8,128)(2,1)S(1)}, bf16[2,128,128]{2,1,0:T(8,128)(2,1)S(1)}, u32[]{:S(2)}, u32[]{:S(2)}) collective-permute-start(bf16[2,128,128]{2,1,0:T(8,128)(2,1)S(1)} %add_convert_fusion.5), channel_id=1, source_target_pairs={{0,16},{16,0},{1,17},{17,1},{2,18},{18,2},{3,19},{19,3},{4,20},{20... | collective-permute-start | bytes 196616 | tf_op jit(solution)/shard_map/ppermute | solution.py:244
  41.4 1.6 %collective-permute-start.16 = (bf16[576,128]{1,0:T(8,128)(2,1)S(1)}, bf16[576,128]{1,0:T(8,128)(2,1)S(1)}, u32[]{:S(2)}, u32[]{:S(2)}) collective-permute-start(bf16[576,128]{1,0:T(8,128)(2,1)S(1)} %get-tuple-element.61), channel_id=1, source_target_pairs={{0,4},{1,5},{2,6},{3,7},{4,0},{5,1},{6,2},{7,3},{8,12},{9,13},{10,... | collective-permute-start | bytes 442376 | tf_op jit(solution)/shard_map/ppermute | solution.py:197
  43.0 0.4 collective-permute-start.17
  43.4 0.9 %collective-permute-done.19 = bf16[2,128,128]{2,1,0:T(8,128)(2,1)S(1)} collective-permute-done((bf16[2,128,128]{2,1,0:T(8,128)(2,1)S(1)}, bf16[2,128,128]{2,1,0:T(8,128)(2,1)S(1)}, u32[]{:S(2)}, u32[]{:S(2)}) %collective-permute-start.19) | collective-permute-done | bytes 65568 | tf_op jit(solution)/shard_map/ppermute | solution.py:244
  44.4 0.3 collective-permute-start.22
  44.7 1.0 %collective-permute-start.21 = (bf16[2,128,128]{2,1,0:T(8,128)(2,1)S(1)}, bf16[2,128,128]{2,1,0:T(8,128)(2,1)S(1)}, u32[]{:S(2)}, u32[]{:S(2)}) collective-permute-start(bf16[2,128,128]{2,1,0:T(8,128)(2,1)S(1)} %add_convert_fusion.4.refs_0_), channel_id=1, source_target_pairs={{0,2},{1,3},{2,0},{3,1},{4,6},{5,7},{6,4},{7,5},{8,10},{9,11},{10,... | collective-permute-start | bytes 196616 | tf_op jit(solution)/shard_map/ppermute | solution.py:197
  45.7 4.7 %collective-permute-done.17 = bf16[576,128]{1,0:T(8,128)(2,1)S(1)} collective-permute-done((bf16[576,128]{1,0:T(8,128)(2,1)S(1)}, bf16[576,128]{1,0:T(8,128)(2,1)S(1)}, u32[]{:S(2)}, u32[]{:S(2)}) %collective-permute-start.17) | collective-permute-done | bytes 147488 | tf_op jit(solution)/shard_map/ppermute | solution.py:197
  50.5 0.0 collective-permute-start.20
  50.5 0.0 collective-permute-done.14
  50.6 1.7 %collective-permute-start.18 = (bf16[576,128]{1,0:T(8,128)(2,1)S(1)}, bf16[576,128]{1,0:T(8,128)(2,1)S(1)}, u32[]{:S(2)}, u32[]{:S(2)}) collective-permute-start(bf16[576,128]{1,0:T(8,128)(2,1)S(1)} %add_convert_fusion.3), channel_id=1, source_target_pairs={{0,8},{1,9},{2,10},{3,11},{4,12},{5,13},{6,14},{7,15},{8,0},{9,1},... | collective-permute-start | bytes 442376 | tf_op jit(solution)/shard_map/ppermute | solution.py:197
  52.3 0.1 add_convert_fusion.1
  52.4 0.0 collective-permute-done.22.refs_3_
  52.4 1.5 %collective-permute-start.15 = (bf16[2,576,128]{2,1,0:T(8,128)(2,1)S(1)}, bf16[2,576,128]{2,1,0:T(8,128)(2,1)S(1)}, u32[]{:S(2)}, u32[]{:S(2)}) collective-permute-start(bf16[2,576,128]{2,1,0:T(8,128)(2,1)S(1)} %add_convert_fusion.1), channel_id=1, source_target_pairs={{0,2},{1,3},{2,0},{3,1},{4,6},{5,7},{6,4},{7,5},{8,10},{9,11},{10,... | collective-permute-start | bytes 884744 | tf_op jit(solution)/shard_map/ppermute | solution.py:197
  53.9 0.0 collective-permute-done.21.refs_2_
  53.9 0.0 collective-permute-done.20.refs_1_
  53.9 0.8 %spread.1 = f32[2,512,128]{2,1,0:T(8,128)} custom-call(s32[1]{0:T(128)} %bitcast.5.idx_ref, bf16[2,128,128]{2,1,0:T(8,128)(2,1)S(1)} %add_convert_fusion.4.refs_0_, bf16[2,128,128]{2,1,0:T(8,128)(2,1)S(1)} %collective-permute-done.20.refs_1_, bf16[2,128,128]{2,1,0:T(8,128)(2,1)S(1)} %collective-permute-done.21.refs_2_, ...), custom_call_target="tpu_custom_call" | custom-call | bytes 786436 | tf_op jit(solution)/shard_map/spread/pallas_call | solution.py:37
  54.7 0.0 collective-permute-done.16
  54.7 6.2 %collective-permute-done.18 = bf16[576,128]{1,0:T(8,128)(2,1)S(1)} collective-permute-done((bf16[576,128]{1,0:T(8,128)(2,1)S(1)}, bf16[576,128]{1,0:T(8,128)(2,1)S(1)}, u32[]{:S(2)}, u32[]{:S(2)}) %collective-permute-start.18) | collective-permute-done | bytes 147488 | tf_op jit(solution)/shard_map/ppermute | solution.py:197
  60.9 0.7 %fusion.1 = bf16[1,128,576]{1,2,0:T(8,128)(2,1)} fusion(bf16[576,128]{1,0:T(8,128)(2,1)S(1)} %collective-permute-done.18, bf16[576,128]{1,0:T(8,128)(2,1)S(1)} %collective-permute-done.16, bf16[576,128]{1,0:T(8,128)(2,1)S(1)} %get-tuple-element.60), kind=kLoop, calls=%fused_computation.5 | loop fusion | flops 442368 | bytes 589824 | tf_op jit(solution)/shard_map/broadcast_in_dim | solution.py:301
  61.7 0.0 collective-permute-done.15
  61.7 0.8 %fusion = bf16[1,128,2,576]{1,3,2,0:T(8,128)(2,1)} fusion(bf16[2,576,128]{2,1,0:T(8,128)(2,1)S(1)} %collective-permute-done.15, bf16[2,576,128]{2,1,0:T(8,128)(2,1)S(1)} %get-tuple-element.57, bf16[4,576,128]{2,1,0:T(8,128)(2,1)S(1)} %collective-permute-done.14), kind=kLoop, calls=%fused_computation.2 | loop fusion | flops 884736 | bytes 1179648 | tf_op jit(solution)/shard_map/broadcast_in_dim | solution.py:301
  (12 shorter events, 0.2 us)
Async XLA Ops:
  1.5 1.0 %copy-start = (bf16[1,128,2,576]{1,3,2,0:T(8,128)(2,1)S(1)}, bf16[1,128,2,576]{1,3,2,0:T(8,128)(2,1)}, u32[]{:S(2)}) copy-start(bf16[1,128,2,576]{1,3,2,0:T(8,128)(2,1)} %param.7) | copy-start | bytes 884740
  2.4 0.9 %copy-start.4 = (bf16[1,128,576]{1,2,0:T(8,128)(2,1)S(1)}, bf16[1,128,576]{1,2,0:T(8,128)(2,1)}, u32[]{:S(2)}) copy-start(bf16[1,128,576]{1,2,0:T(8,128)(2,1)} %param.8) | copy-start | bytes 442372
  3.3 0.8 %copy-start.5 = (bf16[1,128,2,128]{3,2,1,0:T(2,128)(2,1)S(1)}, bf16[1,128,2,128]{3,2,1,0:T(2,128)(2,1)}, u32[]{:S(2)}) copy-start(bf16[1,128,2,128]{3,2,1,0:T(2,128)(2,1)} %param.9) | copy-start | bytes 196612
  4.2 30.1 %copy-start.3 = (bf16[2,512,128]{2,1,0:T(8,128)(2,1)S(1)}, bf16[2,512,128]{2,1,0:T(8,128)(2,1)}, u32[]{:S(2)}) copy-start(bf16[2,512,128]{2,1,0:T(8,128)(2,1)} %refs_4_.1) | copy-start | bytes 786436
  4.4 11.5 %collective-permute-start.4 = (bf16[1424,128]{1,0:T(8,128)(2,1)S(1)}, bf16[1424,128]{1,0:T(8,128)(2,1)S(1)}, u32[]{:S(2)}, u32[]{:S(2)}) collective-permute-start(bf16[1424,128]{1,0:T(8,128)(2,1)S(1)} %get-tuple-element.36.msg_ref.refs_4_.refs_0_), channel_id=1, source_target_pairs={{0,2},{1,3},{2,0},{3,1},{4,6},{5,7},{6,4},{7,5},{8,10},{9,11},{10,... | collective-permute-start | bytes 1093640 | tf_op jit(solution)/shard_map/ppermute | solution.py:197
  7.4 8.5 %collective-permute-start.3 = (bf16[1424,128]{1,0:T(8,128)(2,1)S(1)}, bf16[1424,128]{1,0:T(8,128)(2,1)S(1)}, u32[]{:S(2)}, u32[]{:S(2)}) collective-permute-start(bf16[1424,128]{1,0:T(8,128)(2,1)S(1)} %get-tuple-element.36.msg_ref.refs_4_.refs_0_), channel_id=1, source_target_pairs={{0,1},{1,0},{2,3},{3,2},{4,5},{5,4},{6,7},{7,6},{8,9},{9,8},{10,11... | collective-permute-start | bytes 1093640 | tf_op jit(solution)/shard_map/ppermute | solution.py:197
  7.4 11.3 %collective-permute-start.1 = (bf16[592,128]{1,0:T(8,128)(2,1)S(1)}, bf16[592,128]{1,0:T(8,128)(2,1)S(1)}, u32[]{:S(2)}, u32[]{:S(2)}) collective-permute-start(bf16[592,128]{1,0:T(8,128)(2,1)S(1)} %get-tuple-element.34.refs_0_), channel_id=1, source_target_pairs={{0,8},{1,9},{2,10},{3,11},{4,12},{5,13},{6,14},{7,15},{8,0},{9,1},... | collective-permute-start | bytes 454664 | tf_op jit(solution)/shard_map/ppermute | solution.py:197
  10.0 8.7 %collective-permute-start = (bf16[592,128]{1,0:T(8,128)(2,1)S(1)}, bf16[592,128]{1,0:T(8,128)(2,1)S(1)}, u32[]{:S(2)}, u32[]{:S(2)}) collective-permute-start(bf16[592,128]{1,0:T(8,128)(2,1)S(1)} %get-tuple-element.34.refs_0_), channel_id=1, source_target_pairs={{0,4},{1,5},{2,6},{3,7},{4,0},{5,1},{6,2},{7,3},{8,12},{9,13},{10,... | collective-permute-start | bytes 454664 | tf_op jit(solution)/shard_map/ppermute | solution.py:197
  15.9 11.4 %collective-permute-start.5 = (bf16[1424,128]{1,0:T(8,128)(2,1)S(1)}, bf16[1424,128]{1,0:T(8,128)(2,1)S(1)}, u32[]{:S(2)}, u32[]{:S(2)}) collective-permute-start(bf16[1424,128]{1,0:T(8,128)(2,1)S(1)} %collective-permute-done.4.refs_6_.refs_2_), channel_id=1, source_target_pairs={{0,1},{1,0},{2,3},{3,2},{4,5},{5,4},{6,7},{7,6},{8,9},{9,8},{10,11... | collective-permute-start | bytes 1093640 | tf_op jit(solution)/shard_map/ppermute | solution.py:197
  15.9 1.0 %copy-start.1 = (bf16[1,128,2,512]{3,2,1,0:T(2,128)(2,1)S(1)}, bf16[1,128,2,512]{3,2,1,0:T(2,128)(2,1)}, u32[]{:S(2)}) copy-start(bf16[1,128,2,512]{3,2,1,0:T(2,128)(2,1)} %param.10) | copy-start | bytes 786436
  16.9 0.9 %copy-start.2 = (bf16[2,512,128]{2,1,0:T(8,128)(2,1)S(1)}, bf16[2,512,128]{2,1,0:T(8,128)(2,1)}, u32[]{:S(2)}) copy-start(bf16[2,512,128]{2,1,0:T(8,128)(2,1)} %refs_4_.1) | copy-start | bytes 786436
  18.7 3.9 %collective-permute-start.6 = (bf16[2,128,128]{2,1,0:T(8,128)(2,1)S(1)}, bf16[2,128,128]{2,1,0:T(8,128)(2,1)S(1)}, u32[]{:S(2)}, u32[]{:S(2)}) collective-permute-start(bf16[2,128,128]{2,1,0:T(8,128)(2,1)S(1)} %get-tuple-element.44), channel_id=1, source_target_pairs={{0,1},{1,0},{2,3},{3,2},{4,5},{5,4},{6,7},{7,6},{8,9},{9,8},{10,11... | collective-permute-start | bytes 196616 | tf_op jit(solution)/shard_map/ppermute | solution.py:197
  19.3 4.3 %collective-permute-start.7 = (bf16[2,128,128]{2,1,0:T(8,128)(2,1)S(1)}, bf16[2,128,128]{2,1,0:T(8,128)(2,1)S(1)}, u32[]{:S(2)}, u32[]{:S(2)}) collective-permute-start(bf16[2,128,128]{2,1,0:T(8,128)(2,1)S(1)} %get-tuple-element.45), channel_id=1, source_target_pairs={{0,2},{1,3},{2,0},{3,1},{4,6},{5,7},{6,4},{7,5},{8,10},{9,11},{10,... | collective-permute-start | bytes 196616 | tf_op jit(solution)/shard_map/ppermute | solution.py:197
  21.0 4.4 %collective-permute-start.8 = (bf16[2,128,128]{2,1,0:T(8,128)(2,1)S(1)}, bf16[2,128,128]{2,1,0:T(8,128)(2,1)S(1)}, u32[]{:S(2)}, u32[]{:S(2)}) collective-permute-start(bf16[2,128,128]{2,1,0:T(8,128)(2,1)S(1)} %get-tuple-element.46), channel_id=1, source_target_pairs={{0,3},{1,2},{2,1},{3,0},{4,7},{5,6},{6,5},{7,4},{8,11},{9,10},{10,... | collective-permute-start | bytes 196616 | tf_op jit(solution)/shard_map/ppermute | solution.py:197
  21.0 6.3 %collective-permute-start.2 = (bf16[592,128]{1,0:T(8,128)(2,1)S(1)}, bf16[592,128]{1,0:T(8,128)(2,1)S(1)}, u32[]{:S(2)}, u32[]{:S(2)}) collective-permute-start(bf16[592,128]{1,0:T(8,128)(2,1)S(1)} %collective-permute-done.1.refs_2_), channel_id=1, source_target_pairs={{0,4},{1,5},{2,6},{3,7},{4,0},{5,1},{6,2},{7,3},{8,12},{9,13},{10,... | collective-permute-start | bytes 454664 | tf_op jit(solution)/shard_map/ppermute | solution.py:197
  25.4 4.3 %collective-permute-start.9 = (bf16[2,128,128]{2,1,0:T(8,128)(2,1)S(1)}, bf16[2,128,128]{2,1,0:T(8,128)(2,1)S(1)}, u32[]{:S(2)}, u32[]{:S(2)}) collective-permute-start(bf16[2,128,128]{2,1,0:T(8,128)(2,1)S(1)} %multiply_convert_fusion), channel_id=1, source_target_pairs={{0,4},{1,5},{2,6},{3,7},{4,0},{5,1},{6,2},{7,3},{8,12},{9,13},{10,... | collective-permute-start | bytes 196616 | tf_op jit(solution)/shard_map/ppermute | solution.py:244
  29.8 5.8 %collective-permute-start.10 = (bf16[2,128,128]{2,1,0:T(8,128)(2,1)S(1)}, bf16[2,128,128]{2,1,0:T(8,128)(2,1)S(1)}, u32[]{:S(2)}, u32[]{:S(2)}) collective-permute-start(bf16[2,128,128]{2,1,0:T(8,128)(2,1)S(1)} %add_convert_fusion.6), channel_id=1, source_target_pairs={{0,8},{1,9},{2,10},{3,11},{4,12},{5,13},{6,14},{7,15},{8,0},{9,1},... | collective-permute-start | bytes 196616 | tf_op jit(solution)/shard_map/ppermute | solution.py:244
  32.5 3.1 %collective-permute-start.13 = (f32[16,128]{1,0:T(8,128)S(1)}, f32[16,128]{1,0:T(8,128)S(1)}, u32[]{:S(2)}, u32[]{:S(2)}) collective-permute-start(f32[16,128]{1,0:T(8,128)S(1)} %get-tuple-element.54.refs_8_), channel_id=1, source_target_pairs={{0,3},{1,2},{2,1},{3,0},{4,7},{5,6},{6,5},{7,4},{8,11},{9,10},{10,... | collective-permute-start | bytes 24584 | tf_op jit(solution)/shard_map/ppermute | solution.py:197
  32.8 3.7 %collective-permute-start.12 = (f32[16,128]{1,0:T(8,128)S(1)}, f32[16,128]{1,0:T(8,128)S(1)}, u32[]{:S(2)}, u32[]{:S(2)}) collective-permute-start(f32[16,128]{1,0:T(8,128)S(1)} %get-tuple-element.54.refs_8_), channel_id=1, source_target_pairs={{0,2},{1,3},{2,0},{3,1},{4,6},{5,7},{6,4},{7,5},{8,10},{9,11},{10,... | collective-permute-start | bytes 24584 | tf_op jit(solution)/shard_map/ppermute | solution.py:197
  33.6 2.9 %collective-permute-start.11 = (f32[16,128]{1,0:T(8,128)S(1)}, f32[16,128]{1,0:T(8,128)S(1)}, u32[]{:S(2)}, u32[]{:S(2)}) collective-permute-start(f32[16,128]{1,0:T(8,128)S(1)} %get-tuple-element.54.refs_8_), channel_id=1, source_target_pairs={{0,1},{1,0},{2,3},{3,2},{4,5},{5,4},{6,7},{7,6},{8,9},{9,8},{10,11... | collective-permute-start | bytes 24584 | tf_op jit(solution)/shard_map/ppermute | solution.py:197
  39.8 10.8 %collective-permute-start.14 = (bf16[4,576,128]{2,1,0:T(8,128)(2,1)S(1)}, bf16[4,576,128]{2,1,0:T(8,128)(2,1)S(1)}, u32[]{:S(2)}, u32[]{:S(2)}) collective-permute-start(bf16[4,576,128]{2,1,0:T(8,128)(2,1)S(1)} %get-tuple-element.58), channel_id=1, source_target_pairs={{0,1},{1,0},{2,3},{3,2},{4,5},{5,4},{6,7},{7,6},{8,9},{9,8},{10,11... | collective-permute-start | bytes 1769480 | tf_op jit(solution)/shard_map/ppermute | solution.py:197
  39.9 4.5 %collective-permute-start.19 = (bf16[2,128,128]{2,1,0:T(8,128)(2,1)S(1)}, bf16[2,128,128]{2,1,0:T(8,128)(2,1)S(1)}, u32[]{:S(2)}, u32[]{:S(2)}) collective-permute-start(bf16[2,128,128]{2,1,0:T(8,128)(2,1)S(1)} %add_convert_fusion.5), channel_id=1, source_target_pairs={{0,16},{16,0},{1,17},{17,1},{2,18},{18,2},{3,19},{19,3},{4,20},{20... | collective-permute-start | bytes 196616 | tf_op jit(solution)/shard_map/ppermute | solution.py:244
  41.4 13.3 %collective-permute-start.16 = (bf16[576,128]{1,0:T(8,128)(2,1)S(1)}, bf16[576,128]{1,0:T(8,128)(2,1)S(1)}, u32[]{:S(2)}, u32[]{:S(2)}) collective-permute-start(bf16[576,128]{1,0:T(8,128)(2,1)S(1)} %get-tuple-element.61), channel_id=1, source_target_pairs={{0,4},{1,5},{2,6},{3,7},{4,0},{5,1},{6,2},{7,3},{8,12},{9,13},{10,... | collective-permute-start | bytes 442376 | tf_op jit(solution)/shard_map/ppermute | solution.py:197
  43.0 7.5 %collective-permute-start.17 = (bf16[576,128]{1,0:T(8,128)(2,1)S(1)}, bf16[576,128]{1,0:T(8,128)(2,1)S(1)}, u32[]{:S(2)}, u32[]{:S(2)}) collective-permute-start(bf16[576,128]{1,0:T(8,128)(2,1)S(1)} %get-tuple-element.63), channel_id=1, source_target_pairs={{0,4},{1,5},{2,6},{3,7},{4,0},{5,1},{6,2},{7,3},{8,12},{9,13},{10,... | collective-permute-start | bytes 442376 | tf_op jit(solution)/shard_map/ppermute | solution.py:197
  44.4 8.0 %collective-permute-start.22 = (bf16[2,128,128]{2,1,0:T(8,128)(2,1)S(1)}, bf16[2,128,128]{2,1,0:T(8,128)(2,1)S(1)}, u32[]{:S(2)}, u32[]{:S(2)}) collective-permute-start(bf16[2,128,128]{2,1,0:T(8,128)(2,1)S(1)} %add_convert_fusion.4.refs_0_), channel_id=1, source_target_pairs={{0,3},{1,2},{2,1},{3,0},{4,7},{5,6},{6,5},{7,4},{8,11},{9,10},{10,... | collective-permute-start | bytes 196616 | tf_op jit(solution)/shard_map/ppermute | solution.py:197
  44.7 9.2 %collective-permute-start.21 = (bf16[2,128,128]{2,1,0:T(8,128)(2,1)S(1)}, bf16[2,128,128]{2,1,0:T(8,128)(2,1)S(1)}, u32[]{:S(2)}, u32[]{:S(2)}) collective-permute-start(bf16[2,128,128]{2,1,0:T(8,128)(2,1)S(1)} %add_convert_fusion.4.refs_0_), channel_id=1, source_target_pairs={{0,2},{1,3},{2,0},{3,1},{4,6},{5,7},{6,4},{7,5},{8,10},{9,11},{10,... | collective-permute-start | bytes 196616 | tf_op jit(solution)/shard_map/ppermute | solution.py:197
  50.5 3.4 %collective-permute-start.20 = (bf16[2,128,128]{2,1,0:T(8,128)(2,1)S(1)}, bf16[2,128,128]{2,1,0:T(8,128)(2,1)S(1)}, u32[]{:S(2)}, u32[]{:S(2)}) collective-permute-start(bf16[2,128,128]{2,1,0:T(8,128)(2,1)S(1)} %add_convert_fusion.4.refs_0_), channel_id=1, source_target_pairs={{0,1},{1,0},{2,3},{3,2},{4,5},{5,4},{6,7},{7,6},{8,9},{9,8},{10,11... | collective-permute-start | bytes 196616 | tf_op jit(solution)/shard_map/ppermute | solution.py:197
  50.6 10.4 %collective-permute-start.18 = (bf16[576,128]{1,0:T(8,128)(2,1)S(1)}, bf16[576,128]{1,0:T(8,128)(2,1)S(1)}, u32[]{:S(2)}, u32[]{:S(2)}) collective-permute-start(bf16[576,128]{1,0:T(8,128)(2,1)S(1)} %add_convert_fusion.3), channel_id=1, source_target_pairs={{0,8},{1,9},{2,10},{3,11},{4,12},{5,13},{6,14},{7,15},{8,0},{9,1},... | collective-permute-start | bytes 442376 | tf_op jit(solution)/shard_map/ppermute | solution.py:197
  52.4 9.3 %collective-permute-start.15 = (bf16[2,576,128]{2,1,0:T(8,128)(2,1)S(1)}, bf16[2,576,128]{2,1,0:T(8,128)(2,1)S(1)}, u32[]{:S(2)}, u32[]{:S(2)}) collective-permute-start(bf16[2,576,128]{2,1,0:T(8,128)(2,1)S(1)} %add_convert_fusion.1), channel_id=1, source_target_pairs={{0,2},{1,3},{2,0},{3,1},{4,6},{5,7},{6,4},{7,5},{8,10},{9,11},{10,... | collective-permute-start | bytes 884744 | tf_op jit(solution)/shard_map/ppermute | solution.py:197

commit v3 on v2

--- a/solution.py
+++ b/solution.py
@@ -12,6 +12,7 @@
 HEAD_DIM = 128
 GROUP = 4
 EXTRA = 16
+PACK_LIMIT = 63 << 20
 F32 = jnp.float32
 BF16 = jnp.bfloat16
 
@@ -28,42 +29,60 @@
     return math.prod(shape) * jnp.dtype(dtype).itemsize
 
 
-def call(kernel, name, outs, args, scratch=(), flops=0, smem=()):
-    specs = [
-        pl.BlockSpec(memory_space=pltpu.SMEM if i in smem else pltpu.VMEM) for i in range(len(args))
-    ]
+def call(kernel, name, outs, args, scratch=(), flops=0, smem=(), hbm=(), copies=0, limit=None):
+    def place(i):
+        return pltpu.SMEM if i in smem else pltpu.HBM if i in hbm else pltpu.VMEM
+
     moved = sum(size_of(a.shape, a.dtype) for a in args) + sum(size_of(*o) for o in outs)
     held = moved + sum(size_of(*s) for s in scratch)
+    semaphores = [pltpu.SemaphoreType.DMA((copies,))] if copies else []
     return pl.pallas_call(
         kernel,
         out_shape=[jax.ShapeDtypeStruct(s, d) for s, d in outs],
-        in_specs=specs,
+        in_specs=[pl.BlockSpec(memory_space=place(i)) for i in range(len(args))],
         out_specs=[pl.BlockSpec(memory_space=pltpu.VMEM) for _ in outs],
-        scratch_shapes=[pltpu.VMEM(s, d) for s, d in scratch],
-        compiler_params=pltpu.CompilerParams(vmem_limit_bytes=int(1.2 * held) + (8 << 20)),
+        scratch_shapes=[pltpu.VMEM(s, d) for s, d in scratch] + semaphores,
+        compiler_params=pltpu.CompilerParams(vmem_limit_bytes=limit or int(1.2 * held) + (8 << 20)),
         cost_estimate=pl.CostEstimate(flops=flops, bytes_accessed=moved, transcendentals=0),
         name=name,
     )(*args)
 
 
-def pack_kernel(pos_ref, q_ref, og_ref, lat_ref, lat_msg_ref, msg_ref):
-    heads, width, tok = q_ref.shape
-    lat_msg_ref[:width, :] = lat_ref[...]
-    lat_msg_ref[width:, :] = pos_ref[...]
+def fetch(pairs, sems):
+    copies = [pltpu.make_async_copy(src, dst, sems.at[i]) for i, (src, dst) in enumerate(pairs)]
+    for copy in copies:
+        copy.start()
+    return copies
+
+
+def pack_kernel(
+    idx_ref, pos_hbm, q_hbm, og_hbm, lat_hbm, attn_hbm, wuv_hbm,
+    lat_msg, q_msg, delta_ref, term_ref,
+    pos_ref, og_ref, attn_ref, wuv_ref, term, sems,
+):
+    heads, width, tok = q_hbm.shape
+    pairs = [(pos_hbm, pos_ref), (og_hbm, og_ref), (wuv_hbm, wuv_ref), (attn_hbm, attn_ref)]
+    pairs += [(lat_hbm, lat_msg.at[pl.ds(0, width), :])]
+    pairs += [(q_hbm.at[h], q_msg.at[pl.ds(h * width, width), :]) for h in range(heads)]
+    copies = [pltpu.make_async_copy(src, dst, sems.at[i]) for i, (src, dst) in enumerate(pairs)]
+    for copy in copies:
+        copy.start()
+    copies[0].wait()
+    pos = jnp.broadcast_to(pos_ref[...], (EXTRA, tok))
+    row = lax.broadcasted_iota(jnp.int32, (EXTRA, tok), 0)
+    high = lax.shift_right_logical(pos, 6)
+    both = jnp.where(row == 0, high, jnp.where(row == 1, pos - high * 64, 0))
+    rows = both.astype(F32).astype(BF16)
+    lat_msg[width:, :] = rows
+    q_msg[heads * (width + HEAD_DIM) :, :] = rows
+    delta_ref[...] = jnp.zeros_like(delta_ref)
+    for copy in copies[1:4]:
+        copy.wait()
+    _, lat, _ = wuv_ref.shape
     for h in range(heads):
-        msg_ref[h * width : (h + 1) * width, :] = q_ref[h]
+        og = og_ref[:, h, :].T
         at = heads * width + h * HEAD_DIM
-        msg_ref[at : at + HEAD_DIM, :] = og_ref[:, h, :].T
-    msg_ref[heads * (width + HEAD_DIM) :, :] = pos_ref[...]
-
-
-def own_kernel(width, idx_ref, attn_ref, msg_ref, wuv_ref, delta_ref, *rest):
-    chunks, term = rest[:GROUP], rest[GROUP]
-    heads, lat, _ = wuv_ref.shape
-    delta_ref[...] = jnp.zeros_like(delta_ref)
-    for h in range(heads):
-        at = heads * width + h * HEAD_DIM
-        og = msg_ref[at : at + HEAD_DIM, :]
+        q_msg[at : at + HEAD_DIM, :] = og
         attn = attn_ref[:, h, :].T
         g = mm(wuv_ref[h], og).astype(BF16).astype(F32)
         delta_ref[h : h + 1, :] = jnp.sum(g * attn.astype(F32), axis=0, keepdims=True)
@@ -72,7 +91,9 @@
     me = lax.rem(idx_ref[0], GROUP)
     for k in range(GROUP):
         at = pl.multiple_of(jnp.bitwise_xor(me, k) * step, step)
-        chunks[k][...] = term[:, pl.ds(at, step), :].astype(BF16)
+        term_ref[k * heads : (k + 1) * heads] = term[:, pl.ds(at, step), :].astype(BF16)
+    for copy in copies[4:]:
+        copy.wait()
 
 
 def score_kernel(factor, nkey, width, heads, *refs):
@@ -173,13 +194,13 @@
         part_refs[a][lat:, :] = along[lat:].astype(BF16)
 
 
-def spread_kernel(idx_ref, *refs):
+def spread_kernel(scale, idx_ref, *refs):
     chunks, out_ref = refs[:GROUP], refs[GROUP]
     step = chunks[0].shape[1]
     me = lax.rem(idx_ref[0], GROUP)
     for k in range(GROUP):
         at = pl.multiple_of(jnp.bitwise_xor(me, k) * step, step)
-        out_ref[:, pl.ds(at, step), :] = chunks[k][...].astype(F32)
+        out_ref[:, pl.ds(at, step), :] = chunks[k][...].astype(F32) * scale
 
 
 def body(n_ctx, n_dp, positions, queries, latent, out_grad, attn_out, wuv):
@@ -200,76 +221,96 @@
         return lax.optimization_barrier((x, done))[0]
 
     idx = lax.axis_index("ctx").reshape(1)
-    pos_rows = jnp.concatenate(
-        [positions // 64, positions % 64, jnp.zeros((EXTRA - 2, tok), positions.dtype)], axis=0
-    ).astype(BF16)
-    lat_msg, q_msg = call(
+    step = lat // GROUP
+    lat_msg, q_msg, delta, term = call(
         pack_kernel,
         "pack",
-        [((width + EXTRA, tok), BF16), ((heads * (width + HEAD_DIM) + EXTRA, tok), BF16)],
-        [pos_rows, jnp.transpose(queries[0], (1, 2, 0)), out_grad[0], latent[0].T],
-    )
-    held, firsts = {0: lat_msg}, []
-    for bit in reversed(range(line_bits)):
-        first = swap(lat_msg, GROUP << bit)
-        ahead = {m: after(x, first) for m, x in held.items() if m}
-        held.update({m | 1 << bit: swap(x, GROUP << bit) for m, x in ahead.items()})
-        held[1 << bit] = first
-        firsts.append(first)
-    lats = [held[m] for m in range(lines)]
+        [
+            ((width + EXTRA, tok), BF16),
+            ((heads * (width + HEAD_DIM) + EXTRA, tok), BF16),
+            ((8, tok), F32),
+            ((GROUP * heads, step, HEAD_DIM), BF16),
+        ],
+        [
+            idx,
+            positions,
+            jnp.transpose(queries[0], (1, 2, 0)),
+            out_grad[0],
+            latent[0].T,
+            attn_out[0],
+            wuv,
+        ],
+        [
+            ((1, tok), jnp.int32),
+            (out_grad.shape[1:], BF16),
+            (attn_out.shape[1:], BF16),
+            (wuv.shape, BF16),
+            ((heads, lat, HEAD_DIM), F32),
+        ],
+        smem=(0,),
+        hbm=(1, 2, 3, 4, 5, 6),
+        copies=5 + heads,
+        limit=PACK_LIMIT,
+    )
+
+    def hop(total, axis, size, mask, *done):
+        other = lax.ppermute(total, axis, [(i, i ^ mask) for i in range(size)])
+        return total, after(other, *done) if done else other
+
+    def add(pair):
+        return (pair[0].astype(F32) + pair[1].astype(F32)).astype(BF16)
+
+    dp_hops = [("dp", n_dp, 1 << bit) for bit in range((n_dp - 1).bit_length())]
+    line_hops = [("ctx", n_ctx, GROUP << bit) for bit in range(line_bits)]
+
+    firsts = {1 << bit: swap(lat_msg, GROUP << bit) for bit in range(line_bits)}
     q_across = swap(q_msg, 2)
     q_core = swap(q_msg, 1)
-    q_far = swap(after(q_across, q_core), 1)
+    twins = hop(term, *dp_hops[0])
+    firsts, q_across, q_core, twins = lax.optimization_barrier((firsts, q_across, q_core, twins))
+    for step_hop in dp_hops[1:]:
+        twins = hop(add(twins), *step_hop)
+    total = add(twins)
+
+    held = {0: lat_msg}
+    for bit in reversed(range(line_bits)):
+        held.update({m | 1 << bit: swap(x, GROUP << bit) for m, x in held.items() if m})
+        held[1 << bit] = firsts[1 << bit]
+    lats = [held[m] for m in range(lines)]
+    q_far = swap(q_across, 1)
+    half = 2 * heads
+    got_half = swap(total[half:], 2)
+    lats, q_far, got_half = lax.optimization_barrier((lats, q_far, got_half))
     qs = [q_msg, q_core, q_across, q_far]
-
-    step = lat // GROUP
-    delta, *chunks = call(
-        functools.partial(own_kernel, width),
-        "own_rows",
-        [((8, tok), F32)] + [((heads, step, HEAD_DIM), BF16)] * GROUP,
-        [idx, attn_out[0], q_msg, wuv],
-        [((heads, lat, HEAD_DIM), F32)],
-        flops=4 * rows * lat * HEAD_DIM,
-        smem=(0,),
-    )
-    chunks = after(chunks, *firsts, q_core, q_across)
-    got = [chunks[0]] + [swap(chunks[k], k) for k in range(1, GROUP)]
-    scale = 1.0 / math.sqrt(tok * n_ctx * n_dp)
-    mine = (sum(c.astype(F32) for c in got) * scale).astype(BF16)
-    hops = [("ctx", n_ctx, GROUP << bit) for bit in range(line_bits)]
-    hops += [("dp", n_dp, 1 << bit) for bit in range((n_dp - 1).bit_length())]
-
-    def climb(total, steps, *done):
-        for axis, size, mask in steps:
-            other = lax.ppermute(total, axis, [(i, i ^ mask) for i in range(size)])
-            other = after(other, *done)
-            total = (total.astype(F32) + other.astype(F32)).astype(BF16)
-        return total
+    total = add((total[:half], got_half))
+    got_own = swap(total[heads:], 1)
 
     s, k_nat, stat = call(
         functools.partial(score_kernel, factor, lines, width, heads),
         "scores",
         [((keys, all_rows), F32), ((keys, wide), BF16), ((EXTRA, tok), F32)],
-        lats + qs + [after(delta, mine)],
+        lats + qs + [delta],
         [((wide, keys), BF16), ((wide, rows), BF16)],
         flops=2 * keys * all_rows * wide,
     )
     stats = [stat] + [swap(stat, k) for k in range(1, GROUP)]
-    mine = climb(mine, hops[:1], stat)
+    mine = add((total[:heads], after(got_own, stat)))
+    near = hop(mine, *line_hops[0])
     g, gp = call(
         functools.partial(context_kernel, width, heads),
         "context",
         [((lat, all_rows), BF16), ((keys, all_rows), F32)],
-        qs + [wuv, after(k_nat, mine)],
+        qs + [wuv, k_nat],
         flops=2 * keys * all_rows * lat + 2 * all_rows * lat * HEAD_DIM,
     )
-    mine = climb(mine, hops[1:-1], gp)
+    mine = add((near[0], after(near[1], gp)))
+    mine, stats = lax.optimization_barrier((mine, stats))
     outs = call(
         functools.partial(grad_kernel, factor, lines, width, heads),
         "gradients",
         [((width, tok), BF16)] * lines
         + [((heads, width, tok), BF16), ((2 * heads, width, tok), BF16), ((heads, width, tok), BF16)],
-        lats + qs + [after(stats[0], mine)] + stats[1:] + [s, gp, g],
+        lats + qs + stats + [s, gp, g],
         [
             ((width, keys), BF16),
             ((width, all_rows), BF16),
@@ -279,24 +320,26 @@
         flops=2 * keys * all_rows * (2 * width + lat),
     )
     parts, (gq_own, gq_core, gq_across) = list(outs[:lines]), outs[lines:]
-    mine = climb(mine, hops[-1:], gq_own)
     kept = [parts[0]]
+    gq_got = swap(gq_core, 1)
+    for step_hop in line_hops[1:]:
+        mine = add(hop(after(mine, gq_own), *step_hop))
     for bit in range(line_bits):
-        for m in reversed(range(1 << bit, lines, 2 << bit)):
-            got_part = swap(parts[m], GROUP << bit)
-            target = m ^ 1 << bit
-            if target:
-                parts[target] = (parts[target].astype(F32) + got_part.astype(F32)).astype(BF16)
-            else:
-                kept.append(got_part)
-    gq_got = swap(gq_core, 1)
-    gq_sum = (gq_across.astype(F32) + gq_got[heads:].astype(F32)).astype(BF16)
-    gq_last = swap(gq_sum, 2)
+        for m in [m for m in range(2 << bit, lines) if m >> bit & 1 and not m & (1 << bit) - 1]:
+            parts[m ^ 1 << bit] = add((parts[m ^ 1 << bit], swap(parts[m], GROUP << bit)))
+        if bit == 0:
+            parts, gq_got, mine = lax.optimization_barrier((parts, gq_got, mine))
+    kept += [swap(parts[1 << bit], GROUP << bit) for bit in reversed(range(line_bits))]
+    gq_last = swap(add((gq_across, gq_got[heads:])), 2)
+    mine_two = jnp.concatenate([mine, swap(mine, 2)], axis=0)
+    kept, gq_last, mine_two = lax.optimization_barrier((kept, gq_last, mine_two))
+    other_two = swap(mine_two, 1)
     grad_lat = sum(p.astype(F32) for p in kept).astype(BF16)
     grad_q = sum(p.astype(F32) for p in (gq_own, gq_got[:heads], gq_last)).astype(BF16)
-    pieces = [mine] + [swap(mine, k) for k in range(1, GROUP)]
+    scale = 1.0 / math.sqrt(tok * n_ctx * n_dp)
+    pieces = [mine_two[:heads], other_two[:heads], mine_two[heads:], other_two[heads:]]
     (grad_w,) = call(
-        spread_kernel, "spread", [((heads, lat, HEAD_DIM), F32)], [idx] + pieces, smem=(0,)
+        functools.partial(spread_kernel, scale), "spread", [((heads, lat, HEAD_DIM), F32)], [idx] + pieces, smem=(0,)
     )
     return (jnp.transpose(grad_q, (2, 0, 1))[None], grad_lat.T[None], grad_w)
 

time: 62.8 us -> 62.5 us (level)
  starting transfers between devices: 25.5 us -> 22.4 us
  waiting for transfers between devices: 21 us -> 23.5 us
  local copies, waits for them, and re-layouts: 4.69 us -> 2.63 us
  Pallas kernels: 8.04 us -> 10 us
    ppermute x3, waiting for transfers between devices: 1.78 us -> 3.86 us  [hop(): other = lax.ppermute(total, axis, [(i, i ^ mask) for i in range(size)])]
    unnamed x12, local copies, waits for them, and re-layouts: 4.61 us -> 2.59 us
    pallas_call x6 -> x5, Pallas kernels: 8.04 us -> 10 us  [call(): pl.pallas_call(kernel, out_shape=[jax.ShapeDtypeStruct(s, d) for s, d in...]
    ppermute x20 -> x18, starting transfers between devices: 19.7 us -> 17.9 us  [swap(): return lax.ppermute(x, 'ctx', [(i, i ^ mask) for i in range(n_ctx)])]
    ppermute x3, starting transfers between devices: 5.85 us -> 4.54 us  [hop(): other = lax.ppermute(total, axis, [(i, i ^ mask) for i in range(size)])]
    convert_element_type x6 -> x7, other arithmetic: 0.23 us -> 1.25 us  [add(): return (pair[0].astype(F32) + pair[1].astype(F32)).astype(BF16)]
    another operation x1 -> x0, other arithmetic: 0.67 us -> none
    ppermute x20 -> x18, waiting for transfers between devices: 19.2 us -> 19.7 us  [swap(): return lax.ppermute(x, 'ctx', [(i, i ^ mask) for i in range(n_ctx)])]
  transfers between devices with their start and end apart: 23 -> 21, of which waited for: 9 -> 9; matrix products, arithmetic and copies ran while one was open for 1% -> 3% of each run, Pallas kernels for 7% -> 5%
where the time goes in v3:
time: 62.5 us; the launch traced here: 62.2 us
  waiting for transfers between devices  23.5 us (38%)
  starting transfers between devices  22.4 us (36%)
  Pallas kernels  10 us (16%)
  other arithmetic  2.82 us (5%)
  local copies, waits for them, and re-layouts  2.63 us (4%)
  between operations  0.79 us (1%)
    ppermute x18, waiting for transfers between devices, swap(): return lax.ppermute(x, 'ctx', [(i, i ^ mask) for i in range(n_ctx)])  19.7 us
    ppermute x18, starting transfers between devices, swap(): return lax.ppermute(x, 'ctx', [(i, i ^ mask) for i in range(n_ctx)])  17.9 us
    pallas_call x5, Pallas kernels, call(): pl.pallas_call(kernel, out_shape=[jax.ShapeDtypeStruct(s, d) for s, d in...  10 us
    ppermute x3, starting transfers between devices, hop(): other = lax.ppermute(total, axis, [(i, i ^ mask) for i in range(size)])  4.54 us
    ppermute x3, waiting for transfers between devices, hop(): other = lax.ppermute(total, axis, [(i, i ^ mask) for i in range(size)])  3.86 us
    unnamed x12, local copies, waits for them, and re-layouts  2.59 us
    broadcast_in_dim x2, other arithmetic, body(): return (jnp.transpose(grad_q, (2, 0, 1))[None], grad_lat.T[None], grad_w)  1.56 us
  transfers between devices with their start and end apart: 21, of which 9 were waited for; matrix products, arithmetic and copies ran while one was open for 3% of the time, Pallas kernels for 5%

profile of v3, /device:TPU:0, one launch (start us, length us, event | category | flops | bytes accessed | tf_op | source)
XLA Modules:
  0.0 62.2 jit_solution(9148019601476057141)
XLA Ops:
  0.6 3.0 %pack.1 = (bf16[592,128]{1,0:T(8,128)(2,1)}, bf16[1424,128]{1,0:T(8,128)(2,1)}, f32[8,128]{1,0:T(8,128)}, bf16[8,128,128]{2,1,0:T(8,128)(2,1)}) custom-call(s32[1]{0:T(128)} %bitcast.idx_ref, s32[1,128]{1,0:T(1,128)} %pos_hbm.1, bf16[2,576,128]{2,1,0:T(8,128)(2,1)} %bitcast.17, bf16[128,2,128]{2,1,0:T(2,128)(2,1)} %bitcast.20, bf16[576,128]{1,0:T(8,128)(2,1)} %bitcast.19, ...), custom_call_target="tpu_custom_call" | custom-call | bytes 1815044 | tf_op jit(solution)/shard_map/pack/pallas_call | solution.py:39
  3.7 0.5 collective-permute-start.3
  4.2 2.6 %collective-permute-start.2 = (bf16[1424,128]{1,0:T(8,128)(2,1)}, bf16[1424,128]{1,0:T(8,128)(2,1)S(1)}, u32[]{:S(2)}, u32[]{:S(2)}) collective-permute-start(bf16[1424,128]{1,0:T(8,128)(2,1)} %get-tuple-element.49.refs_4_.refs_0_), channel_id=1, source_target_pairs={{0,2},{1,3},{2,0},{3,1},{4,6},{5,7},{6,4},{7,5},{8,10},{9,11},{10,... | collective-permute-start | bytes 1093640 | tf_op jit(solution)/shard_map/ppermute | solution.py:218
  6.8 1.5 %collective-permute-start.4 = (bf16[8,128,128]{2,1,0:T(8,128)(2,1)}, bf16[8,128,128]{2,1,0:T(8,128)(2,1)S(1)}, u32[]{:S(2)}, u32[]{:S(2)}) collective-permute-start(bf16[8,128,128]{2,1,0:T(8,128)(2,1)} %get-tuple-element.54), channel_id=1, source_target_pairs={{0,16},{16,0},{1,17},{17,1},{2,18},{18,2},{3,19},{19,3},{4,20},{20... | collective-permute-start | bytes 786440 | tf_op jit(solution)/shard_map/ppermute | solution.py:257
  8.3 0.0 copy-start.1
  8.3 0.0 copy-start.2
  8.3 2.6 %collective-permute-start.1 = (bf16[592,128]{1,0:T(8,128)(2,1)}, bf16[592,128]{1,0:T(8,128)(2,1)S(1)}, u32[]{:S(2)}, u32[]{:S(2)}) collective-permute-start(bf16[592,128]{1,0:T(8,128)(2,1)} %get-tuple-element.56.refs_0_), channel_id=1, source_target_pairs={{0,8},{1,9},{2,10},{3,11},{4,12},{5,13},{6,14},{7,15},{8,0},{9,1},... | collective-permute-start | bytes 454664 | tf_op jit(solution)/shard_map/ppermute | solution.py:218
  10.9 1.6 %collective-permute-start = (bf16[592,128]{1,0:T(8,128)(2,1)}, bf16[592,128]{1,0:T(8,128)(2,1)S(1)}, u32[]{:S(2)}, u32[]{:S(2)}) collective-permute-start(bf16[592,128]{1,0:T(8,128)(2,1)} %get-tuple-element.56.refs_0_), channel_id=1, source_target_pairs={{0,4},{1,5},{2,6},{3,7},{4,0},{5,1},{6,2},{7,3},{8,12},{9,13},{10,... | collective-permute-start | bytes 454664 | tf_op jit(solution)/shard_map/ppermute | solution.py:218
  12.5 6.0 %collective-permute-done.1.refs_2_ = bf16[592,128]{1,0:T(8,128)(2,1)S(1)} collective-permute-done((bf16[592,128]{1,0:T(8,128)(2,1)}, bf16[592,128]{1,0:T(8,128)(2,1)S(1)}, u32[]{:S(2)}, u32[]{:S(2)}) %collective-permute-start.1) | collective-permute-done | bytes 151584 | tf_op jit(solution)/shard_map/ppermute | solution.py:218
  18.5 0.2 collective-permute-done.refs_1_
  18.7 0.0 collective-permute-done.4
  18.7 0.0 collective-permute-done.3.refs_5_.refs_1_
  18.7 0.0 collective-permute-done.2.refs_6_.refs_2_
  18.7 1.5 %collective-permute-start.5 = (bf16[592,128]{1,0:T(8,128)(2,1)S(1)}, bf16[592,128]{1,0:T(8,128)(2,1)S(1)}, u32[]{:S(2)}, u32[]{:S(2)}) collective-permute-start(bf16[592,128]{1,0:T(8,128)(2,1)S(1)} %collective-permute-done.1.refs_2_), channel_id=1, source_target_pairs={{0,4},{1,5},{2,6},{3,7},{4,0},{5,1},{6,2},{7,3},{8,12},{9,13},{10,... | collective-permute-start | bytes 454664 | tf_op jit(solution)/shard_map/ppermute | solution.py:218
  20.2 0.0 collective-permute-start.6
  20.2 1.0 %add_convert_fusion.2 = bf16[8,128,128]{2,1,0:T(8,128)(2,1)S(1)} fusion(bf16[8,128,128]{2,1,0:T(8,128)(2,1)S(1)} %collective-permute-done.4, bf16[8,128,128]{2,1,0:T(8,128)(2,1)} %get-tuple-element.54), kind=kLoop, calls=%fused_computation.2 | loop fusion | flops 524288 | bytes 786432 | tf_op jit(solution)/shard_map/convert_element_type | solution.py:261
  21.2 0.6 collective-permute-start.7
  21.8 5.4 %collective-permute-done.7 = bf16[4,128,128]{2,1,0:T(8,128)(2,1)S(1)} collective-permute-done((bf16[4,128,128]{2,1,0:T(8,128)(2,1)S(1)}, bf16[4,128,128]{2,1,0:T(8,128)(2,1)S(1)}, u32[]{:S(2)}, u32[]{:S(2)}) %collective-permute-start.7) | collective-permute-done | bytes 131104 | tf_op jit(solution)/shard_map/ppermute | solution.py:218
  27.2 0.0 collective-permute-done.5.refs_3_
  27.2 0.0 collective-permute-done.6.refs_7_.refs_3_
  27.3 0.1 collective-permute-start.8
  27.4 0.0 copy-start
  27.4 1.0 %copy-done = bf16[1424,128]{1,0:T(8,128)(2,1)S(1)} copy-done((bf16[1424,128]{1,0:T(8,128)(2,1)S(1)}, bf16[1424,128]{1,0:T(8,128)(2,1)}, u32[]{:S(2)}) %copy-start) | copy-done | bytes 364568
  28.4 0.0 copy-start.3
  28.4 0.9 %copy-done.3 = bf16[592,128]{1,0:T(8,128)(2,1)S(1)} copy-done((bf16[592,128]{1,0:T(8,128)(2,1)S(1)}, bf16[592,128]{1,0:T(8,128)(2,1)}, u32[]{:S(2)}) %copy-start.3) | copy-done | bytes 151576
  29.3 0.0 copy-start.5
  29.3 0.7 %copy-done.5 = f32[8,128]{1,0:T(8,128)S(1)} copy-done((f32[8,128]{1,0:T(8,128)S(1)}, f32[8,128]{1,0:T(8,128)}, u32[]{:S(2)}) %copy-start.5) | copy-done | bytes 4120
  30.0 0.0 copy-start.4
  30.0 1.6 %scores.1 = (f32[512,1024]{1,0:T(8,128)S(1)}, bf16[512,640]{1,0:T(8,128)(2,1)S(1)}, f32[16,128]{1,0:T(8,128)S(1)}) custom-call(bf16[592,128]{1,0:T(8,128)(2,1)S(1)} %copy-done.3, bf16[592,128]{1,0:T(8,128)(2,1)S(1)} %collective-permute-done.refs_1_, bf16[592,128]{1,0:T(8,128)(2,1)S(1)} %collective-permute-done.1.refs_2_, ...), custom_call_target="tpu_custom_call" | custom-call | flops 671088640 | bytes 4829184 | tf_op jit(solution)/shard_map/scores/pallas_call | solution.py:39
  31.6 0.0 collective-permute-done.8
  31.6 0.7 %collective-permute-start.9 = (bf16[2,128,128]{2,1,0:T(8,128)(2,1)S(1)}, bf16[2,128,128]{2,1,0:T(8,128)(2,1)S(1)}, u32[]{:S(2)}, u32[]{:S(2)}) collective-permute-start(bf16[2,128,128]{2,1,0:T(8,128)(2,1)S(1)} %add_convert_fusion.8), channel_id=1, source_target_pairs={{0,4},{1,5},{2,6},{3,7},{4,0},{5,1},{6,2},{7,3},{8,12},{9,13},{10,... | collective-permute-start | bytes 196616 | tf_op jit(solution)/shard_map/ppermute | solution.py:257
  32.3 0.3 collective-permute-start.12
  32.6 1.5 %collective-permute-start.11 = (f32[16,128]{1,0:T(8,128)S(1)}, f32[16,128]{1,0:T(8,128)S(1)}, u32[]{:S(2)}, u32[]{:S(2)}) collective-permute-start(f32[16,128]{1,0:T(8,128)S(1)} %get-tuple-element.69.refs_8_), channel_id=1, source_target_pairs={{0,2},{1,3},{2,0},{3,1},{4,6},{5,7},{6,4},{7,5},{8,10},{9,11},{10,... | collective-permute-start | bytes 24584 | tf_op jit(solution)/shard_map/ppermute | solution.py:218
  34.1 0.0 collective-permute-start.10
  34.1 0.0 copy-done.1
  34.1 0.0 copy-done.2
  34.1 1.2 %context.1 = (bf16[512,1024]{1,0:T(8,128)(2,1)S(1)}, f32[512,1024]{1,0:T(8,128)S(1)}) custom-call(bf16[1424,128]{1,0:T(8,128)(2,1)S(1)} %copy-done.1, bf16[1424,128]{1,0:T(8,128)(2,1)S(1)} %collective-permute-done.3.refs_5_.refs_1_, bf16[1424,128]{1,0:T(8,128)(2,1)S(1)} %collective-permute-done.2.refs_6_.refs_2_, ...), custom_call_target="tpu_custom_call" | custom-call | flops 671088640 | bytes 5521408 | tf_op jit(solution)/shard_map/context/pallas_call | solution.py:39
  35.4 0.8 %collective-permute-done.9 = bf16[2,128,128]{2,1,0:T(8,128)(2,1)S(1)} collective-permute-done((bf16[2,128,128]{2,1,0:T(8,128)(2,1)S(1)}, bf16[2,128,128]{2,1,0:T(8,128)(2,1)S(1)}, u32[]{:S(2)}, u32[]{:S(2)}) %collective-permute-start.9) | collective-permute-done | bytes 65568 | tf_op jit(solution)/shard_map/ppermute | solution.py:257
  36.2 0.0 collective-permute-done.12.refs_11_
  36.2 0.0 collective-permute-done.11.refs_10_
  36.2 0.0 collective-permute-done.10.refs_9_
  36.2 0.0 copy-done.4
  36.2 3.3 %gradients.1 = (bf16[576,128]{1,0:T(8,128)(2,1)S(1)}, bf16[576,128]{1,0:T(8,128)(2,1)S(1)}, bf16[576,128]{1,0:T(8,128)(2,1)S(1)}, bf16[576,128]{1,0:T(8,128)(2,1...) custom-call(bf16[592,128]{1,0:T(8,128)(2,1)S(1)} %copy-done.4, ...), custom_call_target="tpu_custom_call" | custom-call | flops 1744830464 | bytes 9109504 | tf_op jit(solution)/shard_map/gradients/pallas_call | solution.py:39
  39.6 0.1 collective-permute-start.14
  39.6 2.4 %collective-permute-start.15 = (bf16[2,128,128]{2,1,0:T(8,128)(2,1)S(1)}, bf16[2,128,128]{2,1,0:T(8,128)(2,1)S(1)}, u32[]{:S(2)}, u32[]{:S(2)}) collective-permute-start(bf16[2,128,128]{2,1,0:T(8,128)(2,1)S(1)} %add_convert_fusion.7), channel_id=1, source_target_pairs={{0,8},{1,9},{2,10},{3,11},{4,12},{5,13},{6,14},{7,15},{8,0},{9,1},... | collective-permute-start | bytes 196616 | tf_op jit(solution)/shard_map/ppermute | solution.py:257
  42.0 1.4 %collective-permute-start.13 = (bf16[576,128]{1,0:T(8,128)(2,1)S(1)}, bf16[576,128]{1,0:T(8,128)(2,1)S(1)}, u32[]{:S(2)}, u32[]{:S(2)}) collective-permute-start(bf16[576,128]{1,0:T(8,128)(2,1)S(1)} %get-tuple-element.79), channel_id=1, source_target_pairs={{0,4},{1,5},{2,6},{3,7},{4,0},{5,1},{6,2},{7,3},{8,12},{9,13},{10,... | collective-permute-start | bytes 442376 | tf_op jit(solution)/shard_map/ppermute | solution.py:218
  43.5 3.1 %collective-permute-done.15 = bf16[2,128,128]{2,1,0:T(8,128)(2,1)S(1)} collective-permute-done((bf16[2,128,128]{2,1,0:T(8,128)(2,1)S(1)}, bf16[2,128,128]{2,1,0:T(8,128)(2,1)S(1)}, u32[]{:S(2)}, u32[]{:S(2)}) %collective-permute-start.15) | collective-permute-done | bytes 65568 | tf_op jit(solution)/shard_map/ppermute | solution.py:257
  46.6 1.8 %collective-permute-done.13 = bf16[576,128]{1,0:T(8,128)(2,1)S(1)} collective-permute-done((bf16[576,128]{1,0:T(8,128)(2,1)S(1)}, bf16[576,128]{1,0:T(8,128)(2,1)S(1)}, u32[]{:S(2)}, u32[]{:S(2)}) %collective-permute-start.13) | collective-permute-done | bytes 147488 | tf_op jit(solution)/shard_map/ppermute | solution.py:218
  48.4 0.0 collective-permute-done.14
  48.4 0.1 add_convert_fusion.1
  48.5 1.4 %collective-permute-start.18 = (bf16[2,576,128]{2,1,0:T(8,128)(2,1)S(1)}, bf16[2,576,128]{2,1,0:T(8,128)(2,1)S(1)}, u32[]{:S(2)}, u32[]{:S(2)}) collective-permute-start(bf16[2,576,128]{2,1,0:T(8,128)(2,1)S(1)} %add_convert_fusion.1), channel_id=1, source_target_pairs={{0,2},{1,3},{2,0},{3,1},{4,6},{5,7},{6,4},{7,5},{8,10},{9,11},{10,... | collective-permute-start | bytes 884744 | tf_op jit(solution)/shard_map/ppermute | solution.py:218
  49.9 0.7 %collective-permute-start.19 = (bf16[2,128,128]{2,1,0:T(8,128)(2,1)S(1)}, bf16[2,128,128]{2,1,0:T(8,128)(2,1)S(1)}, u32[]{:S(2)}, u32[]{:S(2)}) collective-permute-start(bf16[2,128,128]{2,1,0:T(8,128)(2,1)S(1)} %add_convert_fusion.6), channel_id=1, source_target_pairs={{0,2},{1,3},{2,0},{3,1},{4,6},{5,7},{6,4},{7,5},{8,10},{9,11},{10,... | collective-permute-start | bytes 196616 | tf_op jit(solution)/shard_map/ppermute | solution.py:218
  50.6 1.3 %collective-permute-start.16 = (bf16[576,128]{1,0:T(8,128)(2,1)S(1)}, bf16[576,128]{1,0:T(8,128)(2,1)S(1)}, u32[]{:S(2)}, u32[]{:S(2)}) collective-permute-start(bf16[576,128]{1,0:T(8,128)(2,1)S(1)} %add_convert_fusion.4), channel_id=1, source_target_pairs={{0,8},{1,9},{2,10},{3,11},{4,12},{5,13},{6,14},{7,15},{8,0},{9,1},... | collective-permute-start | bytes 442376 | tf_op jit(solution)/shard_map/ppermute | solution.py:218
  51.9 1.7 %collective-permute-start.17 = (bf16[576,128]{1,0:T(8,128)(2,1)S(1)}, bf16[576,128]{1,0:T(8,128)(2,1)S(1)}, u32[]{:S(2)}, u32[]{:S(2)}) collective-permute-start(bf16[576,128]{1,0:T(8,128)(2,1)S(1)} %get-tuple-element.85), channel_id=1, source_target_pairs={{0,4},{1,5},{2,6},{3,7},{4,0},{5,1},{6,2},{7,3},{8,12},{9,13},{10,... | collective-permute-start | bytes 442376 | tf_op jit(solution)/shard_map/ppermute | solution.py:218
  53.6 4.6 %collective-permute-done.19 = bf16[2,128,128]{2,1,0:T(8,128)(2,1)S(1)} collective-permute-done((bf16[2,128,128]{2,1,0:T(8,128)(2,1)S(1)}, bf16[2,128,128]{2,1,0:T(8,128)(2,1)S(1)}, u32[]{:S(2)}, u32[]{:S(2)}) %collective-permute-start.19) | collective-permute-done | bytes 65568 | tf_op jit(solution)/shard_map/ppermute | solution.py:218
  58.3 0.9 %collective-permute-done.16 = bf16[576,128]{1,0:T(8,128)(2,1)S(1)} collective-permute-done((bf16[576,128]{1,0:T(8,128)(2,1)S(1)}, bf16[576,128]{1,0:T(8,128)(2,1)S(1)}, u32[]{:S(2)}, u32[]{:S(2)}) %collective-permute-start.16) | collective-permute-done | bytes 147488 | tf_op jit(solution)/shard_map/ppermute | solution.py:218
  59.2 0.0 collective-permute-done.17
  59.2 0.0 collective-permute-done.18
  59.2 0.8 %fusion = bf16[1,128,2,576]{1,3,2,0:T(8,128)(2,1)} fusion(bf16[2,576,128]{2,1,0:T(8,128)(2,1)S(1)} %collective-permute-done.18, bf16[2,576,128]{2,1,0:T(8,128)(2,1)S(1)} %get-tuple-element.75, bf16[4,576,128]{2,1,0:T(8,128)(2,1)S(1)} %collective-permute-done.14), kind=kLoop, calls=%fused_computation.3 | loop fusion | flops 884736 | bytes 1179648 | tf_op jit(solution)/shard_map/broadcast_in_dim | solution.py:344
  60.0 0.0 collective-permute-start.20
  60.0 0.7 %fusion.1 = bf16[1,128,576]{1,2,0:T(8,128)(2,1)} fusion(bf16[576,128]{1,0:T(8,128)(2,1)S(1)} %collective-permute-done.17, bf16[576,128]{1,0:T(8,128)(2,1)S(1)} %collective-permute-done.16, bf16[576,128]{1,0:T(8,128)(2,1)S(1)} %get-tuple-element.89), kind=kLoop, calls=%fused_computation.7 | loop fusion | flops 442368 | bytes 589824 | tf_op jit(solution)/shard_map/broadcast_in_dim | solution.py:344
  60.8 0.6 collective-permute-done.20
  61.4 0.8 %spread.1 = f32[2,512,128]{2,1,0:T(8,128)} custom-call(s32[1]{0:T(128)} %bitcast.idx_ref, bf16[2,128,128]{2,1,0:T(8,128)(2,1)S(1)} %get-tuple-element.96.refs_0_, bf16[2,128,128]{2,1,0:T(8,128)(2,1)S(1)} %get-tuple-element.94.refs_1_, bf16[2,128,128]{2,1,0:T(8,128)(2,1)S(1)} %get-tuple-element.95.refs_2_, bf16[2,128,128]{2,1,0:T(8,128)(2,1)S(1)} %get-tuple-element.93.refs_3_), custom_call_target="tpu_custom_call" | custom-call | bytes 786436 | tf_op jit(solution)/shard_map/spread/pallas_call | solution.py:39
  (10 shorter events, 0.2 us)
Async XLA Ops:
  3.7 15.0 %collective-permute-start.3 = (bf16[1424,128]{1,0:T(8,128)(2,1)}, bf16[1424,128]{1,0:T(8,128)(2,1)S(1)}, u32[]{:S(2)}, u32[]{:S(2)}) collective-permute-start(bf16[1424,128]{1,0:T(8,128)(2,1)} %get-tuple-element.49.refs_4_.refs_0_), channel_id=1, source_target_pairs={{0,1},{1,0},{2,3},{3,2},{4,5},{5,4},{6,7},{7,6},{8,9},{9,8},{10,11... | collective-permute-start | bytes 1093640 | tf_op jit(solution)/shard_map/ppermute | solution.py:218
  4.2 14.5 %collective-permute-start.2 = (bf16[1424,128]{1,0:T(8,128)(2,1)}, bf16[1424,128]{1,0:T(8,128)(2,1)S(1)}, u32[]{:S(2)}, u32[]{:S(2)}) collective-permute-start(bf16[1424,128]{1,0:T(8,128)(2,1)} %get-tuple-element.49.refs_4_.refs_0_), channel_id=1, source_target_pairs={{0,2},{1,3},{2,0},{3,1},{4,6},{5,7},{6,4},{7,5},{8,10},{9,11},{10,... | collective-permute-start | bytes 1093640 | tf_op jit(solution)/shard_map/ppermute | solution.py:218
  6.8 11.9 %collective-permute-start.4 = (bf16[8,128,128]{2,1,0:T(8,128)(2,1)}, bf16[8,128,128]{2,1,0:T(8,128)(2,1)S(1)}, u32[]{:S(2)}, u32[]{:S(2)}) collective-permute-start(bf16[8,128,128]{2,1,0:T(8,128)(2,1)} %get-tuple-element.54), channel_id=1, source_target_pairs={{0,16},{16,0},{1,17},{17,1},{2,18},{18,2},{3,19},{19,3},{4,20},{20... | collective-permute-start | bytes 786440 | tf_op jit(solution)/shard_map/ppermute | solution.py:257
  8.3 25.8 %copy-start.1 = (bf16[1424,128]{1,0:T(8,128)(2,1)S(1)}, bf16[1424,128]{1,0:T(8,128)(2,1)}, u32[]{:S(2)}) copy-start(bf16[1424,128]{1,0:T(8,128)(2,1)} %get-tuple-element.49.refs_4_.refs_0_) | copy-start | bytes 1093636
  8.3 25.8 %copy-start.2 = (bf16[2,512,128]{2,1,0:T(8,128)(2,1)S(1)}, bf16[2,512,128]{2,1,0:T(8,128)(2,1)}, u32[]{:S(2)}) copy-start(bf16[2,512,128]{2,1,0:T(8,128)(2,1)} %refs_4_.1) | copy-start | bytes 786436
  8.3 10.2 %collective-permute-start.1 = (bf16[592,128]{1,0:T(8,128)(2,1)}, bf16[592,128]{1,0:T(8,128)(2,1)S(1)}, u32[]{:S(2)}, u32[]{:S(2)}) collective-permute-start(bf16[592,128]{1,0:T(8,128)(2,1)} %get-tuple-element.56.refs_0_), channel_id=1, source_target_pairs={{0,8},{1,9},{2,10},{3,11},{4,12},{5,13},{6,14},{7,15},{8,0},{9,1},... | collective-permute-start | bytes 454664 | tf_op jit(solution)/shard_map/ppermute | solution.py:218
  10.9 7.8 %collective-permute-start = (bf16[592,128]{1,0:T(8,128)(2,1)}, bf16[592,128]{1,0:T(8,128)(2,1)S(1)}, u32[]{:S(2)}, u32[]{:S(2)}) collective-permute-start(bf16[592,128]{1,0:T(8,128)(2,1)} %get-tuple-element.56.refs_0_), channel_id=1, source_target_pairs={{0,4},{1,5},{2,6},{3,7},{4,0},{5,1},{6,2},{7,3},{8,12},{9,13},{10,... | collective-permute-start | bytes 454664 | tf_op jit(solution)/shard_map/ppermute | solution.py:218
  18.7 8.5 %collective-permute-start.5 = (bf16[592,128]{1,0:T(8,128)(2,1)S(1)}, bf16[592,128]{1,0:T(8,128)(2,1)S(1)}, u32[]{:S(2)}, u32[]{:S(2)}) collective-permute-start(bf16[592,128]{1,0:T(8,128)(2,1)S(1)} %collective-permute-done.1.refs_2_), channel_id=1, source_target_pairs={{0,4},{1,5},{2,6},{3,7},{4,0},{5,1},{6,2},{7,3},{8,12},{9,13},{10,... | collective-permute-start | bytes 454664 | tf_op jit(solution)/shard_map/ppermute | solution.py:218
  20.2 7.0 %collective-permute-start.6 = (bf16[1424,128]{1,0:T(8,128)(2,1)S(1)}, bf16[1424,128]{1,0:T(8,128)(2,1)S(1)}, u32[]{:S(2)}, u32[]{:S(2)}) collective-permute-start(bf16[1424,128]{1,0:T(8,128)(2,1)S(1)} %collective-permute-done.2.refs_6_.refs_2_), channel_id=1, source_target_pairs={{0,1},{1,0},{2,3},{3,2},{4,5},{5,4},{6,7},{7,6},{8,9},{9,8},{10,11... | collective-permute-start | bytes 1093640 | tf_op jit(solution)/shard_map/ppermute | solution.py:218
  21.2 6.0 %collective-permute-start.7 = (bf16[4,128,128]{2,1,0:T(8,128)(2,1)S(1)}, bf16[4,128,128]{2,1,0:T(8,128)(2,1)S(1)}, u32[]{:S(2)}, u32[]{:S(2)}) collective-permute-start(bf16[4,128,128]{2,1,0:T(8,128)(2,1)S(1)} %slice.40), channel_id=1, source_target_pairs={{0,2},{1,3},{2,0},{3,1},{4,6},{5,7},{6,4},{7,5},{8,10},{9,11},{10,... | collective-permute-start | bytes 393224 | tf_op jit(solution)/shard_map/ppermute | solution.py:218
  27.3 4.3 %collective-permute-start.8 = (bf16[2,128,128]{2,1,0:T(8,128)(2,1)S(1)}, bf16[2,128,128]{2,1,0:T(8,128)(2,1)S(1)}, u32[]{:S(2)}, u32[]{:S(2)}) collective-permute-start(bf16[2,128,128]{2,1,0:T(8,128)(2,1)S(1)} %slice.43), channel_id=1, source_target_pairs={{0,1},{1,0},{2,3},{3,2},{4,5},{5,4},{6,7},{7,6},{8,9},{9,8},{10,11... | collective-permute-start | bytes 196616 | tf_op jit(solution)/shard_map/ppermute | solution.py:218
  27.4 1.0 %copy-start = (bf16[1424,128]{1,0:T(8,128)(2,1)S(1)}, bf16[1424,128]{1,0:T(8,128)(2,1)}, u32[]{:S(2)}) copy-start(bf16[1424,128]{1,0:T(8,128)(2,1)} %get-tuple-element.49.refs_4_.refs_0_) | copy-start | bytes 1093636
  28.4 0.9 %copy-start.3 = (bf16[592,128]{1,0:T(8,128)(2,1)S(1)}, bf16[592,128]{1,0:T(8,128)(2,1)}, u32[]{:S(2)}) copy-start(bf16[592,128]{1,0:T(8,128)(2,1)} %get-tuple-element.56.refs_0_) | copy-start | bytes 454660
  29.3 0.7 %copy-start.5 = (f32[8,128]{1,0:T(8,128)S(1)}, f32[8,128]{1,0:T(8,128)}, u32[]{:S(2)}) copy-start(f32[8,128]{1,0:T(8,128)} %get-tuple-element.63.refs_8_) | copy-start | bytes 12292
  30.0 6.3 %copy-start.4 = (bf16[592,128]{1,0:T(8,128)(2,1)S(1)}, bf16[592,128]{1,0:T(8,128)(2,1)}, u32[]{:S(2)}) copy-start(bf16[592,128]{1,0:T(8,128)(2,1)} %get-tuple-element.56.refs_0_) | copy-start | bytes 454660
  31.6 4.6 %collective-permute-start.9 = (bf16[2,128,128]{2,1,0:T(8,128)(2,1)S(1)}, bf16[2,128,128]{2,1,0:T(8,128)(2,1)S(1)}, u32[]{:S(2)}, u32[]{:S(2)}) collective-permute-start(bf16[2,128,128]{2,1,0:T(8,128)(2,1)S(1)} %add_convert_fusion.8), channel_id=1, source_target_pairs={{0,4},{1,5},{2,6},{3,7},{4,0},{5,1},{6,2},{7,3},{8,12},{9,13},{10,... | collective-permute-start | bytes 196616 | tf_op jit(solution)/shard_map/ppermute | solution.py:257
  32.3 3.9 %collective-permute-start.12 = (f32[16,128]{1,0:T(8,128)S(1)}, f32[16,128]{1,0:T(8,128)S(1)}, u32[]{:S(2)}, u32[]{:S(2)}) collective-permute-start(f32[16,128]{1,0:T(8,128)S(1)} %get-tuple-element.69.refs_8_), channel_id=1, source_target_pairs={{0,3},{1,2},{2,1},{3,0},{4,7},{5,6},{6,5},{7,4},{8,11},{9,10},{10,... | collective-permute-start | bytes 24584 | tf_op jit(solution)/shard_map/ppermute | solution.py:218
  32.6 3.7 %collective-permute-start.11 = (f32[16,128]{1,0:T(8,128)S(1)}, f32[16,128]{1,0:T(8,128)S(1)}, u32[]{:S(2)}, u32[]{:S(2)}) collective-permute-start(f32[16,128]{1,0:T(8,128)S(1)} %get-tuple-element.69.refs_8_), channel_id=1, source_target_pairs={{0,2},{1,3},{2,0},{3,1},{4,6},{5,7},{6,4},{7,5},{8,10},{9,11},{10,... | collective-permute-start | bytes 24584 | tf_op jit(solution)/shard_map/ppermute | solution.py:218
  34.1 2.1 %collective-permute-start.10 = (f32[16,128]{1,0:T(8,128)S(1)}, f32[16,128]{1,0:T(8,128)S(1)}, u32[]{:S(2)}, u32[]{:S(2)}) collective-permute-start(f32[16,128]{1,0:T(8,128)S(1)} %get-tuple-element.69.refs_8_), channel_id=1, source_target_pairs={{0,1},{1,0},{2,3},{3,2},{4,5},{5,4},{6,7},{7,6},{8,9},{9,8},{10,11... | collective-permute-start | bytes 24584 | tf_op jit(solution)/shard_map/ppermute | solution.py:218
  39.6 8.9 %collective-permute-start.14 = (bf16[4,576,128]{2,1,0:T(8,128)(2,1)S(1)}, bf16[4,576,128]{2,1,0:T(8,128)(2,1)S(1)}, u32[]{:S(2)}, u32[]{:S(2)}) collective-permute-start(bf16[4,576,128]{2,1,0:T(8,128)(2,1)S(1)} %get-tuple-element.80), channel_id=1, source_target_pairs={{0,1},{1,0},{2,3},{3,2},{4,5},{5,4},{6,7},{7,6},{8,9},{9,8},{10,11... | collective-permute-start | bytes 1769480 | tf_op jit(solution)/shard_map/ppermute | solution.py:218
  39.6 6.9 %collective-permute-start.15 = (bf16[2,128,128]{2,1,0:T(8,128)(2,1)S(1)}, bf16[2,128,128]{2,1,0:T(8,128)(2,1)S(1)}, u32[]{:S(2)}, u32[]{:S(2)}) collective-permute-start(bf16[2,128,128]{2,1,0:T(8,128)(2,1)S(1)} %add_convert_fusion.7), channel_id=1, source_target_pairs={{0,8},{1,9},{2,10},{3,11},{4,12},{5,13},{6,14},{7,15},{8,0},{9,1},... | collective-permute-start | bytes 196616 | tf_op jit(solution)/shard_map/ppermute | solution.py:257
  42.0 6.3 %collective-permute-start.13 = (bf16[576,128]{1,0:T(8,128)(2,1)S(1)}, bf16[576,128]{1,0:T(8,128)(2,1)S(1)}, u32[]{:S(2)}, u32[]{:S(2)}) collective-permute-start(bf16[576,128]{1,0:T(8,128)(2,1)S(1)} %get-tuple-element.79), channel_id=1, source_target_pairs={{0,4},{1,5},{2,6},{3,7},{4,0},{5,1},{6,2},{7,3},{8,12},{9,13},{10,... | collective-permute-start | bytes 442376 | tf_op jit(solution)/shard_map/ppermute | solution.py:218
  48.5 10.7 %collective-permute-start.18 = (bf16[2,576,128]{2,1,0:T(8,128)(2,1)S(1)}, bf16[2,576,128]{2,1,0:T(8,128)(2,1)S(1)}, u32[]{:S(2)}, u32[]{:S(2)}) collective-permute-start(bf16[2,576,128]{2,1,0:T(8,128)(2,1)S(1)} %add_convert_fusion.1), channel_id=1, source_target_pairs={{0,2},{1,3},{2,0},{3,1},{4,6},{5,7},{6,4},{7,5},{8,10},{9,11},{10,... | collective-permute-start | bytes 884744 | tf_op jit(solution)/shard_map/ppermute | solution.py:218
  49.9 8.3 %collective-permute-start.19 = (bf16[2,128,128]{2,1,0:T(8,128)(2,1)S(1)}, bf16[2,128,128]{2,1,0:T(8,128)(2,1)S(1)}, u32[]{:S(2)}, u32[]{:S(2)}) collective-permute-start(bf16[2,128,128]{2,1,0:T(8,128)(2,1)S(1)} %add_convert_fusion.6), channel_id=1, source_target_pairs={{0,2},{1,3},{2,0},{3,1},{4,6},{5,7},{6,4},{7,5},{8,10},{9,11},{10,... | collective-permute-start | bytes 196616 | tf_op jit(solution)/shard_map/ppermute | solution.py:218
  50.6 8.6 %collective-permute-start.16 = (bf16[576,128]{1,0:T(8,128)(2,1)S(1)}, bf16[576,128]{1,0:T(8,128)(2,1)S(1)}, u32[]{:S(2)}, u32[]{:S(2)}) collective-permute-start(bf16[576,128]{1,0:T(8,128)(2,1)S(1)} %add_convert_fusion.4), channel_id=1, source_target_pairs={{0,8},{1,9},{2,10},{3,11},{4,12},{5,13},{6,14},{7,15},{8,0},{9,1},... | collective-permute-start | bytes 442376 | tf_op jit(solution)/shard_map/ppermute | solution.py:218
  51.9 7.3 %collective-permute-start.17 = (bf16[576,128]{1,0:T(8,128)(2,1)S(1)}, bf16[576,128]{1,0:T(8,128)(2,1)S(1)}, u32[]{:S(2)}, u32[]{:S(2)}) collective-permute-start(bf16[576,128]{1,0:T(8,128)(2,1)S(1)} %get-tuple-element.85), channel_id=1, source_target_pairs={{0,4},{1,5},{2,6},{3,7},{4,0},{5,1},{6,2},{7,3},{8,12},{9,13},{10,... | collective-permute-start | bytes 442376 | tf_op jit(solution)/shard_map/ppermute | solution.py:218
  60.0 1.3 %collective-permute-start.20 = (bf16[4,128,128]{2,1,0:T(8,128)(2,1)S(1)}, bf16[4,128,128]{2,1,0:T(8,128)(2,1)S(1)}, u32[]{:S(2)}, u32[]{:S(2)}) collective-permute-start(bf16[4,128,128]{2,1,0:T(8,128)(2,1)S(1)} %pad_maximum_fusion), channel_id=1, source_target_pairs={{0,1},{1,0},{2,3},{3,2},{4,5},{5,4},{6,7},{7,6},{8,9},{9,8},{10,11... | collective-permute-start | bytes 393224 | tf_op jit(solution)/shard_map/ppermute | solution.py:218

commit v4 on v3

--- a/solution.py
+++ b/solution.py
@@ -97,14 +97,14 @@
 
 
 def score_kernel(factor, nkey, width, heads, *refs):
-    lat_refs = refs[:nkey]
-    q_refs = refs[nkey : nkey + GROUP]
-    delta_ref, s_ref, k_ref, stat_ref, kt, qt = refs[nkey + GROUP :]
+    lat_ref = refs[0]
+    q_refs = refs[1 : 1 + GROUP]
+    delta_ref, s_ref, k_ref, stat_ref, kt, qt = refs[1 + GROUP :]
     wide = kt.shape[0]
-    tok = lat_refs[0].shape[1]
+    tok = lat_ref.shape[2]
     rows = heads * tok
     for a in range(nkey):
-        kt[: width + EXTRA, a * tok : (a + 1) * tok] = lat_refs[a][...]
+        kt[: width + EXTRA, a * tok : (a + 1) * tok] = lat_ref[a]
     kt[width + EXTRA :, :] = jnp.zeros((wide - width - EXTRA, nkey * tok), BF16)
     k_ref[...] = kt[...].T
     pos = k_ref[:, wide - 128 :].astype(F32)
@@ -148,17 +148,17 @@
 
 
 def grad_kernel(factor, nkey, width, heads, *refs):
-    lat_refs, refs = refs[:nkey], refs[nkey:]
+    lat_ref, refs = refs[0], refs[1:]
     q_refs, refs = refs[:GROUP], refs[GROUP:]
     stats, refs = refs[:GROUP], refs[GROUP:]
     (s_ref, gp_ref, g_ref), refs = refs[:3], refs[3:]
-    part_refs, refs = refs[:nkey], refs[nkey:]
+    part_ref, refs = refs[0], refs[1:]
     own_ref, core_ref, across_ref, kt, qt, gs_all, p_all = refs
     tok = q_refs[0].shape[1]
     rows = heads * tok
     lat = g_ref.shape[0]
     for a in range(nkey):
-        kt[:, a * tok : (a + 1) * tok] = lat_refs[a][:width, :]
+        kt[:, a * tok : (a + 1) * tok] = lat_ref[a, :width, :]
     for j in range(GROUP):
         cols = slice(j * rows, (j + 1) * rows)
         lse_parts = []
@@ -190,8 +190,8 @@
         at = slice(a * tok, (a + 1) * tok)
         along = mm_t(qt[...], gs_all[at, :]) * factor
         value = mm_t(g_ref[...], p_all[at, :])
-        part_refs[a][:lat, :] = (along[:lat] + value).astype(BF16)
-        part_refs[a][lat:, :] = along[lat:].astype(BF16)
+        part_ref[a, :lat, :] = (along[:lat] + value).astype(BF16)
+        part_ref[a, lat:, :] = along[lat:].astype(BF16)
 
 
 def spread_kernel(scale, idx_ref, *refs):
@@ -207,7 +207,6 @@
     tok, heads, width = queries.shape[1:]
     lat = attn_out.shape[3]
     lines = n_ctx // GROUP
-    line_bits = (lines - 1).bit_length()
     rows = heads * tok
     all_rows = GROUP * rows
     keys = lines * tok
@@ -261,26 +260,22 @@
         return (pair[0].astype(F32) + pair[1].astype(F32)).astype(BF16)
 
     dp_hops = [("dp", n_dp, 1 << bit) for bit in range((n_dp - 1).bit_length())]
+
+    line_bits = (lines - 1).bit_length()
     line_hops = [("ctx", n_ctx, GROUP << bit) for bit in range(line_bits)]
-
-    firsts = {1 << bit: swap(lat_msg, GROUP << bit) for bit in range(line_bits)}
+    line_groups = [[r + GROUP * a for a in range(lines)] for r in range(GROUP)]
+    lats = lax.all_gather(lat_msg, "ctx", axis_index_groups=line_groups)
     q_across = swap(q_msg, 2)
     q_core = swap(q_msg, 1)
     twins = hop(term, *dp_hops[0])
-    firsts, q_across, q_core, twins = lax.optimization_barrier((firsts, q_across, q_core, twins))
+    q_across, q_core, twins = lax.optimization_barrier((q_across, q_core, twins))
     for step_hop in dp_hops[1:]:
         twins = hop(add(twins), *step_hop)
     total = add(twins)
-
-    held = {0: lat_msg}
-    for bit in reversed(range(line_bits)):
-        held.update({m | 1 << bit: swap(x, GROUP << bit) for m, x in held.items() if m})
-        held[1 << bit] = firsts[1 << bit]
-    lats = [held[m] for m in range(lines)]
     q_far = swap(q_across, 1)
     half = 2 * heads
     got_half = swap(total[half:], 2)
-    lats, q_far, got_half = lax.optimization_barrier((lats, q_far, got_half))
+    q_far, got_half = lax.optimization_barrier((q_far, got_half))
     qs = [q_msg, q_core, q_across, q_far]
     total = add((total[:half], got_half))
     got_own = swap(total[heads:], 1)
@@ -289,7 +284,7 @@
         functools.partial(score_kernel, factor, lines, width, heads),
         "scores",
         [((keys, all_rows), F32), ((keys, wide), BF16), ((EXTRA, tok), F32)],
-        lats + qs + [delta],
+        [lats] + qs + [delta],
         [((wide, keys), BF16), ((wide, rows), BF16)],
         flops=2 * keys * all_rows * wide,
     )
@@ -308,9 +303,9 @@
     outs = call(
         functools.partial(grad_kernel, factor, lines, width, heads),
         "gradients",
-        [((width, tok), BF16)] * lines
+        [((lines, width, tok), BF16)]
         + [((heads, width, tok), BF16), ((2 * heads, width, tok), BF16), ((heads, width, tok), BF16)],
-        lats + qs + stats + [s, gp, g],
+        [lats] + qs + stats + [s, gp, g],
         [
             ((width, keys), BF16),
             ((width, all_rows), BF16),
@@ -319,22 +314,15 @@
         ],
         flops=2 * keys * all_rows * (2 * width + lat),
     )
-    parts, (gq_own, gq_core, gq_across) = list(outs[:lines]), outs[lines:]
-    kept = [parts[0]]
+    parts, gq_own, gq_core, gq_across = outs
+    grad_lat = lax.psum_scatter(parts, "ctx", axis_index_groups=line_groups)
     gq_got = swap(gq_core, 1)
     for step_hop in line_hops[1:]:
         mine = add(hop(after(mine, gq_own), *step_hop))
-    for bit in range(line_bits):
-        for m in [m for m in range(2 << bit, lines) if m >> bit & 1 and not m & (1 << bit) - 1]:
-            parts[m ^ 1 << bit] = add((parts[m ^ 1 << bit], swap(parts[m], GROUP << bit)))
-        if bit == 0:
-            parts, gq_got, mine = lax.optimization_barrier((parts, gq_got, mine))
-    kept += [swap(parts[1 << bit], GROUP << bit) for bit in reversed(range(line_bits))]
+    gq_got, mine = lax.optimization_barrier((gq_got, mine))
     gq_last = swap(add((gq_across, gq_got[heads:])), 2)
     mine_two = jnp.concatenate([mine, swap(mine, 2)], axis=0)
-    kept, gq_last, mine_two = lax.optimization_barrier((kept, gq_last, mine_two))
     other_two = swap(mine_two, 1)
-    grad_lat = sum(p.astype(F32) for p in kept).astype(BF16)
     grad_q = sum(p.astype(F32) for p in (gq_own, gq_got[:heads], gq_last)).astype(BF16)
     scale = 1.0 / math.sqrt(tok * n_ctx * n_dp)
     pieces = [mine_two[:heads], other_two[:heads], mine_two[heads:], other_two[heads:]]

time: 62.5 us -> 88.9 us (1.42)
  blocking collectives: 0 us -> 18.2 us
  between operations: 0.79 us -> 14.2 us
  starting transfers between devices: 22.4 us -> 14.9 us
  waiting for transfers between devices: 23.5 us -> 28.4 us
  local copies, waits for them, and re-layouts: 2.63 us -> 0.05 us
  Pallas kernels: 10 us -> 10.9 us
    all_gather x0 -> x1, blocking collectives: none -> 18.2 us  [body(): lats = lax.all_gather(lat_msg, 'ctx', axis_index_groups=line_groups)]
    ppermute x3, waiting for transfers between devices: 3.86 us -> 11.7 us  [hop(): other = lax.ppermute(total, axis, [(i, i ^ mask) for i in range(size)])]
    ppermute x18 -> x12, starting transfers between devices: 17.9 us -> 10.2 us  [swap(): return lax.ppermute(x, 'ctx', [(i, i ^ mask) for i in range(n_ctx)])]
    ppermute x18 -> x12, waiting for transfers between devices: 19.7 us -> 14.9 us  [swap(): return lax.ppermute(x, 'ctx', [(i, i ^ mask) for i in range(n_ctx)])]
    unnamed x12 -> x6, local copies, waits for them, and re-layouts: 2.59 us -> 0.02 us
    reduce_scatter x0 -> x1, waiting for transfers between devices: none -> 1.82 us  [body(): grad_lat = lax.psum_scatter(parts, 'ctx', axis_index_groups=line_groups)]
  transfers between devices with their start and end apart: 21 -> 16, of which waited for: 9 -> 8; matrix products, arithmetic and copies ran while one was open for 3% -> 2% of each run, Pallas kernels for 5% -> 4%
where the time goes in v4:
time: 88.9 us; the launch traced here: 88.8 us
  waiting for transfers between devices  28.4 us (32%)
  blocking collectives  18.2 us (20%)
  starting transfers between devices  14.9 us (17%)
  between operations  14.2 us (16%)
  Pallas kernels  10.9 us (12%)
  other arithmetic  2.05 us (2%)
    all_gather x1, blocking collectives, body(): lats = lax.all_gather(lat_msg, 'ctx', axis_index_groups=line_groups)  18.2 us
    ppermute x12, waiting for transfers between devices, swap(): return lax.ppermute(x, 'ctx', [(i, i ^ mask) for i in range(n_ctx)])  14.9 us
    ppermute x3, waiting for transfers between devices, hop(): other = lax.ppermute(total, axis, [(i, i ^ mask) for i in range(size)])  11.7 us
    pallas_call x5, Pallas kernels, call(): pl.pallas_call(kernel, out_shape=[jax.ShapeDtypeStruct(s, d) for s, d in...  10.9 us
    ppermute x12, starting transfers between devices, swap(): return lax.ppermute(x, 'ctx', [(i, i ^ mask) for i in range(n_ctx)])  10.2 us
    ppermute x3, starting transfers between devices, hop(): other = lax.ppermute(total, axis, [(i, i ^ mask) for i in range(size)])  4.65 us
    reduce_scatter x1, waiting for transfers between devices, body(): grad_lat = lax.psum_scatter(parts, 'ctx', axis_index_groups=line_groups)  1.82 us
  transfers between devices with their start and end apart: 16, of which 8 were waited for; matrix products, arithmetic and copies ran while one was open for 2% of the time, Pallas kernels for 4%

profile of v4, /device:TPU:0, one launch (start us, length us, event | category | flops | bytes accessed | tf_op | source)
XLA Modules:
  0.0 88.8 jit_solution(11537620215671809448)
XLA Ops:
  7.2 0.0 reduce-scatter.2.cloned.1.call-start
  7.2 3.0 %pack.1 = (bf16[592,128]{1,0:T(8,128)(2,1)}, bf16[1424,128]{1,0:T(8,128)(2,1)}, f32[8,128]{1,0:T(8,128)}, bf16[8,128,128]{2,1,0:T(8,128)(2,1)}) custom-call(s32[1]{0:T(128)} %bitcast.idx_ref, s32[1,128]{1,0:T(1,128)} %pos_hbm.1, bf16[2,576,128]{2,1,0:T(8,128)(2,1)} %bitcast.21, bf16[128,2,128]{2,1,0:T(2,128)(2,1)} %bitcast.24, bf16[576,128]{1,0:T(8,128)(2,1)} %bitcast.23, ...), custom_call_target="tpu_custom_call" | custom-call | bytes 1815044 | tf_op jit(solution)/shard_map/pack/pallas_call | solution.py:39
  10.3 0.0 copy-start
  10.3 0.0 copy-start.2
  10.3 0.5 collective-permute-start.1
  10.8 2.6 %collective-permute-start = (bf16[1424,128]{1,0:T(8,128)(2,1)}, bf16[1424,128]{1,0:T(8,128)(2,1)S(1)}, u32[]{:S(2)}, u32[]{:S(2)}) collective-permute-start(bf16[1424,128]{1,0:T(8,128)(2,1)} %get-tuple-element.33.refs_1_.refs_0_), channel_id=1, source_target_pairs={{0,2},{1,3},{2,0},{3,1},{4,6},{5,7},{6,4},{7,5},{8,10},{9,11},{10,... | collective-permute-start | bytes 1093640 | tf_op jit(solution)/shard_map/ppermute | solution.py:217
  13.4 1.5 %collective-permute-start.2 = (bf16[8,128,128]{2,1,0:T(8,128)(2,1)}, bf16[8,128,128]{2,1,0:T(8,128)(2,1)S(1)}, u32[]{:S(2)}, u32[]{:S(2)}) collective-permute-start(bf16[8,128,128]{2,1,0:T(8,128)(2,1)} %get-tuple-element.37), channel_id=1, source_target_pairs={{0,16},{16,0},{1,17},{17,1},{2,18},{18,2},{3,19},{19,3},{4,20},{20... | collective-permute-start | bytes 786440 | tf_op jit(solution)/shard_map/ppermute | solution.py:256
  14.9 7.1 %collective-permute-done.2 = bf16[8,128,128]{2,1,0:T(8,128)(2,1)S(1)} collective-permute-done((bf16[8,128,128]{2,1,0:T(8,128)(2,1)}, bf16[8,128,128]{2,1,0:T(8,128)(2,1)S(1)}, u32[]{:S(2)}, u32[]{:S(2)}) %collective-permute-start.2) | collective-permute-done | bytes 262176 | tf_op jit(solution)/shard_map/ppermute | solution.py:256
  22.0 0.0 collective-permute-done.1.refs_2_.refs_1_
  22.0 0.7 collective-permute-done.refs_3_.refs_2_
  22.7 0.0 collective-permute-start.3
  22.7 1.0 %add_convert_fusion.2 = bf16[8,128,128]{2,1,0:T(8,128)(2,1)S(1)} fusion(bf16[8,128,128]{2,1,0:T(8,128)(2,1)S(1)} %collective-permute-done.2, bf16[8,128,128]{2,1,0:T(8,128)(2,1)} %get-tuple-element.37), kind=kLoop, calls=%fused_computation.2 | loop fusion | flops 524288 | bytes 786432 | tf_op jit(solution)/shard_map/convert_element_type | solution.py:260
  23.7 0.0 copy-start.1
  23.8 1.8 %collective-permute-start.4 = (bf16[4,128,128]{2,1,0:T(8,128)(2,1)S(1)}, bf16[4,128,128]{2,1,0:T(8,128)(2,1)S(1)}, u32[]{:S(2)}, u32[]{:S(2)}) collective-permute-start(bf16[4,128,128]{2,1,0:T(8,128)(2,1)S(1)} %slice.32), channel_id=1, source_target_pairs={{0,2},{1,3},{2,0},{3,1},{4,6},{5,7},{6,4},{7,5},{8,10},{9,11},{10,... | collective-permute-start | bytes 393224 | tf_op jit(solution)/shard_map/ppermute | solution.py:217
  25.6 4.2 %collective-permute-done.4 = bf16[4,128,128]{2,1,0:T(8,128)(2,1)S(1)} collective-permute-done((bf16[4,128,128]{2,1,0:T(8,128)(2,1)S(1)}, bf16[4,128,128]{2,1,0:T(8,128)(2,1)S(1)}, u32[]{:S(2)}, u32[]{:S(2)}) %collective-permute-start.4) | collective-permute-done | bytes 131104 | tf_op jit(solution)/shard_map/ppermute | solution.py:217
  29.8 0.0 collective-permute-done.3.refs_4_.refs_3_
  29.8 0.1 collective-permute-start.5
  29.9 18.2 %all-gather = bf16[2368,128]{1,0:T(8,128)(2,1)S(1)} all-gather(bf16[592,128]{1,0:T(8,128)(2,1)} %get-tuple-element.32), channel_id=2, replica_groups={{0,4,8,12},{1,5,9,13},{2,6,10,14},{3,7,11,15},{16,20,24,28},{17,21,25,2..., dimensions={0}, use_global_device_ids=true | all-gather | bytes 757760 | tf_op jit(solution)/shard_map/all_gather | solution.py:267
  48.1 0.0 copy-done
  48.2 0.0 copy-done.2
  48.2 1.6 %scores.1 = (f32[512,1024]{1,0:T(8,128)S(1)}, bf16[512,640]{1,0:T(8,128)(2,1)S(1)}, f32[16,128]{1,0:T(8,128)S(1)}) custom-call(bf16[4,592,128]{2,1,0:T(8,128)(2,1)S(1)} %bitcast.19, bf16[1424,128]{1,0:T(8,128)(2,1)S(1)} %copy-done, bf16[1424,128]{1,0:T(8,128)(2,1)S(1)} %collective-permute-done.1.refs_2_.refs_1_, ...), custom_call_target="tpu_custom_call" | custom-call | flops 671088640 | bytes 4829184 | tf_op jit(solution)/shard_map/scores/pallas_call | solution.py:39
  49.8 0.0 collective-permute-done.5
  49.8 0.6 collective-permute-start.6
  50.4 0.0 collective-permute-start.9
  50.4 1.6 %collective-permute-start.8 = (f32[16,128]{1,0:T(8,128)S(1)}, f32[16,128]{1,0:T(8,128)S(1)}, u32[]{:S(2)}, u32[]{:S(2)}) collective-permute-start(f32[16,128]{1,0:T(8,128)S(1)} %get-tuple-element.47.refs_5_), channel_id=1, source_target_pairs={{0,2},{1,3},{2,0},{3,1},{4,6},{5,7},{6,4},{7,5},{8,10},{9,11},{10,... | collective-permute-start | bytes 24584 | tf_op jit(solution)/shard_map/ppermute | solution.py:217
  52.0 0.3 collective-permute-start.7
  52.3 0.0 copy-done.1
  52.3 1.2 %context.1 = (bf16[512,1024]{1,0:T(8,128)(2,1)S(1)}, f32[512,1024]{1,0:T(8,128)S(1)}) custom-call(bf16[1424,128]{1,0:T(8,128)(2,1)S(1)} %copy-done, bf16[1424,128]{1,0:T(8,128)(2,1)S(1)} %collective-permute-done.1.refs_2_.refs_1_, bf16[1424,128]{1,0:T(8,128)(2,1)S(1)} %collective-permute-done.refs_3_.refs_2_, ...), custom_call_target="tpu_custom_call" | custom-call | flops 671088640 | bytes 5521408 | tf_op jit(solution)/shard_map/context/pallas_call | solution.py:39
  53.5 0.6 collective-permute-done.6
  54.2 0.0 collective-permute-done.9.refs_8_
  54.2 0.0 collective-permute-done.8.refs_7_
  54.2 0.0 collective-permute-done.7.refs_6_
  54.2 4.1 %gradients.1 = (bf16[4,576,128]{2,1,0:T(8,128)(2,1)}, bf16[2,576,128]{2,1,0:T(8,128)(2,1)S(1)}, bf16[4,576,128]{2,1,0:T(8,128)(2,1)S(1)}, bf16[2,576,128]{2,1,0:T(8,128)(2,1)S(1)}) custom-call(bf16[4,592,128]{2,1,0:T(8,128)(2,1)S(1)} %bitcast.20, bf16[1424,128]{1,0:T(8,128)(2,1)S(1)} %copy-done, ...), custom_call_target="tpu_custom_call" | custom-call | flops 1744830464 | bytes 9109504 | tf_op jit(solution)/shard_map/gradients/pallas_call | solution.py:39
  58.3 0.3 collective-permute-start.10
  58.7 2.6 %collective-permute-start.11 = (bf16[2,128,128]{2,1,0:T(8,128)(2,1)S(1)}, bf16[2,128,128]{2,1,0:T(8,128)(2,1)S(1)}, u32[]{:S(2)}, u32[]{:S(2)}) collective-permute-start(bf16[2,128,128]{2,1,0:T(8,128)(2,1)S(1)} %add_convert_fusion.5), channel_id=1, source_target_pairs={{0,8},{1,9},{2,10},{3,11},{4,12},{5,13},{6,14},{7,15},{8,0},{9,1},... | collective-permute-start | bytes 196616 | tf_op jit(solution)/shard_map/ppermute | solution.py:256
  61.2 0.0 reduce-scatter.2.cloned.1.call-update
  61.3 4.0 %collective-permute-done.11 = bf16[2,128,128]{2,1,0:T(8,128)(2,1)S(1)} collective-permute-done((bf16[2,128,128]{2,1,0:T(8,128)(2,1)S(1)}, bf16[2,128,128]{2,1,0:T(8,128)(2,1)S(1)}, u32[]{:S(2)}, u32[]{:S(2)}) %collective-permute-start.11) | collective-permute-done | bytes 65568 | tf_op jit(solution)/shard_map/ppermute | solution.py:256
  65.3 0.0 collective-permute-done.10
  65.3 1.5 %collective-permute-start.13 = (bf16[2,128,128]{2,1,0:T(8,128)(2,1)S(1)}, bf16[2,128,128]{2,1,0:T(8,128)(2,1)S(1)}, u32[]{:S(2)}, u32[]{:S(2)}) collective-permute-start(bf16[2,128,128]{2,1,0:T(8,128)(2,1)S(1)} %add_convert_fusion.4.refs_0_), channel_id=1, source_target_pairs={{0,2},{1,3},{2,0},{3,1},{4,6},{5,7},{6,4},{7,5},{8,10},{9,11},{10,... | collective-permute-start | bytes 196616 | tf_op jit(solution)/shard_map/ppermute | solution.py:217
  66.8 2.9 %collective-permute-done.13.refs_2_ = bf16[2,128,128]{2,1,0:T(8,128)(2,1)S(1)} collective-permute-done((bf16[2,128,128]{2,1,0:T(8,128)(2,1)S(1)}, bf16[2,128,128]{2,1,0:T(8,128)(2,1)S(1)}, u32[]{:S(2)}, u32[]{:S(2)}) %collective-permute-start.13) | collective-permute-done | bytes 65568 | tf_op jit(solution)/shard_map/ppermute | solution.py:217
  69.6 0.1 collective-permute-start.14
  69.7 0.1 add_convert_fusion.1
  69.8 1.5 %collective-permute-start.12 = (bf16[2,576,128]{2,1,0:T(8,128)(2,1)S(1)}, bf16[2,576,128]{2,1,0:T(8,128)(2,1)S(1)}, u32[]{:S(2)}, u32[]{:S(2)}) collective-permute-start(bf16[2,576,128]{2,1,0:T(8,128)(2,1)S(1)} %add_convert_fusion.1), channel_id=1, source_target_pairs={{0,2},{1,3},{2,0},{3,1},{4,6},{5,7},{6,4},{7,5},{8,10},{9,11},{10,... | collective-permute-start | bytes 884744 | tf_op jit(solution)/shard_map/ppermute | solution.py:217
  71.3 0.0 collective-permute-done.14
  71.3 0.8 spread.1
  72.1 7.1 %collective-permute-done.12 = bf16[2,576,128]{2,1,0:T(8,128)(2,1)S(1)} collective-permute-done((bf16[2,576,128]{2,1,0:T(8,128)(2,1)S(1)}, bf16[2,576,128]{2,1,0:T(8,128)(2,1)S(1)}, u32[]{:S(2)}, u32[]{:S(2)}) %collective-permute-start.12) | collective-permute-done | bytes 294944 | tf_op jit(solution)/shard_map/ppermute | solution.py:217
  79.3 0.8 fusion
  80.1 1.8 %reduce-scatter.2.cloned.1.call-done = bf16[1,576,128]{2,1,0:T(8,128)(2,1)} async-done(((bf16[4,576,128]{2,1,0:T(8,128)(2,1)}), bf16[1,576,128]{2,1,0:T(8,128)(2,1)}) %reduce-scatter.2.cloned.1.call-update) | async-done | bytes 147472 | tf_op jit(solution)/shard_map/reduce_scatter | solution.py:318
  (8 shorter events, 0.1 us)
Async XLA Ops:
  7.2 74.8 %reduce-scatter.2.cloned.1.call-start = ((), (), s32[]{:S(2)}) async-start(), calls=%async_computation.1 | async-start | bytes 737280 | tf_op jit(solution)/shard_map/reduce_scatter | solution.py:318
  10.3 37.9 %copy-start = (bf16[1424,128]{1,0:T(8,128)(2,1)S(1)}, bf16[1424,128]{1,0:T(8,128)(2,1)}, u32[]{:S(2)}) copy-start(bf16[1424,128]{1,0:T(8,128)(2,1)} %get-tuple-element.33.refs_1_.refs_0_) | copy-start | bytes 1093636
  10.3 37.9 %copy-start.2 = (f32[8,128]{1,0:T(8,128)S(1)}, f32[8,128]{1,0:T(8,128)}, u32[]{:S(2)}) copy-start(f32[8,128]{1,0:T(8,128)} %get-tuple-element.41.refs_5_) | copy-start | bytes 12292
  10.3 11.7 %collective-permute-start.1 = (bf16[1424,128]{1,0:T(8,128)(2,1)}, bf16[1424,128]{1,0:T(8,128)(2,1)S(1)}, u32[]{:S(2)}, u32[]{:S(2)}) collective-permute-start(bf16[1424,128]{1,0:T(8,128)(2,1)} %get-tuple-element.33.refs_1_.refs_0_), channel_id=1, source_target_pairs={{0,1},{1,0},{2,3},{3,2},{4,5},{5,4},{6,7},{7,6},{8,9},{9,8},{10,11... | collective-permute-start | bytes 1093640 | tf_op jit(solution)/shard_map/ppermute | solution.py:217
  10.8 11.9 %collective-permute-start = (bf16[1424,128]{1,0:T(8,128)(2,1)}, bf16[1424,128]{1,0:T(8,128)(2,1)S(1)}, u32[]{:S(2)}, u32[]{:S(2)}) collective-permute-start(bf16[1424,128]{1,0:T(8,128)(2,1)} %get-tuple-element.33.refs_1_.refs_0_), channel_id=1, source_target_pairs={{0,2},{1,3},{2,0},{3,1},{4,6},{5,7},{6,4},{7,5},{8,10},{9,11},{10,... | collective-permute-start | bytes 1093640 | tf_op jit(solution)/shard_map/ppermute | solution.py:217
  13.4 8.6 %collective-permute-start.2 = (bf16[8,128,128]{2,1,0:T(8,128)(2,1)}, bf16[8,128,128]{2,1,0:T(8,128)(2,1)S(1)}, u32[]{:S(2)}, u32[]{:S(2)}) collective-permute-start(bf16[8,128,128]{2,1,0:T(8,128)(2,1)} %get-tuple-element.37), channel_id=1, source_target_pairs={{0,16},{16,0},{1,17},{17,1},{2,18},{18,2},{3,19},{19,3},{4,20},{20... | collective-permute-start | bytes 786440 | tf_op jit(solution)/shard_map/ppermute | solution.py:256
  22.7 7.1 %collective-permute-start.3 = (bf16[1424,128]{1,0:T(8,128)(2,1)S(1)}, bf16[1424,128]{1,0:T(8,128)(2,1)S(1)}, u32[]{:S(2)}, u32[]{:S(2)}) collective-permute-start(bf16[1424,128]{1,0:T(8,128)(2,1)S(1)} %collective-permute-done.refs_3_.refs_2_), channel_id=1, source_target_pairs={{0,1},{1,0},{2,3},{3,2},{4,5},{5,4},{6,7},{7,6},{8,9},{9,8},{10,11... | collective-permute-start | bytes 1093640 | tf_op jit(solution)/shard_map/ppermute | solution.py:217
  23.7 28.5 %copy-start.1 = (bf16[2,512,128]{2,1,0:T(8,128)(2,1)S(1)}, bf16[2,512,128]{2,1,0:T(8,128)(2,1)}, u32[]{:S(2)}) copy-start(bf16[2,512,128]{2,1,0:T(8,128)(2,1)} %refs_4_.1) | copy-start | bytes 786436
  23.8 6.0 %collective-permute-start.4 = (bf16[4,128,128]{2,1,0:T(8,128)(2,1)S(1)}, bf16[4,128,128]{2,1,0:T(8,128)(2,1)S(1)}, u32[]{:S(2)}, u32[]{:S(2)}) collective-permute-start(bf16[4,128,128]{2,1,0:T(8,128)(2,1)S(1)} %slice.32), channel_id=1, source_target_pairs={{0,2},{1,3},{2,0},{3,1},{4,6},{5,7},{6,4},{7,5},{8,10},{9,11},{10,... | collective-permute-start | bytes 393224 | tf_op jit(solution)/shard_map/ppermute | solution.py:217
  29.8 19.9 %collective-permute-start.5 = (bf16[2,128,128]{2,1,0:T(8,128)(2,1)S(1)}, bf16[2,128,128]{2,1,0:T(8,128)(2,1)S(1)}, u32[]{:S(2)}, u32[]{:S(2)}) collective-permute-start(bf16[2,128,128]{2,1,0:T(8,128)(2,1)S(1)} %slice.35), channel_id=1, source_target_pairs={{0,1},{1,0},{2,3},{3,2},{4,5},{5,4},{6,7},{7,6},{8,9},{9,8},{10,11... | collective-permute-start | bytes 196616 | tf_op jit(solution)/shard_map/ppermute | solution.py:217
  49.8 4.3 %collective-permute-start.6 = (bf16[2,128,128]{2,1,0:T(8,128)(2,1)S(1)}, bf16[2,128,128]{2,1,0:T(8,128)(2,1)S(1)}, u32[]{:S(2)}, u32[]{:S(2)}) collective-permute-start(bf16[2,128,128]{2,1,0:T(8,128)(2,1)S(1)} %add_convert_fusion.6), channel_id=1, source_target_pairs={{0,4},{1,5},{2,6},{3,7},{4,0},{5,1},{6,2},{7,3},{8,12},{9,13},{10,... | collective-permute-start | bytes 196616 | tf_op jit(solution)/shard_map/ppermute | solution.py:256
  50.4 3.8 %collective-permute-start.9 = (f32[16,128]{1,0:T(8,128)S(1)}, f32[16,128]{1,0:T(8,128)S(1)}, u32[]{:S(2)}, u32[]{:S(2)}) collective-permute-start(f32[16,128]{1,0:T(8,128)S(1)} %get-tuple-element.47.refs_5_), channel_id=1, source_target_pairs={{0,3},{1,2},{2,1},{3,0},{4,7},{5,6},{6,5},{7,4},{8,11},{9,10},{10,... | collective-permute-start | bytes 24584 | tf_op jit(solution)/shard_map/ppermute | solution.py:217
  50.4 3.8 %collective-permute-start.8 = (f32[16,128]{1,0:T(8,128)S(1)}, f32[16,128]{1,0:T(8,128)S(1)}, u32[]{:S(2)}, u32[]{:S(2)}) collective-permute-start(f32[16,128]{1,0:T(8,128)S(1)} %get-tuple-element.47.refs_5_), channel_id=1, source_target_pairs={{0,2},{1,3},{2,0},{3,1},{4,6},{5,7},{6,4},{7,5},{8,10},{9,11},{10,... | collective-permute-start | bytes 24584 | tf_op jit(solution)/shard_map/ppermute | solution.py:217
  52.0 2.2 %collective-permute-start.7 = (f32[16,128]{1,0:T(8,128)S(1)}, f32[16,128]{1,0:T(8,128)S(1)}, u32[]{:S(2)}, u32[]{:S(2)}) collective-permute-start(f32[16,128]{1,0:T(8,128)S(1)} %get-tuple-element.47.refs_5_), channel_id=1, source_target_pairs={{0,1},{1,0},{2,3},{3,2},{4,5},{5,4},{6,7},{7,6},{8,9},{9,8},{10,11... | collective-permute-start | bytes 24584 | tf_op jit(solution)/shard_map/ppermute | solution.py:217
  58.3 6.9 %collective-permute-start.10 = (bf16[4,576,128]{2,1,0:T(8,128)(2,1)S(1)}, bf16[4,576,128]{2,1,0:T(8,128)(2,1)S(1)}, u32[]{:S(2)}, u32[]{:S(2)}) collective-permute-start(bf16[4,576,128]{2,1,0:T(8,128)(2,1)S(1)} %get-tuple-element.54), channel_id=1, source_target_pairs={{0,1},{1,0},{2,3},{3,2},{4,5},{5,4},{6,7},{7,6},{8,9},{9,8},{10,11... | collective-permute-start | bytes 1769480 | tf_op jit(solution)/shard_map/ppermute | solution.py:217
  58.7 6.6 %collective-permute-start.11 = (bf16[2,128,128]{2,1,0:T(8,128)(2,1)S(1)}, bf16[2,128,128]{2,1,0:T(8,128)(2,1)S(1)}, u32[]{:S(2)}, u32[]{:S(2)}) collective-permute-start(bf16[2,128,128]{2,1,0:T(8,128)(2,1)S(1)} %add_convert_fusion.5), channel_id=1, source_target_pairs={{0,8},{1,9},{2,10},{3,11},{4,12},{5,13},{6,14},{7,15},{8,0},{9,1},... | collective-permute-start | bytes 196616 | tf_op jit(solution)/shard_map/ppermute | solution.py:256
  65.3 4.3 %collective-permute-start.13 = (bf16[2,128,128]{2,1,0:T(8,128)(2,1)S(1)}, bf16[2,128,128]{2,1,0:T(8,128)(2,1)S(1)}, u32[]{:S(2)}, u32[]{:S(2)}) collective-permute-start(bf16[2,128,128]{2,1,0:T(8,128)(2,1)S(1)} %add_convert_fusion.4.refs_0_), channel_id=1, source_target_pairs={{0,2},{1,3},{2,0},{3,1},{4,6},{5,7},{6,4},{7,5},{8,10},{9,11},{10,... | collective-permute-start | bytes 196616 | tf_op jit(solution)/shard_map/ppermute | solution.py:217
  69.6 1.6 %collective-permute-start.14 = (bf16[4,128,128]{2,1,0:T(8,128)(2,1)S(1)}, bf16[4,128,128]{2,1,0:T(8,128)(2,1)S(1)}, u32[]{:S(2)}, u32[]{:S(2)}) collective-permute-start(bf16[4,128,128]{2,1,0:T(8,128)(2,1)S(1)} %pad_maximum_fusion), channel_id=1, source_target_pairs={{0,1},{1,0},{2,3},{3,2},{4,5},{5,4},{6,7},{7,6},{8,9},{9,8},{10,11... | collective-permute-start | bytes 393224 | tf_op jit(solution)/shard_map/ppermute | solution.py:217
  69.8 9.5 %collective-permute-start.12 = (bf16[2,576,128]{2,1,0:T(8,128)(2,1)S(1)}, bf16[2,576,128]{2,1,0:T(8,128)(2,1)S(1)}, u32[]{:S(2)}, u32[]{:S(2)}) collective-permute-start(bf16[2,576,128]{2,1,0:T(8,128)(2,1)S(1)} %add_convert_fusion.1), channel_id=1, source_target_pairs={{0,2},{1,3},{2,0},{3,1},{4,6},{5,7},{6,4},{7,5},{8,10},{9,11},{10,... | collective-permute-start | bytes 884744 | tf_op jit(solution)/shard_map/ppermute | solution.py:217
Sparse Core Ops, SparseCore 0:
  61.4 20.4 reduce-scatter.1

commit v5 on v3

--- a/solution.py
+++ b/solution.py
@@ -57,7 +57,7 @@
 
 def pack_kernel(
     idx_ref, pos_hbm, q_hbm, og_hbm, lat_hbm, attn_hbm, wuv_hbm,
-    lat_msg, q_msg, delta_ref, term_ref,
+    lat_msg, q_msg, delta_ref, keep_ref, send_ref,
     pos_ref, og_ref, attn_ref, wuv_ref, term, sems,
 ):
     heads, width, tok = q_hbm.shape
@@ -91,7 +91,8 @@
     me = lax.rem(idx_ref[0], GROUP)
     for k in range(GROUP):
         at = pl.multiple_of(jnp.bitwise_xor(me, k) * step, step)
-        term_ref[k * heads : (k + 1) * heads] = term[:, pl.ds(at, step), :].astype(BF16)
+        target = send_ref if k % 2 else keep_ref
+        target[k // 2 * heads : (k // 2 + 1) * heads] = term[:, pl.ds(at, step), :].astype(BF16)
     for copy in copies[4:]:
         copy.wait()
 
@@ -194,6 +195,14 @@
         part_refs[a][lat:, :] = along[lat:].astype(BF16)
 
 
+def sum_kernel(gq_own_ref, gq_got_ref, gq_last_ref, *refs):
+    parts, (lat_out_ref, q_out_ref) = refs[:-2], refs[-2:]
+    lat_out_ref[...] = sum(part[...].astype(F32) for part in parts).astype(BF16)
+    for h in range(q_out_ref.shape[0]):
+        pieces = (gq_own_ref[h], gq_got_ref[h], gq_last_ref[h])
+        q_out_ref[h] = sum(piece.astype(F32) for piece in pieces).astype(BF16)
+
+
 def spread_kernel(scale, idx_ref, *refs):
     chunks, out_ref = refs[:GROUP], refs[GROUP]
     step = chunks[0].shape[1]
@@ -214,22 +223,23 @@
     wide = -(-(width + EXTRA) // 128) * 128
     factor = (HEAD_DIM + ROPE) ** (-0.5)
 
-    def swap(x, mask):
-        return lax.ppermute(x, "ctx", [(i, i ^ mask) for i in range(n_ctx)])
+    def swap(x, mask, axis="ctx", size=n_ctx):
+        return lax.ppermute(x, axis, [(i, i ^ mask) for i in range(size)])
 
     def after(x, *done):
         return lax.optimization_barrier((x, done))[0]
 
     idx = lax.axis_index("ctx").reshape(1)
     step = lat // GROUP
-    lat_msg, q_msg, delta, term = call(
+    lat_msg, q_msg, delta, keep, send = call(
         pack_kernel,
         "pack",
         [
             ((width + EXTRA, tok), BF16),
             ((heads * (width + HEAD_DIM) + EXTRA, tok), BF16),
             ((8, tok), F32),
-            ((GROUP * heads, step, HEAD_DIM), BF16),
+            ((2 * heads, step, HEAD_DIM), BF16),
+            ((2 * heads, step, HEAD_DIM), BF16),
         ],
         [
             idx,
@@ -253,37 +263,34 @@
         limit=PACK_LIMIT,
     )
 
-    def hop(total, axis, size, mask, *done):
-        other = lax.ppermute(total, axis, [(i, i ^ mask) for i in range(size)])
-        return total, after(other, *done) if done else other
-
-    def add(pair):
-        return (pair[0].astype(F32) + pair[1].astype(F32)).astype(BF16)
-
-    dp_hops = [("dp", n_dp, 1 << bit) for bit in range((n_dp - 1).bit_length())]
-    line_hops = [("ctx", n_ctx, GROUP << bit) for bit in range(line_bits)]
-
-    firsts = {1 << bit: swap(lat_msg, GROUP << bit) for bit in range(line_bits)}
+    def add(a, b):
+        return (a.astype(F32) + b.astype(F32)).astype(BF16)
+
+    dp_hops = [(1 << bit, "dp", n_dp) for bit in range((n_dp - 1).bit_length())]
+    line_hops = [(GROUP << bit,) for bit in range(line_bits)]
+
+    firsts = [swap(lat_msg, GROUP << bit) for bit in range(line_bits)]
     q_across = swap(q_msg, 2)
     q_core = swap(q_msg, 1)
-    twins = hop(term, *dp_hops[0])
-    firsts, q_across, q_core, twins = lax.optimization_barrier((firsts, q_across, q_core, twins))
-    for step_hop in dp_hops[1:]:
-        twins = hop(add(twins), *step_hop)
-    total = add(twins)
+    got_pair = swap(send, 1)
+    q_core, q_across, firsts, got_pair = lax.optimization_barrier(
+        (q_core, q_across, firsts, got_pair)
+    )
+    pair = add(keep, got_pair)
 
     held = {0: lat_msg}
     for bit in reversed(range(line_bits)):
         held.update({m | 1 << bit: swap(x, GROUP << bit) for m, x in held.items() if m})
-        held[1 << bit] = firsts[1 << bit]
+        held[1 << bit] = firsts[bit]
     lats = [held[m] for m in range(lines)]
     q_far = swap(q_across, 1)
-    half = 2 * heads
-    got_half = swap(total[half:], 2)
-    lats, q_far, got_half = lax.optimization_barrier((lats, q_far, got_half))
+    got_pair = swap(pair, *dp_hops[0])
+    q_far, lats, got_pair = lax.optimization_barrier((q_far, lats, got_pair))
+    pair = add(pair, got_pair)
+    for step_hop in dp_hops[1:]:
+        pair = add(pair, swap(pair, *step_hop))
     qs = [q_msg, q_core, q_across, q_far]
-    total = add((total[:half], got_half))
-    got_own = swap(total[heads:], 1)
+    got_own = swap(pair[heads:], 2)
 
     s, k_nat, stat = call(
         functools.partial(score_kernel, factor, lines, width, heads),
@@ -294,8 +301,8 @@
         flops=2 * keys * all_rows * wide,
     )
     stats = [stat] + [swap(stat, k) for k in range(1, GROUP)]
-    mine = add((total[:heads], after(got_own, stat)))
-    near = hop(mine, *line_hops[0])
+    mine = add(pair[:heads], after(got_own, stat))
+    near = swap(mine, *line_hops[0])
     g, gp = call(
         functools.partial(context_kernel, width, heads),
         "context",
@@ -303,8 +310,8 @@
         qs + [wuv, k_nat],
         flops=2 * keys * all_rows * lat + 2 * all_rows * lat * HEAD_DIM,
     )
-    mine = add((near[0], after(near[1], gp)))
-    mine, stats = lax.optimization_barrier((mine, stats))
+    near, stats = lax.optimization_barrier((after(near, gp), stats))
+    mine = add(mine, near)
     outs = call(
         functools.partial(grad_kernel, factor, lines, width, heads),
         "gradients",
@@ -320,22 +327,31 @@
         flops=2 * keys * all_rows * (2 * width + lat),
     )
     parts, (gq_own, gq_core, gq_across) = list(outs[:lines]), outs[lines:]
-    kept = [parts[0]]
     gq_got = swap(gq_core, 1)
-    for step_hop in line_hops[1:]:
-        mine = add(hop(after(mine, gq_own), *step_hop))
-    for bit in range(line_bits):
-        for m in [m for m in range(2 << bit, lines) if m >> bit & 1 and not m & (1 << bit) - 1]:
-            parts[m ^ 1 << bit] = add((parts[m ^ 1 << bit], swap(parts[m], GROUP << bit)))
-        if bit == 0:
-            parts, gq_got, mine = lax.optimization_barrier((parts, gq_got, mine))
-    kept += [swap(parts[1 << bit], GROUP << bit) for bit in reversed(range(line_bits))]
-    gq_last = swap(add((gq_across, gq_got[heads:])), 2)
-    mine_two = jnp.concatenate([mine, swap(mine, 2)], axis=0)
-    kept, gq_last, mine_two = lax.optimization_barrier((kept, gq_last, mine_two))
+    for step_hop in line_hops[1:-1]:
+        mine = add(mine, swap(mine, *step_hop))
+    far = [m for m in range(3, lines, 2)]
+    got_far = [swap(parts[m], GROUP) for m in far]
+    got_mine = swap(mine, *line_hops[-1])
+    gq_got, got_far, got_mine = lax.optimization_barrier((gq_got, got_far, got_mine))
+    mine = add(mine, got_mine)
+    for m, got in zip(far, got_far):
+        parts[m ^ 1] = add(parts[m ^ 1], got)
+    for bit in range(1, line_bits):
+        for m in range(3 << bit, lines, 2 << bit):
+            parts[m ^ 1 << bit] = add(parts[m ^ 1 << bit], swap(parts[m], GROUP << bit))
+    gq_last = swap(add(gq_across, gq_got[heads:]), 2)
+    kept = [swap(parts[1 << bit], GROUP << bit) for bit in reversed(range(line_bits))]
+    across = swap(mine, 2)
+    gq_last, kept, across = lax.optimization_barrier((gq_last, kept, across))
+    mine_two = jnp.concatenate([mine, across], axis=0)
     other_two = swap(mine_two, 1)
-    grad_lat = sum(p.astype(F32) for p in kept).astype(BF16)
-    grad_q = sum(p.astype(F32) for p in (gq_own, gq_got[:heads], gq_last)).astype(BF16)
+    grad_lat, grad_q = call(
+        sum_kernel,
+        "last_sums",
+        [((width, tok), BF16), ((heads, width, tok), BF16)],
+        [gq_own, gq_got, gq_last, parts[0]] + kept,
+    )
     scale = 1.0 / math.sqrt(tok * n_ctx * n_dp)
     pieces = [mine_two[:heads], other_two[:heads], mine_two[heads:], other_two[heads:]]
     (grad_w,) = call(

time: 62.5 us -> 60.2 us (0.963)
  other arithmetic: 2.82 us -> 1.18 us
  waiting for transfers between devices: 23.5 us -> 22.2 us
  Pallas kernels: 10 us -> 10.9 us
    broadcast_in_dim x2 -> x0, other arithmetic: 1.56 us -> none  [body(): return (jnp.transpose(grad_q, (2, 0, 1))[None], grad_lat.T[None], grad_w)]
    ppermute x21, waiting for transfers between devices: 23.5 us -> 22.2 us  [swap(): return lax.ppermute(x, axis, [(i, i ^ mask) for i in range(size)])]
    pallas_call x5 -> x6, Pallas kernels: 10 us -> 10.9 us  [call(): pl.pallas_call(kernel, out_shape=[jax.ShapeDtypeStruct(s, d) for s, d in...]
  transfers between devices with their start and end apart: 21 -> 21, of which waited for: 9 -> 11; matrix products, arithmetic and copies ran while one was open for 3% -> 2% of each run, Pallas kernels for 5% -> 6%
where the time goes in v5:
time: 60.2 us; the launch traced here: 60 us
  starting transfers between devices  22.3 us (37%)
  waiting for transfers between devices  22.2 us (37%)
  Pallas kernels  10.9 us (18%)
  local copies, waits for them, and re-layouts  2.61 us (4%)
  other arithmetic  1.18 us (2%)
  between operations  0.76 us (1%)
    ppermute x21, starting transfers between devices, swap(): return lax.ppermute(x, axis, [(i, i ^ mask) for i in range(size)])  22.3 us
    ppermute x21, waiting for transfers between devices, swap(): return lax.ppermute(x, axis, [(i, i ^ mask) for i in range(size)])  22.2 us
    pallas_call x6, Pallas kernels, call(): pl.pallas_call(kernel, out_shape=[jax.ShapeDtypeStruct(s, d) for s, d in...  10.9 us
    unnamed x12, local copies, waits for them, and re-layouts  2.59 us
  transfers between devices with their start and end apart: 21, of which 11 were waited for; matrix products, arithmetic and copies ran while one was open for 2% of the time, Pallas kernels for 6%

profile of v5, /device:TPU:0, one launch (start us, length us, event | category | flops | bytes accessed | tf_op | source)
XLA Modules:
  0.0 60.0 jit_solution(16209169370326146909)
XLA Ops:
  0.6 0.0 copy-start.2
  0.6 3.1 %pack.1 = (bf16[592,128]{1,0:T(8,128)(2,1)}, bf16[1424,128]{1,0:T(8,128)(2,1)}, f32[8,128]{1,0:T(8,128)}, bf16[4,128,128]{2,1,0:T(8,128)(2,1)}, bf16[4,128,128]{2,1,0:T(8,128)(2,1)}) custom-call(s32[1]{0:T(128)} %bitcast.idx_ref, s32[1,128]{1,0:T(1,128)} %pos_hbm.1, bf16[2,576,128]{2,1,0:T(8,128)(2,1)} %bitcast.15, bf16[128,2,128]{2,1,0:T(2,128)(2,1)} %bitcast.18, ...), custom_call_target="tpu_custom_call" | custom-call | bytes 1815044 | tf_op jit(solution)/shard_map/pack/pallas_call | solution.py:39
  3.7 0.0 copy-start.1
  3.7 3.0 %collective-permute-start.1 = (bf16[1424,128]{1,0:T(8,128)(2,1)}, bf16[1424,128]{1,0:T(8,128)(2,1)S(1)}, u32[]{:S(2)}, u32[]{:S(2)}) collective-permute-start(bf16[1424,128]{1,0:T(8,128)(2,1)} %get-tuple-element.47.refs_4_.refs_0_), channel_id=1, source_target_pairs={{0,2},{1,3},{2,0},{3,1},{4,6},{5,7},{6,4},{7,5},{8,10},{9,11},{10,... | collective-permute-start | bytes 1093640 | tf_op jit(solution)/shard_map/ppermute | solution.py:227
  6.8 0.0 collective-permute-start
  6.8 2.6 %collective-permute-start.3 = (bf16[592,128]{1,0:T(8,128)(2,1)}, bf16[592,128]{1,0:T(8,128)(2,1)S(1)}, u32[]{:S(2)}, u32[]{:S(2)}) collective-permute-start(bf16[592,128]{1,0:T(8,128)(2,1)} %get-tuple-element.55.refs_0_), channel_id=1, source_target_pairs={{0,8},{1,9},{2,10},{3,11},{4,12},{5,13},{6,14},{7,15},{8,0},{9,1},... | collective-permute-start | bytes 454664 | tf_op jit(solution)/shard_map/ppermute | solution.py:227
  9.4 1.6 %collective-permute-start.2 = (bf16[592,128]{1,0:T(8,128)(2,1)}, bf16[592,128]{1,0:T(8,128)(2,1)S(1)}, u32[]{:S(2)}, u32[]{:S(2)}) collective-permute-start(bf16[592,128]{1,0:T(8,128)(2,1)} %get-tuple-element.55.refs_0_), channel_id=1, source_target_pairs={{0,4},{1,5},{2,6},{3,7},{4,0},{5,1},{6,2},{7,3},{8,12},{9,13},{10,... | collective-permute-start | bytes 454664 | tf_op jit(solution)/shard_map/ppermute | solution.py:227
  10.9 0.0 collective-permute-start.4
  10.9 1.6 %collective-permute-done.4 = bf16[4,128,128]{2,1,0:T(8,128)(2,1)S(1)} collective-permute-done((bf16[4,128,128]{2,1,0:T(8,128)(2,1)}, bf16[4,128,128]{2,1,0:T(8,128)(2,1)S(1)}, u32[]{:S(2)}, u32[]{:S(2)}) %collective-permute-start.4) | collective-permute-done | bytes 131104 | tf_op jit(solution)/shard_map/ppermute | solution.py:227
  12.5 5.1 %collective-permute-done.3.refs_2_ = bf16[592,128]{1,0:T(8,128)(2,1)S(1)} collective-permute-done((bf16[592,128]{1,0:T(8,128)(2,1)}, bf16[592,128]{1,0:T(8,128)(2,1)S(1)}, u32[]{:S(2)}, u32[]{:S(2)}) %collective-permute-start.3) | collective-permute-done | bytes 151584 | tf_op jit(solution)/shard_map/ppermute | solution.py:227
  17.6 0.2 collective-permute-done.2.refs_1_
  17.8 0.0 collective-permute-done.1.refs_6_.refs_2_
  17.8 0.0 collective-permute-done.refs_5_.refs_1_
  17.8 1.4 %collective-permute-start.6 = (bf16[592,128]{1,0:T(8,128)(2,1)S(1)}, bf16[592,128]{1,0:T(8,128)(2,1)S(1)}, u32[]{:S(2)}, u32[]{:S(2)}) collective-permute-start(bf16[592,128]{1,0:T(8,128)(2,1)S(1)} %collective-permute-done.3.refs_2_), channel_id=1, source_target_pairs={{0,4},{1,5},{2,6},{3,7},{4,0},{5,1},{6,2},{7,3},{8,12},{9,13},{10,... | collective-permute-start | bytes 454664 | tf_op jit(solution)/shard_map/ppermute | solution.py:227
  19.2 0.0 collective-permute-start.5
  19.2 0.9 %add_convert_fusion.3 = bf16[4,128,128]{2,1,0:T(8,128)(2,1)S(1)} fusion(bf16[4,128,128]{2,1,0:T(8,128)(2,1)S(1)} %collective-permute-done.4, bf16[4,128,128]{2,1,0:T(8,128)(2,1)} %get-tuple-element.53), kind=kLoop, calls=%fused_computation.3 | loop fusion | flops 262144 | bytes 393216 | tf_op jit(solution)/shard_map/convert_element_type | solution.py:267
  20.2 1.6 %collective-permute-start.7 = (bf16[4,128,128]{2,1,0:T(8,128)(2,1)S(1)}, bf16[4,128,128]{2,1,0:T(8,128)(2,1)S(1)}, u32[]{:S(2)}, u32[]{:S(2)}) collective-permute-start(bf16[4,128,128]{2,1,0:T(8,128)(2,1)S(1)} %add_convert_fusion.3), channel_id=1, source_target_pairs={{0,16},{16,0},{1,17},{17,1},{2,18},{18,2},{3,19},{19,3},{4,20},{20... | collective-permute-start | bytes 393224 | tf_op jit(solution)/shard_map/ppermute | solution.py:227
  21.7 4.4 %collective-permute-done.7 = bf16[4,128,128]{2,1,0:T(8,128)(2,1)S(1)} collective-permute-done((bf16[4,128,128]{2,1,0:T(8,128)(2,1)S(1)}, bf16[4,128,128]{2,1,0:T(8,128)(2,1)S(1)}, u32[]{:S(2)}, u32[]{:S(2)}) %collective-permute-start.7) | collective-permute-done | bytes 131104 | tf_op jit(solution)/shard_map/ppermute | solution.py:227
  26.2 0.0 collective-permute-done.6.refs_3_
  26.2 0.0 collective-permute-done.5.refs_7_.refs_3_
  26.2 0.6 collective-permute-start.8
  26.8 0.0 copy-start
  26.8 1.0 %copy-done = bf16[1424,128]{1,0:T(8,128)(2,1)S(1)} copy-done((bf16[1424,128]{1,0:T(8,128)(2,1)S(1)}, bf16[1424,128]{1,0:T(8,128)(2,1)}, u32[]{:S(2)}) %copy-start) | copy-done | bytes 364568
  27.8 0.0 copy-start.3
  27.8 0.9 %copy-done.3 = bf16[592,128]{1,0:T(8,128)(2,1)S(1)} copy-done((bf16[592,128]{1,0:T(8,128)(2,1)S(1)}, bf16[592,128]{1,0:T(8,128)(2,1)}, u32[]{:S(2)}) %copy-start.3) | copy-done | bytes 151576
  28.7 0.0 copy-start.5
  28.7 0.7 %copy-done.5 = f32[8,128]{1,0:T(8,128)S(1)} copy-done((f32[8,128]{1,0:T(8,128)S(1)}, f32[8,128]{1,0:T(8,128)}, u32[]{:S(2)}) %copy-start.5) | copy-done | bytes 4120
  29.4 0.0 copy-start.4
  29.4 1.6 %scores.1 = (f32[512,1024]{1,0:T(8,128)S(1)}, bf16[512,640]{1,0:T(8,128)(2,1)S(1)}, f32[16,128]{1,0:T(8,128)S(1)}) custom-call(bf16[592,128]{1,0:T(8,128)(2,1)S(1)} %copy-done.3, bf16[592,128]{1,0:T(8,128)(2,1)S(1)} %collective-permute-done.2.refs_1_, bf16[592,128]{1,0:T(8,128)(2,1)S(1)} %collective-permute-done.3.refs_2_, ...), custom_call_target="tpu_custom_call" | custom-call | flops 671088640 | bytes 4829184 | tf_op jit(solution)/shard_map/scores/pallas_call | solution.py:39
  31.0 0.0 collective-permute-done.8
  31.0 0.6 collective-permute-start.9
  31.6 0.3 collective-permute-start.12
  32.0 1.3 %collective-permute-start.11 = (f32[16,128]{1,0:T(8,128)S(1)}, f32[16,128]{1,0:T(8,128)S(1)}, u32[]{:S(2)}, u32[]{:S(2)}) collective-permute-start(f32[16,128]{1,0:T(8,128)S(1)} %get-tuple-element.68.refs_8_), channel_id=1, source_target_pairs={{0,2},{1,3},{2,0},{3,1},{4,6},{5,7},{6,4},{7,5},{8,10},{9,11},{10,... | collective-permute-start | bytes 24584 | tf_op jit(solution)/shard_map/ppermute | solution.py:227
  33.2 0.3 collective-permute-start.10
  33.5 0.0 copy-done.2
  33.5 0.0 copy-done.1
  33.5 1.2 %context.1 = (bf16[512,1024]{1,0:T(8,128)(2,1)S(1)}, f32[512,1024]{1,0:T(8,128)S(1)}) custom-call(bf16[1424,128]{1,0:T(8,128)(2,1)S(1)} %copy-done.1, bf16[1424,128]{1,0:T(8,128)(2,1)S(1)} %collective-permute-done.refs_5_.refs_1_, bf16[1424,128]{1,0:T(8,128)(2,1)S(1)} %collective-permute-done.1.refs_6_.refs_2_, ...), custom_call_target="tpu_custom_call" | custom-call | flops 671088640 | bytes 5521408 | tf_op jit(solution)/shard_map/context/pallas_call | solution.py:39
  34.7 0.6 %collective-permute-done.9 = bf16[2,128,128]{2,1,0:T(8,128)(2,1)S(1)} collective-permute-done((bf16[2,128,128]{2,1,0:T(8,128)(2,1)S(1)}, bf16[2,128,128]{2,1,0:T(8,128)(2,1)S(1)}, u32[]{:S(2)}, u32[]{:S(2)}) %collective-permute-start.9) | collective-permute-done | bytes 65568 | tf_op jit(solution)/shard_map/ppermute | solution.py:227
  35.3 0.0 collective-permute-done.12.refs_11_
  35.4 0.3 collective-permute-done.11.refs_10_
  35.6 0.0 collective-permute-done.10.refs_9_
  35.6 0.0 copy-done.4
  35.6 3.3 %gradients.1 = (bf16[576,128]{1,0:T(8,128)(2,1)S(1)}, bf16[576,128]{1,0:T(8,128)(2,1)S(1)}, bf16[576,128]{1,0:T(8,128)(2,1)S(1)}, bf16[576,128]{1,0:T(8,128)(2,1...) custom-call(bf16[592,128]{1,0:T(8,128)(2,1)S(1)} %copy-done.4, ...), custom_call_target="tpu_custom_call" | custom-call | flops 1744830464 | bytes 9109504 | tf_op jit(solution)/shard_map/gradients/pallas_call | solution.py:39
  38.9 0.3 collective-permute-start.13
  39.2 1.4 %collective-permute-start.14 = (bf16[576,128]{1,0:T(8,128)(2,1)S(1)}, bf16[576,128]{1,0:T(8,128)(2,1)S(1)}, u32[]{:S(2)}, u32[]{:S(2)}) collective-permute-start(bf16[576,128]{1,0:T(8,128)(2,1)S(1)} %get-tuple-element.76), channel_id=1, source_target_pairs={{0,4},{1,5},{2,6},{3,7},{4,0},{5,1},{6,2},{7,3},{8,12},{9,13},{10,... | collective-permute-start | bytes 442376 | tf_op jit(solution)/shard_map/ppermute | solution.py:227
  40.7 2.5 %collective-permute-start.15 = (bf16[2,128,128]{2,1,0:T(8,128)(2,1)S(1)}, bf16[2,128,128]{2,1,0:T(8,128)(2,1)S(1)}, u32[]{:S(2)}, u32[]{:S(2)}) collective-permute-start(bf16[2,128,128]{2,1,0:T(8,128)(2,1)S(1)} %add_convert_fusion.5), channel_id=1, source_target_pairs={{0,8},{1,9},{2,10},{3,11},{4,12},{5,13},{6,14},{7,15},{8,0},{9,1},... | collective-permute-start | bytes 196616 | tf_op jit(solution)/shard_map/ppermute | solution.py:227
  43.1 0.3 collective-permute-start.18
  43.4 2.8 %collective-permute-done.15 = bf16[2,128,128]{2,1,0:T(8,128)(2,1)S(1)} collective-permute-done((bf16[2,128,128]{2,1,0:T(8,128)(2,1)S(1)}, bf16[2,128,128]{2,1,0:T(8,128)(2,1)S(1)}, u32[]{:S(2)}, u32[]{:S(2)}) %collective-permute-start.15) | collective-permute-done | bytes 65568 | tf_op jit(solution)/shard_map/ppermute | solution.py:227
  46.2 1.0 %collective-permute-done.14 = bf16[576,128]{1,0:T(8,128)(2,1)S(1)} collective-permute-done((bf16[576,128]{1,0:T(8,128)(2,1)S(1)}, bf16[576,128]{1,0:T(8,128)(2,1)S(1)}, u32[]{:S(2)}, u32[]{:S(2)}) %collective-permute-start.14) | collective-permute-done | bytes 147488 | tf_op jit(solution)/shard_map/ppermute | solution.py:227
  47.3 0.0 collective-permute-done.13.gq_got_ref
  47.3 0.1 add_convert_fusion
  47.4 1.2 %collective-permute-start.16 = (bf16[2,576,128]{2,1,0:T(8,128)(2,1)S(1)}, bf16[2,576,128]{2,1,0:T(8,128)(2,1)S(1)}, u32[]{:S(2)}, u32[]{:S(2)}) collective-permute-start(bf16[2,576,128]{2,1,0:T(8,128)(2,1)S(1)} %add_convert_fusion), channel_id=1, source_target_pairs={{0,2},{1,3},{2,0},{3,1},{4,6},{5,7},{6,4},{7,5},{8,10},{9,11},{10,... | collective-permute-start | bytes 884744 | tf_op jit(solution)/shard_map/ppermute | solution.py:227
  48.6 2.4 %collective-permute-start.17 = (bf16[576,128]{1,0:T(8,128)(2,1)S(1)}, bf16[576,128]{1,0:T(8,128)(2,1)S(1)}, u32[]{:S(2)}, u32[]{:S(2)}) collective-permute-start(bf16[576,128]{1,0:T(8,128)(2,1)S(1)} %add_convert_fusion.1), channel_id=1, source_target_pairs={{0,8},{1,9},{2,10},{3,11},{4,12},{5,13},{6,14},{7,15},{8,0},{9,1},... | collective-permute-start | bytes 442376 | tf_op jit(solution)/shard_map/ppermute | solution.py:227
  51.0 1.0 %collective-permute-start.19 = (bf16[2,128,128]{2,1,0:T(8,128)(2,1)S(1)}, bf16[2,128,128]{2,1,0:T(8,128)(2,1)S(1)}, u32[]{:S(2)}, u32[]{:S(2)}) collective-permute-start(bf16[2,128,128]{2,1,0:T(8,128)(2,1)S(1)} %add_convert_fusion.4.refs_0_), channel_id=1, source_target_pairs={{0,2},{1,3},{2,0},{3,1},{4,6},{5,7},{6,4},{7,5},{8,10},{9,11},{10,... | collective-permute-start | bytes 196616 | tf_op jit(solution)/shard_map/ppermute | solution.py:227
  52.0 0.0 collective-permute-done.18.refs_2_
  52.0 4.7 %collective-permute-done.19.refs_2_ = bf16[2,128,128]{2,1,0:T(8,128)(2,1)S(1)} collective-permute-done((bf16[2,128,128]{2,1,0:T(8,128)(2,1)S(1)}, bf16[2,128,128]{2,1,0:T(8,128)(2,1)S(1)}, u32[]{:S(2)}, u32[]{:S(2)}) %collective-permute-start.19) | collective-permute-done | bytes 65568 | tf_op jit(solution)/shard_map/ppermute | solution.py:227
  56.7 1.0 %collective-permute-done.17.refs_1_ = bf16[576,128]{1,0:T(8,128)(2,1)S(1)} collective-permute-done((bf16[576,128]{1,0:T(8,128)(2,1)S(1)}, bf16[576,128]{1,0:T(8,128)(2,1)S(1)}, u32[]{:S(2)}, u32[]{:S(2)}) %collective-permute-start.17) | collective-permute-done | bytes 147488 | tf_op jit(solution)/shard_map/ppermute | solution.py:227
  57.7 0.0 collective-permute-done.16.gq_last_ref
  57.7 0.1 collective-permute-start.20
  57.8 0.9 %last_sums.1 = (bf16[576,128]{1,0:T(8,128)(2,1)}, bf16[2,576,128]{2,1,0:T(8,128)(2,1)}) custom-call(bf16[2,576,128]{2,1,0:T(8,128)(2,1)S(1)} %get-tuple-element.74.gq_own_ref, bf16[4,576,128]{2,1,0:T(8,128)(2,1)S(1)} %collective-permute-done.13.gq_got_ref, bf16[2,576,128]{2,1,0:T(8,128)(2,1)S(1)} %collective-permute-done.16.gq_last_ref, ...), custom_call_target="tpu_custom_call" | custom-call | bytes 2064384 | tf_op jit(solution)/shard_map/last_sums/pallas_call | solution.py:39
  58.7 0.5 collective-permute-done.20
  59.1 0.8 %spread.1 = f32[2,512,128]{2,1,0:T(8,128)} custom-call(s32[1]{0:T(128)} %bitcast.idx_ref, bf16[2,128,128]{2,1,0:T(8,128)(2,1)S(1)} %add_convert_fusion.4.refs_0_, bf16[2,128,128]{2,1,0:T(8,128)(2,1)S(1)} %get-tuple-element.92.refs_1_, bf16[2,128,128]{2,1,0:T(8,128)(2,1)S(1)} %collective-permute-done.19.refs_2_, ...), custom_call_target="tpu_custom_call" | custom-call | bytes 786436 | tf_op jit(solution)/shard_map/spread/pallas_call | solution.py:39
  (8 shorter events, 0.2 us)
Async XLA Ops:
  0.6 32.8 %copy-start.2 = (bf16[2,512,128]{2,1,0:T(8,128)(2,1)S(1)}, bf16[2,512,128]{2,1,0:T(8,128)(2,1)}, u32[]{:S(2)}) copy-start(bf16[2,512,128]{2,1,0:T(8,128)(2,1)} %refs_4_.1) | copy-start | bytes 786436
  3.7 29.7 %copy-start.1 = (bf16[1424,128]{1,0:T(8,128)(2,1)S(1)}, bf16[1424,128]{1,0:T(8,128)(2,1)}, u32[]{:S(2)}) copy-start(bf16[1424,128]{1,0:T(8,128)(2,1)} %get-tuple-element.47.refs_4_.refs_0_) | copy-start | bytes 1093636
  3.7 14.0 %collective-permute-start.1 = (bf16[1424,128]{1,0:T(8,128)(2,1)}, bf16[1424,128]{1,0:T(8,128)(2,1)S(1)}, u32[]{:S(2)}, u32[]{:S(2)}) collective-permute-start(bf16[1424,128]{1,0:T(8,128)(2,1)} %get-tuple-element.47.refs_4_.refs_0_), channel_id=1, source_target_pairs={{0,2},{1,3},{2,0},{3,1},{4,6},{5,7},{6,4},{7,5},{8,10},{9,11},{10,... | collective-permute-start | bytes 1093640 | tf_op jit(solution)/shard_map/ppermute | solution.py:227
  6.8 11.0 %collective-permute-start = (bf16[1424,128]{1,0:T(8,128)(2,1)}, bf16[1424,128]{1,0:T(8,128)(2,1)S(1)}, u32[]{:S(2)}, u32[]{:S(2)}) collective-permute-start(bf16[1424,128]{1,0:T(8,128)(2,1)} %get-tuple-element.47.refs_4_.refs_0_), channel_id=1, source_target_pairs={{0,1},{1,0},{2,3},{3,2},{4,5},{5,4},{6,7},{7,6},{8,9},{9,8},{10,11... | collective-permute-start | bytes 1093640 | tf_op jit(solution)/shard_map/ppermute | solution.py:227
  6.8 10.8 %collective-permute-start.3 = (bf16[592,128]{1,0:T(8,128)(2,1)}, bf16[592,128]{1,0:T(8,128)(2,1)S(1)}, u32[]{:S(2)}, u32[]{:S(2)}) collective-permute-start(bf16[592,128]{1,0:T(8,128)(2,1)} %get-tuple-element.55.refs_0_), channel_id=1, source_target_pairs={{0,8},{1,9},{2,10},{3,11},{4,12},{5,13},{6,14},{7,15},{8,0},{9,1},... | collective-permute-start | bytes 454664 | tf_op jit(solution)/shard_map/ppermute | solution.py:227
  9.4 8.4 %collective-permute-start.2 = (bf16[592,128]{1,0:T(8,128)(2,1)}, bf16[592,128]{1,0:T(8,128)(2,1)S(1)}, u32[]{:S(2)}, u32[]{:S(2)}) collective-permute-start(bf16[592,128]{1,0:T(8,128)(2,1)} %get-tuple-element.55.refs_0_), channel_id=1, source_target_pairs={{0,4},{1,5},{2,6},{3,7},{4,0},{5,1},{6,2},{7,3},{8,12},{9,13},{10,... | collective-permute-start | bytes 454664 | tf_op jit(solution)/shard_map/ppermute | solution.py:227
  10.9 1.6 %collective-permute-start.4 = (bf16[4,128,128]{2,1,0:T(8,128)(2,1)}, bf16[4,128,128]{2,1,0:T(8,128)(2,1)S(1)}, u32[]{:S(2)}, u32[]{:S(2)}) collective-permute-start(bf16[4,128,128]{2,1,0:T(8,128)(2,1)} %get-tuple-element.49), channel_id=1, source_target_pairs={{0,1},{1,0},{2,3},{3,2},{4,5},{5,4},{6,7},{7,6},{8,9},{9,8},{10,11... | collective-permute-start | bytes 393224 | tf_op jit(solution)/shard_map/ppermute | solution.py:227
  17.8 8.4 %collective-permute-start.6 = (bf16[592,128]{1,0:T(8,128)(2,1)S(1)}, bf16[592,128]{1,0:T(8,128)(2,1)S(1)}, u32[]{:S(2)}, u32[]{:S(2)}) collective-permute-start(bf16[592,128]{1,0:T(8,128)(2,1)S(1)} %collective-permute-done.3.refs_2_), channel_id=1, source_target_pairs={{0,4},{1,5},{2,6},{3,7},{4,0},{5,1},{6,2},{7,3},{8,12},{9,13},{10,... | collective-permute-start | bytes 454664 | tf_op jit(solution)/shard_map/ppermute | solution.py:227
  19.2 6.9 %collective-permute-start.5 = (bf16[1424,128]{1,0:T(8,128)(2,1)S(1)}, bf16[1424,128]{1,0:T(8,128)(2,1)S(1)}, u32[]{:S(2)}, u32[]{:S(2)}) collective-permute-start(bf16[1424,128]{1,0:T(8,128)(2,1)S(1)} %collective-permute-done.1.refs_6_.refs_2_), channel_id=1, source_target_pairs={{0,1},{1,0},{2,3},{3,2},{4,5},{5,4},{6,7},{7,6},{8,9},{9,8},{10,11... | collective-permute-start | bytes 1093640 | tf_op jit(solution)/shard_map/ppermute | solution.py:227
  20.2 6.0 %collective-permute-start.7 = (bf16[4,128,128]{2,1,0:T(8,128)(2,1)S(1)}, bf16[4,128,128]{2,1,0:T(8,128)(2,1)S(1)}, u32[]{:S(2)}, u32[]{:S(2)}) collective-permute-start(bf16[4,128,128]{2,1,0:T(8,128)(2,1)S(1)} %add_convert_fusion.3), channel_id=1, source_target_pairs={{0,16},{16,0},{1,17},{17,1},{2,18},{18,2},{3,19},{19,3},{4,20},{20... | collective-permute-start | bytes 393224 | tf_op jit(solution)/shard_map/ppermute | solution.py:227
  26.2 4.8 %collective-permute-start.8 = (bf16[2,128,128]{2,1,0:T(8,128)(2,1)S(1)}, bf16[2,128,128]{2,1,0:T(8,128)(2,1)S(1)}, u32[]{:S(2)}, u32[]{:S(2)}) collective-permute-start(bf16[2,128,128]{2,1,0:T(8,128)(2,1)S(1)} %slice.21), channel_id=1, source_target_pairs={{0,2},{1,3},{2,0},{3,1},{4,6},{5,7},{6,4},{7,5},{8,10},{9,11},{10,... | collective-permute-start | bytes 196616 | tf_op jit(solution)/shard_map/ppermute | solution.py:227
  26.8 1.0 %copy-start = (bf16[1424,128]{1,0:T(8,128)(2,1)S(1)}, bf16[1424,128]{1,0:T(8,128)(2,1)}, u32[]{:S(2)}) copy-start(bf16[1424,128]{1,0:T(8,128)(2,1)} %get-tuple-element.47.refs_4_.refs_0_) | copy-start | bytes 1093636
  27.8 0.9 %copy-start.3 = (bf16[592,128]{1,0:T(8,128)(2,1)S(1)}, bf16[592,128]{1,0:T(8,128)(2,1)}, u32[]{:S(2)}) copy-start(bf16[592,128]{1,0:T(8,128)(2,1)} %get-tuple-element.55.refs_0_) | copy-start | bytes 454660
  28.7 0.7 %copy-start.5 = (f32[8,128]{1,0:T(8,128)S(1)}, f32[8,128]{1,0:T(8,128)}, u32[]{:S(2)}) copy-start(f32[8,128]{1,0:T(8,128)} %get-tuple-element.62.refs_8_) | copy-start | bytes 12292
  29.4 6.2 %copy-start.4 = (bf16[592,128]{1,0:T(8,128)(2,1)S(1)}, bf16[592,128]{1,0:T(8,128)(2,1)}, u32[]{:S(2)}) copy-start(bf16[592,128]{1,0:T(8,128)(2,1)} %get-tuple-element.55.refs_0_) | copy-start | bytes 454660
  31.0 4.3 %collective-permute-start.9 = (bf16[2,128,128]{2,1,0:T(8,128)(2,1)S(1)}, bf16[2,128,128]{2,1,0:T(8,128)(2,1)S(1)}, u32[]{:S(2)}, u32[]{:S(2)}) collective-permute-start(bf16[2,128,128]{2,1,0:T(8,128)(2,1)S(1)} %add_convert_fusion.6), channel_id=1, source_target_pairs={{0,4},{1,5},{2,6},{3,7},{4,0},{5,1},{6,2},{7,3},{8,12},{9,13},{10,... | collective-permute-start | bytes 196616 | tf_op jit(solution)/shard_map/ppermute | solution.py:227
  31.6 3.7 %collective-permute-start.12 = (f32[16,128]{1,0:T(8,128)S(1)}, f32[16,128]{1,0:T(8,128)S(1)}, u32[]{:S(2)}, u32[]{:S(2)}) collective-permute-start(f32[16,128]{1,0:T(8,128)S(1)} %get-tuple-element.68.refs_8_), channel_id=1, source_target_pairs={{0,3},{1,2},{2,1},{3,0},{4,7},{5,6},{6,5},{7,4},{8,11},{9,10},{10,... | collective-permute-start | bytes 24584 | tf_op jit(solution)/shard_map/ppermute | solution.py:227
  32.0 3.7 %collective-permute-start.11 = (f32[16,128]{1,0:T(8,128)S(1)}, f32[16,128]{1,0:T(8,128)S(1)}, u32[]{:S(2)}, u32[]{:S(2)}) collective-permute-start(f32[16,128]{1,0:T(8,128)S(1)} %get-tuple-element.68.refs_8_), channel_id=1, source_target_pairs={{0,2},{1,3},{2,0},{3,1},{4,6},{5,7},{6,4},{7,5},{8,10},{9,11},{10,... | collective-permute-start | bytes 24584 | tf_op jit(solution)/shard_map/ppermute | solution.py:227
  33.2 2.4 %collective-permute-start.10 = (f32[16,128]{1,0:T(8,128)S(1)}, f32[16,128]{1,0:T(8,128)S(1)}, u32[]{:S(2)}, u32[]{:S(2)}) collective-permute-start(f32[16,128]{1,0:T(8,128)S(1)} %get-tuple-element.68.refs_8_), channel_id=1, source_target_pairs={{0,1},{1,0},{2,3},{3,2},{4,5},{5,4},{6,7},{7,6},{8,9},{9,8},{10,11... | collective-permute-start | bytes 24584 | tf_op jit(solution)/shard_map/ppermute | solution.py:227
  38.9 8.3 %collective-permute-start.13 = (bf16[4,576,128]{2,1,0:T(8,128)(2,1)S(1)}, bf16[4,576,128]{2,1,0:T(8,128)(2,1)S(1)}, u32[]{:S(2)}, u32[]{:S(2)}) collective-permute-start(bf16[4,576,128]{2,1,0:T(8,128)(2,1)S(1)} %get-tuple-element.75), channel_id=1, source_target_pairs={{0,1},{1,0},{2,3},{3,2},{4,5},{5,4},{6,7},{7,6},{8,9},{9,8},{10,11... | collective-permute-start | bytes 1769480 | tf_op jit(solution)/shard_map/ppermute | solution.py:227
  39.2 8.1 %collective-permute-start.14 = (bf16[576,128]{1,0:T(8,128)(2,1)S(1)}, bf16[576,128]{1,0:T(8,128)(2,1)S(1)}, u32[]{:S(2)}, u32[]{:S(2)}) collective-permute-start(bf16[576,128]{1,0:T(8,128)(2,1)S(1)} %get-tuple-element.76), channel_id=1, source_target_pairs={{0,4},{1,5},{2,6},{3,7},{4,0},{5,1},{6,2},{7,3},{8,12},{9,13},{10,... | collective-permute-start | bytes 442376 | tf_op jit(solution)/shard_map/ppermute | solution.py:227
  40.7 5.6 %collective-permute-start.15 = (bf16[2,128,128]{2,1,0:T(8,128)(2,1)S(1)}, bf16[2,128,128]{2,1,0:T(8,128)(2,1)S(1)}, u32[]{:S(2)}, u32[]{:S(2)}) collective-permute-start(bf16[2,128,128]{2,1,0:T(8,128)(2,1)S(1)} %add_convert_fusion.5), channel_id=1, source_target_pairs={{0,8},{1,9},{2,10},{3,11},{4,12},{5,13},{6,14},{7,15},{8,0},{9,1},... | collective-permute-start | bytes 196616 | tf_op jit(solution)/shard_map/ppermute | solution.py:227
  43.1 8.9 %collective-permute-start.18 = (bf16[576,128]{1,0:T(8,128)(2,1)S(1)}, bf16[576,128]{1,0:T(8,128)(2,1)S(1)}, u32[]{:S(2)}, u32[]{:S(2)}) collective-permute-start(bf16[576,128]{1,0:T(8,128)(2,1)S(1)} %get-tuple-element.82), channel_id=1, source_target_pairs={{0,4},{1,5},{2,6},{3,7},{4,0},{5,1},{6,2},{7,3},{8,12},{9,13},{10,... | collective-permute-start | bytes 442376 | tf_op jit(solution)/shard_map/ppermute | solution.py:227
  47.4 10.3 %collective-permute-start.16 = (bf16[2,576,128]{2,1,0:T(8,128)(2,1)S(1)}, bf16[2,576,128]{2,1,0:T(8,128)(2,1)S(1)}, u32[]{:S(2)}, u32[]{:S(2)}) collective-permute-start(bf16[2,576,128]{2,1,0:T(8,128)(2,1)S(1)} %add_convert_fusion), channel_id=1, source_target_pairs={{0,2},{1,3},{2,0},{3,1},{4,6},{5,7},{6,4},{7,5},{8,10},{9,11},{10,... | collective-permute-start | bytes 884744 | tf_op jit(solution)/shard_map/ppermute | solution.py:227
  48.6 9.1 %collective-permute-start.17 = (bf16[576,128]{1,0:T(8,128)(2,1)S(1)}, bf16[576,128]{1,0:T(8,128)(2,1)S(1)}, u32[]{:S(2)}, u32[]{:S(2)}) collective-permute-start(bf16[576,128]{1,0:T(8,128)(2,1)S(1)} %add_convert_fusion.1), channel_id=1, source_target_pairs={{0,8},{1,9},{2,10},{3,11},{4,12},{5,13},{6,14},{7,15},{8,0},{9,1},... | collective-permute-start | bytes 442376 | tf_op jit(solution)/shard_map/ppermute | solution.py:227
  51.0 5.6 %collective-permute-start.19 = (bf16[2,128,128]{2,1,0:T(8,128)(2,1)S(1)}, bf16[2,128,128]{2,1,0:T(8,128)(2,1)S(1)}, u32[]{:S(2)}, u32[]{:S(2)}) collective-permute-start(bf16[2,128,128]{2,1,0:T(8,128)(2,1)S(1)} %add_convert_fusion.4.refs_0_), channel_id=1, source_target_pairs={{0,2},{1,3},{2,0},{3,1},{4,6},{5,7},{6,4},{7,5},{8,10},{9,11},{10,... | collective-permute-start | bytes 196616 | tf_op jit(solution)/shard_map/ppermute | solution.py:227
  57.7 1.4 %collective-permute-start.20 = (bf16[4,128,128]{2,1,0:T(8,128)(2,1)S(1)}, bf16[4,128,128]{2,1,0:T(8,128)(2,1)S(1)}, u32[]{:S(2)}, u32[]{:S(2)}) collective-permute-start(bf16[4,128,128]{2,1,0:T(8,128)(2,1)S(1)} %pad_maximum_fusion), channel_id=1, source_target_pairs={{0,1},{1,0},{2,3},{3,2},{4,5},{5,4},{6,7},{7,6},{8,9},{9,8},{10,11... | collective-permute-start | bytes 393224 | tf_op jit(solution)/shard_map/ppermute | solution.py:227

commit v6 on v5

--- a/solution.py
+++ b/solution.py
@@ -95,6 +95,12 @@
         target[k // 2 * heads : (k // 2 + 1) * heads] = term[:, pl.ds(at, step), :].astype(BF16)
     for copy in copies[4:]:
         copy.wait()
+
+
+def hold_kernel(*refs):
+    half = len(refs) // 2
+    for source, target in zip(refs[:half], refs[half:]):
+        target[...] = source[...]
 
 
 def score_kernel(factor, nkey, width, heads, *refs):
@@ -269,28 +275,34 @@
     dp_hops = [(1 << bit, "dp", n_dp) for bit in range((n_dp - 1).bit_length())]
     line_hops = [(GROUP << bit,) for bit in range(line_bits)]
 
-    firsts = [swap(lat_msg, GROUP << bit) for bit in range(line_bits)]
     q_across = swap(q_msg, 2)
     q_core = swap(q_msg, 1)
-    got_pair = swap(send, 1)
-    q_core, q_across, firsts, got_pair = lax.optimization_barrier(
-        (q_core, q_across, firsts, got_pair)
-    )
-    pair = add(keep, got_pair)
-
+    pair = add(keep, swap(send, 1))
+    got_pair = swap(pair, *dp_hops[0])
+    firsts = [swap(after(lat_msg, pair) if bit + 1 < line_bits else lat_msg, GROUP << bit) for bit in range(line_bits)]
+    own = call(
+        hold_kernel,
+        "hold_own",
+        [(lat_msg.shape, BF16), (q_msg.shape, BF16), (delta.shape, F32)],
+        [lat_msg, q_msg, delta],
+    )
+    q_core, q_across, firsts, got_pair = lax.optimization_barrier((q_core, q_across, firsts, got_pair))
     held = {0: lat_msg}
     for bit in reversed(range(line_bits)):
         held.update({m | 1 << bit: swap(x, GROUP << bit) for m, x in held.items() if m})
         held[1 << bit] = firsts[bit]
-    lats = [held[m] for m in range(lines)]
-    q_far = swap(q_across, 1)
-    got_pair = swap(pair, *dp_hops[0])
-    q_far, lats, got_pair = lax.optimization_barrier((q_far, lats, got_pair))
     pair = add(pair, got_pair)
     for step_hop in dp_hops[1:]:
         pair = add(pair, swap(pair, *step_hop))
-    qs = [q_msg, q_core, q_across, q_far]
+    lats = [held[m] for m in range(lines)]
+    q_far = swap(q_across, 1)
     got_own = swap(pair[heads:], 2)
+    q_far, lats, got_own, own = lax.optimization_barrier((q_far, lats, got_own, own))
+    lat_own, q_own, delta = own
+    lats[0] = lat_own
+    qs = [q_own, q_core, q_across, q_far]
+    mine = add(pair[:heads], got_own)
+    near = swap(mine, *line_hops[0])
 
     s, k_nat, stat = call(
         functools.partial(score_kernel, factor, lines, width, heads),
@@ -301,8 +313,10 @@
         flops=2 * keys * all_rows * wide,
     )
     stats = [stat] + [swap(stat, k) for k in range(1, GROUP)]
-    mine = add(pair[:heads], after(got_own, stat))
-    near = swap(mine, *line_hops[0])
+    mine = add(mine, after(near, stat))
+    for step_hop in line_hops[1:-1]:
+        mine = add(mine, swap(mine, *step_hop))
+    near = swap(mine, *line_hops[-1])
     g, gp = call(
         functools.partial(context_kernel, width, heads),
         "context",
@@ -328,34 +342,27 @@
     )
     parts, (gq_own, gq_core, gq_across) = list(outs[:lines]), outs[lines:]
     gq_got = swap(gq_core, 1)
-    for step_hop in line_hops[1:-1]:
-        mine = add(mine, swap(mine, *step_hop))
-    far = [m for m in range(3, lines, 2)]
-    got_far = [swap(parts[m], GROUP) for m in far]
-    got_mine = swap(mine, *line_hops[-1])
-    gq_got, got_far, got_mine = lax.optimization_barrier((gq_got, got_far, got_mine))
-    mine = add(mine, got_mine)
-    for m, got in zip(far, got_far):
-        parts[m ^ 1] = add(parts[m ^ 1], got)
-    for bit in range(1, line_bits):
+    gq_sum = add(gq_across, gq_got[heads:])
+    gq_last = swap(gq_sum, 2)
+    across = swap(after(mine, gq_sum), 2)
+    for bit in range(line_bits):
         for m in range(3 << bit, lines, 2 << bit):
-            parts[m ^ 1 << bit] = add(parts[m ^ 1 << bit], swap(parts[m], GROUP << bit))
-    gq_last = swap(add(gq_across, gq_got[heads:]), 2)
+            got = swap(parts[m], GROUP << bit)
+            parts[m ^ 1 << bit] = add(parts[m ^ 1 << bit], after(got, gq_sum))
+    parts[1] = after(parts[1], parts[lines // 2])
     kept = [swap(parts[1 << bit], GROUP << bit) for bit in reversed(range(line_bits))]
-    across = swap(mine, 2)
-    gq_last, kept, across = lax.optimization_barrier((gq_last, kept, across))
-    mine_two = jnp.concatenate([mine, across], axis=0)
+    mine_two = jnp.concatenate([mine, after(across, gq_sum)], axis=0)
     other_two = swap(mine_two, 1)
+    scale = 1.0 / math.sqrt(tok * n_ctx * n_dp)
+    pieces = [mine_two[:heads], other_two[:heads], mine_two[heads:], other_two[heads:]]
+    (grad_w,) = call(
+        functools.partial(spread_kernel, scale), "spread", [((heads, lat, HEAD_DIM), F32)], [idx] + pieces, smem=(0,)
+    )
     grad_lat, grad_q = call(
         sum_kernel,
         "last_sums",
         [((width, tok), BF16), ((heads, width, tok), BF16)],
-        [gq_own, gq_got, gq_last, parts[0]] + kept,
-    )
-    scale = 1.0 / math.sqrt(tok * n_ctx * n_dp)
-    pieces = [mine_two[:heads], other_two[:heads], mine_two[heads:], other_two[heads:]]
-    (grad_w,) = call(
-        functools.partial(spread_kernel, scale), "spread", [((heads, lat, HEAD_DIM), F32)], [idx] + pieces, smem=(0,)
+        [gq_own, gq_got, gq_last, after(parts[0], grad_w)] + kept,
     )
     return (jnp.transpose(grad_q, (2, 0, 1))[None], grad_lat.T[None], grad_w)
 

time: 60.2 us -> 57.5 us (0.955)
  starting transfers between devices: 22.3 us -> 20 us
    ppermute x21, starting transfers between devices: 22.3 us -> 20 us  [swap(): return lax.ppermute(x, axis, [(i, i ^ mask) for i in range(size)])]
    unnamed x12 -> x8, local copies, waits for them, and re-layouts: 2.59 us -> 2.56 us
    pallas_call x6 -> x7, Pallas kernels: 10.9 us -> 10.9 us  [call(): pl.pallas_call(kernel, out_shape=[jax.ShapeDtypeStruct(s, d) for s, d in...]
where the time goes in v6:
time: 57.5 us; the launch traced here: 57.2 us
  waiting for transfers between devices  21.8 us (38%)
  starting transfers between devices  20 us (35%)
  Pallas kernels  10.9 us (19%)
  local copies, waits for them, and re-layouts  2.58 us (4%)
  other arithmetic  1.23 us (2%)
  between operations  0.75 us (1%)
    ppermute x21, waiting for transfers between devices, swap(): return lax.ppermute(x, axis, [(i, i ^ mask) for i in range(size)])  21.8 us
    ppermute x21, starting transfers between devices, swap(): return lax.ppermute(x, axis, [(i, i ^ mask) for i in range(size)])  20 us
    pallas_call x7, Pallas kernels, call(): pl.pallas_call(kernel, out_shape=[jax.ShapeDtypeStruct(s, d) for s, d in...  10.9 us
    unnamed x8, local copies, waits for them, and re-layouts  2.56 us
    convert_element_type x7, other arithmetic, add(): return (a.astype(F32) + b.astype(F32)).astype(BF16)  1.21 us
  transfers between devices with their start and end apart: 21, of which 11 were waited for; matrix products, arithmetic and copies ran while one was open for 2% of the time, Pallas kernels for 6%

profile of v6, /device:TPU:0, one launch (start us, length us, event | category | flops | bytes accessed | tf_op | source)
XLA Modules:
  0.0 57.2 jit_solution(15794503174564758518)
XLA Ops:
  0.6 3.0 %pack.1 = (bf16[592,128]{1,0:T(8,128)(2,1)}, bf16[1424,128]{1,0:T(8,128)(2,1)}, f32[8,128]{1,0:T(8,128)}, bf16[4,128,128]{2,1,0:T(8,128)(2,1)}, bf16[4,128,128]{2,1,0:T(8,128)(2,1)}) custom-call(s32[1]{0:T(128)} %bitcast.idx_ref, s32[1,128]{1,0:T(1,128)} %pos_hbm.1, bf16[2,576,128]{2,1,0:T(8,128)(2,1)} %bitcast.15, bf16[128,2,128]{2,1,0:T(2,128)(2,1)} %bitcast.18, ...), custom_call_target="tpu_custom_call" | custom-call | bytes 1815044 | tf_op jit(solution)/shard_map/pack/pallas_call | solution.py:39
  3.7 0.5 collective-permute-start.2
  4.2 2.6 %collective-permute-start.1 = (bf16[1424,128]{1,0:T(8,128)(2,1)}, bf16[1424,128]{1,0:T(8,128)(2,1)S(1)}, u32[]{:S(2)}, u32[]{:S(2)}) collective-permute-start(bf16[1424,128]{1,0:T(8,128)(2,1)} %get-tuple-element.51.refs_1_), channel_id=1, source_target_pairs={{0,2},{1,3},{2,0},{3,1},{4,6},{5,7},{6,4},{7,5},{8,10},{9,11},{10,... | collective-permute-start | bytes 1093640 | tf_op jit(solution)/shard_map/ppermute | solution.py:233
  6.8 0.2 collective-permute-start
  7.0 2.6 %collective-permute-start.4 = (bf16[592,128]{1,0:T(8,128)(2,1)}, bf16[592,128]{1,0:T(8,128)(2,1)S(1)}, u32[]{:S(2)}, u32[]{:S(2)}) collective-permute-start(bf16[592,128]{1,0:T(8,128)(2,1)} %get-tuple-element.55.refs_0_), channel_id=1, source_target_pairs={{0,8},{1,9},{2,10},{3,11},{4,12},{5,13},{6,14},{7,15},{8,0},{9,1},... | collective-permute-start | bytes 454664 | tf_op jit(solution)/shard_map/ppermute | solution.py:233
  9.5 0.0 collective-permute-done.2
  9.6 0.0 copy-start.1
  9.6 1.0 %add_convert_fusion.3 = bf16[4,128,128]{2,1,0:T(8,128)(2,1)S(1)} fusion(bf16[4,128,128]{2,1,0:T(8,128)(2,1)S(1)} %collective-permute-done.2, bf16[4,128,128]{2,1,0:T(8,128)(2,1)} %get-tuple-element.53), kind=kLoop, calls=%fused_computation.3 | loop fusion | flops 262144 | bytes 393216 | tf_op jit(solution)/shard_map/convert_element_type | solution.py:273
  10.5 1.6 %collective-permute-start.3 = (bf16[592,128]{1,0:T(8,128)(2,1)}, bf16[592,128]{1,0:T(8,128)(2,1)S(1)}, u32[]{:S(2)}, u32[]{:S(2)}) collective-permute-start(bf16[592,128]{1,0:T(8,128)(2,1)} %get-tuple-element.55.refs_0_), channel_id=1, source_target_pairs={{0,4},{1,5},{2,6},{3,7},{4,0},{5,1},{6,2},{7,3},{8,12},{9,13},{10,... | collective-permute-start | bytes 454664 | tf_op jit(solution)/shard_map/ppermute | solution.py:233
  12.2 1.5 %collective-permute-start.5 = (bf16[4,128,128]{2,1,0:T(8,128)(2,1)S(1)}, bf16[4,128,128]{2,1,0:T(8,128)(2,1)S(1)}, u32[]{:S(2)}, u32[]{:S(2)}) collective-permute-start(bf16[4,128,128]{2,1,0:T(8,128)(2,1)S(1)} %add_convert_fusion.3), channel_id=1, source_target_pairs={{0,16},{16,0},{1,17},{17,1},{2,18},{18,2},{3,19},{19,3},{4,20},{20... | collective-permute-start | bytes 393224 | tf_op jit(solution)/shard_map/ppermute | solution.py:233
  13.7 3.9 %collective-permute-done.4.refs_2_ = bf16[592,128]{1,0:T(8,128)(2,1)S(1)} collective-permute-done((bf16[592,128]{1,0:T(8,128)(2,1)}, bf16[592,128]{1,0:T(8,128)(2,1)S(1)}, u32[]{:S(2)}, u32[]{:S(2)}) %collective-permute-start.4) | collective-permute-done | bytes 151584 | tf_op jit(solution)/shard_map/ppermute | solution.py:233
  17.6 0.0 collective-permute-done.5
  17.6 1.2 %collective-permute-done.3.refs_1_ = bf16[592,128]{1,0:T(8,128)(2,1)S(1)} collective-permute-done((bf16[592,128]{1,0:T(8,128)(2,1)}, bf16[592,128]{1,0:T(8,128)(2,1)S(1)}, u32[]{:S(2)}, u32[]{:S(2)}) %collective-permute-start.3) | collective-permute-done | bytes 151584 | tf_op jit(solution)/shard_map/ppermute | solution.py:233
  18.9 0.0 collective-permute-done.1.refs_6_.refs_2_
  18.9 0.0 collective-permute-done.refs_5_.refs_1_
  18.9 0.0 collective-permute-start.6
  18.9 0.4 collective-permute-start.7
  19.4 0.6 collective-permute-start.8
  19.9 0.0 copy-start
  19.9 1.0 %copy-done = bf16[1424,128]{1,0:T(8,128)(2,1)S(1)} copy-done((bf16[1424,128]{1,0:T(8,128)(2,1)S(1)}, bf16[1424,128]{1,0:T(8,128)(2,1)}, u32[]{:S(2)}) %copy-start) | copy-done | bytes 364568
  20.9 0.0 copy-start.2
  20.9 0.9 %copy-done.2 = bf16[592,128]{1,0:T(8,128)(2,1)S(1)} copy-done((bf16[592,128]{1,0:T(8,128)(2,1)S(1)}, bf16[592,128]{1,0:T(8,128)(2,1)}, u32[]{:S(2)}) %copy-start.2) | copy-done | bytes 151576
  21.8 0.0 copy-start.3
  21.8 0.7 %copy-done.3 = f32[8,128]{1,0:T(8,128)S(1)} copy-done((f32[8,128]{1,0:T(8,128)S(1)}, f32[8,128]{1,0:T(8,128)}, u32[]{:S(2)}) %copy-start.3) | copy-done | bytes 4120
  22.5 1.2 %collective-permute-done.8 = bf16[2,128,128]{2,1,0:T(8,128)(2,1)S(1)} collective-permute-done((bf16[2,128,128]{2,1,0:T(8,128)(2,1)S(1)}, bf16[2,128,128]{2,1,0:T(8,128)(2,1)S(1)}, u32[]{:S(2)}, u32[]{:S(2)}) %collective-permute-start.8) | collective-permute-done | bytes 65568 | tf_op jit(solution)/shard_map/ppermute | solution.py:233
  23.7 1.5 %collective-permute-done.7.refs_3_ = bf16[592,128]{1,0:T(8,128)(2,1)S(1)} collective-permute-done((bf16[592,128]{1,0:T(8,128)(2,1)S(1)}, bf16[592,128]{1,0:T(8,128)(2,1)S(1)}, u32[]{:S(2)}, u32[]{:S(2)}) %collective-permute-start.7) | collective-permute-done | bytes 151584 | tf_op jit(solution)/shard_map/ppermute | solution.py:233
  25.2 0.0 collective-permute-done.6.refs_7_.refs_3_
  25.2 0.4 collective-permute-start.9
  25.7 1.6 %scores.1 = (f32[512,1024]{1,0:T(8,128)S(1)}, bf16[512,640]{1,0:T(8,128)(2,1)S(1)}, f32[16,128]{1,0:T(8,128)S(1)}) custom-call(bf16[592,128]{1,0:T(8,128)(2,1)S(1)} %get-tuple-element.64.refs_0_, bf16[592,128]{1,0:T(8,128)(2,1)S(1)} %collective-permute-done.3.refs_1_, bf16[592,128]{1,0:T(8,128)(2,1)S(1)} %collective-permute-done.4.refs_2_, ...), custom_call_target="tpu_custom_call" | custom-call | flops 671088640 | bytes 4829184 | tf_op jit(solution)/shard_map/scores/pallas_call | solution.py:39
  27.3 2.3 %collective-permute-done.9 = bf16[2,128,128]{2,1,0:T(8,128)(2,1)S(1)} collective-permute-done((bf16[2,128,128]{2,1,0:T(8,128)(2,1)S(1)}, bf16[2,128,128]{2,1,0:T(8,128)(2,1)S(1)}, u32[]{:S(2)}, u32[]{:S(2)}) %collective-permute-start.9) | collective-permute-done | bytes 65568 | tf_op jit(solution)/shard_map/ppermute | solution.py:233
  29.6 1.3 %collective-permute-start.10 = (bf16[2,128,128]{2,1,0:T(8,128)(2,1)S(1)}, bf16[2,128,128]{2,1,0:T(8,128)(2,1)S(1)}, u32[]{:S(2)}, u32[]{:S(2)}) collective-permute-start(bf16[2,128,128]{2,1,0:T(8,128)(2,1)S(1)} %add_convert_fusion.5), channel_id=1, source_target_pairs={{0,8},{1,9},{2,10},{3,11},{4,12},{5,13},{6,14},{7,15},{8,0},{9,1},... | collective-permute-start | bytes 196616 | tf_op jit(solution)/shard_map/ppermute | solution.py:233
  30.9 0.0 collective-permute-start.13
  30.9 1.0 %collective-permute-start.12 = (f32[16,128]{1,0:T(8,128)S(1)}, f32[16,128]{1,0:T(8,128)S(1)}, u32[]{:S(2)}, u32[]{:S(2)}) collective-permute-start(f32[16,128]{1,0:T(8,128)S(1)} %get-tuple-element.78.refs_8_), channel_id=1, source_target_pairs={{0,2},{1,3},{2,0},{3,1},{4,6},{5,7},{6,4},{7,5},{8,10},{9,11},{10,... | collective-permute-start | bytes 24584 | tf_op jit(solution)/shard_map/ppermute | solution.py:233
  32.0 0.8 %collective-permute-start.11 = (f32[16,128]{1,0:T(8,128)S(1)}, f32[16,128]{1,0:T(8,128)S(1)}, u32[]{:S(2)}, u32[]{:S(2)}) collective-permute-start(f32[16,128]{1,0:T(8,128)S(1)} %get-tuple-element.78.refs_8_), channel_id=1, source_target_pairs={{0,1},{1,0},{2,3},{3,2},{4,5},{5,4},{6,7},{7,6},{8,9},{9,8},{10,11... | collective-permute-start | bytes 24584 | tf_op jit(solution)/shard_map/ppermute | solution.py:233
  32.8 0.0 copy-done.1
  32.8 1.2 %context.1 = (bf16[512,1024]{1,0:T(8,128)(2,1)S(1)}, f32[512,1024]{1,0:T(8,128)S(1)}) custom-call(bf16[1424,128]{1,0:T(8,128)(2,1)S(1)} %get-tuple-element.68.refs_4_.refs_0_, bf16[1424,128]{1,0:T(8,128)(2,1)S(1)} %collective-permute-done.refs_5_.refs_1_, bf16[1424,128]{1,0:T(8,128)(2,1)S(1)} %collective-permute-done.1.refs_6_.refs_2_, ...), custom_call_target="tpu_custom_call" | custom-call | flops 671088640 | bytes 5521408 | tf_op jit(solution)/shard_map/context/pallas_call | solution.py:39
  34.0 1.3 %collective-permute-done.10 = bf16[2,128,128]{2,1,0:T(8,128)(2,1)S(1)} collective-permute-done((bf16[2,128,128]{2,1,0:T(8,128)(2,1)S(1)}, bf16[2,128,128]{2,1,0:T(8,128)(2,1)S(1)}, u32[]{:S(2)}, u32[]{:S(2)}) %collective-permute-start.10) | collective-permute-done | bytes 65568 | tf_op jit(solution)/shard_map/ppermute | solution.py:233
  35.3 0.0 collective-permute-done.13.refs_11_
  35.4 0.0 collective-permute-done.12.refs_10_
  35.4 0.0 collective-permute-done.11.refs_9_
  35.4 3.3 %gradients.1 = (bf16[576,128]{1,0:T(8,128)(2,1)S(1)}, bf16[576,128]{1,0:T(8,128)(2,1)S(1)}, bf16[576,128]{1,0:T(8,128)(2,1)S(1)}, bf16[576,128]{1,0:T(8,128)(2,1...) custom-call(bf16[592,128]{1,0:T(8,128)(2,1)S(1)} %get-tuple-element.64.r, ...), custom_call_target="tpu_custom_call" | custom-call | flops 1744830464 | bytes 9109504 | tf_op jit(solution)/shard_map/gradients/pallas_call | solution.py:39
  38.7 0.1 collective-permute-start.14
  38.8 1.1 %collective-permute-start.18 = (bf16[576,128]{1,0:T(8,128)(2,1)S(1)}, bf16[576,128]{1,0:T(8,128)(2,1)S(1)}, u32[]{:S(2)}, u32[]{:S(2)}) collective-permute-start(bf16[576,128]{1,0:T(8,128)(2,1)S(1)} %get-tuple-element.93), channel_id=1, source_target_pairs={{0,4},{1,5},{2,6},{3,7},{4,0},{5,1},{6,2},{7,3},{8,12},{9,13},{10,... | collective-permute-start | bytes 442376 | tf_op jit(solution)/shard_map/ppermute | solution.py:233
  39.9 0.9 %collective-permute-done.14.gq_got_ref = bf16[4,576,128]{2,1,0:T(8,128)(2,1)S(1)} collective-permute-done((bf16[4,576,128]{2,1,0:T(8,128)(2,1)S(1)}, bf16[4,576,128]{2,1,0:T(8,128)(2,1)S(1)}, u32[]{:S(2)}, u32[]{:S(2)}) %collective-permute-start.14) | collective-permute-done | bytes 589856 | tf_op jit(solution)/shard_map/ppermute | solution.py:233
  40.8 0.1 add_convert_fusion
  40.8 0.7 %collective-permute-start.16 = (bf16[2,128,128]{2,1,0:T(8,128)(2,1)S(1)}, bf16[2,128,128]{2,1,0:T(8,128)(2,1)S(1)}, u32[]{:S(2)}, u32[]{:S(2)}) collective-permute-start(bf16[2,128,128]{2,1,0:T(8,128)(2,1)S(1)} %add_convert_fusion.4.refs_0_), channel_id=1, source_target_pairs={{0,2},{1,3},{2,0},{3,1},{4,6},{5,7},{6,4},{7,5},{8,10},{9,11},{10,... | collective-permute-start | bytes 196616 | tf_op jit(solution)/shard_map/ppermute | solution.py:233
  41.5 1.4 %collective-permute-start.15 = (bf16[2,576,128]{2,1,0:T(8,128)(2,1)S(1)}, bf16[2,576,128]{2,1,0:T(8,128)(2,1)S(1)}, u32[]{:S(2)}, u32[]{:S(2)}) collective-permute-start(bf16[2,576,128]{2,1,0:T(8,128)(2,1)S(1)} %add_convert_fusion), channel_id=1, source_target_pairs={{0,2},{1,3},{2,0},{3,1},{4,6},{5,7},{6,4},{7,5},{8,10},{9,11},{10,... | collective-permute-start | bytes 884744 | tf_op jit(solution)/shard_map/ppermute | solution.py:233
  42.9 2.1 %collective-permute-done.18 = bf16[576,128]{1,0:T(8,128)(2,1)S(1)} collective-permute-done((bf16[576,128]{1,0:T(8,128)(2,1)S(1)}, bf16[576,128]{1,0:T(8,128)(2,1)S(1)}, u32[]{:S(2)}, u32[]{:S(2)}) %collective-permute-start.18) | collective-permute-done | bytes 147488 | tf_op jit(solution)/shard_map/ppermute | solution.py:233
  45.0 0.8 %collective-permute-done.16.refs_2_ = bf16[2,128,128]{2,1,0:T(8,128)(2,1)S(1)} collective-permute-done((bf16[2,128,128]{2,1,0:T(8,128)(2,1)S(1)}, bf16[2,128,128]{2,1,0:T(8,128)(2,1)S(1)}, u32[]{:S(2)}, u32[]{:S(2)}) %collective-permute-start.16) | collective-permute-done | bytes 65568 | tf_op jit(solution)/shard_map/ppermute | solution.py:233
  45.9 0.1 collective-permute-start.17
  46.0 1.1 %collective-permute-start.19 = (bf16[576,128]{1,0:T(8,128)(2,1)S(1)}, bf16[576,128]{1,0:T(8,128)(2,1)S(1)}, u32[]{:S(2)}, u32[]{:S(2)}) collective-permute-start(bf16[576,128]{1,0:T(8,128)(2,1)S(1)} %add_convert_fusion.1), channel_id=1, source_target_pairs={{0,8},{1,9},{2,10},{3,11},{4,12},{5,13},{6,14},{7,15},{8,0},{9,1},... | collective-permute-start | bytes 442376 | tf_op jit(solution)/shard_map/ppermute | solution.py:233
  47.1 1.9 %collective-permute-start.20 = (bf16[576,128]{1,0:T(8,128)(2,1)S(1)}, bf16[576,128]{1,0:T(8,128)(2,1)S(1)}, u32[]{:S(2)}, u32[]{:S(2)}) collective-permute-start(bf16[576,128]{1,0:T(8,128)(2,1)S(1)} %get-tuple-element.96), channel_id=1, source_target_pairs={{0,4},{1,5},{2,6},{3,7},{4,0},{5,1},{6,2},{7,3},{8,12},{9,13},{10,... | collective-permute-start | bytes 442376 | tf_op jit(solution)/shard_map/ppermute | solution.py:233
  49.0 0.0 collective-permute-done.17
  49.0 0.8 %spread.1 = f32[2,512,128]{2,1,0:T(8,128)} custom-call(s32[1]{0:T(128)} %bitcast.idx_ref, bf16[2,128,128]{2,1,0:T(8,128)(2,1)S(1)} %add_convert_fusion.4.refs_0_, bf16[2,128,128]{2,1,0:T(8,128)(2,1)S(1)} %get-tuple-element.100.refs_1_, bf16[2,128,128]{2,1,0:T(8,128)(2,1)S(1)} %collective-permute-done.16.refs_2_, ...), custom_call_target="tpu_custom_call" | custom-call | bytes 786436 | tf_op jit(solution)/shard_map/spread/pallas_call | solution.py:39
  49.9 4.3 %collective-permute-done.20.refs_2_ = bf16[576,128]{1,0:T(8,128)(2,1)S(1)} collective-permute-done((bf16[576,128]{1,0:T(8,128)(2,1)S(1)}, bf16[576,128]{1,0:T(8,128)(2,1)S(1)}, u32[]{:S(2)}, u32[]{:S(2)}) %collective-permute-start.20) | collective-permute-done | bytes 147488 | tf_op jit(solution)/shard_map/ppermute | solution.py:233
  54.1 2.2 %collective-permute-done.19.refs_1_ = bf16[576,128]{1,0:T(8,128)(2,1)S(1)} collective-permute-done((bf16[576,128]{1,0:T(8,128)(2,1)S(1)}, bf16[576,128]{1,0:T(8,128)(2,1)S(1)}, u32[]{:S(2)}, u32[]{:S(2)}) %collective-permute-start.19) | collective-permute-done | bytes 147488 | tf_op jit(solution)/shard_map/ppermute | solution.py:233
  56.4 0.0 collective-permute-done.15.gq_last_ref
  56.4 0.9 %last_sums.1 = (bf16[576,128]{1,0:T(8,128)(2,1)}, bf16[2,576,128]{2,1,0:T(8,128)(2,1)}) custom-call(bf16[2,576,128]{2,1,0:T(8,128)(2,1)S(1)} %get-tuple-element.84.gq_own_ref, bf16[4,576,128]{2,1,0:T(8,128)(2,1)S(1)} %collective-permute-done.14.gq_got_ref, bf16[2,576,128]{2,1,0:T(8,128)(2,1)S(1)} %collective-permute-done.15.gq_last_ref, ...), custom_call_target="tpu_custom_call" | custom-call | bytes 2064384 | tf_op jit(solution)/shard_map/last_sums/pallas_call | solution.py:39
  (9 shorter events, 0.2 us)
Async XLA Ops:
  3.7 5.9 %collective-permute-start.2 = (bf16[4,128,128]{2,1,0:T(8,128)(2,1)}, bf16[4,128,128]{2,1,0:T(8,128)(2,1)S(1)}, u32[]{:S(2)}, u32[]{:S(2)}) collective-permute-start(bf16[4,128,128]{2,1,0:T(8,128)(2,1)} %get-tuple-element.54), channel_id=1, source_target_pairs={{0,1},{1,0},{2,3},{3,2},{4,5},{5,4},{6,7},{7,6},{8,9},{9,8},{10,11... | collective-permute-start | bytes 393224 | tf_op jit(solution)/shard_map/ppermute | solution.py:233
  4.2 14.7 %collective-permute-start.1 = (bf16[1424,128]{1,0:T(8,128)(2,1)}, bf16[1424,128]{1,0:T(8,128)(2,1)S(1)}, u32[]{:S(2)}, u32[]{:S(2)}) collective-permute-start(bf16[1424,128]{1,0:T(8,128)(2,1)} %get-tuple-element.51.refs_1_), channel_id=1, source_target_pairs={{0,2},{1,3},{2,0},{3,1},{4,6},{5,7},{6,4},{7,5},{8,10},{9,11},{10,... | collective-permute-start | bytes 1093640 | tf_op jit(solution)/shard_map/ppermute | solution.py:233
  6.8 12.1 %collective-permute-start = (bf16[1424,128]{1,0:T(8,128)(2,1)}, bf16[1424,128]{1,0:T(8,128)(2,1)S(1)}, u32[]{:S(2)}, u32[]{:S(2)}) collective-permute-start(bf16[1424,128]{1,0:T(8,128)(2,1)} %get-tuple-element.51.refs_1_), channel_id=1, source_target_pairs={{0,1},{1,0},{2,3},{3,2},{4,5},{5,4},{6,7},{7,6},{8,9},{9,8},{10,11... | collective-permute-start | bytes 1093640 | tf_op jit(solution)/shard_map/ppermute | solution.py:233
  7.0 10.6 %collective-permute-start.4 = (bf16[592,128]{1,0:T(8,128)(2,1)}, bf16[592,128]{1,0:T(8,128)(2,1)S(1)}, u32[]{:S(2)}, u32[]{:S(2)}) collective-permute-start(bf16[592,128]{1,0:T(8,128)(2,1)} %get-tuple-element.55.refs_0_), channel_id=1, source_target_pairs={{0,8},{1,9},{2,10},{3,11},{4,12},{5,13},{6,14},{7,15},{8,0},{9,1},... | collective-permute-start | bytes 454664 | tf_op jit(solution)/shard_map/ppermute | solution.py:233
  9.6 23.3 %copy-start.1 = (bf16[2,512,128]{2,1,0:T(8,128)(2,1)S(1)}, bf16[2,512,128]{2,1,0:T(8,128)(2,1)}, u32[]{:S(2)}) copy-start(bf16[2,512,128]{2,1,0:T(8,128)(2,1)} %refs_4_.1) | copy-start | bytes 786436
  10.5 8.3 %collective-permute-start.3 = (bf16[592,128]{1,0:T(8,128)(2,1)}, bf16[592,128]{1,0:T(8,128)(2,1)S(1)}, u32[]{:S(2)}, u32[]{:S(2)}) collective-permute-start(bf16[592,128]{1,0:T(8,128)(2,1)} %get-tuple-element.55.refs_0_), channel_id=1, source_target_pairs={{0,4},{1,5},{2,6},{3,7},{4,0},{5,1},{6,2},{7,3},{8,12},{9,13},{10,... | collective-permute-start | bytes 454664 | tf_op jit(solution)/shard_map/ppermute | solution.py:233
  12.2 5.4 %collective-permute-start.5 = (bf16[4,128,128]{2,1,0:T(8,128)(2,1)S(1)}, bf16[4,128,128]{2,1,0:T(8,128)(2,1)S(1)}, u32[]{:S(2)}, u32[]{:S(2)}) collective-permute-start(bf16[4,128,128]{2,1,0:T(8,128)(2,1)S(1)} %add_convert_fusion.3), channel_id=1, source_target_pairs={{0,16},{16,0},{1,17},{17,1},{2,18},{18,2},{3,19},{19,3},{4,20},{20... | collective-permute-start | bytes 393224 | tf_op jit(solution)/shard_map/ppermute | solution.py:233
  18.9 6.4 %collective-permute-start.6 = (bf16[1424,128]{1,0:T(8,128)(2,1)S(1)}, bf16[1424,128]{1,0:T(8,128)(2,1)S(1)}, u32[]{:S(2)}, u32[]{:S(2)}) collective-permute-start(bf16[1424,128]{1,0:T(8,128)(2,1)S(1)} %collective-permute-done.1.refs_6_.refs_2_), channel_id=1, source_target_pairs={{0,1},{1,0},{2,3},{3,2},{4,5},{5,4},{6,7},{7,6},{8,9},{9,8},{10,11... | collective-permute-start | bytes 1093640 | tf_op jit(solution)/shard_map/ppermute | solution.py:233
  18.9 6.3 %collective-permute-start.7 = (bf16[592,128]{1,0:T(8,128)(2,1)S(1)}, bf16[592,128]{1,0:T(8,128)(2,1)S(1)}, u32[]{:S(2)}, u32[]{:S(2)}) collective-permute-start(bf16[592,128]{1,0:T(8,128)(2,1)S(1)} %collective-permute-done.4.refs_2_), channel_id=1, source_target_pairs={{0,4},{1,5},{2,6},{3,7},{4,0},{5,1},{6,2},{7,3},{8,12},{9,13},{10,... | collective-permute-start | bytes 454664 | tf_op jit(solution)/shard_map/ppermute | solution.py:233
  19.4 4.3 %collective-permute-start.8 = (bf16[2,128,128]{2,1,0:T(8,128)(2,1)S(1)}, bf16[2,128,128]{2,1,0:T(8,128)(2,1)S(1)}, u32[]{:S(2)}, u32[]{:S(2)}) collective-permute-start(bf16[2,128,128]{2,1,0:T(8,128)(2,1)S(1)} %slice.20), channel_id=1, source_target_pairs={{0,2},{1,3},{2,0},{3,1},{4,6},{5,7},{6,4},{7,5},{8,10},{9,11},{10,... | collective-permute-start | bytes 196616 | tf_op jit(solution)/shard_map/ppermute | solution.py:233
  19.9 1.0 %copy-start = (bf16[1424,128]{1,0:T(8,128)(2,1)S(1)}, bf16[1424,128]{1,0:T(8,128)(2,1)}, u32[]{:S(2)}) copy-start(bf16[1424,128]{1,0:T(8,128)(2,1)} %get-tuple-element.51.refs_1_) | copy-start | bytes 1093636
  20.9 0.9 %copy-start.2 = (bf16[592,128]{1,0:T(8,128)(2,1)S(1)}, bf16[592,128]{1,0:T(8,128)(2,1)}, u32[]{:S(2)}) copy-start(bf16[592,128]{1,0:T(8,128)(2,1)} %get-tuple-element.55.refs_0_) | copy-start | bytes 454660
  21.8 0.7 %copy-start.3 = (f32[8,128]{1,0:T(8,128)S(1)}, f32[8,128]{1,0:T(8,128)}, u32[]{:S(2)}) copy-start(f32[8,128]{1,0:T(8,128)} %get-tuple-element.60.refs_2_) | copy-start | bytes 12292
  25.2 4.3 %collective-permute-start.9 = (bf16[2,128,128]{2,1,0:T(8,128)(2,1)S(1)}, bf16[2,128,128]{2,1,0:T(8,128)(2,1)S(1)}, u32[]{:S(2)}, u32[]{:S(2)}) collective-permute-start(bf16[2,128,128]{2,1,0:T(8,128)(2,1)S(1)} %add_convert_fusion.6), channel_id=1, source_target_pairs={{0,4},{1,5},{2,6},{3,7},{4,0},{5,1},{6,2},{7,3},{8,12},{9,13},{10,... | collective-permute-start | bytes 196616 | tf_op jit(solution)/shard_map/ppermute | solution.py:233
  29.6 5.7 %collective-permute-start.10 = (bf16[2,128,128]{2,1,0:T(8,128)(2,1)S(1)}, bf16[2,128,128]{2,1,0:T(8,128)(2,1)S(1)}, u32[]{:S(2)}, u32[]{:S(2)}) collective-permute-start(bf16[2,128,128]{2,1,0:T(8,128)(2,1)S(1)} %add_convert_fusion.5), channel_id=1, source_target_pairs={{0,8},{1,9},{2,10},{3,11},{4,12},{5,13},{6,14},{7,15},{8,0},{9,1},... | collective-permute-start | bytes 196616 | tf_op jit(solution)/shard_map/ppermute | solution.py:233
  30.9 4.4 %collective-permute-start.13 = (f32[16,128]{1,0:T(8,128)S(1)}, f32[16,128]{1,0:T(8,128)S(1)}, u32[]{:S(2)}, u32[]{:S(2)}) collective-permute-start(f32[16,128]{1,0:T(8,128)S(1)} %get-tuple-element.78.refs_8_), channel_id=1, source_target_pairs={{0,3},{1,2},{2,1},{3,0},{4,7},{5,6},{6,5},{7,4},{8,11},{9,10},{10,... | collective-permute-start | bytes 24584 | tf_op jit(solution)/shard_map/ppermute | solution.py:233
  30.9 4.4 %collective-permute-start.12 = (f32[16,128]{1,0:T(8,128)S(1)}, f32[16,128]{1,0:T(8,128)S(1)}, u32[]{:S(2)}, u32[]{:S(2)}) collective-permute-start(f32[16,128]{1,0:T(8,128)S(1)} %get-tuple-element.78.refs_8_), channel_id=1, source_target_pairs={{0,2},{1,3},{2,0},{3,1},{4,6},{5,7},{6,4},{7,5},{8,10},{9,11},{10,... | collective-permute-start | bytes 24584 | tf_op jit(solution)/shard_map/ppermute | solution.py:233
  32.0 3.4 %collective-permute-start.11 = (f32[16,128]{1,0:T(8,128)S(1)}, f32[16,128]{1,0:T(8,128)S(1)}, u32[]{:S(2)}, u32[]{:S(2)}) collective-permute-start(f32[16,128]{1,0:T(8,128)S(1)} %get-tuple-element.78.refs_8_), channel_id=1, source_target_pairs={{0,1},{1,0},{2,3},{3,2},{4,5},{5,4},{6,7},{7,6},{8,9},{9,8},{10,11... | collective-permute-start | bytes 24584 | tf_op jit(solution)/shard_map/ppermute | solution.py:233
  38.7 2.1 %collective-permute-start.14 = (bf16[4,576,128]{2,1,0:T(8,128)(2,1)S(1)}, bf16[4,576,128]{2,1,0:T(8,128)(2,1)S(1)}, u32[]{:S(2)}, u32[]{:S(2)}) collective-permute-start(bf16[4,576,128]{2,1,0:T(8,128)(2,1)S(1)} %get-tuple-element.85), channel_id=1, source_target_pairs={{0,1},{1,0},{2,3},{3,2},{4,5},{5,4},{6,7},{7,6},{8,9},{9,8},{10,11... | collective-permute-start | bytes 1769480 | tf_op jit(solution)/shard_map/ppermute | solution.py:233
  38.8 6.3 %collective-permute-start.18 = (bf16[576,128]{1,0:T(8,128)(2,1)S(1)}, bf16[576,128]{1,0:T(8,128)(2,1)S(1)}, u32[]{:S(2)}, u32[]{:S(2)}) collective-permute-start(bf16[576,128]{1,0:T(8,128)(2,1)S(1)} %get-tuple-element.93), channel_id=1, source_target_pairs={{0,4},{1,5},{2,6},{3,7},{4,0},{5,1},{6,2},{7,3},{8,12},{9,13},{10,... | collective-permute-start | bytes 442376 | tf_op jit(solution)/shard_map/ppermute | solution.py:233
  40.8 5.0 %collective-permute-start.16 = (bf16[2,128,128]{2,1,0:T(8,128)(2,1)S(1)}, bf16[2,128,128]{2,1,0:T(8,128)(2,1)S(1)}, u32[]{:S(2)}, u32[]{:S(2)}) collective-permute-start(bf16[2,128,128]{2,1,0:T(8,128)(2,1)S(1)} %add_convert_fusion.4.refs_0_), channel_id=1, source_target_pairs={{0,2},{1,3},{2,0},{3,1},{4,6},{5,7},{6,4},{7,5},{8,10},{9,11},{10,... | collective-permute-start | bytes 196616 | tf_op jit(solution)/shard_map/ppermute | solution.py:233
  41.5 14.8 %collective-permute-start.15 = (bf16[2,576,128]{2,1,0:T(8,128)(2,1)S(1)}, bf16[2,576,128]{2,1,0:T(8,128)(2,1)S(1)}, u32[]{:S(2)}, u32[]{:S(2)}) collective-permute-start(bf16[2,576,128]{2,1,0:T(8,128)(2,1)S(1)} %add_convert_fusion), channel_id=1, source_target_pairs={{0,2},{1,3},{2,0},{3,1},{4,6},{5,7},{6,4},{7,5},{8,10},{9,11},{10,... | collective-permute-start | bytes 884744 | tf_op jit(solution)/shard_map/ppermute | solution.py:233
  45.9 3.1 %collective-permute-start.17 = (bf16[4,128,128]{2,1,0:T(8,128)(2,1)S(1)}, bf16[4,128,128]{2,1,0:T(8,128)(2,1)S(1)}, u32[]{:S(2)}, u32[]{:S(2)}) collective-permute-start(bf16[4,128,128]{2,1,0:T(8,128)(2,1)S(1)} %pad_maximum_fusion), channel_id=1, source_target_pairs={{0,1},{1,0},{2,3},{3,2},{4,5},{5,4},{6,7},{7,6},{8,9},{9,8},{10,11... | collective-permute-start | bytes 393224 | tf_op jit(solution)/shard_map/ppermute | solution.py:233
  46.0 10.4 %collective-permute-start.19 = (bf16[576,128]{1,0:T(8,128)(2,1)S(1)}, bf16[576,128]{1,0:T(8,128)(2,1)S(1)}, u32[]{:S(2)}, u32[]{:S(2)}) collective-permute-start(bf16[576,128]{1,0:T(8,128)(2,1)S(1)} %add_convert_fusion.1), channel_id=1, source_target_pairs={{0,8},{1,9},{2,10},{3,11},{4,12},{5,13},{6,14},{7,15},{8,0},{9,1},... | collective-permute-start | bytes 442376 | tf_op jit(solution)/shard_map/ppermute | solution.py:233
  47.1 7.0 %collective-permute-start.20 = (bf16[576,128]{1,0:T(8,128)(2,1)S(1)}, bf16[576,128]{1,0:T(8,128)(2,1)S(1)}, u32[]{:S(2)}, u32[]{:S(2)}) collective-permute-start(bf16[576,128]{1,0:T(8,128)(2,1)S(1)} %get-tuple-element.96), channel_id=1, source_target_pairs={{0,4},{1,5},{2,6},{3,7},{4,0},{5,1},{6,2},{7,3},{8,12},{9,13},{10,... | collective-permute-start | bytes 442376 | tf_op jit(solution)/shard_map/ppermute | solution.py:233

commit v7 on v6

--- a/solution.py
+++ b/solution.py
@@ -29,7 +29,7 @@
     return math.prod(shape) * jnp.dtype(dtype).itemsize
 
 
-def call(kernel, name, outs, args, scratch=(), flops=0, smem=(), hbm=(), copies=0, limit=None):
+def call(kernel, name, outs, args, scratch=(), flops=0, smem=(), hbm=(), copies=0, limit=None, share=1):
     def place(i):
         return pltpu.SMEM if i in smem else pltpu.HBM if i in hbm else pltpu.VMEM
 
@@ -43,7 +43,7 @@
         out_specs=[pl.BlockSpec(memory_space=pltpu.VMEM) for _ in outs],
         scratch_shapes=[pltpu.VMEM(s, d) for s, d in scratch] + semaphores,
         compiler_params=pltpu.CompilerParams(vmem_limit_bytes=limit or int(1.2 * held) + (8 << 20)),
-        cost_estimate=pl.CostEstimate(flops=flops, bytes_accessed=moved, transcendentals=0),
+        cost_estimate=pl.CostEstimate(flops=flops * share, bytes_accessed=moved * share, transcendentals=0),
         name=name,
     )(*args)
 
@@ -103,44 +103,57 @@
         target[...] = source[...]
 
 
-def score_kernel(factor, nkey, width, heads, *refs):
-    lat_refs = refs[:nkey]
-    q_refs = refs[nkey : nkey + GROUP]
-    delta_ref, s_ref, k_ref, stat_ref, kt, qt = refs[nkey + GROUP :]
-    wide = kt.shape[0]
+def score_kernel(factor, nkey, width, heads, last, *refs):
+    lat_refs, refs = refs[:nkey], refs[nkey:]
     tok = lat_refs[0].shape[1]
     rows = heads * tok
+    if last:
+        q_all_ref, near_ref, delta_ref, s_ref, k_ref, stat_ref, kt = refs
+    else:
+        q_refs, refs = refs[:GROUP], refs[GROUP:]
+        s_ref, k_ref, stat_ref, q_all_ref, kt = refs
+        for j in range(GROUP):
+            for h in range(heads):
+                cols = slice(j * rows + h * tok, j * rows + (h + 1) * tok)
+                q_all_ref[:width, cols] = q_refs[j][h * width : (h + 1) * width, :]
+                q_all_ref[width : width + EXTRA, cols] = q_refs[j][q_refs[j].shape[0] - EXTRA :, :]
+        spare = q_all_ref.shape[0] - width - EXTRA
+        q_all_ref[width + EXTRA :, :] = jnp.zeros((spare, GROUP * rows), BF16)
+    wide = kt.shape[0]
     for a in range(nkey):
         kt[: width + EXTRA, a * tok : (a + 1) * tok] = lat_refs[a][...]
     kt[width + EXTRA :, :] = jnp.zeros((wide - width - EXTRA, nkey * tok), BF16)
-    k_ref[...] = kt[...].T
-    pos = k_ref[:, wide - 128 :].astype(F32)
+    keys = kt[...].T
+    pos = keys[:, wide - 128 :].astype(F32)
     at = width - (wide - 128)
     key_pos = pos[:, at : at + 1] * 64.0 + pos[:, at + 1 : at + 2]
-    qt[width:, :] = jnp.zeros((wide - width, rows), BF16)
+    lane = lax.broadcasted_iota(jnp.int32, keys.shape, 1)
+    k_ref[...] = jnp.where(lane < width, keys, jnp.zeros_like(keys))
     stat_ref[...] = jnp.zeros_like(stat_ref)
-    stat_ref[GROUP * heads : GROUP * heads + heads, :] = delta_ref[:heads, :]
+    if last:
+        stat_ref[GROUP * heads : GROUP * heads + heads, :] = delta_ref[:heads, :]
     for j in range(GROUP):
-        q_ref = q_refs[j]
-        for h in range(heads):
-            qt[:width, h * tok : (h + 1) * tok] = q_ref[h * width : (h + 1) * width, :]
-        base = q_ref.shape[0] - EXTRA
-        qp = q_ref[base:, :].astype(F32)
-        one = qp[0:1, :] * 64.0 + qp[1:2, :]
-        row_pos = jnp.concatenate([one] * heads, axis=1)
-        s = mm(k_ref[...], qt[...]) * factor
+        cols = slice(j * rows, (j + 1) * rows)
+        qp = q_all_ref[width : width + EXTRA, cols].astype(F32)
+        row_pos = qp[0:1, :] * 64.0 + qp[1:2, :]
+        s = mm(k_ref[...], q_all_ref[:, cols]) * factor
         s = jnp.where(key_pos <= row_pos, s, -1e30)
-        s_ref[:, j * rows : (j + 1) * rows] = s
+        s_ref[:, cols] = s
         top = jnp.max(s, axis=0, keepdims=True)
         lse = top + jnp.log(jnp.sum(jnp.exp(s - top), axis=0, keepdims=True))
         for h in range(heads):
             at = j * heads + h
-            stat_ref[at : at + 1, :] = lse[:, h * tok : (h + 1) * tok]
+            part = lse[:, h * tok : (h + 1) * tok]
+            if last:
+                near = near_ref[at : at + 1, :]
+                most = jnp.maximum(part, near)
+                part = most + jnp.log(jnp.exp(part - most) + jnp.exp(near - most))
+            stat_ref[at : at + 1, :] = part
 
 
 def context_kernel(width, heads, *refs):
     q_refs = refs[:GROUP]
-    wuv_ref, k_ref, g_ref, gp_ref = refs[GROUP:]
+    wuv_ref, near_k_ref, last_k_ref, g_ref, near_gp_ref, last_gp_ref = refs[GROUP:]
     lat, all_rows = g_ref.shape
     tok = q_refs[0].shape[1]
     rows = heads * tok
@@ -151,21 +164,27 @@
             col = j * rows + h * tok
             g_ref[:, col : col + tok] = mm(wuv_ref[h], og).astype(BF16)
         cols = slice(j * rows, (j + 1) * rows)
-        gp_ref[:, cols] = mm(k_ref[:, :lat], g_ref[:, cols])
-
-
-def grad_kernel(factor, nkey, width, heads, *refs):
-    lat_refs, refs = refs[:nkey], refs[nkey:]
-    q_refs, refs = refs[:GROUP], refs[GROUP:]
+        near_gp_ref[:, cols] = mm(near_k_ref[:, :lat], g_ref[:, cols])
+        last_gp_ref[:, cols] = mm(last_k_ref[:, :lat], g_ref[:, cols])
+
+
+def grad_kernel(factor, nkey, width, heads, last, *refs):
     stats, refs = refs[:GROUP], refs[GROUP:]
-    (s_ref, gp_ref, g_ref), refs = refs[:3], refs[3:]
-    part_refs, refs = refs[:nkey], refs[nkey:]
-    own_ref, core_ref, across_ref, kt, qt, gs_all, p_all = refs
-    tok = q_refs[0].shape[1]
-    rows = heads * tok
-    lat = g_ref.shape[0]
-    for a in range(nkey):
-        kt[:, a * tok : (a + 1) * tok] = lat_refs[a][:width, :]
+    (s_ref, gp_ref, g_ref, q_all_ref), refs = refs[:4], refs[4:]
+    if last:
+        part_refs, gs_all, p_all = refs[:nkey], refs[nkey], refs[nkey + 1]
+    else:
+        lat_refs, refs = refs[: nkey + 1], refs[nkey + 1 :]
+        last_gs_ref, refs = refs[0], refs[1:]
+        part_refs, refs = refs[:nkey], refs[nkey:]
+        own_ref, core_ref, across_ref, kt, gs_all, p_all = refs
+    lat, all_rows = g_ref.shape
+    rows = all_rows // GROUP
+    tok = rows // heads
+    keys = nkey * tok
+    if not last:
+        for a in range(nkey + 1):
+            kt[:, a * tok : (a + 1) * tok] = lat_refs[a][:width, :]
     for j in range(GROUP):
         cols = slice(j * rows, (j + 1) * rows)
         lse_parts = []
@@ -182,10 +201,11 @@
         gs = (p * (gp_ref[:, cols] - delta)).astype(BF16)
         gs_all[:, cols] = gs
         p_all[:, cols] = p.astype(BF16)
-        gq = (mm(kt[...], gs) * factor).astype(BF16)
+        if last:
+            continue
+        gq = mm(kt[:, :keys], gs) + mm(kt[:, keys:], last_gs_ref[:, cols])
+        gq = (gq * factor).astype(BF16)
         for h in range(heads):
-            head_cols = slice(j * rows + h * tok, j * rows + (h + 1) * tok)
-            qt[:, head_cols] = q_refs[j][h * width : (h + 1) * width, :]
             part = gq[:, h * tok : (h + 1) * tok]
             if j == 0:
                 own_ref[h] = part
@@ -195,18 +215,14 @@
                 core_ref[j // 2 * heads + h] = part
     for a in range(nkey):
         at = slice(a * tok, (a + 1) * tok)
-        along = mm_t(qt[...], gs_all[at, :]) * factor
+        along = mm_t(q_all_ref[:width, :], gs_all[at, :]) * factor
         value = mm_t(g_ref[...], p_all[at, :])
         part_refs[a][:lat, :] = (along[:lat] + value).astype(BF16)
         part_refs[a][lat:, :] = along[lat:].astype(BF16)
 
 
-def sum_kernel(gq_own_ref, gq_got_ref, gq_last_ref, *refs):
-    parts, (lat_out_ref, q_out_ref) = refs[:-2], refs[-2:]
-    lat_out_ref[...] = sum(part[...].astype(F32) for part in parts).astype(BF16)
-    for h in range(q_out_ref.shape[0]):
-        pieces = (gq_own_ref[h], gq_got_ref[h], gq_last_ref[h])
-        q_out_ref[h] = sum(piece.astype(F32) for piece in pieces).astype(BF16)
+def sum_kernel(*refs):
+    refs[-1][...] = sum(ref[...].astype(F32) for ref in refs[:-1]).astype(BF16)
 
 
 def spread_kernel(scale, idx_ref, *refs):
@@ -285,8 +301,11 @@
         "hold_own",
         [(lat_msg.shape, BF16), (q_msg.shape, BF16), (delta.shape, F32)],
         [lat_msg, q_msg, delta],
-    )
-    q_core, q_across, firsts, got_pair = lax.optimization_barrier((q_core, q_across, firsts, got_pair))
+        share=0,
+    )
+    q_core, q_across, firsts, got_pair, own = lax.optimization_barrier(
+        (q_core, q_across, firsts, got_pair, own)
+    )
     held = {0: lat_msg}
     for bit in reversed(range(line_bits)):
         held.update({m | 1 << bit: swap(x, GROUP << bit) for m, x in held.items() if m})
@@ -297,73 +316,83 @@
     lats = [held[m] for m in range(lines)]
     q_far = swap(q_across, 1)
     got_own = swap(pair[heads:], 2)
-    q_far, lats, got_own, own = lax.optimization_barrier((q_far, lats, got_own, own))
     lat_own, q_own, delta = own
     lats[0] = lat_own
     qs = [q_own, q_core, q_across, q_far]
-    mine = add(pair[:heads], got_own)
+
+    most = lines - 1
+    keys = most * tok
+    score_flops = 2 * tok * all_rows * wide
+    near_s, near_k, near_stat, q_all = call(
+        functools.partial(score_kernel, factor, most, width, heads, False),
+        "near_scores",
+        [((keys, all_rows), F32), ((keys, wide), BF16), ((EXTRA, tok), F32), ((wide, all_rows), BF16)],
+        lats[:most] + qs,
+        [((wide, keys), BF16)],
+        flops=most * score_flops,
+        share=0,
+    )
+    mine = add(pair[:heads], after(got_own, near_stat))
     near = swap(mine, *line_hops[0])
-
-    s, k_nat, stat = call(
-        functools.partial(score_kernel, factor, lines, width, heads),
-        "scores",
-        [((keys, all_rows), F32), ((keys, wide), BF16), ((EXTRA, tok), F32)],
-        lats + qs + [delta],
-        [((wide, keys), BF16), ((wide, rows), BF16)],
-        flops=2 * keys * all_rows * wide,
+    last_s, last_k, stat = call(
+        functools.partial(score_kernel, factor, 1, width, heads, True),
+        "last_scores",
+        [((tok, all_rows), F32), ((tok, wide), BF16), ((EXTRA, tok), F32)],
+        [lats[most], q_all, near_stat, delta],
+        [((wide, tok), BF16)],
+        flops=score_flops,
     )
     stats = [stat] + [swap(stat, k) for k in range(1, GROUP)]
-    mine = add(mine, after(near, stat))
+    g, near_gp, last_gp = call(
+        functools.partial(context_kernel, width, heads),
+        "context",
+        [((lat, all_rows), BF16), ((keys, all_rows), F32), ((tok, all_rows), F32)],
+        qs + [wuv, near_k, last_k],
+        flops=2 * lines * tok * all_rows * lat + 2 * all_rows * lat * HEAD_DIM,
+    )
+    near, stats = lax.optimization_barrier((after(near, last_gp), stats))
+    mine = add(mine, near)
     for step_hop in line_hops[1:-1]:
         mine = add(mine, swap(mine, *step_hop))
     near = swap(mine, *line_hops[-1])
-    g, gp = call(
-        functools.partial(context_kernel, width, heads),
-        "context",
-        [((lat, all_rows), BF16), ((keys, all_rows), F32)],
-        qs + [wuv, k_nat],
-        flops=2 * keys * all_rows * lat + 2 * all_rows * lat * HEAD_DIM,
-    )
-    near, stats = lax.optimization_barrier((after(near, gp), stats))
+    last_part, last_gs = call(
+        functools.partial(grad_kernel, factor, 1, width, heads, True),
+        "last_gradients",
+        [((width, tok), BF16), ((tok, all_rows), BF16)],
+        stats + [last_s, last_gp, g, q_all],
+        [((tok, all_rows), BF16)],
+        flops=2 * tok * all_rows * (width + lat),
+    )
+    last_got = swap(last_part, GROUP)
+    outs = call(
+        functools.partial(grad_kernel, factor, most, width, heads, False),
+        "near_gradients",
+        [((width, tok), BF16)] * most
+        + [((heads, width, tok), BF16), ((2 * heads, width, tok), BF16), ((heads, width, tok), BF16)],
+        stats + [near_s, near_gp, g, q_all] + lats + [last_gs],
+        [((width, lines * tok), BF16), ((keys, all_rows), BF16), ((keys, all_rows), BF16)],
+        flops=2 * keys * all_rows * (width + lat) + 2 * lines * tok * all_rows * width,
+    )
+    parts, (gq_own, gq_core, gq_across) = list(outs[:most]) + [last_part], outs[most:]
     mine = add(mine, near)
-    outs = call(
-        functools.partial(grad_kernel, factor, lines, width, heads),
-        "gradients",
-        [((width, tok), BF16)] * lines
-        + [((heads, width, tok), BF16), ((2 * heads, width, tok), BF16), ((heads, width, tok), BF16)],
-        lats + qs + stats + [s, gp, g],
-        [
-            ((width, keys), BF16),
-            ((width, all_rows), BF16),
-            ((keys, all_rows), BF16),
-            ((keys, all_rows), BF16),
-        ],
-        flops=2 * keys * all_rows * (2 * width + lat),
-    )
-    parts, (gq_own, gq_core, gq_across) = list(outs[:lines]), outs[lines:]
-    gq_got = swap(gq_core, 1)
+    kept = [parts[0]]
+    gq_got = swap(after(gq_core, last_got, near), 1)
     gq_sum = add(gq_across, gq_got[heads:])
     gq_last = swap(gq_sum, 2)
-    across = swap(after(mine, gq_sum), 2)
     for bit in range(line_bits):
         for m in range(3 << bit, lines, 2 << bit):
-            got = swap(parts[m], GROUP << bit)
-            parts[m ^ 1 << bit] = add(parts[m ^ 1 << bit], after(got, gq_sum))
-    parts[1] = after(parts[1], parts[lines // 2])
-    kept = [swap(parts[1 << bit], GROUP << bit) for bit in reversed(range(line_bits))]
-    mine_two = jnp.concatenate([mine, after(across, gq_sum)], axis=0)
-    other_two = swap(mine_two, 1)
+            got = last_got if m == most and bit == 0 else swap(parts[m], GROUP << bit)
+            parts[m ^ 1 << bit] = add(parts[m ^ 1 << bit], got)
+    pieces = [mine] + [swap(mine, k) for k in range(1, GROUP)]
+    parts[1] = after(parts[1], gq_sum)
+    kept += [swap(parts[1 << bit], GROUP << bit) for bit in reversed(range(line_bits))]
     scale = 1.0 / math.sqrt(tok * n_ctx * n_dp)
-    pieces = [mine_two[:heads], other_two[:heads], mine_two[heads:], other_two[heads:]]
     (grad_w,) = call(
         functools.partial(spread_kernel, scale), "spread", [((heads, lat, HEAD_DIM), F32)], [idx] + pieces, smem=(0,)
     )
-    grad_lat, grad_q = call(
-        sum_kernel,
-        "last_sums",
-        [((width, tok), BF16), ((heads, width, tok), BF16)],
-        [gq_own, gq_got, gq_last, after(parts[0], grad_w)] + kept,
-    )
+    (grad_lat,) = call(sum_kernel, "latent_sum", [((width, tok), BF16)], kept)
+    gq_pieces = [gq_own, gq_got[:heads], after(gq_last, grad_lat)]
+    (grad_q,) = call(sum_kernel, "query_sum", [((heads, width, tok), BF16)], gq_pieces)
     return (jnp.transpose(grad_q, (2, 0, 1))[None], grad_lat.T[None], grad_w)
 
 

time: 57.5 us -> 55.4 us (0.963)
  waiting for transfers between devices: 21.8 us -> 17.3 us
  Pallas kernels: 10.9 us -> 12.5 us
  starting transfers between devices: 20 us -> 20.7 us
    ppermute x21 -> x22, waiting for transfers between devices: 21.8 us -> 17.3 us  [swap(): return lax.ppermute(x, axis, [(i, i ^ mask) for i in range(size)])]
    pallas_call x7 -> x10, Pallas kernels: 10.9 us -> 12.5 us  [call(): pl.pallas_call(kernel, out_shape=[jax.ShapeDtypeStruct(s, d) for s, d in...]
    ppermute x21 -> x22, starting transfers between devices: 20 us -> 20.7 us  [swap(): return lax.ppermute(x, axis, [(i, i ^ mask) for i in range(size)])]
  transfers between devices with their start and end apart: 21 -> 22, of which waited for: 11 -> 11; matrix products, arithmetic and copies ran while one was open for 2% -> 2% of each run, Pallas kernels for 6% -> 14%
where the time goes in v7:
time: 55.4 us; the launch traced here: 55.1 us
  starting transfers between devices  20.7 us (37%)
  waiting for transfers between devices  17.3 us (31%)
  Pallas kernels  12.5 us (23%)
  local copies, waits for them, and re-layouts  2.61 us (5%)
  other arithmetic  1.17 us (2%)
  between operations  0.8 us (1%)
    ppermute x22, starting transfers between devices, swap(): return lax.ppermute(x, axis, [(i, i ^ mask) for i in range(size)])  20.7 us
    ppermute x22, waiting for transfers between devices, swap(): return lax.ppermute(x, axis, [(i, i ^ mask) for i in range(size)])  17.3 us
    pallas_call x10, Pallas kernels, call(): pl.pallas_call(kernel, out_shape=[jax.ShapeDtypeStruct(s, d) for s, d in...  12.5 us
    unnamed x8, local copies, waits for them, and re-layouts  2.58 us
    convert_element_type x7, other arithmetic, add(): return (a.astype(F32) + b.astype(F32)).astype(BF16)  1.17 us
  transfers between devices with their start and end apart: 22, of which 11 were waited for; matrix products, arithmetic and copies ran while one was open for 2% of the time, Pallas kernels for 14%

profile of v7, /device:TPU:0, one launch (start us, length us, event | category | flops | bytes accessed | tf_op | source)
XLA Modules:
  0.0 55.1 jit_solution(7910910308772680480)
XLA Ops:
  0.6 3.0 %pack.1 = (bf16[592,128]{1,0:T(8,128)(2,1)}, bf16[1424,128]{1,0:T(8,128)(2,1)}, f32[8,128]{1,0:T(8,128)}, bf16[4,128,128]{2,1,0:T(8,128)(2,1)}, bf16[4,128,128]{2,1,0:T(8,128)(2,1)}) custom-call(s32[1]{0:T(128)} %bitcast.idx_ref, s32[1,128]{1,0:T(1,128)} %pos_hbm.1, bf16[2,576,128]{2,1,0:T(8,128)(2,1)} %bitcast.15, bf16[128,2,128]{2,1,0:T(2,128)(2,1)} %bitcast.20, ...), custom_call_target="tpu_custom_call" | custom-call | bytes 1815044 | tf_op jit(solution)/shard_map/pack/pallas_call | solution.py:39
  3.7 0.5 collective-permute-start
  4.2 0.1 collective-permute-start.1
  4.3 2.9 %collective-permute-start.2 = (bf16[1424,128]{1,0:T(8,128)(2,1)}, bf16[1424,128]{1,0:T(8,128)(2,1)S(1)}, u32[]{:S(2)}, u32[]{:S(2)}) collective-permute-start(bf16[1424,128]{1,0:T(8,128)(2,1)} %get-tuple-element.50.refs_1_), channel_id=1, source_target_pairs={{0,2},{1,3},{2,0},{3,1},{4,6},{5,7},{6,4},{7,5},{8,10},{9,11},{10,... | collective-permute-start | bytes 1093640 | tf_op jit(solution)/shard_map/ppermute | solution.py:249
  7.2 2.6 %collective-permute-start.4 = (bf16[592,128]{1,0:T(8,128)(2,1)}, bf16[592,128]{1,0:T(8,128)(2,1)S(1)}, u32[]{:S(2)}, u32[]{:S(2)}) collective-permute-start(bf16[592,128]{1,0:T(8,128)(2,1)} %get-tuple-element.52.refs_0_), channel_id=1, source_target_pairs={{0,8},{1,9},{2,10},{3,11},{4,12},{5,13},{6,14},{7,15},{8,0},{9,1},... | collective-permute-start | bytes 454664 | tf_op jit(solution)/shard_map/ppermute | solution.py:249
  9.8 0.0 collective-permute-done
  9.8 0.9 %add_convert_fusion.3 = bf16[4,128,128]{2,1,0:T(8,128)(2,1)S(1)} fusion(bf16[4,128,128]{2,1,0:T(8,128)(2,1)S(1)} %collective-permute-done, bf16[4,128,128]{2,1,0:T(8,128)(2,1)} %get-tuple-element.48), kind=kLoop, calls=%fused_computation.3 | loop fusion | flops 262144 | bytes 393216 | tf_op jit(solution)/shard_map/convert_element_type | solution.py:289
  10.8 1.6 %collective-permute-start.3 = (bf16[592,128]{1,0:T(8,128)(2,1)}, bf16[592,128]{1,0:T(8,128)(2,1)S(1)}, u32[]{:S(2)}, u32[]{:S(2)}) collective-permute-start(bf16[592,128]{1,0:T(8,128)(2,1)} %get-tuple-element.52.refs_0_), channel_id=1, source_target_pairs={{0,4},{1,5},{2,6},{3,7},{4,0},{5,1},{6,2},{7,3},{8,12},{9,13},{10,... | collective-permute-start | bytes 454664 | tf_op jit(solution)/shard_map/ppermute | solution.py:249
  12.4 1.5 %collective-permute-start.5 = (bf16[4,128,128]{2,1,0:T(8,128)(2,1)S(1)}, bf16[4,128,128]{2,1,0:T(8,128)(2,1)S(1)}, u32[]{:S(2)}, u32[]{:S(2)}) collective-permute-start(bf16[4,128,128]{2,1,0:T(8,128)(2,1)S(1)} %add_convert_fusion.3), channel_id=1, source_target_pairs={{0,16},{16,0},{1,17},{17,1},{2,18},{18,2},{3,19},{19,3},{4,20},{20... | collective-permute-start | bytes 393224 | tf_op jit(solution)/shard_map/ppermute | solution.py:249
  13.9 0.0 copy-start
  13.9 1.0 %copy-done = bf16[1424,128]{1,0:T(8,128)(2,1)S(1)} copy-done((bf16[1424,128]{1,0:T(8,128)(2,1)S(1)}, bf16[1424,128]{1,0:T(8,128)(2,1)}, u32[]{:S(2)}) %copy-start) | copy-done | bytes 364568
  14.9 0.0 copy-start.2
  14.9 0.9 %copy-done.2 = bf16[592,128]{1,0:T(8,128)(2,1)S(1)} copy-done((bf16[592,128]{1,0:T(8,128)(2,1)S(1)}, bf16[592,128]{1,0:T(8,128)(2,1)}, u32[]{:S(2)}) %copy-start.2) | copy-done | bytes 151576
  15.8 0.0 copy-start.3
  15.8 0.7 %copy-done.3 = f32[8,128]{1,0:T(8,128)S(1)} copy-done((f32[8,128]{1,0:T(8,128)S(1)}, f32[8,128]{1,0:T(8,128)}, u32[]{:S(2)}) %copy-start.3) | copy-done | bytes 4120
  16.5 0.8 %collective-permute-done.4.refs_2_.refs_10_ = bf16[592,128]{1,0:T(8,128)(2,1)S(1)} collective-permute-done((bf16[592,128]{1,0:T(8,128)(2,1)}, bf16[592,128]{1,0:T(8,128)(2,1)S(1)}, u32[]{:S(2)}, u32[]{:S(2)}) %collective-permute-start.4) | collective-permute-done | bytes 151584 | tf_op jit(solution)/shard_map/ppermute | solution.py:249
  17.3 0.0 collective-permute-done.5
  17.4 1.2 %collective-permute-done.3.refs_1_.refs_9_ = bf16[592,128]{1,0:T(8,128)(2,1)S(1)} collective-permute-done((bf16[592,128]{1,0:T(8,128)(2,1)}, bf16[592,128]{1,0:T(8,128)(2,1)S(1)}, u32[]{:S(2)}, u32[]{:S(2)}) %collective-permute-start.3) | collective-permute-done | bytes 151584 | tf_op jit(solution)/shard_map/ppermute | solution.py:249
  18.5 0.0 collective-permute-done.1.refs_4_.refs_1_
  18.5 0.0 collective-permute-done.2.refs_5_.refs_2_
  18.5 0.0 collective-permute-start.7
  18.6 0.0 copy-start.1
  18.6 0.5 collective-permute-start.6
  19.1 0.5 collective-permute-start.9
  19.6 0.6 %collective-permute-done.7.refs_6_.refs_3_ = bf16[1424,128]{1,0:T(8,128)(2,1)S(1)} collective-permute-done((bf16[1424,128]{1,0:T(8,128)(2,1)S(1)}, bf16[1424,128]{1,0:T(8,128)(2,1)S(1)}, u32[]{:S(2)}, u32[]{:S(2)}) %collective-permute-start.7) | collective-permute-done | bytes 364576 | tf_op jit(solution)/shard_map/ppermute | solution.py:249
  20.2 1.2 %near_scores.1 = (f32[384,1024]{1,0:T(8,128)S(1)}, bf16[384,640]{1,0:T(8,128)(2,1)S(1)}, f32[16,128]{1,0:T(8,128)S(1)}, bf16[640,1024]{1,0:T(8,128)(2,1)S(1)}) custom-call(bf16[592,128]{1,0:T(8,128)(2,1)S(1)} %get-tuple-element.58.refs_0_.refs_8_, bf16[592,128]{1,0:T(8,128)(2,1)S(1)} %collective-permute-done.3.refs_1_.refs_9_, ...), custom_call_target="tpu_custom_call" | custom-call | tf_op jit(solution)/shard_map/near_scores/pallas_call | solution.py:39
  21.5 1.7 %collective-permute-done.6 = bf16[2,128,128]{2,1,0:T(8,128)(2,1)S(1)} collective-permute-done((bf16[2,128,128]{2,1,0:T(8,128)(2,1)S(1)}, bf16[2,128,128]{2,1,0:T(8,128)(2,1)S(1)}, u32[]{:S(2)}, u32[]{:S(2)}) %collective-permute-start.6) | collective-permute-done | bytes 65568 | tf_op jit(solution)/shard_map/ppermute | solution.py:249
  23.2 0.5 collective-permute-start.8
  23.7 1.5 %collective-permute-done.9.refs_0_.refs_11_ = bf16[592,128]{1,0:T(8,128)(2,1)S(1)} collective-permute-done((bf16[592,128]{1,0:T(8,128)(2,1)S(1)}, bf16[592,128]{1,0:T(8,128)(2,1)S(1)}, u32[]{:S(2)}, u32[]{:S(2)}) %collective-permute-start.9) | collective-permute-done | bytes 151584 | tf_op jit(solution)/shard_map/ppermute | solution.py:249
  25.2 0.5 last_scores.1
  25.7 0.1 collective-permute-start.10
  25.8 2.3 %collective-permute-start.11 = (f32[16,128]{1,0:T(8,128)S(1)}, f32[16,128]{1,0:T(8,128)S(1)}, u32[]{:S(2)}, u32[]{:S(2)}) collective-permute-start(f32[16,128]{1,0:T(8,128)S(1)} %get-tuple-element.73.refs_0_), channel_id=1, source_target_pairs={{0,2},{1,3},{2,0},{3,1},{4,6},{5,7},{6,4},{7,5},{8,10},{9,11},{10,... | collective-permute-start | bytes 24584 | tf_op jit(solution)/shard_map/ppermute | solution.py:249
  28.1 0.1 collective-permute-start.12
  28.2 0.0 copy-done.1
  28.2 1.6 %context.1 = (bf16[512,1024]{1,0:T(8,128)(2,1)S(1)}, f32[384,1024]{1,0:T(8,128)S(1)}, f32[128,1024]{1,0:T(8,128)S(1)}) custom-call(bf16[1424,128]{1,0:T(8,128)(2,1)S(1)} %get-tuple-element.61.refs_3_.refs_0_, bf16[1424,128]{1,0:T(8,128)(2,1)S(1)} %collective-permute-done.1.refs_4_.refs_1_, bf16[1424,128]{1,0:T(8,128)(2,1)S(1)} %collective-permute-done.2.refs_5_.refs_2_, ...), custom_call_target="tpu_custom_call" | custom-call | flops 671088640 | bytes 5521408 | tf_op jit(solution)/shard_map/context/pallas_call | solution.py:39
  29.8 0.0 collective-permute-done.8
  29.8 0.0 collective-permute-done.10.refs_1_
  29.8 0.0 collective-permute-done.11.refs_2_
  29.8 1.4 %collective-permute-done.12.refs_3_ = f32[16,128]{1,0:T(8,128)S(1)} collective-permute-done((f32[16,128]{1,0:T(8,128)S(1)}, f32[16,128]{1,0:T(8,128)S(1)}, u32[]{:S(2)}, u32[]{:S(2)}) %collective-permute-start.12) | collective-permute-done | bytes 8224 | tf_op jit(solution)/shard_map/ppermute | solution.py:249
  31.2 0.8 %last_gradients.1 = (bf16[576,128]{1,0:T(8,128)(2,1)S(1)}, bf16[128,1024]{1,0:T(8,128)(2,1)S(1)}) custom-call(f32[16,128]{1,0:T(8,128)S(1)} %get-tuple-element.73.refs_0_, f32[16,128]{1,0:T(8,128)S(1)} %collective-permute-done.10.refs_1_, f32[16,128]{1,0:T(8,128)S(1)} %collective-permute-done.11.refs_2_, f32[16,128]{1,0:T(8,128)S(1)} %collective-permute-done.12.refs_3_, ...), custom_call_target="tpu_custom_call" | custom-call | flops 285212672 | bytes 3850240 | tf_op jit(solution)/shard_map/last_gradients/pallas_call | solution.py:39
  32.0 0.3 collective-permute-start.13
  32.4 2.3 %collective-permute-start.14 = (bf16[2,128,128]{2,1,0:T(8,128)(2,1)S(1)}, bf16[2,128,128]{2,1,0:T(8,128)(2,1)S(1)}, u32[]{:S(2)}, u32[]{:S(2)}) collective-permute-start(bf16[2,128,128]{2,1,0:T(8,128)(2,1)S(1)} %add_convert_fusion.5), channel_id=1, source_target_pairs={{0,8},{1,9},{2,10},{3,11},{4,12},{5,13},{6,14},{7,15},{8,0},{9,1},... | collective-permute-start | bytes 196616 | tf_op jit(solution)/shard_map/ppermute | solution.py:249
  34.6 2.9 %near_gradients.1 = (bf16[576,128]{1,0:T(8,128)(2,1)S(1)}, bf16[576,128]{1,0:T(8,128)(2,1)S(1)}, bf16[576,128]{1,0:T(8,128)(2,1)S(1)}, bf16[2,576,128]{2,1,0:T(8...) custom-call(f32[16,128]{1,0:T(8,128)S(1)} %get-tuple-element.73.refs_0_, ...), custom_call_target="tpu_custom_call" | custom-call | flops 1459617792 | bytes 8028160 | tf_op jit(solution)/shard_map/near_gradients/pallas_call | solution.py:39
  37.5 0.2 collective-permute-done.14
  37.7 1.7 %collective-permute-done.13 = bf16[576,128]{1,0:T(8,128)(2,1)S(1)} collective-permute-done((bf16[576,128]{1,0:T(8,128)(2,1)S(1)}, bf16[576,128]{1,0:T(8,128)(2,1)S(1)}, u32[]{:S(2)}, u32[]{:S(2)}) %collective-permute-start.13) | collective-permute-done | bytes 147488 | tf_op jit(solution)/shard_map/ppermute | solution.py:249
  39.4 0.0 collective-permute-start.15
  39.4 1.3 %collective-permute-start.17 = (bf16[576,128]{1,0:T(8,128)(2,1)S(1)}, bf16[576,128]{1,0:T(8,128)(2,1)S(1)}, u32[]{:S(2)}, u32[]{:S(2)}) collective-permute-start(bf16[576,128]{1,0:T(8,128)(2,1)S(1)} %add_convert_fusion.1), channel_id=1, source_target_pairs={{0,8},{1,9},{2,10},{3,11},{4,12},{5,13},{6,14},{7,15},{8,0},{9,1},... | collective-permute-start | bytes 442376 | tf_op jit(solution)/shard_map/ppermute | solution.py:249
  40.7 0.7 %collective-permute-done.15 = bf16[4,576,128]{2,1,0:T(8,128)(2,1)S(1)} collective-permute-done((bf16[4,576,128]{2,1,0:T(8,128)(2,1)S(1)}, bf16[4,576,128]{2,1,0:T(8,128)(2,1)S(1)}, u32[]{:S(2)}, u32[]{:S(2)}) %collective-permute-start.15) | collective-permute-done | bytes 589856 | tf_op jit(solution)/shard_map/ppermute | solution.py:249
  41.4 0.1 add_convert_fusion
  41.5 0.6 %collective-permute-start.16 = (bf16[2,576,128]{2,1,0:T(8,128)(2,1)S(1)}, bf16[2,576,128]{2,1,0:T(8,128)(2,1)S(1)}, u32[]{:S(2)}, u32[]{:S(2)}) collective-permute-start(bf16[2,576,128]{2,1,0:T(8,128)(2,1)S(1)} %add_convert_fusion), channel_id=1, source_target_pairs={{0,2},{1,3},{2,0},{3,1},{4,6},{5,7},{6,4},{7,5},{8,10},{9,11},{10,... | collective-permute-start | bytes 884744 | tf_op jit(solution)/shard_map/ppermute | solution.py:249
  42.1 1.7 %collective-permute-start.18 = (bf16[576,128]{1,0:T(8,128)(2,1)S(1)}, bf16[576,128]{1,0:T(8,128)(2,1)S(1)}, u32[]{:S(2)}, u32[]{:S(2)}) collective-permute-start(bf16[576,128]{1,0:T(8,128)(2,1)S(1)} %get-tuple-element.91), channel_id=1, source_target_pairs={{0,4},{1,5},{2,6},{3,7},{4,0},{5,1},{6,2},{7,3},{8,12},{9,13},{10,... | collective-permute-start | bytes 442376 | tf_op jit(solution)/shard_map/ppermute | solution.py:249
  43.8 0.1 collective-permute-start.19
  43.9 0.6 %collective-permute-start.20 = (bf16[2,128,128]{2,1,0:T(8,128)(2,1)S(1)}, bf16[2,128,128]{2,1,0:T(8,128)(2,1)S(1)}, u32[]{:S(2)}, u32[]{:S(2)}) collective-permute-start(bf16[2,128,128]{2,1,0:T(8,128)(2,1)S(1)} %add_convert_fusion.4.refs_0_), channel_id=1, source_target_pairs={{0,2},{1,3},{2,0},{3,1},{4,6},{5,7},{6,4},{7,5},{8,10},{9,11},{10,... | collective-permute-start | bytes 196616 | tf_op jit(solution)/shard_map/ppermute | solution.py:249
  44.5 0.6 %collective-permute-done.19.refs_1_ = bf16[2,128,128]{2,1,0:T(8,128)(2,1)S(1)} collective-permute-done((bf16[2,128,128]{2,1,0:T(8,128)(2,1)S(1)}, bf16[2,128,128]{2,1,0:T(8,128)(2,1)S(1)}, u32[]{:S(2)}, u32[]{:S(2)}) %collective-permute-start.19) | collective-permute-done | bytes 65568 | tf_op jit(solution)/shard_map/ppermute | solution.py:249
  45.1 0.6 %collective-permute-start.21 = (bf16[2,128,128]{2,1,0:T(8,128)(2,1)S(1)}, bf16[2,128,128]{2,1,0:T(8,128)(2,1)S(1)}, u32[]{:S(2)}, u32[]{:S(2)}) collective-permute-start(bf16[2,128,128]{2,1,0:T(8,128)(2,1)S(1)} %add_convert_fusion.4.refs_0_), channel_id=1, source_target_pairs={{0,3},{1,2},{2,1},{3,0},{4,7},{5,6},{6,5},{7,4},{8,11},{9,10},{10,... | collective-permute-start | bytes 196616 | tf_op jit(solution)/shard_map/ppermute | solution.py:249
  45.8 7.0 %collective-permute-done.20.refs_2_ = bf16[2,128,128]{2,1,0:T(8,128)(2,1)S(1)} collective-permute-done((bf16[2,128,128]{2,1,0:T(8,128)(2,1)S(1)}, bf16[2,128,128]{2,1,0:T(8,128)(2,1)S(1)}, u32[]{:S(2)}, u32[]{:S(2)}) %collective-permute-start.20) | collective-permute-done | bytes 65568 | tf_op jit(solution)/shard_map/ppermute | solution.py:249
  52.7 0.0 collective-permute-done.21.refs_3_
  52.7 0.8 %spread.1 = f32[2,512,128]{2,1,0:T(8,128)} custom-call(s32[1]{0:T(128)} %bitcast.idx_ref, bf16[2,128,128]{2,1,0:T(8,128)(2,1)S(1)} %add_convert_fusion.4.refs_0_, bf16[2,128,128]{2,1,0:T(8,128)(2,1)S(1)} %collective-permute-done.19.refs_1_, bf16[2,128,128]{2,1,0:T(8,128)(2,1)S(1)} %collective-permute-done.20.refs_2_, ...), custom_call_target="tpu_custom_call" | custom-call | bytes 786436 | tf_op jit(solution)/shard_map/spread/pallas_call | solution.py:39
  53.6 0.0 collective-permute-done.17.refs_1_
  53.6 0.0 collective-permute-done.18.refs_2_
  53.6 0.7 %latent_sum.1 = bf16[576,128]{1,0:T(8,128)(2,1)} custom-call(bf16[576,128]{1,0:T(8,128)(2,1)S(1)} %get-tuple-element.88.refs_0_, bf16[576,128]{1,0:T(8,128)(2,1)S(1)} %collective-permute-done.17.refs_1_, bf16[576,128]{1,0:T(8,128)(2,1)S(1)} %collective-permute-done.18.refs_2_), custom_call_target="tpu_custom_call" | custom-call | bytes 589824 | tf_op jit(solution)/shard_map/latent_sum/pallas_call | solution.py:39
  54.3 0.0 collective-permute-done.16.refs_2_
  54.3 0.8 %query_sum.1 = bf16[2,576,128]{2,1,0:T(8,128)(2,1)} custom-call(bf16[2,576,128]{2,1,0:T(8,128)(2,1)S(1)} %get-tuple-element.82.refs_0_, bf16[2,576,128]{2,1,0:T(8,128)(2,1)S(1)} %slice.18.refs_1_, bf16[2,576,128]{2,1,0:T(8,128)(2,1)S(1)} %collective-permute-done.16.refs_2_), custom_call_target="tpu_custom_call" | custom-call | bytes 1179648 | tf_op jit(solution)/shard_map/query_sum/pallas_call | solution.py:39
  (8 shorter events, 0.2 us)
Async XLA Ops:
  3.7 6.1 %collective-permute-start = (bf16[4,128,128]{2,1,0:T(8,128)(2,1)}, bf16[4,128,128]{2,1,0:T(8,128)(2,1)S(1)}, u32[]{:S(2)}, u32[]{:S(2)}) collective-permute-start(bf16[4,128,128]{2,1,0:T(8,128)(2,1)} %get-tuple-element.49), channel_id=1, source_target_pairs={{0,1},{1,0},{2,3},{3,2},{4,5},{5,4},{6,7},{7,6},{8,9},{9,8},{10,11... | collective-permute-start | bytes 393224 | tf_op jit(solution)/shard_map/ppermute | solution.py:249
  4.2 14.3 %collective-permute-start.1 = (bf16[1424,128]{1,0:T(8,128)(2,1)}, bf16[1424,128]{1,0:T(8,128)(2,1)S(1)}, u32[]{:S(2)}, u32[]{:S(2)}) collective-permute-start(bf16[1424,128]{1,0:T(8,128)(2,1)} %get-tuple-element.50.refs_1_), channel_id=1, source_target_pairs={{0,1},{1,0},{2,3},{3,2},{4,5},{5,4},{6,7},{7,6},{8,9},{9,8},{10,11... | collective-permute-start | bytes 1093640 | tf_op jit(solution)/shard_map/ppermute | solution.py:249
  4.3 14.3 %collective-permute-start.2 = (bf16[1424,128]{1,0:T(8,128)(2,1)}, bf16[1424,128]{1,0:T(8,128)(2,1)S(1)}, u32[]{:S(2)}, u32[]{:S(2)}) collective-permute-start(bf16[1424,128]{1,0:T(8,128)(2,1)} %get-tuple-element.50.refs_1_), channel_id=1, source_target_pairs={{0,2},{1,3},{2,0},{3,1},{4,6},{5,7},{6,4},{7,5},{8,10},{9,11},{10,... | collective-permute-start | bytes 1093640 | tf_op jit(solution)/shard_map/ppermute | solution.py:249
  7.2 10.1 %collective-permute-start.4 = (bf16[592,128]{1,0:T(8,128)(2,1)}, bf16[592,128]{1,0:T(8,128)(2,1)S(1)}, u32[]{:S(2)}, u32[]{:S(2)}) collective-permute-start(bf16[592,128]{1,0:T(8,128)(2,1)} %get-tuple-element.52.refs_0_), channel_id=1, source_target_pairs={{0,8},{1,9},{2,10},{3,11},{4,12},{5,13},{6,14},{7,15},{8,0},{9,1},... | collective-permute-start | bytes 454664 | tf_op jit(solution)/shard_map/ppermute | solution.py:249
  10.8 7.8 %collective-permute-start.3 = (bf16[592,128]{1,0:T(8,128)(2,1)}, bf16[592,128]{1,0:T(8,128)(2,1)S(1)}, u32[]{:S(2)}, u32[]{:S(2)}) collective-permute-start(bf16[592,128]{1,0:T(8,128)(2,1)} %get-tuple-element.52.refs_0_), channel_id=1, source_target_pairs={{0,4},{1,5},{2,6},{3,7},{4,0},{5,1},{6,2},{7,3},{8,12},{9,13},{10,... | collective-permute-start | bytes 454664 | tf_op jit(solution)/shard_map/ppermute | solution.py:249
  12.4 5.0 %collective-permute-start.5 = (bf16[4,128,128]{2,1,0:T(8,128)(2,1)S(1)}, bf16[4,128,128]{2,1,0:T(8,128)(2,1)S(1)}, u32[]{:S(2)}, u32[]{:S(2)}) collective-permute-start(bf16[4,128,128]{2,1,0:T(8,128)(2,1)S(1)} %add_convert_fusion.3), channel_id=1, source_target_pairs={{0,16},{16,0},{1,17},{17,1},{2,18},{18,2},{3,19},{19,3},{4,20},{20... | collective-permute-start | bytes 393224 | tf_op jit(solution)/shard_map/ppermute | solution.py:249
  13.9 1.0 %copy-start = (bf16[1424,128]{1,0:T(8,128)(2,1)S(1)}, bf16[1424,128]{1,0:T(8,128)(2,1)}, u32[]{:S(2)}) copy-start(bf16[1424,128]{1,0:T(8,128)(2,1)} %get-tuple-element.50.refs_1_) | copy-start | bytes 1093636
  14.9 0.9 %copy-start.2 = (bf16[592,128]{1,0:T(8,128)(2,1)S(1)}, bf16[592,128]{1,0:T(8,128)(2,1)}, u32[]{:S(2)}) copy-start(bf16[592,128]{1,0:T(8,128)(2,1)} %get-tuple-element.52.refs_0_) | copy-start | bytes 454660
  15.8 0.7 %copy-start.3 = (f32[8,128]{1,0:T(8,128)S(1)}, f32[8,128]{1,0:T(8,128)}, u32[]{:S(2)}) copy-start(f32[8,128]{1,0:T(8,128)} %get-tuple-element.53.refs_2_) | copy-start | bytes 12292
  18.5 1.7 %collective-permute-start.7 = (bf16[1424,128]{1,0:T(8,128)(2,1)S(1)}, bf16[1424,128]{1,0:T(8,128)(2,1)S(1)}, u32[]{:S(2)}, u32[]{:S(2)}) collective-permute-start(bf16[1424,128]{1,0:T(8,128)(2,1)S(1)} %collective-permute-done.2.refs_5_.refs_2_), channel_id=1, source_target_pairs={{0,1},{1,0},{2,3},{3,2},{4,5},{5,4},{6,7},{7,6},{8,9},{9,8},{10,11... | collective-permute-start | bytes 1093640 | tf_op jit(solution)/shard_map/ppermute | solution.py:249
  18.6 9.6 %copy-start.1 = (bf16[2,512,128]{2,1,0:T(8,128)(2,1)S(1)}, bf16[2,512,128]{2,1,0:T(8,128)(2,1)}, u32[]{:S(2)}) copy-start(bf16[2,512,128]{2,1,0:T(8,128)(2,1)} %refs_4_.1) | copy-start | bytes 786436
  18.6 4.6 %collective-permute-start.6 = (bf16[2,128,128]{2,1,0:T(8,128)(2,1)S(1)}, bf16[2,128,128]{2,1,0:T(8,128)(2,1)S(1)}, u32[]{:S(2)}, u32[]{:S(2)}) collective-permute-start(bf16[2,128,128]{2,1,0:T(8,128)(2,1)S(1)} %slice.17), channel_id=1, source_target_pairs={{0,2},{1,3},{2,0},{3,1},{4,6},{5,7},{6,4},{7,5},{8,10},{9,11},{10,... | collective-permute-start | bytes 196616 | tf_op jit(solution)/shard_map/ppermute | solution.py:249
  19.1 6.1 %collective-permute-start.9 = (bf16[592,128]{1,0:T(8,128)(2,1)S(1)}, bf16[592,128]{1,0:T(8,128)(2,1)S(1)}, u32[]{:S(2)}, u32[]{:S(2)}) collective-permute-start(bf16[592,128]{1,0:T(8,128)(2,1)S(1)} %collective-permute-done.4.refs_2_.refs_10_), channel_id=1, source_target_pairs={{0,4},{1,5},{2,6},{3,7},{4,0},{5,1},{6,2},{7,3},{8,12},{9,13},{10,... | collective-permute-start | bytes 454664 | tf_op jit(solution)/shard_map/ppermute | solution.py:249
  23.2 6.6 %collective-permute-start.8 = (bf16[2,128,128]{2,1,0:T(8,128)(2,1)S(1)}, bf16[2,128,128]{2,1,0:T(8,128)(2,1)S(1)}, u32[]{:S(2)}, u32[]{:S(2)}) collective-permute-start(bf16[2,128,128]{2,1,0:T(8,128)(2,1)S(1)} %add_convert_fusion.6), channel_id=1, source_target_pairs={{0,4},{1,5},{2,6},{3,7},{4,0},{5,1},{6,2},{7,3},{8,12},{9,13},{10,... | collective-permute-start | bytes 196616 | tf_op jit(solution)/shard_map/ppermute | solution.py:249
  25.7 4.1 %collective-permute-start.10 = (f32[16,128]{1,0:T(8,128)S(1)}, f32[16,128]{1,0:T(8,128)S(1)}, u32[]{:S(2)}, u32[]{:S(2)}) collective-permute-start(f32[16,128]{1,0:T(8,128)S(1)} %get-tuple-element.73.refs_0_), channel_id=1, source_target_pairs={{0,1},{1,0},{2,3},{3,2},{4,5},{5,4},{6,7},{7,6},{8,9},{9,8},{10,11... | collective-permute-start | bytes 24584 | tf_op jit(solution)/shard_map/ppermute | solution.py:249
  25.8 4.1 %collective-permute-start.11 = (f32[16,128]{1,0:T(8,128)S(1)}, f32[16,128]{1,0:T(8,128)S(1)}, u32[]{:S(2)}, u32[]{:S(2)}) collective-permute-start(f32[16,128]{1,0:T(8,128)S(1)} %get-tuple-element.73.refs_0_), channel_id=1, source_target_pairs={{0,2},{1,3},{2,0},{3,1},{4,6},{5,7},{6,4},{7,5},{8,10},{9,11},{10,... | collective-permute-start | bytes 24584 | tf_op jit(solution)/shard_map/ppermute | solution.py:249
  28.1 3.1 %collective-permute-start.12 = (f32[16,128]{1,0:T(8,128)S(1)}, f32[16,128]{1,0:T(8,128)S(1)}, u32[]{:S(2)}, u32[]{:S(2)}) collective-permute-start(f32[16,128]{1,0:T(8,128)S(1)} %get-tuple-element.73.refs_0_), channel_id=1, source_target_pairs={{0,3},{1,2},{2,1},{3,0},{4,7},{5,6},{6,5},{7,4},{8,11},{9,10},{10,... | collective-permute-start | bytes 24584 | tf_op jit(solution)/shard_map/ppermute | solution.py:249
  32.0 7.4 %collective-permute-start.13 = (bf16[576,128]{1,0:T(8,128)(2,1)S(1)}, bf16[576,128]{1,0:T(8,128)(2,1)S(1)}, u32[]{:S(2)}, u32[]{:S(2)}) collective-permute-start(bf16[576,128]{1,0:T(8,128)(2,1)S(1)} %get-tuple-element.84), channel_id=1, source_target_pairs={{0,4},{1,5},{2,6},{3,7},{4,0},{5,1},{6,2},{7,3},{8,12},{9,13},{10,... | collective-permute-start | bytes 442376 | tf_op jit(solution)/shard_map/ppermute | solution.py:249
  32.4 5.4 %collective-permute-start.14 = (bf16[2,128,128]{2,1,0:T(8,128)(2,1)S(1)}, bf16[2,128,128]{2,1,0:T(8,128)(2,1)S(1)}, u32[]{:S(2)}, u32[]{:S(2)}) collective-permute-start(bf16[2,128,128]{2,1,0:T(8,128)(2,1)S(1)} %add_convert_fusion.5), channel_id=1, source_target_pairs={{0,8},{1,9},{2,10},{3,11},{4,12},{5,13},{6,14},{7,15},{8,0},{9,1},... | collective-permute-start | bytes 196616 | tf_op jit(solution)/shard_map/ppermute | solution.py:249
  39.4 2.0 %collective-permute-start.15 = (bf16[4,576,128]{2,1,0:T(8,128)(2,1)S(1)}, bf16[4,576,128]{2,1,0:T(8,128)(2,1)S(1)}, u32[]{:S(2)}, u32[]{:S(2)}) collective-permute-start(bf16[4,576,128]{2,1,0:T(8,128)(2,1)S(1)} %get-tuple-element.86), channel_id=1, source_target_pairs={{0,1},{1,0},{2,3},{3,2},{4,5},{5,4},{6,7},{7,6},{8,9},{9,8},{10,11... | collective-permute-start | bytes 1769480 | tf_op jit(solution)/shard_map/ppermute | solution.py:249
  39.4 14.1 %collective-permute-start.17 = (bf16[576,128]{1,0:T(8,128)(2,1)S(1)}, bf16[576,128]{1,0:T(8,128)(2,1)S(1)}, u32[]{:S(2)}, u32[]{:S(2)}) collective-permute-start(bf16[576,128]{1,0:T(8,128)(2,1)S(1)} %add_convert_fusion.1), channel_id=1, source_target_pairs={{0,8},{1,9},{2,10},{3,11},{4,12},{5,13},{6,14},{7,15},{8,0},{9,1},... | collective-permute-start | bytes 442376 | tf_op jit(solution)/shard_map/ppermute | solution.py:249
  41.5 12.8 %collective-permute-start.16 = (bf16[2,576,128]{2,1,0:T(8,128)(2,1)S(1)}, bf16[2,576,128]{2,1,0:T(8,128)(2,1)S(1)}, u32[]{:S(2)}, u32[]{:S(2)}) collective-permute-start(bf16[2,576,128]{2,1,0:T(8,128)(2,1)S(1)} %add_convert_fusion), channel_id=1, source_target_pairs={{0,2},{1,3},{2,0},{3,1},{4,6},{5,7},{6,4},{7,5},{8,10},{9,11},{10,... | collective-permute-start | bytes 884744 | tf_op jit(solution)/shard_map/ppermute | solution.py:249
  42.1 11.5 %collective-permute-start.18 = (bf16[576,128]{1,0:T(8,128)(2,1)S(1)}, bf16[576,128]{1,0:T(8,128)(2,1)S(1)}, u32[]{:S(2)}, u32[]{:S(2)}) collective-permute-start(bf16[576,128]{1,0:T(8,128)(2,1)S(1)} %get-tuple-element.91), channel_id=1, source_target_pairs={{0,4},{1,5},{2,6},{3,7},{4,0},{5,1},{6,2},{7,3},{8,12},{9,13},{10,... | collective-permute-start | bytes 442376 | tf_op jit(solution)/shard_map/ppermute | solution.py:249
  43.8 1.3 %collective-permute-start.19 = (bf16[2,128,128]{2,1,0:T(8,128)(2,1)S(1)}, bf16[2,128,128]{2,1,0:T(8,128)(2,1)S(1)}, u32[]{:S(2)}, u32[]{:S(2)}) collective-permute-start(bf16[2,128,128]{2,1,0:T(8,128)(2,1)S(1)} %add_convert_fusion.4.refs_0_), channel_id=1, source_target_pairs={{0,1},{1,0},{2,3},{3,2},{4,5},{5,4},{6,7},{7,6},{8,9},{9,8},{10,11... | collective-permute-start | bytes 196616 | tf_op jit(solution)/shard_map/ppermute | solution.py:249
  43.9 8.8 %collective-permute-start.20 = (bf16[2,128,128]{2,1,0:T(8,128)(2,1)S(1)}, bf16[2,128,128]{2,1,0:T(8,128)(2,1)S(1)}, u32[]{:S(2)}, u32[]{:S(2)}) collective-permute-start(bf16[2,128,128]{2,1,0:T(8,128)(2,1)S(1)} %add_convert_fusion.4.refs_0_), channel_id=1, source_target_pairs={{0,2},{1,3},{2,0},{3,1},{4,6},{5,7},{6,4},{7,5},{8,10},{9,11},{10,... | collective-permute-start | bytes 196616 | tf_op jit(solution)/shard_map/ppermute | solution.py:249
  45.1 7.6 %collective-permute-start.21 = (bf16[2,128,128]{2,1,0:T(8,128)(2,1)S(1)}, bf16[2,128,128]{2,1,0:T(8,128)(2,1)S(1)}, u32[]{:S(2)}, u32[]{:S(2)}) collective-permute-start(bf16[2,128,128]{2,1,0:T(8,128)(2,1)S(1)} %add_convert_fusion.4.refs_0_), channel_id=1, source_target_pairs={{0,3},{1,2},{2,1},{3,0},{4,7},{5,6},{6,5},{7,4},{8,11},{9,10},{10,... | collective-permute-start | bytes 196616 | tf_op jit(solution)/shard_map/ppermute | solution.py:249

commit v8 on v7

--- a/solution.py
+++ b/solution.py
@@ -29,7 +29,7 @@
     return math.prod(shape) * jnp.dtype(dtype).itemsize
 
 
-def call(kernel, name, outs, args, scratch=(), flops=0, smem=(), hbm=(), copies=0, limit=None, share=1):
+def call(kernel, name, outs, args, scratch=(), flops=0, smem=(), hbm=(), copies=0, limit=None, share=1, out=pltpu.VMEM):
     def place(i):
         return pltpu.SMEM if i in smem else pltpu.HBM if i in hbm else pltpu.VMEM
 
@@ -40,7 +40,7 @@
         kernel,
         out_shape=[jax.ShapeDtypeStruct(s, d) for s, d in outs],
         in_specs=[pl.BlockSpec(memory_space=place(i)) for i in range(len(args))],
-        out_specs=[pl.BlockSpec(memory_space=pltpu.VMEM) for _ in outs],
+        out_specs=[pl.BlockSpec(memory_space=out) for _ in outs],
         scratch_shapes=[pltpu.VMEM(s, d) for s, d in scratch] + semaphores,
         compiler_params=pltpu.CompilerParams(vmem_limit_bytes=limit or int(1.2 * held) + (8 << 20)),
         cost_estimate=pl.CostEstimate(flops=flops * share, bytes_accessed=moved * share, transcendentals=0),
@@ -57,43 +57,56 @@
 
 def pack_kernel(
     idx_ref, pos_hbm, q_hbm, og_hbm, lat_hbm, attn_hbm, wuv_hbm,
-    lat_msg, q_msg, delta_ref, keep_ref, send_ref,
-    pos_ref, og_ref, attn_ref, wuv_ref, term, sems,
+    lat_msg, q_msg, delta_hbm, keep_hbm, send_hbm,
+    pos_ref, og_ref, attn_ref, wuv_ref, term, rows_ref, og_t_ref, delta_ref, keep_ref, send_ref, sems,
 ):
     heads, width, tok = q_hbm.shape
-    pairs = [(pos_hbm, pos_ref), (og_hbm, og_ref), (wuv_hbm, wuv_ref), (attn_hbm, attn_ref)]
-    pairs += [(lat_hbm, lat_msg.at[pl.ds(0, width), :])]
-    pairs += [(q_hbm.at[h], q_msg.at[pl.ds(h * width, width), :]) for h in range(heads)]
-    copies = [pltpu.make_async_copy(src, dst, sems.at[i]) for i, (src, dst) in enumerate(pairs)]
-    for copy in copies:
+    _, lat, _ = wuv_ref.shape
+    started = []
+
+    def send_off(src, dst):
+        copy = pltpu.make_async_copy(src, dst, sems.at[len(started)])
         copy.start()
-    copies[0].wait()
+        started.append(copy)
+
+    send_off(og_hbm, og_ref)
+    send_off(pos_hbm, pos_ref)
+    send_off(attn_hbm, attn_ref)
+    send_off(wuv_hbm, wuv_ref)
+    send_off(lat_hbm, lat_msg.at[pl.ds(0, width), :])
+    for h in range(heads):
+        send_off(q_hbm.at[h], q_msg.at[pl.ds(h * width, width), :])
+    started[0].wait()
+    for h in range(heads):
+        og_t_ref[h] = og_ref[:, h, :].T
+        send_off(og_t_ref.at[h], q_msg.at[pl.ds(heads * width + h * HEAD_DIM, HEAD_DIM), :])
+    started[1].wait()
     pos = jnp.broadcast_to(pos_ref[...], (EXTRA, tok))
     row = lax.broadcasted_iota(jnp.int32, (EXTRA, tok), 0)
     high = lax.shift_right_logical(pos, 6)
     both = jnp.where(row == 0, high, jnp.where(row == 1, pos - high * 64, 0))
-    rows = both.astype(F32).astype(BF16)
-    lat_msg[width:, :] = rows
-    q_msg[heads * (width + HEAD_DIM) :, :] = rows
+    rows_ref[...] = both.astype(F32).astype(BF16)
+    send_off(rows_ref, lat_msg.at[pl.ds(width, EXTRA), :])
+    send_off(rows_ref, q_msg.at[pl.ds(heads * (width + HEAD_DIM), EXTRA), :])
     delta_ref[...] = jnp.zeros_like(delta_ref)
-    for copy in copies[1:4]:
-        copy.wait()
-    _, lat, _ = wuv_ref.shape
+    started[2].wait()
+    attn = [attn_ref[:, h, :].T for h in range(heads)]
     for h in range(heads):
-        og = og_ref[:, h, :].T
-        at = heads * width + h * HEAD_DIM
-        q_msg[at : at + HEAD_DIM, :] = og
-        attn = attn_ref[:, h, :].T
-        g = mm(wuv_ref[h], og).astype(BF16).astype(F32)
-        delta_ref[h : h + 1, :] = jnp.sum(g * attn.astype(F32), axis=0, keepdims=True)
-        term[h] = mm_t(attn, og)
+        term[h] = mm_t(attn[h], og_t_ref[h])
     step = lat // GROUP
     me = lax.rem(idx_ref[0], GROUP)
     for k in range(GROUP):
         at = pl.multiple_of(jnp.bitwise_xor(me, k) * step, step)
         target = send_ref if k % 2 else keep_ref
         target[k // 2 * heads : (k // 2 + 1) * heads] = term[:, pl.ds(at, step), :].astype(BF16)
-    for copy in copies[4:]:
+    send_off(send_ref, send_hbm)
+    send_off(keep_ref, keep_hbm)
+    started[3].wait()
+    for h in range(heads):
+        g = mm(wuv_ref[h], og_t_ref[h]).astype(BF16).astype(F32)
+        delta_ref[h : h + 1, :] = jnp.sum(g * attn[h].astype(F32), axis=0, keepdims=True)
+    send_off(delta_ref, delta_hbm)
+    for copy in started[4:]:
         copy.wait()
 
 
@@ -278,10 +291,16 @@
             (attn_out.shape[1:], BF16),
             (wuv.shape, BF16),
             ((heads, lat, HEAD_DIM), F32),
+            ((EXTRA, tok), BF16),
+            ((heads, HEAD_DIM, tok), BF16),
+            ((8, tok), F32),
+            ((2 * heads, step, HEAD_DIM), BF16),
+            ((2 * heads, step, HEAD_DIM), BF16),
         ],
         smem=(0,),
         hbm=(1, 2, 3, 4, 5, 6),
-        copies=5 + heads,
+        copies=10 + 2 * heads,
+        out=pltpu.HBM,
         limit=PACK_LIMIT,
     )
 
@@ -295,7 +314,7 @@
     q_core = swap(q_msg, 1)
     pair = add(keep, swap(send, 1))
     got_pair = swap(pair, *dp_hops[0])
-    firsts = [swap(after(lat_msg, pair) if bit + 1 < line_bits else lat_msg, GROUP << bit) for bit in range(line_bits)]
+    firsts = [swap(after(lat_msg, q_core) if bit + 1 < line_bits else lat_msg, GROUP << bit) for bit in range(line_bits)]
     own = call(
         hold_kernel,
         "hold_own",
@@ -364,33 +383,36 @@
         flops=2 * tok * all_rows * (width + lat),
     )
     last_got = swap(last_part, GROUP)
+    mine = add(mine, near)
     outs = call(
         functools.partial(grad_kernel, factor, most, width, heads, False),
         "near_gradients",
         [((width, tok), BF16)] * most
         + [((heads, width, tok), BF16), ((2 * heads, width, tok), BF16), ((heads, width, tok), BF16)],
-        stats + [near_s, near_gp, g, q_all] + lats + [last_gs],
+        stats + [near_s, near_gp, g, q_all] + lats + [after(last_gs, mine)],
         [((width, lines * tok), BF16), ((keys, all_rows), BF16), ((keys, all_rows), BF16)],
         flops=2 * keys * all_rows * (width + lat) + 2 * lines * tok * all_rows * width,
     )
     parts, (gq_own, gq_core, gq_across) = list(outs[:most]) + [last_part], outs[most:]
-    mine = add(mine, near)
+    across = swap(mine, 2)
     kept = [parts[0]]
-    gq_got = swap(after(gq_core, last_got, near), 1)
+    gq_got = swap(after(gq_core, last_got, across), 1)
     gq_sum = add(gq_across, gq_got[heads:])
     gq_last = swap(gq_sum, 2)
     for bit in range(line_bits):
         for m in range(3 << bit, lines, 2 << bit):
             got = last_got if m == most and bit == 0 else swap(parts[m], GROUP << bit)
             parts[m ^ 1 << bit] = add(parts[m ^ 1 << bit], got)
-    pieces = [mine] + [swap(mine, k) for k in range(1, GROUP)]
+    mine_two = jnp.concatenate([mine, across], axis=0)
+    other_two = swap(mine_two, 1)
+    pieces = [mine_two[:heads], other_two[:heads], mine_two[heads:], other_two[heads:]]
     parts[1] = after(parts[1], gq_sum)
     kept += [swap(parts[1 << bit], GROUP << bit) for bit in reversed(range(line_bits))]
     scale = 1.0 / math.sqrt(tok * n_ctx * n_dp)
     (grad_w,) = call(
         functools.partial(spread_kernel, scale), "spread", [((heads, lat, HEAD_DIM), F32)], [idx] + pieces, smem=(0,)
     )
-    (grad_lat,) = call(sum_kernel, "latent_sum", [((width, tok), BF16)], kept)
+    (grad_lat,) = call(sum_kernel, "latent_sum", [((width, tok), BF16)], kept, flops=3*10**9)
     gq_pieces = [gq_own, gq_got[:heads], after(gq_last, grad_lat)]
     (grad_q,) = call(sum_kernel, "query_sum", [((heads, width, tok), BF16)], gq_pieces)
     return (jnp.transpose(grad_q, (2, 0, 1))[None], grad_lat.T[None], grad_w)

time: 55.4 us -> 66.2 us (1.19)
  Pallas kernels: 12.5 us -> 24.1 us
  waiting for transfers between devices: 17.3 us -> 14.3 us
  starting transfers between devices: 20.7 us -> 22.9 us
    pallas_call x10, Pallas kernels: 12.5 us -> 24.1 us  [call(): pl.pallas_call(kernel, out_shape=[jax.ShapeDtypeStruct(s, d) for s, d in...]
    ppermute x22 -> x21, waiting for transfers between devices: 17.3 us -> 14.3 us  [swap(): return lax.ppermute(x, axis, [(i, i ^ mask) for i in range(size)])]
    ppermute x22 -> x21, starting transfers between devices: 20.7 us -> 22.9 us  [swap(): return lax.ppermute(x, axis, [(i, i ^ mask) for i in range(size)])]
  transfers between devices with their start and end apart: 22 -> 21, of which waited for: 11 -> 10; matrix products, arithmetic and copies ran while one was open for 2% -> 2% of each run, Pallas kernels for 14% -> 13%
where the time goes in v8:
time: 66.2 us; the launch traced here: 65.9 us
  Pallas kernels  24.1 us (36%)
  starting transfers between devices  22.9 us (35%)
  waiting for transfers between devices  14.3 us (22%)
  local copies, waits for them, and re-layouts  2.62 us (4%)
  other arithmetic  1.18 us (2%)
  between operations  0.78 us (1%)
    pallas_call x10, Pallas kernels, call(): pl.pallas_call(kernel, out_shape=[jax.ShapeDtypeStruct(s, d) for s, d in...  24.1 us
    ppermute x21, starting transfers between devices, swap(): return lax.ppermute(x, axis, [(i, i ^ mask) for i in range(size)])  22.9 us
    ppermute x21, waiting for transfers between devices, swap(): return lax.ppermute(x, axis, [(i, i ^ mask) for i in range(size)])  14.3 us
    unnamed x8, local copies, waits for them, and re-layouts  2.58 us
  transfers between devices with their start and end apart: 21, of which 10 were waited for; matrix products, arithmetic and copies ran while one was open for 2% of the time, Pallas kernels for 13%

profile of v8, /device:TPU:0, one launch (start us, length us, event | category | flops | bytes accessed | tf_op | source)
XLA Modules:
  0.0 65.9 jit_solution(15739822726349936576)
XLA Ops:
  0.6 14.6 %pack.1 = (bf16[592,128]{1,0:T(8,128)(2,1)}, bf16[1424,128]{1,0:T(8,128)(2,1)}, f32[8,128]{1,0:T(8,128)}, bf16[4,128,128]{2,1,0:T(8,128)(2,1)}, bf16[4,128,128]{2,1,0:T(8,128)(2,1)}) custom-call(s32[1]{0:T(128)} %bitcast.idx_ref, s32[1,128]{1,0:T(1,128)} %pos_hbm.1, bf16[2,576,128]{2,1,0:T(8,128)(2,1)} %bitcast.15, bf16[128,2,128]{2,1,0:T(2,128)(2,1)} %bitcast.19, ...), custom_call_target="tpu_custom_call" | custom-call | bytes 1815044 | tf_op jit(solution)/shard_map/pack/pallas_call | solution.py:39
  15.3 0.5 collective-permute-start.1
  15.8 0.1 collective-permute-start
  15.9 2.9 %collective-permute-start.2 = (bf16[1424,128]{1,0:T(8,128)(2,1)}, bf16[1424,128]{1,0:T(8,128)(2,1)S(1)}, u32[]{:S(2)}, u32[]{:S(2)}) collective-permute-start(bf16[1424,128]{1,0:T(8,128)(2,1)} %get-tuple-element.51.refs_1_), channel_id=1, source_target_pairs={{0,2},{1,3},{2,0},{3,1},{4,6},{5,7},{6,4},{7,5},{8,10},{9,11},{10,... | collective-permute-start | bytes 1093640 | tf_op jit(solution)/shard_map/ppermute | solution.py:262
  18.8 2.6 %collective-permute-start.4 = (bf16[592,128]{1,0:T(8,128)(2,1)}, bf16[592,128]{1,0:T(8,128)(2,1)S(1)}, u32[]{:S(2)}, u32[]{:S(2)}) collective-permute-start(bf16[592,128]{1,0:T(8,128)(2,1)} %get-tuple-element.53.refs_0_), channel_id=1, source_target_pairs={{0,8},{1,9},{2,10},{3,11},{4,12},{5,13},{6,14},{7,15},{8,0},{9,1},... | collective-permute-start | bytes 454664 | tf_op jit(solution)/shard_map/ppermute | solution.py:262
  21.4 0.0 collective-permute-done.1.refs_4_.refs_1_
  21.4 1.6 %collective-permute-start.3 = (bf16[592,128]{1,0:T(8,128)(2,1)}, bf16[592,128]{1,0:T(8,128)(2,1)S(1)}, u32[]{:S(2)}, u32[]{:S(2)}) collective-permute-start(bf16[592,128]{1,0:T(8,128)(2,1)} %get-tuple-element.53.refs_0_), channel_id=1, source_target_pairs={{0,4},{1,5},{2,6},{3,7},{4,0},{5,1},{6,2},{7,3},{8,12},{9,13},{10,... | collective-permute-start | bytes 454664 | tf_op jit(solution)/shard_map/ppermute | solution.py:262
  23.0 0.0 collective-permute-done
  23.0 0.9 %add_convert_fusion.3 = bf16[4,128,128]{2,1,0:T(8,128)(2,1)S(1)} fusion(bf16[4,128,128]{2,1,0:T(8,128)(2,1)S(1)} %collective-permute-done, bf16[4,128,128]{2,1,0:T(8,128)(2,1)} %get-tuple-element.49), kind=kLoop, calls=%fused_computation.3 | loop fusion | flops 262144 | bytes 393216 | tf_op jit(solution)/shard_map/convert_element_type | solution.py:308
  23.9 1.6 %collective-permute-start.5 = (bf16[4,128,128]{2,1,0:T(8,128)(2,1)S(1)}, bf16[4,128,128]{2,1,0:T(8,128)(2,1)S(1)}, u32[]{:S(2)}, u32[]{:S(2)}) collective-permute-start(bf16[4,128,128]{2,1,0:T(8,128)(2,1)S(1)} %add_convert_fusion.3), channel_id=1, source_target_pairs={{0,16},{16,0},{1,17},{17,1},{2,18},{18,2},{3,19},{19,3},{4,20},{20... | collective-permute-start | bytes 393224 | tf_op jit(solution)/shard_map/ppermute | solution.py:262
  25.5 0.0 copy-start
  25.5 1.0 %copy-done = bf16[1424,128]{1,0:T(8,128)(2,1)S(1)} copy-done((bf16[1424,128]{1,0:T(8,128)(2,1)S(1)}, bf16[1424,128]{1,0:T(8,128)(2,1)}, u32[]{:S(2)}) %copy-start) | copy-done | bytes 364568
  26.5 0.0 copy-start.2
  26.5 0.9 %copy-done.2 = bf16[592,128]{1,0:T(8,128)(2,1)S(1)} copy-done((bf16[592,128]{1,0:T(8,128)(2,1)S(1)}, bf16[592,128]{1,0:T(8,128)(2,1)}, u32[]{:S(2)}) %copy-start.2) | copy-done | bytes 151576
  27.4 0.0 copy-start.3
  27.4 0.7 %copy-done.3 = f32[8,128]{1,0:T(8,128)S(1)} copy-done((f32[8,128]{1,0:T(8,128)S(1)}, f32[8,128]{1,0:T(8,128)}, u32[]{:S(2)}) %copy-start.3) | copy-done | bytes 4120
  28.1 0.8 %collective-permute-done.4.refs_2_.refs_10_ = bf16[592,128]{1,0:T(8,128)(2,1)S(1)} collective-permute-done((bf16[592,128]{1,0:T(8,128)(2,1)}, bf16[592,128]{1,0:T(8,128)(2,1)S(1)}, u32[]{:S(2)}, u32[]{:S(2)}) %collective-permute-start.4) | collective-permute-done | bytes 151584 | tf_op jit(solution)/shard_map/ppermute | solution.py:262
  28.9 0.0 collective-permute-done.5
  29.0 0.0 collective-permute-done.2.refs_5_.refs_2_
  29.0 0.1 collective-permute-done.3.refs_1_.refs_9_
  29.1 0.0 collective-permute-start.7
  29.2 0.0 copy-start.1
  29.2 0.5 collective-permute-start.6
  29.7 1.5 %collective-permute-start.9 = (bf16[592,128]{1,0:T(8,128)(2,1)S(1)}, bf16[592,128]{1,0:T(8,128)(2,1)S(1)}, u32[]{:S(2)}, u32[]{:S(2)}) collective-permute-start(bf16[592,128]{1,0:T(8,128)(2,1)S(1)} %collective-permute-done.4.refs_2_.refs_10_), channel_id=1, source_target_pairs={{0,4},{1,5},{2,6},{3,7},{4,0},{5,1},{6,2},{7,3},{8,12},{9,13},{10,... | collective-permute-start | bytes 454664 | tf_op jit(solution)/shard_map/ppermute | solution.py:262
  31.2 0.0 collective-permute-done.7.refs_6_.refs_3_
  31.2 1.2 %near_scores.1 = (f32[384,1024]{1,0:T(8,128)S(1)}, bf16[384,640]{1,0:T(8,128)(2,1)S(1)}, f32[16,128]{1,0:T(8,128)S(1)}, bf16[640,1024]{1,0:T(8,128)(2,1)S(1)}) custom-call(bf16[592,128]{1,0:T(8,128)(2,1)S(1)} %get-tuple-element.59.refs_0_.refs_8_, bf16[592,128]{1,0:T(8,128)(2,1)S(1)} %collective-permute-done.3.refs_1_.refs_9_, ...), custom_call_target="tpu_custom_call" | custom-call | tf_op jit(solution)/shard_map/near_scores/pallas_call | solution.py:39
  32.5 1.3 %collective-permute-done.6 = bf16[2,128,128]{2,1,0:T(8,128)(2,1)S(1)} collective-permute-done((bf16[2,128,128]{2,1,0:T(8,128)(2,1)S(1)}, bf16[2,128,128]{2,1,0:T(8,128)(2,1)S(1)}, u32[]{:S(2)}, u32[]{:S(2)}) %collective-permute-start.6) | collective-permute-done | bytes 65568 | tf_op jit(solution)/shard_map/ppermute | solution.py:262
  33.8 1.5 %collective-permute-start.8 = (bf16[2,128,128]{2,1,0:T(8,128)(2,1)S(1)}, bf16[2,128,128]{2,1,0:T(8,128)(2,1)S(1)}, u32[]{:S(2)}, u32[]{:S(2)}) collective-permute-start(bf16[2,128,128]{2,1,0:T(8,128)(2,1)S(1)} %add_convert_fusion.6), channel_id=1, source_target_pairs={{0,4},{1,5},{2,6},{3,7},{4,0},{5,1},{6,2},{7,3},{8,12},{9,13},{10,... | collective-permute-start | bytes 196616 | tf_op jit(solution)/shard_map/ppermute | solution.py:262
  35.3 0.5 collective-permute-done.9.refs_0_.refs_11_
  35.8 0.5 last_scores.1
  36.3 0.1 collective-permute-start.10
  36.4 2.3 %collective-permute-start.11 = (f32[16,128]{1,0:T(8,128)S(1)}, f32[16,128]{1,0:T(8,128)S(1)}, u32[]{:S(2)}, u32[]{:S(2)}) collective-permute-start(f32[16,128]{1,0:T(8,128)S(1)} %get-tuple-element.74.refs_0_), channel_id=1, source_target_pairs={{0,2},{1,3},{2,0},{3,1},{4,6},{5,7},{6,4},{7,5},{8,10},{9,11},{10,... | collective-permute-start | bytes 24584 | tf_op jit(solution)/shard_map/ppermute | solution.py:262
  38.7 0.1 collective-permute-start.12
  38.8 0.0 copy-done.1
  38.8 1.6 %context.1 = (bf16[512,1024]{1,0:T(8,128)(2,1)S(1)}, f32[384,1024]{1,0:T(8,128)S(1)}, f32[128,1024]{1,0:T(8,128)S(1)}) custom-call(bf16[1424,128]{1,0:T(8,128)(2,1)S(1)} %get-tuple-element.62.refs_3_.refs_0_, bf16[1424,128]{1,0:T(8,128)(2,1)S(1)} %collective-permute-done.1.refs_4_.refs_1_, bf16[1424,128]{1,0:T(8,128)(2,1)S(1)} %collective-permute-done.2.refs_5_.refs_2_, ...), custom_call_target="tpu_custom_call" | custom-call | flops 671088640 | bytes 5521408 | tf_op jit(solution)/shard_map/context/pallas_call | solution.py:39
  40.4 0.0 collective-permute-done.8
  40.4 0.0 collective-permute-done.10.refs_1_
  40.4 0.0 collective-permute-done.11.refs_2_
  40.4 1.4 %collective-permute-done.12.refs_3_ = f32[16,128]{1,0:T(8,128)S(1)} collective-permute-done((f32[16,128]{1,0:T(8,128)S(1)}, f32[16,128]{1,0:T(8,128)S(1)}, u32[]{:S(2)}, u32[]{:S(2)}) %collective-permute-start.12) | collective-permute-done | bytes 8224 | tf_op jit(solution)/shard_map/ppermute | solution.py:262
  41.8 1.7 %collective-permute-start.13 = (bf16[2,128,128]{2,1,0:T(8,128)(2,1)S(1)}, bf16[2,128,128]{2,1,0:T(8,128)(2,1)S(1)}, u32[]{:S(2)}, u32[]{:S(2)}) collective-permute-start(bf16[2,128,128]{2,1,0:T(8,128)(2,1)S(1)} %add_convert_fusion.5), channel_id=1, source_target_pairs={{0,8},{1,9},{2,10},{3,11},{4,12},{5,13},{6,14},{7,15},{8,0},{9,1},... | collective-permute-start | bytes 196616 | tf_op jit(solution)/shard_map/ppermute | solution.py:262
  43.5 0.8 %last_gradients.1 = (bf16[576,128]{1,0:T(8,128)(2,1)S(1)}, bf16[128,1024]{1,0:T(8,128)(2,1)S(1)}) custom-call(f32[16,128]{1,0:T(8,128)S(1)} %get-tuple-element.74.refs_0_, f32[16,128]{1,0:T(8,128)S(1)} %collective-permute-done.10.refs_1_, f32[16,128]{1,0:T(8,128)S(1)} %collective-permute-done.11.refs_2_, f32[16,128]{1,0:T(8,128)S(1)} %collective-permute-done.12.refs_3_, ...), custom_call_target="tpu_custom_call" | custom-call | flops 285212672 | bytes 3850240 | tf_op jit(solution)/shard_map/last_gradients/pallas_call | solution.py:39
  44.3 1.9 %collective-permute-start.14 = (bf16[576,128]{1,0:T(8,128)(2,1)S(1)}, bf16[576,128]{1,0:T(8,128)(2,1)S(1)}, u32[]{:S(2)}, u32[]{:S(2)}) collective-permute-start(bf16[576,128]{1,0:T(8,128)(2,1)S(1)} %get-tuple-element.87), channel_id=1, source_target_pairs={{0,4},{1,5},{2,6},{3,7},{4,0},{5,1},{6,2},{7,3},{8,12},{9,13},{10,... | collective-permute-start | bytes 442376 | tf_op jit(solution)/shard_map/ppermute | solution.py:262
  46.2 2.2 %collective-permute-done.13 = bf16[2,128,128]{2,1,0:T(8,128)(2,1)S(1)} collective-permute-done((bf16[2,128,128]{2,1,0:T(8,128)(2,1)S(1)}, bf16[2,128,128]{2,1,0:T(8,128)(2,1)S(1)}, u32[]{:S(2)}, u32[]{:S(2)}) %collective-permute-start.13) | collective-permute-done | bytes 65568 | tf_op jit(solution)/shard_map/ppermute | solution.py:262
  48.4 0.6 collective-permute-start.15
  49.1 2.9 %near_gradients.1 = (bf16[576,128]{1,0:T(8,128)(2,1)S(1)}, bf16[576,128]{1,0:T(8,128)(2,1)S(1)}, bf16[576,128]{1,0:T(8,128)(2,1)S(1)}, bf16[2,576,128]{2,1,0:T(8...) custom-call(f32[16,128]{1,0:T(8,128)S(1)} %get-tuple-element.74.refs_0_, ...), custom_call_target="tpu_custom_call" | custom-call | flops 1459617792 | bytes 8028160 | tf_op jit(solution)/shard_map/near_gradients/pallas_call | solution.py:39
  52.0 0.8 %collective-permute-done.15.refs_2_ = bf16[2,128,128]{2,1,0:T(8,128)(2,1)S(1)} collective-permute-done((bf16[2,128,128]{2,1,0:T(8,128)(2,1)S(1)}, bf16[2,128,128]{2,1,0:T(8,128)(2,1)S(1)}, u32[]{:S(2)}, u32[]{:S(2)}) %collective-permute-start.15) | collective-permute-done | bytes 65568 | tf_op jit(solution)/shard_map/ppermute | solution.py:262
  52.8 0.0 collective-permute-done.14
  52.8 0.0 collective-permute-start.16
  52.8 0.6 collective-permute-start.20
  53.4 0.3 collective-permute-start.18
  53.7 1.1 %collective-permute-done.16 = bf16[4,576,128]{2,1,0:T(8,128)(2,1)S(1)} collective-permute-done((bf16[4,576,128]{2,1,0:T(8,128)(2,1)S(1)}, bf16[4,576,128]{2,1,0:T(8,128)(2,1)S(1)}, u32[]{:S(2)}, u32[]{:S(2)}) %collective-permute-start.16) | collective-permute-done | bytes 589856 | tf_op jit(solution)/shard_map/ppermute | solution.py:262
  54.8 0.1 add_convert_fusion
  54.9 0.8 %collective-permute-start.17 = (bf16[2,576,128]{2,1,0:T(8,128)(2,1)S(1)}, bf16[2,576,128]{2,1,0:T(8,128)(2,1)S(1)}, u32[]{:S(2)}, u32[]{:S(2)}) collective-permute-start(bf16[2,576,128]{2,1,0:T(8,128)(2,1)S(1)} %add_convert_fusion), channel_id=1, source_target_pairs={{0,2},{1,3},{2,0},{3,1},{4,6},{5,7},{6,4},{7,5},{8,10},{9,11},{10,... | collective-permute-start | bytes 884744 | tf_op jit(solution)/shard_map/ppermute | solution.py:262
  55.7 1.8 %collective-permute-start.19 = (bf16[576,128]{1,0:T(8,128)(2,1)S(1)}, bf16[576,128]{1,0:T(8,128)(2,1)S(1)}, u32[]{:S(2)}, u32[]{:S(2)}) collective-permute-start(bf16[576,128]{1,0:T(8,128)(2,1)S(1)} %get-tuple-element.93), channel_id=1, source_target_pairs={{0,4},{1,5},{2,6},{3,7},{4,0},{5,1},{6,2},{7,3},{8,12},{9,13},{10,... | collective-permute-start | bytes 442376 | tf_op jit(solution)/shard_map/ppermute | solution.py:262
  57.5 0.0 collective-permute-done.20
  57.5 0.8 %spread.1 = f32[2,512,128]{2,1,0:T(8,128)} custom-call(s32[1]{0:T(128)} %bitcast.idx_ref, bf16[2,128,128]{2,1,0:T(8,128)(2,1)S(1)} %add_convert_fusion.4.refs_0_, bf16[2,128,128]{2,1,0:T(8,128)(2,1)S(1)} %get-tuple-element.96.refs_1_, bf16[2,128,128]{2,1,0:T(8,128)(2,1)S(1)} %collective-permute-done.15.refs_2_, ...), custom_call_target="tpu_custom_call" | custom-call | bytes 786436 | tf_op jit(solution)/shard_map/spread/pallas_call | solution.py:39
  58.4 4.9 %collective-permute-done.18.refs_1_ = bf16[576,128]{1,0:T(8,128)(2,1)S(1)} collective-permute-done((bf16[576,128]{1,0:T(8,128)(2,1)S(1)}, bf16[576,128]{1,0:T(8,128)(2,1)S(1)}, u32[]{:S(2)}, u32[]{:S(2)}) %collective-permute-start.18) | collective-permute-done | bytes 147488 | tf_op jit(solution)/shard_map/ppermute | solution.py:262
  63.3 1.1 %collective-permute-done.19.refs_2_ = bf16[576,128]{1,0:T(8,128)(2,1)S(1)} collective-permute-done((bf16[576,128]{1,0:T(8,128)(2,1)S(1)}, bf16[576,128]{1,0:T(8,128)(2,1)S(1)}, u32[]{:S(2)}, u32[]{:S(2)}) %collective-permute-start.19) | collective-permute-done | bytes 147488 | tf_op jit(solution)/shard_map/ppermute | solution.py:262
  64.4 0.7 %latent_sum.1 = bf16[576,128]{1,0:T(8,128)(2,1)} custom-call(bf16[576,128]{1,0:T(8,128)(2,1)S(1)} %get-tuple-element.90.refs_0_, bf16[576,128]{1,0:T(8,128)(2,1)S(1)} %collective-permute-done.18.refs_1_, bf16[576,128]{1,0:T(8,128)(2,1)S(1)} %collective-permute-done.19.refs_2_), custom_call_target="tpu_custom_call" | custom-call | flops 3000000000 | bytes 589824 | tf_op jit(solution)/shard_map/latent_sum/pallas_call | solution.py:39
  65.1 0.0 collective-permute-done.17.refs_2_
  65.1 0.8 %query_sum.1 = bf16[2,576,128]{2,1,0:T(8,128)(2,1)} custom-call(bf16[2,576,128]{2,1,0:T(8,128)(2,1)S(1)} %get-tuple-element.85.refs_0_, bf16[2,576,128]{2,1,0:T(8,128)(2,1)S(1)} %slice.26.refs_1_, bf16[2,576,128]{2,1,0:T(8,128)(2,1)S(1)} %collective-permute-done.17.refs_2_), custom_call_target="tpu_custom_call" | custom-call | bytes 1179648 | tf_op jit(solution)/shard_map/query_sum/pallas_call | solution.py:39
  (10 shorter events, 0.2 us)
Async XLA Ops:
  15.3 6.1 %collective-permute-start.1 = (bf16[1424,128]{1,0:T(8,128)(2,1)}, bf16[1424,128]{1,0:T(8,128)(2,1)S(1)}, u32[]{:S(2)}, u32[]{:S(2)}) collective-permute-start(bf16[1424,128]{1,0:T(8,128)(2,1)} %get-tuple-element.51.refs_1_), channel_id=1, source_target_pairs={{0,1},{1,0},{2,3},{3,2},{4,5},{5,4},{6,7},{7,6},{8,9},{9,8},{10,11... | collective-permute-start | bytes 1093640 | tf_op jit(solution)/shard_map/ppermute | solution.py:262
  15.8 7.2 %collective-permute-start = (bf16[4,128,128]{2,1,0:T(8,128)(2,1)}, bf16[4,128,128]{2,1,0:T(8,128)(2,1)S(1)}, u32[]{:S(2)}, u32[]{:S(2)}) collective-permute-start(bf16[4,128,128]{2,1,0:T(8,128)(2,1)} %get-tuple-element.50), channel_id=1, source_target_pairs={{0,1},{1,0},{2,3},{3,2},{4,5},{5,4},{6,7},{7,6},{8,9},{9,8},{10,11... | collective-permute-start | bytes 393224 | tf_op jit(solution)/shard_map/ppermute | solution.py:262
  15.9 13.1 %collective-permute-start.2 = (bf16[1424,128]{1,0:T(8,128)(2,1)}, bf16[1424,128]{1,0:T(8,128)(2,1)S(1)}, u32[]{:S(2)}, u32[]{:S(2)}) collective-permute-start(bf16[1424,128]{1,0:T(8,128)(2,1)} %get-tuple-element.51.refs_1_), channel_id=1, source_target_pairs={{0,2},{1,3},{2,0},{3,1},{4,6},{5,7},{6,4},{7,5},{8,10},{9,11},{10,... | collective-permute-start | bytes 1093640 | tf_op jit(solution)/shard_map/ppermute | solution.py:262
  18.8 10.1 %collective-permute-start.4 = (bf16[592,128]{1,0:T(8,128)(2,1)}, bf16[592,128]{1,0:T(8,128)(2,1)S(1)}, u32[]{:S(2)}, u32[]{:S(2)}) collective-permute-start(bf16[592,128]{1,0:T(8,128)(2,1)} %get-tuple-element.53.refs_0_), channel_id=1, source_target_pairs={{0,8},{1,9},{2,10},{3,11},{4,12},{5,13},{6,14},{7,15},{8,0},{9,1},... | collective-permute-start | bytes 454664 | tf_op jit(solution)/shard_map/ppermute | solution.py:262
  21.4 7.7 %collective-permute-start.3 = (bf16[592,128]{1,0:T(8,128)(2,1)}, bf16[592,128]{1,0:T(8,128)(2,1)S(1)}, u32[]{:S(2)}, u32[]{:S(2)}) collective-permute-start(bf16[592,128]{1,0:T(8,128)(2,1)} %get-tuple-element.53.refs_0_), channel_id=1, source_target_pairs={{0,4},{1,5},{2,6},{3,7},{4,0},{5,1},{6,2},{7,3},{8,12},{9,13},{10,... | collective-permute-start | bytes 454664 | tf_op jit(solution)/shard_map/ppermute | solution.py:262
  23.9 5.0 %collective-permute-start.5 = (bf16[4,128,128]{2,1,0:T(8,128)(2,1)S(1)}, bf16[4,128,128]{2,1,0:T(8,128)(2,1)S(1)}, u32[]{:S(2)}, u32[]{:S(2)}) collective-permute-start(bf16[4,128,128]{2,1,0:T(8,128)(2,1)S(1)} %add_convert_fusion.3), channel_id=1, source_target_pairs={{0,16},{16,0},{1,17},{17,1},{2,18},{18,2},{3,19},{19,3},{4,20},{20... | collective-permute-start | bytes 393224 | tf_op jit(solution)/shard_map/ppermute | solution.py:262
  25.5 1.0 %copy-start = (bf16[1424,128]{1,0:T(8,128)(2,1)S(1)}, bf16[1424,128]{1,0:T(8,128)(2,1)}, u32[]{:S(2)}) copy-start(bf16[1424,128]{1,0:T(8,128)(2,1)} %get-tuple-element.51.refs_1_) | copy-start | bytes 1093636
  26.5 0.9 %copy-start.2 = (bf16[592,128]{1,0:T(8,128)(2,1)S(1)}, bf16[592,128]{1,0:T(8,128)(2,1)}, u32[]{:S(2)}) copy-start(bf16[592,128]{1,0:T(8,128)(2,1)} %get-tuple-element.53.refs_0_) | copy-start | bytes 454660
  27.4 0.7 %copy-start.3 = (f32[8,128]{1,0:T(8,128)S(1)}, f32[8,128]{1,0:T(8,128)}, u32[]{:S(2)}) copy-start(f32[8,128]{1,0:T(8,128)} %get-tuple-element.54.refs_2_) | copy-start | bytes 12292
  29.1 2.1 %collective-permute-start.7 = (bf16[1424,128]{1,0:T(8,128)(2,1)S(1)}, bf16[1424,128]{1,0:T(8,128)(2,1)S(1)}, u32[]{:S(2)}, u32[]{:S(2)}) collective-permute-start(bf16[1424,128]{1,0:T(8,128)(2,1)S(1)} %collective-permute-done.2.refs_5_.refs_2_), channel_id=1, source_target_pairs={{0,1},{1,0},{2,3},{3,2},{4,5},{5,4},{6,7},{7,6},{8,9},{9,8},{10,11... | collective-permute-start | bytes 1093640 | tf_op jit(solution)/shard_map/ppermute | solution.py:262
  29.2 9.6 %copy-start.1 = (bf16[2,512,128]{2,1,0:T(8,128)(2,1)S(1)}, bf16[2,512,128]{2,1,0:T(8,128)(2,1)}, u32[]{:S(2)}) copy-start(bf16[2,512,128]{2,1,0:T(8,128)(2,1)} %refs_4_.1) | copy-start | bytes 786436
  29.2 4.6 %collective-permute-start.6 = (bf16[2,128,128]{2,1,0:T(8,128)(2,1)S(1)}, bf16[2,128,128]{2,1,0:T(8,128)(2,1)S(1)}, u32[]{:S(2)}, u32[]{:S(2)}) collective-permute-start(bf16[2,128,128]{2,1,0:T(8,128)(2,1)S(1)} %slice.25), channel_id=1, source_target_pairs={{0,2},{1,3},{2,0},{3,1},{4,6},{5,7},{6,4},{7,5},{8,10},{9,11},{10,... | collective-permute-start | bytes 196616 | tf_op jit(solution)/shard_map/ppermute | solution.py:262
  29.7 6.1 %collective-permute-start.9 = (bf16[592,128]{1,0:T(8,128)(2,1)S(1)}, bf16[592,128]{1,0:T(8,128)(2,1)S(1)}, u32[]{:S(2)}, u32[]{:S(2)}) collective-permute-start(bf16[592,128]{1,0:T(8,128)(2,1)S(1)} %collective-permute-done.4.refs_2_.refs_10_), channel_id=1, source_target_pairs={{0,4},{1,5},{2,6},{3,7},{4,0},{5,1},{6,2},{7,3},{8,12},{9,13},{10,... | collective-permute-start | bytes 454664 | tf_op jit(solution)/shard_map/ppermute | solution.py:262
  33.8 6.6 %collective-permute-start.8 = (bf16[2,128,128]{2,1,0:T(8,128)(2,1)S(1)}, bf16[2,128,128]{2,1,0:T(8,128)(2,1)S(1)}, u32[]{:S(2)}, u32[]{:S(2)}) collective-permute-start(bf16[2,128,128]{2,1,0:T(8,128)(2,1)S(1)} %add_convert_fusion.6), channel_id=1, source_target_pairs={{0,4},{1,5},{2,6},{3,7},{4,0},{5,1},{6,2},{7,3},{8,12},{9,13},{10,... | collective-permute-start | bytes 196616 | tf_op jit(solution)/shard_map/ppermute | solution.py:262
  36.3 4.1 %collective-permute-start.10 = (f32[16,128]{1,0:T(8,128)S(1)}, f32[16,128]{1,0:T(8,128)S(1)}, u32[]{:S(2)}, u32[]{:S(2)}) collective-permute-start(f32[16,128]{1,0:T(8,128)S(1)} %get-tuple-element.74.refs_0_), channel_id=1, source_target_pairs={{0,1},{1,0},{2,3},{3,2},{4,5},{5,4},{6,7},{7,6},{8,9},{9,8},{10,11... | collective-permute-start | bytes 24584 | tf_op jit(solution)/shard_map/ppermute | solution.py:262
  36.4 4.1 %collective-permute-start.11 = (f32[16,128]{1,0:T(8,128)S(1)}, f32[16,128]{1,0:T(8,128)S(1)}, u32[]{:S(2)}, u32[]{:S(2)}) collective-permute-start(f32[16,128]{1,0:T(8,128)S(1)} %get-tuple-element.74.refs_0_), channel_id=1, source_target_pairs={{0,2},{1,3},{2,0},{3,1},{4,6},{5,7},{6,4},{7,5},{8,10},{9,11},{10,... | collective-permute-start | bytes 24584 | tf_op jit(solution)/shard_map/ppermute | solution.py:262
  38.7 3.1 %collective-permute-start.12 = (f32[16,128]{1,0:T(8,128)S(1)}, f32[16,128]{1,0:T(8,128)S(1)}, u32[]{:S(2)}, u32[]{:S(2)}) collective-permute-start(f32[16,128]{1,0:T(8,128)S(1)} %get-tuple-element.74.refs_0_), channel_id=1, source_target_pairs={{0,3},{1,2},{2,1},{3,0},{4,7},{5,6},{6,5},{7,4},{8,11},{9,10},{10,... | collective-permute-start | bytes 24584 | tf_op jit(solution)/shard_map/ppermute | solution.py:262
  41.8 6.6 %collective-permute-start.13 = (bf16[2,128,128]{2,1,0:T(8,128)(2,1)S(1)}, bf16[2,128,128]{2,1,0:T(8,128)(2,1)S(1)}, u32[]{:S(2)}, u32[]{:S(2)}) collective-permute-start(bf16[2,128,128]{2,1,0:T(8,128)(2,1)S(1)} %add_convert_fusion.5), channel_id=1, source_target_pairs={{0,8},{1,9},{2,10},{3,11},{4,12},{5,13},{6,14},{7,15},{8,0},{9,1},... | collective-permute-start | bytes 196616 | tf_op jit(solution)/shard_map/ppermute | solution.py:262
  44.3 8.5 %collective-permute-start.14 = (bf16[576,128]{1,0:T(8,128)(2,1)S(1)}, bf16[576,128]{1,0:T(8,128)(2,1)S(1)}, u32[]{:S(2)}, u32[]{:S(2)}) collective-permute-start(bf16[576,128]{1,0:T(8,128)(2,1)S(1)} %get-tuple-element.87), channel_id=1, source_target_pairs={{0,4},{1,5},{2,6},{3,7},{4,0},{5,1},{6,2},{7,3},{8,12},{9,13},{10,... | collective-permute-start | bytes 442376 | tf_op jit(solution)/shard_map/ppermute | solution.py:262
  48.4 4.3 %collective-permute-start.15 = (bf16[2,128,128]{2,1,0:T(8,128)(2,1)S(1)}, bf16[2,128,128]{2,1,0:T(8,128)(2,1)S(1)}, u32[]{:S(2)}, u32[]{:S(2)}) collective-permute-start(bf16[2,128,128]{2,1,0:T(8,128)(2,1)S(1)} %add_convert_fusion.4.refs_0_), channel_id=1, source_target_pairs={{0,2},{1,3},{2,0},{3,1},{4,6},{5,7},{6,4},{7,5},{8,10},{9,11},{10,... | collective-permute-start | bytes 196616 | tf_op jit(solution)/shard_map/ppermute | solution.py:262
  52.8 2.0 %collective-permute-start.16 = (bf16[4,576,128]{2,1,0:T(8,128)(2,1)S(1)}, bf16[4,576,128]{2,1,0:T(8,128)(2,1)S(1)}, u32[]{:S(2)}, u32[]{:S(2)}) collective-permute-start(bf16[4,576,128]{2,1,0:T(8,128)(2,1)S(1)} %get-tuple-element.88), channel_id=1, source_target_pairs={{0,1},{1,0},{2,3},{3,2},{4,5},{5,4},{6,7},{7,6},{8,9},{9,8},{10,11... | collective-permute-start | bytes 1769480 | tf_op jit(solution)/shard_map/ppermute | solution.py:262
  52.8 4.7 %collective-permute-start.20 = (bf16[4,128,128]{2,1,0:T(8,128)(2,1)S(1)}, bf16[4,128,128]{2,1,0:T(8,128)(2,1)S(1)}, u32[]{:S(2)}, u32[]{:S(2)}) collective-permute-start(bf16[4,128,128]{2,1,0:T(8,128)(2,1)S(1)} %pad_maximum_fusion), channel_id=1, source_target_pairs={{0,1},{1,0},{2,3},{3,2},{4,5},{5,4},{6,7},{7,6},{8,9},{9,8},{10,11... | collective-permute-start | bytes 393224 | tf_op jit(solution)/shard_map/ppermute | solution.py:262
  53.4 9.9 %collective-permute-start.18 = (bf16[576,128]{1,0:T(8,128)(2,1)S(1)}, bf16[576,128]{1,0:T(8,128)(2,1)S(1)}, u32[]{:S(2)}, u32[]{:S(2)}) collective-permute-start(bf16[576,128]{1,0:T(8,128)(2,1)S(1)} %add_convert_fusion.1), channel_id=1, source_target_pairs={{0,8},{1,9},{2,10},{3,11},{4,12},{5,13},{6,14},{7,15},{8,0},{9,1},... | collective-permute-start | bytes 442376 | tf_op jit(solution)/shard_map/ppermute | solution.py:262
  54.9 10.2 %collective-permute-start.17 = (bf16[2,576,128]{2,1,0:T(8,128)(2,1)S(1)}, bf16[2,576,128]{2,1,0:T(8,128)(2,1)S(1)}, u32[]{:S(2)}, u32[]{:S(2)}) collective-permute-start(bf16[2,576,128]{2,1,0:T(8,128)(2,1)S(1)} %add_convert_fusion), channel_id=1, source_target_pairs={{0,2},{1,3},{2,0},{3,1},{4,6},{5,7},{6,4},{7,5},{8,10},{9,11},{10,... | collective-permute-start | bytes 884744 | tf_op jit(solution)/shard_map/ppermute | solution.py:262
  55.7 8.7 %collective-permute-start.19 = (bf16[576,128]{1,0:T(8,128)(2,1)S(1)}, bf16[576,128]{1,0:T(8,128)(2,1)S(1)}, u32[]{:S(2)}, u32[]{:S(2)}) collective-permute-start(bf16[576,128]{1,0:T(8,128)(2,1)S(1)} %get-tuple-element.93), channel_id=1, source_target_pairs={{0,4},{1,5},{2,6},{3,7},{4,0},{5,1},{6,2},{7,3},{8,12},{9,13},{10,... | collective-permute-start | bytes 442376 | tf_op jit(solution)/shard_map/ppermute | solution.py:262

commit v9 on v8

--- a/solution.py
+++ b/solution.py
@@ -58,7 +58,8 @@
 def pack_kernel(
     idx_ref, pos_hbm, q_hbm, og_hbm, lat_hbm, attn_hbm, wuv_hbm,
     lat_msg, q_msg, delta_hbm, keep_hbm, send_hbm,
-    pos_ref, og_ref, attn_ref, wuv_ref, term, rows_ref, og_t_ref, delta_ref, keep_ref, send_ref, sems,
+    pos_ref, og_ref, attn_ref, wuv_ref, term, rows_ref, og_t_ref, delta_ref, keep_ref, send_ref,
+    lat_ref, q_ref, sems,
 ):
     heads, width, tok = q_hbm.shape
     _, lat, _ = wuv_ref.shape
@@ -73,9 +74,9 @@
     send_off(pos_hbm, pos_ref)
     send_off(attn_hbm, attn_ref)
     send_off(wuv_hbm, wuv_ref)
-    send_off(lat_hbm, lat_msg.at[pl.ds(0, width), :])
+    send_off(lat_hbm, lat_ref)
     for h in range(heads):
-        send_off(q_hbm.at[h], q_msg.at[pl.ds(h * width, width), :])
+        send_off(q_hbm.at[h], q_ref.at[h])
     started[0].wait()
     for h in range(heads):
         og_t_ref[h] = og_ref[:, h, :].T
@@ -88,6 +89,11 @@
     rows_ref[...] = both.astype(F32).astype(BF16)
     send_off(rows_ref, lat_msg.at[pl.ds(width, EXTRA), :])
     send_off(rows_ref, q_msg.at[pl.ds(heads * (width + HEAD_DIM), EXTRA), :])
+    started[4].wait()
+    send_off(lat_ref, lat_msg.at[pl.ds(0, width), :])
+    for h in range(heads):
+        started[5 + h].wait()
+        send_off(q_ref.at[h], q_msg.at[pl.ds(h * width, width), :])
     delta_ref[...] = jnp.zeros_like(delta_ref)
     started[2].wait()
     attn = [attn_ref[:, h, :].T for h in range(heads)]
@@ -106,7 +112,7 @@
         g = mm(wuv_ref[h], og_t_ref[h]).astype(BF16).astype(F32)
         delta_ref[h : h + 1, :] = jnp.sum(g * attn[h].astype(F32), axis=0, keepdims=True)
     send_off(delta_ref, delta_hbm)
-    for copy in started[4:]:
+    for copy in started[5 + heads :]:
         copy.wait()
 
 
@@ -296,10 +302,12 @@
             ((8, tok), F32),
             ((2 * heads, step, HEAD_DIM), BF16),
             ((2 * heads, step, HEAD_DIM), BF16),
+            ((width, tok), BF16),
+            ((heads, width, tok), BF16),
         ],
         smem=(0,),
         hbm=(1, 2, 3, 4, 5, 6),
-        copies=10 + 2 * heads,
+        copies=11 + 3 * heads,
         out=pltpu.HBM,
         limit=PACK_LIMIT,
     )
@@ -369,8 +377,7 @@
         qs + [wuv, near_k, last_k],
         flops=2 * lines * tok * all_rows * lat + 2 * all_rows * lat * HEAD_DIM,
     )
-    near, stats = lax.optimization_barrier((after(near, last_gp), stats))
-    mine = add(mine, near)
+    mine = add(mine, after(near, stat))
     for step_hop in line_hops[1:-1]:
         mine = add(mine, swap(mine, *step_hop))
     near = swap(mine, *line_hops[-1])

time: 66.2 us -> 52.5 us (0.79)
  Pallas kernels: 24.1 us -> 12.4 us
  waiting for transfers between devices: 14.3 us -> 10.6 us
  starting transfers between devices: 22.9 us -> 24.6 us
    pallas_call x10, Pallas kernels: 24.1 us -> 12.4 us  [call(): pl.pallas_call(kernel, out_shape=[jax.ShapeDtypeStruct(s, d) for s, d in...]
    ppermute x21, waiting for transfers between devices: 14.3 us -> 10.6 us  [swap(): return lax.ppermute(x, axis, [(i, i ^ mask) for i in range(size)])]
    ppermute x21, starting transfers between devices: 22.9 us -> 24.6 us  [swap(): return lax.ppermute(x, axis, [(i, i ^ mask) for i in range(size)])]
  transfers between devices with their start and end apart: 21 -> 21, of which waited for: 10 -> 9; matrix products, arithmetic and copies ran while one was open for 2% -> 2% of each run, Pallas kernels for 13% -> 17%
where the time goes in v9:
time: 52.5 us; the launch traced here: 52.3 us
  starting transfers between devices  24.6 us (47%)
  Pallas kernels  12.4 us (24%)
  waiting for transfers between devices  10.6 us (20%)
  local copies, waits for them, and re-layouts  2.62 us (5%)
  other arithmetic  1.18 us (2%)
  between operations  0.81 us (2%)
    ppermute x21, starting transfers between devices, swap(): return lax.ppermute(x, axis, [(i, i ^ mask) for i in range(size)])  24.6 us
    pallas_call x10, Pallas kernels, call(): pl.pallas_call(kernel, out_shape=[jax.ShapeDtypeStruct(s, d) for s, d in...  12.4 us
    ppermute x21, waiting for transfers between devices, swap(): return lax.ppermute(x, axis, [(i, i ^ mask) for i in range(size)])  10.6 us
    unnamed x8, local copies, waits for them, and re-layouts  2.58 us
    convert_element_type x7, other arithmetic, add(): return (a.astype(F32) + b.astype(F32)).astype(BF16)  1.17 us
  transfers between devices with their start and end apart: 21, of which 9 were waited for; matrix products, arithmetic and copies ran while one was open for 2% of the time, Pallas kernels for 17%

profile of v9, /device:TPU:0, one launch (start us, length us, event | category | flops | bytes accessed | tf_op | source)
XLA Modules:
  0.0 52.3 jit_solution(4504792731891093328)
XLA Ops:
  0.6 3.0 %pack.1 = (bf16[592,128]{1,0:T(8,128)(2,1)}, bf16[1424,128]{1,0:T(8,128)(2,1)}, f32[8,128]{1,0:T(8,128)}, bf16[4,128,128]{2,1,0:T(8,128)(2,1)}, bf16[4,128,128]{2,1,0:T(8,128)(2,1)}) custom-call(s32[1]{0:T(128)} %bitcast.idx_ref, s32[1,128]{1,0:T(1,128)} %pos_hbm.1, bf16[2,576,128]{2,1,0:T(8,128)(2,1)} %bitcast.15, bf16[128,2,128]{2,1,0:T(2,128)(2,1)} %bitcast.19, ...), custom_call_target="tpu_custom_call" | custom-call | bytes 1815044 | tf_op jit(solution)/shard_map/pack/pallas_call | solution.py:39
  3.6 0.5 collective-permute-start
  4.1 0.1 collective-permute-start.4
  4.2 2.9 %collective-permute-start.1 = (bf16[1424,128]{1,0:T(8,128)(2,1)}, bf16[1424,128]{1,0:T(8,128)(2,1)S(1)}, u32[]{:S(2)}, u32[]{:S(2)}) collective-permute-start(bf16[1424,128]{1,0:T(8,128)(2,1)} %get-tuple-element.44.refs_1_), channel_id=1, source_target_pairs={{0,2},{1,3},{2,0},{3,1},{4,6},{5,7},{6,4},{7,5},{8,10},{9,11},{10,... | collective-permute-start | bytes 1093640 | tf_op jit(solution)/shard_map/ppermute | solution.py:268
  7.1 2.6 %collective-permute-start.3 = (bf16[592,128]{1,0:T(8,128)(2,1)}, bf16[592,128]{1,0:T(8,128)(2,1)S(1)}, u32[]{:S(2)}, u32[]{:S(2)}) collective-permute-start(bf16[592,128]{1,0:T(8,128)(2,1)} %get-tuple-element.46.refs_0_), channel_id=1, source_target_pairs={{0,8},{1,9},{2,10},{3,11},{4,12},{5,13},{6,14},{7,15},{8,0},{9,1},... | collective-permute-start | bytes 454664 | tf_op jit(solution)/shard_map/ppermute | solution.py:268
  9.7 0.0 collective-permute-done.refs_4_.refs_1_
  9.7 1.6 %collective-permute-start.2 = (bf16[592,128]{1,0:T(8,128)(2,1)}, bf16[592,128]{1,0:T(8,128)(2,1)S(1)}, u32[]{:S(2)}, u32[]{:S(2)}) collective-permute-start(bf16[592,128]{1,0:T(8,128)(2,1)} %get-tuple-element.46.refs_0_), channel_id=1, source_target_pairs={{0,4},{1,5},{2,6},{3,7},{4,0},{5,1},{6,2},{7,3},{8,12},{9,13},{10,... | collective-permute-start | bytes 454664 | tf_op jit(solution)/shard_map/ppermute | solution.py:268
  11.3 0.0 collective-permute-done.4
  11.3 0.9 %add_convert_fusion.3 = bf16[4,128,128]{2,1,0:T(8,128)(2,1)S(1)} fusion(bf16[4,128,128]{2,1,0:T(8,128)(2,1)S(1)} %collective-permute-done.4, bf16[4,128,128]{2,1,0:T(8,128)(2,1)} %get-tuple-element.47), kind=kLoop, calls=%fused_computation.3 | loop fusion | flops 262144 | bytes 393216 | tf_op jit(solution)/shard_map/convert_element_type | solution.py:316
  12.3 1.6 %collective-permute-start.5 = (bf16[4,128,128]{2,1,0:T(8,128)(2,1)S(1)}, bf16[4,128,128]{2,1,0:T(8,128)(2,1)S(1)}, u32[]{:S(2)}, u32[]{:S(2)}) collective-permute-start(bf16[4,128,128]{2,1,0:T(8,128)(2,1)S(1)} %add_convert_fusion.3), channel_id=1, source_target_pairs={{0,16},{16,0},{1,17},{17,1},{2,18},{18,2},{3,19},{19,3},{4,20},{20... | collective-permute-start | bytes 393224 | tf_op jit(solution)/shard_map/ppermute | solution.py:268
  13.8 0.0 copy-start
  13.8 1.0 %copy-done = bf16[1424,128]{1,0:T(8,128)(2,1)S(1)} copy-done((bf16[1424,128]{1,0:T(8,128)(2,1)S(1)}, bf16[1424,128]{1,0:T(8,128)(2,1)}, u32[]{:S(2)}) %copy-start) | copy-done | bytes 364568
  14.8 0.0 copy-start.2
  14.8 0.9 %copy-done.2 = bf16[592,128]{1,0:T(8,128)(2,1)S(1)} copy-done((bf16[592,128]{1,0:T(8,128)(2,1)S(1)}, bf16[592,128]{1,0:T(8,128)(2,1)}, u32[]{:S(2)}) %copy-start.2) | copy-done | bytes 151576
  15.7 0.0 copy-start.3
  15.7 0.7 %copy-done.3 = f32[8,128]{1,0:T(8,128)S(1)} copy-done((f32[8,128]{1,0:T(8,128)S(1)}, f32[8,128]{1,0:T(8,128)}, u32[]{:S(2)}) %copy-start.3) | copy-done | bytes 4120
  16.4 0.8 %collective-permute-done.3.refs_2_.refs_10_ = bf16[592,128]{1,0:T(8,128)(2,1)S(1)} collective-permute-done((bf16[592,128]{1,0:T(8,128)(2,1)}, bf16[592,128]{1,0:T(8,128)(2,1)S(1)}, u32[]{:S(2)}, u32[]{:S(2)}) %collective-permute-start.3) | collective-permute-done | bytes 151584 | tf_op jit(solution)/shard_map/ppermute | solution.py:268
  17.2 0.1 collective-permute-done.5
  17.3 0.0 collective-permute-done.1.refs_5_.refs_2_
  17.3 0.1 collective-permute-done.2.refs_1_.refs_9_
  17.4 0.0 collective-permute-start.7
  17.5 0.0 copy-start.1
  17.5 0.5 %collective-permute-start.11 = (bf16[2,128,128]{2,1,0:T(8,128)(2,1)S(1)}, bf16[2,128,128]{2,1,0:T(8,128)(2,1)S(1)}, u32[]{:S(2)}, u32[]{:S(2)}) collective-permute-start(bf16[2,128,128]{2,1,0:T(8,128)(2,1)S(1)} %slice.25), channel_id=1, source_target_pairs={{0,2},{1,3},{2,0},{3,1},{4,6},{5,7},{6,4},{7,5},{8,10},{9,11},{10,... | collective-permute-start | bytes 196616 | tf_op jit(solution)/shard_map/ppermute | solution.py:268
  18.0 1.5 %collective-permute-start.6 = (bf16[592,128]{1,0:T(8,128)(2,1)S(1)}, bf16[592,128]{1,0:T(8,128)(2,1)S(1)}, u32[]{:S(2)}, u32[]{:S(2)}) collective-permute-start(bf16[592,128]{1,0:T(8,128)(2,1)S(1)} %collective-permute-done.3.refs_2_.refs_10_), channel_id=1, source_target_pairs={{0,4},{1,5},{2,6},{3,7},{4,0},{5,1},{6,2},{7,3},{8,12},{9,13},{10,... | collective-permute-start | bytes 454664 | tf_op jit(solution)/shard_map/ppermute | solution.py:268
  19.6 0.0 collective-permute-done.7.refs_6_.refs_3_
  19.6 1.2 %near_scores.1 = (f32[384,1024]{1,0:T(8,128)S(1)}, bf16[384,640]{1,0:T(8,128)(2,1)S(1)}, f32[16,128]{1,0:T(8,128)S(1)}, bf16[640,1024]{1,0:T(8,128)(2,1)S(1)}) custom-call(bf16[592,128]{1,0:T(8,128)(2,1)S(1)} %get-tuple-element.54.refs_0_.refs_8_, bf16[592,128]{1,0:T(8,128)(2,1)S(1)} %collective-permute-done.2.refs_1_.refs_9_, ...), custom_call_target="tpu_custom_call" | custom-call | tf_op jit(solution)/shard_map/near_scores/pallas_call | solution.py:39
  20.8 1.3 %collective-permute-done.11 = bf16[2,128,128]{2,1,0:T(8,128)(2,1)S(1)} collective-permute-done((bf16[2,128,128]{2,1,0:T(8,128)(2,1)S(1)}, bf16[2,128,128]{2,1,0:T(8,128)(2,1)S(1)}, u32[]{:S(2)}, u32[]{:S(2)}) %collective-permute-start.11) | collective-permute-done | bytes 65568 | tf_op jit(solution)/shard_map/ppermute | solution.py:268
  22.1 1.5 %collective-permute-start.12 = (bf16[2,128,128]{2,1,0:T(8,128)(2,1)S(1)}, bf16[2,128,128]{2,1,0:T(8,128)(2,1)S(1)}, u32[]{:S(2)}, u32[]{:S(2)}) collective-permute-start(bf16[2,128,128]{2,1,0:T(8,128)(2,1)S(1)} %add_convert_fusion.6), channel_id=1, source_target_pairs={{0,4},{1,5},{2,6},{3,7},{4,0},{5,1},{6,2},{7,3},{8,12},{9,13},{10,... | collective-permute-start | bytes 196616 | tf_op jit(solution)/shard_map/ppermute | solution.py:268
  23.6 0.5 collective-permute-done.6.refs_0_.refs_11_
  24.1 0.5 last_scores.1
  24.6 0.1 collective-permute-start.8
  24.7 2.3 %collective-permute-start.9 = (f32[16,128]{1,0:T(8,128)S(1)}, f32[16,128]{1,0:T(8,128)S(1)}, u32[]{:S(2)}, u32[]{:S(2)}) collective-permute-start(f32[16,128]{1,0:T(8,128)S(1)} %get-tuple-element.62.refs_0_), channel_id=1, source_target_pairs={{0,2},{1,3},{2,0},{3,1},{4,6},{5,7},{6,4},{7,5},{8,10},{9,11},{10,... | collective-permute-start | bytes 24584 | tf_op jit(solution)/shard_map/ppermute | solution.py:268
  27.0 0.1 collective-permute-start.10
  27.1 0.0 collective-permute-done.12
  27.1 2.1 %collective-permute-start.13 = (bf16[2,128,128]{2,1,0:T(8,128)(2,1)S(1)}, bf16[2,128,128]{2,1,0:T(8,128)(2,1)S(1)}, u32[]{:S(2)}, u32[]{:S(2)}) collective-permute-start(bf16[2,128,128]{2,1,0:T(8,128)(2,1)S(1)} %add_convert_fusion.5), channel_id=1, source_target_pairs={{0,8},{1,9},{2,10},{3,11},{4,12},{5,13},{6,14},{7,15},{8,0},{9,1},... | collective-permute-start | bytes 196616 | tf_op jit(solution)/shard_map/ppermute | solution.py:268
  29.2 0.0 copy-done.1
  29.2 1.6 %context.1 = (bf16[512,1024]{1,0:T(8,128)(2,1)S(1)}, f32[384,1024]{1,0:T(8,128)S(1)}, f32[128,1024]{1,0:T(8,128)S(1)}) custom-call(bf16[1424,128]{1,0:T(8,128)(2,1)S(1)} %get-tuple-element.56.refs_3_.refs_0_, bf16[1424,128]{1,0:T(8,128)(2,1)S(1)} %collective-permute-done.refs_4_.refs_1_, bf16[1424,128]{1,0:T(8,128)(2,1)S(1)} %collective-permute-done.1.refs_5_.refs_2_, ...), custom_call_target="tpu_custom_call" | custom-call | flops 671088640 | bytes 5521408 | tf_op jit(solution)/shard_map/context/pallas_call | solution.py:39
  30.8 0.0 collective-permute-done.8.refs_1_
  30.8 0.0 collective-permute-done.9.refs_2_
  30.8 0.0 collective-permute-done.10.refs_3_
  30.8 0.8 %last_gradients.1 = (bf16[576,128]{1,0:T(8,128)(2,1)S(1)}, bf16[128,1024]{1,0:T(8,128)(2,1)S(1)}) custom-call(f32[16,128]{1,0:T(8,128)S(1)} %get-tuple-element.62.refs_0_, f32[16,128]{1,0:T(8,128)S(1)} %collective-permute-done.8.refs_1_, f32[16,128]{1,0:T(8,128)S(1)} %collective-permute-done.9.refs_2_, f32[16,128]{1,0:T(8,128)S(1)} %collective-permute-done.10.refs_3_, ...), custom_call_target="tpu_custom_call" | custom-call | flops 285212672 | bytes 3850240 | tf_op jit(solution)/shard_map/last_gradients/pallas_call | solution.py:39
  31.7 1.7 %collective-permute-start.14 = (bf16[576,128]{1,0:T(8,128)(2,1)S(1)}, bf16[576,128]{1,0:T(8,128)(2,1)S(1)}, u32[]{:S(2)}, u32[]{:S(2)}) collective-permute-start(bf16[576,128]{1,0:T(8,128)(2,1)S(1)} %get-tuple-element.77), channel_id=1, source_target_pairs={{0,4},{1,5},{2,6},{3,7},{4,0},{5,1},{6,2},{7,3},{8,12},{9,13},{10,... | collective-permute-start | bytes 442376 | tf_op jit(solution)/shard_map/ppermute | solution.py:268
  33.4 0.3 collective-permute-done.13
  33.7 2.0 %collective-permute-start.15 = (bf16[2,128,128]{2,1,0:T(8,128)(2,1)S(1)}, bf16[2,128,128]{2,1,0:T(8,128)(2,1)S(1)}, u32[]{:S(2)}, u32[]{:S(2)}) collective-permute-start(bf16[2,128,128]{2,1,0:T(8,128)(2,1)S(1)} %add_convert_fusion.4.refs_0_), channel_id=1, source_target_pairs={{0,2},{1,3},{2,0},{3,1},{4,6},{5,7},{6,4},{7,5},{8,10},{9,11},{10,... | collective-permute-start | bytes 196616 | tf_op jit(solution)/shard_map/ppermute | solution.py:268
  35.6 2.9 %near_gradients.1 = (bf16[576,128]{1,0:T(8,128)(2,1)S(1)}, bf16[576,128]{1,0:T(8,128)(2,1)S(1)}, bf16[576,128]{1,0:T(8,128)(2,1)S(1)}, bf16[2,576,128]{2,1,0:T(8...) custom-call(f32[16,128]{1,0:T(8,128)S(1)} %get-tuple-element.62.refs_0_, ...), custom_call_target="tpu_custom_call" | custom-call | flops 1459617792 | bytes 8028160 | tf_op jit(solution)/shard_map/near_gradients/pallas_call | solution.py:39
  38.6 0.0 collective-permute-done.14
  38.6 0.0 collective-permute-done.15.refs_2_
  38.6 0.1 collective-permute-start.16
  38.7 0.4 collective-permute-start.18
  39.1 0.3 collective-permute-start.20
  39.4 1.3 %collective-permute-done.16 = bf16[4,576,128]{2,1,0:T(8,128)(2,1)S(1)} collective-permute-done((bf16[4,576,128]{2,1,0:T(8,128)(2,1)S(1)}, bf16[4,576,128]{2,1,0:T(8,128)(2,1)S(1)}, u32[]{:S(2)}, u32[]{:S(2)}) %collective-permute-start.16) | collective-permute-done | bytes 589856 | tf_op jit(solution)/shard_map/ppermute | solution.py:268
  40.7 0.1 add_convert_fusion
  40.7 1.3 %collective-permute-start.17 = (bf16[2,576,128]{2,1,0:T(8,128)(2,1)S(1)}, bf16[2,576,128]{2,1,0:T(8,128)(2,1)S(1)}, u32[]{:S(2)}, u32[]{:S(2)}) collective-permute-start(bf16[2,576,128]{2,1,0:T(8,128)(2,1)S(1)} %add_convert_fusion), channel_id=1, source_target_pairs={{0,2},{1,3},{2,0},{3,1},{4,6},{5,7},{6,4},{7,5},{8,10},{9,11},{10,... | collective-permute-start | bytes 884744 | tf_op jit(solution)/shard_map/ppermute | solution.py:268
  42.1 1.5 %collective-permute-start.19 = (bf16[576,128]{1,0:T(8,128)(2,1)S(1)}, bf16[576,128]{1,0:T(8,128)(2,1)S(1)}, u32[]{:S(2)}, u32[]{:S(2)}) collective-permute-start(bf16[576,128]{1,0:T(8,128)(2,1)S(1)} %get-tuple-element.83), channel_id=1, source_target_pairs={{0,4},{1,5},{2,6},{3,7},{4,0},{5,1},{6,2},{7,3},{8,12},{9,13},{10,... | collective-permute-start | bytes 442376 | tf_op jit(solution)/shard_map/ppermute | solution.py:268
  43.6 0.0 collective-permute-done.20
  43.6 0.8 %spread.1 = f32[2,512,128]{2,1,0:T(8,128)} custom-call(s32[1]{0:T(128)} %bitcast.idx_ref, bf16[2,128,128]{2,1,0:T(8,128)(2,1)S(1)} %add_convert_fusion.4.refs_0_, bf16[2,128,128]{2,1,0:T(8,128)(2,1)S(1)} %get-tuple-element.86.refs_1_, bf16[2,128,128]{2,1,0:T(8,128)(2,1)S(1)} %collective-permute-done.15.refs_2_, ...), custom_call_target="tpu_custom_call" | custom-call | bytes 786436 | tf_op jit(solution)/shard_map/spread/pallas_call | solution.py:39
  44.4 4.7 %collective-permute-done.18.refs_1_ = bf16[576,128]{1,0:T(8,128)(2,1)S(1)} collective-permute-done((bf16[576,128]{1,0:T(8,128)(2,1)S(1)}, bf16[576,128]{1,0:T(8,128)(2,1)S(1)}, u32[]{:S(2)}, u32[]{:S(2)}) %collective-permute-start.18) | collective-permute-done | bytes 147488 | tf_op jit(solution)/shard_map/ppermute | solution.py:268
  49.2 1.6 %collective-permute-done.19.refs_2_ = bf16[576,128]{1,0:T(8,128)(2,1)S(1)} collective-permute-done((bf16[576,128]{1,0:T(8,128)(2,1)S(1)}, bf16[576,128]{1,0:T(8,128)(2,1)S(1)}, u32[]{:S(2)}, u32[]{:S(2)}) %collective-permute-start.19) | collective-permute-done | bytes 147488 | tf_op jit(solution)/shard_map/ppermute | solution.py:268
  50.7 0.7 %latent_sum.1 = bf16[576,128]{1,0:T(8,128)(2,1)} custom-call(bf16[576,128]{1,0:T(8,128)(2,1)S(1)} %get-tuple-element.80.refs_0_, bf16[576,128]{1,0:T(8,128)(2,1)S(1)} %collective-permute-done.18.refs_1_, bf16[576,128]{1,0:T(8,128)(2,1)S(1)} %collective-permute-done.19.refs_2_), custom_call_target="tpu_custom_call" | custom-call | flops 3000000000 | bytes 589824 | tf_op jit(solution)/shard_map/latent_sum/pallas_call | solution.py:39
  51.5 0.0 collective-permute-done.17.refs_2_
  51.5 0.8 %query_sum.1 = bf16[2,576,128]{2,1,0:T(8,128)(2,1)} custom-call(bf16[2,576,128]{2,1,0:T(8,128)(2,1)S(1)} %get-tuple-element.75.refs_0_, bf16[2,576,128]{2,1,0:T(8,128)(2,1)S(1)} %slice.26.refs_1_, bf16[2,576,128]{2,1,0:T(8,128)(2,1)S(1)} %collective-permute-done.17.refs_2_), custom_call_target="tpu_custom_call" | custom-call | bytes 1179648 | tf_op jit(solution)/shard_map/query_sum/pallas_call | solution.py:39
  (10 shorter events, 0.2 us)
Async XLA Ops:
  3.6 6.1 %collective-permute-start = (bf16[1424,128]{1,0:T(8,128)(2,1)}, bf16[1424,128]{1,0:T(8,128)(2,1)S(1)}, u32[]{:S(2)}, u32[]{:S(2)}) collective-permute-start(bf16[1424,128]{1,0:T(8,128)(2,1)} %get-tuple-element.44.refs_1_), channel_id=1, source_target_pairs={{0,1},{1,0},{2,3},{3,2},{4,5},{5,4},{6,7},{7,6},{8,9},{9,8},{10,11... | collective-permute-start | bytes 1093640 | tf_op jit(solution)/shard_map/ppermute | solution.py:268
  4.1 7.2 %collective-permute-start.4 = (bf16[4,128,128]{2,1,0:T(8,128)(2,1)}, bf16[4,128,128]{2,1,0:T(8,128)(2,1)S(1)}, u32[]{:S(2)}, u32[]{:S(2)}) collective-permute-start(bf16[4,128,128]{2,1,0:T(8,128)(2,1)} %get-tuple-element.48), channel_id=1, source_target_pairs={{0,1},{1,0},{2,3},{3,2},{4,5},{5,4},{6,7},{7,6},{8,9},{9,8},{10,11... | collective-permute-start | bytes 393224 | tf_op jit(solution)/shard_map/ppermute | solution.py:268
  4.2 13.1 %collective-permute-start.1 = (bf16[1424,128]{1,0:T(8,128)(2,1)}, bf16[1424,128]{1,0:T(8,128)(2,1)S(1)}, u32[]{:S(2)}, u32[]{:S(2)}) collective-permute-start(bf16[1424,128]{1,0:T(8,128)(2,1)} %get-tuple-element.44.refs_1_), channel_id=1, source_target_pairs={{0,2},{1,3},{2,0},{3,1},{4,6},{5,7},{6,4},{7,5},{8,10},{9,11},{10,... | collective-permute-start | bytes 1093640 | tf_op jit(solution)/shard_map/ppermute | solution.py:268
  7.1 10.1 %collective-permute-start.3 = (bf16[592,128]{1,0:T(8,128)(2,1)}, bf16[592,128]{1,0:T(8,128)(2,1)S(1)}, u32[]{:S(2)}, u32[]{:S(2)}) collective-permute-start(bf16[592,128]{1,0:T(8,128)(2,1)} %get-tuple-element.46.refs_0_), channel_id=1, source_target_pairs={{0,8},{1,9},{2,10},{3,11},{4,12},{5,13},{6,14},{7,15},{8,0},{9,1},... | collective-permute-start | bytes 454664 | tf_op jit(solution)/shard_map/ppermute | solution.py:268
  9.7 7.7 %collective-permute-start.2 = (bf16[592,128]{1,0:T(8,128)(2,1)}, bf16[592,128]{1,0:T(8,128)(2,1)S(1)}, u32[]{:S(2)}, u32[]{:S(2)}) collective-permute-start(bf16[592,128]{1,0:T(8,128)(2,1)} %get-tuple-element.46.refs_0_), channel_id=1, source_target_pairs={{0,4},{1,5},{2,6},{3,7},{4,0},{5,1},{6,2},{7,3},{8,12},{9,13},{10,... | collective-permute-start | bytes 454664 | tf_op jit(solution)/shard_map/ppermute | solution.py:268
  12.3 5.0 %collective-permute-start.5 = (bf16[4,128,128]{2,1,0:T(8,128)(2,1)S(1)}, bf16[4,128,128]{2,1,0:T(8,128)(2,1)S(1)}, u32[]{:S(2)}, u32[]{:S(2)}) collective-permute-start(bf16[4,128,128]{2,1,0:T(8,128)(2,1)S(1)} %add_convert_fusion.3), channel_id=1, source_target_pairs={{0,16},{16,0},{1,17},{17,1},{2,18},{18,2},{3,19},{19,3},{4,20},{20... | collective-permute-start | bytes 393224 | tf_op jit(solution)/shard_map/ppermute | solution.py:268
  13.8 1.0 %copy-start = (bf16[1424,128]{1,0:T(8,128)(2,1)S(1)}, bf16[1424,128]{1,0:T(8,128)(2,1)}, u32[]{:S(2)}) copy-start(bf16[1424,128]{1,0:T(8,128)(2,1)} %get-tuple-element.44.refs_1_) | copy-start | bytes 1093636
  14.8 0.9 %copy-start.2 = (bf16[592,128]{1,0:T(8,128)(2,1)S(1)}, bf16[592,128]{1,0:T(8,128)(2,1)}, u32[]{:S(2)}) copy-start(bf16[592,128]{1,0:T(8,128)(2,1)} %get-tuple-element.46.refs_0_) | copy-start | bytes 454660
  15.7 0.7 %copy-start.3 = (f32[8,128]{1,0:T(8,128)S(1)}, f32[8,128]{1,0:T(8,128)}, u32[]{:S(2)}) copy-start(f32[8,128]{1,0:T(8,128)} %get-tuple-element.49.refs_2_) | copy-start | bytes 12292
  17.4 2.1 %collective-permute-start.7 = (bf16[1424,128]{1,0:T(8,128)(2,1)S(1)}, bf16[1424,128]{1,0:T(8,128)(2,1)S(1)}, u32[]{:S(2)}, u32[]{:S(2)}) collective-permute-start(bf16[1424,128]{1,0:T(8,128)(2,1)S(1)} %collective-permute-done.1.refs_5_.refs_2_), channel_id=1, source_target_pairs={{0,1},{1,0},{2,3},{3,2},{4,5},{5,4},{6,7},{7,6},{8,9},{9,8},{10,11... | collective-permute-start | bytes 1093640 | tf_op jit(solution)/shard_map/ppermute | solution.py:268
  17.5 11.7 %copy-start.1 = (bf16[2,512,128]{2,1,0:T(8,128)(2,1)S(1)}, bf16[2,512,128]{2,1,0:T(8,128)(2,1)}, u32[]{:S(2)}) copy-start(bf16[2,512,128]{2,1,0:T(8,128)(2,1)} %refs_4_.1) | copy-start | bytes 786436
  17.5 4.6 %collective-permute-start.11 = (bf16[2,128,128]{2,1,0:T(8,128)(2,1)S(1)}, bf16[2,128,128]{2,1,0:T(8,128)(2,1)S(1)}, u32[]{:S(2)}, u32[]{:S(2)}) collective-permute-start(bf16[2,128,128]{2,1,0:T(8,128)(2,1)S(1)} %slice.25), channel_id=1, source_target_pairs={{0,2},{1,3},{2,0},{3,1},{4,6},{5,7},{6,4},{7,5},{8,10},{9,11},{10,... | collective-permute-start | bytes 196616 | tf_op jit(solution)/shard_map/ppermute | solution.py:268
  18.0 6.1 %collective-permute-start.6 = (bf16[592,128]{1,0:T(8,128)(2,1)S(1)}, bf16[592,128]{1,0:T(8,128)(2,1)S(1)}, u32[]{:S(2)}, u32[]{:S(2)}) collective-permute-start(bf16[592,128]{1,0:T(8,128)(2,1)S(1)} %collective-permute-done.3.refs_2_.refs_10_), channel_id=1, source_target_pairs={{0,4},{1,5},{2,6},{3,7},{4,0},{5,1},{6,2},{7,3},{8,12},{9,13},{10,... | collective-permute-start | bytes 454664 | tf_op jit(solution)/shard_map/ppermute | solution.py:268
  22.1 5.0 %collective-permute-start.12 = (bf16[2,128,128]{2,1,0:T(8,128)(2,1)S(1)}, bf16[2,128,128]{2,1,0:T(8,128)(2,1)S(1)}, u32[]{:S(2)}, u32[]{:S(2)}) collective-permute-start(bf16[2,128,128]{2,1,0:T(8,128)(2,1)S(1)} %add_convert_fusion.6), channel_id=1, source_target_pairs={{0,4},{1,5},{2,6},{3,7},{4,0},{5,1},{6,2},{7,3},{8,12},{9,13},{10,... | collective-permute-start | bytes 196616 | tf_op jit(solution)/shard_map/ppermute | solution.py:268
  24.6 6.2 %collective-permute-start.8 = (f32[16,128]{1,0:T(8,128)S(1)}, f32[16,128]{1,0:T(8,128)S(1)}, u32[]{:S(2)}, u32[]{:S(2)}) collective-permute-start(f32[16,128]{1,0:T(8,128)S(1)} %get-tuple-element.62.refs_0_), channel_id=1, source_target_pairs={{0,1},{1,0},{2,3},{3,2},{4,5},{5,4},{6,7},{7,6},{8,9},{9,8},{10,11... | collective-permute-start | bytes 24584 | tf_op jit(solution)/shard_map/ppermute | solution.py:268
  24.7 6.1 %collective-permute-start.9 = (f32[16,128]{1,0:T(8,128)S(1)}, f32[16,128]{1,0:T(8,128)S(1)}, u32[]{:S(2)}, u32[]{:S(2)}) collective-permute-start(f32[16,128]{1,0:T(8,128)S(1)} %get-tuple-element.62.refs_0_), channel_id=1, source_target_pairs={{0,2},{1,3},{2,0},{3,1},{4,6},{5,7},{6,4},{7,5},{8,10},{9,11},{10,... | collective-permute-start | bytes 24584 | tf_op jit(solution)/shard_map/ppermute | solution.py:268
  27.0 3.8 %collective-permute-start.10 = (f32[16,128]{1,0:T(8,128)S(1)}, f32[16,128]{1,0:T(8,128)S(1)}, u32[]{:S(2)}, u32[]{:S(2)}) collective-permute-start(f32[16,128]{1,0:T(8,128)S(1)} %get-tuple-element.62.refs_0_), channel_id=1, source_target_pairs={{0,3},{1,2},{2,1},{3,0},{4,7},{5,6},{6,5},{7,4},{8,11},{9,10},{10,... | collective-permute-start | bytes 24584 | tf_op jit(solution)/shard_map/ppermute | solution.py:268
  27.1 6.5 %collective-permute-start.13 = (bf16[2,128,128]{2,1,0:T(8,128)(2,1)S(1)}, bf16[2,128,128]{2,1,0:T(8,128)(2,1)S(1)}, u32[]{:S(2)}, u32[]{:S(2)}) collective-permute-start(bf16[2,128,128]{2,1,0:T(8,128)(2,1)S(1)} %add_convert_fusion.5), channel_id=1, source_target_pairs={{0,8},{1,9},{2,10},{3,11},{4,12},{5,13},{6,14},{7,15},{8,0},{9,1},... | collective-permute-start | bytes 196616 | tf_op jit(solution)/shard_map/ppermute | solution.py:268
  31.7 6.9 %collective-permute-start.14 = (bf16[576,128]{1,0:T(8,128)(2,1)S(1)}, bf16[576,128]{1,0:T(8,128)(2,1)S(1)}, u32[]{:S(2)}, u32[]{:S(2)}) collective-permute-start(bf16[576,128]{1,0:T(8,128)(2,1)S(1)} %get-tuple-element.77), channel_id=1, source_target_pairs={{0,4},{1,5},{2,6},{3,7},{4,0},{5,1},{6,2},{7,3},{8,12},{9,13},{10,... | collective-permute-start | bytes 442376 | tf_op jit(solution)/shard_map/ppermute | solution.py:268
  33.7 4.9 %collective-permute-start.15 = (bf16[2,128,128]{2,1,0:T(8,128)(2,1)S(1)}, bf16[2,128,128]{2,1,0:T(8,128)(2,1)S(1)}, u32[]{:S(2)}, u32[]{:S(2)}) collective-permute-start(bf16[2,128,128]{2,1,0:T(8,128)(2,1)S(1)} %add_convert_fusion.4.refs_0_), channel_id=1, source_target_pairs={{0,2},{1,3},{2,0},{3,1},{4,6},{5,7},{6,4},{7,5},{8,10},{9,11},{10,... | collective-permute-start | bytes 196616 | tf_op jit(solution)/shard_map/ppermute | solution.py:268
  38.6 2.1 %collective-permute-start.16 = (bf16[4,576,128]{2,1,0:T(8,128)(2,1)S(1)}, bf16[4,576,128]{2,1,0:T(8,128)(2,1)S(1)}, u32[]{:S(2)}, u32[]{:S(2)}) collective-permute-start(bf16[4,576,128]{2,1,0:T(8,128)(2,1)S(1)} %get-tuple-element.78), channel_id=1, source_target_pairs={{0,1},{1,0},{2,3},{3,2},{4,5},{5,4},{6,7},{7,6},{8,9},{9,8},{10,11... | collective-permute-start | bytes 1769480 | tf_op jit(solution)/shard_map/ppermute | solution.py:268
  38.7 10.5 %collective-permute-start.18 = (bf16[576,128]{1,0:T(8,128)(2,1)S(1)}, bf16[576,128]{1,0:T(8,128)(2,1)S(1)}, u32[]{:S(2)}, u32[]{:S(2)}) collective-permute-start(bf16[576,128]{1,0:T(8,128)(2,1)S(1)} %add_convert_fusion.1), channel_id=1, source_target_pairs={{0,8},{1,9},{2,10},{3,11},{4,12},{5,13},{6,14},{7,15},{8,0},{9,1},... | collective-permute-start | bytes 442376 | tf_op jit(solution)/shard_map/ppermute | solution.py:268
  39.1 4.5 %collective-permute-start.20 = (bf16[4,128,128]{2,1,0:T(8,128)(2,1)S(1)}, bf16[4,128,128]{2,1,0:T(8,128)(2,1)S(1)}, u32[]{:S(2)}, u32[]{:S(2)}) collective-permute-start(bf16[4,128,128]{2,1,0:T(8,128)(2,1)S(1)} %pad_maximum_fusion), channel_id=1, source_target_pairs={{0,1},{1,0},{2,3},{3,2},{4,5},{5,4},{6,7},{7,6},{8,9},{9,8},{10,11... | collective-permute-start | bytes 393224 | tf_op jit(solution)/shard_map/ppermute | solution.py:268
  40.7 10.7 %collective-permute-start.17 = (bf16[2,576,128]{2,1,0:T(8,128)(2,1)S(1)}, bf16[2,576,128]{2,1,0:T(8,128)(2,1)S(1)}, u32[]{:S(2)}, u32[]{:S(2)}) collective-permute-start(bf16[2,576,128]{2,1,0:T(8,128)(2,1)S(1)} %add_convert_fusion), channel_id=1, source_target_pairs={{0,2},{1,3},{2,0},{3,1},{4,6},{5,7},{6,4},{7,5},{8,10},{9,11},{10,... | collective-permute-start | bytes 884744 | tf_op jit(solution)/shard_map/ppermute | solution.py:268
  42.1 8.7 %collective-permute-start.19 = (bf16[576,128]{1,0:T(8,128)(2,1)S(1)}, bf16[576,128]{1,0:T(8,128)(2,1)S(1)}, u32[]{:S(2)}, u32[]{:S(2)}) collective-permute-start(bf16[576,128]{1,0:T(8,128)(2,1)S(1)} %get-tuple-element.83), channel_id=1, source_target_pairs={{0,4},{1,5},{2,6},{3,7},{4,0},{5,1},{6,2},{7,3},{8,12},{9,13},{10,... | collective-permute-start | bytes 442376 | tf_op jit(solution)/shard_map/ppermute | solution.py:268

commit v10 on v9

--- a/solution.py
+++ b/solution.py
@@ -12,6 +12,7 @@
 HEAD_DIM = 128
 GROUP = 4
 EXTRA = 16
+CUTS = 2
 PACK_LIMIT = 63 << 20
 F32 = jnp.float32
 BF16 = jnp.bfloat16
@@ -100,11 +101,13 @@
     for h in range(heads):
         term[h] = mm_t(attn[h], og_t_ref[h])
     step = lat // GROUP
-    me = lax.rem(idx_ref[0], GROUP)
-    for k in range(GROUP):
-        at = pl.multiple_of(jnp.bitwise_xor(me, k) * step, step)
-        target = send_ref if k % 2 else keep_ref
-        target[k // 2 * heads : (k // 2 + 1) * heads] = term[:, pl.ds(at, step), :].astype(BF16)
+    side = lax.rem(idx_ref[0], 2)
+    for i in range(GROUP // 2):
+        rows = slice(i * heads, (i + 1) * heads)
+        at = pl.multiple_of((2 * i + side) * step, step)
+        keep_ref[rows] = term[:, pl.ds(at, step), :].astype(BF16)
+        at = pl.multiple_of((2 * i + 1 - side) * step, step)
+        send_ref[rows] = term[:, pl.ds(at, step), :].astype(BF16)
     send_off(send_ref, send_hbm)
     send_off(keep_ref, keep_hbm)
     started[3].wait()
@@ -187,23 +190,10 @@
         last_gp_ref[:, cols] = mm(last_k_ref[:, :lat], g_ref[:, cols])
 
 
-def grad_kernel(factor, nkey, width, heads, last, *refs):
-    stats, refs = refs[:GROUP], refs[GROUP:]
-    (s_ref, gp_ref, g_ref, q_all_ref), refs = refs[:4], refs[4:]
-    if last:
-        part_refs, gs_all, p_all = refs[:nkey], refs[nkey], refs[nkey + 1]
-    else:
-        lat_refs, refs = refs[: nkey + 1], refs[nkey + 1 :]
-        last_gs_ref, refs = refs[0], refs[1:]
-        part_refs, refs = refs[:nkey], refs[nkey:]
-        own_ref, core_ref, across_ref, kt, gs_all, p_all = refs
-    lat, all_rows = g_ref.shape
+def pair_kernel(heads, *refs):
+    stats, (s_ref, gp_ref, gs_ref, p_ref) = refs[:GROUP], refs[GROUP : GROUP + 4]
+    all_rows = s_ref.shape[1]
     rows = all_rows // GROUP
-    tok = rows // heads
-    keys = nkey * tok
-    if not last:
-        for a in range(nkey + 1):
-            kt[:, a * tok : (a + 1) * tok] = lat_refs[a][:width, :]
     for j in range(GROUP):
         cols = slice(j * rows, (j + 1) * rows)
         lse_parts = []
@@ -217,40 +207,77 @@
         at = GROUP * heads
         delta = jnp.concatenate([stats[j][at + h : at + h + 1, :] for h in range(heads)], axis=1)
         p = jnp.exp(s_ref[:, cols] - lse)
-        gs = (p * (gp_ref[:, cols] - delta)).astype(BF16)
-        gs_all[:, cols] = gs
-        p_all[:, cols] = p.astype(BF16)
-        if last:
-            continue
-        gq = mm(kt[:, :keys], gs) + mm(kt[:, keys:], last_gs_ref[:, cols])
+        gs_ref[:, cols] = (p * (gp_ref[:, cols] - delta)).astype(BF16)
+        p_ref[:, cols] = p.astype(BF16)
+
+
+def partial_kernel(factor, nkey, width, g_ref, q_all_ref, gs_ref, p_ref, *part_refs):
+    lat = g_ref.shape[0]
+    tok = part_refs[0].shape[1]
+    for a in range(nkey):
+        at = slice(a * tok, (a + 1) * tok)
+        along = mm_t(q_all_ref[:width, :], gs_ref[at, :]) * factor
+        value = mm_t(g_ref[...], p_ref[at, :])
+        part_refs[a][:lat, :] = (along[:lat] + value).astype(BF16)
+        part_refs[a][lat:, :] = along[lat:].astype(BF16)
+
+
+def last_kernel(factor, width, heads, *refs):
+    stats, refs = refs[:GROUP], refs[GROUP:]
+    s_ref, gp_ref, g_ref, q_all_ref, part_ref, gs_ref, p_ref = refs
+    pair_kernel(heads, *stats, s_ref, gp_ref, gs_ref, p_ref)
+    partial_kernel(factor, 1, width, g_ref, q_all_ref, gs_ref, p_ref, part_ref)
+
+
+def query_kernel(factor, nkey, width, heads, *refs):
+    stats, refs = refs[:GROUP], refs[GROUP:]
+    (s_ref, gp_ref, last_gs_ref), refs = refs[:3], refs[3:]
+    lat_refs, refs = refs[:nkey], refs[nkey:]
+    gq_refs, far_refs, (gs_ref, p_ref, kt) = refs[: GROUP - 1], refs[GROUP - 1 : -3], refs[-3:]
+    cut = far_refs[0].shape[0]
+    cuts = width // cut
+    tok = lat_refs[0].shape[1]
+    keys = s_ref.shape[0]
+    rows = heads * tok
+    for a in range(nkey):
+        kt[:, a * tok : (a + 1) * tok] = lat_refs[a][:width, :]
+    pair_kernel(heads, *stats, s_ref, gp_ref, gs_ref, p_ref)
+    for j in range(GROUP):
+        cols = slice(j * rows, (j + 1) * rows)
+        gq = mm(kt[:, :keys], gs_ref[:, cols]) + mm(kt[:, keys:], last_gs_ref[:, cols])
         gq = (gq * factor).astype(BF16)
         for h in range(heads):
             part = gq[:, h * tok : (h + 1) * tok]
-            if j == 0:
-                own_ref[h] = part
-            elif j == 2:
-                across_ref[h] = part
+            if j < GROUP - 1:
+                gq_refs[j][h] = part
             else:
-                core_ref[j // 2 * heads + h] = part
-    for a in range(nkey):
-        at = slice(a * tok, (a + 1) * tok)
-        along = mm_t(q_all_ref[:width, :], gs_all[at, :]) * factor
-        value = mm_t(g_ref[...], p_all[at, :])
-        part_refs[a][:lat, :] = (along[:lat] + value).astype(BF16)
-        part_refs[a][lat:, :] = along[lat:].astype(BF16)
+                for c in range(cuts):
+                    far_refs[h * cuts + c][...] = part[c * cut : (c + 1) * cut]
+
+
+def join_kernel(whole_ref, *refs):
+    pieces, out_ref = refs[:-1], refs[-1]
+    cut = pieces[0].shape[0]
+    cuts = whole_ref.shape[1] // cut
+    for i, piece in enumerate(pieces):
+        at = (i // cuts, slice(i % cuts * cut, (i % cuts + 1) * cut))
+        out_ref[at] = (whole_ref[at].astype(F32) + piece[...].astype(F32)).astype(BF16)
 
 
 def sum_kernel(*refs):
     refs[-1][...] = sum(ref[...].astype(F32) for ref in refs[:-1]).astype(BF16)
 
 
-def spread_kernel(scale, idx_ref, *refs):
-    chunks, out_ref = refs[:GROUP], refs[GROUP]
-    step = chunks[0].shape[1]
-    me = lax.rem(idx_ref[0], GROUP)
-    for k in range(GROUP):
-        at = pl.multiple_of(jnp.bitwise_xor(me, k) * step, step)
-        out_ref[:, pl.ds(at, step), :] = chunks[k][...].astype(F32) * scale
+def spread_kernel(scale, idx_ref, mine_ref, other_ref, out_ref):
+    heads, lat, _ = out_ref.shape
+    step = lat // GROUP
+    side = lax.rem(idx_ref[0], 2)
+    for i in range(GROUP // 2):
+        rows = slice(i * heads, (i + 1) * heads)
+        at = pl.multiple_of((2 * i + side) * step, step)
+        out_ref[:, pl.ds(at, step), :] = mine_ref[rows].astype(F32) * scale
+        at = pl.multiple_of((2 * i + 1 - side) * step, step)
+        out_ref[:, pl.ds(at, step), :] = other_ref[rows].astype(F32) * scale
 
 
 def body(n_ctx, n_dp, positions, queries, latent, out_grad, attn_out, wuv):
@@ -342,7 +369,7 @@
         pair = add(pair, swap(pair, *step_hop))
     lats = [held[m] for m in range(lines)]
     q_far = swap(q_across, 1)
-    got_own = swap(pair[heads:], 2)
+    got_across = swap(pair, 2)
     lat_own, q_own, delta = own
     lats[0] = lat_own
     qs = [q_own, q_core, q_across, q_far]
@@ -359,7 +386,7 @@
         flops=most * score_flops,
         share=0,
     )
-    mine = add(pair[:heads], after(got_own, near_stat))
+    mine = add(pair, after(got_across, near_stat))
     near = swap(mine, *line_hops[0])
     last_s, last_k, stat = call(
         functools.partial(score_kernel, factor, 1, width, heads, True),
@@ -376,13 +403,14 @@
         [((lat, all_rows), BF16), ((keys, all_rows), F32), ((tok, all_rows), F32)],
         qs + [wuv, near_k, last_k],
         flops=2 * lines * tok * all_rows * lat + 2 * all_rows * lat * HEAD_DIM,
+        share=3,
     )
     mine = add(mine, after(near, stat))
     for step_hop in line_hops[1:-1]:
         mine = add(mine, swap(mine, *step_hop))
     near = swap(mine, *line_hops[-1])
     last_part, last_gs = call(
-        functools.partial(grad_kernel, factor, 1, width, heads, True),
+        functools.partial(last_kernel, factor, width, heads),
         "last_gradients",
         [((width, tok), BF16), ((tok, all_rows), BF16)],
         stats + [last_s, last_gp, g, q_all],
@@ -391,37 +419,49 @@
     )
     last_got = swap(last_part, GROUP)
     mine = add(mine, near)
-    outs = call(
-        functools.partial(grad_kernel, factor, most, width, heads, False),
+    gq_shape, cut_shape = (heads, width, tok), (width // CUTS, tok)
+    gq_own, gq_core, gq_across, *far_cuts, near_gs, near_p = call(
+        functools.partial(query_kernel, factor, lines, width, heads),
+        "query_gradients",
+        [(gq_shape, BF16)] * 3 + [(cut_shape, BF16)] * (CUTS * heads) + [((keys, all_rows), BF16)] * 2,
+        stats + [near_s, near_gp, after(last_gs, mine)] + lats,
+        [((width, lines * tok), BF16)],
+        flops=2 * lines * tok * all_rows * width,
+        share=0,
+    )
+    far_cuts = [swap(cut, 1) for cut in far_cuts]
+    (gq_sum,) = call(join_kernel, "join", [(gq_shape, BF16)], [gq_across] + far_cuts)
+    gq_core = swap(gq_core, 1)
+    gq_last = swap(gq_sum, 2)
+    near_parts = call(
+        functools.partial(partial_kernel, factor, most, width),
         "near_gradients",
-        [((width, tok), BF16)] * most
-        + [((heads, width, tok), BF16), ((2 * heads, width, tok), BF16), ((heads, width, tok), BF16)],
-        stats + [near_s, near_gp, g, q_all] + lats + [after(last_gs, mine)],
-        [((width, lines * tok), BF16), ((keys, all_rows), BF16), ((keys, all_rows), BF16)],
-        flops=2 * keys * all_rows * (width + lat) + 2 * lines * tok * all_rows * width,
-    )
-    parts, (gq_own, gq_core, gq_across) = list(outs[:most]) + [last_part], outs[most:]
-    across = swap(mine, 2)
+        [((width, tok), BF16)] * most,
+        [g, q_all, near_gs, near_p],
+        flops=2 * keys * all_rows * (width + lat),
+        share=0,
+    )
+    parts = list(near_parts) + [last_part]
     kept = [parts[0]]
-    gq_got = swap(after(gq_core, last_got, across), 1)
-    gq_sum = add(gq_across, gq_got[heads:])
-    gq_last = swap(gq_sum, 2)
     for bit in range(line_bits):
         for m in range(3 << bit, lines, 2 << bit):
             got = last_got if m == most and bit == 0 else swap(parts[m], GROUP << bit)
             parts[m ^ 1 << bit] = add(parts[m ^ 1 << bit], got)
-    mine_two = jnp.concatenate([mine, across], axis=0)
-    other_two = swap(mine_two, 1)
-    pieces = [mine_two[:heads], other_two[:heads], mine_two[heads:], other_two[heads:]]
+    other = swap(mine, 1)
     parts[1] = after(parts[1], gq_sum)
     kept += [swap(parts[1 << bit], GROUP << bit) for bit in reversed(range(line_bits))]
     scale = 1.0 / math.sqrt(tok * n_ctx * n_dp)
     (grad_w,) = call(
-        functools.partial(spread_kernel, scale), "spread", [((heads, lat, HEAD_DIM), F32)], [idx] + pieces, smem=(0,)
-    )
-    (grad_lat,) = call(sum_kernel, "latent_sum", [((width, tok), BF16)], kept, flops=3*10**9)
-    gq_pieces = [gq_own, gq_got[:heads], after(gq_last, grad_lat)]
+        functools.partial(spread_kernel, scale),
+        "spread",
+        [((heads, lat, HEAD_DIM), F32)],
+        [idx, mine, other],
+        smem=(0,),
+    )
+    gq_pieces = [gq_own, gq_core, gq_last]
     (grad_q,) = call(sum_kernel, "query_sum", [((heads, width, tok), BF16)], gq_pieces)
+    kept[0] = after(kept[0], grad_q)
+    (grad_lat,) = call(sum_kernel, "latent_sum", [((width, tok), BF16)], kept)
     return (jnp.transpose(grad_q, (2, 0, 1))[None], grad_lat.T[None], grad_w)
 
 

time: 52.5 us -> 53.5 us (1.019)
  waiting for transfers between devices: 10.6 us -> 11.7 us
    ppermute x21 -> x24, waiting for transfers between devices: 10.6 us -> 11.7 us  [swap(): return lax.ppermute(x, axis, [(i, i ^ mask) for i in range(size)])]
    pallas_call x10 -> x12, Pallas kernels: 12.4 us -> 12.6 us  [call(): pl.pallas_call(kernel, out_shape=[jax.ShapeDtypeStruct(s, d) for s, d in...]
    ppermute x21 -> x24, starting transfers between devices: 24.6 us -> 24.5 us  [swap(): return lax.ppermute(x, axis, [(i, i ^ mask) for i in range(size)])]
    convert_element_type x7 -> x6, other arithmetic: 1.17 us -> 1.14 us  [add(): return (a.astype(F32) + b.astype(F32)).astype(BF16)]
  transfers between devices with their start and end apart: 21 -> 24, of which waited for: 9 -> 9; matrix products, arithmetic and copies ran while one was open for 2% -> 2% of each run, Pallas kernels for 17% -> 17%
where the time goes in v10:
time: 53.5 us; the launch traced here: 53.3 us
  starting transfers between devices  24.5 us (46%)
  Pallas kernels  12.6 us (24%)
  waiting for transfers between devices  11.7 us (22%)
  local copies, waits for them, and re-layouts  2.58 us (5%)
  other arithmetic  1.14 us (2%)
  between operations  0.8 us (1%)
    ppermute x24, starting transfers between devices, swap(): return lax.ppermute(x, axis, [(i, i ^ mask) for i in range(size)])  24.5 us
    pallas_call x12, Pallas kernels, call(): pl.pallas_call(kernel, out_shape=[jax.ShapeDtypeStruct(s, d) for s, d in...  12.6 us
    ppermute x24, waiting for transfers between devices, swap(): return lax.ppermute(x, axis, [(i, i ^ mask) for i in range(size)])  11.7 us
    unnamed x8, local copies, waits for them, and re-layouts  2.58 us
    convert_element_type x6, other arithmetic, add(): return (a.astype(F32) + b.astype(F32)).astype(BF16)  1.14 us
  transfers between devices with their start and end apart: 24, of which 9 were waited for; matrix products, arithmetic and copies ran while one was open for 2% of the time, Pallas kernels for 17%

profile of v10, /device:TPU:0, one launch (start us, length us, event | category | flops | bytes accessed | tf_op | source)
XLA Modules:
  0.0 53.3 jit_solution(6614313127743729694)
XLA Ops:
  0.6 3.0 %pack.1 = (bf16[592,128]{1,0:T(8,128)(2,1)}, bf16[1424,128]{1,0:T(8,128)(2,1)}, f32[8,128]{1,0:T(8,128)}, bf16[4,128,128]{2,1,0:T(8,128)(2,1)}, bf16[4,128,128]{2,1,0:T(8,128)(2,1)}) custom-call(s32[1]{0:T(128)} %bitcast.idx_ref, s32[1,128]{1,0:T(1,128)} %pos_hbm.1, bf16[2,576,128]{2,1,0:T(8,128)(2,1)} %bitcast.15, bf16[128,2,128]{2,1,0:T(2,128)(2,1)} %bitcast.20, ...), custom_call_target="tpu_custom_call" | custom-call | bytes 1815044 | tf_op jit(solution)/shard_map/pack/pallas_call | solution.py:40
  3.6 0.5 collective-permute-start
  4.1 0.1 collective-permute-start.4
  4.2 2.9 %collective-permute-start.1 = (bf16[1424,128]{1,0:T(8,128)(2,1)}, bf16[1424,128]{1,0:T(8,128)(2,1)S(1)}, u32[]{:S(2)}, u32[]{:S(2)}) collective-permute-start(bf16[1424,128]{1,0:T(8,128)(2,1)} %get-tuple-element.49.refs_1_), channel_id=1, source_target_pairs={{0,2},{1,3},{2,0},{3,1},{4,6},{5,7},{6,4},{7,5},{8,10},{9,11},{10,... | collective-permute-start | bytes 1093640 | tf_op jit(solution)/shard_map/ppermute | solution.py:295
  7.2 2.6 %collective-permute-start.3 = (bf16[592,128]{1,0:T(8,128)(2,1)}, bf16[592,128]{1,0:T(8,128)(2,1)S(1)}, u32[]{:S(2)}, u32[]{:S(2)}) collective-permute-start(bf16[592,128]{1,0:T(8,128)(2,1)} %get-tuple-element.51.refs_0_), channel_id=1, source_target_pairs={{0,8},{1,9},{2,10},{3,11},{4,12},{5,13},{6,14},{7,15},{8,0},{9,1},... | collective-permute-start | bytes 454664 | tf_op jit(solution)/shard_map/ppermute | solution.py:295
  9.7 0.0 collective-permute-done.refs_4_.refs_1_
  9.7 1.6 %collective-permute-start.2 = (bf16[592,128]{1,0:T(8,128)(2,1)}, bf16[592,128]{1,0:T(8,128)(2,1)S(1)}, u32[]{:S(2)}, u32[]{:S(2)}) collective-permute-start(bf16[592,128]{1,0:T(8,128)(2,1)} %get-tuple-element.51.refs_0_), channel_id=1, source_target_pairs={{0,4},{1,5},{2,6},{3,7},{4,0},{5,1},{6,2},{7,3},{8,12},{9,13},{10,... | collective-permute-start | bytes 454664 | tf_op jit(solution)/shard_map/ppermute | solution.py:295
  11.3 0.0 collective-permute-done.4
  11.3 0.9 %add_convert_fusion.5 = bf16[4,128,128]{2,1,0:T(8,128)(2,1)S(1)} fusion(bf16[4,128,128]{2,1,0:T(8,128)(2,1)S(1)} %collective-permute-done.4, bf16[4,128,128]{2,1,0:T(8,128)(2,1)} %get-tuple-element.52), kind=kLoop, calls=%fused_computation.5 | loop fusion | flops 262144 | bytes 393216 | tf_op jit(solution)/shard_map/convert_element_type | solution.py:343
  12.3 1.6 %collective-permute-start.5 = (bf16[4,128,128]{2,1,0:T(8,128)(2,1)S(1)}, bf16[4,128,128]{2,1,0:T(8,128)(2,1)S(1)}, u32[]{:S(2)}, u32[]{:S(2)}) collective-permute-start(bf16[4,128,128]{2,1,0:T(8,128)(2,1)S(1)} %add_convert_fusion.5), channel_id=1, source_target_pairs={{0,16},{16,0},{1,17},{17,1},{2,18},{18,2},{3,19},{19,3},{4,20},{20... | collective-permute-start | bytes 393224 | tf_op jit(solution)/shard_map/ppermute | solution.py:295
  13.8 1.0 %copy-done = bf16[1424,128]{1,0:T(8,128)(2,1)S(1)} copy-done((bf16[1424,128]{1,0:T(8,128)(2,1)S(1)}, bf16[1424,128]{1,0:T(8,128)(2,1)}, u32[]{:S(2)}) %copy-start) | copy-done | bytes 364568
  14.8 0.9 %copy-done.2 = bf16[592,128]{1,0:T(8,128)(2,1)S(1)} copy-done((bf16[592,128]{1,0:T(8,128)(2,1)S(1)}, bf16[592,128]{1,0:T(8,128)(2,1)}, u32[]{:S(2)}) %copy-start.2) | copy-done | bytes 151576
  15.7 0.7 %copy-done.3 = f32[8,128]{1,0:T(8,128)S(1)} copy-done((f32[8,128]{1,0:T(8,128)S(1)}, f32[8,128]{1,0:T(8,128)}, u32[]{:S(2)}) %copy-start.3) | copy-done | bytes 4120
  16.4 0.8 %collective-permute-done.3.refs_2_.refs_9_ = bf16[592,128]{1,0:T(8,128)(2,1)S(1)} collective-permute-done((bf16[592,128]{1,0:T(8,128)(2,1)}, bf16[592,128]{1,0:T(8,128)(2,1)S(1)}, u32[]{:S(2)}, u32[]{:S(2)}) %collective-permute-start.3) | collective-permute-done | bytes 151584 | tf_op jit(solution)/shard_map/ppermute | solution.py:295
  17.3 0.0 collective-permute-done.5
  17.3 0.0 collective-permute-done.1.refs_5_.refs_2_
  17.3 0.1 collective-permute-done.2.refs_1_.refs_8_
  17.5 0.0 collective-permute-start.7
  17.5 0.5 collective-permute-start.11
  18.0 1.5 %collective-permute-start.6 = (bf16[592,128]{1,0:T(8,128)(2,1)S(1)}, bf16[592,128]{1,0:T(8,128)(2,1)S(1)}, u32[]{:S(2)}, u32[]{:S(2)}) collective-permute-start(bf16[592,128]{1,0:T(8,128)(2,1)S(1)} %collective-permute-done.3.refs_2_.refs_9_), channel_id=1, source_target_pairs={{0,4},{1,5},{2,6},{3,7},{4,0},{5,1},{6,2},{7,3},{8,12},{9,13},{10,... | collective-permute-start | bytes 454664 | tf_op jit(solution)/shard_map/ppermute | solution.py:295
  19.5 0.0 collective-permute-done.7.refs_6_.refs_3_
  19.5 1.2 %near_scores.1 = (f32[384,1024]{1,0:T(8,128)S(1)}, bf16[384,640]{1,0:T(8,128)(2,1)S(1)}, f32[16,128]{1,0:T(8,128)S(1)}, bf16[640,1024]{1,0:T(8,128)(2,1)S(1)}) custom-call(bf16[592,128]{1,0:T(8,128)(2,1)S(1)} %get-tuple-element.59.refs_0_.refs_7_, bf16[592,128]{1,0:T(8,128)(2,1)S(1)} %collective-permute-done.2.refs_1_.refs_8_, ...), custom_call_target="tpu_custom_call" | custom-call | tf_op jit(solution)/shard_map/near_scores/pallas_call | solution.py:40
  20.8 0.0 copy-start.1
  20.8 2.7 %collective-permute-done.11 = bf16[4,128,128]{2,1,0:T(8,128)(2,1)S(1)} collective-permute-done((bf16[4,128,128]{2,1,0:T(8,128)(2,1)S(1)}, bf16[4,128,128]{2,1,0:T(8,128)(2,1)S(1)}, u32[]{:S(2)}, u32[]{:S(2)}) %collective-permute-start.11) | collective-permute-done | bytes 131104 | tf_op jit(solution)/shard_map/ppermute | solution.py:295
  23.5 1.5 %collective-permute-start.12 = (bf16[4,128,128]{2,1,0:T(8,128)(2,1)S(1)}, bf16[4,128,128]{2,1,0:T(8,128)(2,1)S(1)}, u32[]{:S(2)}, u32[]{:S(2)}) collective-permute-start(bf16[4,128,128]{2,1,0:T(8,128)(2,1)S(1)} %add_convert_fusion.3), channel_id=1, source_target_pairs={{0,4},{1,5},{2,6},{3,7},{4,0},{5,1},{6,2},{7,3},{8,12},{9,13},{10,... | collective-permute-start | bytes 393224 | tf_op jit(solution)/shard_map/ppermute | solution.py:295
  25.0 0.0 collective-permute-done.6.refs_0_.refs_10_
  25.0 0.5 last_scores.1
  25.5 0.1 collective-permute-start.8
  25.6 0.7 %collective-permute-start.9 = (f32[16,128]{1,0:T(8,128)S(1)}, f32[16,128]{1,0:T(8,128)S(1)}, u32[]{:S(2)}, u32[]{:S(2)}) collective-permute-start(f32[16,128]{1,0:T(8,128)S(1)} %get-tuple-element.67.refs_0_), channel_id=1, source_target_pairs={{0,2},{1,3},{2,0},{3,1},{4,6},{5,7},{6,4},{7,5},{8,10},{9,11},{10,... | collective-permute-start | bytes 24584 | tf_op jit(solution)/shard_map/ppermute | solution.py:295
  26.3 1.1 %collective-permute-start.10 = (f32[16,128]{1,0:T(8,128)S(1)}, f32[16,128]{1,0:T(8,128)S(1)}, u32[]{:S(2)}, u32[]{:S(2)}) collective-permute-start(f32[16,128]{1,0:T(8,128)S(1)} %get-tuple-element.67.refs_0_), channel_id=1, source_target_pairs={{0,3},{1,2},{2,1},{3,0},{4,7},{5,6},{6,5},{7,4},{8,11},{9,10},{10,... | collective-permute-start | bytes 24584 | tf_op jit(solution)/shard_map/ppermute | solution.py:295
  27.5 1.3 %collective-permute-done.12 = bf16[4,128,128]{2,1,0:T(8,128)(2,1)S(1)} collective-permute-done((bf16[4,128,128]{2,1,0:T(8,128)(2,1)S(1)}, bf16[4,128,128]{2,1,0:T(8,128)(2,1)S(1)}, u32[]{:S(2)}, u32[]{:S(2)}) %collective-permute-start.12) | collective-permute-done | bytes 131104 | tf_op jit(solution)/shard_map/ppermute | solution.py:295
  28.8 2.1 %collective-permute-start.13 = (bf16[4,128,128]{2,1,0:T(8,128)(2,1)S(1)}, bf16[4,128,128]{2,1,0:T(8,128)(2,1)S(1)}, u32[]{:S(2)}, u32[]{:S(2)}) collective-permute-start(bf16[4,128,128]{2,1,0:T(8,128)(2,1)S(1)} %add_convert_fusion.2), channel_id=1, source_target_pairs={{0,8},{1,9},{2,10},{3,11},{4,12},{5,13},{6,14},{7,15},{8,0},{9,1},... | collective-permute-start | bytes 393224 | tf_op jit(solution)/shard_map/ppermute | solution.py:295
  30.9 1.6 %context.1 = (bf16[512,1024]{1,0:T(8,128)(2,1)S(1)}, f32[384,1024]{1,0:T(8,128)S(1)}, f32[128,1024]{1,0:T(8,128)S(1)}) custom-call(bf16[1424,128]{1,0:T(8,128)(2,1)S(1)} %get-tuple-element.61.refs_3_.refs_0_, bf16[1424,128]{1,0:T(8,128)(2,1)S(1)} %collective-permute-done.refs_4_.refs_1_, bf16[1424,128]{1,0:T(8,128)(2,1)S(1)} %collective-permute-done.1.refs_5_.refs_2_, ...), custom_call_target="tpu_custom_call" | custom-call | flops 2013265920 | bytes 16564224 | tf_op jit(solution)/shard_map/context/pallas_call | solution.py:40
  32.5 0.0 collective-permute-done.8.refs_1_
  32.5 0.0 collective-permute-done.9.refs_2_
  32.5 0.0 collective-permute-done.10.refs_3_
  32.5 0.8 %last_gradients.1 = (bf16[576,128]{1,0:T(8,128)(2,1)S(1)}, bf16[128,1024]{1,0:T(8,128)(2,1)S(1)}) custom-call(f32[16,128]{1,0:T(8,128)S(1)} %get-tuple-element.67.refs_0_, f32[16,128]{1,0:T(8,128)S(1)} %collective-permute-done.8.refs_1_, f32[16,128]{1,0:T(8,128)S(1)} %collective-permute-done.9.refs_2_, f32[16,128]{1,0:T(8,128)S(1)} %collective-permute-done.10.refs_3_, ...), custom_call_target="tpu_custom_call" | custom-call | flops 285212672 | bytes 3850240 | tf_op jit(solution)/shard_map/last_gradients/pallas_call | solution.py:40
  33.3 1.8 %collective-permute-start.20 = (bf16[576,128]{1,0:T(8,128)(2,1)S(1)}, bf16[576,128]{1,0:T(8,128)(2,1)S(1)}, u32[]{:S(2)}, u32[]{:S(2)}) collective-permute-start(bf16[576,128]{1,0:T(8,128)(2,1)S(1)} %get-tuple-element.92), channel_id=1, source_target_pairs={{0,4},{1,5},{2,6},{3,7},{4,0},{5,1},{6,2},{7,3},{8,12},{9,13},{10,... | collective-permute-start | bytes 442376 | tf_op jit(solution)/shard_map/ppermute | solution.py:295
  35.1 2.0 %collective-permute-done.13 = bf16[4,128,128]{2,1,0:T(8,128)(2,1)S(1)} collective-permute-done((bf16[4,128,128]{2,1,0:T(8,128)(2,1)S(1)}, bf16[4,128,128]{2,1,0:T(8,128)(2,1)S(1)}, u32[]{:S(2)}, u32[]{:S(2)}) %collective-permute-start.13) | collective-permute-done | bytes 131104 | tf_op jit(solution)/shard_map/ppermute | solution.py:295
  37.2 1.1 %query_gradients.1 = (bf16[2,576,128]{2,1,0:T(8,128)(2,1)S(1)}, bf16[2,576,128]{2,1,0:T(8,128)(2,1)S(1)}, bf16[2,576,128]{2,1,0:T(8,128)(2,1)S(1)}, bf16[288,128...) custom-call(f32[16,128]{1,0:T(8,128)S(1)} %get-tuple-element.67.refs, ...), custom_call_target="tpu_custom_call" | custom-call | tf_op jit(solution)/shard_map/query_gradients/pallas_call | solution.py:40
  38.3 0.1 collective-permute-start.15
  38.4 0.5 collective-permute-start.16
  38.9 0.1 collective-permute-start.17
  39.0 0.4 collective-permute-start.18
  39.4 1.9 %near_gradients.1 = (bf16[576,128]{1,0:T(8,128)(2,1)S(1)}, bf16[576,128]{1,0:T(8,128)(2,1)S(1)}, bf16[576,128]{1,0:T(8,128)(2,1)S(1)}) custom-call(bf16[512,1024]{1,0:T(8,128)(2,1)S(1)} %get-tuple-element.74.refs_6_.g_ref, bf16[640,1024]{1,0:T(8,128)(2,1)S(1)} %get-tuple-element.64.refs_1_.refs_7_.q_all_ref, bf16[384,1024]{1,0:T(8,128)(2,1)S(1)} %get-tuple-element.87.gs_ref, ...), custom_call_target="tpu_custom_call" | custom-call | tf_op jit(solution)/shard_map/near_gradients/pallas_call | solution.py:40
  41.3 0.0 collective-permute-done.15.refs_0_
  41.3 0.1 collective-permute-start.14
  41.5 0.0 collective-permute-done.16.refs_1_
  41.5 0.0 collective-permute-done.17.refs_2_
  41.5 0.0 collective-permute-done.18.refs_3_
  41.5 0.1 join.1
  41.6 0.7 %collective-permute-start.19 = (bf16[2,576,128]{2,1,0:T(8,128)(2,1)S(1)}, bf16[2,576,128]{2,1,0:T(8,128)(2,1)S(1)}, u32[]{:S(2)}, u32[]{:S(2)}) collective-permute-start(bf16[2,576,128]{2,1,0:T(8,128)(2,1)S(1)} %join.1), channel_id=1, source_target_pairs={{0,2},{1,3},{2,0},{3,1},{4,6},{5,7},{6,4},{7,5},{8,10},{9,11},{10,... | collective-permute-start | bytes 884744 | tf_op jit(solution)/shard_map/ppermute | solution.py:295
  42.3 0.0 collective-permute-done.20
  42.3 0.1 collective-permute-start.21
  42.4 3.8 %collective-permute-start.22 = (bf16[576,128]{1,0:T(8,128)(2,1)S(1)}, bf16[576,128]{1,0:T(8,128)(2,1)S(1)}, u32[]{:S(2)}, u32[]{:S(2)}) collective-permute-start(bf16[576,128]{1,0:T(8,128)(2,1)S(1)} %get-tuple-element.94), channel_id=1, source_target_pairs={{0,4},{1,5},{2,6},{3,7},{4,0},{5,1},{6,2},{7,3},{8,12},{9,13},{10,... | collective-permute-start | bytes 442376 | tf_op jit(solution)/shard_map/ppermute | solution.py:295
  46.2 0.0 collective-permute-start.23
  46.2 1.3 %collective-permute-done.23.other_ref = bf16[4,128,128]{2,1,0:T(8,128)(2,1)S(1)} collective-permute-done((bf16[4,128,128]{2,1,0:T(8,128)(2,1)S(1)}, bf16[4,128,128]{2,1,0:T(8,128)(2,1)S(1)}, u32[]{:S(2)}, u32[]{:S(2)}) %collective-permute-start.23) | collective-permute-done | bytes 131104 | tf_op jit(solution)/shard_map/ppermute | solution.py:295
  47.6 0.8 %spread.1 = f32[2,512,128]{2,1,0:T(8,128)} custom-call(s32[1]{0:T(128)} %bitcast.idx_ref, bf16[4,128,128]{2,1,0:T(8,128)(2,1)S(1)} %add_convert_fusion.1.mine_ref, bf16[4,128,128]{2,1,0:T(8,128)(2,1)S(1)} %collective-permute-done.23.other_ref), custom_call_target="tpu_custom_call" | custom-call | bytes 786436 | tf_op jit(solution)/shard_map/spread/pallas_call | solution.py:40
  48.4 0.0 collective-permute-done.14.refs_1_
  48.4 2.6 %collective-permute-done.19.refs_2_ = bf16[2,576,128]{2,1,0:T(8,128)(2,1)S(1)} collective-permute-done((bf16[2,576,128]{2,1,0:T(8,128)(2,1)S(1)}, bf16[2,576,128]{2,1,0:T(8,128)(2,1)S(1)}, u32[]{:S(2)}, u32[]{:S(2)}) %collective-permute-start.19) | collective-permute-done | bytes 294944 | tf_op jit(solution)/shard_map/ppermute | solution.py:295
  51.0 0.8 %query_sum.1 = bf16[2,576,128]{2,1,0:T(8,128)(2,1)} custom-call(bf16[2,576,128]{2,1,0:T(8,128)(2,1)S(1)} %get-tuple-element.80.refs_0_, bf16[2,576,128]{2,1,0:T(8,128)(2,1)S(1)} %collective-permute-done.14.refs_1_, bf16[2,576,128]{2,1,0:T(8,128)(2,1)S(1)} %collective-permute-done.19.refs_2_), custom_call_target="tpu_custom_call" | custom-call | bytes 1179648 | tf_op jit(solution)/shard_map/query_sum/pallas_call | solution.py:40
  51.8 0.7 %collective-permute-done.21.refs_1_ = bf16[576,128]{1,0:T(8,128)(2,1)S(1)} collective-permute-done((bf16[576,128]{1,0:T(8,128)(2,1)S(1)}, bf16[576,128]{1,0:T(8,128)(2,1)S(1)}, u32[]{:S(2)}, u32[]{:S(2)}) %collective-permute-start.21) | collective-permute-done | bytes 147488 | tf_op jit(solution)/shard_map/ppermute | solution.py:295
  52.5 0.1 collective-permute-done.22.refs_2_
  52.6 0.7 %latent_sum.1 = bf16[576,128]{1,0:T(8,128)(2,1)} custom-call(bf16[576,128]{1,0:T(8,128)(2,1)S(1)} %get-tuple-element.90.refs_0_, bf16[576,128]{1,0:T(8,128)(2,1)S(1)} %collective-permute-done.21.refs_1_, bf16[576,128]{1,0:T(8,128)(2,1)S(1)} %collective-permute-done.22.refs_2_), custom_call_target="tpu_custom_call" | custom-call | bytes 589824 | tf_op jit(solution)/shard_map/latent_sum/pallas_call | solution.py:40
  (10 shorter events, 0.2 us)
Async XLA Ops:
  3.6 6.1 %collective-permute-start = (bf16[1424,128]{1,0:T(8,128)(2,1)}, bf16[1424,128]{1,0:T(8,128)(2,1)S(1)}, u32[]{:S(2)}, u32[]{:S(2)}) collective-permute-start(bf16[1424,128]{1,0:T(8,128)(2,1)} %get-tuple-element.49.refs_1_), channel_id=1, source_target_pairs={{0,1},{1,0},{2,3},{3,2},{4,5},{5,4},{6,7},{7,6},{8,9},{9,8},{10,11... | collective-permute-start | bytes 1093640 | tf_op jit(solution)/shard_map/ppermute | solution.py:295
  4.1 7.2 %collective-permute-start.4 = (bf16[4,128,128]{2,1,0:T(8,128)(2,1)}, bf16[4,128,128]{2,1,0:T(8,128)(2,1)S(1)}, u32[]{:S(2)}, u32[]{:S(2)}) collective-permute-start(bf16[4,128,128]{2,1,0:T(8,128)(2,1)} %get-tuple-element.53), channel_id=1, source_target_pairs={{0,1},{1,0},{2,3},{3,2},{4,5},{5,4},{6,7},{7,6},{8,9},{9,8},{10,11... | collective-permute-start | bytes 393224 | tf_op jit(solution)/shard_map/ppermute | solution.py:295
  4.2 13.1 %collective-permute-start.1 = (bf16[1424,128]{1,0:T(8,128)(2,1)}, bf16[1424,128]{1,0:T(8,128)(2,1)S(1)}, u32[]{:S(2)}, u32[]{:S(2)}) collective-permute-start(bf16[1424,128]{1,0:T(8,128)(2,1)} %get-tuple-element.49.refs_1_), channel_id=1, source_target_pairs={{0,2},{1,3},{2,0},{3,1},{4,6},{5,7},{6,4},{7,5},{8,10},{9,11},{10,... | collective-permute-start | bytes 1093640 | tf_op jit(solution)/shard_map/ppermute | solution.py:295
  7.2 10.1 %collective-permute-start.3 = (bf16[592,128]{1,0:T(8,128)(2,1)}, bf16[592,128]{1,0:T(8,128)(2,1)S(1)}, u32[]{:S(2)}, u32[]{:S(2)}) collective-permute-start(bf16[592,128]{1,0:T(8,128)(2,1)} %get-tuple-element.51.refs_0_), channel_id=1, source_target_pairs={{0,8},{1,9},{2,10},{3,11},{4,12},{5,13},{6,14},{7,15},{8,0},{9,1},... | collective-permute-start | bytes 454664 | tf_op jit(solution)/shard_map/ppermute | solution.py:295
  9.7 7.7 %collective-permute-start.2 = (bf16[592,128]{1,0:T(8,128)(2,1)}, bf16[592,128]{1,0:T(8,128)(2,1)S(1)}, u32[]{:S(2)}, u32[]{:S(2)}) collective-permute-start(bf16[592,128]{1,0:T(8,128)(2,1)} %get-tuple-element.51.refs_0_), channel_id=1, source_target_pairs={{0,4},{1,5},{2,6},{3,7},{4,0},{5,1},{6,2},{7,3},{8,12},{9,13},{10,... | collective-permute-start | bytes 454664 | tf_op jit(solution)/shard_map/ppermute | solution.py:295
  12.3 5.0 %collective-permute-start.5 = (bf16[4,128,128]{2,1,0:T(8,128)(2,1)S(1)}, bf16[4,128,128]{2,1,0:T(8,128)(2,1)S(1)}, u32[]{:S(2)}, u32[]{:S(2)}) collective-permute-start(bf16[4,128,128]{2,1,0:T(8,128)(2,1)S(1)} %add_convert_fusion.5), channel_id=1, source_target_pairs={{0,16},{16,0},{1,17},{17,1},{2,18},{18,2},{3,19},{19,3},{4,20},{20... | collective-permute-start | bytes 393224 | tf_op jit(solution)/shard_map/ppermute | solution.py:295
  13.8 1.0 %copy-start = (bf16[1424,128]{1,0:T(8,128)(2,1)S(1)}, bf16[1424,128]{1,0:T(8,128)(2,1)}, u32[]{:S(2)}) copy-start(bf16[1424,128]{1,0:T(8,128)(2,1)} %get-tuple-element.49.refs_1_) | copy-start | bytes 1093636
  14.8 0.9 %copy-start.2 = (bf16[592,128]{1,0:T(8,128)(2,1)S(1)}, bf16[592,128]{1,0:T(8,128)(2,1)}, u32[]{:S(2)}) copy-start(bf16[592,128]{1,0:T(8,128)(2,1)} %get-tuple-element.51.refs_0_) | copy-start | bytes 454660
  15.7 0.7 %copy-start.3 = (f32[8,128]{1,0:T(8,128)S(1)}, f32[8,128]{1,0:T(8,128)}, u32[]{:S(2)}) copy-start(f32[8,128]{1,0:T(8,128)} %get-tuple-element.54.refs_2_) | copy-start | bytes 12292
  17.5 2.1 %collective-permute-start.7 = (bf16[1424,128]{1,0:T(8,128)(2,1)S(1)}, bf16[1424,128]{1,0:T(8,128)(2,1)S(1)}, u32[]{:S(2)}, u32[]{:S(2)}) collective-permute-start(bf16[1424,128]{1,0:T(8,128)(2,1)S(1)} %collective-permute-done.1.refs_5_.refs_2_), channel_id=1, source_target_pairs={{0,1},{1,0},{2,3},{3,2},{4,5},{5,4},{6,7},{7,6},{8,9},{9,8},{10,11... | collective-permute-start | bytes 1093640 | tf_op jit(solution)/shard_map/ppermute | solution.py:295
  17.5 6.0 %collective-permute-start.11 = (bf16[4,128,128]{2,1,0:T(8,128)(2,1)S(1)}, bf16[4,128,128]{2,1,0:T(8,128)(2,1)S(1)}, u32[]{:S(2)}, u32[]{:S(2)}) collective-permute-start(bf16[4,128,128]{2,1,0:T(8,128)(2,1)S(1)} %add_convert_fusion.4), channel_id=1, source_target_pairs={{0,2},{1,3},{2,0},{3,1},{4,6},{5,7},{6,4},{7,5},{8,10},{9,11},{10,... | collective-permute-start | bytes 393224 | tf_op jit(solution)/shard_map/ppermute | solution.py:295
  18.0 7.0 %collective-permute-start.6 = (bf16[592,128]{1,0:T(8,128)(2,1)S(1)}, bf16[592,128]{1,0:T(8,128)(2,1)S(1)}, u32[]{:S(2)}, u32[]{:S(2)}) collective-permute-start(bf16[592,128]{1,0:T(8,128)(2,1)S(1)} %collective-permute-done.3.refs_2_.refs_9_), channel_id=1, source_target_pairs={{0,4},{1,5},{2,6},{3,7},{4,0},{5,1},{6,2},{7,3},{8,12},{9,13},{10,... | collective-permute-start | bytes 454664 | tf_op jit(solution)/shard_map/ppermute | solution.py:295
  20.8 10.1 %copy-start.1 = (bf16[2,512,128]{2,1,0:T(8,128)(2,1)S(1)}, bf16[2,512,128]{2,1,0:T(8,128)(2,1)}, u32[]{:S(2)}) copy-start(bf16[2,512,128]{2,1,0:T(8,128)(2,1)} %refs_4_.1) | copy-start | bytes 786436
  23.5 5.2 %collective-permute-start.12 = (bf16[4,128,128]{2,1,0:T(8,128)(2,1)S(1)}, bf16[4,128,128]{2,1,0:T(8,128)(2,1)S(1)}, u32[]{:S(2)}, u32[]{:S(2)}) collective-permute-start(bf16[4,128,128]{2,1,0:T(8,128)(2,1)S(1)} %add_convert_fusion.3), channel_id=1, source_target_pairs={{0,4},{1,5},{2,6},{3,7},{4,0},{5,1},{6,2},{7,3},{8,12},{9,13},{10,... | collective-permute-start | bytes 393224 | tf_op jit(solution)/shard_map/ppermute | solution.py:295
  25.5 7.0 %collective-permute-start.8 = (f32[16,128]{1,0:T(8,128)S(1)}, f32[16,128]{1,0:T(8,128)S(1)}, u32[]{:S(2)}, u32[]{:S(2)}) collective-permute-start(f32[16,128]{1,0:T(8,128)S(1)} %get-tuple-element.67.refs_0_), channel_id=1, source_target_pairs={{0,1},{1,0},{2,3},{3,2},{4,5},{5,4},{6,7},{7,6},{8,9},{9,8},{10,11... | collective-permute-start | bytes 24584 | tf_op jit(solution)/shard_map/ppermute | solution.py:295
  25.6 6.9 %collective-permute-start.9 = (f32[16,128]{1,0:T(8,128)S(1)}, f32[16,128]{1,0:T(8,128)S(1)}, u32[]{:S(2)}, u32[]{:S(2)}) collective-permute-start(f32[16,128]{1,0:T(8,128)S(1)} %get-tuple-element.67.refs_0_), channel_id=1, source_target_pairs={{0,2},{1,3},{2,0},{3,1},{4,6},{5,7},{6,4},{7,5},{8,10},{9,11},{10,... | collective-permute-start | bytes 24584 | tf_op jit(solution)/shard_map/ppermute | solution.py:295
  26.3 6.2 %collective-permute-start.10 = (f32[16,128]{1,0:T(8,128)S(1)}, f32[16,128]{1,0:T(8,128)S(1)}, u32[]{:S(2)}, u32[]{:S(2)}) collective-permute-start(f32[16,128]{1,0:T(8,128)S(1)} %get-tuple-element.67.refs_0_), channel_id=1, source_target_pairs={{0,3},{1,2},{2,1},{3,0},{4,7},{5,6},{6,5},{7,4},{8,11},{9,10},{10,... | collective-permute-start | bytes 24584 | tf_op jit(solution)/shard_map/ppermute | solution.py:295
  28.8 8.4 %collective-permute-start.13 = (bf16[4,128,128]{2,1,0:T(8,128)(2,1)S(1)}, bf16[4,128,128]{2,1,0:T(8,128)(2,1)S(1)}, u32[]{:S(2)}, u32[]{:S(2)}) collective-permute-start(bf16[4,128,128]{2,1,0:T(8,128)(2,1)S(1)} %add_convert_fusion.2), channel_id=1, source_target_pairs={{0,8},{1,9},{2,10},{3,11},{4,12},{5,13},{6,14},{7,15},{8,0},{9,1},... | collective-permute-start | bytes 393224 | tf_op jit(solution)/shard_map/ppermute | solution.py:295
  33.3 9.0 %collective-permute-start.20 = (bf16[576,128]{1,0:T(8,128)(2,1)S(1)}, bf16[576,128]{1,0:T(8,128)(2,1)S(1)}, u32[]{:S(2)}, u32[]{:S(2)}) collective-permute-start(bf16[576,128]{1,0:T(8,128)(2,1)S(1)} %get-tuple-element.92), channel_id=1, source_target_pairs={{0,4},{1,5},{2,6},{3,7},{4,0},{5,1},{6,2},{7,3},{8,12},{9,13},{10,... | collective-permute-start | bytes 442376 | tf_op jit(solution)/shard_map/ppermute | solution.py:295
  38.3 3.0 %collective-permute-start.15 = (bf16[288,128]{1,0:T(8,128)(2,1)S(1)}, bf16[288,128]{1,0:T(8,128)(2,1)S(1)}, u32[]{:S(2)}, u32[]{:S(2)}) collective-permute-start(bf16[288,128]{1,0:T(8,128)(2,1)S(1)} %get-tuple-element.83), channel_id=1, source_target_pairs={{0,1},{1,0},{2,3},{3,2},{4,5},{5,4},{6,7},{7,6},{8,9},{9,8},{10,11... | collective-permute-start | bytes 221192 | tf_op jit(solution)/shard_map/ppermute | solution.py:295
  38.4 3.1 %collective-permute-start.16 = (bf16[288,128]{1,0:T(8,128)(2,1)S(1)}, bf16[288,128]{1,0:T(8,128)(2,1)S(1)}, u32[]{:S(2)}, u32[]{:S(2)}) collective-permute-start(bf16[288,128]{1,0:T(8,128)(2,1)S(1)} %get-tuple-element.84), channel_id=1, source_target_pairs={{0,1},{1,0},{2,3},{3,2},{4,5},{5,4},{6,7},{7,6},{8,9},{9,8},{10,11... | collective-permute-start | bytes 221192 | tf_op jit(solution)/shard_map/ppermute | solution.py:295
  38.9 2.6 %collective-permute-start.17 = (bf16[288,128]{1,0:T(8,128)(2,1)S(1)}, bf16[288,128]{1,0:T(8,128)(2,1)S(1)}, u32[]{:S(2)}, u32[]{:S(2)}) collective-permute-start(bf16[288,128]{1,0:T(8,128)(2,1)S(1)} %get-tuple-element.85), channel_id=1, source_target_pairs={{0,1},{1,0},{2,3},{3,2},{4,5},{5,4},{6,7},{7,6},{8,9},{9,8},{10,11... | collective-permute-start | bytes 221192 | tf_op jit(solution)/shard_map/ppermute | solution.py:295
  39.0 2.5 %collective-permute-start.18 = (bf16[288,128]{1,0:T(8,128)(2,1)S(1)}, bf16[288,128]{1,0:T(8,128)(2,1)S(1)}, u32[]{:S(2)}, u32[]{:S(2)}) collective-permute-start(bf16[288,128]{1,0:T(8,128)(2,1)S(1)} %get-tuple-element.86), channel_id=1, source_target_pairs={{0,1},{1,0},{2,3},{3,2},{4,5},{5,4},{6,7},{7,6},{8,9},{9,8},{10,11... | collective-permute-start | bytes 221192 | tf_op jit(solution)/shard_map/ppermute | solution.py:295
  41.3 7.1 %collective-permute-start.14 = (bf16[2,576,128]{2,1,0:T(8,128)(2,1)S(1)}, bf16[2,576,128]{2,1,0:T(8,128)(2,1)S(1)}, u32[]{:S(2)}, u32[]{:S(2)}) collective-permute-start(bf16[2,576,128]{2,1,0:T(8,128)(2,1)S(1)} %get-tuple-element.81), channel_id=1, source_target_pairs={{0,1},{1,0},{2,3},{3,2},{4,5},{5,4},{6,7},{7,6},{8,9},{9,8},{10,11... | collective-permute-start | bytes 884744 | tf_op jit(solution)/shard_map/ppermute | solution.py:295
  41.6 9.4 %collective-permute-start.19 = (bf16[2,576,128]{2,1,0:T(8,128)(2,1)S(1)}, bf16[2,576,128]{2,1,0:T(8,128)(2,1)S(1)}, u32[]{:S(2)}, u32[]{:S(2)}) collective-permute-start(bf16[2,576,128]{2,1,0:T(8,128)(2,1)S(1)} %join.1), channel_id=1, source_target_pairs={{0,2},{1,3},{2,0},{3,1},{4,6},{5,7},{6,4},{7,5},{8,10},{9,11},{10,... | collective-permute-start | bytes 884744 | tf_op jit(solution)/shard_map/ppermute | solution.py:295
  42.3 10.1 %collective-permute-start.21 = (bf16[576,128]{1,0:T(8,128)(2,1)S(1)}, bf16[576,128]{1,0:T(8,128)(2,1)S(1)}, u32[]{:S(2)}, u32[]{:S(2)}) collective-permute-start(bf16[576,128]{1,0:T(8,128)(2,1)S(1)} %add_convert_fusion), channel_id=1, source_target_pairs={{0,8},{1,9},{2,10},{3,11},{4,12},{5,13},{6,14},{7,15},{8,0},{9,1},... | collective-permute-start | bytes 442376 | tf_op jit(solution)/shard_map/ppermute | solution.py:295
  42.4 10.1 %collective-permute-start.22 = (bf16[576,128]{1,0:T(8,128)(2,1)S(1)}, bf16[576,128]{1,0:T(8,128)(2,1)S(1)}, u32[]{:S(2)}, u32[]{:S(2)}) collective-permute-start(bf16[576,128]{1,0:T(8,128)(2,1)S(1)} %get-tuple-element.94), channel_id=1, source_target_pairs={{0,4},{1,5},{2,6},{3,7},{4,0},{5,1},{6,2},{7,3},{8,12},{9,13},{10,... | collective-permute-start | bytes 442376 | tf_op jit(solution)/shard_map/ppermute | solution.py:295
  46.2 1.3 %collective-permute-start.23 = (bf16[4,128,128]{2,1,0:T(8,128)(2,1)S(1)}, bf16[4,128,128]{2,1,0:T(8,128)(2,1)S(1)}, u32[]{:S(2)}, u32[]{:S(2)}) collective-permute-start(bf16[4,128,128]{2,1,0:T(8,128)(2,1)S(1)} %add_convert_fusion.1.mine_ref), channel_id=1, source_target_pairs={{0,1},{1,0},{2,3},{3,2},{4,5},{5,4},{6,7},{7,6},{8,9},{9,8},{10,11... | collective-permute-start | bytes 393224 | tf_op jit(solution)/shard_map/ppermute | solution.py:295

commit v11 on v10

--- a/solution.py
+++ b/solution.py
@@ -211,11 +211,9 @@
         p_ref[:, cols] = p.astype(BF16)
 
 
-def partial_kernel(factor, nkey, width, g_ref, q_all_ref, gs_ref, p_ref, *part_refs):
+def partial_kernel(factor, places, width, g_ref, q_all_ref, gs_ref, p_ref, *part_refs):
     lat = g_ref.shape[0]
-    tok = part_refs[0].shape[1]
-    for a in range(nkey):
-        at = slice(a * tok, (a + 1) * tok)
+    for a, at in enumerate(places):
         along = mm_t(q_all_ref[:width, :], gs_ref[at, :]) * factor
         value = mm_t(g_ref[...], p_ref[at, :])
         part_refs[a][:lat, :] = (along[:lat] + value).astype(BF16)
@@ -226,7 +224,7 @@
     stats, refs = refs[:GROUP], refs[GROUP:]
     s_ref, gp_ref, g_ref, q_all_ref, part_ref, gs_ref, p_ref = refs
     pair_kernel(heads, *stats, s_ref, gp_ref, gs_ref, p_ref)
-    partial_kernel(factor, 1, width, g_ref, q_all_ref, gs_ref, p_ref, part_ref)
+    partial_kernel(factor, [slice(None)], width, g_ref, q_all_ref, gs_ref, p_ref, part_ref)
 
 
 def query_kernel(factor, nkey, width, heads, *refs):
@@ -433,14 +431,21 @@
     (gq_sum,) = call(join_kernel, "join", [(gq_shape, BF16)], [gq_across] + far_cuts)
     gq_core = swap(gq_core, 1)
     gq_last = swap(gq_sum, 2)
-    near_parts = call(
-        functools.partial(partial_kernel, factor, most, width),
-        "near_gradients",
-        [((width, tok), BF16)] * most,
-        [g, q_all, near_gs, near_p],
-        flops=2 * keys * all_rows * (width + lat),
-        share=0,
-    )
+    def partials(name, blocks, gs, p):
+        rows = [slice(m * tok, (m + 1) * tok) for m in blocks]
+        made = call(
+            functools.partial(partial_kernel, factor, rows, width),
+            name,
+            [((width, tok), BF16)] * len(blocks),
+            [g, q_all, gs, p],
+            flops=2 * len(blocks) * tok * all_rows * (width + lat),
+        )
+        return dict(zip(blocks, made))
+
+    middle = lines // 2
+    made = partials("middle_gradients", [middle], near_gs, near_p)
+    made.update(partials("near_gradients", [m for m in range(most) if m != middle], near_gs, near_p))
+    near_parts = [made[m] for m in range(most)]
     parts = list(near_parts) + [last_part]
     kept = [parts[0]]
     for bit in range(line_bits):

time: 53.5 us -> 53.8 us (level)
    pallas_call x12 -> x13, Pallas kernels: 12.6 us -> 12.8 us  [call(): pl.pallas_call(kernel, out_shape=[jax.ShapeDtypeStruct(s, d) for s, d in...]
where the time goes in v11:
time: 53.8 us; the launch traced here: 53.5 us
  starting transfers between devices  24.5 us (46%)
  Pallas kernels  12.8 us (24%)
  waiting for transfers between devices  11.7 us (22%)
  local copies, waits for them, and re-layouts  2.58 us (5%)
  other arithmetic  1.14 us (2%)
  between operations  0.81 us (2%)
    ppermute x24, starting transfers between devices, swap(): return lax.ppermute(x, axis, [(i, i ^ mask) for i in range(size)])  24.5 us
    pallas_call x13, Pallas kernels, call(): pl.pallas_call(kernel, out_shape=[jax.ShapeDtypeStruct(s, d) for s, d in...  12.8 us
    ppermute x24, waiting for transfers between devices, swap(): return lax.ppermute(x, axis, [(i, i ^ mask) for i in range(size)])  11.7 us
    unnamed x8, local copies, waits for them, and re-layouts  2.58 us
    convert_element_type x6, other arithmetic, add(): return (a.astype(F32) + b.astype(F32)).astype(BF16)  1.14 us
  transfers between devices with their start and end apart: 24, of which 9 were waited for; matrix products, arithmetic and copies ran while one was open for 2% of the time, Pallas kernels for 17%

profile of v11, /device:TPU:0, one launch (start us, length us, event | category | flops | bytes accessed | tf_op | source)
XLA Modules:
  0.0 53.5 jit_solution(16444138423251396713)
XLA Ops:
  0.6 3.0 %pack.1 = (bf16[592,128]{1,0:T(8,128)(2,1)}, bf16[1424,128]{1,0:T(8,128)(2,1)}, f32[8,128]{1,0:T(8,128)}, bf16[4,128,128]{2,1,0:T(8,128)(2,1)}, bf16[4,128,128]{2,1,0:T(8,128)(2,1)}) custom-call(s32[1]{0:T(128)} %bitcast.idx_ref, s32[1,128]{1,0:T(1,128)} %pos_hbm.1, bf16[2,576,128]{2,1,0:T(8,128)(2,1)} %bitcast.15, bf16[128,2,128]{2,1,0:T(2,128)(2,1)} %bitcast.20, ...), custom_call_target="tpu_custom_call" | custom-call | bytes 1815044 | tf_op jit(solution)/shard_map/pack/pallas_call | solution.py:40
  3.6 0.5 collective-permute-start
  4.1 0.1 collective-permute-start.4
  4.2 2.9 %collective-permute-start.1 = (bf16[1424,128]{1,0:T(8,128)(2,1)}, bf16[1424,128]{1,0:T(8,128)(2,1)S(1)}, u32[]{:S(2)}, u32[]{:S(2)}) collective-permute-start(bf16[1424,128]{1,0:T(8,128)(2,1)} %get-tuple-element.48.refs_1_), channel_id=1, source_target_pairs={{0,2},{1,3},{2,0},{3,1},{4,6},{5,7},{6,4},{7,5},{8,10},{9,11},{10,... | collective-permute-start | bytes 1093640 | tf_op jit(solution)/shard_map/ppermute | solution.py:293
  7.2 2.6 %collective-permute-start.3 = (bf16[592,128]{1,0:T(8,128)(2,1)}, bf16[592,128]{1,0:T(8,128)(2,1)S(1)}, u32[]{:S(2)}, u32[]{:S(2)}) collective-permute-start(bf16[592,128]{1,0:T(8,128)(2,1)} %get-tuple-element.50.refs_0_), channel_id=1, source_target_pairs={{0,8},{1,9},{2,10},{3,11},{4,12},{5,13},{6,14},{7,15},{8,0},{9,1},... | collective-permute-start | bytes 454664 | tf_op jit(solution)/shard_map/ppermute | solution.py:293
  9.7 0.0 collective-permute-done.refs_4_.refs_1_
  9.7 1.6 %collective-permute-start.2 = (bf16[592,128]{1,0:T(8,128)(2,1)}, bf16[592,128]{1,0:T(8,128)(2,1)S(1)}, u32[]{:S(2)}, u32[]{:S(2)}) collective-permute-start(bf16[592,128]{1,0:T(8,128)(2,1)} %get-tuple-element.50.refs_0_), channel_id=1, source_target_pairs={{0,4},{1,5},{2,6},{3,7},{4,0},{5,1},{6,2},{7,3},{8,12},{9,13},{10,... | collective-permute-start | bytes 454664 | tf_op jit(solution)/shard_map/ppermute | solution.py:293
  11.3 0.0 collective-permute-done.4
  11.3 0.9 %add_convert_fusion.5 = bf16[4,128,128]{2,1,0:T(8,128)(2,1)S(1)} fusion(bf16[4,128,128]{2,1,0:T(8,128)(2,1)S(1)} %collective-permute-done.4, bf16[4,128,128]{2,1,0:T(8,128)(2,1)} %get-tuple-element.51), kind=kLoop, calls=%fused_computation.5 | loop fusion | flops 262144 | bytes 393216 | tf_op jit(solution)/shard_map/convert_element_type | solution.py:341
  12.3 1.6 %collective-permute-start.5 = (bf16[4,128,128]{2,1,0:T(8,128)(2,1)S(1)}, bf16[4,128,128]{2,1,0:T(8,128)(2,1)S(1)}, u32[]{:S(2)}, u32[]{:S(2)}) collective-permute-start(bf16[4,128,128]{2,1,0:T(8,128)(2,1)S(1)} %add_convert_fusion.5), channel_id=1, source_target_pairs={{0,16},{16,0},{1,17},{17,1},{2,18},{18,2},{3,19},{19,3},{4,20},{20... | collective-permute-start | bytes 393224 | tf_op jit(solution)/shard_map/ppermute | solution.py:293
  13.8 1.0 %copy-done = bf16[1424,128]{1,0:T(8,128)(2,1)S(1)} copy-done((bf16[1424,128]{1,0:T(8,128)(2,1)S(1)}, bf16[1424,128]{1,0:T(8,128)(2,1)}, u32[]{:S(2)}) %copy-start) | copy-done | bytes 364568
  14.8 0.9 %copy-done.2 = bf16[592,128]{1,0:T(8,128)(2,1)S(1)} copy-done((bf16[592,128]{1,0:T(8,128)(2,1)S(1)}, bf16[592,128]{1,0:T(8,128)(2,1)}, u32[]{:S(2)}) %copy-start.2) | copy-done | bytes 151576
  15.7 0.7 %copy-done.3 = f32[8,128]{1,0:T(8,128)S(1)} copy-done((f32[8,128]{1,0:T(8,128)S(1)}, f32[8,128]{1,0:T(8,128)}, u32[]{:S(2)}) %copy-start.3) | copy-done | bytes 4120
  16.4 0.8 %collective-permute-done.3.refs_2_.refs_9_ = bf16[592,128]{1,0:T(8,128)(2,1)S(1)} collective-permute-done((bf16[592,128]{1,0:T(8,128)(2,1)}, bf16[592,128]{1,0:T(8,128)(2,1)S(1)}, u32[]{:S(2)}, u32[]{:S(2)}) %collective-permute-start.3) | collective-permute-done | bytes 151584 | tf_op jit(solution)/shard_map/ppermute | solution.py:293
  17.3 0.0 collective-permute-done.5
  17.3 0.0 collective-permute-done.1.refs_5_.refs_2_
  17.3 0.1 collective-permute-done.2.refs_1_.refs_8_
  17.5 0.0 collective-permute-start.7
  17.5 0.5 collective-permute-start.11
  18.0 1.5 %collective-permute-start.6 = (bf16[592,128]{1,0:T(8,128)(2,1)S(1)}, bf16[592,128]{1,0:T(8,128)(2,1)S(1)}, u32[]{:S(2)}, u32[]{:S(2)}) collective-permute-start(bf16[592,128]{1,0:T(8,128)(2,1)S(1)} %collective-permute-done.3.refs_2_.refs_9_), channel_id=1, source_target_pairs={{0,4},{1,5},{2,6},{3,7},{4,0},{5,1},{6,2},{7,3},{8,12},{9,13},{10,... | collective-permute-start | bytes 454664 | tf_op jit(solution)/shard_map/ppermute | solution.py:293
  19.5 0.0 collective-permute-done.7.refs_6_.refs_3_
  19.5 1.2 %near_scores.1 = (f32[384,1024]{1,0:T(8,128)S(1)}, bf16[384,640]{1,0:T(8,128)(2,1)S(1)}, f32[16,128]{1,0:T(8,128)S(1)}, bf16[640,1024]{1,0:T(8,128)(2,1)S(1)}) custom-call(bf16[592,128]{1,0:T(8,128)(2,1)S(1)} %get-tuple-element.58.refs_0_.refs_7_, bf16[592,128]{1,0:T(8,128)(2,1)S(1)} %collective-permute-done.2.refs_1_.refs_8_, ...), custom_call_target="tpu_custom_call" | custom-call | tf_op jit(solution)/shard_map/near_scores/pallas_call | solution.py:40
  20.8 0.0 copy-start.1
  20.8 2.7 %collective-permute-done.11 = bf16[4,128,128]{2,1,0:T(8,128)(2,1)S(1)} collective-permute-done((bf16[4,128,128]{2,1,0:T(8,128)(2,1)S(1)}, bf16[4,128,128]{2,1,0:T(8,128)(2,1)S(1)}, u32[]{:S(2)}, u32[]{:S(2)}) %collective-permute-start.11) | collective-permute-done | bytes 131104 | tf_op jit(solution)/shard_map/ppermute | solution.py:293
  23.5 1.5 %collective-permute-start.12 = (bf16[4,128,128]{2,1,0:T(8,128)(2,1)S(1)}, bf16[4,128,128]{2,1,0:T(8,128)(2,1)S(1)}, u32[]{:S(2)}, u32[]{:S(2)}) collective-permute-start(bf16[4,128,128]{2,1,0:T(8,128)(2,1)S(1)} %add_convert_fusion.3), channel_id=1, source_target_pairs={{0,4},{1,5},{2,6},{3,7},{4,0},{5,1},{6,2},{7,3},{8,12},{9,13},{10,... | collective-permute-start | bytes 393224 | tf_op jit(solution)/shard_map/ppermute | solution.py:293
  25.0 0.0 collective-permute-done.6.refs_0_.refs_10_
  25.0 0.5 last_scores.1
  25.5 0.1 collective-permute-start.8
  25.6 0.7 %collective-permute-start.9 = (f32[16,128]{1,0:T(8,128)S(1)}, f32[16,128]{1,0:T(8,128)S(1)}, u32[]{:S(2)}, u32[]{:S(2)}) collective-permute-start(f32[16,128]{1,0:T(8,128)S(1)} %get-tuple-element.66.refs_0_), channel_id=1, source_target_pairs={{0,2},{1,3},{2,0},{3,1},{4,6},{5,7},{6,4},{7,5},{8,10},{9,11},{10,... | collective-permute-start | bytes 24584 | tf_op jit(solution)/shard_map/ppermute | solution.py:293
  26.3 1.1 %collective-permute-start.10 = (f32[16,128]{1,0:T(8,128)S(1)}, f32[16,128]{1,0:T(8,128)S(1)}, u32[]{:S(2)}, u32[]{:S(2)}) collective-permute-start(f32[16,128]{1,0:T(8,128)S(1)} %get-tuple-element.66.refs_0_), channel_id=1, source_target_pairs={{0,3},{1,2},{2,1},{3,0},{4,7},{5,6},{6,5},{7,4},{8,11},{9,10},{10,... | collective-permute-start | bytes 24584 | tf_op jit(solution)/shard_map/ppermute | solution.py:293
  27.5 1.3 %collective-permute-done.12 = bf16[4,128,128]{2,1,0:T(8,128)(2,1)S(1)} collective-permute-done((bf16[4,128,128]{2,1,0:T(8,128)(2,1)S(1)}, bf16[4,128,128]{2,1,0:T(8,128)(2,1)S(1)}, u32[]{:S(2)}, u32[]{:S(2)}) %collective-permute-start.12) | collective-permute-done | bytes 131104 | tf_op jit(solution)/shard_map/ppermute | solution.py:293
  28.8 2.1 %collective-permute-start.13 = (bf16[4,128,128]{2,1,0:T(8,128)(2,1)S(1)}, bf16[4,128,128]{2,1,0:T(8,128)(2,1)S(1)}, u32[]{:S(2)}, u32[]{:S(2)}) collective-permute-start(bf16[4,128,128]{2,1,0:T(8,128)(2,1)S(1)} %add_convert_fusion.2), channel_id=1, source_target_pairs={{0,8},{1,9},{2,10},{3,11},{4,12},{5,13},{6,14},{7,15},{8,0},{9,1},... | collective-permute-start | bytes 393224 | tf_op jit(solution)/shard_map/ppermute | solution.py:293
  30.9 1.6 %context.1 = (bf16[512,1024]{1,0:T(8,128)(2,1)S(1)}, f32[384,1024]{1,0:T(8,128)S(1)}, f32[128,1024]{1,0:T(8,128)S(1)}) custom-call(bf16[1424,128]{1,0:T(8,128)(2,1)S(1)} %get-tuple-element.60.refs_3_.refs_0_, bf16[1424,128]{1,0:T(8,128)(2,1)S(1)} %collective-permute-done.refs_4_.refs_1_, bf16[1424,128]{1,0:T(8,128)(2,1)S(1)} %collective-permute-done.1.refs_5_.refs_2_, ...), custom_call_target="tpu_custom_call" | custom-call | flops 2013265920 | bytes 16564224 | tf_op jit(solution)/shard_map/context/pallas_call | solution.py:40
  32.5 0.0 collective-permute-done.8.refs_1_
  32.5 0.0 collective-permute-done.9.refs_2_
  32.5 0.0 collective-permute-done.10.refs_3_
  32.5 0.8 %last_gradients.1 = (bf16[576,128]{1,0:T(8,128)(2,1)S(1)}, bf16[128,1024]{1,0:T(8,128)(2,1)S(1)}) custom-call(f32[16,128]{1,0:T(8,128)S(1)} %get-tuple-element.66.refs_0_, f32[16,128]{1,0:T(8,128)S(1)} %collective-permute-done.8.refs_1_, f32[16,128]{1,0:T(8,128)S(1)} %collective-permute-done.9.refs_2_, f32[16,128]{1,0:T(8,128)S(1)} %collective-permute-done.10.refs_3_, ...), custom_call_target="tpu_custom_call" | custom-call | flops 285212672 | bytes 3850240 | tf_op jit(solution)/shard_map/last_gradients/pallas_call | solution.py:40
  33.3 1.8 %collective-permute-start.20 = (bf16[576,128]{1,0:T(8,128)(2,1)S(1)}, bf16[576,128]{1,0:T(8,128)(2,1)S(1)}, u32[]{:S(2)}, u32[]{:S(2)}) collective-permute-start(bf16[576,128]{1,0:T(8,128)(2,1)S(1)} %get-tuple-element.90), channel_id=1, source_target_pairs={{0,4},{1,5},{2,6},{3,7},{4,0},{5,1},{6,2},{7,3},{8,12},{9,13},{10,... | collective-permute-start | bytes 442376 | tf_op jit(solution)/shard_map/ppermute | solution.py:293
  35.1 2.0 %collective-permute-done.13 = bf16[4,128,128]{2,1,0:T(8,128)(2,1)S(1)} collective-permute-done((bf16[4,128,128]{2,1,0:T(8,128)(2,1)S(1)}, bf16[4,128,128]{2,1,0:T(8,128)(2,1)S(1)}, u32[]{:S(2)}, u32[]{:S(2)}) %collective-permute-start.13) | collective-permute-done | bytes 131104 | tf_op jit(solution)/shard_map/ppermute | solution.py:293
  37.2 1.1 %query_gradients.1 = (bf16[2,576,128]{2,1,0:T(8,128)(2,1)S(1)}, bf16[2,576,128]{2,1,0:T(8,128)(2,1)S(1)}, bf16[2,576,128]{2,1,0:T(8,128)(2,1)S(1)}, bf16[288,128...) custom-call(f32[16,128]{1,0:T(8,128)S(1)} %get-tuple-element.66.refs, ...), custom_call_target="tpu_custom_call" | custom-call | tf_op jit(solution)/shard_map/query_gradients/pallas_call | solution.py:40
  38.3 0.1 collective-permute-start.15
  38.4 0.5 collective-permute-start.16
  38.9 0.1 collective-permute-start.17
  39.0 0.4 collective-permute-start.18
  39.4 0.7 %middle_gradients.1 = bf16[576,128]{1,0:T(8,128)(2,1)S(1)} custom-call(bf16[512,1024]{1,0:T(8,128)(2,1)S(1)} %get-tuple-element.73.refs_6_.g_ref, bf16[640,1024]{1,0:T(8,128)(2,1)S(1)} %get-tuple-element.63.refs_1_.refs_7_.q_all_ref, bf16[384,1024]{1,0:T(8,128)(2,1)S(1)} %get-tuple-element.86.gs_ref, bf16[384,1024]{1,0:T(8,128)(2,1)S(1)} %get-tuple-element.87.p_ref), custom_call_target="tpu_custom_call" | custom-call | flops 285212672 | bytes 4079616 | tf_op jit(solution)/shard_map/middle_gradients/pallas_call | solution.py:40
  40.2 0.0 collective-permute-done.15.refs_0_
  40.2 0.1 collective-permute-start.14
  40.3 0.0 collective-permute-done.16.refs_1_
  40.3 0.0 collective-permute-done.17.refs_2_
  40.3 0.0 collective-permute-done.18.refs_3_
  40.3 0.1 join.1
  40.4 0.7 %collective-permute-start.19 = (bf16[2,576,128]{2,1,0:T(8,128)(2,1)S(1)}, bf16[2,576,128]{2,1,0:T(8,128)(2,1)S(1)}, u32[]{:S(2)}, u32[]{:S(2)}) collective-permute-start(bf16[2,576,128]{2,1,0:T(8,128)(2,1)S(1)} %join.1), channel_id=1, source_target_pairs={{0,2},{1,3},{2,0},{3,1},{4,6},{5,7},{6,4},{7,5},{8,10},{9,11},{10,... | collective-permute-start | bytes 884744 | tf_op jit(solution)/shard_map/ppermute | solution.py:293
  41.1 0.0 collective-permute-done.20
  41.2 0.1 collective-permute-start.21
  41.3 1.3 %near_gradients.1 = (bf16[576,128]{1,0:T(8,128)(2,1)S(1)}, bf16[576,128]{1,0:T(8,128)(2,1)S(1)}) custom-call(bf16[512,1024]{1,0:T(8,128)(2,1)S(1)} %get-tuple-element.73.refs_6_.g_ref, bf16[640,1024]{1,0:T(8,128)(2,1)S(1)} %get-tuple-element.63.refs_1_.refs_7_.q_all_ref, bf16[384,1024]{1,0:T(8,128)(2,1)S(1)} %get-tuple-element.86.gs_ref, ...), custom_call_target="tpu_custom_call" | custom-call | flops 570425344 | bytes 4227072 | tf_op jit(solution)/shard_map/near_gradients/pallas_call | solution.py:40
  42.6 3.9 %collective-permute-start.22 = (bf16[576,128]{1,0:T(8,128)(2,1)S(1)}, bf16[576,128]{1,0:T(8,128)(2,1)S(1)}, u32[]{:S(2)}, u32[]{:S(2)}) collective-permute-start(bf16[576,128]{1,0:T(8,128)(2,1)S(1)} %get-tuple-element.92), channel_id=1, source_target_pairs={{0,4},{1,5},{2,6},{3,7},{4,0},{5,1},{6,2},{7,3},{8,12},{9,13},{10,... | collective-permute-start | bytes 442376 | tf_op jit(solution)/shard_map/ppermute | solution.py:293
  46.5 1.3 %collective-permute-done.23.other_ref = bf16[4,128,128]{2,1,0:T(8,128)(2,1)S(1)} collective-permute-done((bf16[4,128,128]{2,1,0:T(8,128)(2,1)S(1)}, bf16[4,128,128]{2,1,0:T(8,128)(2,1)S(1)}, u32[]{:S(2)}, u32[]{:S(2)}) %collective-permute-start.23) | collective-permute-done | bytes 131104 | tf_op jit(solution)/shard_map/ppermute | solution.py:293
  47.8 0.8 %spread.1 = f32[2,512,128]{2,1,0:T(8,128)} custom-call(s32[1]{0:T(128)} %bitcast.idx_ref, bf16[4,128,128]{2,1,0:T(8,128)(2,1)S(1)} %add_convert_fusion.1.mine_ref, bf16[4,128,128]{2,1,0:T(8,128)(2,1)S(1)} %collective-permute-done.23.other_ref), custom_call_target="tpu_custom_call" | custom-call | bytes 786436 | tf_op jit(solution)/shard_map/spread/pallas_call | solution.py:40
  48.6 0.0 collective-permute-done.14.refs_1_
  48.6 1.2 %collective-permute-done.19.refs_2_ = bf16[2,576,128]{2,1,0:T(8,128)(2,1)S(1)} collective-permute-done((bf16[2,576,128]{2,1,0:T(8,128)(2,1)S(1)}, bf16[2,576,128]{2,1,0:T(8,128)(2,1)S(1)}, u32[]{:S(2)}, u32[]{:S(2)}) %collective-permute-start.19) | collective-permute-done | bytes 294944 | tf_op jit(solution)/shard_map/ppermute | solution.py:293
  49.8 0.8 %query_sum.1 = bf16[2,576,128]{2,1,0:T(8,128)(2,1)} custom-call(bf16[2,576,128]{2,1,0:T(8,128)(2,1)S(1)} %get-tuple-element.79.refs_0_, bf16[2,576,128]{2,1,0:T(8,128)(2,1)S(1)} %collective-permute-done.14.refs_1_, bf16[2,576,128]{2,1,0:T(8,128)(2,1)S(1)} %collective-permute-done.19.refs_2_), custom_call_target="tpu_custom_call" | custom-call | bytes 1179648 | tf_op jit(solution)/shard_map/query_sum/pallas_call | solution.py:40
  50.7 0.7 %collective-permute-done.21.refs_1_ = bf16[576,128]{1,0:T(8,128)(2,1)S(1)} collective-permute-done((bf16[576,128]{1,0:T(8,128)(2,1)S(1)}, bf16[576,128]{1,0:T(8,128)(2,1)S(1)}, u32[]{:S(2)}, u32[]{:S(2)}) %collective-permute-start.21) | collective-permute-done | bytes 147488 | tf_op jit(solution)/shard_map/ppermute | solution.py:293
  51.3 1.5 %collective-permute-done.22.refs_2_ = bf16[576,128]{1,0:T(8,128)(2,1)S(1)} collective-permute-done((bf16[576,128]{1,0:T(8,128)(2,1)S(1)}, bf16[576,128]{1,0:T(8,128)(2,1)S(1)}, u32[]{:S(2)}, u32[]{:S(2)}) %collective-permute-start.22) | collective-permute-done | bytes 147488 | tf_op jit(solution)/shard_map/ppermute | solution.py:293
  52.8 0.7 %latent_sum.1 = bf16[576,128]{1,0:T(8,128)(2,1)} custom-call(bf16[576,128]{1,0:T(8,128)(2,1)S(1)} %get-tuple-element.89.refs_0_, bf16[576,128]{1,0:T(8,128)(2,1)S(1)} %collective-permute-done.21.refs_1_, bf16[576,128]{1,0:T(8,128)(2,1)S(1)} %collective-permute-done.22.refs_2_), custom_call_target="tpu_custom_call" | custom-call | bytes 589824 | tf_op jit(solution)/shard_map/latent_sum/pallas_call | solution.py:40
  (11 shorter events, 0.2 us)
Async XLA Ops:
  3.6 6.1 %collective-permute-start = (bf16[1424,128]{1,0:T(8,128)(2,1)}, bf16[1424,128]{1,0:T(8,128)(2,1)S(1)}, u32[]{:S(2)}, u32[]{:S(2)}) collective-permute-start(bf16[1424,128]{1,0:T(8,128)(2,1)} %get-tuple-element.48.refs_1_), channel_id=1, source_target_pairs={{0,1},{1,0},{2,3},{3,2},{4,5},{5,4},{6,7},{7,6},{8,9},{9,8},{10,11... | collective-permute-start | bytes 1093640 | tf_op jit(solution)/shard_map/ppermute | solution.py:293
  4.1 7.2 %collective-permute-start.4 = (bf16[4,128,128]{2,1,0:T(8,128)(2,1)}, bf16[4,128,128]{2,1,0:T(8,128)(2,1)S(1)}, u32[]{:S(2)}, u32[]{:S(2)}) collective-permute-start(bf16[4,128,128]{2,1,0:T(8,128)(2,1)} %get-tuple-element.52), channel_id=1, source_target_pairs={{0,1},{1,0},{2,3},{3,2},{4,5},{5,4},{6,7},{7,6},{8,9},{9,8},{10,11... | collective-permute-start | bytes 393224 | tf_op jit(solution)/shard_map/ppermute | solution.py:293
  4.2 13.1 %collective-permute-start.1 = (bf16[1424,128]{1,0:T(8,128)(2,1)}, bf16[1424,128]{1,0:T(8,128)(2,1)S(1)}, u32[]{:S(2)}, u32[]{:S(2)}) collective-permute-start(bf16[1424,128]{1,0:T(8,128)(2,1)} %get-tuple-element.48.refs_1_), channel_id=1, source_target_pairs={{0,2},{1,3},{2,0},{3,1},{4,6},{5,7},{6,4},{7,5},{8,10},{9,11},{10,... | collective-permute-start | bytes 1093640 | tf_op jit(solution)/shard_map/ppermute | solution.py:293
  7.2 10.1 %collective-permute-start.3 = (bf16[592,128]{1,0:T(8,128)(2,1)}, bf16[592,128]{1,0:T(8,128)(2,1)S(1)}, u32[]{:S(2)}, u32[]{:S(2)}) collective-permute-start(bf16[592,128]{1,0:T(8,128)(2,1)} %get-tuple-element.50.refs_0_), channel_id=1, source_target_pairs={{0,8},{1,9},{2,10},{3,11},{4,12},{5,13},{6,14},{7,15},{8,0},{9,1},... | collective-permute-start | bytes 454664 | tf_op jit(solution)/shard_map/ppermute | solution.py:293
  9.7 7.7 %collective-permute-start.2 = (bf16[592,128]{1,0:T(8,128)(2,1)}, bf16[592,128]{1,0:T(8,128)(2,1)S(1)}, u32[]{:S(2)}, u32[]{:S(2)}) collective-permute-start(bf16[592,128]{1,0:T(8,128)(2,1)} %get-tuple-element.50.refs_0_), channel_id=1, source_target_pairs={{0,4},{1,5},{2,6},{3,7},{4,0},{5,1},{6,2},{7,3},{8,12},{9,13},{10,... | collective-permute-start | bytes 454664 | tf_op jit(solution)/shard_map/ppermute | solution.py:293
  12.3 5.0 %collective-permute-start.5 = (bf16[4,128,128]{2,1,0:T(8,128)(2,1)S(1)}, bf16[4,128,128]{2,1,0:T(8,128)(2,1)S(1)}, u32[]{:S(2)}, u32[]{:S(2)}) collective-permute-start(bf16[4,128,128]{2,1,0:T(8,128)(2,1)S(1)} %add_convert_fusion.5), channel_id=1, source_target_pairs={{0,16},{16,0},{1,17},{17,1},{2,18},{18,2},{3,19},{19,3},{4,20},{20... | collective-permute-start | bytes 393224 | tf_op jit(solution)/shard_map/ppermute | solution.py:293
  13.8 1.0 %copy-start = (bf16[1424,128]{1,0:T(8,128)(2,1)S(1)}, bf16[1424,128]{1,0:T(8,128)(2,1)}, u32[]{:S(2)}) copy-start(bf16[1424,128]{1,0:T(8,128)(2,1)} %get-tuple-element.48.refs_1_) | copy-start | bytes 1093636
  14.8 0.9 %copy-start.2 = (bf16[592,128]{1,0:T(8,128)(2,1)S(1)}, bf16[592,128]{1,0:T(8,128)(2,1)}, u32[]{:S(2)}) copy-start(bf16[592,128]{1,0:T(8,128)(2,1)} %get-tuple-element.50.refs_0_) | copy-start | bytes 454660
  15.7 0.7 %copy-start.3 = (f32[8,128]{1,0:T(8,128)S(1)}, f32[8,128]{1,0:T(8,128)}, u32[]{:S(2)}) copy-start(f32[8,128]{1,0:T(8,128)} %get-tuple-element.53.refs_2_) | copy-start | bytes 12292
  17.5 2.1 %collective-permute-start.7 = (bf16[1424,128]{1,0:T(8,128)(2,1)S(1)}, bf16[1424,128]{1,0:T(8,128)(2,1)S(1)}, u32[]{:S(2)}, u32[]{:S(2)}) collective-permute-start(bf16[1424,128]{1,0:T(8,128)(2,1)S(1)} %collective-permute-done.1.refs_5_.refs_2_), channel_id=1, source_target_pairs={{0,1},{1,0},{2,3},{3,2},{4,5},{5,4},{6,7},{7,6},{8,9},{9,8},{10,11... | collective-permute-start | bytes 1093640 | tf_op jit(solution)/shard_map/ppermute | solution.py:293
  17.5 6.0 %collective-permute-start.11 = (bf16[4,128,128]{2,1,0:T(8,128)(2,1)S(1)}, bf16[4,128,128]{2,1,0:T(8,128)(2,1)S(1)}, u32[]{:S(2)}, u32[]{:S(2)}) collective-permute-start(bf16[4,128,128]{2,1,0:T(8,128)(2,1)S(1)} %add_convert_fusion.4), channel_id=1, source_target_pairs={{0,2},{1,3},{2,0},{3,1},{4,6},{5,7},{6,4},{7,5},{8,10},{9,11},{10,... | collective-permute-start | bytes 393224 | tf_op jit(solution)/shard_map/ppermute | solution.py:293
  18.0 7.0 %collective-permute-start.6 = (bf16[592,128]{1,0:T(8,128)(2,1)S(1)}, bf16[592,128]{1,0:T(8,128)(2,1)S(1)}, u32[]{:S(2)}, u32[]{:S(2)}) collective-permute-start(bf16[592,128]{1,0:T(8,128)(2,1)S(1)} %collective-permute-done.3.refs_2_.refs_9_), channel_id=1, source_target_pairs={{0,4},{1,5},{2,6},{3,7},{4,0},{5,1},{6,2},{7,3},{8,12},{9,13},{10,... | collective-permute-start | bytes 454664 | tf_op jit(solution)/shard_map/ppermute | solution.py:293
  20.8 10.1 %copy-start.1 = (bf16[2,512,128]{2,1,0:T(8,128)(2,1)S(1)}, bf16[2,512,128]{2,1,0:T(8,128)(2,1)}, u32[]{:S(2)}) copy-start(bf16[2,512,128]{2,1,0:T(8,128)(2,1)} %refs_4_.1) | copy-start | bytes 786436
  23.5 5.2 %collective-permute-start.12 = (bf16[4,128,128]{2,1,0:T(8,128)(2,1)S(1)}, bf16[4,128,128]{2,1,0:T(8,128)(2,1)S(1)}, u32[]{:S(2)}, u32[]{:S(2)}) collective-permute-start(bf16[4,128,128]{2,1,0:T(8,128)(2,1)S(1)} %add_convert_fusion.3), channel_id=1, source_target_pairs={{0,4},{1,5},{2,6},{3,7},{4,0},{5,1},{6,2},{7,3},{8,12},{9,13},{10,... | collective-permute-start | bytes 393224 | tf_op jit(solution)/shard_map/ppermute | solution.py:293
  25.5 7.0 %collective-permute-start.8 = (f32[16,128]{1,0:T(8,128)S(1)}, f32[16,128]{1,0:T(8,128)S(1)}, u32[]{:S(2)}, u32[]{:S(2)}) collective-permute-start(f32[16,128]{1,0:T(8,128)S(1)} %get-tuple-element.66.refs_0_), channel_id=1, source_target_pairs={{0,1},{1,0},{2,3},{3,2},{4,5},{5,4},{6,7},{7,6},{8,9},{9,8},{10,11... | collective-permute-start | bytes 24584 | tf_op jit(solution)/shard_map/ppermute | solution.py:293
  25.6 6.9 %collective-permute-start.9 = (f32[16,128]{1,0:T(8,128)S(1)}, f32[16,128]{1,0:T(8,128)S(1)}, u32[]{:S(2)}, u32[]{:S(2)}) collective-permute-start(f32[16,128]{1,0:T(8,128)S(1)} %get-tuple-element.66.refs_0_), channel_id=1, source_target_pairs={{0,2},{1,3},{2,0},{3,1},{4,6},{5,7},{6,4},{7,5},{8,10},{9,11},{10,... | collective-permute-start | bytes 24584 | tf_op jit(solution)/shard_map/ppermute | solution.py:293
  26.3 6.2 %collective-permute-start.10 = (f32[16,128]{1,0:T(8,128)S(1)}, f32[16,128]{1,0:T(8,128)S(1)}, u32[]{:S(2)}, u32[]{:S(2)}) collective-permute-start(f32[16,128]{1,0:T(8,128)S(1)} %get-tuple-element.66.refs_0_), channel_id=1, source_target_pairs={{0,3},{1,2},{2,1},{3,0},{4,7},{5,6},{6,5},{7,4},{8,11},{9,10},{10,... | collective-permute-start | bytes 24584 | tf_op jit(solution)/shard_map/ppermute | solution.py:293
  28.8 8.4 %collective-permute-start.13 = (bf16[4,128,128]{2,1,0:T(8,128)(2,1)S(1)}, bf16[4,128,128]{2,1,0:T(8,128)(2,1)S(1)}, u32[]{:S(2)}, u32[]{:S(2)}) collective-permute-start(bf16[4,128,128]{2,1,0:T(8,128)(2,1)S(1)} %add_convert_fusion.2), channel_id=1, source_target_pairs={{0,8},{1,9},{2,10},{3,11},{4,12},{5,13},{6,14},{7,15},{8,0},{9,1},... | collective-permute-start | bytes 393224 | tf_op jit(solution)/shard_map/ppermute | solution.py:293
  33.3 7.8 %collective-permute-start.20 = (bf16[576,128]{1,0:T(8,128)(2,1)S(1)}, bf16[576,128]{1,0:T(8,128)(2,1)S(1)}, u32[]{:S(2)}, u32[]{:S(2)}) collective-permute-start(bf16[576,128]{1,0:T(8,128)(2,1)S(1)} %get-tuple-element.90), channel_id=1, source_target_pairs={{0,4},{1,5},{2,6},{3,7},{4,0},{5,1},{6,2},{7,3},{8,12},{9,13},{10,... | collective-permute-start | bytes 442376 | tf_op jit(solution)/shard_map/ppermute | solution.py:293
  38.3 1.8 %collective-permute-start.15 = (bf16[288,128]{1,0:T(8,128)(2,1)S(1)}, bf16[288,128]{1,0:T(8,128)(2,1)S(1)}, u32[]{:S(2)}, u32[]{:S(2)}) collective-permute-start(bf16[288,128]{1,0:T(8,128)(2,1)S(1)} %get-tuple-element.82), channel_id=1, source_target_pairs={{0,1},{1,0},{2,3},{3,2},{4,5},{5,4},{6,7},{7,6},{8,9},{9,8},{10,11... | collective-permute-start | bytes 221192 | tf_op jit(solution)/shard_map/ppermute | solution.py:293
  38.4 1.9 %collective-permute-start.16 = (bf16[288,128]{1,0:T(8,128)(2,1)S(1)}, bf16[288,128]{1,0:T(8,128)(2,1)S(1)}, u32[]{:S(2)}, u32[]{:S(2)}) collective-permute-start(bf16[288,128]{1,0:T(8,128)(2,1)S(1)} %get-tuple-element.83), channel_id=1, source_target_pairs={{0,1},{1,0},{2,3},{3,2},{4,5},{5,4},{6,7},{7,6},{8,9},{9,8},{10,11... | collective-permute-start | bytes 221192 | tf_op jit(solution)/shard_map/ppermute | solution.py:293
  38.9 1.4 %collective-permute-start.17 = (bf16[288,128]{1,0:T(8,128)(2,1)S(1)}, bf16[288,128]{1,0:T(8,128)(2,1)S(1)}, u32[]{:S(2)}, u32[]{:S(2)}) collective-permute-start(bf16[288,128]{1,0:T(8,128)(2,1)S(1)} %get-tuple-element.84), channel_id=1, source_target_pairs={{0,1},{1,0},{2,3},{3,2},{4,5},{5,4},{6,7},{7,6},{8,9},{9,8},{10,11... | collective-permute-start | bytes 221192 | tf_op jit(solution)/shard_map/ppermute | solution.py:293
  39.0 1.3 %collective-permute-start.18 = (bf16[288,128]{1,0:T(8,128)(2,1)S(1)}, bf16[288,128]{1,0:T(8,128)(2,1)S(1)}, u32[]{:S(2)}, u32[]{:S(2)}) collective-permute-start(bf16[288,128]{1,0:T(8,128)(2,1)S(1)} %get-tuple-element.85), channel_id=1, source_target_pairs={{0,1},{1,0},{2,3},{3,2},{4,5},{5,4},{6,7},{7,6},{8,9},{9,8},{10,11... | collective-permute-start | bytes 221192 | tf_op jit(solution)/shard_map/ppermute | solution.py:293
  40.2 8.5 %collective-permute-start.14 = (bf16[2,576,128]{2,1,0:T(8,128)(2,1)S(1)}, bf16[2,576,128]{2,1,0:T(8,128)(2,1)S(1)}, u32[]{:S(2)}, u32[]{:S(2)}) collective-permute-start(bf16[2,576,128]{2,1,0:T(8,128)(2,1)S(1)} %get-tuple-element.80), channel_id=1, source_target_pairs={{0,1},{1,0},{2,3},{3,2},{4,5},{5,4},{6,7},{7,6},{8,9},{9,8},{10,11... | collective-permute-start | bytes 884744 | tf_op jit(solution)/shard_map/ppermute | solution.py:293
  40.4 9.4 %collective-permute-start.19 = (bf16[2,576,128]{2,1,0:T(8,128)(2,1)S(1)}, bf16[2,576,128]{2,1,0:T(8,128)(2,1)S(1)}, u32[]{:S(2)}, u32[]{:S(2)}) collective-permute-start(bf16[2,576,128]{2,1,0:T(8,128)(2,1)S(1)} %join.1), channel_id=1, source_target_pairs={{0,2},{1,3},{2,0},{3,1},{4,6},{5,7},{6,4},{7,5},{8,10},{9,11},{10,... | collective-permute-start | bytes 884744 | tf_op jit(solution)/shard_map/ppermute | solution.py:293
  41.2 10.1 %collective-permute-start.21 = (bf16[576,128]{1,0:T(8,128)(2,1)S(1)}, bf16[576,128]{1,0:T(8,128)(2,1)S(1)}, u32[]{:S(2)}, u32[]{:S(2)}) collective-permute-start(bf16[576,128]{1,0:T(8,128)(2,1)S(1)} %add_convert_fusion), channel_id=1, source_target_pairs={{0,8},{1,9},{2,10},{3,11},{4,12},{5,13},{6,14},{7,15},{8,0},{9,1},... | collective-permute-start | bytes 442376 | tf_op jit(solution)/shard_map/ppermute | solution.py:293
  42.6 10.2 %collective-permute-start.22 = (bf16[576,128]{1,0:T(8,128)(2,1)S(1)}, bf16[576,128]{1,0:T(8,128)(2,1)S(1)}, u32[]{:S(2)}, u32[]{:S(2)}) collective-permute-start(bf16[576,128]{1,0:T(8,128)(2,1)S(1)} %get-tuple-element.92), channel_id=1, source_target_pairs={{0,4},{1,5},{2,6},{3,7},{4,0},{5,1},{6,2},{7,3},{8,12},{9,13},{10,... | collective-permute-start | bytes 442376 | tf_op jit(solution)/shard_map/ppermute | solution.py:293
  46.5 1.3 %collective-permute-start.23 = (bf16[4,128,128]{2,1,0:T(8,128)(2,1)S(1)}, bf16[4,128,128]{2,1,0:T(8,128)(2,1)S(1)}, u32[]{:S(2)}, u32[]{:S(2)}) collective-permute-start(bf16[4,128,128]{2,1,0:T(8,128)(2,1)S(1)} %add_convert_fusion.1.mine_ref), channel_id=1, source_target_pairs={{0,1},{1,0},{2,3},{3,2},{4,5},{5,4},{6,7},{7,6},{8,9},{9,8},{10,11... | collective-permute-start | bytes 393224 | tf_op jit(solution)/shard_map/ppermute | solution.py:293

commit v12 on v11

--- a/solution.py
+++ b/solution.py
@@ -101,13 +101,11 @@
     for h in range(heads):
         term[h] = mm_t(attn[h], og_t_ref[h])
     step = lat // GROUP
-    side = lax.rem(idx_ref[0], 2)
-    for i in range(GROUP // 2):
-        rows = slice(i * heads, (i + 1) * heads)
-        at = pl.multiple_of((2 * i + side) * step, step)
-        keep_ref[rows] = term[:, pl.ds(at, step), :].astype(BF16)
-        at = pl.multiple_of((2 * i + 1 - side) * step, step)
-        send_ref[rows] = term[:, pl.ds(at, step), :].astype(BF16)
+    me = lax.rem(idx_ref[0], GROUP)
+    for k in range(GROUP):
+        at = pl.multiple_of(jnp.bitwise_xor(me, k) * step, step)
+        target = send_ref if k % 2 else keep_ref
+        target[k // 2 * heads : (k // 2 + 1) * heads] = term[:, pl.ds(at, step), :].astype(BF16)
     send_off(send_ref, send_hbm)
     send_off(keep_ref, keep_hbm)
     started[3].wait()
@@ -266,16 +264,13 @@
     refs[-1][...] = sum(ref[...].astype(F32) for ref in refs[:-1]).astype(BF16)
 
 
-def spread_kernel(scale, idx_ref, mine_ref, other_ref, out_ref):
-    heads, lat, _ = out_ref.shape
-    step = lat // GROUP
-    side = lax.rem(idx_ref[0], 2)
-    for i in range(GROUP // 2):
-        rows = slice(i * heads, (i + 1) * heads)
-        at = pl.multiple_of((2 * i + side) * step, step)
-        out_ref[:, pl.ds(at, step), :] = mine_ref[rows].astype(F32) * scale
-        at = pl.multiple_of((2 * i + 1 - side) * step, step)
-        out_ref[:, pl.ds(at, step), :] = other_ref[rows].astype(F32) * scale
+def spread_kernel(scale, idx_ref, *refs):
+    chunks, out_ref = refs[:GROUP], refs[GROUP]
+    step = chunks[0].shape[1]
+    me = lax.rem(idx_ref[0], GROUP)
+    for k in range(GROUP):
+        at = pl.multiple_of(jnp.bitwise_xor(me, k) * step, step)
+        out_ref[:, pl.ds(at, step), :] = chunks[k][...].astype(F32) * scale
 
 
 def body(n_ctx, n_dp, positions, queries, latent, out_grad, attn_out, wuv):
@@ -367,7 +362,7 @@
         pair = add(pair, swap(pair, *step_hop))
     lats = [held[m] for m in range(lines)]
     q_far = swap(q_across, 1)
-    got_across = swap(pair, 2)
+    got_own = swap(pair[heads:], 2)
     lat_own, q_own, delta = own
     lats[0] = lat_own
     qs = [q_own, q_core, q_across, q_far]
@@ -384,7 +379,7 @@
         flops=most * score_flops,
         share=0,
     )
-    mine = add(pair, after(got_across, near_stat))
+    mine = add(pair[:heads], after(got_own, near_stat))
     near = swap(mine, *line_hops[0])
     last_s, last_k, stat = call(
         functools.partial(score_kernel, factor, 1, width, heads, True),
@@ -427,8 +422,9 @@
         flops=2 * lines * tok * all_rows * width,
         share=0,
     )
+    across = swap(mine, 2)
     far_cuts = [swap(cut, 1) for cut in far_cuts]
-    (gq_sum,) = call(join_kernel, "join", [(gq_shape, BF16)], [gq_across] + far_cuts)
+    (gq_sum,) = call(join_kernel, "join", [(gq_shape, BF16)], [after(gq_across, across)] + far_cuts)
     gq_core = swap(gq_core, 1)
     gq_last = swap(gq_sum, 2)
     def partials(name, blocks, gs, p):
@@ -444,7 +440,7 @@
 
     middle = lines // 2
     made = partials("middle_gradients", [middle], near_gs, near_p)
-    made.update(partials("near_gradients", [m for m in range(most) if m != middle], near_gs, near_p))
+    made.update(partials("near_gradients", [m for m in range(most) if m != middle], near_gs, after(near_p, made[middle])))
     near_parts = [made[m] for m in range(most)]
     parts = list(near_parts) + [last_part]
     kept = [parts[0]]
@@ -452,7 +448,9 @@
         for m in range(3 << bit, lines, 2 << bit):
             got = last_got if m == most and bit == 0 else swap(parts[m], GROUP << bit)
             parts[m ^ 1 << bit] = add(parts[m ^ 1 << bit], got)
-    other = swap(mine, 1)
+    mine_two = jnp.concatenate([mine, across], axis=0)
+    other_two = swap(mine_two, 1)
+    pieces = [mine_two[:heads], other_two[:heads], mine_two[heads:], other_two[heads:]]
     parts[1] = after(parts[1], gq_sum)
     kept += [swap(parts[1 << bit], GROUP << bit) for bit in reversed(range(line_bits))]
     scale = 1.0 / math.sqrt(tok * n_ctx * n_dp)
@@ -460,7 +458,7 @@
         functools.partial(spread_kernel, scale),
         "spread",
         [((heads, lat, HEAD_DIM), F32)],
-        [idx, mine, other],
+        [idx] + pieces,
         smem=(0,),
     )
     gq_pieces = [gq_own, gq_core, gq_last]

time: 53.8 us -> 52.5 us (0.976)
  waiting for transfers between devices: 11.7 us -> 8.38 us
  starting transfers between devices: 24.5 us -> 26.7 us
    ppermute x24 -> x25, waiting for transfers between devices: 11.7 us -> 8.38 us  [swap(): return lax.ppermute(x, axis, [(i, i ^ mask) for i in range(size)])]
    ppermute x24 -> x25, starting transfers between devices: 24.5 us -> 26.7 us  [swap(): return lax.ppermute(x, axis, [(i, i ^ mask) for i in range(size)])]
  transfers between devices with their start and end apart: 24 -> 25, of which waited for: 9 -> 10; matrix products, arithmetic and copies ran while one was open for 2% -> 2% of each run, Pallas kernels for 17% -> 17%
where the time goes in v12:
time: 52.5 us; the launch traced here: 52.3 us
  starting transfers between devices  26.7 us (51%)
  Pallas kernels  12.7 us (24%)
  waiting for transfers between devices  8.38 us (16%)
  local copies, waits for them, and re-layouts  2.58 us (5%)
  other arithmetic  1.1 us (2%)
  between operations  0.81 us (2%)
    ppermute x25, starting transfers between devices, swap(): return lax.ppermute(x, axis, [(i, i ^ mask) for i in range(size)])  26.7 us
    pallas_call x13, Pallas kernels, call(): pl.pallas_call(kernel, out_shape=[jax.ShapeDtypeStruct(s, d) for s, d in...  12.7 us
    ppermute x25, waiting for transfers between devices, swap(): return lax.ppermute(x, axis, [(i, i ^ mask) for i in range(size)])  8.38 us
    unnamed x8, local copies, waits for them, and re-layouts  2.57 us
    convert_element_type x6, other arithmetic, add(): return (a.astype(F32) + b.astype(F32)).astype(BF16)  1.09 us
  transfers between devices with their start and end apart: 25, of which 10 were waited for; matrix products, arithmetic and copies ran while one was open for 2% of the time, Pallas kernels for 17%

profile of v12, /device:TPU:0, one launch (start us, length us, event | category | flops | bytes accessed | tf_op | source)
XLA Modules:
  0.0 52.3 jit_solution(7919165427880816965)
XLA Ops:
  0.6 2.9 %pack.1 = (bf16[592,128]{1,0:T(8,128)(2,1)}, bf16[1424,128]{1,0:T(8,128)(2,1)}, f32[8,128]{1,0:T(8,128)}, bf16[4,128,128]{2,1,0:T(8,128)(2,1)}, bf16[4,128,128]{2,1,0:T(8,128)(2,1)}) custom-call(s32[1]{0:T(128)} %bitcast.idx_ref, s32[1,128]{1,0:T(1,128)} %pos_hbm.1, bf16[2,576,128]{2,1,0:T(8,128)(2,1)} %bitcast.15, bf16[128,2,128]{2,1,0:T(2,128)(2,1)} %bitcast.20, ...), custom_call_target="tpu_custom_call" | custom-call | bytes 1815044 | tf_op jit(solution)/shard_map/pack/pallas_call | solution.py:40
  3.6 0.5 collective-permute-start
  4.1 0.1 collective-permute-start.4
  4.2 2.9 %collective-permute-start.1 = (bf16[1424,128]{1,0:T(8,128)(2,1)}, bf16[1424,128]{1,0:T(8,128)(2,1)S(1)}, u32[]{:S(2)}, u32[]{:S(2)}) collective-permute-start(bf16[1424,128]{1,0:T(8,128)(2,1)} %get-tuple-element.50.refs_1_), channel_id=1, source_target_pairs={{0,2},{1,3},{2,0},{3,1},{4,6},{5,7},{6,4},{7,5},{8,10},{9,11},{10,... | collective-permute-start | bytes 1093640 | tf_op jit(solution)/shard_map/ppermute | solution.py:288
  7.1 2.6 %collective-permute-start.3 = (bf16[592,128]{1,0:T(8,128)(2,1)}, bf16[592,128]{1,0:T(8,128)(2,1)S(1)}, u32[]{:S(2)}, u32[]{:S(2)}) collective-permute-start(bf16[592,128]{1,0:T(8,128)(2,1)} %get-tuple-element.52.refs_0_), channel_id=1, source_target_pairs={{0,8},{1,9},{2,10},{3,11},{4,12},{5,13},{6,14},{7,15},{8,0},{9,1},... | collective-permute-start | bytes 454664 | tf_op jit(solution)/shard_map/ppermute | solution.py:288
  9.7 0.0 collective-permute-done.refs_4_.refs_1_
  9.7 1.6 %collective-permute-start.2 = (bf16[592,128]{1,0:T(8,128)(2,1)}, bf16[592,128]{1,0:T(8,128)(2,1)S(1)}, u32[]{:S(2)}, u32[]{:S(2)}) collective-permute-start(bf16[592,128]{1,0:T(8,128)(2,1)} %get-tuple-element.52.refs_0_), channel_id=1, source_target_pairs={{0,4},{1,5},{2,6},{3,7},{4,0},{5,1},{6,2},{7,3},{8,12},{9,13},{10,... | collective-permute-start | bytes 454664 | tf_op jit(solution)/shard_map/ppermute | solution.py:288
  11.3 0.0 collective-permute-done.4
  11.3 0.9 %add_convert_fusion.2 = bf16[4,128,128]{2,1,0:T(8,128)(2,1)S(1)} fusion(bf16[4,128,128]{2,1,0:T(8,128)(2,1)S(1)} %collective-permute-done.4, bf16[4,128,128]{2,1,0:T(8,128)(2,1)} %get-tuple-element.53), kind=kLoop, calls=%fused_computation.2 | loop fusion | flops 262144 | bytes 393216 | tf_op jit(solution)/shard_map/convert_element_type | solution.py:336
  12.2 1.6 %collective-permute-start.5 = (bf16[4,128,128]{2,1,0:T(8,128)(2,1)S(1)}, bf16[4,128,128]{2,1,0:T(8,128)(2,1)S(1)}, u32[]{:S(2)}, u32[]{:S(2)}) collective-permute-start(bf16[4,128,128]{2,1,0:T(8,128)(2,1)S(1)} %add_convert_fusion.2), channel_id=1, source_target_pairs={{0,16},{16,0},{1,17},{17,1},{2,18},{18,2},{3,19},{19,3},{4,20},{20... | collective-permute-start | bytes 393224 | tf_op jit(solution)/shard_map/ppermute | solution.py:288
  13.8 1.0 %copy-done = bf16[1424,128]{1,0:T(8,128)(2,1)S(1)} copy-done((bf16[1424,128]{1,0:T(8,128)(2,1)S(1)}, bf16[1424,128]{1,0:T(8,128)(2,1)}, u32[]{:S(2)}) %copy-start) | copy-done | bytes 364568
  14.8 0.9 %copy-done.2 = bf16[592,128]{1,0:T(8,128)(2,1)S(1)} copy-done((bf16[592,128]{1,0:T(8,128)(2,1)S(1)}, bf16[592,128]{1,0:T(8,128)(2,1)}, u32[]{:S(2)}) %copy-start.2) | copy-done | bytes 151576
  15.7 0.7 %copy-done.3 = f32[8,128]{1,0:T(8,128)S(1)} copy-done((f32[8,128]{1,0:T(8,128)S(1)}, f32[8,128]{1,0:T(8,128)}, u32[]{:S(2)}) %copy-start.3) | copy-done | bytes 4120
  16.4 0.8 %collective-permute-done.3.refs_2_.refs_9_ = bf16[592,128]{1,0:T(8,128)(2,1)S(1)} collective-permute-done((bf16[592,128]{1,0:T(8,128)(2,1)}, bf16[592,128]{1,0:T(8,128)(2,1)S(1)}, u32[]{:S(2)}, u32[]{:S(2)}) %collective-permute-start.3) | collective-permute-done | bytes 151584 | tf_op jit(solution)/shard_map/ppermute | solution.py:288
  17.2 0.1 collective-permute-done.5
  17.3 0.0 collective-permute-done.1.refs_5_.refs_2_
  17.3 0.1 collective-permute-done.2.refs_1_.refs_8_
  17.4 0.0 collective-permute-start.7
  17.5 0.0 copy-start.1
  17.5 0.5 %collective-permute-start.11 = (bf16[2,128,128]{2,1,0:T(8,128)(2,1)S(1)}, bf16[2,128,128]{2,1,0:T(8,128)(2,1)S(1)}, u32[]{:S(2)}, u32[]{:S(2)}) collective-permute-start(bf16[2,128,128]{2,1,0:T(8,128)(2,1)S(1)} %slice.17), channel_id=1, source_target_pairs={{0,2},{1,3},{2,0},{3,1},{4,6},{5,7},{6,4},{7,5},{8,10},{9,11},{10,... | collective-permute-start | bytes 196616 | tf_op jit(solution)/shard_map/ppermute | solution.py:288
  18.0 1.5 %collective-permute-start.6 = (bf16[592,128]{1,0:T(8,128)(2,1)S(1)}, bf16[592,128]{1,0:T(8,128)(2,1)S(1)}, u32[]{:S(2)}, u32[]{:S(2)}) collective-permute-start(bf16[592,128]{1,0:T(8,128)(2,1)S(1)} %collective-permute-done.3.refs_2_.refs_9_), channel_id=1, source_target_pairs={{0,4},{1,5},{2,6},{3,7},{4,0},{5,1},{6,2},{7,3},{8,12},{9,13},{10,... | collective-permute-start | bytes 454664 | tf_op jit(solution)/shard_map/ppermute | solution.py:288
  19.5 0.0 collective-permute-done.7.refs_6_.refs_3_
  19.5 1.2 %near_scores.1 = (f32[384,1024]{1,0:T(8,128)S(1)}, bf16[384,640]{1,0:T(8,128)(2,1)S(1)}, f32[16,128]{1,0:T(8,128)S(1)}, bf16[640,1024]{1,0:T(8,128)(2,1)S(1)}) custom-call(bf16[592,128]{1,0:T(8,128)(2,1)S(1)} %get-tuple-element.60.refs_0_.refs_7_, bf16[592,128]{1,0:T(8,128)(2,1)S(1)} %collective-permute-done.2.refs_1_.refs_8_, ...), custom_call_target="tpu_custom_call" | custom-call | tf_op jit(solution)/shard_map/near_scores/pallas_call | solution.py:40
  20.7 1.3 %collective-permute-done.11 = bf16[2,128,128]{2,1,0:T(8,128)(2,1)S(1)} collective-permute-done((bf16[2,128,128]{2,1,0:T(8,128)(2,1)S(1)}, bf16[2,128,128]{2,1,0:T(8,128)(2,1)S(1)}, u32[]{:S(2)}, u32[]{:S(2)}) %collective-permute-start.11) | collective-permute-done | bytes 65568 | tf_op jit(solution)/shard_map/ppermute | solution.py:288
  22.1 1.5 %collective-permute-start.12 = (bf16[2,128,128]{2,1,0:T(8,128)(2,1)S(1)}, bf16[2,128,128]{2,1,0:T(8,128)(2,1)S(1)}, u32[]{:S(2)}, u32[]{:S(2)}) collective-permute-start(bf16[2,128,128]{2,1,0:T(8,128)(2,1)S(1)} %add_convert_fusion.5), channel_id=1, source_target_pairs={{0,4},{1,5},{2,6},{3,7},{4,0},{5,1},{6,2},{7,3},{8,12},{9,13},{10,... | collective-permute-start | bytes 196616 | tf_op jit(solution)/shard_map/ppermute | solution.py:288
  23.6 0.5 collective-permute-done.6.refs_0_.refs_10_
  24.1 0.5 last_scores.1
  24.6 0.1 collective-permute-start.8
  24.7 2.3 %collective-permute-start.9 = (f32[16,128]{1,0:T(8,128)S(1)}, f32[16,128]{1,0:T(8,128)S(1)}, u32[]{:S(2)}, u32[]{:S(2)}) collective-permute-start(f32[16,128]{1,0:T(8,128)S(1)} %get-tuple-element.68.refs_0_), channel_id=1, source_target_pairs={{0,2},{1,3},{2,0},{3,1},{4,6},{5,7},{6,4},{7,5},{8,10},{9,11},{10,... | collective-permute-start | bytes 24584 | tf_op jit(solution)/shard_map/ppermute | solution.py:288
  27.0 0.1 collective-permute-start.10
  27.1 2.1 %collective-permute-start.13 = (bf16[2,128,128]{2,1,0:T(8,128)(2,1)S(1)}, bf16[2,128,128]{2,1,0:T(8,128)(2,1)S(1)}, u32[]{:S(2)}, u32[]{:S(2)}) collective-permute-start(bf16[2,128,128]{2,1,0:T(8,128)(2,1)S(1)} %add_convert_fusion.4), channel_id=1, source_target_pairs={{0,8},{1,9},{2,10},{3,11},{4,12},{5,13},{6,14},{7,15},{8,0},{9,1},... | collective-permute-start | bytes 196616 | tf_op jit(solution)/shard_map/ppermute | solution.py:288
  29.2 1.6 %context.1 = (bf16[512,1024]{1,0:T(8,128)(2,1)S(1)}, f32[384,1024]{1,0:T(8,128)S(1)}, f32[128,1024]{1,0:T(8,128)S(1)}) custom-call(bf16[1424,128]{1,0:T(8,128)(2,1)S(1)} %get-tuple-element.62.refs_3_.refs_0_, bf16[1424,128]{1,0:T(8,128)(2,1)S(1)} %collective-permute-done.refs_4_.refs_1_, bf16[1424,128]{1,0:T(8,128)(2,1)S(1)} %collective-permute-done.1.refs_5_.refs_2_, ...), custom_call_target="tpu_custom_call" | custom-call | flops 2013265920 | bytes 16564224 | tf_op jit(solution)/shard_map/context/pallas_call | solution.py:40
  30.8 0.0 collective-permute-done.9.refs_2_
  30.8 0.0 collective-permute-done.10.refs_3_
  30.8 0.8 %last_gradients.1 = (bf16[576,128]{1,0:T(8,128)(2,1)S(1)}, bf16[128,1024]{1,0:T(8,128)(2,1)S(1)}) custom-call(f32[16,128]{1,0:T(8,128)S(1)} %get-tuple-element.68.refs_0_, f32[16,128]{1,0:T(8,128)S(1)} %collective-permute-done.8.refs_1_, f32[16,128]{1,0:T(8,128)S(1)} %collective-permute-done.9.refs_2_, f32[16,128]{1,0:T(8,128)S(1)} %collective-permute-done.10.refs_3_, ...), custom_call_target="tpu_custom_call" | custom-call | flops 285212672 | bytes 3850240 | tf_op jit(solution)/shard_map/last_gradients/pallas_call | solution.py:40
  31.6 1.7 %collective-permute-start.21 = (bf16[576,128]{1,0:T(8,128)(2,1)S(1)}, bf16[576,128]{1,0:T(8,128)(2,1)S(1)}, u32[]{:S(2)}, u32[]{:S(2)}) collective-permute-start(bf16[576,128]{1,0:T(8,128)(2,1)S(1)} %get-tuple-element.94), channel_id=1, source_target_pairs={{0,4},{1,5},{2,6},{3,7},{4,0},{5,1},{6,2},{7,3},{8,12},{9,13},{10,... | collective-permute-start | bytes 442376 | tf_op jit(solution)/shard_map/ppermute | solution.py:288
  33.3 0.3 collective-permute-done.13
  33.7 2.0 %collective-permute-start.15 = (bf16[2,128,128]{2,1,0:T(8,128)(2,1)S(1)}, bf16[2,128,128]{2,1,0:T(8,128)(2,1)S(1)}, u32[]{:S(2)}, u32[]{:S(2)}) collective-permute-start(bf16[2,128,128]{2,1,0:T(8,128)(2,1)S(1)} %add_convert_fusion.3.refs_0_), channel_id=1, source_target_pairs={{0,2},{1,3},{2,0},{3,1},{4,6},{5,7},{6,4},{7,5},{8,10},{9,11},{10,... | collective-permute-start | bytes 196616 | tf_op jit(solution)/shard_map/ppermute | solution.py:288
  35.6 1.1 %query_gradients.1 = (bf16[2,576,128]{2,1,0:T(8,128)(2,1)S(1)}, bf16[2,576,128]{2,1,0:T(8,128)(2,1)S(1)}, bf16[2,576,128]{2,1,0:T(8,128)(2,1)S(1)}, bf16[288,128...) custom-call(f32[16,128]{1,0:T(8,128)S(1)} %get-tuple-element.68.refs, ...), custom_call_target="tpu_custom_call" | custom-call | tf_op jit(solution)/shard_map/query_gradients/pallas_call | solution.py:40
  36.8 0.1 collective-permute-start.16
  36.9 0.5 collective-permute-start.17
  37.4 0.1 collective-permute-start.18
  37.4 0.7 %middle_gradients.1 = bf16[576,128]{1,0:T(8,128)(2,1)S(1)} custom-call(bf16[512,1024]{1,0:T(8,128)(2,1)S(1)} %get-tuple-element.75.refs_6_.g_ref, bf16[640,1024]{1,0:T(8,128)(2,1)S(1)} %get-tuple-element.65.refs_1_.refs_7_.q_all_ref, bf16[384,1024]{1,0:T(8,128)(2,1)S(1)} %get-tuple-element.89.gs_ref, bf16[384,1024]{1,0:T(8,128)(2,1)S(1)} %get-tuple-element.91.p_ref), custom_call_target="tpu_custom_call" | custom-call | flops 285212672 | bytes 4079616 | tf_op jit(solution)/shard_map/middle_gradients/pallas_call | solution.py:40
  38.2 1.3 %near_gradients.1 = (bf16[576,128]{1,0:T(8,128)(2,1)S(1)}, bf16[576,128]{1,0:T(8,128)(2,1)S(1)}) custom-call(bf16[512,1024]{1,0:T(8,128)(2,1)S(1)} %get-tuple-element.75.refs_6_.g_ref, bf16[640,1024]{1,0:T(8,128)(2,1)S(1)} %get-tuple-element.65.refs_1_.refs_7_.q_all_ref, bf16[384,1024]{1,0:T(8,128)(2,1)S(1)} %get-tuple-element.89.gs_ref, ...), custom_call_target="tpu_custom_call" | custom-call | flops 570425344 | bytes 4227072 | tf_op jit(solution)/shard_map/near_gradients/pallas_call | solution.py:40
  39.5 0.0 collective-permute-done.15.refs_2_
  39.5 0.5 collective-permute-start.19
  40.0 0.0 collective-permute-done.16.refs_0_
  40.0 0.1 collective-permute-start.14
  40.2 0.0 collective-permute-done.17.refs_1_
  40.2 0.4 collective-permute-start.24
  40.6 0.0 collective-permute-done.18.refs_2_
  40.6 0.3 collective-permute-done.19.refs_3_
  40.9 0.1 join.1
  41.0 0.3 collective-permute-start.20
  41.3 0.0 collective-permute-done.21
  41.4 0.8 %collective-permute-start.22 = (bf16[576,128]{1,0:T(8,128)(2,1)S(1)}, bf16[576,128]{1,0:T(8,128)(2,1)S(1)}, u32[]{:S(2)}, u32[]{:S(2)}) collective-permute-start(bf16[576,128]{1,0:T(8,128)(2,1)S(1)} %add_convert_fusion), channel_id=1, source_target_pairs={{0,8},{1,9},{2,10},{3,11},{4,12},{5,13},{6,14},{7,15},{8,0},{9,1},... | collective-permute-start | bytes 442376 | tf_op jit(solution)/shard_map/ppermute | solution.py:288
  42.2 2.8 %collective-permute-start.23 = (bf16[576,128]{1,0:T(8,128)(2,1)S(1)}, bf16[576,128]{1,0:T(8,128)(2,1)S(1)}, u32[]{:S(2)}, u32[]{:S(2)}) collective-permute-start(bf16[576,128]{1,0:T(8,128)(2,1)S(1)} %get-tuple-element.96), channel_id=1, source_target_pairs={{0,4},{1,5},{2,6},{3,7},{4,0},{5,1},{6,2},{7,3},{8,12},{9,13},{10,... | collective-permute-start | bytes 442376 | tf_op jit(solution)/shard_map/ppermute | solution.py:288
  45.0 0.8 %spread.1 = f32[2,512,128]{2,1,0:T(8,128)} custom-call(s32[1]{0:T(128)} %bitcast.idx_ref, bf16[2,128,128]{2,1,0:T(8,128)(2,1)S(1)} %add_convert_fusion.3.refs_0_, bf16[2,128,128]{2,1,0:T(8,128)(2,1)S(1)} %get-tuple-element.98.refs_1_, bf16[2,128,128]{2,1,0:T(8,128)(2,1)S(1)} %collective-permute-done.15.refs_2_, ...), custom_call_target="tpu_custom_call" | custom-call | bytes 786436 | tf_op jit(solution)/shard_map/spread/pallas_call | solution.py:40
  45.8 0.0 collective-permute-done.14.refs_1_
  45.8 4.5 %collective-permute-done.20.refs_2_ = bf16[2,576,128]{2,1,0:T(8,128)(2,1)S(1)} collective-permute-done((bf16[2,576,128]{2,1,0:T(8,128)(2,1)S(1)}, bf16[2,576,128]{2,1,0:T(8,128)(2,1)S(1)}, u32[]{:S(2)}, u32[]{:S(2)}) %collective-permute-start.20) | collective-permute-done | bytes 294944 | tf_op jit(solution)/shard_map/ppermute | solution.py:288
  50.3 0.8 %query_sum.1 = bf16[2,576,128]{2,1,0:T(8,128)(2,1)} custom-call(bf16[2,576,128]{2,1,0:T(8,128)(2,1)S(1)} %get-tuple-element.81.refs_0_, bf16[2,576,128]{2,1,0:T(8,128)(2,1)S(1)} %collective-permute-done.14.refs_1_, bf16[2,576,128]{2,1,0:T(8,128)(2,1)S(1)} %collective-permute-done.20.refs_2_), custom_call_target="tpu_custom_call" | custom-call | bytes 1179648 | tf_op jit(solution)/shard_map/query_sum/pallas_call | solution.py:40
  51.2 0.3 collective-permute-done.22.refs_1_
  51.5 0.1 collective-permute-done.23.refs_2_
  51.6 0.7 %latent_sum.1 = bf16[576,128]{1,0:T(8,128)(2,1)} custom-call(bf16[576,128]{1,0:T(8,128)(2,1)S(1)} %get-tuple-element.93.refs_0_, bf16[576,128]{1,0:T(8,128)(2,1)S(1)} %collective-permute-done.22.refs_1_, bf16[576,128]{1,0:T(8,128)(2,1)S(1)} %collective-permute-done.23.refs_2_), custom_call_target="tpu_custom_call" | custom-call | bytes 589824 | tf_op jit(solution)/shard_map/latent_sum/pallas_call | solution.py:40
  (16 shorter events, 0.2 us)
Async XLA Ops:
  3.6 6.1 %collective-permute-start = (bf16[1424,128]{1,0:T(8,128)(2,1)}, bf16[1424,128]{1,0:T(8,128)(2,1)S(1)}, u32[]{:S(2)}, u32[]{:S(2)}) collective-permute-start(bf16[1424,128]{1,0:T(8,128)(2,1)} %get-tuple-element.50.refs_1_), channel_id=1, source_target_pairs={{0,1},{1,0},{2,3},{3,2},{4,5},{5,4},{6,7},{7,6},{8,9},{9,8},{10,11... | collective-permute-start | bytes 1093640 | tf_op jit(solution)/shard_map/ppermute | solution.py:288
  4.1 7.2 %collective-permute-start.4 = (bf16[4,128,128]{2,1,0:T(8,128)(2,1)}, bf16[4,128,128]{2,1,0:T(8,128)(2,1)S(1)}, u32[]{:S(2)}, u32[]{:S(2)}) collective-permute-start(bf16[4,128,128]{2,1,0:T(8,128)(2,1)} %get-tuple-element.54), channel_id=1, source_target_pairs={{0,1},{1,0},{2,3},{3,2},{4,5},{5,4},{6,7},{7,6},{8,9},{9,8},{10,11... | collective-permute-start | bytes 393224 | tf_op jit(solution)/shard_map/ppermute | solution.py:288
  4.2 13.1 %collective-permute-start.1 = (bf16[1424,128]{1,0:T(8,128)(2,1)}, bf16[1424,128]{1,0:T(8,128)(2,1)S(1)}, u32[]{:S(2)}, u32[]{:S(2)}) collective-permute-start(bf16[1424,128]{1,0:T(8,128)(2,1)} %get-tuple-element.50.refs_1_), channel_id=1, source_target_pairs={{0,2},{1,3},{2,0},{3,1},{4,6},{5,7},{6,4},{7,5},{8,10},{9,11},{10,... | collective-permute-start | bytes 1093640 | tf_op jit(solution)/shard_map/ppermute | solution.py:288
  7.1 10.1 %collective-permute-start.3 = (bf16[592,128]{1,0:T(8,128)(2,1)}, bf16[592,128]{1,0:T(8,128)(2,1)S(1)}, u32[]{:S(2)}, u32[]{:S(2)}) collective-permute-start(bf16[592,128]{1,0:T(8,128)(2,1)} %get-tuple-element.52.refs_0_), channel_id=1, source_target_pairs={{0,8},{1,9},{2,10},{3,11},{4,12},{5,13},{6,14},{7,15},{8,0},{9,1},... | collective-permute-start | bytes 454664 | tf_op jit(solution)/shard_map/ppermute | solution.py:288
  9.7 7.7 %collective-permute-start.2 = (bf16[592,128]{1,0:T(8,128)(2,1)}, bf16[592,128]{1,0:T(8,128)(2,1)S(1)}, u32[]{:S(2)}, u32[]{:S(2)}) collective-permute-start(bf16[592,128]{1,0:T(8,128)(2,1)} %get-tuple-element.52.refs_0_), channel_id=1, source_target_pairs={{0,4},{1,5},{2,6},{3,7},{4,0},{5,1},{6,2},{7,3},{8,12},{9,13},{10,... | collective-permute-start | bytes 454664 | tf_op jit(solution)/shard_map/ppermute | solution.py:288
  12.2 5.0 %collective-permute-start.5 = (bf16[4,128,128]{2,1,0:T(8,128)(2,1)S(1)}, bf16[4,128,128]{2,1,0:T(8,128)(2,1)S(1)}, u32[]{:S(2)}, u32[]{:S(2)}) collective-permute-start(bf16[4,128,128]{2,1,0:T(8,128)(2,1)S(1)} %add_convert_fusion.2), channel_id=1, source_target_pairs={{0,16},{16,0},{1,17},{17,1},{2,18},{18,2},{3,19},{19,3},{4,20},{20... | collective-permute-start | bytes 393224 | tf_op jit(solution)/shard_map/ppermute | solution.py:288
  13.8 1.0 %copy-start = (bf16[1424,128]{1,0:T(8,128)(2,1)S(1)}, bf16[1424,128]{1,0:T(8,128)(2,1)}, u32[]{:S(2)}) copy-start(bf16[1424,128]{1,0:T(8,128)(2,1)} %get-tuple-element.50.refs_1_) | copy-start | bytes 1093636
  14.8 0.9 %copy-start.2 = (bf16[592,128]{1,0:T(8,128)(2,1)S(1)}, bf16[592,128]{1,0:T(8,128)(2,1)}, u32[]{:S(2)}) copy-start(bf16[592,128]{1,0:T(8,128)(2,1)} %get-tuple-element.52.refs_0_) | copy-start | bytes 454660
  15.7 0.7 %copy-start.3 = (f32[8,128]{1,0:T(8,128)S(1)}, f32[8,128]{1,0:T(8,128)}, u32[]{:S(2)}) copy-start(f32[8,128]{1,0:T(8,128)} %get-tuple-element.55.refs_2_) | copy-start | bytes 12292
  17.4 2.1 %collective-permute-start.7 = (bf16[1424,128]{1,0:T(8,128)(2,1)S(1)}, bf16[1424,128]{1,0:T(8,128)(2,1)S(1)}, u32[]{:S(2)}, u32[]{:S(2)}) collective-permute-start(bf16[1424,128]{1,0:T(8,128)(2,1)S(1)} %collective-permute-done.1.refs_5_.refs_2_), channel_id=1, source_target_pairs={{0,1},{1,0},{2,3},{3,2},{4,5},{5,4},{6,7},{7,6},{8,9},{9,8},{10,11... | collective-permute-start | bytes 1093640 | tf_op jit(solution)/shard_map/ppermute | solution.py:288
  17.5 11.7 %copy-start.1 = (bf16[2,512,128]{2,1,0:T(8,128)(2,1)S(1)}, bf16[2,512,128]{2,1,0:T(8,128)(2,1)}, u32[]{:S(2)}) copy-start(bf16[2,512,128]{2,1,0:T(8,128)(2,1)} %refs_4_.1) | copy-start | bytes 786436
  17.5 4.6 %collective-permute-start.11 = (bf16[2,128,128]{2,1,0:T(8,128)(2,1)S(1)}, bf16[2,128,128]{2,1,0:T(8,128)(2,1)S(1)}, u32[]{:S(2)}, u32[]{:S(2)}) collective-permute-start(bf16[2,128,128]{2,1,0:T(8,128)(2,1)S(1)} %slice.17), channel_id=1, source_target_pairs={{0,2},{1,3},{2,0},{3,1},{4,6},{5,7},{6,4},{7,5},{8,10},{9,11},{10,... | collective-permute-start | bytes 196616 | tf_op jit(solution)/shard_map/ppermute | solution.py:288
  18.0 6.1 %collective-permute-start.6 = (bf16[592,128]{1,0:T(8,128)(2,1)S(1)}, bf16[592,128]{1,0:T(8,128)(2,1)S(1)}, u32[]{:S(2)}, u32[]{:S(2)}) collective-permute-start(bf16[592,128]{1,0:T(8,128)(2,1)S(1)} %collective-permute-done.3.refs_2_.refs_9_), channel_id=1, source_target_pairs={{0,4},{1,5},{2,6},{3,7},{4,0},{5,1},{6,2},{7,3},{8,12},{9,13},{10,... | collective-permute-start | bytes 454664 | tf_op jit(solution)/shard_map/ppermute | solution.py:288
  22.1 5.0 %collective-permute-start.12 = (bf16[2,128,128]{2,1,0:T(8,128)(2,1)S(1)}, bf16[2,128,128]{2,1,0:T(8,128)(2,1)S(1)}, u32[]{:S(2)}, u32[]{:S(2)}) collective-permute-start(bf16[2,128,128]{2,1,0:T(8,128)(2,1)S(1)} %add_convert_fusion.5), channel_id=1, source_target_pairs={{0,4},{1,5},{2,6},{3,7},{4,0},{5,1},{6,2},{7,3},{8,12},{9,13},{10,... | collective-permute-start | bytes 196616 | tf_op jit(solution)/shard_map/ppermute | solution.py:288
  24.6 6.2 %collective-permute-start.8 = (f32[16,128]{1,0:T(8,128)S(1)}, f32[16,128]{1,0:T(8,128)S(1)}, u32[]{:S(2)}, u32[]{:S(2)}) collective-permute-start(f32[16,128]{1,0:T(8,128)S(1)} %get-tuple-element.68.refs_0_), channel_id=1, source_target_pairs={{0,1},{1,0},{2,3},{3,2},{4,5},{5,4},{6,7},{7,6},{8,9},{9,8},{10,11... | collective-permute-start | bytes 24584 | tf_op jit(solution)/shard_map/ppermute | solution.py:288
  24.7 6.1 %collective-permute-start.9 = (f32[16,128]{1,0:T(8,128)S(1)}, f32[16,128]{1,0:T(8,128)S(1)}, u32[]{:S(2)}, u32[]{:S(2)}) collective-permute-start(f32[16,128]{1,0:T(8,128)S(1)} %get-tuple-element.68.refs_0_), channel_id=1, source_target_pairs={{0,2},{1,3},{2,0},{3,1},{4,6},{5,7},{6,4},{7,5},{8,10},{9,11},{10,... | collective-permute-start | bytes 24584 | tf_op jit(solution)/shard_map/ppermute | solution.py:288
  27.0 3.8 %collective-permute-start.10 = (f32[16,128]{1,0:T(8,128)S(1)}, f32[16,128]{1,0:T(8,128)S(1)}, u32[]{:S(2)}, u32[]{:S(2)}) collective-permute-start(f32[16,128]{1,0:T(8,128)S(1)} %get-tuple-element.68.refs_0_), channel_id=1, source_target_pairs={{0,3},{1,2},{2,1},{3,0},{4,7},{5,6},{6,5},{7,4},{8,11},{9,10},{10,... | collective-permute-start | bytes 24584 | tf_op jit(solution)/shard_map/ppermute | solution.py:288
  27.1 6.5 %collective-permute-start.13 = (bf16[2,128,128]{2,1,0:T(8,128)(2,1)S(1)}, bf16[2,128,128]{2,1,0:T(8,128)(2,1)S(1)}, u32[]{:S(2)}, u32[]{:S(2)}) collective-permute-start(bf16[2,128,128]{2,1,0:T(8,128)(2,1)S(1)} %add_convert_fusion.4), channel_id=1, source_target_pairs={{0,8},{1,9},{2,10},{3,11},{4,12},{5,13},{6,14},{7,15},{8,0},{9,1},... | collective-permute-start | bytes 196616 | tf_op jit(solution)/shard_map/ppermute | solution.py:288
  31.6 9.7 %collective-permute-start.21 = (bf16[576,128]{1,0:T(8,128)(2,1)S(1)}, bf16[576,128]{1,0:T(8,128)(2,1)S(1)}, u32[]{:S(2)}, u32[]{:S(2)}) collective-permute-start(bf16[576,128]{1,0:T(8,128)(2,1)S(1)} %get-tuple-element.94), channel_id=1, source_target_pairs={{0,4},{1,5},{2,6},{3,7},{4,0},{5,1},{6,2},{7,3},{8,12},{9,13},{10,... | collective-permute-start | bytes 442376 | tf_op jit(solution)/shard_map/ppermute | solution.py:288
  33.7 5.9 %collective-permute-start.15 = (bf16[2,128,128]{2,1,0:T(8,128)(2,1)S(1)}, bf16[2,128,128]{2,1,0:T(8,128)(2,1)S(1)}, u32[]{:S(2)}, u32[]{:S(2)}) collective-permute-start(bf16[2,128,128]{2,1,0:T(8,128)(2,1)S(1)} %add_convert_fusion.3.refs_0_), channel_id=1, source_target_pairs={{0,2},{1,3},{2,0},{3,1},{4,6},{5,7},{6,4},{7,5},{8,10},{9,11},{10,... | collective-permute-start | bytes 196616 | tf_op jit(solution)/shard_map/ppermute | solution.py:288
  36.8 3.3 %collective-permute-start.16 = (bf16[288,128]{1,0:T(8,128)(2,1)S(1)}, bf16[288,128]{1,0:T(8,128)(2,1)S(1)}, u32[]{:S(2)}, u32[]{:S(2)}) collective-permute-start(bf16[288,128]{1,0:T(8,128)(2,1)S(1)} %get-tuple-element.85), channel_id=1, source_target_pairs={{0,1},{1,0},{2,3},{3,2},{4,5},{5,4},{6,7},{7,6},{8,9},{9,8},{10,11... | collective-permute-start | bytes 221192 | tf_op jit(solution)/shard_map/ppermute | solution.py:288
  36.9 3.3 %collective-permute-start.17 = (bf16[288,128]{1,0:T(8,128)(2,1)S(1)}, bf16[288,128]{1,0:T(8,128)(2,1)S(1)}, u32[]{:S(2)}, u32[]{:S(2)}) collective-permute-start(bf16[288,128]{1,0:T(8,128)(2,1)S(1)} %get-tuple-element.86), channel_id=1, source_target_pairs={{0,1},{1,0},{2,3},{3,2},{4,5},{5,4},{6,7},{7,6},{8,9},{9,8},{10,11... | collective-permute-start | bytes 221192 | tf_op jit(solution)/shard_map/ppermute | solution.py:288
  37.4 3.3 %collective-permute-start.18 = (bf16[288,128]{1,0:T(8,128)(2,1)S(1)}, bf16[288,128]{1,0:T(8,128)(2,1)S(1)}, u32[]{:S(2)}, u32[]{:S(2)}) collective-permute-start(bf16[288,128]{1,0:T(8,128)(2,1)S(1)} %get-tuple-element.87), channel_id=1, source_target_pairs={{0,1},{1,0},{2,3},{3,2},{4,5},{5,4},{6,7},{7,6},{8,9},{9,8},{10,11... | collective-permute-start | bytes 221192 | tf_op jit(solution)/shard_map/ppermute | solution.py:288
  39.5 1.4 %collective-permute-start.19 = (bf16[288,128]{1,0:T(8,128)(2,1)S(1)}, bf16[288,128]{1,0:T(8,128)(2,1)S(1)}, u32[]{:S(2)}, u32[]{:S(2)}) collective-permute-start(bf16[288,128]{1,0:T(8,128)(2,1)S(1)} %get-tuple-element.88), channel_id=1, source_target_pairs={{0,1},{1,0},{2,3},{3,2},{4,5},{5,4},{6,7},{7,6},{8,9},{9,8},{10,11... | collective-permute-start | bytes 221192 | tf_op jit(solution)/shard_map/ppermute | solution.py:288
  40.0 5.8 %collective-permute-start.14 = (bf16[2,576,128]{2,1,0:T(8,128)(2,1)S(1)}, bf16[2,576,128]{2,1,0:T(8,128)(2,1)S(1)}, u32[]{:S(2)}, u32[]{:S(2)}) collective-permute-start(bf16[2,576,128]{2,1,0:T(8,128)(2,1)S(1)} %get-tuple-element.82), channel_id=1, source_target_pairs={{0,1},{1,0},{2,3},{3,2},{4,5},{5,4},{6,7},{7,6},{8,9},{9,8},{10,11... | collective-permute-start | bytes 884744 | tf_op jit(solution)/shard_map/ppermute | solution.py:288
  40.2 4.8 %collective-permute-start.24 = (bf16[4,128,128]{2,1,0:T(8,128)(2,1)S(1)}, bf16[4,128,128]{2,1,0:T(8,128)(2,1)S(1)}, u32[]{:S(2)}, u32[]{:S(2)}) collective-permute-start(bf16[4,128,128]{2,1,0:T(8,128)(2,1)S(1)} %pad_maximum_fusion), channel_id=1, source_target_pairs={{0,1},{1,0},{2,3},{3,2},{4,5},{5,4},{6,7},{7,6},{8,9},{9,8},{10,11... | collective-permute-start | bytes 393224 | tf_op jit(solution)/shard_map/ppermute | solution.py:288
  41.0 9.3 %collective-permute-start.20 = (bf16[2,576,128]{2,1,0:T(8,128)(2,1)S(1)}, bf16[2,576,128]{2,1,0:T(8,128)(2,1)S(1)}, u32[]{:S(2)}, u32[]{:S(2)}) collective-permute-start(bf16[2,576,128]{2,1,0:T(8,128)(2,1)S(1)} %join.1), channel_id=1, source_target_pairs={{0,2},{1,3},{2,0},{3,1},{4,6},{5,7},{6,4},{7,5},{8,10},{9,11},{10,... | collective-permute-start | bytes 884744 | tf_op jit(solution)/shard_map/ppermute | solution.py:288
  41.4 10.1 %collective-permute-start.22 = (bf16[576,128]{1,0:T(8,128)(2,1)S(1)}, bf16[576,128]{1,0:T(8,128)(2,1)S(1)}, u32[]{:S(2)}, u32[]{:S(2)}) collective-permute-start(bf16[576,128]{1,0:T(8,128)(2,1)S(1)} %add_convert_fusion), channel_id=1, source_target_pairs={{0,8},{1,9},{2,10},{3,11},{4,12},{5,13},{6,14},{7,15},{8,0},{9,1},... | collective-permute-start | bytes 442376 | tf_op jit(solution)/shard_map/ppermute | solution.py:288
  42.2 9.4 %collective-permute-start.23 = (bf16[576,128]{1,0:T(8,128)(2,1)S(1)}, bf16[576,128]{1,0:T(8,128)(2,1)S(1)}, u32[]{:S(2)}, u32[]{:S(2)}) collective-permute-start(bf16[576,128]{1,0:T(8,128)(2,1)S(1)} %get-tuple-element.96), channel_id=1, source_target_pairs={{0,4},{1,5},{2,6},{3,7},{4,0},{5,1},{6,2},{7,3},{8,12},{9,13},{10,... | collective-permute-start | bytes 442376 | tf_op jit(solution)/shard_map/ppermute | solution.py:288

commit v13 on v12

--- a/solution.py
+++ b/solution.py
@@ -12,7 +12,7 @@
 HEAD_DIM = 128
 GROUP = 4
 EXTRA = 16
-CUTS = 2
+CUTS = 3
 PACK_LIMIT = 63 << 20
 F32 = jnp.float32
 BF16 = jnp.bfloat16
@@ -230,8 +230,6 @@
     (s_ref, gp_ref, last_gs_ref), refs = refs[:3], refs[3:]
     lat_refs, refs = refs[:nkey], refs[nkey:]
     gq_refs, far_refs, (gs_ref, p_ref, kt) = refs[: GROUP - 1], refs[GROUP - 1 : -3], refs[-3:]
-    cut = far_refs[0].shape[0]
-    cuts = width // cut
     tok = lat_refs[0].shape[1]
     keys = s_ref.shape[0]
     rows = heads * tok
@@ -247,17 +245,28 @@
             if j < GROUP - 1:
                 gq_refs[j][h] = part
             else:
-                for c in range(cuts):
-                    far_refs[h * cuts + c][...] = part[c * cut : (c + 1) * cut]
+                for c, at, here in segments(h, width, far_refs):
+                    far_refs[c][here, :] = part[at]
+
+
+def segments(head, width, pieces):
+    cut = pieces[0].shape[0]
+    found = []
+    for c in range(len(pieces)):
+        low, high = max(head * width, c * cut), min((head + 1) * width, (c + 1) * cut)
+        if low < high:
+            at = slice(low - head * width, high - head * width)
+            found.append((c, at, slice(low - c * cut, high - c * cut)))
+    return found
 
 
 def join_kernel(whole_ref, *refs):
     pieces, out_ref = refs[:-1], refs[-1]
-    cut = pieces[0].shape[0]
-    cuts = whole_ref.shape[1] // cut
-    for i, piece in enumerate(pieces):
-        at = (i // cuts, slice(i % cuts * cut, (i % cuts + 1) * cut))
-        out_ref[at] = (whole_ref[at].astype(F32) + piece[...].astype(F32)).astype(BF16)
+    heads, width, _ = out_ref.shape
+    for h in range(heads):
+        for c, at, here in segments(h, width, pieces):
+            both = whole_ref[h, at, :].astype(F32) + pieces[c][here, :].astype(F32)
+            out_ref[h, at, :] = both.astype(BF16)
 
 
 def sum_kernel(*refs):
@@ -412,11 +421,11 @@
     )
     last_got = swap(last_part, GROUP)
     mine = add(mine, near)
-    gq_shape, cut_shape = (heads, width, tok), (width // CUTS, tok)
+    gq_shape, cut_shape = (heads, width, tok), (heads * width // CUTS, tok)
     gq_own, gq_core, gq_across, *far_cuts, near_gs, near_p = call(
         functools.partial(query_kernel, factor, lines, width, heads),
         "query_gradients",
-        [(gq_shape, BF16)] * 3 + [(cut_shape, BF16)] * (CUTS * heads) + [((keys, all_rows), BF16)] * 2,
+        [(gq_shape, BF16)] * 3 + [(cut_shape, BF16)] * CUTS + [((keys, all_rows), BF16)] * 2,
         stats + [near_s, near_gp, after(last_gs, mine)] + lats,
         [((width, lines * tok), BF16)],
         flops=2 * lines * tok * all_rows * width,
@@ -425,9 +434,9 @@
     across = swap(mine, 2)
     far_cuts = [swap(cut, 1) for cut in far_cuts]
     (gq_sum,) = call(join_kernel, "join", [(gq_shape, BF16)], [after(gq_across, across)] + far_cuts)
-    gq_core = swap(gq_core, 1)
     gq_last = swap(gq_sum, 2)
-    def partials(name, blocks, gs, p):
+    gq_core = swap(after(gq_core, gq_sum), 1)
+    def partials(name, blocks, gs, p, share=1):
         rows = [slice(m * tok, (m + 1) * tok) for m in blocks]
         made = call(
             functools.partial(partial_kernel, factor, rows, width),
@@ -435,12 +444,13 @@
             [((width, tok), BF16)] * len(blocks),
             [g, q_all, gs, p],
             flops=2 * len(blocks) * tok * all_rows * (width + lat),
+            share=share,
         )
         return dict(zip(blocks, made))
 
     middle = lines // 2
-    made = partials("middle_gradients", [middle], near_gs, near_p)
-    made.update(partials("near_gradients", [m for m in range(most) if m != middle], near_gs, after(near_p, made[middle])))
+    made = partials("middle_gradients", [middle], near_gs, near_p, 3)
+    made.update(partials("near_gradients", [m for m in range(most) if m != middle], near_gs, after(near_p, *far_cuts)))
     near_parts = [made[m] for m in range(most)]
     parts = list(near_parts) + [last_part]
     kept = [parts[0]]

time: 52.5 us -> 53.1 us (1.011)
    ppermute x25 -> x24, starting transfers between devices: 26.7 us -> 27 us  [swap(): return lax.ppermute(x, axis, [(i, i ^ mask) for i in range(size)])]
    ppermute x25 -> x24, waiting for transfers between devices: 8.38 us -> 8.55 us  [swap(): return lax.ppermute(x, axis, [(i, i ^ mask) for i in range(size)])]
  transfers between devices with their start and end apart: 25 -> 24, of which waited for: 10 -> 9; matrix products, arithmetic and copies ran while one was open for 2% -> 2% of each run, Pallas kernels for 17% -> 17%
where the time goes in v13:
time: 53.1 us; the launch traced here: 52.8 us
  starting transfers between devices  27 us (51%)
  Pallas kernels  12.8 us (24%)
  waiting for transfers between devices  8.55 us (16%)
  local copies, waits for them, and re-layouts  2.6 us (5%)
  other arithmetic  1.1 us (2%)
  between operations  0.82 us (2%)
    ppermute x24, starting transfers between devices, swap(): return lax.ppermute(x, axis, [(i, i ^ mask) for i in range(size)])  27 us
    pallas_call x13, Pallas kernels, call(): pl.pallas_call(kernel, out_shape=[jax.ShapeDtypeStruct(s, d) for s, d in...  12.8 us
    ppermute x24, waiting for transfers between devices, swap(): return lax.ppermute(x, axis, [(i, i ^ mask) for i in range(size)])  8.55 us
    unnamed x8, local copies, waits for them, and re-layouts  2.59 us
    convert_element_type x6, other arithmetic, add(): return (a.astype(F32) + b.astype(F32)).astype(BF16)  1.09 us
  transfers between devices with their start and end apart: 24, of which 9 were waited for; matrix products, arithmetic and copies ran while one was open for 2% of the time, Pallas kernels for 17%

profile of v13, /device:TPU:0, one launch (start us, length us, event | category | flops | bytes accessed | tf_op | source)
XLA Modules:
  0.0 52.8 jit_solution(16682250168944061985)
XLA Ops:
  0.6 3.0 %pack.1 = (bf16[592,128]{1,0:T(8,128)(2,1)}, bf16[1424,128]{1,0:T(8,128)(2,1)}, f32[8,128]{1,0:T(8,128)}, bf16[4,128,128]{2,1,0:T(8,128)(2,1)}, bf16[4,128,128]{2,1,0:T(8,128)(2,1)}) custom-call(s32[1]{0:T(128)} %bitcast.idx_ref, s32[1,128]{1,0:T(1,128)} %pos_hbm.1, bf16[2,576,128]{2,1,0:T(8,128)(2,1)} %bitcast.15, bf16[128,2,128]{2,1,0:T(2,128)(2,1)} %bitcast.20, ...), custom_call_target="tpu_custom_call" | custom-call | bytes 1815044 | tf_op jit(solution)/shard_map/pack/pallas_call | solution.py:40
  3.6 0.5 collective-permute-start
  4.1 0.1 collective-permute-start.4
  4.2 2.9 %collective-permute-start.1 = (bf16[1424,128]{1,0:T(8,128)(2,1)}, bf16[1424,128]{1,0:T(8,128)(2,1)S(1)}, u32[]{:S(2)}, u32[]{:S(2)}) collective-permute-start(bf16[1424,128]{1,0:T(8,128)(2,1)} %get-tuple-element.50.refs_1_), channel_id=1, source_target_pairs={{0,2},{1,3},{2,0},{3,1},{4,6},{5,7},{6,4},{7,5},{8,10},{9,11},{10,... | collective-permute-start | bytes 1093640 | tf_op jit(solution)/shard_map/ppermute | solution.py:297
  7.1 2.6 %collective-permute-start.3 = (bf16[592,128]{1,0:T(8,128)(2,1)}, bf16[592,128]{1,0:T(8,128)(2,1)S(1)}, u32[]{:S(2)}, u32[]{:S(2)}) collective-permute-start(bf16[592,128]{1,0:T(8,128)(2,1)} %get-tuple-element.52.refs_0_), channel_id=1, source_target_pairs={{0,8},{1,9},{2,10},{3,11},{4,12},{5,13},{6,14},{7,15},{8,0},{9,1},... | collective-permute-start | bytes 454664 | tf_op jit(solution)/shard_map/ppermute | solution.py:297
  9.7 0.0 collective-permute-done.refs_4_.refs_1_
  9.7 1.6 %collective-permute-start.2 = (bf16[592,128]{1,0:T(8,128)(2,1)}, bf16[592,128]{1,0:T(8,128)(2,1)S(1)}, u32[]{:S(2)}, u32[]{:S(2)}) collective-permute-start(bf16[592,128]{1,0:T(8,128)(2,1)} %get-tuple-element.52.refs_0_), channel_id=1, source_target_pairs={{0,4},{1,5},{2,6},{3,7},{4,0},{5,1},{6,2},{7,3},{8,12},{9,13},{10,... | collective-permute-start | bytes 454664 | tf_op jit(solution)/shard_map/ppermute | solution.py:297
  11.3 0.0 collective-permute-done.4
  11.3 0.9 %add_convert_fusion.2 = bf16[4,128,128]{2,1,0:T(8,128)(2,1)S(1)} fusion(bf16[4,128,128]{2,1,0:T(8,128)(2,1)S(1)} %collective-permute-done.4, bf16[4,128,128]{2,1,0:T(8,128)(2,1)} %get-tuple-element.53), kind=kLoop, calls=%fused_computation.2 | loop fusion | flops 262144 | bytes 393216 | tf_op jit(solution)/shard_map/convert_element_type | solution.py:345
  12.3 1.6 %collective-permute-start.5 = (bf16[4,128,128]{2,1,0:T(8,128)(2,1)S(1)}, bf16[4,128,128]{2,1,0:T(8,128)(2,1)S(1)}, u32[]{:S(2)}, u32[]{:S(2)}) collective-permute-start(bf16[4,128,128]{2,1,0:T(8,128)(2,1)S(1)} %add_convert_fusion.2), channel_id=1, source_target_pairs={{0,16},{16,0},{1,17},{17,1},{2,18},{18,2},{3,19},{19,3},{4,20},{20... | collective-permute-start | bytes 393224 | tf_op jit(solution)/shard_map/ppermute | solution.py:297
  13.8 1.0 %copy-done = bf16[1424,128]{1,0:T(8,128)(2,1)S(1)} copy-done((bf16[1424,128]{1,0:T(8,128)(2,1)S(1)}, bf16[1424,128]{1,0:T(8,128)(2,1)}, u32[]{:S(2)}) %copy-start) | copy-done | bytes 364568
  14.8 0.9 %copy-done.2 = bf16[592,128]{1,0:T(8,128)(2,1)S(1)} copy-done((bf16[592,128]{1,0:T(8,128)(2,1)S(1)}, bf16[592,128]{1,0:T(8,128)(2,1)}, u32[]{:S(2)}) %copy-start.2) | copy-done | bytes 151576
  15.7 0.7 %copy-done.3 = f32[8,128]{1,0:T(8,128)S(1)} copy-done((f32[8,128]{1,0:T(8,128)S(1)}, f32[8,128]{1,0:T(8,128)}, u32[]{:S(2)}) %copy-start.3) | copy-done | bytes 4120
  16.4 0.8 %collective-permute-done.3.refs_2_.refs_9_ = bf16[592,128]{1,0:T(8,128)(2,1)S(1)} collective-permute-done((bf16[592,128]{1,0:T(8,128)(2,1)}, bf16[592,128]{1,0:T(8,128)(2,1)S(1)}, u32[]{:S(2)}, u32[]{:S(2)}) %collective-permute-start.3) | collective-permute-done | bytes 151584 | tf_op jit(solution)/shard_map/ppermute | solution.py:297
  17.2 0.1 collective-permute-done.5
  17.3 0.0 collective-permute-done.1.refs_5_.refs_2_
  17.3 0.1 collective-permute-done.2.refs_1_.refs_8_
  17.4 0.0 collective-permute-start.7
  17.5 0.0 copy-start.1
  17.5 0.5 collective-permute-start.11
  18.0 1.5 %collective-permute-start.6 = (bf16[592,128]{1,0:T(8,128)(2,1)S(1)}, bf16[592,128]{1,0:T(8,128)(2,1)S(1)}, u32[]{:S(2)}, u32[]{:S(2)}) collective-permute-start(bf16[592,128]{1,0:T(8,128)(2,1)S(1)} %collective-permute-done.3.refs_2_.refs_9_), channel_id=1, source_target_pairs={{0,4},{1,5},{2,6},{3,7},{4,0},{5,1},{6,2},{7,3},{8,12},{9,13},{10,... | collective-permute-start | bytes 454664 | tf_op jit(solution)/shard_map/ppermute | solution.py:297
  19.6 0.0 collective-permute-done.7.refs_6_.refs_3_
  19.6 1.2 %near_scores.1 = (f32[384,1024]{1,0:T(8,128)S(1)}, bf16[384,640]{1,0:T(8,128)(2,1)S(1)}, f32[16,128]{1,0:T(8,128)S(1)}, bf16[640,1024]{1,0:T(8,128)(2,1)S(1)}) custom-call(bf16[592,128]{1,0:T(8,128)(2,1)S(1)} %get-tuple-element.60.refs_0_.refs_7_, bf16[592,128]{1,0:T(8,128)(2,1)S(1)} %collective-permute-done.2.refs_1_.refs_8_, ...), custom_call_target="tpu_custom_call" | custom-call | tf_op jit(solution)/shard_map/near_scores/pallas_call | solution.py:40
  20.8 1.3 %collective-permute-done.11 = bf16[2,128,128]{2,1,0:T(8,128)(2,1)S(1)} collective-permute-done((bf16[2,128,128]{2,1,0:T(8,128)(2,1)S(1)}, bf16[2,128,128]{2,1,0:T(8,128)(2,1)S(1)}, u32[]{:S(2)}, u32[]{:S(2)}) %collective-permute-start.11) | collective-permute-done | bytes 65568 | tf_op jit(solution)/shard_map/ppermute | solution.py:297
  22.1 1.5 %collective-permute-start.12 = (bf16[2,128,128]{2,1,0:T(8,128)(2,1)S(1)}, bf16[2,128,128]{2,1,0:T(8,128)(2,1)S(1)}, u32[]{:S(2)}, u32[]{:S(2)}) collective-permute-start(bf16[2,128,128]{2,1,0:T(8,128)(2,1)S(1)} %add_convert_fusion.5), channel_id=1, source_target_pairs={{0,4},{1,5},{2,6},{3,7},{4,0},{5,1},{6,2},{7,3},{8,12},{9,13},{10,... | collective-permute-start | bytes 196616 | tf_op jit(solution)/shard_map/ppermute | solution.py:297
  23.6 0.5 collective-permute-done.6.refs_0_.refs_10_
  24.1 0.5 last_scores.1
  24.6 0.1 collective-permute-start.8
  24.7 2.3 %collective-permute-start.9 = (f32[16,128]{1,0:T(8,128)S(1)}, f32[16,128]{1,0:T(8,128)S(1)}, u32[]{:S(2)}, u32[]{:S(2)}) collective-permute-start(f32[16,128]{1,0:T(8,128)S(1)} %get-tuple-element.68.refs_0_), channel_id=1, source_target_pairs={{0,2},{1,3},{2,0},{3,1},{4,6},{5,7},{6,4},{7,5},{8,10},{9,11},{10,... | collective-permute-start | bytes 24584 | tf_op jit(solution)/shard_map/ppermute | solution.py:297
  27.0 0.1 collective-permute-start.10
  27.1 0.0 collective-permute-done.12
  27.1 2.1 %collective-permute-start.13 = (bf16[2,128,128]{2,1,0:T(8,128)(2,1)S(1)}, bf16[2,128,128]{2,1,0:T(8,128)(2,1)S(1)}, u32[]{:S(2)}, u32[]{:S(2)}) collective-permute-start(bf16[2,128,128]{2,1,0:T(8,128)(2,1)S(1)} %add_convert_fusion.4), channel_id=1, source_target_pairs={{0,8},{1,9},{2,10},{3,11},{4,12},{5,13},{6,14},{7,15},{8,0},{9,1},... | collective-permute-start | bytes 196616 | tf_op jit(solution)/shard_map/ppermute | solution.py:297
  29.2 1.6 %context.1 = (bf16[512,1024]{1,0:T(8,128)(2,1)S(1)}, f32[384,1024]{1,0:T(8,128)S(1)}, f32[128,1024]{1,0:T(8,128)S(1)}) custom-call(bf16[1424,128]{1,0:T(8,128)(2,1)S(1)} %get-tuple-element.62.refs_3_.refs_0_, bf16[1424,128]{1,0:T(8,128)(2,1)S(1)} %collective-permute-done.refs_4_.refs_1_, bf16[1424,128]{1,0:T(8,128)(2,1)S(1)} %collective-permute-done.1.refs_5_.refs_2_, ...), custom_call_target="tpu_custom_call" | custom-call | flops 2013265920 | bytes 16564224 | tf_op jit(solution)/shard_map/context/pallas_call | solution.py:40
  30.8 0.0 collective-permute-done.8.refs_1_
  30.8 0.0 collective-permute-done.9.refs_2_
  30.8 0.0 collective-permute-done.10.refs_3_
  30.8 0.8 %last_gradients.1 = (bf16[576,128]{1,0:T(8,128)(2,1)S(1)}, bf16[128,1024]{1,0:T(8,128)(2,1)S(1)}) custom-call(f32[16,128]{1,0:T(8,128)S(1)} %get-tuple-element.68.refs_0_, f32[16,128]{1,0:T(8,128)S(1)} %collective-permute-done.8.refs_1_, f32[16,128]{1,0:T(8,128)S(1)} %collective-permute-done.9.refs_2_, f32[16,128]{1,0:T(8,128)S(1)} %collective-permute-done.10.refs_3_, ...), custom_call_target="tpu_custom_call" | custom-call | flops 285212672 | bytes 3850240 | tf_op jit(solution)/shard_map/last_gradients/pallas_call | solution.py:40
  31.6 1.7 %collective-permute-start.20 = (bf16[576,128]{1,0:T(8,128)(2,1)S(1)}, bf16[576,128]{1,0:T(8,128)(2,1)S(1)}, u32[]{:S(2)}, u32[]{:S(2)}) collective-permute-start(bf16[576,128]{1,0:T(8,128)(2,1)S(1)} %get-tuple-element.94), channel_id=1, source_target_pairs={{0,4},{1,5},{2,6},{3,7},{4,0},{5,1},{6,2},{7,3},{8,12},{9,13},{10,... | collective-permute-start | bytes 442376 | tf_op jit(solution)/shard_map/ppermute | solution.py:297
  33.4 0.3 collective-permute-done.13
  33.7 2.0 %collective-permute-start.14 = (bf16[2,128,128]{2,1,0:T(8,128)(2,1)S(1)}, bf16[2,128,128]{2,1,0:T(8,128)(2,1)S(1)}, u32[]{:S(2)}, u32[]{:S(2)}) collective-permute-start(bf16[2,128,128]{2,1,0:T(8,128)(2,1)S(1)} %add_convert_fusion.3.refs_0_), channel_id=1, source_target_pairs={{0,2},{1,3},{2,0},{3,1},{4,6},{5,7},{6,4},{7,5},{8,10},{9,11},{10,... | collective-permute-start | bytes 196616 | tf_op jit(solution)/shard_map/ppermute | solution.py:297
  35.6 1.1 %query_gradients.1 = (bf16[2,576,128]{2,1,0:T(8,128)(2,1)S(1)}, bf16[2,576,128]{2,1,0:T(8,128)(2,1)S(1)}, bf16[2,576,128]{2,1,0:T(8,128)(2,1)S(1)}, bf16[384,128...) custom-call(f32[16,128]{1,0:T(8,128)S(1)} %get-tuple-element.68.refs, ...), custom_call_target="tpu_custom_call" | custom-call | tf_op jit(solution)/shard_map/query_gradients/pallas_call | solution.py:40
  36.8 0.1 collective-permute-start.15
  36.9 0.5 collective-permute-start.16
  37.4 0.1 collective-permute-start.17
  37.5 0.7 %middle_gradients.1 = bf16[576,128]{1,0:T(8,128)(2,1)S(1)} custom-call(bf16[512,1024]{1,0:T(8,128)(2,1)S(1)} %get-tuple-element.75.refs_6_.g_ref, bf16[640,1024]{1,0:T(8,128)(2,1)S(1)} %get-tuple-element.65.refs_1_.refs_7_.q_all_ref, bf16[384,1024]{1,0:T(8,128)(2,1)S(1)} %get-tuple-element.89.gs_ref, bf16[384,1024]{1,0:T(8,128)(2,1)S(1)} %get-tuple-element.91.p_ref), custom_call_target="tpu_custom_call" | custom-call | flops 855638016 | bytes 12238848 | tf_op jit(solution)/shard_map/middle_gradients/pallas_call | solution.py:40
  38.2 0.0 collective-permute-done.14.refs_2_
  38.2 0.5 collective-permute-start.23
  38.7 0.0 collective-permute-done.15.refs_0_
  38.7 0.0 collective-permute-done.16.refs_1_
  38.7 0.0 collective-permute-done.17.refs_2_
  38.7 0.1 join.1
  38.8 1.4 %collective-permute-start.19 = (bf16[2,576,128]{2,1,0:T(8,128)(2,1)S(1)}, bf16[2,576,128]{2,1,0:T(8,128)(2,1)S(1)}, u32[]{:S(2)}, u32[]{:S(2)}) collective-permute-start(bf16[2,576,128]{2,1,0:T(8,128)(2,1)S(1)} %join.1), channel_id=1, source_target_pairs={{0,2},{1,3},{2,0},{3,1},{4,6},{5,7},{6,4},{7,5},{8,10},{9,11},{10,... | collective-permute-start | bytes 884744 | tf_op jit(solution)/shard_map/ppermute | solution.py:297
  40.2 0.2 collective-permute-start.18
  40.4 0.0 collective-permute-done.20
  40.4 0.4 collective-permute-start.21
  40.8 1.3 %near_gradients.1 = (bf16[576,128]{1,0:T(8,128)(2,1)S(1)}, bf16[576,128]{1,0:T(8,128)(2,1)S(1)}) custom-call(bf16[512,1024]{1,0:T(8,128)(2,1)S(1)} %get-tuple-element.75.refs_6_.g_ref, bf16[640,1024]{1,0:T(8,128)(2,1)S(1)} %get-tuple-element.65.refs_1_.refs_7_.q_all_ref, bf16[384,1024]{1,0:T(8,128)(2,1)S(1)} %get-tuple-element.89.gs_ref, ...), custom_call_target="tpu_custom_call" | custom-call | flops 570425344 | bytes 4227072 | tf_op jit(solution)/shard_map/near_gradients/pallas_call | solution.py:40
  42.1 2.9 %collective-permute-start.22 = (bf16[576,128]{1,0:T(8,128)(2,1)S(1)}, bf16[576,128]{1,0:T(8,128)(2,1)S(1)}, u32[]{:S(2)}, u32[]{:S(2)}) collective-permute-start(bf16[576,128]{1,0:T(8,128)(2,1)S(1)} %get-tuple-element.96), channel_id=1, source_target_pairs={{0,4},{1,5},{2,6},{3,7},{4,0},{5,1},{6,2},{7,3},{8,12},{9,13},{10,... | collective-permute-start | bytes 442376 | tf_op jit(solution)/shard_map/ppermute | solution.py:297
  45.0 0.0 collective-permute-done.23
  45.0 0.8 %spread.1 = f32[2,512,128]{2,1,0:T(8,128)} custom-call(s32[1]{0:T(128)} %bitcast.idx_ref, bf16[2,128,128]{2,1,0:T(8,128)(2,1)S(1)} %add_convert_fusion.3.refs_0_, bf16[2,128,128]{2,1,0:T(8,128)(2,1)S(1)} %get-tuple-element.98.refs_1_, bf16[2,128,128]{2,1,0:T(8,128)(2,1)S(1)} %collective-permute-done.14.refs_2_, ...), custom_call_target="tpu_custom_call" | custom-call | bytes 786436 | tf_op jit(solution)/shard_map/spread/pallas_call | solution.py:40
  45.8 2.0 %collective-permute-done.19.refs_2_ = bf16[2,576,128]{2,1,0:T(8,128)(2,1)S(1)} collective-permute-done((bf16[2,576,128]{2,1,0:T(8,128)(2,1)S(1)}, bf16[2,576,128]{2,1,0:T(8,128)(2,1)S(1)}, u32[]{:S(2)}, u32[]{:S(2)}) %collective-permute-start.19) | collective-permute-done | bytes 294944 | tf_op jit(solution)/shard_map/ppermute | solution.py:297
  47.9 0.8 %query_sum.1 = bf16[2,576,128]{2,1,0:T(8,128)(2,1)} custom-call(bf16[2,576,128]{2,1,0:T(8,128)(2,1)S(1)} %get-tuple-element.81.refs_0_, bf16[2,576,128]{2,1,0:T(8,128)(2,1)S(1)} %collective-permute-done.18.refs_1_, bf16[2,576,128]{2,1,0:T(8,128)(2,1)S(1)} %collective-permute-done.19.refs_2_), custom_call_target="tpu_custom_call" | custom-call | bytes 1179648 | tf_op jit(solution)/shard_map/query_sum/pallas_call | solution.py:40
  48.7 1.9 %collective-permute-done.21.refs_1_ = bf16[576,128]{1,0:T(8,128)(2,1)S(1)} collective-permute-done((bf16[576,128]{1,0:T(8,128)(2,1)S(1)}, bf16[576,128]{1,0:T(8,128)(2,1)S(1)}, u32[]{:S(2)}, u32[]{:S(2)}) %collective-permute-start.21) | collective-permute-done | bytes 147488 | tf_op jit(solution)/shard_map/ppermute | solution.py:297
  50.6 1.5 %collective-permute-done.22.refs_2_ = bf16[576,128]{1,0:T(8,128)(2,1)S(1)} collective-permute-done((bf16[576,128]{1,0:T(8,128)(2,1)S(1)}, bf16[576,128]{1,0:T(8,128)(2,1)S(1)}, u32[]{:S(2)}, u32[]{:S(2)}) %collective-permute-start.22) | collective-permute-done | bytes 147488 | tf_op jit(solution)/shard_map/ppermute | solution.py:297
  52.1 0.7 %latent_sum.1 = bf16[576,128]{1,0:T(8,128)(2,1)} custom-call(bf16[576,128]{1,0:T(8,128)(2,1)S(1)} %get-tuple-element.93.refs_0_, bf16[576,128]{1,0:T(8,128)(2,1)S(1)} %collective-permute-done.21.refs_1_, bf16[576,128]{1,0:T(8,128)(2,1)S(1)} %collective-permute-done.22.refs_2_), custom_call_target="tpu_custom_call" | custom-call | bytes 589824 | tf_op jit(solution)/shard_map/latent_sum/pallas_call | solution.py:40
  (14 shorter events, 0.2 us)
Async XLA Ops:
  3.6 6.1 %collective-permute-start = (bf16[1424,128]{1,0:T(8,128)(2,1)}, bf16[1424,128]{1,0:T(8,128)(2,1)S(1)}, u32[]{:S(2)}, u32[]{:S(2)}) collective-permute-start(bf16[1424,128]{1,0:T(8,128)(2,1)} %get-tuple-element.50.refs_1_), channel_id=1, source_target_pairs={{0,1},{1,0},{2,3},{3,2},{4,5},{5,4},{6,7},{7,6},{8,9},{9,8},{10,11... | collective-permute-start | bytes 1093640 | tf_op jit(solution)/shard_map/ppermute | solution.py:297
  4.1 7.2 %collective-permute-start.4 = (bf16[4,128,128]{2,1,0:T(8,128)(2,1)}, bf16[4,128,128]{2,1,0:T(8,128)(2,1)S(1)}, u32[]{:S(2)}, u32[]{:S(2)}) collective-permute-start(bf16[4,128,128]{2,1,0:T(8,128)(2,1)} %get-tuple-element.54), channel_id=1, source_target_pairs={{0,1},{1,0},{2,3},{3,2},{4,5},{5,4},{6,7},{7,6},{8,9},{9,8},{10,11... | collective-permute-start | bytes 393224 | tf_op jit(solution)/shard_map/ppermute | solution.py:297
  4.2 13.1 %collective-permute-start.1 = (bf16[1424,128]{1,0:T(8,128)(2,1)}, bf16[1424,128]{1,0:T(8,128)(2,1)S(1)}, u32[]{:S(2)}, u32[]{:S(2)}) collective-permute-start(bf16[1424,128]{1,0:T(8,128)(2,1)} %get-tuple-element.50.refs_1_), channel_id=1, source_target_pairs={{0,2},{1,3},{2,0},{3,1},{4,6},{5,7},{6,4},{7,5},{8,10},{9,11},{10,... | collective-permute-start | bytes 1093640 | tf_op jit(solution)/shard_map/ppermute | solution.py:297
  7.1 10.1 %collective-permute-start.3 = (bf16[592,128]{1,0:T(8,128)(2,1)}, bf16[592,128]{1,0:T(8,128)(2,1)S(1)}, u32[]{:S(2)}, u32[]{:S(2)}) collective-permute-start(bf16[592,128]{1,0:T(8,128)(2,1)} %get-tuple-element.52.refs_0_), channel_id=1, source_target_pairs={{0,8},{1,9},{2,10},{3,11},{4,12},{5,13},{6,14},{7,15},{8,0},{9,1},... | collective-permute-start | bytes 454664 | tf_op jit(solution)/shard_map/ppermute | solution.py:297
  9.7 7.7 %collective-permute-start.2 = (bf16[592,128]{1,0:T(8,128)(2,1)}, bf16[592,128]{1,0:T(8,128)(2,1)S(1)}, u32[]{:S(2)}, u32[]{:S(2)}) collective-permute-start(bf16[592,128]{1,0:T(8,128)(2,1)} %get-tuple-element.52.refs_0_), channel_id=1, source_target_pairs={{0,4},{1,5},{2,6},{3,7},{4,0},{5,1},{6,2},{7,3},{8,12},{9,13},{10,... | collective-permute-start | bytes 454664 | tf_op jit(solution)/shard_map/ppermute | solution.py:297
  12.3 5.0 %collective-permute-start.5 = (bf16[4,128,128]{2,1,0:T(8,128)(2,1)S(1)}, bf16[4,128,128]{2,1,0:T(8,128)(2,1)S(1)}, u32[]{:S(2)}, u32[]{:S(2)}) collective-permute-start(bf16[4,128,128]{2,1,0:T(8,128)(2,1)S(1)} %add_convert_fusion.2), channel_id=1, source_target_pairs={{0,16},{16,0},{1,17},{17,1},{2,18},{18,2},{3,19},{19,3},{4,20},{20... | collective-permute-start | bytes 393224 | tf_op jit(solution)/shard_map/ppermute | solution.py:297
  13.8 1.0 %copy-start = (bf16[1424,128]{1,0:T(8,128)(2,1)S(1)}, bf16[1424,128]{1,0:T(8,128)(2,1)}, u32[]{:S(2)}) copy-start(bf16[1424,128]{1,0:T(8,128)(2,1)} %get-tuple-element.50.refs_1_) | copy-start | bytes 1093636
  14.8 0.9 %copy-start.2 = (bf16[592,128]{1,0:T(8,128)(2,1)S(1)}, bf16[592,128]{1,0:T(8,128)(2,1)}, u32[]{:S(2)}) copy-start(bf16[592,128]{1,0:T(8,128)(2,1)} %get-tuple-element.52.refs_0_) | copy-start | bytes 454660
  15.7 0.7 %copy-start.3 = (f32[8,128]{1,0:T(8,128)S(1)}, f32[8,128]{1,0:T(8,128)}, u32[]{:S(2)}) copy-start(f32[8,128]{1,0:T(8,128)} %get-tuple-element.55.refs_2_) | copy-start | bytes 12292
  17.4 2.1 %collective-permute-start.7 = (bf16[1424,128]{1,0:T(8,128)(2,1)S(1)}, bf16[1424,128]{1,0:T(8,128)(2,1)S(1)}, u32[]{:S(2)}, u32[]{:S(2)}) collective-permute-start(bf16[1424,128]{1,0:T(8,128)(2,1)S(1)} %collective-permute-done.1.refs_5_.refs_2_), channel_id=1, source_target_pairs={{0,1},{1,0},{2,3},{3,2},{4,5},{5,4},{6,7},{7,6},{8,9},{9,8},{10,11... | collective-permute-start | bytes 1093640 | tf_op jit(solution)/shard_map/ppermute | solution.py:297
  17.5 11.7 %copy-start.1 = (bf16[2,512,128]{2,1,0:T(8,128)(2,1)S(1)}, bf16[2,512,128]{2,1,0:T(8,128)(2,1)}, u32[]{:S(2)}) copy-start(bf16[2,512,128]{2,1,0:T(8,128)(2,1)} %refs_4_.1) | copy-start | bytes 786436
  17.5 4.6 %collective-permute-start.11 = (bf16[2,128,128]{2,1,0:T(8,128)(2,1)S(1)}, bf16[2,128,128]{2,1,0:T(8,128)(2,1)S(1)}, u32[]{:S(2)}, u32[]{:S(2)}) collective-permute-start(bf16[2,128,128]{2,1,0:T(8,128)(2,1)S(1)} %slice.17), channel_id=1, source_target_pairs={{0,2},{1,3},{2,0},{3,1},{4,6},{5,7},{6,4},{7,5},{8,10},{9,11},{10,... | collective-permute-start | bytes 196616 | tf_op jit(solution)/shard_map/ppermute | solution.py:297
  18.0 6.1 %collective-permute-start.6 = (bf16[592,128]{1,0:T(8,128)(2,1)S(1)}, bf16[592,128]{1,0:T(8,128)(2,1)S(1)}, u32[]{:S(2)}, u32[]{:S(2)}) collective-permute-start(bf16[592,128]{1,0:T(8,128)(2,1)S(1)} %collective-permute-done.3.refs_2_.refs_9_), channel_id=1, source_target_pairs={{0,4},{1,5},{2,6},{3,7},{4,0},{5,1},{6,2},{7,3},{8,12},{9,13},{10,... | collective-permute-start | bytes 454664 | tf_op jit(solution)/shard_map/ppermute | solution.py:297
  22.1 5.0 %collective-permute-start.12 = (bf16[2,128,128]{2,1,0:T(8,128)(2,1)S(1)}, bf16[2,128,128]{2,1,0:T(8,128)(2,1)S(1)}, u32[]{:S(2)}, u32[]{:S(2)}) collective-permute-start(bf16[2,128,128]{2,1,0:T(8,128)(2,1)S(1)} %add_convert_fusion.5), channel_id=1, source_target_pairs={{0,4},{1,5},{2,6},{3,7},{4,0},{5,1},{6,2},{7,3},{8,12},{9,13},{10,... | collective-permute-start | bytes 196616 | tf_op jit(solution)/shard_map/ppermute | solution.py:297
  24.6 6.2 %collective-permute-start.8 = (f32[16,128]{1,0:T(8,128)S(1)}, f32[16,128]{1,0:T(8,128)S(1)}, u32[]{:S(2)}, u32[]{:S(2)}) collective-permute-start(f32[16,128]{1,0:T(8,128)S(1)} %get-tuple-element.68.refs_0_), channel_id=1, source_target_pairs={{0,1},{1,0},{2,3},{3,2},{4,5},{5,4},{6,7},{7,6},{8,9},{9,8},{10,11... | collective-permute-start | bytes 24584 | tf_op jit(solution)/shard_map/ppermute | solution.py:297
  24.7 6.1 %collective-permute-start.9 = (f32[16,128]{1,0:T(8,128)S(1)}, f32[16,128]{1,0:T(8,128)S(1)}, u32[]{:S(2)}, u32[]{:S(2)}) collective-permute-start(f32[16,128]{1,0:T(8,128)S(1)} %get-tuple-element.68.refs_0_), channel_id=1, source_target_pairs={{0,2},{1,3},{2,0},{3,1},{4,6},{5,7},{6,4},{7,5},{8,10},{9,11},{10,... | collective-permute-start | bytes 24584 | tf_op jit(solution)/shard_map/ppermute | solution.py:297
  27.0 3.8 %collective-permute-start.10 = (f32[16,128]{1,0:T(8,128)S(1)}, f32[16,128]{1,0:T(8,128)S(1)}, u32[]{:S(2)}, u32[]{:S(2)}) collective-permute-start(f32[16,128]{1,0:T(8,128)S(1)} %get-tuple-element.68.refs_0_), channel_id=1, source_target_pairs={{0,3},{1,2},{2,1},{3,0},{4,7},{5,6},{6,5},{7,4},{8,11},{9,10},{10,... | collective-permute-start | bytes 24584 | tf_op jit(solution)/shard_map/ppermute | solution.py:297
  27.1 6.5 %collective-permute-start.13 = (bf16[2,128,128]{2,1,0:T(8,128)(2,1)S(1)}, bf16[2,128,128]{2,1,0:T(8,128)(2,1)S(1)}, u32[]{:S(2)}, u32[]{:S(2)}) collective-permute-start(bf16[2,128,128]{2,1,0:T(8,128)(2,1)S(1)} %add_convert_fusion.4), channel_id=1, source_target_pairs={{0,8},{1,9},{2,10},{3,11},{4,12},{5,13},{6,14},{7,15},{8,0},{9,1},... | collective-permute-start | bytes 196616 | tf_op jit(solution)/shard_map/ppermute | solution.py:297
  31.6 8.7 %collective-permute-start.20 = (bf16[576,128]{1,0:T(8,128)(2,1)S(1)}, bf16[576,128]{1,0:T(8,128)(2,1)S(1)}, u32[]{:S(2)}, u32[]{:S(2)}) collective-permute-start(bf16[576,128]{1,0:T(8,128)(2,1)S(1)} %get-tuple-element.94), channel_id=1, source_target_pairs={{0,4},{1,5},{2,6},{3,7},{4,0},{5,1},{6,2},{7,3},{8,12},{9,13},{10,... | collective-permute-start | bytes 442376 | tf_op jit(solution)/shard_map/ppermute | solution.py:297
  33.7 4.5 %collective-permute-start.14 = (bf16[2,128,128]{2,1,0:T(8,128)(2,1)S(1)}, bf16[2,128,128]{2,1,0:T(8,128)(2,1)S(1)}, u32[]{:S(2)}, u32[]{:S(2)}) collective-permute-start(bf16[2,128,128]{2,1,0:T(8,128)(2,1)S(1)} %add_convert_fusion.3.refs_0_), channel_id=1, source_target_pairs={{0,2},{1,3},{2,0},{3,1},{4,6},{5,7},{6,4},{7,5},{8,10},{9,11},{10,... | collective-permute-start | bytes 196616 | tf_op jit(solution)/shard_map/ppermute | solution.py:297
  36.8 1.9 %collective-permute-start.15 = (bf16[384,128]{1,0:T(8,128)(2,1)S(1)}, bf16[384,128]{1,0:T(8,128)(2,1)S(1)}, u32[]{:S(2)}, u32[]{:S(2)}) collective-permute-start(bf16[384,128]{1,0:T(8,128)(2,1)S(1)} %get-tuple-element.85), channel_id=1, source_target_pairs={{0,1},{1,0},{2,3},{3,2},{4,5},{5,4},{6,7},{7,6},{8,9},{9,8},{10,11... | collective-permute-start | bytes 294920 | tf_op jit(solution)/shard_map/ppermute | solution.py:297
  36.9 1.9 %collective-permute-start.16 = (bf16[384,128]{1,0:T(8,128)(2,1)S(1)}, bf16[384,128]{1,0:T(8,128)(2,1)S(1)}, u32[]{:S(2)}, u32[]{:S(2)}) collective-permute-start(bf16[384,128]{1,0:T(8,128)(2,1)S(1)} %get-tuple-element.86), channel_id=1, source_target_pairs={{0,1},{1,0},{2,3},{3,2},{4,5},{5,4},{6,7},{7,6},{8,9},{9,8},{10,11... | collective-permute-start | bytes 294920 | tf_op jit(solution)/shard_map/ppermute | solution.py:297
  37.4 1.4 %collective-permute-start.17 = (bf16[384,128]{1,0:T(8,128)(2,1)S(1)}, bf16[384,128]{1,0:T(8,128)(2,1)S(1)}, u32[]{:S(2)}, u32[]{:S(2)}) collective-permute-start(bf16[384,128]{1,0:T(8,128)(2,1)S(1)} %get-tuple-element.87), channel_id=1, source_target_pairs={{0,1},{1,0},{2,3},{3,2},{4,5},{5,4},{6,7},{7,6},{8,9},{9,8},{10,11... | collective-permute-start | bytes 294920 | tf_op jit(solution)/shard_map/ppermute | solution.py:297
  38.2 6.8 %collective-permute-start.23 = (bf16[4,128,128]{2,1,0:T(8,128)(2,1)S(1)}, bf16[4,128,128]{2,1,0:T(8,128)(2,1)S(1)}, u32[]{:S(2)}, u32[]{:S(2)}) collective-permute-start(bf16[4,128,128]{2,1,0:T(8,128)(2,1)S(1)} %pad_maximum_fusion), channel_id=1, source_target_pairs={{0,1},{1,0},{2,3},{3,2},{4,5},{5,4},{6,7},{7,6},{8,9},{9,8},{10,11... | collective-permute-start | bytes 393224 | tf_op jit(solution)/shard_map/ppermute | solution.py:297
  38.8 9.1 %collective-permute-start.19 = (bf16[2,576,128]{2,1,0:T(8,128)(2,1)S(1)}, bf16[2,576,128]{2,1,0:T(8,128)(2,1)S(1)}, u32[]{:S(2)}, u32[]{:S(2)}) collective-permute-start(bf16[2,576,128]{2,1,0:T(8,128)(2,1)S(1)} %join.1), channel_id=1, source_target_pairs={{0,2},{1,3},{2,0},{3,1},{4,6},{5,7},{6,4},{7,5},{8,10},{9,11},{10,... | collective-permute-start | bytes 884744 | tf_op jit(solution)/shard_map/ppermute | solution.py:297
  40.2 5.7 %collective-permute-start.18 = (bf16[2,576,128]{2,1,0:T(8,128)(2,1)S(1)}, bf16[2,576,128]{2,1,0:T(8,128)(2,1)S(1)}, u32[]{:S(2)}, u32[]{:S(2)}) collective-permute-start(bf16[2,576,128]{2,1,0:T(8,128)(2,1)S(1)} %get-tuple-element.88), channel_id=1, source_target_pairs={{0,1},{1,0},{2,3},{3,2},{4,5},{5,4},{6,7},{7,6},{8,9},{9,8},{10,11... | collective-permute-start | bytes 884744 | tf_op jit(solution)/shard_map/ppermute | solution.py:297
  40.4 10.2 %collective-permute-start.21 = (bf16[576,128]{1,0:T(8,128)(2,1)S(1)}, bf16[576,128]{1,0:T(8,128)(2,1)S(1)}, u32[]{:S(2)}, u32[]{:S(2)}) collective-permute-start(bf16[576,128]{1,0:T(8,128)(2,1)S(1)} %add_convert_fusion), channel_id=1, source_target_pairs={{0,8},{1,9},{2,10},{3,11},{4,12},{5,13},{6,14},{7,15},{8,0},{9,1},... | collective-permute-start | bytes 442376 | tf_op jit(solution)/shard_map/ppermute | solution.py:297
  42.1 10.0 %collective-permute-start.22 = (bf16[576,128]{1,0:T(8,128)(2,1)S(1)}, bf16[576,128]{1,0:T(8,128)(2,1)S(1)}, u32[]{:S(2)}, u32[]{:S(2)}) collective-permute-start(bf16[576,128]{1,0:T(8,128)(2,1)S(1)} %get-tuple-element.96), channel_id=1, source_target_pairs={{0,4},{1,5},{2,6},{3,7},{4,0},{5,1},{6,2},{7,3},{8,12},{9,13},{10,... | collective-permute-start | bytes 442376 | tf_op jit(solution)/shard_map/ppermute | solution.py:297

commit v14 on v13

--- a/solution.py
+++ b/solution.py
@@ -12,7 +12,7 @@
 HEAD_DIM = 128
 GROUP = 4
 EXTRA = 16
-CUTS = 3
+CUTS = 2
 PACK_LIMIT = 63 << 20
 F32 = jnp.float32
 BF16 = jnp.bfloat16
@@ -188,7 +188,7 @@
         last_gp_ref[:, cols] = mm(last_k_ref[:, :lat], g_ref[:, cols])
 
 
-def pair_kernel(heads, *refs):
+def pair_kernel(heads, keys, *refs):
     stats, (s_ref, gp_ref, gs_ref, p_ref) = refs[:GROUP], refs[GROUP : GROUP + 4]
     all_rows = s_ref.shape[1]
     rows = all_rows // GROUP
@@ -204,8 +204,8 @@
         lse = top + jnp.log(sum(jnp.exp(part - top) for part in lse_parts))
         at = GROUP * heads
         delta = jnp.concatenate([stats[j][at + h : at + h + 1, :] for h in range(heads)], axis=1)
-        p = jnp.exp(s_ref[:, cols] - lse)
-        gs_ref[:, cols] = (p * (gp_ref[:, cols] - delta)).astype(BF16)
+        p = jnp.exp(s_ref[keys, cols] - lse)
+        gs_ref[:, cols] = (p * (gp_ref[keys, cols] - delta)).astype(BF16)
         p_ref[:, cols] = p.astype(BF16)
 
 
@@ -218,10 +218,10 @@
         part_refs[a][lat:, :] = along[lat:].astype(BF16)
 
 
-def last_kernel(factor, width, heads, *refs):
+def block_kernel(factor, keys, width, heads, *refs):
     stats, refs = refs[:GROUP], refs[GROUP:]
     s_ref, gp_ref, g_ref, q_all_ref, part_ref, gs_ref, p_ref = refs
-    pair_kernel(heads, *stats, s_ref, gp_ref, gs_ref, p_ref)
+    pair_kernel(heads, keys, *stats, s_ref, gp_ref, gs_ref, p_ref)
     partial_kernel(factor, [slice(None)], width, g_ref, q_all_ref, gs_ref, p_ref, part_ref)
 
 
@@ -235,7 +235,7 @@
     rows = heads * tok
     for a in range(nkey):
         kt[:, a * tok : (a + 1) * tok] = lat_refs[a][:width, :]
-    pair_kernel(heads, *stats, s_ref, gp_ref, gs_ref, p_ref)
+    pair_kernel(heads, slice(None), *stats, s_ref, gp_ref, gs_ref, p_ref)
     for j in range(GROUP):
         cols = slice(j * rows, (j + 1) * rows)
         gq = mm(kt[:, :keys], gs_ref[:, cols]) + mm(kt[:, keys:], last_gs_ref[:, cols])
@@ -411,15 +411,20 @@
     for step_hop in line_hops[1:-1]:
         mine = add(mine, swap(mine, *step_hop))
     near = swap(mine, *line_hops[-1])
-    last_part, last_gs = call(
-        functools.partial(last_kernel, factor, width, heads),
-        "last_gradients",
-        [((width, tok), BF16), ((tok, all_rows), BF16)],
-        stats + [last_s, last_gp, g, q_all],
-        [((tok, all_rows), BF16)],
-        flops=2 * tok * all_rows * (width + lat),
-    )
+    def block(name, keys_at, s, gp):
+        return call(
+            functools.partial(block_kernel, factor, keys_at, width, heads),
+            name,
+            [((width, tok), BF16), ((tok, all_rows), BF16)],
+            stats + [s, gp, g, q_all],
+            [((tok, all_rows), BF16)],
+            flops=2 * tok * all_rows * (width + lat),
+        )
+
+    last_part, last_gs = block("last_gradients", slice(None), last_s, last_gp)
     last_got = swap(last_part, GROUP)
+    next_part, _ = block("next_gradients", slice(tok, 2 * tok), near_s, near_gp)
+    next_got = swap(next_part, GROUP)
     mine = add(mine, near)
     gq_shape, cut_shape = (heads, width, tok), (heads * width // CUTS, tok)
     gq_own, gq_core, gq_across, *far_cuts, near_gs, near_p = call(
@@ -450,7 +455,8 @@
 
     middle = lines // 2
     made = partials("middle_gradients", [middle], near_gs, near_p, 3)
-    made.update(partials("near_gradients", [m for m in range(most) if m != middle], near_gs, after(near_p, *far_cuts)))
+    made.update(partials("near_gradients", [m for m in range(most) if m not in (1, middle)], near_gs, after(near_p, *far_cuts)))
+    made[1] = next_part
     near_parts = [made[m] for m in range(most)]
     parts = list(near_parts) + [last_part]
     kept = [parts[0]]
@@ -461,8 +467,7 @@
     mine_two = jnp.concatenate([mine, across], axis=0)
     other_two = swap(mine_two, 1)
     pieces = [mine_two[:heads], other_two[:heads], mine_two[heads:], other_two[heads:]]
-    parts[1] = after(parts[1], gq_sum)
-    kept += [swap(parts[1 << bit], GROUP << bit) for bit in reversed(range(line_bits))]
+    kept += [swap(parts[1 << bit], GROUP << bit) for bit in range(1, line_bits)] + [next_got]
     scale = 1.0 / math.sqrt(tok * n_ctx * n_dp)
     (grad_w,) = call(
         functools.partial(spread_kernel, scale),

time: 53.1 us -> 52.5 us (0.989)
  starting transfers between devices: 27 us -> 24.5 us
  waiting for transfers between devices: 8.55 us -> 9.64 us
  Pallas kernels: 12.8 us -> 13.6 us
    ppermute x24 -> x23, starting transfers between devices: 27 us -> 24.5 us  [swap(): return lax.ppermute(x, axis, [(i, i ^ mask) for i in range(size)])]
    ppermute x24 -> x23, waiting for transfers between devices: 8.55 us -> 9.64 us  [swap(): return lax.ppermute(x, axis, [(i, i ^ mask) for i in range(size)])]
    pallas_call x13 -> x14, Pallas kernels: 12.8 us -> 13.6 us  [call(): pl.pallas_call(kernel, out_shape=[jax.ShapeDtypeStruct(s, d) for s, d in...]
  transfers between devices with their start and end apart: 24 -> 23, of which waited for: 9 -> 8; matrix products, arithmetic and copies ran while one was open for 2% -> 2% of each run, Pallas kernels for 17% -> 19%
where the time goes in v14:
time: 52.5 us; the launch traced here: 52.2 us
  starting transfers between devices  24.5 us (47%)
  Pallas kernels  13.6 us (26%)
  waiting for transfers between devices  9.64 us (18%)
  local copies, waits for them, and re-layouts  2.6 us (5%)
  other arithmetic  1.1 us (2%)
  between operations  0.84 us (2%)
    ppermute x23, starting transfers between devices, swap(): return lax.ppermute(x, axis, [(i, i ^ mask) for i in range(size)])  24.5 us
    pallas_call x14, Pallas kernels, call(): pl.pallas_call(kernel, out_shape=[jax.ShapeDtypeStruct(s, d) for s, d in...  13.6 us
    ppermute x23, waiting for transfers between devices, swap(): return lax.ppermute(x, axis, [(i, i ^ mask) for i in range(size)])  9.64 us
    unnamed x8, local copies, waits for them, and re-layouts  2.58 us
    convert_element_type x6, other arithmetic, add(): return (a.astype(F32) + b.astype(F32)).astype(BF16)  1.09 us
  transfers between devices with their start and end apart: 23, of which 8 were waited for; matrix products, arithmetic and copies ran while one was open for 2% of the time, Pallas kernels for 19%

profile of v14, /device:TPU:0, one launch (start us, length us, event | category | flops | bytes accessed | tf_op | source)
XLA Modules:
  0.0 52.2 jit_solution(14602476028173495611)
XLA Ops:
  0.6 3.0 %pack.1 = (bf16[592,128]{1,0:T(8,128)(2,1)}, bf16[1424,128]{1,0:T(8,128)(2,1)}, f32[8,128]{1,0:T(8,128)}, bf16[4,128,128]{2,1,0:T(8,128)(2,1)}, bf16[4,128,128]{2,1,0:T(8,128)(2,1)}) custom-call(s32[1]{0:T(128)} %bitcast.idx_ref, s32[1,128]{1,0:T(1,128)} %pos_hbm.1, bf16[2,576,128]{2,1,0:T(8,128)(2,1)} %bitcast.15, bf16[128,2,128]{2,1,0:T(2,128)(2,1)} %bitcast.20, ...), custom_call_target="tpu_custom_call" | custom-call | bytes 1815044 | tf_op jit(solution)/shard_map/pack/pallas_call | solution.py:40
  3.6 0.5 collective-permute-start
  4.1 0.1 collective-permute-start.4
  4.2 2.9 %collective-permute-start.1 = (bf16[1424,128]{1,0:T(8,128)(2,1)}, bf16[1424,128]{1,0:T(8,128)(2,1)S(1)}, u32[]{:S(2)}, u32[]{:S(2)}) collective-permute-start(bf16[1424,128]{1,0:T(8,128)(2,1)} %get-tuple-element.47.refs_1_), channel_id=1, source_target_pairs={{0,2},{1,3},{2,0},{3,1},{4,6},{5,7},{6,4},{7,5},{8,10},{9,11},{10,... | collective-permute-start | bytes 1093640 | tf_op jit(solution)/shard_map/ppermute | solution.py:297
  7.1 2.6 %collective-permute-start.3 = (bf16[592,128]{1,0:T(8,128)(2,1)}, bf16[592,128]{1,0:T(8,128)(2,1)S(1)}, u32[]{:S(2)}, u32[]{:S(2)}) collective-permute-start(bf16[592,128]{1,0:T(8,128)(2,1)} %get-tuple-element.49.refs_0_), channel_id=1, source_target_pairs={{0,8},{1,9},{2,10},{3,11},{4,12},{5,13},{6,14},{7,15},{8,0},{9,1},... | collective-permute-start | bytes 454664 | tf_op jit(solution)/shard_map/ppermute | solution.py:297
  9.7 0.0 collective-permute-done.refs_4_.refs_1_
  9.7 1.6 %collective-permute-start.2 = (bf16[592,128]{1,0:T(8,128)(2,1)}, bf16[592,128]{1,0:T(8,128)(2,1)S(1)}, u32[]{:S(2)}, u32[]{:S(2)}) collective-permute-start(bf16[592,128]{1,0:T(8,128)(2,1)} %get-tuple-element.49.refs_0_), channel_id=1, source_target_pairs={{0,4},{1,5},{2,6},{3,7},{4,0},{5,1},{6,2},{7,3},{8,12},{9,13},{10,... | collective-permute-start | bytes 454664 | tf_op jit(solution)/shard_map/ppermute | solution.py:297
  11.3 0.0 collective-permute-done.4
  11.3 0.9 %add_convert_fusion.2 = bf16[4,128,128]{2,1,0:T(8,128)(2,1)S(1)} fusion(bf16[4,128,128]{2,1,0:T(8,128)(2,1)S(1)} %collective-permute-done.4, bf16[4,128,128]{2,1,0:T(8,128)(2,1)} %get-tuple-element.50), kind=kLoop, calls=%fused_computation.2 | loop fusion | flops 262144 | bytes 393216 | tf_op jit(solution)/shard_map/convert_element_type | solution.py:345
  12.3 1.6 %collective-permute-start.5 = (bf16[4,128,128]{2,1,0:T(8,128)(2,1)S(1)}, bf16[4,128,128]{2,1,0:T(8,128)(2,1)S(1)}, u32[]{:S(2)}, u32[]{:S(2)}) collective-permute-start(bf16[4,128,128]{2,1,0:T(8,128)(2,1)S(1)} %add_convert_fusion.2), channel_id=1, source_target_pairs={{0,16},{16,0},{1,17},{17,1},{2,18},{18,2},{3,19},{19,3},{4,20},{20... | collective-permute-start | bytes 393224 | tf_op jit(solution)/shard_map/ppermute | solution.py:297
  13.8 1.0 %copy-done = bf16[1424,128]{1,0:T(8,128)(2,1)S(1)} copy-done((bf16[1424,128]{1,0:T(8,128)(2,1)S(1)}, bf16[1424,128]{1,0:T(8,128)(2,1)}, u32[]{:S(2)}) %copy-start) | copy-done | bytes 364568
  14.8 0.9 %copy-done.2 = bf16[592,128]{1,0:T(8,128)(2,1)S(1)} copy-done((bf16[592,128]{1,0:T(8,128)(2,1)S(1)}, bf16[592,128]{1,0:T(8,128)(2,1)}, u32[]{:S(2)}) %copy-start.2) | copy-done | bytes 151576
  15.7 0.7 %copy-done.3 = f32[8,128]{1,0:T(8,128)S(1)} copy-done((f32[8,128]{1,0:T(8,128)S(1)}, f32[8,128]{1,0:T(8,128)}, u32[]{:S(2)}) %copy-start.3) | copy-done | bytes 4120
  16.4 0.8 %collective-permute-done.3.refs_2_.refs_9_ = bf16[592,128]{1,0:T(8,128)(2,1)S(1)} collective-permute-done((bf16[592,128]{1,0:T(8,128)(2,1)}, bf16[592,128]{1,0:T(8,128)(2,1)S(1)}, u32[]{:S(2)}, u32[]{:S(2)}) %collective-permute-start.3) | collective-permute-done | bytes 151584 | tf_op jit(solution)/shard_map/ppermute | solution.py:297
  17.2 0.1 collective-permute-done.5
  17.3 0.0 collective-permute-done.1.refs_5_.refs_2_
  17.3 0.1 collective-permute-done.2.refs_1_.refs_8_
  17.4 0.0 collective-permute-start.7
  17.5 0.0 copy-start.1
  17.5 0.5 %collective-permute-start.11 = (bf16[2,128,128]{2,1,0:T(8,128)(2,1)S(1)}, bf16[2,128,128]{2,1,0:T(8,128)(2,1)S(1)}, u32[]{:S(2)}, u32[]{:S(2)}) collective-permute-start(bf16[2,128,128]{2,1,0:T(8,128)(2,1)S(1)} %slice.17), channel_id=1, source_target_pairs={{0,2},{1,3},{2,0},{3,1},{4,6},{5,7},{6,4},{7,5},{8,10},{9,11},{10,... | collective-permute-start | bytes 196616 | tf_op jit(solution)/shard_map/ppermute | solution.py:297
  18.0 1.5 %collective-permute-start.6 = (bf16[592,128]{1,0:T(8,128)(2,1)S(1)}, bf16[592,128]{1,0:T(8,128)(2,1)S(1)}, u32[]{:S(2)}, u32[]{:S(2)}) collective-permute-start(bf16[592,128]{1,0:T(8,128)(2,1)S(1)} %collective-permute-done.3.refs_2_.refs_9_), channel_id=1, source_target_pairs={{0,4},{1,5},{2,6},{3,7},{4,0},{5,1},{6,2},{7,3},{8,12},{9,13},{10,... | collective-permute-start | bytes 454664 | tf_op jit(solution)/shard_map/ppermute | solution.py:297
  19.6 0.0 collective-permute-done.7.refs_6_.refs_3_
  19.6 1.2 %near_scores.1 = (f32[384,1024]{1,0:T(8,128)S(1)}, bf16[384,640]{1,0:T(8,128)(2,1)S(1)}, f32[16,128]{1,0:T(8,128)S(1)}, bf16[640,1024]{1,0:T(8,128)(2,1)S(1)}) custom-call(bf16[592,128]{1,0:T(8,128)(2,1)S(1)} %get-tuple-element.57.refs_0_.refs_7_, bf16[592,128]{1,0:T(8,128)(2,1)S(1)} %collective-permute-done.2.refs_1_.refs_8_, ...), custom_call_target="tpu_custom_call" | custom-call | tf_op jit(solution)/shard_map/near_scores/pallas_call | solution.py:40
  20.8 1.3 %collective-permute-done.11 = bf16[2,128,128]{2,1,0:T(8,128)(2,1)S(1)} collective-permute-done((bf16[2,128,128]{2,1,0:T(8,128)(2,1)S(1)}, bf16[2,128,128]{2,1,0:T(8,128)(2,1)S(1)}, u32[]{:S(2)}, u32[]{:S(2)}) %collective-permute-start.11) | collective-permute-done | bytes 65568 | tf_op jit(solution)/shard_map/ppermute | solution.py:297
  22.1 1.5 %collective-permute-start.12 = (bf16[2,128,128]{2,1,0:T(8,128)(2,1)S(1)}, bf16[2,128,128]{2,1,0:T(8,128)(2,1)S(1)}, u32[]{:S(2)}, u32[]{:S(2)}) collective-permute-start(bf16[2,128,128]{2,1,0:T(8,128)(2,1)S(1)} %add_convert_fusion.5), channel_id=1, source_target_pairs={{0,4},{1,5},{2,6},{3,7},{4,0},{5,1},{6,2},{7,3},{8,12},{9,13},{10,... | collective-permute-start | bytes 196616 | tf_op jit(solution)/shard_map/ppermute | solution.py:297
  23.6 0.5 collective-permute-done.6.refs_0_.refs_10_
  24.1 0.5 last_scores.1
  24.6 0.1 collective-permute-start.8
  24.7 2.3 %collective-permute-start.9 = (f32[16,128]{1,0:T(8,128)S(1)}, f32[16,128]{1,0:T(8,128)S(1)}, u32[]{:S(2)}, u32[]{:S(2)}) collective-permute-start(f32[16,128]{1,0:T(8,128)S(1)} %get-tuple-element.65.refs_0_), channel_id=1, source_target_pairs={{0,2},{1,3},{2,0},{3,1},{4,6},{5,7},{6,4},{7,5},{8,10},{9,11},{10,... | collective-permute-start | bytes 24584 | tf_op jit(solution)/shard_map/ppermute | solution.py:297
  27.0 0.1 collective-permute-start.10
  27.1 0.0 collective-permute-done.12
  27.1 2.1 %collective-permute-start.13 = (bf16[2,128,128]{2,1,0:T(8,128)(2,1)S(1)}, bf16[2,128,128]{2,1,0:T(8,128)(2,1)S(1)}, u32[]{:S(2)}, u32[]{:S(2)}) collective-permute-start(bf16[2,128,128]{2,1,0:T(8,128)(2,1)S(1)} %add_convert_fusion.4), channel_id=1, source_target_pairs={{0,8},{1,9},{2,10},{3,11},{4,12},{5,13},{6,14},{7,15},{8,0},{9,1},... | collective-permute-start | bytes 196616 | tf_op jit(solution)/shard_map/ppermute | solution.py:297
  29.2 1.6 %context.1 = (bf16[512,1024]{1,0:T(8,128)(2,1)S(1)}, f32[384,1024]{1,0:T(8,128)S(1)}, f32[128,1024]{1,0:T(8,128)S(1)}) custom-call(bf16[1424,128]{1,0:T(8,128)(2,1)S(1)} %get-tuple-element.59.refs_3_.refs_0_, bf16[1424,128]{1,0:T(8,128)(2,1)S(1)} %collective-permute-done.refs_4_.refs_1_, bf16[1424,128]{1,0:T(8,128)(2,1)S(1)} %collective-permute-done.1.refs_5_.refs_2_, ...), custom_call_target="tpu_custom_call" | custom-call | flops 2013265920 | bytes 16564224 | tf_op jit(solution)/shard_map/context/pallas_call | solution.py:40
  30.8 0.0 collective-permute-done.8.refs_1_
  30.8 0.0 collective-permute-done.9.refs_2_
  30.8 0.0 collective-permute-done.10.refs_3_
  30.8 0.8 %last_gradients.1 = (bf16[576,128]{1,0:T(8,128)(2,1)S(1)}, bf16[128,1024]{1,0:T(8,128)(2,1)S(1)}) custom-call(f32[16,128]{1,0:T(8,128)S(1)} %get-tuple-element.65.refs_0_, f32[16,128]{1,0:T(8,128)S(1)} %collective-permute-done.8.refs_1_, f32[16,128]{1,0:T(8,128)S(1)} %collective-permute-done.9.refs_2_, f32[16,128]{1,0:T(8,128)S(1)} %collective-permute-done.10.refs_3_, ...), custom_call_target="tpu_custom_call" | custom-call | flops 285212672 | bytes 3850240 | tf_op jit(solution)/shard_map/last_gradients/pallas_call | solution.py:40
  31.6 1.7 %collective-permute-start.19 = (bf16[576,128]{1,0:T(8,128)(2,1)S(1)}, bf16[576,128]{1,0:T(8,128)(2,1)S(1)}, u32[]{:S(2)}, u32[]{:S(2)}) collective-permute-start(bf16[576,128]{1,0:T(8,128)(2,1)S(1)} %get-tuple-element.89), channel_id=1, source_target_pairs={{0,4},{1,5},{2,6},{3,7},{4,0},{5,1},{6,2},{7,3},{8,12},{9,13},{10,... | collective-permute-start | bytes 442376 | tf_op jit(solution)/shard_map/ppermute | solution.py:297
  33.4 1.4 %next_gradients.1 = (bf16[576,128]{1,0:T(8,128)(2,1)S(1)}, bf16[128,1024]{1,0:T(8,128)(2,1)}) custom-call(f32[16,128]{1,0:T(8,128)S(1)} %get-tuple-element.65.refs_0_, f32[16,128]{1,0:T(8,128)S(1)} %collective-permute-done.8.refs_1_, f32[16,128]{1,0:T(8,128)S(1)} %collective-permute-done.9.refs_2_, f32[16,128]{1,0:T(8,128)S(1)} %collective-permute-done.10.refs_3_, ...), custom_call_target="tpu_custom_call" | custom-call | flops 285212672 | bytes 5947392 | tf_op jit(solution)/shard_map/next_gradients/pallas_call | solution.py:40
  34.8 0.4 collective-permute-start.21
  35.1 0.0 collective-permute-done.13
  35.2 1.4 %collective-permute-start.14 = (bf16[2,128,128]{2,1,0:T(8,128)(2,1)S(1)}, bf16[2,128,128]{2,1,0:T(8,128)(2,1)S(1)}, u32[]{:S(2)}, u32[]{:S(2)}) collective-permute-start(bf16[2,128,128]{2,1,0:T(8,128)(2,1)S(1)} %add_convert_fusion.3.refs_0_), channel_id=1, source_target_pairs={{0,2},{1,3},{2,0},{3,1},{4,6},{5,7},{6,4},{7,5},{8,10},{9,11},{10,... | collective-permute-start | bytes 196616 | tf_op jit(solution)/shard_map/ppermute | solution.py:297
  36.5 1.1 %query_gradients.1 = (bf16[2,576,128]{2,1,0:T(8,128)(2,1)S(1)}, bf16[2,576,128]{2,1,0:T(8,128)(2,1)S(1)}, bf16[2,576,128]{2,1,0:T(8,128)(2,1)S(1)}, bf16[576,128...) custom-call(f32[16,128]{1,0:T(8,128)S(1)} %get-tuple-element.65.refs, ...), custom_call_target="tpu_custom_call" | custom-call | tf_op jit(solution)/shard_map/query_gradients/pallas_call | solution.py:40
  37.7 0.1 collective-permute-start.15
  37.8 0.5 collective-permute-start.16
  38.3 0.7 %middle_gradients.1 = bf16[576,128]{1,0:T(8,128)(2,1)S(1)} custom-call(bf16[512,1024]{1,0:T(8,128)(2,1)S(1)} %get-tuple-element.72.refs_6_.g_ref, bf16[640,1024]{1,0:T(8,128)(2,1)S(1)} %get-tuple-element.62.refs_1_.refs_7_.q_all_ref, bf16[384,1024]{1,0:T(8,128)(2,1)S(1)} %get-tuple-element.85.gs_ref, bf16[384,1024]{1,0:T(8,128)(2,1)S(1)} %get-tuple-element.87.p_ref), custom_call_target="tpu_custom_call" | custom-call | flops 855638016 | bytes 12238848 | tf_op jit(solution)/shard_map/middle_gradients/pallas_call | solution.py:40
  39.0 0.5 collective-permute-done.14.refs_2_
  39.5 0.1 collective-permute-start.22
  39.6 0.0 collective-permute-done.15.refs_0_
  39.6 0.0 collective-permute-done.16.refs_1_
  39.6 0.1 join.1
  39.7 1.4 %collective-permute-start.18 = (bf16[2,576,128]{2,1,0:T(8,128)(2,1)S(1)}, bf16[2,576,128]{2,1,0:T(8,128)(2,1)S(1)}, u32[]{:S(2)}, u32[]{:S(2)}) collective-permute-start(bf16[2,576,128]{2,1,0:T(8,128)(2,1)S(1)} %join.1), channel_id=1, source_target_pairs={{0,2},{1,3},{2,0},{3,1},{4,6},{5,7},{6,4},{7,5},{8,10},{9,11},{10,... | collective-permute-start | bytes 884744 | tf_op jit(solution)/shard_map/ppermute | solution.py:297
  41.1 0.2 collective-permute-start.17
  41.3 0.0 collective-permute-done.19
  41.3 1.4 %collective-permute-start.20 = (bf16[576,128]{1,0:T(8,128)(2,1)S(1)}, bf16[576,128]{1,0:T(8,128)(2,1)S(1)}, u32[]{:S(2)}, u32[]{:S(2)}) collective-permute-start(bf16[576,128]{1,0:T(8,128)(2,1)S(1)} %add_convert_fusion), channel_id=1, source_target_pairs={{0,8},{1,9},{2,10},{3,11},{4,12},{5,13},{6,14},{7,15},{8,0},{9,1},... | collective-permute-start | bytes 442376 | tf_op jit(solution)/shard_map/ppermute | solution.py:297
  42.7 0.7 %near_gradients.1.refs_0_ = bf16[576,128]{1,0:T(8,128)(2,1)S(1)} custom-call(bf16[512,1024]{1,0:T(8,128)(2,1)S(1)} %get-tuple-element.72.refs_6_.g_ref, bf16[640,1024]{1,0:T(8,128)(2,1)S(1)} %get-tuple-element.62.refs_1_.refs_7_.q_all_ref, bf16[384,1024]{1,0:T(8,128)(2,1)S(1)} %get-tuple-element.85.gs_ref, bf16[384,1024]{1,0:T(8,128)(2,1)S(1)} %get-tuple-element.87.p_ref), custom_call_target="tpu_custom_call" | custom-call | flops 285212672 | bytes 4079616 | tf_op jit(solution)/shard_map/near_gradients/pallas_call | solution.py:40
  43.5 0.0 collective-permute-done.22
  43.5 0.8 %spread.1 = f32[2,512,128]{2,1,0:T(8,128)} custom-call(s32[1]{0:T(128)} %bitcast.idx_ref, bf16[2,128,128]{2,1,0:T(8,128)(2,1)S(1)} %add_convert_fusion.3.refs_0_, bf16[2,128,128]{2,1,0:T(8,128)(2,1)S(1)} %get-tuple-element.92.refs_1_, bf16[2,128,128]{2,1,0:T(8,128)(2,1)S(1)} %collective-permute-done.14.refs_2_, ...), custom_call_target="tpu_custom_call" | custom-call | bytes 786436 | tf_op jit(solution)/shard_map/spread/pallas_call | solution.py:40
  44.3 0.0 collective-permute-done.17.refs_1_
  44.3 4.8 %collective-permute-done.18.refs_2_ = bf16[2,576,128]{2,1,0:T(8,128)(2,1)S(1)} collective-permute-done((bf16[2,576,128]{2,1,0:T(8,128)(2,1)S(1)}, bf16[2,576,128]{2,1,0:T(8,128)(2,1)S(1)}, u32[]{:S(2)}, u32[]{:S(2)}) %collective-permute-start.18) | collective-permute-done | bytes 294944 | tf_op jit(solution)/shard_map/ppermute | solution.py:297
  49.1 0.8 %query_sum.1 = bf16[2,576,128]{2,1,0:T(8,128)(2,1)} custom-call(bf16[2,576,128]{2,1,0:T(8,128)(2,1)S(1)} %get-tuple-element.78.refs_0_, bf16[2,576,128]{2,1,0:T(8,128)(2,1)S(1)} %collective-permute-done.17.refs_1_, bf16[2,576,128]{2,1,0:T(8,128)(2,1)S(1)} %collective-permute-done.18.refs_2_), custom_call_target="tpu_custom_call" | custom-call | bytes 1179648 | tf_op jit(solution)/shard_map/query_sum/pallas_call | solution.py:40
  50.0 0.0 collective-permute-done.21.refs_2_
  50.0 1.5 %collective-permute-done.20.refs_1_ = bf16[576,128]{1,0:T(8,128)(2,1)S(1)} collective-permute-done((bf16[576,128]{1,0:T(8,128)(2,1)S(1)}, bf16[576,128]{1,0:T(8,128)(2,1)S(1)}, u32[]{:S(2)}, u32[]{:S(2)}) %collective-permute-start.20) | collective-permute-done | bytes 147488 | tf_op jit(solution)/shard_map/ppermute | solution.py:297
  51.5 0.7 %latent_sum.1 = bf16[576,128]{1,0:T(8,128)(2,1)} custom-call(bf16[576,128]{1,0:T(8,128)(2,1)S(1)} %near_gradients.1.refs_0_, bf16[576,128]{1,0:T(8,128)(2,1)S(1)} %collective-permute-done.20.refs_1_, bf16[576,128]{1,0:T(8,128)(2,1)S(1)} %collective-permute-done.21.refs_2_), custom_call_target="tpu_custom_call" | custom-call | bytes 589824 | tf_op jit(solution)/shard_map/latent_sum/pallas_call | solution.py:40
  (13 shorter events, 0.2 us)
Async XLA Ops:
  3.6 6.1 %collective-permute-start = (bf16[1424,128]{1,0:T(8,128)(2,1)}, bf16[1424,128]{1,0:T(8,128)(2,1)S(1)}, u32[]{:S(2)}, u32[]{:S(2)}) collective-permute-start(bf16[1424,128]{1,0:T(8,128)(2,1)} %get-tuple-element.47.refs_1_), channel_id=1, source_target_pairs={{0,1},{1,0},{2,3},{3,2},{4,5},{5,4},{6,7},{7,6},{8,9},{9,8},{10,11... | collective-permute-start | bytes 1093640 | tf_op jit(solution)/shard_map/ppermute | solution.py:297
  4.1 7.2 %collective-permute-start.4 = (bf16[4,128,128]{2,1,0:T(8,128)(2,1)}, bf16[4,128,128]{2,1,0:T(8,128)(2,1)S(1)}, u32[]{:S(2)}, u32[]{:S(2)}) collective-permute-start(bf16[4,128,128]{2,1,0:T(8,128)(2,1)} %get-tuple-element.51), channel_id=1, source_target_pairs={{0,1},{1,0},{2,3},{3,2},{4,5},{5,4},{6,7},{7,6},{8,9},{9,8},{10,11... | collective-permute-start | bytes 393224 | tf_op jit(solution)/shard_map/ppermute | solution.py:297
  4.2 13.1 %collective-permute-start.1 = (bf16[1424,128]{1,0:T(8,128)(2,1)}, bf16[1424,128]{1,0:T(8,128)(2,1)S(1)}, u32[]{:S(2)}, u32[]{:S(2)}) collective-permute-start(bf16[1424,128]{1,0:T(8,128)(2,1)} %get-tuple-element.47.refs_1_), channel_id=1, source_target_pairs={{0,2},{1,3},{2,0},{3,1},{4,6},{5,7},{6,4},{7,5},{8,10},{9,11},{10,... | collective-permute-start | bytes 1093640 | tf_op jit(solution)/shard_map/ppermute | solution.py:297
  7.1 10.1 %collective-permute-start.3 = (bf16[592,128]{1,0:T(8,128)(2,1)}, bf16[592,128]{1,0:T(8,128)(2,1)S(1)}, u32[]{:S(2)}, u32[]{:S(2)}) collective-permute-start(bf16[592,128]{1,0:T(8,128)(2,1)} %get-tuple-element.49.refs_0_), channel_id=1, source_target_pairs={{0,8},{1,9},{2,10},{3,11},{4,12},{5,13},{6,14},{7,15},{8,0},{9,1},... | collective-permute-start | bytes 454664 | tf_op jit(solution)/shard_map/ppermute | solution.py:297
  9.7 7.7 %collective-permute-start.2 = (bf16[592,128]{1,0:T(8,128)(2,1)}, bf16[592,128]{1,0:T(8,128)(2,1)S(1)}, u32[]{:S(2)}, u32[]{:S(2)}) collective-permute-start(bf16[592,128]{1,0:T(8,128)(2,1)} %get-tuple-element.49.refs_0_), channel_id=1, source_target_pairs={{0,4},{1,5},{2,6},{3,7},{4,0},{5,1},{6,2},{7,3},{8,12},{9,13},{10,... | collective-permute-start | bytes 454664 | tf_op jit(solution)/shard_map/ppermute | solution.py:297
  12.3 5.0 %collective-permute-start.5 = (bf16[4,128,128]{2,1,0:T(8,128)(2,1)S(1)}, bf16[4,128,128]{2,1,0:T(8,128)(2,1)S(1)}, u32[]{:S(2)}, u32[]{:S(2)}) collective-permute-start(bf16[4,128,128]{2,1,0:T(8,128)(2,1)S(1)} %add_convert_fusion.2), channel_id=1, source_target_pairs={{0,16},{16,0},{1,17},{17,1},{2,18},{18,2},{3,19},{19,3},{4,20},{20... | collective-permute-start | bytes 393224 | tf_op jit(solution)/shard_map/ppermute | solution.py:297
  13.8 1.0 %copy-start = (bf16[1424,128]{1,0:T(8,128)(2,1)S(1)}, bf16[1424,128]{1,0:T(8,128)(2,1)}, u32[]{:S(2)}) copy-start(bf16[1424,128]{1,0:T(8,128)(2,1)} %get-tuple-element.47.refs_1_) | copy-start | bytes 1093636
  14.8 0.9 %copy-start.2 = (bf16[592,128]{1,0:T(8,128)(2,1)S(1)}, bf16[592,128]{1,0:T(8,128)(2,1)}, u32[]{:S(2)}) copy-start(bf16[592,128]{1,0:T(8,128)(2,1)} %get-tuple-element.49.refs_0_) | copy-start | bytes 454660
  15.7 0.7 %copy-start.3 = (f32[8,128]{1,0:T(8,128)S(1)}, f32[8,128]{1,0:T(8,128)}, u32[]{:S(2)}) copy-start(f32[8,128]{1,0:T(8,128)} %get-tuple-element.52.refs_2_) | copy-start | bytes 12292
  17.4 2.1 %collective-permute-start.7 = (bf16[1424,128]{1,0:T(8,128)(2,1)S(1)}, bf16[1424,128]{1,0:T(8,128)(2,1)S(1)}, u32[]{:S(2)}, u32[]{:S(2)}) collective-permute-start(bf16[1424,128]{1,0:T(8,128)(2,1)S(1)} %collective-permute-done.1.refs_5_.refs_2_), channel_id=1, source_target_pairs={{0,1},{1,0},{2,3},{3,2},{4,5},{5,4},{6,7},{7,6},{8,9},{9,8},{10,11... | collective-permute-start | bytes 1093640 | tf_op jit(solution)/shard_map/ppermute | solution.py:297
  17.5 11.7 %copy-start.1 = (bf16[2,512,128]{2,1,0:T(8,128)(2,1)S(1)}, bf16[2,512,128]{2,1,0:T(8,128)(2,1)}, u32[]{:S(2)}) copy-start(bf16[2,512,128]{2,1,0:T(8,128)(2,1)} %refs_4_.1) | copy-start | bytes 786436
  17.5 4.6 %collective-permute-start.11 = (bf16[2,128,128]{2,1,0:T(8,128)(2,1)S(1)}, bf16[2,128,128]{2,1,0:T(8,128)(2,1)S(1)}, u32[]{:S(2)}, u32[]{:S(2)}) collective-permute-start(bf16[2,128,128]{2,1,0:T(8,128)(2,1)S(1)} %slice.17), channel_id=1, source_target_pairs={{0,2},{1,3},{2,0},{3,1},{4,6},{5,7},{6,4},{7,5},{8,10},{9,11},{10,... | collective-permute-start | bytes 196616 | tf_op jit(solution)/shard_map/ppermute | solution.py:297
  18.0 6.1 %collective-permute-start.6 = (bf16[592,128]{1,0:T(8,128)(2,1)S(1)}, bf16[592,128]{1,0:T(8,128)(2,1)S(1)}, u32[]{:S(2)}, u32[]{:S(2)}) collective-permute-start(bf16[592,128]{1,0:T(8,128)(2,1)S(1)} %collective-permute-done.3.refs_2_.refs_9_), channel_id=1, source_target_pairs={{0,4},{1,5},{2,6},{3,7},{4,0},{5,1},{6,2},{7,3},{8,12},{9,13},{10,... | collective-permute-start | bytes 454664 | tf_op jit(solution)/shard_map/ppermute | solution.py:297
  22.1 5.0 %collective-permute-start.12 = (bf16[2,128,128]{2,1,0:T(8,128)(2,1)S(1)}, bf16[2,128,128]{2,1,0:T(8,128)(2,1)S(1)}, u32[]{:S(2)}, u32[]{:S(2)}) collective-permute-start(bf16[2,128,128]{2,1,0:T(8,128)(2,1)S(1)} %add_convert_fusion.5), channel_id=1, source_target_pairs={{0,4},{1,5},{2,6},{3,7},{4,0},{5,1},{6,2},{7,3},{8,12},{9,13},{10,... | collective-permute-start | bytes 196616 | tf_op jit(solution)/shard_map/ppermute | solution.py:297
  24.6 6.2 %collective-permute-start.8 = (f32[16,128]{1,0:T(8,128)S(1)}, f32[16,128]{1,0:T(8,128)S(1)}, u32[]{:S(2)}, u32[]{:S(2)}) collective-permute-start(f32[16,128]{1,0:T(8,128)S(1)} %get-tuple-element.65.refs_0_), channel_id=1, source_target_pairs={{0,1},{1,0},{2,3},{3,2},{4,5},{5,4},{6,7},{7,6},{8,9},{9,8},{10,11... | collective-permute-start | bytes 24584 | tf_op jit(solution)/shard_map/ppermute | solution.py:297
  24.7 6.1 %collective-permute-start.9 = (f32[16,128]{1,0:T(8,128)S(1)}, f32[16,128]{1,0:T(8,128)S(1)}, u32[]{:S(2)}, u32[]{:S(2)}) collective-permute-start(f32[16,128]{1,0:T(8,128)S(1)} %get-tuple-element.65.refs_0_), channel_id=1, source_target_pairs={{0,2},{1,3},{2,0},{3,1},{4,6},{5,7},{6,4},{7,5},{8,10},{9,11},{10,... | collective-permute-start | bytes 24584 | tf_op jit(solution)/shard_map/ppermute | solution.py:297
  27.0 3.8 %collective-permute-start.10 = (f32[16,128]{1,0:T(8,128)S(1)}, f32[16,128]{1,0:T(8,128)S(1)}, u32[]{:S(2)}, u32[]{:S(2)}) collective-permute-start(f32[16,128]{1,0:T(8,128)S(1)} %get-tuple-element.65.refs_0_), channel_id=1, source_target_pairs={{0,3},{1,2},{2,1},{3,0},{4,7},{5,6},{6,5},{7,4},{8,11},{9,10},{10,... | collective-permute-start | bytes 24584 | tf_op jit(solution)/shard_map/ppermute | solution.py:297
  27.1 8.0 %collective-permute-start.13 = (bf16[2,128,128]{2,1,0:T(8,128)(2,1)S(1)}, bf16[2,128,128]{2,1,0:T(8,128)(2,1)S(1)}, u32[]{:S(2)}, u32[]{:S(2)}) collective-permute-start(bf16[2,128,128]{2,1,0:T(8,128)(2,1)S(1)} %add_convert_fusion.4), channel_id=1, source_target_pairs={{0,8},{1,9},{2,10},{3,11},{4,12},{5,13},{6,14},{7,15},{8,0},{9,1},... | collective-permute-start | bytes 196616 | tf_op jit(solution)/shard_map/ppermute | solution.py:297
  31.6 9.6 %collective-permute-start.19 = (bf16[576,128]{1,0:T(8,128)(2,1)S(1)}, bf16[576,128]{1,0:T(8,128)(2,1)S(1)}, u32[]{:S(2)}, u32[]{:S(2)}) collective-permute-start(bf16[576,128]{1,0:T(8,128)(2,1)S(1)} %get-tuple-element.89), channel_id=1, source_target_pairs={{0,4},{1,5},{2,6},{3,7},{4,0},{5,1},{6,2},{7,3},{8,12},{9,13},{10,... | collective-permute-start | bytes 442376 | tf_op jit(solution)/shard_map/ppermute | solution.py:297
  34.8 15.2 %collective-permute-start.21 = (bf16[576,128]{1,0:T(8,128)(2,1)S(1)}, bf16[576,128]{1,0:T(8,128)(2,1)S(1)}, u32[]{:S(2)}, u32[]{:S(2)}) collective-permute-start(bf16[576,128]{1,0:T(8,128)(2,1)S(1)} %get-tuple-element.90), channel_id=1, source_target_pairs={{0,4},{1,5},{2,6},{3,7},{4,0},{5,1},{6,2},{7,3},{8,12},{9,13},{10,... | collective-permute-start | bytes 442376 | tf_op jit(solution)/shard_map/ppermute | solution.py:297
  35.2 4.3 %collective-permute-start.14 = (bf16[2,128,128]{2,1,0:T(8,128)(2,1)S(1)}, bf16[2,128,128]{2,1,0:T(8,128)(2,1)S(1)}, u32[]{:S(2)}, u32[]{:S(2)}) collective-permute-start(bf16[2,128,128]{2,1,0:T(8,128)(2,1)S(1)} %add_convert_fusion.3.refs_0_), channel_id=1, source_target_pairs={{0,2},{1,3},{2,0},{3,1},{4,6},{5,7},{6,4},{7,5},{8,10},{9,11},{10,... | collective-permute-start | bytes 196616 | tf_op jit(solution)/shard_map/ppermute | solution.py:297
  37.7 1.9 %collective-permute-start.15 = (bf16[576,128]{1,0:T(8,128)(2,1)S(1)}, bf16[576,128]{1,0:T(8,128)(2,1)S(1)}, u32[]{:S(2)}, u32[]{:S(2)}) collective-permute-start(bf16[576,128]{1,0:T(8,128)(2,1)S(1)} %get-tuple-element.82), channel_id=1, source_target_pairs={{0,1},{1,0},{2,3},{3,2},{4,5},{5,4},{6,7},{7,6},{8,9},{9,8},{10,11... | collective-permute-start | bytes 442376 | tf_op jit(solution)/shard_map/ppermute | solution.py:297
  37.8 1.8 %collective-permute-start.16 = (bf16[576,128]{1,0:T(8,128)(2,1)S(1)}, bf16[576,128]{1,0:T(8,128)(2,1)S(1)}, u32[]{:S(2)}, u32[]{:S(2)}) collective-permute-start(bf16[576,128]{1,0:T(8,128)(2,1)S(1)} %get-tuple-element.83), channel_id=1, source_target_pairs={{0,1},{1,0},{2,3},{3,2},{4,5},{5,4},{6,7},{7,6},{8,9},{9,8},{10,11... | collective-permute-start | bytes 442376 | tf_op jit(solution)/shard_map/ppermute | solution.py:297
  39.5 4.0 %collective-permute-start.22 = (bf16[4,128,128]{2,1,0:T(8,128)(2,1)S(1)}, bf16[4,128,128]{2,1,0:T(8,128)(2,1)S(1)}, u32[]{:S(2)}, u32[]{:S(2)}) collective-permute-start(bf16[4,128,128]{2,1,0:T(8,128)(2,1)S(1)} %pad_maximum_fusion), channel_id=1, source_target_pairs={{0,1},{1,0},{2,3},{3,2},{4,5},{5,4},{6,7},{7,6},{8,9},{9,8},{10,11... | collective-permute-start | bytes 393224 | tf_op jit(solution)/shard_map/ppermute | solution.py:297
  39.7 9.5 %collective-permute-start.18 = (bf16[2,576,128]{2,1,0:T(8,128)(2,1)S(1)}, bf16[2,576,128]{2,1,0:T(8,128)(2,1)S(1)}, u32[]{:S(2)}, u32[]{:S(2)}) collective-permute-start(bf16[2,576,128]{2,1,0:T(8,128)(2,1)S(1)} %join.1), channel_id=1, source_target_pairs={{0,2},{1,3},{2,0},{3,1},{4,6},{5,7},{6,4},{7,5},{8,10},{9,11},{10,... | collective-permute-start | bytes 884744 | tf_op jit(solution)/shard_map/ppermute | solution.py:297
  41.1 3.3 %collective-permute-start.17 = (bf16[2,576,128]{2,1,0:T(8,128)(2,1)S(1)}, bf16[2,576,128]{2,1,0:T(8,128)(2,1)S(1)}, u32[]{:S(2)}, u32[]{:S(2)}) collective-permute-start(bf16[2,576,128]{2,1,0:T(8,128)(2,1)S(1)} %get-tuple-element.84), channel_id=1, source_target_pairs={{0,1},{1,0},{2,3},{3,2},{4,5},{5,4},{6,7},{7,6},{8,9},{9,8},{10,11... | collective-permute-start | bytes 884744 | tf_op jit(solution)/shard_map/ppermute | solution.py:297
  41.3 10.2 %collective-permute-start.20 = (bf16[576,128]{1,0:T(8,128)(2,1)S(1)}, bf16[576,128]{1,0:T(8,128)(2,1)S(1)}, u32[]{:S(2)}, u32[]{:S(2)}) collective-permute-start(bf16[576,128]{1,0:T(8,128)(2,1)S(1)} %add_convert_fusion), channel_id=1, source_target_pairs={{0,8},{1,9},{2,10},{3,11},{4,12},{5,13},{6,14},{7,15},{8,0},{9,1},... | collective-permute-start | bytes 442376 | tf_op jit(solution)/shard_map/ppermute | solution.py:297

commit v15 on v14

--- a/solution.py
+++ b/solution.py
@@ -411,19 +411,20 @@
     for step_hop in line_hops[1:-1]:
         mine = add(mine, swap(mine, *step_hop))
     near = swap(mine, *line_hops[-1])
-    def block(name, keys_at, s, gp):
+    def block(name, keys_at, s, gp, keep):
+        part, pairs = ((width, tok), BF16), ((tok, all_rows), BF16)
         return call(
             functools.partial(block_kernel, factor, keys_at, width, heads),
             name,
-            [((width, tok), BF16), ((tok, all_rows), BF16)],
+            [part, pairs] if keep else [part],
             stats + [s, gp, g, q_all],
-            [((tok, all_rows), BF16)],
+            [pairs] if keep else [pairs] * 2,
             flops=2 * tok * all_rows * (width + lat),
         )
 
-    last_part, last_gs = block("last_gradients", slice(None), last_s, last_gp)
+    last_part, last_gs = block("last_gradients", slice(None), last_s, last_gp, True)
     last_got = swap(last_part, GROUP)
-    next_part, _ = block("next_gradients", slice(tok, 2 * tok), near_s, near_gp)
+    (next_part,) = block("next_gradients", slice(tok, 2 * tok), near_s, after(near_gp, last_part), False)
     next_got = swap(next_part, GROUP)
     mine = add(mine, near)
     gq_shape, cut_shape = (heads, width, tok), (heads * width // CUTS, tok)
@@ -476,10 +477,10 @@
         [idx] + pieces,
         smem=(0,),
     )
-    gq_pieces = [gq_own, gq_core, gq_last]
+    kept[0] = after(kept[0], grad_w)
+    (grad_lat,) = call(sum_kernel, "latent_sum", [((width, tok), BF16)], kept, flops=3 * 10**9)
+    gq_pieces = [gq_own, gq_core, after(gq_last, grad_lat)]
     (grad_q,) = call(sum_kernel, "query_sum", [((heads, width, tok), BF16)], gq_pieces)
-    kept[0] = after(kept[0], grad_q)
-    (grad_lat,) = call(sum_kernel, "latent_sum", [((width, tok), BF16)], kept)
     return (jnp.transpose(grad_q, (2, 0, 1))[None], grad_lat.T[None], grad_w)
 
 

time: 52.5 us -> 51.5 us (0.981)
  Pallas kernels: 13.6 us -> 13 us
    pallas_call x14, Pallas kernels: 13.6 us -> 13 us  [call(): pl.pallas_call(kernel, out_shape=[jax.ShapeDtypeStruct(s, d) for s, d in...]
  transfers between devices with their start and end apart: 23 -> 23, of which waited for: 8 -> 7; matrix products, arithmetic and copies ran while one was open for 2% -> 2% of each run, Pallas kernels for 19% -> 18%
where the time goes in v15:
time: 51.5 us; the launch traced here: 51.3 us
  starting transfers between devices  24.6 us (48%)
  Pallas kernels  13 us (25%)
  waiting for transfers between devices  9.17 us (18%)
  local copies, waits for them, and re-layouts  2.6 us (5%)
  other arithmetic  1.1 us (2%)
  between operations  0.83 us (2%)
    ppermute x23, starting transfers between devices, swap(): return lax.ppermute(x, axis, [(i, i ^ mask) for i in range(size)])  24.6 us
    pallas_call x14, Pallas kernels, call(): pl.pallas_call(kernel, out_shape=[jax.ShapeDtypeStruct(s, d) for s, d in...  13 us
    ppermute x23, waiting for transfers between devices, swap(): return lax.ppermute(x, axis, [(i, i ^ mask) for i in range(size)])  9.17 us
    unnamed x8, local copies, waits for them, and re-layouts  2.59 us
    convert_element_type x6, other arithmetic, add(): return (a.astype(F32) + b.astype(F32)).astype(BF16)  1.09 us
  transfers between devices with their start and end apart: 23, of which 7 were waited for; matrix products, arithmetic and copies ran while one was open for 2% of the time, Pallas kernels for 18%

profile of v15, /device:TPU:0, one launch (start us, length us, event | category | flops | bytes accessed | tf_op | source)
XLA Modules:
  0.0 51.3 jit_solution(3401550556365141276)
XLA Ops:
  0.6 3.0 %pack.1 = (bf16[592,128]{1,0:T(8,128)(2,1)}, bf16[1424,128]{1,0:T(8,128)(2,1)}, f32[8,128]{1,0:T(8,128)}, bf16[4,128,128]{2,1,0:T(8,128)(2,1)}, bf16[4,128,128]{2,1,0:T(8,128)(2,1)}) custom-call(s32[1]{0:T(128)} %bitcast.idx_ref, s32[1,128]{1,0:T(1,128)} %pos_hbm.1, bf16[2,576,128]{2,1,0:T(8,128)(2,1)} %bitcast.15, bf16[128,2,128]{2,1,0:T(2,128)(2,1)} %bitcast.19, ...), custom_call_target="tpu_custom_call" | custom-call | bytes 1815044 | tf_op jit(solution)/shard_map/pack/pallas_call | solution.py:40
  3.6 0.5 %collective-permute-start = (bf16[1424,128]{1,0:T(8,128)(2,1)}, bf16[1424,128]{1,0:T(8,128)(2,1)S(1)}, u32[]{:S(2)}, u32[]{:S(2)}) collective-permute-start(bf16[1424,128]{1,0:T(8,128)(2,1)} %get-tuple-element.48.refs_1_), channel_id=1, source_target_pairs={{0,1},{1,0},{2,3},{3,2},{4,5},{5,4},{6,7},{7,6},{8,9},{9,8},{10,11... | collective-permute-start | bytes 1093640 | tf_op jit(solution)/shard_map/ppermute | solution.py:297
  4.1 0.1 collective-permute-start.4
  4.2 2.9 %collective-permute-start.1 = (bf16[1424,128]{1,0:T(8,128)(2,1)}, bf16[1424,128]{1,0:T(8,128)(2,1)S(1)}, u32[]{:S(2)}, u32[]{:S(2)}) collective-permute-start(bf16[1424,128]{1,0:T(8,128)(2,1)} %get-tuple-element.48.refs_1_), channel_id=1, source_target_pairs={{0,2},{1,3},{2,0},{3,1},{4,6},{5,7},{6,4},{7,5},{8,10},{9,11},{10,... | collective-permute-start | bytes 1093640 | tf_op jit(solution)/shard_map/ppermute | solution.py:297
  7.1 2.6 %collective-permute-start.3 = (bf16[592,128]{1,0:T(8,128)(2,1)}, bf16[592,128]{1,0:T(8,128)(2,1)S(1)}, u32[]{:S(2)}, u32[]{:S(2)}) collective-permute-start(bf16[592,128]{1,0:T(8,128)(2,1)} %get-tuple-element.50.refs_0_), channel_id=1, source_target_pairs={{0,8},{1,9},{2,10},{3,11},{4,12},{5,13},{6,14},{7,15},{8,0},{9,1},... | collective-permute-start | bytes 454664 | tf_op jit(solution)/shard_map/ppermute | solution.py:297
  9.7 0.0 collective-permute-done.refs_4_.refs_1_
  9.7 1.6 %collective-permute-start.2 = (bf16[592,128]{1,0:T(8,128)(2,1)}, bf16[592,128]{1,0:T(8,128)(2,1)S(1)}, u32[]{:S(2)}, u32[]{:S(2)}) collective-permute-start(bf16[592,128]{1,0:T(8,128)(2,1)} %get-tuple-element.50.refs_0_), channel_id=1, source_target_pairs={{0,4},{1,5},{2,6},{3,7},{4,0},{5,1},{6,2},{7,3},{8,12},{9,13},{10,... | collective-permute-start | bytes 454664 | tf_op jit(solution)/shard_map/ppermute | solution.py:297
  11.3 0.0 collective-permute-done.4
  11.3 0.9 %add_convert_fusion.2 = bf16[4,128,128]{2,1,0:T(8,128)(2,1)S(1)} fusion(bf16[4,128,128]{2,1,0:T(8,128)(2,1)S(1)} %collective-permute-done.4, bf16[4,128,128]{2,1,0:T(8,128)(2,1)} %get-tuple-element.51), kind=kLoop, calls=%fused_computation.2 | loop fusion | flops 262144 | bytes 393216 | tf_op jit(solution)/shard_map/convert_element_type | solution.py:345
  12.3 1.6 %collective-permute-start.5 = (bf16[4,128,128]{2,1,0:T(8,128)(2,1)S(1)}, bf16[4,128,128]{2,1,0:T(8,128)(2,1)S(1)}, u32[]{:S(2)}, u32[]{:S(2)}) collective-permute-start(bf16[4,128,128]{2,1,0:T(8,128)(2,1)S(1)} %add_convert_fusion.2), channel_id=1, source_target_pairs={{0,16},{16,0},{1,17},{17,1},{2,18},{18,2},{3,19},{19,3},{4,20},{20... | collective-permute-start | bytes 393224 | tf_op jit(solution)/shard_map/ppermute | solution.py:297
  13.8 1.0 %copy-done = bf16[1424,128]{1,0:T(8,128)(2,1)S(1)} copy-done((bf16[1424,128]{1,0:T(8,128)(2,1)S(1)}, bf16[1424,128]{1,0:T(8,128)(2,1)}, u32[]{:S(2)}) %copy-start) | copy-done | bytes 364568
  14.8 0.9 %copy-done.2 = bf16[592,128]{1,0:T(8,128)(2,1)S(1)} copy-done((bf16[592,128]{1,0:T(8,128)(2,1)S(1)}, bf16[592,128]{1,0:T(8,128)(2,1)}, u32[]{:S(2)}) %copy-start.2) | copy-done | bytes 151576
  15.7 0.7 %copy-done.3 = f32[8,128]{1,0:T(8,128)S(1)} copy-done((f32[8,128]{1,0:T(8,128)S(1)}, f32[8,128]{1,0:T(8,128)}, u32[]{:S(2)}) %copy-start.3) | copy-done | bytes 4120
  16.4 0.8 %collective-permute-done.3.refs_2_.refs_9_ = bf16[592,128]{1,0:T(8,128)(2,1)S(1)} collective-permute-done((bf16[592,128]{1,0:T(8,128)(2,1)}, bf16[592,128]{1,0:T(8,128)(2,1)S(1)}, u32[]{:S(2)}, u32[]{:S(2)}) %collective-permute-start.3) | collective-permute-done | bytes 151584 | tf_op jit(solution)/shard_map/ppermute | solution.py:297
  17.2 0.1 collective-permute-done.5
  17.3 0.0 collective-permute-done.1.refs_5_.refs_2_
  17.3 0.1 collective-permute-done.2.refs_1_.refs_8_
  17.4 0.0 collective-permute-start.7
  17.5 0.0 copy-start.1
  17.5 0.5 %collective-permute-start.11 = (bf16[2,128,128]{2,1,0:T(8,128)(2,1)S(1)}, bf16[2,128,128]{2,1,0:T(8,128)(2,1)S(1)}, u32[]{:S(2)}, u32[]{:S(2)}) collective-permute-start(bf16[2,128,128]{2,1,0:T(8,128)(2,1)S(1)} %slice.17), channel_id=1, source_target_pairs={{0,2},{1,3},{2,0},{3,1},{4,6},{5,7},{6,4},{7,5},{8,10},{9,11},{10,... | collective-permute-start | bytes 196616 | tf_op jit(solution)/shard_map/ppermute | solution.py:297
  18.0 1.5 %collective-permute-start.6 = (bf16[592,128]{1,0:T(8,128)(2,1)S(1)}, bf16[592,128]{1,0:T(8,128)(2,1)S(1)}, u32[]{:S(2)}, u32[]{:S(2)}) collective-permute-start(bf16[592,128]{1,0:T(8,128)(2,1)S(1)} %collective-permute-done.3.refs_2_.refs_9_), channel_id=1, source_target_pairs={{0,4},{1,5},{2,6},{3,7},{4,0},{5,1},{6,2},{7,3},{8,12},{9,13},{10,... | collective-permute-start | bytes 454664 | tf_op jit(solution)/shard_map/ppermute | solution.py:297
  19.6 0.0 collective-permute-done.7.refs_6_.refs_3_
  19.6 1.2 %near_scores.1 = (f32[384,1024]{1,0:T(8,128)S(1)}, bf16[384,640]{1,0:T(8,128)(2,1)S(1)}, f32[16,128]{1,0:T(8,128)S(1)}, bf16[640,1024]{1,0:T(8,128)(2,1)S(1)}) custom-call(bf16[592,128]{1,0:T(8,128)(2,1)S(1)} %get-tuple-element.58.refs_0_.refs_7_, bf16[592,128]{1,0:T(8,128)(2,1)S(1)} %collective-permute-done.2.refs_1_.refs_8_, ...), custom_call_target="tpu_custom_call" | custom-call | tf_op jit(solution)/shard_map/near_scores/pallas_call | solution.py:40
  20.8 1.3 %collective-permute-done.11 = bf16[2,128,128]{2,1,0:T(8,128)(2,1)S(1)} collective-permute-done((bf16[2,128,128]{2,1,0:T(8,128)(2,1)S(1)}, bf16[2,128,128]{2,1,0:T(8,128)(2,1)S(1)}, u32[]{:S(2)}, u32[]{:S(2)}) %collective-permute-start.11) | collective-permute-done | bytes 65568 | tf_op jit(solution)/shard_map/ppermute | solution.py:297
  22.1 1.5 %collective-permute-start.12 = (bf16[2,128,128]{2,1,0:T(8,128)(2,1)S(1)}, bf16[2,128,128]{2,1,0:T(8,128)(2,1)S(1)}, u32[]{:S(2)}, u32[]{:S(2)}) collective-permute-start(bf16[2,128,128]{2,1,0:T(8,128)(2,1)S(1)} %add_convert_fusion.5), channel_id=1, source_target_pairs={{0,4},{1,5},{2,6},{3,7},{4,0},{5,1},{6,2},{7,3},{8,12},{9,13},{10,... | collective-permute-start | bytes 196616 | tf_op jit(solution)/shard_map/ppermute | solution.py:297
  23.6 0.5 collective-permute-done.6.refs_0_.refs_10_
  24.1 0.5 last_scores.1
  24.6 0.6 %collective-permute-start.10 = (f32[16,128]{1,0:T(8,128)S(1)}, f32[16,128]{1,0:T(8,128)S(1)}, u32[]{:S(2)}, u32[]{:S(2)}) collective-permute-start(f32[16,128]{1,0:T(8,128)S(1)} %get-tuple-element.66.refs_0_), channel_id=1, source_target_pairs={{0,3},{1,2},{2,1},{3,0},{4,7},{5,6},{6,5},{7,4},{8,11},{9,10},{10,... | collective-permute-start | bytes 24584 | tf_op jit(solution)/shard_map/ppermute | solution.py:297
  25.2 1.8 %collective-permute-start.8 = (f32[16,128]{1,0:T(8,128)S(1)}, f32[16,128]{1,0:T(8,128)S(1)}, u32[]{:S(2)}, u32[]{:S(2)}) collective-permute-start(f32[16,128]{1,0:T(8,128)S(1)} %get-tuple-element.66.refs_0_), channel_id=1, source_target_pairs={{0,1},{1,0},{2,3},{3,2},{4,5},{5,4},{6,7},{7,6},{8,9},{9,8},{10,11... | collective-permute-start | bytes 24584 | tf_op jit(solution)/shard_map/ppermute | solution.py:297
  27.1 0.0 collective-permute-start.9
  27.1 0.0 collective-permute-done.12
  27.1 2.3 %collective-permute-start.13 = (bf16[2,128,128]{2,1,0:T(8,128)(2,1)S(1)}, bf16[2,128,128]{2,1,0:T(8,128)(2,1)S(1)}, u32[]{:S(2)}, u32[]{:S(2)}) collective-permute-start(bf16[2,128,128]{2,1,0:T(8,128)(2,1)S(1)} %add_convert_fusion.4), channel_id=1, source_target_pairs={{0,8},{1,9},{2,10},{3,11},{4,12},{5,13},{6,14},{7,15},{8,0},{9,1},... | collective-permute-start | bytes 196616 | tf_op jit(solution)/shard_map/ppermute | solution.py:297
  29.4 1.6 %context.1 = (bf16[512,1024]{1,0:T(8,128)(2,1)S(1)}, f32[384,1024]{1,0:T(8,128)S(1)}, f32[128,1024]{1,0:T(8,128)S(1)}) custom-call(bf16[1424,128]{1,0:T(8,128)(2,1)S(1)} %get-tuple-element.60.refs_3_.refs_0_, bf16[1424,128]{1,0:T(8,128)(2,1)S(1)} %collective-permute-done.refs_4_.refs_1_, bf16[1424,128]{1,0:T(8,128)(2,1)S(1)} %collective-permute-done.1.refs_5_.refs_2_, ...), custom_call_target="tpu_custom_call" | custom-call | flops 2013265920 | bytes 16564224 | tf_op jit(solution)/shard_map/context/pallas_call | solution.py:40
  31.1 0.0 collective-permute-done.10.refs_3_
  31.1 0.0 collective-permute-done.8.refs_1_
  31.1 0.0 collective-permute-done.9.refs_2_
  31.1 0.8 %last_gradients.1 = (bf16[576,128]{1,0:T(8,128)(2,1)S(1)}, bf16[128,1024]{1,0:T(8,128)(2,1)S(1)}) custom-call(f32[16,128]{1,0:T(8,128)S(1)} %get-tuple-element.66.refs_0_, f32[16,128]{1,0:T(8,128)S(1)} %collective-permute-done.8.refs_1_, f32[16,128]{1,0:T(8,128)S(1)} %collective-permute-done.9.refs_2_, f32[16,128]{1,0:T(8,128)S(1)} %collective-permute-done.10.refs_3_, ...), custom_call_target="tpu_custom_call" | custom-call | flops 285212672 | bytes 3850240 | tf_op jit(solution)/shard_map/last_gradients/pallas_call | solution.py:40
  31.9 1.8 %collective-permute-start.20 = (bf16[576,128]{1,0:T(8,128)(2,1)S(1)}, bf16[576,128]{1,0:T(8,128)(2,1)S(1)}, u32[]{:S(2)}, u32[]{:S(2)}) collective-permute-start(bf16[576,128]{1,0:T(8,128)(2,1)S(1)} %get-tuple-element.90), channel_id=1, source_target_pairs={{0,4},{1,5},{2,6},{3,7},{4,0},{5,1},{6,2},{7,3},{8,12},{9,13},{10,... | collective-permute-start | bytes 442376 | tf_op jit(solution)/shard_map/ppermute | solution.py:297
  33.7 0.8 %next_gradients.1 = bf16[576,128]{1,0:T(8,128)(2,1)S(1)} custom-call(f32[16,128]{1,0:T(8,128)S(1)} %get-tuple-element.66.refs_0_, f32[16,128]{1,0:T(8,128)S(1)} %collective-permute-done.8.refs_1_, f32[16,128]{1,0:T(8,128)S(1)} %collective-permute-done.9.refs_2_, f32[16,128]{1,0:T(8,128)S(1)} %collective-permute-done.10.refs_3_, ...), custom_call_target="tpu_custom_call" | custom-call | flops 285212672 | bytes 5685248 | tf_op jit(solution)/shard_map/next_gradients/pallas_call | solution.py:40
  34.5 0.4 collective-permute-start.22
  34.9 0.0 collective-permute-done.13
  34.9 1.4 %collective-permute-start.14 = (bf16[2,128,128]{2,1,0:T(8,128)(2,1)S(1)}, bf16[2,128,128]{2,1,0:T(8,128)(2,1)S(1)}, u32[]{:S(2)}, u32[]{:S(2)}) collective-permute-start(bf16[2,128,128]{2,1,0:T(8,128)(2,1)S(1)} %add_convert_fusion.3.refs_0_), channel_id=1, source_target_pairs={{0,2},{1,3},{2,0},{3,1},{4,6},{5,7},{6,4},{7,5},{8,10},{9,11},{10,... | collective-permute-start | bytes 196616 | tf_op jit(solution)/shard_map/ppermute | solution.py:297
  36.3 1.1 %query_gradients.1 = (bf16[2,576,128]{2,1,0:T(8,128)(2,1)S(1)}, bf16[2,576,128]{2,1,0:T(8,128)(2,1)S(1)}, bf16[2,576,128]{2,1,0:T(8,128)(2,1)S(1)}, bf16[576,128...) custom-call(f32[16,128]{1,0:T(8,128)S(1)} %get-tuple-element.66.refs, ...), custom_call_target="tpu_custom_call" | custom-call | tf_op jit(solution)/shard_map/query_gradients/pallas_call | solution.py:40
  37.4 0.1 collective-permute-start.15
  37.5 0.5 collective-permute-start.16
  38.0 0.7 %middle_gradients.1 = bf16[576,128]{1,0:T(8,128)(2,1)S(1)} custom-call(bf16[512,1024]{1,0:T(8,128)(2,1)S(1)} %get-tuple-element.73.refs_6_.g_ref, bf16[640,1024]{1,0:T(8,128)(2,1)S(1)} %get-tuple-element.63.refs_1_.refs_7_.q_all_ref, bf16[384,1024]{1,0:T(8,128)(2,1)S(1)} %get-tuple-element.86.gs_ref, bf16[384,1024]{1,0:T(8,128)(2,1)S(1)} %get-tuple-element.88.p_ref), custom_call_target="tpu_custom_call" | custom-call | flops 855638016 | bytes 12238848 | tf_op jit(solution)/shard_map/middle_gradients/pallas_call | solution.py:40
  38.7 0.5 collective-permute-done.14.refs_2_
  39.2 0.1 collective-permute-start.19
  39.3 0.0 collective-permute-done.20
  39.4 1.3 %collective-permute-start.21 = (bf16[576,128]{1,0:T(8,128)(2,1)S(1)}, bf16[576,128]{1,0:T(8,128)(2,1)S(1)}, u32[]{:S(2)}, u32[]{:S(2)}) collective-permute-start(bf16[576,128]{1,0:T(8,128)(2,1)S(1)} %add_convert_fusion), channel_id=1, source_target_pairs={{0,8},{1,9},{2,10},{3,11},{4,12},{5,13},{6,14},{7,15},{8,0},{9,1},... | collective-permute-start | bytes 442376 | tf_op jit(solution)/shard_map/ppermute | solution.py:297
  40.7 0.0 collective-permute-done.15.refs_0_
  40.7 0.0 collective-permute-done.16.refs_1_
  40.7 0.1 join.1
  40.7 1.5 %collective-permute-start.18 = (bf16[2,576,128]{2,1,0:T(8,128)(2,1)S(1)}, bf16[2,576,128]{2,1,0:T(8,128)(2,1)S(1)}, u32[]{:S(2)}, u32[]{:S(2)}) collective-permute-start(bf16[2,576,128]{2,1,0:T(8,128)(2,1)S(1)} %join.1), channel_id=1, source_target_pairs={{0,2},{1,3},{2,0},{3,1},{4,6},{5,7},{6,4},{7,5},{8,10},{9,11},{10,... | collective-permute-start | bytes 884744 | tf_op jit(solution)/shard_map/ppermute | solution.py:297
  42.2 0.0 collective-permute-start.17
  42.2 0.7 %near_gradients.1.refs_0_ = bf16[576,128]{1,0:T(8,128)(2,1)S(1)} custom-call(bf16[512,1024]{1,0:T(8,128)(2,1)S(1)} %get-tuple-element.73.refs_6_.g_ref, bf16[640,1024]{1,0:T(8,128)(2,1)S(1)} %get-tuple-element.63.refs_1_.refs_7_.q_all_ref, bf16[384,1024]{1,0:T(8,128)(2,1)S(1)} %get-tuple-element.86.gs_ref, bf16[384,1024]{1,0:T(8,128)(2,1)S(1)} %get-tuple-element.88.p_ref), custom_call_target="tpu_custom_call" | custom-call | flops 285212672 | bytes 4079616 | tf_op jit(solution)/shard_map/near_gradients/pallas_call | solution.py:40
  43.0 0.0 collective-permute-done.19
  43.0 0.8 %spread.1 = f32[2,512,128]{2,1,0:T(8,128)} custom-call(s32[1]{0:T(128)} %bitcast.idx_ref, bf16[2,128,128]{2,1,0:T(8,128)(2,1)S(1)} %add_convert_fusion.3.refs_0_, bf16[2,128,128]{2,1,0:T(8,128)(2,1)S(1)} %get-tuple-element.94.refs_1_, bf16[2,128,128]{2,1,0:T(8,128)(2,1)S(1)} %collective-permute-done.14.refs_2_, ...), custom_call_target="tpu_custom_call" | custom-call | bytes 786436 | tf_op jit(solution)/shard_map/spread/pallas_call | solution.py:40
  43.9 0.0 collective-permute-done.22.refs_2_
  43.9 5.9 %collective-permute-done.21.refs_1_ = bf16[576,128]{1,0:T(8,128)(2,1)S(1)} collective-permute-done((bf16[576,128]{1,0:T(8,128)(2,1)S(1)}, bf16[576,128]{1,0:T(8,128)(2,1)S(1)}, u32[]{:S(2)}, u32[]{:S(2)}) %collective-permute-start.21) | collective-permute-done | bytes 147488 | tf_op jit(solution)/shard_map/ppermute | solution.py:297
  49.7 0.7 %latent_sum.1 = bf16[576,128]{1,0:T(8,128)(2,1)} custom-call(bf16[576,128]{1,0:T(8,128)(2,1)S(1)} %near_gradients.1.refs_0_, bf16[576,128]{1,0:T(8,128)(2,1)S(1)} %collective-permute-done.21.refs_1_, bf16[576,128]{1,0:T(8,128)(2,1)S(1)} %collective-permute-done.22.refs_2_), custom_call_target="tpu_custom_call" | custom-call | flops 3000000000 | bytes 589824 | tf_op jit(solution)/shard_map/latent_sum/pallas_call | solution.py:40
  50.5 0.0 collective-permute-done.18.refs_2_
  50.5 0.0 collective-permute-done.17.refs_1_
  50.5 0.8 %query_sum.1 = bf16[2,576,128]{2,1,0:T(8,128)(2,1)} custom-call(bf16[2,576,128]{2,1,0:T(8,128)(2,1)S(1)} %get-tuple-element.79.refs_0_, bf16[2,576,128]{2,1,0:T(8,128)(2,1)S(1)} %collective-permute-done.17.refs_1_, bf16[2,576,128]{2,1,0:T(8,128)(2,1)S(1)} %collective-permute-done.18.refs_2_), custom_call_target="tpu_custom_call" | custom-call | bytes 1179648 | tf_op jit(solution)/shard_map/query_sum/pallas_call | solution.py:40
  (13 shorter events, 0.2 us)
Async XLA Ops:
  3.6 6.1 %collective-permute-start = (bf16[1424,128]{1,0:T(8,128)(2,1)}, bf16[1424,128]{1,0:T(8,128)(2,1)S(1)}, u32[]{:S(2)}, u32[]{:S(2)}) collective-permute-start(bf16[1424,128]{1,0:T(8,128)(2,1)} %get-tuple-element.48.refs_1_), channel_id=1, source_target_pairs={{0,1},{1,0},{2,3},{3,2},{4,5},{5,4},{6,7},{7,6},{8,9},{9,8},{10,11... | collective-permute-start | bytes 1093640 | tf_op jit(solution)/shard_map/ppermute | solution.py:297
  4.1 7.2 %collective-permute-start.4 = (bf16[4,128,128]{2,1,0:T(8,128)(2,1)}, bf16[4,128,128]{2,1,0:T(8,128)(2,1)S(1)}, u32[]{:S(2)}, u32[]{:S(2)}) collective-permute-start(bf16[4,128,128]{2,1,0:T(8,128)(2,1)} %get-tuple-element.52), channel_id=1, source_target_pairs={{0,1},{1,0},{2,3},{3,2},{4,5},{5,4},{6,7},{7,6},{8,9},{9,8},{10,11... | collective-permute-start | bytes 393224 | tf_op jit(solution)/shard_map/ppermute | solution.py:297
  4.2 13.1 %collective-permute-start.1 = (bf16[1424,128]{1,0:T(8,128)(2,1)}, bf16[1424,128]{1,0:T(8,128)(2,1)S(1)}, u32[]{:S(2)}, u32[]{:S(2)}) collective-permute-start(bf16[1424,128]{1,0:T(8,128)(2,1)} %get-tuple-element.48.refs_1_), channel_id=1, source_target_pairs={{0,2},{1,3},{2,0},{3,1},{4,6},{5,7},{6,4},{7,5},{8,10},{9,11},{10,... | collective-permute-start | bytes 1093640 | tf_op jit(solution)/shard_map/ppermute | solution.py:297
  7.1 10.1 %collective-permute-start.3 = (bf16[592,128]{1,0:T(8,128)(2,1)}, bf16[592,128]{1,0:T(8,128)(2,1)S(1)}, u32[]{:S(2)}, u32[]{:S(2)}) collective-permute-start(bf16[592,128]{1,0:T(8,128)(2,1)} %get-tuple-element.50.refs_0_), channel_id=1, source_target_pairs={{0,8},{1,9},{2,10},{3,11},{4,12},{5,13},{6,14},{7,15},{8,0},{9,1},... | collective-permute-start | bytes 454664 | tf_op jit(solution)/shard_map/ppermute | solution.py:297
  9.7 7.7 %collective-permute-start.2 = (bf16[592,128]{1,0:T(8,128)(2,1)}, bf16[592,128]{1,0:T(8,128)(2,1)S(1)}, u32[]{:S(2)}, u32[]{:S(2)}) collective-permute-start(bf16[592,128]{1,0:T(8,128)(2,1)} %get-tuple-element.50.refs_0_), channel_id=1, source_target_pairs={{0,4},{1,5},{2,6},{3,7},{4,0},{5,1},{6,2},{7,3},{8,12},{9,13},{10,... | collective-permute-start | bytes 454664 | tf_op jit(solution)/shard_map/ppermute | solution.py:297
  12.3 5.0 %collective-permute-start.5 = (bf16[4,128,128]{2,1,0:T(8,128)(2,1)S(1)}, bf16[4,128,128]{2,1,0:T(8,128)(2,1)S(1)}, u32[]{:S(2)}, u32[]{:S(2)}) collective-permute-start(bf16[4,128,128]{2,1,0:T(8,128)(2,1)S(1)} %add_convert_fusion.2), channel_id=1, source_target_pairs={{0,16},{16,0},{1,17},{17,1},{2,18},{18,2},{3,19},{19,3},{4,20},{20... | collective-permute-start | bytes 393224 | tf_op jit(solution)/shard_map/ppermute | solution.py:297
  13.8 1.0 %copy-start = (bf16[1424,128]{1,0:T(8,128)(2,1)S(1)}, bf16[1424,128]{1,0:T(8,128)(2,1)}, u32[]{:S(2)}) copy-start(bf16[1424,128]{1,0:T(8,128)(2,1)} %get-tuple-element.48.refs_1_) | copy-start | bytes 1093636
  14.8 0.9 %copy-start.2 = (bf16[592,128]{1,0:T(8,128)(2,1)S(1)}, bf16[592,128]{1,0:T(8,128)(2,1)}, u32[]{:S(2)}) copy-start(bf16[592,128]{1,0:T(8,128)(2,1)} %get-tuple-element.50.refs_0_) | copy-start | bytes 454660
  15.7 0.7 %copy-start.3 = (f32[8,128]{1,0:T(8,128)S(1)}, f32[8,128]{1,0:T(8,128)}, u32[]{:S(2)}) copy-start(f32[8,128]{1,0:T(8,128)} %get-tuple-element.53.refs_2_) | copy-start | bytes 12292
  17.4 2.1 %collective-permute-start.7 = (bf16[1424,128]{1,0:T(8,128)(2,1)S(1)}, bf16[1424,128]{1,0:T(8,128)(2,1)S(1)}, u32[]{:S(2)}, u32[]{:S(2)}) collective-permute-start(bf16[1424,128]{1,0:T(8,128)(2,1)S(1)} %collective-permute-done.1.refs_5_.refs_2_), channel_id=1, source_target_pairs={{0,1},{1,0},{2,3},{3,2},{4,5},{5,4},{6,7},{7,6},{8,9},{9,8},{10,11... | collective-permute-start | bytes 1093640 | tf_op jit(solution)/shard_map/ppermute | solution.py:297
  17.5 12.0 %copy-start.1 = (bf16[2,512,128]{2,1,0:T(8,128)(2,1)S(1)}, bf16[2,512,128]{2,1,0:T(8,128)(2,1)}, u32[]{:S(2)}) copy-start(bf16[2,512,128]{2,1,0:T(8,128)(2,1)} %refs_4_.1) | copy-start | bytes 786436
  17.5 4.6 %collective-permute-start.11 = (bf16[2,128,128]{2,1,0:T(8,128)(2,1)S(1)}, bf16[2,128,128]{2,1,0:T(8,128)(2,1)S(1)}, u32[]{:S(2)}, u32[]{:S(2)}) collective-permute-start(bf16[2,128,128]{2,1,0:T(8,128)(2,1)S(1)} %slice.17), channel_id=1, source_target_pairs={{0,2},{1,3},{2,0},{3,1},{4,6},{5,7},{6,4},{7,5},{8,10},{9,11},{10,... | collective-permute-start | bytes 196616 | tf_op jit(solution)/shard_map/ppermute | solution.py:297
  18.0 6.1 %collective-permute-start.6 = (bf16[592,128]{1,0:T(8,128)(2,1)S(1)}, bf16[592,128]{1,0:T(8,128)(2,1)S(1)}, u32[]{:S(2)}, u32[]{:S(2)}) collective-permute-start(bf16[592,128]{1,0:T(8,128)(2,1)S(1)} %collective-permute-done.3.refs_2_.refs_9_), channel_id=1, source_target_pairs={{0,4},{1,5},{2,6},{3,7},{4,0},{5,1},{6,2},{7,3},{8,12},{9,13},{10,... | collective-permute-start | bytes 454664 | tf_op jit(solution)/shard_map/ppermute | solution.py:297
  22.1 5.0 %collective-permute-start.12 = (bf16[2,128,128]{2,1,0:T(8,128)(2,1)S(1)}, bf16[2,128,128]{2,1,0:T(8,128)(2,1)S(1)}, u32[]{:S(2)}, u32[]{:S(2)}) collective-permute-start(bf16[2,128,128]{2,1,0:T(8,128)(2,1)S(1)} %add_convert_fusion.5), channel_id=1, source_target_pairs={{0,4},{1,5},{2,6},{3,7},{4,0},{5,1},{6,2},{7,3},{8,12},{9,13},{10,... | collective-permute-start | bytes 196616 | tf_op jit(solution)/shard_map/ppermute | solution.py:297
  24.6 6.5 %collective-permute-start.10 = (f32[16,128]{1,0:T(8,128)S(1)}, f32[16,128]{1,0:T(8,128)S(1)}, u32[]{:S(2)}, u32[]{:S(2)}) collective-permute-start(f32[16,128]{1,0:T(8,128)S(1)} %get-tuple-element.66.refs_0_), channel_id=1, source_target_pairs={{0,3},{1,2},{2,1},{3,0},{4,7},{5,6},{6,5},{7,4},{8,11},{9,10},{10,... | collective-permute-start | bytes 24584 | tf_op jit(solution)/shard_map/ppermute | solution.py:297
  25.2 5.8 %collective-permute-start.8 = (f32[16,128]{1,0:T(8,128)S(1)}, f32[16,128]{1,0:T(8,128)S(1)}, u32[]{:S(2)}, u32[]{:S(2)}) collective-permute-start(f32[16,128]{1,0:T(8,128)S(1)} %get-tuple-element.66.refs_0_), channel_id=1, source_target_pairs={{0,1},{1,0},{2,3},{3,2},{4,5},{5,4},{6,7},{7,6},{8,9},{9,8},{10,11... | collective-permute-start | bytes 24584 | tf_op jit(solution)/shard_map/ppermute | solution.py:297
  27.1 4.0 %collective-permute-start.9 = (f32[16,128]{1,0:T(8,128)S(1)}, f32[16,128]{1,0:T(8,128)S(1)}, u32[]{:S(2)}, u32[]{:S(2)}) collective-permute-start(f32[16,128]{1,0:T(8,128)S(1)} %get-tuple-element.66.refs_0_), channel_id=1, source_target_pairs={{0,2},{1,3},{2,0},{3,1},{4,6},{5,7},{6,4},{7,5},{8,10},{9,11},{10,... | collective-permute-start | bytes 24584 | tf_op jit(solution)/shard_map/ppermute | solution.py:297
  27.1 7.7 %collective-permute-start.13 = (bf16[2,128,128]{2,1,0:T(8,128)(2,1)S(1)}, bf16[2,128,128]{2,1,0:T(8,128)(2,1)S(1)}, u32[]{:S(2)}, u32[]{:S(2)}) collective-permute-start(bf16[2,128,128]{2,1,0:T(8,128)(2,1)S(1)} %add_convert_fusion.4), channel_id=1, source_target_pairs={{0,8},{1,9},{2,10},{3,11},{4,12},{5,13},{6,14},{7,15},{8,0},{9,1},... | collective-permute-start | bytes 196616 | tf_op jit(solution)/shard_map/ppermute | solution.py:297
  31.9 7.4 %collective-permute-start.20 = (bf16[576,128]{1,0:T(8,128)(2,1)S(1)}, bf16[576,128]{1,0:T(8,128)(2,1)S(1)}, u32[]{:S(2)}, u32[]{:S(2)}) collective-permute-start(bf16[576,128]{1,0:T(8,128)(2,1)S(1)} %get-tuple-element.90), channel_id=1, source_target_pairs={{0,4},{1,5},{2,6},{3,7},{4,0},{5,1},{6,2},{7,3},{8,12},{9,13},{10,... | collective-permute-start | bytes 442376 | tf_op jit(solution)/shard_map/ppermute | solution.py:297
  34.5 9.4 %collective-permute-start.22 = (bf16[576,128]{1,0:T(8,128)(2,1)S(1)}, bf16[576,128]{1,0:T(8,128)(2,1)S(1)}, u32[]{:S(2)}, u32[]{:S(2)}) collective-permute-start(bf16[576,128]{1,0:T(8,128)(2,1)S(1)} %next_gradients.1), channel_id=1, source_target_pairs={{0,4},{1,5},{2,6},{3,7},{4,0},{5,1},{6,2},{7,3},{8,12},{9,13},{10,... | collective-permute-start | bytes 442376 | tf_op jit(solution)/shard_map/ppermute | solution.py:297
  34.9 4.3 %collective-permute-start.14 = (bf16[2,128,128]{2,1,0:T(8,128)(2,1)S(1)}, bf16[2,128,128]{2,1,0:T(8,128)(2,1)S(1)}, u32[]{:S(2)}, u32[]{:S(2)}) collective-permute-start(bf16[2,128,128]{2,1,0:T(8,128)(2,1)S(1)} %add_convert_fusion.3.refs_0_), channel_id=1, source_target_pairs={{0,2},{1,3},{2,0},{3,1},{4,6},{5,7},{6,4},{7,5},{8,10},{9,11},{10,... | collective-permute-start | bytes 196616 | tf_op jit(solution)/shard_map/ppermute | solution.py:297
  37.4 3.3 %collective-permute-start.15 = (bf16[576,128]{1,0:T(8,128)(2,1)S(1)}, bf16[576,128]{1,0:T(8,128)(2,1)S(1)}, u32[]{:S(2)}, u32[]{:S(2)}) collective-permute-start(bf16[576,128]{1,0:T(8,128)(2,1)S(1)} %get-tuple-element.83), channel_id=1, source_target_pairs={{0,1},{1,0},{2,3},{3,2},{4,5},{5,4},{6,7},{7,6},{8,9},{9,8},{10,11... | collective-permute-start | bytes 442376 | tf_op jit(solution)/shard_map/ppermute | solution.py:297
  37.5 3.2 %collective-permute-start.16 = (bf16[576,128]{1,0:T(8,128)(2,1)S(1)}, bf16[576,128]{1,0:T(8,128)(2,1)S(1)}, u32[]{:S(2)}, u32[]{:S(2)}) collective-permute-start(bf16[576,128]{1,0:T(8,128)(2,1)S(1)} %get-tuple-element.84), channel_id=1, source_target_pairs={{0,1},{1,0},{2,3},{3,2},{4,5},{5,4},{6,7},{7,6},{8,9},{9,8},{10,11... | collective-permute-start | bytes 442376 | tf_op jit(solution)/shard_map/ppermute | solution.py:297
  39.2 3.8 %collective-permute-start.19 = (bf16[4,128,128]{2,1,0:T(8,128)(2,1)S(1)}, bf16[4,128,128]{2,1,0:T(8,128)(2,1)S(1)}, u32[]{:S(2)}, u32[]{:S(2)}) collective-permute-start(bf16[4,128,128]{2,1,0:T(8,128)(2,1)S(1)} %pad_maximum_fusion), channel_id=1, source_target_pairs={{0,1},{1,0},{2,3},{3,2},{4,5},{5,4},{6,7},{7,6},{8,9},{9,8},{10,11... | collective-permute-start | bytes 393224 | tf_op jit(solution)/shard_map/ppermute | solution.py:297
  39.4 10.4 %collective-permute-start.21 = (bf16[576,128]{1,0:T(8,128)(2,1)S(1)}, bf16[576,128]{1,0:T(8,128)(2,1)S(1)}, u32[]{:S(2)}, u32[]{:S(2)}) collective-permute-start(bf16[576,128]{1,0:T(8,128)(2,1)S(1)} %add_convert_fusion), channel_id=1, source_target_pairs={{0,8},{1,9},{2,10},{3,11},{4,12},{5,13},{6,14},{7,15},{8,0},{9,1},... | collective-permute-start | bytes 442376 | tf_op jit(solution)/shard_map/ppermute | solution.py:297
  40.7 9.7 %collective-permute-start.18 = (bf16[2,576,128]{2,1,0:T(8,128)(2,1)S(1)}, bf16[2,576,128]{2,1,0:T(8,128)(2,1)S(1)}, u32[]{:S(2)}, u32[]{:S(2)}) collective-permute-start(bf16[2,576,128]{2,1,0:T(8,128)(2,1)S(1)} %join.1), channel_id=1, source_target_pairs={{0,2},{1,3},{2,0},{3,1},{4,6},{5,7},{6,4},{7,5},{8,10},{9,11},{10,... | collective-permute-start | bytes 884744 | tf_op jit(solution)/shard_map/ppermute | solution.py:297
  42.2 8.2 %collective-permute-start.17 = (bf16[2,576,128]{2,1,0:T(8,128)(2,1)S(1)}, bf16[2,576,128]{2,1,0:T(8,128)(2,1)S(1)}, u32[]{:S(2)}, u32[]{:S(2)}) collective-permute-start(bf16[2,576,128]{2,1,0:T(8,128)(2,1)S(1)} %get-tuple-element.85), channel_id=1, source_target_pairs={{0,1},{1,0},{2,3},{3,2},{4,5},{5,4},{6,7},{7,6},{8,9},{9,8},{10,11... | collective-permute-start | bytes 884744 | tf_op jit(solution)/shard_map/ppermute | solution.py:297

commit v16 on v15

--- a/solution.py
+++ b/solution.py
@@ -270,7 +270,13 @@
 
 
 def sum_kernel(*refs):
-    refs[-1][...] = sum(ref[...].astype(F32) for ref in refs[:-1]).astype(BF16)
+    refs[-1][...] = sum(ref[...].astype(F32) for ref in refs[:-1])
+
+
+def finish_kernel(lat_sum_ref, *refs):
+    pieces, lat_out_ref, q_out_ref = refs[:-2], refs[-2], refs[-1]
+    lat_out_ref[...] = lat_sum_ref[...].astype(BF16)
+    q_out_ref[...] = sum(piece[...].astype(F32) for piece in pieces).astype(BF16)
 
 
 def spread_kernel(scale, idx_ref, *refs):
@@ -478,9 +484,13 @@
         smem=(0,),
     )
     kept[0] = after(kept[0], grad_w)
-    (grad_lat,) = call(sum_kernel, "latent_sum", [((width, tok), BF16)], kept, flops=3 * 10**9)
-    gq_pieces = [gq_own, gq_core, after(gq_last, grad_lat)]
-    (grad_q,) = call(sum_kernel, "query_sum", [((heads, width, tok), BF16)], gq_pieces)
+    (lat_sum,) = call(sum_kernel, "latent_sum", [((width, tok), F32)], kept, flops=3 * 10**9)
+    grad_lat, grad_q = call(
+        finish_kernel,
+        "finish",
+        [((width, tok), BF16), ((heads, width, tok), BF16)],
+        [lat_sum, gq_own, gq_core, gq_last],
+    )
     return (jnp.transpose(grad_q, (2, 0, 1))[None], grad_lat.T[None], grad_w)
 
 

time: 51.5 us -> 51 us (level)
  Pallas kernels: 13 us -> 12.3 us
    pallas_call x14, Pallas kernels: 13 us -> 12.3 us  [call(): pl.pallas_call(kernel, out_shape=[jax.ShapeDtypeStruct(s, d) for s, d in...]
  transfers between devices with their start and end apart: 23 -> 23, of which waited for: 7 -> 8; matrix products, arithmetic and copies ran while one was open for 2% -> 2% of each run, Pallas kernels for 18% -> 17%
where the time goes in v16:
time: 51 us; the launch traced here: 50.8 us
  starting transfers between devices  24.6 us (48%)
  Pallas kernels  12.3 us (24%)
  waiting for transfers between devices  9.28 us (18%)
  local copies, waits for them, and re-layouts  2.6 us (5%)
  other arithmetic  1.1 us (2%)
  between operations  0.84 us (2%)
    ppermute x23, starting transfers between devices, swap(): return lax.ppermute(x, axis, [(i, i ^ mask) for i in range(size)])  24.6 us
    pallas_call x14, Pallas kernels, call(): pl.pallas_call(kernel, out_shape=[jax.ShapeDtypeStruct(s, d) for s, d in...  12.3 us
    ppermute x23, waiting for transfers between devices, swap(): return lax.ppermute(x, axis, [(i, i ^ mask) for i in range(size)])  9.28 us
    unnamed x8, local copies, waits for them, and re-layouts  2.58 us
    convert_element_type x6, other arithmetic, add(): return (a.astype(F32) + b.astype(F32)).astype(BF16)  1.09 us
  transfers between devices with their start and end apart: 23, of which 8 were waited for; matrix products, arithmetic and copies ran while one was open for 2% of the time, Pallas kernels for 17%

profile of v16, /device:TPU:0, one launch (start us, length us, event | category | flops | bytes accessed | tf_op | source)
XLA Modules:
  0.0 50.8 jit_solution(1677939656250876091)
XLA Ops:
  0.6 3.0 %pack.1 = (bf16[592,128]{1,0:T(8,128)(2,1)}, bf16[1424,128]{1,0:T(8,128)(2,1)}, f32[8,128]{1,0:T(8,128)}, bf16[4,128,128]{2,1,0:T(8,128)(2,1)}, bf16[4,128,128]{2,1,0:T(8,128)(2,1)}) custom-call(s32[1]{0:T(128)} %bitcast.idx_ref, s32[1,128]{1,0:T(1,128)} %pos_hbm.1, bf16[2,576,128]{2,1,0:T(8,128)(2,1)} %bitcast.15, bf16[128,2,128]{2,1,0:T(2,128)(2,1)} %bitcast.18, ...), custom_call_target="tpu_custom_call" | custom-call | bytes 1815044 | tf_op jit(solution)/shard_map/pack/pallas_call | solution.py:40
  3.6 0.5 %collective-permute-start = (bf16[1424,128]{1,0:T(8,128)(2,1)}, bf16[1424,128]{1,0:T(8,128)(2,1)S(1)}, u32[]{:S(2)}, u32[]{:S(2)}) collective-permute-start(bf16[1424,128]{1,0:T(8,128)(2,1)} %get-tuple-element.49.refs_1_), channel_id=1, source_target_pairs={{0,1},{1,0},{2,3},{3,2},{4,5},{5,4},{6,7},{7,6},{8,9},{9,8},{10,11... | collective-permute-start | bytes 1093640 | tf_op jit(solution)/shard_map/ppermute | solution.py:303
  4.1 0.1 collective-permute-start.4
  4.2 2.9 %collective-permute-start.1 = (bf16[1424,128]{1,0:T(8,128)(2,1)}, bf16[1424,128]{1,0:T(8,128)(2,1)S(1)}, u32[]{:S(2)}, u32[]{:S(2)}) collective-permute-start(bf16[1424,128]{1,0:T(8,128)(2,1)} %get-tuple-element.49.refs_1_), channel_id=1, source_target_pairs={{0,2},{1,3},{2,0},{3,1},{4,6},{5,7},{6,4},{7,5},{8,10},{9,11},{10,... | collective-permute-start | bytes 1093640 | tf_op jit(solution)/shard_map/ppermute | solution.py:303
  7.1 2.6 %collective-permute-start.3 = (bf16[592,128]{1,0:T(8,128)(2,1)}, bf16[592,128]{1,0:T(8,128)(2,1)S(1)}, u32[]{:S(2)}, u32[]{:S(2)}) collective-permute-start(bf16[592,128]{1,0:T(8,128)(2,1)} %get-tuple-element.51.refs_0_), channel_id=1, source_target_pairs={{0,8},{1,9},{2,10},{3,11},{4,12},{5,13},{6,14},{7,15},{8,0},{9,1},... | collective-permute-start | bytes 454664 | tf_op jit(solution)/shard_map/ppermute | solution.py:303
  9.7 0.0 collective-permute-done.refs_4_.refs_1_
  9.7 1.6 %collective-permute-start.2 = (bf16[592,128]{1,0:T(8,128)(2,1)}, bf16[592,128]{1,0:T(8,128)(2,1)S(1)}, u32[]{:S(2)}, u32[]{:S(2)}) collective-permute-start(bf16[592,128]{1,0:T(8,128)(2,1)} %get-tuple-element.51.refs_0_), channel_id=1, source_target_pairs={{0,4},{1,5},{2,6},{3,7},{4,0},{5,1},{6,2},{7,3},{8,12},{9,13},{10,... | collective-permute-start | bytes 454664 | tf_op jit(solution)/shard_map/ppermute | solution.py:303
  11.3 0.0 collective-permute-done.4
  11.3 0.9 %add_convert_fusion.2 = bf16[4,128,128]{2,1,0:T(8,128)(2,1)S(1)} fusion(bf16[4,128,128]{2,1,0:T(8,128)(2,1)S(1)} %collective-permute-done.4, bf16[4,128,128]{2,1,0:T(8,128)(2,1)} %get-tuple-element.52), kind=kLoop, calls=%fused_computation.2 | loop fusion | flops 262144 | bytes 393216 | tf_op jit(solution)/shard_map/convert_element_type | solution.py:351
  12.3 1.6 %collective-permute-start.5 = (bf16[4,128,128]{2,1,0:T(8,128)(2,1)S(1)}, bf16[4,128,128]{2,1,0:T(8,128)(2,1)S(1)}, u32[]{:S(2)}, u32[]{:S(2)}) collective-permute-start(bf16[4,128,128]{2,1,0:T(8,128)(2,1)S(1)} %add_convert_fusion.2), channel_id=1, source_target_pairs={{0,16},{16,0},{1,17},{17,1},{2,18},{18,2},{3,19},{19,3},{4,20},{20... | collective-permute-start | bytes 393224 | tf_op jit(solution)/shard_map/ppermute | solution.py:303
  13.8 1.0 %copy-done = bf16[1424,128]{1,0:T(8,128)(2,1)S(1)} copy-done((bf16[1424,128]{1,0:T(8,128)(2,1)S(1)}, bf16[1424,128]{1,0:T(8,128)(2,1)}, u32[]{:S(2)}) %copy-start) | copy-done | bytes 364568
  14.8 0.9 %copy-done.2 = bf16[592,128]{1,0:T(8,128)(2,1)S(1)} copy-done((bf16[592,128]{1,0:T(8,128)(2,1)S(1)}, bf16[592,128]{1,0:T(8,128)(2,1)}, u32[]{:S(2)}) %copy-start.2) | copy-done | bytes 151576
  15.7 0.7 %copy-done.3 = f32[8,128]{1,0:T(8,128)S(1)} copy-done((f32[8,128]{1,0:T(8,128)S(1)}, f32[8,128]{1,0:T(8,128)}, u32[]{:S(2)}) %copy-start.3) | copy-done | bytes 4120
  16.4 0.8 %collective-permute-done.3.refs_2_.refs_9_ = bf16[592,128]{1,0:T(8,128)(2,1)S(1)} collective-permute-done((bf16[592,128]{1,0:T(8,128)(2,1)}, bf16[592,128]{1,0:T(8,128)(2,1)S(1)}, u32[]{:S(2)}, u32[]{:S(2)}) %collective-permute-start.3) | collective-permute-done | bytes 151584 | tf_op jit(solution)/shard_map/ppermute | solution.py:303
  17.2 0.1 collective-permute-done.5
  17.3 0.0 collective-permute-done.1.refs_5_.refs_2_
  17.3 0.1 collective-permute-done.2.refs_1_.refs_8_
  17.4 0.0 collective-permute-start.6
  17.5 0.0 copy-start.1
  17.5 0.5 %collective-permute-start.11 = (bf16[2,128,128]{2,1,0:T(8,128)(2,1)S(1)}, bf16[2,128,128]{2,1,0:T(8,128)(2,1)S(1)}, u32[]{:S(2)}, u32[]{:S(2)}) collective-permute-start(bf16[2,128,128]{2,1,0:T(8,128)(2,1)S(1)} %slice.17), channel_id=1, source_target_pairs={{0,2},{1,3},{2,0},{3,1},{4,6},{5,7},{6,4},{7,5},{8,10},{9,11},{10,... | collective-permute-start | bytes 196616 | tf_op jit(solution)/shard_map/ppermute | solution.py:303
  18.0 1.5 %collective-permute-start.7 = (bf16[592,128]{1,0:T(8,128)(2,1)S(1)}, bf16[592,128]{1,0:T(8,128)(2,1)S(1)}, u32[]{:S(2)}, u32[]{:S(2)}) collective-permute-start(bf16[592,128]{1,0:T(8,128)(2,1)S(1)} %collective-permute-done.3.refs_2_.refs_9_), channel_id=1, source_target_pairs={{0,4},{1,5},{2,6},{3,7},{4,0},{5,1},{6,2},{7,3},{8,12},{9,13},{10,... | collective-permute-start | bytes 454664 | tf_op jit(solution)/shard_map/ppermute | solution.py:303
  19.6 0.0 collective-permute-done.6.refs_6_.refs_3_
  19.6 1.2 %near_scores.1 = (f32[384,1024]{1,0:T(8,128)S(1)}, bf16[384,640]{1,0:T(8,128)(2,1)S(1)}, f32[16,128]{1,0:T(8,128)S(1)}, bf16[640,1024]{1,0:T(8,128)(2,1)S(1)}) custom-call(bf16[592,128]{1,0:T(8,128)(2,1)S(1)} %get-tuple-element.61.refs_0_.refs_7_, bf16[592,128]{1,0:T(8,128)(2,1)S(1)} %collective-permute-done.2.refs_1_.refs_8_, ...), custom_call_target="tpu_custom_call" | custom-call | tf_op jit(solution)/shard_map/near_scores/pallas_call | solution.py:40
  20.8 1.3 %collective-permute-done.11 = bf16[2,128,128]{2,1,0:T(8,128)(2,1)S(1)} collective-permute-done((bf16[2,128,128]{2,1,0:T(8,128)(2,1)S(1)}, bf16[2,128,128]{2,1,0:T(8,128)(2,1)S(1)}, u32[]{:S(2)}, u32[]{:S(2)}) %collective-permute-start.11) | collective-permute-done | bytes 65568 | tf_op jit(solution)/shard_map/ppermute | solution.py:303
  22.1 1.5 %collective-permute-start.12 = (bf16[2,128,128]{2,1,0:T(8,128)(2,1)S(1)}, bf16[2,128,128]{2,1,0:T(8,128)(2,1)S(1)}, u32[]{:S(2)}, u32[]{:S(2)}) collective-permute-start(bf16[2,128,128]{2,1,0:T(8,128)(2,1)S(1)} %add_convert_fusion.5), channel_id=1, source_target_pairs={{0,4},{1,5},{2,6},{3,7},{4,0},{5,1},{6,2},{7,3},{8,12},{9,13},{10,... | collective-permute-start | bytes 196616 | tf_op jit(solution)/shard_map/ppermute | solution.py:303
  23.6 0.5 collective-permute-done.7.refs_0_.refs_10_
  24.1 0.5 last_scores.1
  24.6 0.6 %collective-permute-start.10 = (f32[16,128]{1,0:T(8,128)S(1)}, f32[16,128]{1,0:T(8,128)S(1)}, u32[]{:S(2)}, u32[]{:S(2)}) collective-permute-start(f32[16,128]{1,0:T(8,128)S(1)} %get-tuple-element.70.refs_0_), channel_id=1, source_target_pairs={{0,3},{1,2},{2,1},{3,0},{4,7},{5,6},{6,5},{7,4},{8,11},{9,10},{10,... | collective-permute-start | bytes 24584 | tf_op jit(solution)/shard_map/ppermute | solution.py:303
  25.2 1.8 %collective-permute-start.8 = (f32[16,128]{1,0:T(8,128)S(1)}, f32[16,128]{1,0:T(8,128)S(1)}, u32[]{:S(2)}, u32[]{:S(2)}) collective-permute-start(f32[16,128]{1,0:T(8,128)S(1)} %get-tuple-element.70.refs_0_), channel_id=1, source_target_pairs={{0,1},{1,0},{2,3},{3,2},{4,5},{5,4},{6,7},{7,6},{8,9},{9,8},{10,11... | collective-permute-start | bytes 24584 | tf_op jit(solution)/shard_map/ppermute | solution.py:303
  27.1 0.0 collective-permute-start.9
  27.1 0.0 collective-permute-done.12
  27.1 2.3 %collective-permute-start.13 = (bf16[2,128,128]{2,1,0:T(8,128)(2,1)S(1)}, bf16[2,128,128]{2,1,0:T(8,128)(2,1)S(1)}, u32[]{:S(2)}, u32[]{:S(2)}) collective-permute-start(bf16[2,128,128]{2,1,0:T(8,128)(2,1)S(1)} %add_convert_fusion.4), channel_id=1, source_target_pairs={{0,8},{1,9},{2,10},{3,11},{4,12},{5,13},{6,14},{7,15},{8,0},{9,1},... | collective-permute-start | bytes 196616 | tf_op jit(solution)/shard_map/ppermute | solution.py:303
  29.4 1.6 %context.1 = (bf16[512,1024]{1,0:T(8,128)(2,1)S(1)}, f32[384,1024]{1,0:T(8,128)S(1)}, f32[128,1024]{1,0:T(8,128)S(1)}) custom-call(bf16[1424,128]{1,0:T(8,128)(2,1)S(1)} %get-tuple-element.58.refs_3_.refs_0_, bf16[1424,128]{1,0:T(8,128)(2,1)S(1)} %collective-permute-done.refs_4_.refs_1_, bf16[1424,128]{1,0:T(8,128)(2,1)S(1)} %collective-permute-done.1.refs_5_.refs_2_, ...), custom_call_target="tpu_custom_call" | custom-call | flops 2013265920 | bytes 16564224 | tf_op jit(solution)/shard_map/context/pallas_call | solution.py:40
  31.0 0.0 collective-permute-done.10.refs_3_
  31.1 0.0 collective-permute-done.8.refs_1_
  31.1 0.0 collective-permute-done.9.refs_2_
  31.1 0.8 %last_gradients.1 = (bf16[576,128]{1,0:T(8,128)(2,1)S(1)}, bf16[128,1024]{1,0:T(8,128)(2,1)S(1)}) custom-call(f32[16,128]{1,0:T(8,128)S(1)} %get-tuple-element.70.refs_0_, f32[16,128]{1,0:T(8,128)S(1)} %collective-permute-done.8.refs_1_, f32[16,128]{1,0:T(8,128)S(1)} %collective-permute-done.9.refs_2_, f32[16,128]{1,0:T(8,128)S(1)} %collective-permute-done.10.refs_3_, ...), custom_call_target="tpu_custom_call" | custom-call | flops 285212672 | bytes 3850240 | tf_op jit(solution)/shard_map/last_gradients/pallas_call | solution.py:40
  31.9 1.7 %collective-permute-start.18 = (bf16[576,128]{1,0:T(8,128)(2,1)S(1)}, bf16[576,128]{1,0:T(8,128)(2,1)S(1)}, u32[]{:S(2)}, u32[]{:S(2)}) collective-permute-start(bf16[576,128]{1,0:T(8,128)(2,1)S(1)} %get-tuple-element.86), channel_id=1, source_target_pairs={{0,4},{1,5},{2,6},{3,7},{4,0},{5,1},{6,2},{7,3},{8,12},{9,13},{10,... | collective-permute-start | bytes 442376 | tf_op jit(solution)/shard_map/ppermute | solution.py:303
  33.7 0.8 %next_gradients.1 = bf16[576,128]{1,0:T(8,128)(2,1)S(1)} custom-call(f32[16,128]{1,0:T(8,128)S(1)} %get-tuple-element.70.refs_0_, f32[16,128]{1,0:T(8,128)S(1)} %collective-permute-done.8.refs_1_, f32[16,128]{1,0:T(8,128)S(1)} %collective-permute-done.9.refs_2_, f32[16,128]{1,0:T(8,128)S(1)} %collective-permute-done.10.refs_3_, ...), custom_call_target="tpu_custom_call" | custom-call | flops 285212672 | bytes 5685248 | tf_op jit(solution)/shard_map/next_gradients/pallas_call | solution.py:40
  34.5 0.4 collective-permute-start.20
  34.9 0.0 collective-permute-done.13
  34.9 1.4 %collective-permute-start.16 = (bf16[2,128,128]{2,1,0:T(8,128)(2,1)S(1)}, bf16[2,128,128]{2,1,0:T(8,128)(2,1)S(1)}, u32[]{:S(2)}, u32[]{:S(2)}) collective-permute-start(bf16[2,128,128]{2,1,0:T(8,128)(2,1)S(1)} %add_convert_fusion.3.refs_0_), channel_id=1, source_target_pairs={{0,2},{1,3},{2,0},{3,1},{4,6},{5,7},{6,4},{7,5},{8,10},{9,11},{10,... | collective-permute-start | bytes 196616 | tf_op jit(solution)/shard_map/ppermute | solution.py:303
  36.3 1.1 %query_gradients.1 = (bf16[2,576,128]{2,1,0:T(8,128)(2,1)S(1)}, bf16[2,576,128]{2,1,0:T(8,128)(2,1)S(1)}, bf16[2,576,128]{2,1,0:T(8,128)(2,1)S(1)}, bf16[576,128...) custom-call(f32[16,128]{1,0:T(8,128)S(1)} %get-tuple-element.70.refs, ...), custom_call_target="tpu_custom_call" | custom-call | tf_op jit(solution)/shard_map/query_gradients/pallas_call | solution.py:40
  37.4 0.1 collective-permute-start.14
  37.5 0.5 collective-permute-start.15
  38.0 0.7 %middle_gradients.1 = bf16[576,128]{1,0:T(8,128)(2,1)S(1)} custom-call(bf16[512,1024]{1,0:T(8,128)(2,1)S(1)} %get-tuple-element.69.refs_6_.g_ref, bf16[640,1024]{1,0:T(8,128)(2,1)S(1)} %get-tuple-element.65.refs_1_.refs_7_.q_all_ref, bf16[384,1024]{1,0:T(8,128)(2,1)S(1)} %get-tuple-element.80.gs_ref, bf16[384,1024]{1,0:T(8,128)(2,1)S(1)} %get-tuple-element.84.p_ref), custom_call_target="tpu_custom_call" | custom-call | flops 855638016 | bytes 12238848 | tf_op jit(solution)/shard_map/middle_gradients/pallas_call | solution.py:40
  38.7 0.5 collective-permute-done.16.refs_2_
  39.2 0.1 collective-permute-start.17
  39.3 0.0 collective-permute-done.18
  39.4 1.3 %collective-permute-start.19 = (bf16[576,128]{1,0:T(8,128)(2,1)S(1)}, bf16[576,128]{1,0:T(8,128)(2,1)S(1)}, u32[]{:S(2)}, u32[]{:S(2)}) collective-permute-start(bf16[576,128]{1,0:T(8,128)(2,1)S(1)} %add_convert_fusion), channel_id=1, source_target_pairs={{0,8},{1,9},{2,10},{3,11},{4,12},{5,13},{6,14},{7,15},{8,0},{9,1},... | collective-permute-start | bytes 442376 | tf_op jit(solution)/shard_map/ppermute | solution.py:303
  40.7 0.0 collective-permute-done.14.refs_0_
  40.7 0.0 collective-permute-done.15.refs_1_
  40.7 0.1 join.1
  40.7 1.5 %collective-permute-start.22 = (bf16[2,576,128]{2,1,0:T(8,128)(2,1)S(1)}, bf16[2,576,128]{2,1,0:T(8,128)(2,1)S(1)}, u32[]{:S(2)}, u32[]{:S(2)}) collective-permute-start(bf16[2,576,128]{2,1,0:T(8,128)(2,1)S(1)} %join.1), channel_id=1, source_target_pairs={{0,2},{1,3},{2,0},{3,1},{4,6},{5,7},{6,4},{7,5},{8,10},{9,11},{10,... | collective-permute-start | bytes 884744 | tf_op jit(solution)/shard_map/ppermute | solution.py:303
  42.2 0.0 collective-permute-start.21
  42.3 0.7 %near_gradients.1.refs_0_ = bf16[576,128]{1,0:T(8,128)(2,1)S(1)} custom-call(bf16[512,1024]{1,0:T(8,128)(2,1)S(1)} %get-tuple-element.69.refs_6_.g_ref, bf16[640,1024]{1,0:T(8,128)(2,1)S(1)} %get-tuple-element.65.refs_1_.refs_7_.q_all_ref, bf16[384,1024]{1,0:T(8,128)(2,1)S(1)} %get-tuple-element.80.gs_ref, bf16[384,1024]{1,0:T(8,128)(2,1)S(1)} %get-tuple-element.84.p_ref), custom_call_target="tpu_custom_call" | custom-call | flops 285212672 | bytes 4079616 | tf_op jit(solution)/shard_map/near_gradients/pallas_call | solution.py:40
  43.0 0.0 collective-permute-done.17
  43.0 0.8 %spread.1 = f32[2,512,128]{2,1,0:T(8,128)} custom-call(s32[1]{0:T(128)} %bitcast.idx_ref, bf16[2,128,128]{2,1,0:T(8,128)(2,1)S(1)} %add_convert_fusion.3.refs_0_, bf16[2,128,128]{2,1,0:T(8,128)(2,1)S(1)} %get-tuple-element.96.refs_1_, bf16[2,128,128]{2,1,0:T(8,128)(2,1)S(1)} %collective-permute-done.16.refs_2_, ...), custom_call_target="tpu_custom_call" | custom-call | bytes 786436 | tf_op jit(solution)/shard_map/spread/pallas_call | solution.py:40
  43.9 0.0 collective-permute-done.20.refs_2_
  43.9 5.9 %collective-permute-done.19.refs_1_ = bf16[576,128]{1,0:T(8,128)(2,1)S(1)} collective-permute-done((bf16[576,128]{1,0:T(8,128)(2,1)S(1)}, bf16[576,128]{1,0:T(8,128)(2,1)S(1)}, u32[]{:S(2)}, u32[]{:S(2)}) %collective-permute-start.19) | collective-permute-done | bytes 147488 | tf_op jit(solution)/shard_map/ppermute | solution.py:303
  49.7 0.1 latent_sum.1.lat_sum_ref
  49.8 0.0 collective-permute-done.21.refs_1_
  49.8 0.1 collective-permute-done.22.refs_2_
  49.9 0.8 %finish.1 = (bf16[576,128]{1,0:T(8,128)(2,1)}, bf16[2,576,128]{2,1,0:T(8,128)(2,1)}) custom-call(f32[576,128]{1,0:T(8,128)S(1)} %latent_sum.1.lat_sum_ref, bf16[2,576,128]{2,1,0:T(8,128)(2,1)S(1)} %get-tuple-element.88.refs_0_, bf16[2,576,128]{2,1,0:T(8,128)(2,1)S(1)} %collective-permute-done.21.refs_1_, bf16[2,576,128]{2,1,0:T(8,128)(2,1)S(1)} %collective-permute-done.22.refs_2_), custom_call_target="tpu_custom_call" | custom-call | bytes 1622016 | tf_op jit(solution)/shard_map/finish/pallas_call | solution.py:40
  (13 shorter events, 0.2 us)
Async XLA Ops:
  3.6 6.1 %collective-permute-start = (bf16[1424,128]{1,0:T(8,128)(2,1)}, bf16[1424,128]{1,0:T(8,128)(2,1)S(1)}, u32[]{:S(2)}, u32[]{:S(2)}) collective-permute-start(bf16[1424,128]{1,0:T(8,128)(2,1)} %get-tuple-element.49.refs_1_), channel_id=1, source_target_pairs={{0,1},{1,0},{2,3},{3,2},{4,5},{5,4},{6,7},{7,6},{8,9},{9,8},{10,11... | collective-permute-start | bytes 1093640 | tf_op jit(solution)/shard_map/ppermute | solution.py:303
  4.1 7.2 %collective-permute-start.4 = (bf16[4,128,128]{2,1,0:T(8,128)(2,1)}, bf16[4,128,128]{2,1,0:T(8,128)(2,1)S(1)}, u32[]{:S(2)}, u32[]{:S(2)}) collective-permute-start(bf16[4,128,128]{2,1,0:T(8,128)(2,1)} %get-tuple-element.53), channel_id=1, source_target_pairs={{0,1},{1,0},{2,3},{3,2},{4,5},{5,4},{6,7},{7,6},{8,9},{9,8},{10,11... | collective-permute-start | bytes 393224 | tf_op jit(solution)/shard_map/ppermute | solution.py:303
  4.2 13.1 %collective-permute-start.1 = (bf16[1424,128]{1,0:T(8,128)(2,1)}, bf16[1424,128]{1,0:T(8,128)(2,1)S(1)}, u32[]{:S(2)}, u32[]{:S(2)}) collective-permute-start(bf16[1424,128]{1,0:T(8,128)(2,1)} %get-tuple-element.49.refs_1_), channel_id=1, source_target_pairs={{0,2},{1,3},{2,0},{3,1},{4,6},{5,7},{6,4},{7,5},{8,10},{9,11},{10,... | collective-permute-start | bytes 1093640 | tf_op jit(solution)/shard_map/ppermute | solution.py:303
  7.1 10.1 %collective-permute-start.3 = (bf16[592,128]{1,0:T(8,128)(2,1)}, bf16[592,128]{1,0:T(8,128)(2,1)S(1)}, u32[]{:S(2)}, u32[]{:S(2)}) collective-permute-start(bf16[592,128]{1,0:T(8,128)(2,1)} %get-tuple-element.51.refs_0_), channel_id=1, source_target_pairs={{0,8},{1,9},{2,10},{3,11},{4,12},{5,13},{6,14},{7,15},{8,0},{9,1},... | collective-permute-start | bytes 454664 | tf_op jit(solution)/shard_map/ppermute | solution.py:303
  9.7 7.7 %collective-permute-start.2 = (bf16[592,128]{1,0:T(8,128)(2,1)}, bf16[592,128]{1,0:T(8,128)(2,1)S(1)}, u32[]{:S(2)}, u32[]{:S(2)}) collective-permute-start(bf16[592,128]{1,0:T(8,128)(2,1)} %get-tuple-element.51.refs_0_), channel_id=1, source_target_pairs={{0,4},{1,5},{2,6},{3,7},{4,0},{5,1},{6,2},{7,3},{8,12},{9,13},{10,... | collective-permute-start | bytes 454664 | tf_op jit(solution)/shard_map/ppermute | solution.py:303
  12.3 5.0 %collective-permute-start.5 = (bf16[4,128,128]{2,1,0:T(8,128)(2,1)S(1)}, bf16[4,128,128]{2,1,0:T(8,128)(2,1)S(1)}, u32[]{:S(2)}, u32[]{:S(2)}) collective-permute-start(bf16[4,128,128]{2,1,0:T(8,128)(2,1)S(1)} %add_convert_fusion.2), channel_id=1, source_target_pairs={{0,16},{16,0},{1,17},{17,1},{2,18},{18,2},{3,19},{19,3},{4,20},{20... | collective-permute-start | bytes 393224 | tf_op jit(solution)/shard_map/ppermute | solution.py:303
  13.8 1.0 %copy-start = (bf16[1424,128]{1,0:T(8,128)(2,1)S(1)}, bf16[1424,128]{1,0:T(8,128)(2,1)}, u32[]{:S(2)}) copy-start(bf16[1424,128]{1,0:T(8,128)(2,1)} %get-tuple-element.49.refs_1_) | copy-start | bytes 1093636
  14.8 0.9 %copy-start.2 = (bf16[592,128]{1,0:T(8,128)(2,1)S(1)}, bf16[592,128]{1,0:T(8,128)(2,1)}, u32[]{:S(2)}) copy-start(bf16[592,128]{1,0:T(8,128)(2,1)} %get-tuple-element.51.refs_0_) | copy-start | bytes 454660
  15.7 0.7 %copy-start.3 = (f32[8,128]{1,0:T(8,128)S(1)}, f32[8,128]{1,0:T(8,128)}, u32[]{:S(2)}) copy-start(f32[8,128]{1,0:T(8,128)} %get-tuple-element.54.refs_2_) | copy-start | bytes 12292
  17.4 2.1 %collective-permute-start.6 = (bf16[1424,128]{1,0:T(8,128)(2,1)S(1)}, bf16[1424,128]{1,0:T(8,128)(2,1)S(1)}, u32[]{:S(2)}, u32[]{:S(2)}) collective-permute-start(bf16[1424,128]{1,0:T(8,128)(2,1)S(1)} %collective-permute-done.1.refs_5_.refs_2_), channel_id=1, source_target_pairs={{0,1},{1,0},{2,3},{3,2},{4,5},{5,4},{6,7},{7,6},{8,9},{9,8},{10,11... | collective-permute-start | bytes 1093640 | tf_op jit(solution)/shard_map/ppermute | solution.py:303
  17.5 12.0 %copy-start.1 = (bf16[2,512,128]{2,1,0:T(8,128)(2,1)S(1)}, bf16[2,512,128]{2,1,0:T(8,128)(2,1)}, u32[]{:S(2)}) copy-start(bf16[2,512,128]{2,1,0:T(8,128)(2,1)} %refs_4_.1) | copy-start | bytes 786436
  17.5 4.6 %collective-permute-start.11 = (bf16[2,128,128]{2,1,0:T(8,128)(2,1)S(1)}, bf16[2,128,128]{2,1,0:T(8,128)(2,1)S(1)}, u32[]{:S(2)}, u32[]{:S(2)}) collective-permute-start(bf16[2,128,128]{2,1,0:T(8,128)(2,1)S(1)} %slice.17), channel_id=1, source_target_pairs={{0,2},{1,3},{2,0},{3,1},{4,6},{5,7},{6,4},{7,5},{8,10},{9,11},{10,... | collective-permute-start | bytes 196616 | tf_op jit(solution)/shard_map/ppermute | solution.py:303
  18.0 6.1 %collective-permute-start.7 = (bf16[592,128]{1,0:T(8,128)(2,1)S(1)}, bf16[592,128]{1,0:T(8,128)(2,1)S(1)}, u32[]{:S(2)}, u32[]{:S(2)}) collective-permute-start(bf16[592,128]{1,0:T(8,128)(2,1)S(1)} %collective-permute-done.3.refs_2_.refs_9_), channel_id=1, source_target_pairs={{0,4},{1,5},{2,6},{3,7},{4,0},{5,1},{6,2},{7,3},{8,12},{9,13},{10,... | collective-permute-start | bytes 454664 | tf_op jit(solution)/shard_map/ppermute | solution.py:303
  22.1 5.0 %collective-permute-start.12 = (bf16[2,128,128]{2,1,0:T(8,128)(2,1)S(1)}, bf16[2,128,128]{2,1,0:T(8,128)(2,1)S(1)}, u32[]{:S(2)}, u32[]{:S(2)}) collective-permute-start(bf16[2,128,128]{2,1,0:T(8,128)(2,1)S(1)} %add_convert_fusion.5), channel_id=1, source_target_pairs={{0,4},{1,5},{2,6},{3,7},{4,0},{5,1},{6,2},{7,3},{8,12},{9,13},{10,... | collective-permute-start | bytes 196616 | tf_op jit(solution)/shard_map/ppermute | solution.py:303
  24.6 6.5 %collective-permute-start.10 = (f32[16,128]{1,0:T(8,128)S(1)}, f32[16,128]{1,0:T(8,128)S(1)}, u32[]{:S(2)}, u32[]{:S(2)}) collective-permute-start(f32[16,128]{1,0:T(8,128)S(1)} %get-tuple-element.70.refs_0_), channel_id=1, source_target_pairs={{0,3},{1,2},{2,1},{3,0},{4,7},{5,6},{6,5},{7,4},{8,11},{9,10},{10,... | collective-permute-start | bytes 24584 | tf_op jit(solution)/shard_map/ppermute | solution.py:303
  25.2 5.8 %collective-permute-start.8 = (f32[16,128]{1,0:T(8,128)S(1)}, f32[16,128]{1,0:T(8,128)S(1)}, u32[]{:S(2)}, u32[]{:S(2)}) collective-permute-start(f32[16,128]{1,0:T(8,128)S(1)} %get-tuple-element.70.refs_0_), channel_id=1, source_target_pairs={{0,1},{1,0},{2,3},{3,2},{4,5},{5,4},{6,7},{7,6},{8,9},{9,8},{10,11... | collective-permute-start | bytes 24584 | tf_op jit(solution)/shard_map/ppermute | solution.py:303
  27.1 4.0 %collective-permute-start.9 = (f32[16,128]{1,0:T(8,128)S(1)}, f32[16,128]{1,0:T(8,128)S(1)}, u32[]{:S(2)}, u32[]{:S(2)}) collective-permute-start(f32[16,128]{1,0:T(8,128)S(1)} %get-tuple-element.70.refs_0_), channel_id=1, source_target_pairs={{0,2},{1,3},{2,0},{3,1},{4,6},{5,7},{6,4},{7,5},{8,10},{9,11},{10,... | collective-permute-start | bytes 24584 | tf_op jit(solution)/shard_map/ppermute | solution.py:303
  27.1 7.8 %collective-permute-start.13 = (bf16[2,128,128]{2,1,0:T(8,128)(2,1)S(1)}, bf16[2,128,128]{2,1,0:T(8,128)(2,1)S(1)}, u32[]{:S(2)}, u32[]{:S(2)}) collective-permute-start(bf16[2,128,128]{2,1,0:T(8,128)(2,1)S(1)} %add_convert_fusion.4), channel_id=1, source_target_pairs={{0,8},{1,9},{2,10},{3,11},{4,12},{5,13},{6,14},{7,15},{8,0},{9,1},... | collective-permute-start | bytes 196616 | tf_op jit(solution)/shard_map/ppermute | solution.py:303
  31.9 7.4 %collective-permute-start.18 = (bf16[576,128]{1,0:T(8,128)(2,1)S(1)}, bf16[576,128]{1,0:T(8,128)(2,1)S(1)}, u32[]{:S(2)}, u32[]{:S(2)}) collective-permute-start(bf16[576,128]{1,0:T(8,128)(2,1)S(1)} %get-tuple-element.86), channel_id=1, source_target_pairs={{0,4},{1,5},{2,6},{3,7},{4,0},{5,1},{6,2},{7,3},{8,12},{9,13},{10,... | collective-permute-start | bytes 442376 | tf_op jit(solution)/shard_map/ppermute | solution.py:303
  34.5 9.4 %collective-permute-start.20 = (bf16[576,128]{1,0:T(8,128)(2,1)S(1)}, bf16[576,128]{1,0:T(8,128)(2,1)S(1)}, u32[]{:S(2)}, u32[]{:S(2)}) collective-permute-start(bf16[576,128]{1,0:T(8,128)(2,1)S(1)} %next_gradients.1), channel_id=1, source_target_pairs={{0,4},{1,5},{2,6},{3,7},{4,0},{5,1},{6,2},{7,3},{8,12},{9,13},{10,... | collective-permute-start | bytes 442376 | tf_op jit(solution)/shard_map/ppermute | solution.py:303
  34.9 4.3 %collective-permute-start.16 = (bf16[2,128,128]{2,1,0:T(8,128)(2,1)S(1)}, bf16[2,128,128]{2,1,0:T(8,128)(2,1)S(1)}, u32[]{:S(2)}, u32[]{:S(2)}) collective-permute-start(bf16[2,128,128]{2,1,0:T(8,128)(2,1)S(1)} %add_convert_fusion.3.refs_0_), channel_id=1, source_target_pairs={{0,2},{1,3},{2,0},{3,1},{4,6},{5,7},{6,4},{7,5},{8,10},{9,11},{10,... | collective-permute-start | bytes 196616 | tf_op jit(solution)/shard_map/ppermute | solution.py:303
  37.4 3.2 %collective-permute-start.14 = (bf16[576,128]{1,0:T(8,128)(2,1)S(1)}, bf16[576,128]{1,0:T(8,128)(2,1)S(1)}, u32[]{:S(2)}, u32[]{:S(2)}) collective-permute-start(bf16[576,128]{1,0:T(8,128)(2,1)S(1)} %get-tuple-element.82), channel_id=1, source_target_pairs={{0,1},{1,0},{2,3},{3,2},{4,5},{5,4},{6,7},{7,6},{8,9},{9,8},{10,11... | collective-permute-start | bytes 442376 | tf_op jit(solution)/shard_map/ppermute | solution.py:303
  37.5 3.2 %collective-permute-start.15 = (bf16[576,128]{1,0:T(8,128)(2,1)S(1)}, bf16[576,128]{1,0:T(8,128)(2,1)S(1)}, u32[]{:S(2)}, u32[]{:S(2)}) collective-permute-start(bf16[576,128]{1,0:T(8,128)(2,1)S(1)} %get-tuple-element.83), channel_id=1, source_target_pairs={{0,1},{1,0},{2,3},{3,2},{4,5},{5,4},{6,7},{7,6},{8,9},{9,8},{10,11... | collective-permute-start | bytes 442376 | tf_op jit(solution)/shard_map/ppermute | solution.py:303
  39.2 3.8 %collective-permute-start.17 = (bf16[4,128,128]{2,1,0:T(8,128)(2,1)S(1)}, bf16[4,128,128]{2,1,0:T(8,128)(2,1)S(1)}, u32[]{:S(2)}, u32[]{:S(2)}) collective-permute-start(bf16[4,128,128]{2,1,0:T(8,128)(2,1)S(1)} %pad_maximum_fusion), channel_id=1, source_target_pairs={{0,1},{1,0},{2,3},{3,2},{4,5},{5,4},{6,7},{7,6},{8,9},{9,8},{10,11... | collective-permute-start | bytes 393224 | tf_op jit(solution)/shard_map/ppermute | solution.py:303
  39.4 10.4 %collective-permute-start.19 = (bf16[576,128]{1,0:T(8,128)(2,1)S(1)}, bf16[576,128]{1,0:T(8,128)(2,1)S(1)}, u32[]{:S(2)}, u32[]{:S(2)}) collective-permute-start(bf16[576,128]{1,0:T(8,128)(2,1)S(1)} %add_convert_fusion), channel_id=1, source_target_pairs={{0,8},{1,9},{2,10},{3,11},{4,12},{5,13},{6,14},{7,15},{8,0},{9,1},... | collective-permute-start | bytes 442376 | tf_op jit(solution)/shard_map/ppermute | solution.py:303
  40.7 9.2 %collective-permute-start.22 = (bf16[2,576,128]{2,1,0:T(8,128)(2,1)S(1)}, bf16[2,576,128]{2,1,0:T(8,128)(2,1)S(1)}, u32[]{:S(2)}, u32[]{:S(2)}) collective-permute-start(bf16[2,576,128]{2,1,0:T(8,128)(2,1)S(1)} %join.1), channel_id=1, source_target_pairs={{0,2},{1,3},{2,0},{3,1},{4,6},{5,7},{6,4},{7,5},{8,10},{9,11},{10,... | collective-permute-start | bytes 884744 | tf_op jit(solution)/shard_map/ppermute | solution.py:303
  42.2 7.6 %collective-permute-start.21 = (bf16[2,576,128]{2,1,0:T(8,128)(2,1)S(1)}, bf16[2,576,128]{2,1,0:T(8,128)(2,1)S(1)}, u32[]{:S(2)}, u32[]{:S(2)}) collective-permute-start(bf16[2,576,128]{2,1,0:T(8,128)(2,1)S(1)} %get-tuple-element.92), channel_id=1, source_target_pairs={{0,1},{1,0},{2,3},{3,2},{4,5},{5,4},{6,7},{7,6},{8,9},{9,8},{10,11... | collective-permute-start | bytes 884744 | tf_op jit(solution)/shard_map/ppermute | solution.py:303

commit v17 on v16

--- a/solution.py
+++ b/solution.py
@@ -90,11 +90,6 @@
     rows_ref[...] = both.astype(F32).astype(BF16)
     send_off(rows_ref, lat_msg.at[pl.ds(width, EXTRA), :])
     send_off(rows_ref, q_msg.at[pl.ds(heads * (width + HEAD_DIM), EXTRA), :])
-    started[4].wait()
-    send_off(lat_ref, lat_msg.at[pl.ds(0, width), :])
-    for h in range(heads):
-        started[5 + h].wait()
-        send_off(q_ref.at[h], q_msg.at[pl.ds(h * width, width), :])
     delta_ref[...] = jnp.zeros_like(delta_ref)
     started[2].wait()
     attn = [attn_ref[:, h, :].T for h in range(heads)]
@@ -108,6 +103,11 @@
         target[k // 2 * heads : (k // 2 + 1) * heads] = term[:, pl.ds(at, step), :].astype(BF16)
     send_off(send_ref, send_hbm)
     send_off(keep_ref, keep_hbm)
+    started[4].wait()
+    send_off(lat_ref, lat_msg.at[pl.ds(0, width), :])
+    for h in range(heads):
+        started[5 + h].wait()
+        send_off(q_ref.at[h], q_msg.at[pl.ds(h * width, width), :])
     started[3].wait()
     for h in range(heads):
         g = mm(wuv_ref[h], og_t_ref[h]).astype(BF16).astype(F32)

time: 51 us -> 50.9 us (level)
  transfers between devices with their start and end apart: 23 -> 23, of which waited for: 8 -> 7; matrix products, arithmetic and copies ran while one was open for 2% -> 2% of each run, Pallas kernels for 17% -> 17%
where the time goes in v17:
time: 50.9 us; the launch traced here: 50.6 us
  starting transfers between devices  24.6 us (48%)
  Pallas kernels  12.2 us (24%)
  waiting for transfers between devices  9.27 us (18%)
  local copies, waits for them, and re-layouts  2.6 us (5%)
  other arithmetic  1.1 us (2%)
  between operations  0.84 us (2%)
    ppermute x23, starting transfers between devices, swap(): return lax.ppermute(x, axis, [(i, i ^ mask) for i in range(size)])  24.6 us
    pallas_call x14, Pallas kernels, call(): pl.pallas_call(kernel, out_shape=[jax.ShapeDtypeStruct(s, d) for s, d in...  12.2 us
    ppermute x23, waiting for transfers between devices, swap(): return lax.ppermute(x, axis, [(i, i ^ mask) for i in range(size)])  9.27 us
    unnamed x8, local copies, waits for them, and re-layouts  2.58 us
    convert_element_type x6, other arithmetic, add(): return (a.astype(F32) + b.astype(F32)).astype(BF16)  1.09 us
  transfers between devices with their start and end apart: 23, of which 7 were waited for; matrix products, arithmetic and copies ran while one was open for 2% of the time, Pallas kernels for 17%

profile of v17, /device:TPU:0, one launch (start us, length us, event | category | flops | bytes accessed | tf_op | source)
XLA Modules:
  0.0 50.6 jit_solution(13684578790627327088)
XLA Ops:
  0.6 2.8 %pack.1 = (bf16[592,128]{1,0:T(8,128)(2,1)}, bf16[1424,128]{1,0:T(8,128)(2,1)}, f32[8,128]{1,0:T(8,128)}, bf16[4,128,128]{2,1,0:T(8,128)(2,1)}, bf16[4,128,128]{2,1,0:T(8,128)(2,1)}) custom-call(s32[1]{0:T(128)} %bitcast.idx_ref, s32[1,128]{1,0:T(1,128)} %pos_hbm.1, bf16[2,576,128]{2,1,0:T(8,128)(2,1)} %bitcast.15, bf16[128,2,128]{2,1,0:T(2,128)(2,1)} %bitcast.18, ...), custom_call_target="tpu_custom_call" | custom-call | bytes 1815044 | tf_op jit(solution)/shard_map/pack/pallas_call | solution.py:40
  3.5 0.5 %collective-permute-start = (bf16[1424,128]{1,0:T(8,128)(2,1)}, bf16[1424,128]{1,0:T(8,128)(2,1)S(1)}, u32[]{:S(2)}, u32[]{:S(2)}) collective-permute-start(bf16[1424,128]{1,0:T(8,128)(2,1)} %get-tuple-element.49.refs_1_), channel_id=1, source_target_pairs={{0,1},{1,0},{2,3},{3,2},{4,5},{5,4},{6,7},{7,6},{8,9},{9,8},{10,11... | collective-permute-start | bytes 1093640 | tf_op jit(solution)/shard_map/ppermute | solution.py:303
  4.0 0.1 collective-permute-start.4
  4.1 2.9 %collective-permute-start.1 = (bf16[1424,128]{1,0:T(8,128)(2,1)}, bf16[1424,128]{1,0:T(8,128)(2,1)S(1)}, u32[]{:S(2)}, u32[]{:S(2)}) collective-permute-start(bf16[1424,128]{1,0:T(8,128)(2,1)} %get-tuple-element.49.refs_1_), channel_id=1, source_target_pairs={{0,2},{1,3},{2,0},{3,1},{4,6},{5,7},{6,4},{7,5},{8,10},{9,11},{10,... | collective-permute-start | bytes 1093640 | tf_op jit(solution)/shard_map/ppermute | solution.py:303
  7.0 2.6 %collective-permute-start.3 = (bf16[592,128]{1,0:T(8,128)(2,1)}, bf16[592,128]{1,0:T(8,128)(2,1)S(1)}, u32[]{:S(2)}, u32[]{:S(2)}) collective-permute-start(bf16[592,128]{1,0:T(8,128)(2,1)} %get-tuple-element.51.refs_0_), channel_id=1, source_target_pairs={{0,8},{1,9},{2,10},{3,11},{4,12},{5,13},{6,14},{7,15},{8,0},{9,1},... | collective-permute-start | bytes 454664 | tf_op jit(solution)/shard_map/ppermute | solution.py:303
  9.6 0.0 collective-permute-done.refs_4_.refs_1_
  9.6 1.6 %collective-permute-start.2 = (bf16[592,128]{1,0:T(8,128)(2,1)}, bf16[592,128]{1,0:T(8,128)(2,1)S(1)}, u32[]{:S(2)}, u32[]{:S(2)}) collective-permute-start(bf16[592,128]{1,0:T(8,128)(2,1)} %get-tuple-element.51.refs_0_), channel_id=1, source_target_pairs={{0,4},{1,5},{2,6},{3,7},{4,0},{5,1},{6,2},{7,3},{8,12},{9,13},{10,... | collective-permute-start | bytes 454664 | tf_op jit(solution)/shard_map/ppermute | solution.py:303
  11.2 0.0 collective-permute-done.4
  11.2 0.9 %add_convert_fusion.2 = bf16[4,128,128]{2,1,0:T(8,128)(2,1)S(1)} fusion(bf16[4,128,128]{2,1,0:T(8,128)(2,1)S(1)} %collective-permute-done.4, bf16[4,128,128]{2,1,0:T(8,128)(2,1)} %get-tuple-element.52), kind=kLoop, calls=%fused_computation.2 | loop fusion | flops 262144 | bytes 393216 | tf_op jit(solution)/shard_map/convert_element_type | solution.py:351
  12.1 1.6 %collective-permute-start.5 = (bf16[4,128,128]{2,1,0:T(8,128)(2,1)S(1)}, bf16[4,128,128]{2,1,0:T(8,128)(2,1)S(1)}, u32[]{:S(2)}, u32[]{:S(2)}) collective-permute-start(bf16[4,128,128]{2,1,0:T(8,128)(2,1)S(1)} %add_convert_fusion.2), channel_id=1, source_target_pairs={{0,16},{16,0},{1,17},{17,1},{2,18},{18,2},{3,19},{19,3},{4,20},{20... | collective-permute-start | bytes 393224 | tf_op jit(solution)/shard_map/ppermute | solution.py:303
  13.7 1.0 %copy-done = bf16[1424,128]{1,0:T(8,128)(2,1)S(1)} copy-done((bf16[1424,128]{1,0:T(8,128)(2,1)S(1)}, bf16[1424,128]{1,0:T(8,128)(2,1)}, u32[]{:S(2)}) %copy-start) | copy-done | bytes 364568
  14.7 0.9 %copy-done.2 = bf16[592,128]{1,0:T(8,128)(2,1)S(1)} copy-done((bf16[592,128]{1,0:T(8,128)(2,1)S(1)}, bf16[592,128]{1,0:T(8,128)(2,1)}, u32[]{:S(2)}) %copy-start.2) | copy-done | bytes 151576
  15.6 0.7 %copy-done.3 = f32[8,128]{1,0:T(8,128)S(1)} copy-done((f32[8,128]{1,0:T(8,128)S(1)}, f32[8,128]{1,0:T(8,128)}, u32[]{:S(2)}) %copy-start.3) | copy-done | bytes 4120
  16.3 0.8 %collective-permute-done.3.refs_2_.refs_9_ = bf16[592,128]{1,0:T(8,128)(2,1)S(1)} collective-permute-done((bf16[592,128]{1,0:T(8,128)(2,1)}, bf16[592,128]{1,0:T(8,128)(2,1)S(1)}, u32[]{:S(2)}, u32[]{:S(2)}) %collective-permute-start.3) | collective-permute-done | bytes 151584 | tf_op jit(solution)/shard_map/ppermute | solution.py:303
  17.1 0.0 collective-permute-done.5
  17.2 0.0 collective-permute-done.1.refs_5_.refs_2_
  17.2 0.1 collective-permute-done.2.refs_1_.refs_8_
  17.3 0.0 collective-permute-start.6
  17.4 0.0 copy-start.1
  17.4 0.5 %collective-permute-start.11 = (bf16[2,128,128]{2,1,0:T(8,128)(2,1)S(1)}, bf16[2,128,128]{2,1,0:T(8,128)(2,1)S(1)}, u32[]{:S(2)}, u32[]{:S(2)}) collective-permute-start(bf16[2,128,128]{2,1,0:T(8,128)(2,1)S(1)} %slice.17), channel_id=1, source_target_pairs={{0,2},{1,3},{2,0},{3,1},{4,6},{5,7},{6,4},{7,5},{8,10},{9,11},{10,... | collective-permute-start | bytes 196616 | tf_op jit(solution)/shard_map/ppermute | solution.py:303
  17.9 1.5 %collective-permute-start.7 = (bf16[592,128]{1,0:T(8,128)(2,1)S(1)}, bf16[592,128]{1,0:T(8,128)(2,1)S(1)}, u32[]{:S(2)}, u32[]{:S(2)}) collective-permute-start(bf16[592,128]{1,0:T(8,128)(2,1)S(1)} %collective-permute-done.3.refs_2_.refs_9_), channel_id=1, source_target_pairs={{0,4},{1,5},{2,6},{3,7},{4,0},{5,1},{6,2},{7,3},{8,12},{9,13},{10,... | collective-permute-start | bytes 454664 | tf_op jit(solution)/shard_map/ppermute | solution.py:303
  19.4 0.0 collective-permute-done.6.refs_6_.refs_3_
  19.4 1.2 %near_scores.1 = (f32[384,1024]{1,0:T(8,128)S(1)}, bf16[384,640]{1,0:T(8,128)(2,1)S(1)}, f32[16,128]{1,0:T(8,128)S(1)}, bf16[640,1024]{1,0:T(8,128)(2,1)S(1)}) custom-call(bf16[592,128]{1,0:T(8,128)(2,1)S(1)} %get-tuple-element.61.refs_0_.refs_7_, bf16[592,128]{1,0:T(8,128)(2,1)S(1)} %collective-permute-done.2.refs_1_.refs_8_, ...), custom_call_target="tpu_custom_call" | custom-call | tf_op jit(solution)/shard_map/near_scores/pallas_call | solution.py:40
  20.6 1.3 %collective-permute-done.11 = bf16[2,128,128]{2,1,0:T(8,128)(2,1)S(1)} collective-permute-done((bf16[2,128,128]{2,1,0:T(8,128)(2,1)S(1)}, bf16[2,128,128]{2,1,0:T(8,128)(2,1)S(1)}, u32[]{:S(2)}, u32[]{:S(2)}) %collective-permute-start.11) | collective-permute-done | bytes 65568 | tf_op jit(solution)/shard_map/ppermute | solution.py:303
  22.0 1.5 %collective-permute-start.12 = (bf16[2,128,128]{2,1,0:T(8,128)(2,1)S(1)}, bf16[2,128,128]{2,1,0:T(8,128)(2,1)S(1)}, u32[]{:S(2)}, u32[]{:S(2)}) collective-permute-start(bf16[2,128,128]{2,1,0:T(8,128)(2,1)S(1)} %add_convert_fusion.5), channel_id=1, source_target_pairs={{0,4},{1,5},{2,6},{3,7},{4,0},{5,1},{6,2},{7,3},{8,12},{9,13},{10,... | collective-permute-start | bytes 196616 | tf_op jit(solution)/shard_map/ppermute | solution.py:303
  23.5 0.5 collective-permute-done.7.refs_0_.refs_10_
  24.0 0.5 last_scores.1
  24.5 0.7 %collective-permute-start.10 = (f32[16,128]{1,0:T(8,128)S(1)}, f32[16,128]{1,0:T(8,128)S(1)}, u32[]{:S(2)}, u32[]{:S(2)}) collective-permute-start(f32[16,128]{1,0:T(8,128)S(1)} %get-tuple-element.70.refs_0_), channel_id=1, source_target_pairs={{0,3},{1,2},{2,1},{3,0},{4,7},{5,6},{6,5},{7,4},{8,11},{9,10},{10,... | collective-permute-start | bytes 24584 | tf_op jit(solution)/shard_map/ppermute | solution.py:303
  25.1 1.8 %collective-permute-start.8 = (f32[16,128]{1,0:T(8,128)S(1)}, f32[16,128]{1,0:T(8,128)S(1)}, u32[]{:S(2)}, u32[]{:S(2)}) collective-permute-start(f32[16,128]{1,0:T(8,128)S(1)} %get-tuple-element.70.refs_0_), channel_id=1, source_target_pairs={{0,1},{1,0},{2,3},{3,2},{4,5},{5,4},{6,7},{7,6},{8,9},{9,8},{10,11... | collective-permute-start | bytes 24584 | tf_op jit(solution)/shard_map/ppermute | solution.py:303
  26.9 0.0 collective-permute-start.9
  27.0 0.0 collective-permute-done.12
  27.0 2.3 %collective-permute-start.13 = (bf16[2,128,128]{2,1,0:T(8,128)(2,1)S(1)}, bf16[2,128,128]{2,1,0:T(8,128)(2,1)S(1)}, u32[]{:S(2)}, u32[]{:S(2)}) collective-permute-start(bf16[2,128,128]{2,1,0:T(8,128)(2,1)S(1)} %add_convert_fusion.4), channel_id=1, source_target_pairs={{0,8},{1,9},{2,10},{3,11},{4,12},{5,13},{6,14},{7,15},{8,0},{9,1},... | collective-permute-start | bytes 196616 | tf_op jit(solution)/shard_map/ppermute | solution.py:303
  29.3 1.6 %context.1 = (bf16[512,1024]{1,0:T(8,128)(2,1)S(1)}, f32[384,1024]{1,0:T(8,128)S(1)}, f32[128,1024]{1,0:T(8,128)S(1)}) custom-call(bf16[1424,128]{1,0:T(8,128)(2,1)S(1)} %get-tuple-element.58.refs_3_.refs_0_, bf16[1424,128]{1,0:T(8,128)(2,1)S(1)} %collective-permute-done.refs_4_.refs_1_, bf16[1424,128]{1,0:T(8,128)(2,1)S(1)} %collective-permute-done.1.refs_5_.refs_2_, ...), custom_call_target="tpu_custom_call" | custom-call | flops 2013265920 | bytes 16564224 | tf_op jit(solution)/shard_map/context/pallas_call | solution.py:40
  30.9 0.0 collective-permute-done.10.refs_3_
  30.9 0.0 collective-permute-done.8.refs_1_
  30.9 0.0 collective-permute-done.9.refs_2_
  30.9 0.8 %last_gradients.1 = (bf16[576,128]{1,0:T(8,128)(2,1)S(1)}, bf16[128,1024]{1,0:T(8,128)(2,1)S(1)}) custom-call(f32[16,128]{1,0:T(8,128)S(1)} %get-tuple-element.70.refs_0_, f32[16,128]{1,0:T(8,128)S(1)} %collective-permute-done.8.refs_1_, f32[16,128]{1,0:T(8,128)S(1)} %collective-permute-done.9.refs_2_, f32[16,128]{1,0:T(8,128)S(1)} %collective-permute-done.10.refs_3_, ...), custom_call_target="tpu_custom_call" | custom-call | flops 285212672 | bytes 3850240 | tf_op jit(solution)/shard_map/last_gradients/pallas_call | solution.py:40
  31.8 1.8 %collective-permute-start.18 = (bf16[576,128]{1,0:T(8,128)(2,1)S(1)}, bf16[576,128]{1,0:T(8,128)(2,1)S(1)}, u32[]{:S(2)}, u32[]{:S(2)}) collective-permute-start(bf16[576,128]{1,0:T(8,128)(2,1)S(1)} %get-tuple-element.86), channel_id=1, source_target_pairs={{0,4},{1,5},{2,6},{3,7},{4,0},{5,1},{6,2},{7,3},{8,12},{9,13},{10,... | collective-permute-start | bytes 442376 | tf_op jit(solution)/shard_map/ppermute | solution.py:303
  33.5 0.8 %next_gradients.1 = bf16[576,128]{1,0:T(8,128)(2,1)S(1)} custom-call(f32[16,128]{1,0:T(8,128)S(1)} %get-tuple-element.70.refs_0_, f32[16,128]{1,0:T(8,128)S(1)} %collective-permute-done.8.refs_1_, f32[16,128]{1,0:T(8,128)S(1)} %collective-permute-done.9.refs_2_, f32[16,128]{1,0:T(8,128)S(1)} %collective-permute-done.10.refs_3_, ...), custom_call_target="tpu_custom_call" | custom-call | flops 285212672 | bytes 5685248 | tf_op jit(solution)/shard_map/next_gradients/pallas_call | solution.py:40
  34.3 0.4 collective-permute-start.20
  34.7 0.0 collective-permute-done.13
  34.7 1.4 %collective-permute-start.16 = (bf16[2,128,128]{2,1,0:T(8,128)(2,1)S(1)}, bf16[2,128,128]{2,1,0:T(8,128)(2,1)S(1)}, u32[]{:S(2)}, u32[]{:S(2)}) collective-permute-start(bf16[2,128,128]{2,1,0:T(8,128)(2,1)S(1)} %add_convert_fusion.3.refs_0_), channel_id=1, source_target_pairs={{0,2},{1,3},{2,0},{3,1},{4,6},{5,7},{6,4},{7,5},{8,10},{9,11},{10,... | collective-permute-start | bytes 196616 | tf_op jit(solution)/shard_map/ppermute | solution.py:303
  36.1 1.1 %query_gradients.1 = (bf16[2,576,128]{2,1,0:T(8,128)(2,1)S(1)}, bf16[2,576,128]{2,1,0:T(8,128)(2,1)S(1)}, bf16[2,576,128]{2,1,0:T(8,128)(2,1)S(1)}, bf16[576,128...) custom-call(f32[16,128]{1,0:T(8,128)S(1)} %get-tuple-element.70.refs, ...), custom_call_target="tpu_custom_call" | custom-call | tf_op jit(solution)/shard_map/query_gradients/pallas_call | solution.py:40
  37.3 0.1 collective-permute-start.14
  37.4 0.5 collective-permute-start.15
  37.9 0.7 %middle_gradients.1 = bf16[576,128]{1,0:T(8,128)(2,1)S(1)} custom-call(bf16[512,1024]{1,0:T(8,128)(2,1)S(1)} %get-tuple-element.69.refs_6_.g_ref, bf16[640,1024]{1,0:T(8,128)(2,1)S(1)} %get-tuple-element.65.refs_1_.refs_7_.q_all_ref, bf16[384,1024]{1,0:T(8,128)(2,1)S(1)} %get-tuple-element.80.gs_ref, bf16[384,1024]{1,0:T(8,128)(2,1)S(1)} %get-tuple-element.84.p_ref), custom_call_target="tpu_custom_call" | custom-call | flops 855638016 | bytes 12238848 | tf_op jit(solution)/shard_map/middle_gradients/pallas_call | solution.py:40
  38.6 0.5 collective-permute-done.16.refs_2_
  39.1 0.1 collective-permute-start.17
  39.2 0.0 collective-permute-done.18
  39.2 1.3 %collective-permute-start.19 = (bf16[576,128]{1,0:T(8,128)(2,1)S(1)}, bf16[576,128]{1,0:T(8,128)(2,1)S(1)}, u32[]{:S(2)}, u32[]{:S(2)}) collective-permute-start(bf16[576,128]{1,0:T(8,128)(2,1)S(1)} %add_convert_fusion), channel_id=1, source_target_pairs={{0,8},{1,9},{2,10},{3,11},{4,12},{5,13},{6,14},{7,15},{8,0},{9,1},... | collective-permute-start | bytes 442376 | tf_op jit(solution)/shard_map/ppermute | solution.py:303
  40.5 0.0 collective-permute-done.14.refs_0_
  40.5 0.0 collective-permute-done.15.refs_1_
  40.5 0.1 join.1
  40.6 1.5 %collective-permute-start.22 = (bf16[2,576,128]{2,1,0:T(8,128)(2,1)S(1)}, bf16[2,576,128]{2,1,0:T(8,128)(2,1)S(1)}, u32[]{:S(2)}, u32[]{:S(2)}) collective-permute-start(bf16[2,576,128]{2,1,0:T(8,128)(2,1)S(1)} %join.1), channel_id=1, source_target_pairs={{0,2},{1,3},{2,0},{3,1},{4,6},{5,7},{6,4},{7,5},{8,10},{9,11},{10,... | collective-permute-start | bytes 884744 | tf_op jit(solution)/shard_map/ppermute | solution.py:303
  42.1 0.0 collective-permute-start.21
  42.1 0.7 %near_gradients.1.refs_0_ = bf16[576,128]{1,0:T(8,128)(2,1)S(1)} custom-call(bf16[512,1024]{1,0:T(8,128)(2,1)S(1)} %get-tuple-element.69.refs_6_.g_ref, bf16[640,1024]{1,0:T(8,128)(2,1)S(1)} %get-tuple-element.65.refs_1_.refs_7_.q_all_ref, bf16[384,1024]{1,0:T(8,128)(2,1)S(1)} %get-tuple-element.80.gs_ref, bf16[384,1024]{1,0:T(8,128)(2,1)S(1)} %get-tuple-element.84.p_ref), custom_call_target="tpu_custom_call" | custom-call | flops 285212672 | bytes 4079616 | tf_op jit(solution)/shard_map/near_gradients/pallas_call | solution.py:40
  42.9 0.0 collective-permute-done.17
  42.9 0.8 %spread.1 = f32[2,512,128]{2,1,0:T(8,128)} custom-call(s32[1]{0:T(128)} %bitcast.idx_ref, bf16[2,128,128]{2,1,0:T(8,128)(2,1)S(1)} %add_convert_fusion.3.refs_0_, bf16[2,128,128]{2,1,0:T(8,128)(2,1)S(1)} %get-tuple-element.96.refs_1_, bf16[2,128,128]{2,1,0:T(8,128)(2,1)S(1)} %collective-permute-done.16.refs_2_, ...), custom_call_target="tpu_custom_call" | custom-call | bytes 786436 | tf_op jit(solution)/shard_map/spread/pallas_call | solution.py:40
  43.7 0.0 collective-permute-done.20.refs_2_
  43.7 5.9 %collective-permute-done.19.refs_1_ = bf16[576,128]{1,0:T(8,128)(2,1)S(1)} collective-permute-done((bf16[576,128]{1,0:T(8,128)(2,1)S(1)}, bf16[576,128]{1,0:T(8,128)(2,1)S(1)}, u32[]{:S(2)}, u32[]{:S(2)}) %collective-permute-start.19) | collective-permute-done | bytes 147488 | tf_op jit(solution)/shard_map/ppermute | solution.py:303
  49.6 0.1 latent_sum.1.lat_sum_ref
  49.7 0.0 collective-permute-done.21.refs_1_
  49.7 0.1 collective-permute-done.22.refs_2_
  49.8 0.8 %finish.1 = (bf16[576,128]{1,0:T(8,128)(2,1)}, bf16[2,576,128]{2,1,0:T(8,128)(2,1)}) custom-call(f32[576,128]{1,0:T(8,128)S(1)} %latent_sum.1.lat_sum_ref, bf16[2,576,128]{2,1,0:T(8,128)(2,1)S(1)} %get-tuple-element.88.refs_0_, bf16[2,576,128]{2,1,0:T(8,128)(2,1)S(1)} %collective-permute-done.21.refs_1_, bf16[2,576,128]{2,1,0:T(8,128)(2,1)S(1)} %collective-permute-done.22.refs_2_), custom_call_target="tpu_custom_call" | custom-call | bytes 1622016 | tf_op jit(solution)/shard_map/finish/pallas_call | solution.py:40
  (13 shorter events, 0.2 us)
Async XLA Ops:
  3.5 6.1 %collective-permute-start = (bf16[1424,128]{1,0:T(8,128)(2,1)}, bf16[1424,128]{1,0:T(8,128)(2,1)S(1)}, u32[]{:S(2)}, u32[]{:S(2)}) collective-permute-start(bf16[1424,128]{1,0:T(8,128)(2,1)} %get-tuple-element.49.refs_1_), channel_id=1, source_target_pairs={{0,1},{1,0},{2,3},{3,2},{4,5},{5,4},{6,7},{7,6},{8,9},{9,8},{10,11... | collective-permute-start | bytes 1093640 | tf_op jit(solution)/shard_map/ppermute | solution.py:303
  4.0 7.2 %collective-permute-start.4 = (bf16[4,128,128]{2,1,0:T(8,128)(2,1)}, bf16[4,128,128]{2,1,0:T(8,128)(2,1)S(1)}, u32[]{:S(2)}, u32[]{:S(2)}) collective-permute-start(bf16[4,128,128]{2,1,0:T(8,128)(2,1)} %get-tuple-element.53), channel_id=1, source_target_pairs={{0,1},{1,0},{2,3},{3,2},{4,5},{5,4},{6,7},{7,6},{8,9},{9,8},{10,11... | collective-permute-start | bytes 393224 | tf_op jit(solution)/shard_map/ppermute | solution.py:303
  4.1 13.1 %collective-permute-start.1 = (bf16[1424,128]{1,0:T(8,128)(2,1)}, bf16[1424,128]{1,0:T(8,128)(2,1)S(1)}, u32[]{:S(2)}, u32[]{:S(2)}) collective-permute-start(bf16[1424,128]{1,0:T(8,128)(2,1)} %get-tuple-element.49.refs_1_), channel_id=1, source_target_pairs={{0,2},{1,3},{2,0},{3,1},{4,6},{5,7},{6,4},{7,5},{8,10},{9,11},{10,... | collective-permute-start | bytes 1093640 | tf_op jit(solution)/shard_map/ppermute | solution.py:303
  7.0 10.1 %collective-permute-start.3 = (bf16[592,128]{1,0:T(8,128)(2,1)}, bf16[592,128]{1,0:T(8,128)(2,1)S(1)}, u32[]{:S(2)}, u32[]{:S(2)}) collective-permute-start(bf16[592,128]{1,0:T(8,128)(2,1)} %get-tuple-element.51.refs_0_), channel_id=1, source_target_pairs={{0,8},{1,9},{2,10},{3,11},{4,12},{5,13},{6,14},{7,15},{8,0},{9,1},... | collective-permute-start | bytes 454664 | tf_op jit(solution)/shard_map/ppermute | solution.py:303
  9.6 7.7 %collective-permute-start.2 = (bf16[592,128]{1,0:T(8,128)(2,1)}, bf16[592,128]{1,0:T(8,128)(2,1)S(1)}, u32[]{:S(2)}, u32[]{:S(2)}) collective-permute-start(bf16[592,128]{1,0:T(8,128)(2,1)} %get-tuple-element.51.refs_0_), channel_id=1, source_target_pairs={{0,4},{1,5},{2,6},{3,7},{4,0},{5,1},{6,2},{7,3},{8,12},{9,13},{10,... | collective-permute-start | bytes 454664 | tf_op jit(solution)/shard_map/ppermute | solution.py:303
  12.1 5.0 %collective-permute-start.5 = (bf16[4,128,128]{2,1,0:T(8,128)(2,1)S(1)}, bf16[4,128,128]{2,1,0:T(8,128)(2,1)S(1)}, u32[]{:S(2)}, u32[]{:S(2)}) collective-permute-start(bf16[4,128,128]{2,1,0:T(8,128)(2,1)S(1)} %add_convert_fusion.2), channel_id=1, source_target_pairs={{0,16},{16,0},{1,17},{17,1},{2,18},{18,2},{3,19},{19,3},{4,20},{20... | collective-permute-start | bytes 393224 | tf_op jit(solution)/shard_map/ppermute | solution.py:303
  13.7 1.0 %copy-start = (bf16[1424,128]{1,0:T(8,128)(2,1)S(1)}, bf16[1424,128]{1,0:T(8,128)(2,1)}, u32[]{:S(2)}) copy-start(bf16[1424,128]{1,0:T(8,128)(2,1)} %get-tuple-element.49.refs_1_) | copy-start | bytes 1093636
  14.7 0.9 %copy-start.2 = (bf16[592,128]{1,0:T(8,128)(2,1)S(1)}, bf16[592,128]{1,0:T(8,128)(2,1)}, u32[]{:S(2)}) copy-start(bf16[592,128]{1,0:T(8,128)(2,1)} %get-tuple-element.51.refs_0_) | copy-start | bytes 454660
  15.6 0.7 %copy-start.3 = (f32[8,128]{1,0:T(8,128)S(1)}, f32[8,128]{1,0:T(8,128)}, u32[]{:S(2)}) copy-start(f32[8,128]{1,0:T(8,128)} %get-tuple-element.54.refs_2_) | copy-start | bytes 12292
  17.3 2.1 %collective-permute-start.6 = (bf16[1424,128]{1,0:T(8,128)(2,1)S(1)}, bf16[1424,128]{1,0:T(8,128)(2,1)S(1)}, u32[]{:S(2)}, u32[]{:S(2)}) collective-permute-start(bf16[1424,128]{1,0:T(8,128)(2,1)S(1)} %collective-permute-done.1.refs_5_.refs_2_), channel_id=1, source_target_pairs={{0,1},{1,0},{2,3},{3,2},{4,5},{5,4},{6,7},{7,6},{8,9},{9,8},{10,11... | collective-permute-start | bytes 1093640 | tf_op jit(solution)/shard_map/ppermute | solution.py:303
  17.4 11.9 %copy-start.1 = (bf16[2,512,128]{2,1,0:T(8,128)(2,1)S(1)}, bf16[2,512,128]{2,1,0:T(8,128)(2,1)}, u32[]{:S(2)}) copy-start(bf16[2,512,128]{2,1,0:T(8,128)(2,1)} %refs_4_.1) | copy-start | bytes 786436
  17.4 4.6 %collective-permute-start.11 = (bf16[2,128,128]{2,1,0:T(8,128)(2,1)S(1)}, bf16[2,128,128]{2,1,0:T(8,128)(2,1)S(1)}, u32[]{:S(2)}, u32[]{:S(2)}) collective-permute-start(bf16[2,128,128]{2,1,0:T(8,128)(2,1)S(1)} %slice.17), channel_id=1, source_target_pairs={{0,2},{1,3},{2,0},{3,1},{4,6},{5,7},{6,4},{7,5},{8,10},{9,11},{10,... | collective-permute-start | bytes 196616 | tf_op jit(solution)/shard_map/ppermute | solution.py:303
  17.9 6.1 %collective-permute-start.7 = (bf16[592,128]{1,0:T(8,128)(2,1)S(1)}, bf16[592,128]{1,0:T(8,128)(2,1)S(1)}, u32[]{:S(2)}, u32[]{:S(2)}) collective-permute-start(bf16[592,128]{1,0:T(8,128)(2,1)S(1)} %collective-permute-done.3.refs_2_.refs_9_), channel_id=1, source_target_pairs={{0,4},{1,5},{2,6},{3,7},{4,0},{5,1},{6,2},{7,3},{8,12},{9,13},{10,... | collective-permute-start | bytes 454664 | tf_op jit(solution)/shard_map/ppermute | solution.py:303
  22.0 5.0 %collective-permute-start.12 = (bf16[2,128,128]{2,1,0:T(8,128)(2,1)S(1)}, bf16[2,128,128]{2,1,0:T(8,128)(2,1)S(1)}, u32[]{:S(2)}, u32[]{:S(2)}) collective-permute-start(bf16[2,128,128]{2,1,0:T(8,128)(2,1)S(1)} %add_convert_fusion.5), channel_id=1, source_target_pairs={{0,4},{1,5},{2,6},{3,7},{4,0},{5,1},{6,2},{7,3},{8,12},{9,13},{10,... | collective-permute-start | bytes 196616 | tf_op jit(solution)/shard_map/ppermute | solution.py:303
  24.5 6.5 %collective-permute-start.10 = (f32[16,128]{1,0:T(8,128)S(1)}, f32[16,128]{1,0:T(8,128)S(1)}, u32[]{:S(2)}, u32[]{:S(2)}) collective-permute-start(f32[16,128]{1,0:T(8,128)S(1)} %get-tuple-element.70.refs_0_), channel_id=1, source_target_pairs={{0,3},{1,2},{2,1},{3,0},{4,7},{5,6},{6,5},{7,4},{8,11},{9,10},{10,... | collective-permute-start | bytes 24584 | tf_op jit(solution)/shard_map/ppermute | solution.py:303
  25.1 5.8 %collective-permute-start.8 = (f32[16,128]{1,0:T(8,128)S(1)}, f32[16,128]{1,0:T(8,128)S(1)}, u32[]{:S(2)}, u32[]{:S(2)}) collective-permute-start(f32[16,128]{1,0:T(8,128)S(1)} %get-tuple-element.70.refs_0_), channel_id=1, source_target_pairs={{0,1},{1,0},{2,3},{3,2},{4,5},{5,4},{6,7},{7,6},{8,9},{9,8},{10,11... | collective-permute-start | bytes 24584 | tf_op jit(solution)/shard_map/ppermute | solution.py:303
  26.9 4.0 %collective-permute-start.9 = (f32[16,128]{1,0:T(8,128)S(1)}, f32[16,128]{1,0:T(8,128)S(1)}, u32[]{:S(2)}, u32[]{:S(2)}) collective-permute-start(f32[16,128]{1,0:T(8,128)S(1)} %get-tuple-element.70.refs_0_), channel_id=1, source_target_pairs={{0,2},{1,3},{2,0},{3,1},{4,6},{5,7},{6,4},{7,5},{8,10},{9,11},{10,... | collective-permute-start | bytes 24584 | tf_op jit(solution)/shard_map/ppermute | solution.py:303
  27.0 7.7 %collective-permute-start.13 = (bf16[2,128,128]{2,1,0:T(8,128)(2,1)S(1)}, bf16[2,128,128]{2,1,0:T(8,128)(2,1)S(1)}, u32[]{:S(2)}, u32[]{:S(2)}) collective-permute-start(bf16[2,128,128]{2,1,0:T(8,128)(2,1)S(1)} %add_convert_fusion.4), channel_id=1, source_target_pairs={{0,8},{1,9},{2,10},{3,11},{4,12},{5,13},{6,14},{7,15},{8,0},{9,1},... | collective-permute-start | bytes 196616 | tf_op jit(solution)/shard_map/ppermute | solution.py:303
  31.8 7.4 %collective-permute-start.18 = (bf16[576,128]{1,0:T(8,128)(2,1)S(1)}, bf16[576,128]{1,0:T(8,128)(2,1)S(1)}, u32[]{:S(2)}, u32[]{:S(2)}) collective-permute-start(bf16[576,128]{1,0:T(8,128)(2,1)S(1)} %get-tuple-element.86), channel_id=1, source_target_pairs={{0,4},{1,5},{2,6},{3,7},{4,0},{5,1},{6,2},{7,3},{8,12},{9,13},{10,... | collective-permute-start | bytes 442376 | tf_op jit(solution)/shard_map/ppermute | solution.py:303
  34.3 9.4 %collective-permute-start.20 = (bf16[576,128]{1,0:T(8,128)(2,1)S(1)}, bf16[576,128]{1,0:T(8,128)(2,1)S(1)}, u32[]{:S(2)}, u32[]{:S(2)}) collective-permute-start(bf16[576,128]{1,0:T(8,128)(2,1)S(1)} %next_gradients.1), channel_id=1, source_target_pairs={{0,4},{1,5},{2,6},{3,7},{4,0},{5,1},{6,2},{7,3},{8,12},{9,13},{10,... | collective-permute-start | bytes 442376 | tf_op jit(solution)/shard_map/ppermute | solution.py:303
  34.7 4.3 %collective-permute-start.16 = (bf16[2,128,128]{2,1,0:T(8,128)(2,1)S(1)}, bf16[2,128,128]{2,1,0:T(8,128)(2,1)S(1)}, u32[]{:S(2)}, u32[]{:S(2)}) collective-permute-start(bf16[2,128,128]{2,1,0:T(8,128)(2,1)S(1)} %add_convert_fusion.3.refs_0_), channel_id=1, source_target_pairs={{0,2},{1,3},{2,0},{3,1},{4,6},{5,7},{6,4},{7,5},{8,10},{9,11},{10,... | collective-permute-start | bytes 196616 | tf_op jit(solution)/shard_map/ppermute | solution.py:303
  37.3 3.2 %collective-permute-start.14 = (bf16[576,128]{1,0:T(8,128)(2,1)S(1)}, bf16[576,128]{1,0:T(8,128)(2,1)S(1)}, u32[]{:S(2)}, u32[]{:S(2)}) collective-permute-start(bf16[576,128]{1,0:T(8,128)(2,1)S(1)} %get-tuple-element.82), channel_id=1, source_target_pairs={{0,1},{1,0},{2,3},{3,2},{4,5},{5,4},{6,7},{7,6},{8,9},{9,8},{10,11... | collective-permute-start | bytes 442376 | tf_op jit(solution)/shard_map/ppermute | solution.py:303
  37.4 3.2 %collective-permute-start.15 = (bf16[576,128]{1,0:T(8,128)(2,1)S(1)}, bf16[576,128]{1,0:T(8,128)(2,1)S(1)}, u32[]{:S(2)}, u32[]{:S(2)}) collective-permute-start(bf16[576,128]{1,0:T(8,128)(2,1)S(1)} %get-tuple-element.83), channel_id=1, source_target_pairs={{0,1},{1,0},{2,3},{3,2},{4,5},{5,4},{6,7},{7,6},{8,9},{9,8},{10,11... | collective-permute-start | bytes 442376 | tf_op jit(solution)/shard_map/ppermute | solution.py:303
  39.1 3.8 %collective-permute-start.17 = (bf16[4,128,128]{2,1,0:T(8,128)(2,1)S(1)}, bf16[4,128,128]{2,1,0:T(8,128)(2,1)S(1)}, u32[]{:S(2)}, u32[]{:S(2)}) collective-permute-start(bf16[4,128,128]{2,1,0:T(8,128)(2,1)S(1)} %pad_maximum_fusion), channel_id=1, source_target_pairs={{0,1},{1,0},{2,3},{3,2},{4,5},{5,4},{6,7},{7,6},{8,9},{9,8},{10,11... | collective-permute-start | bytes 393224 | tf_op jit(solution)/shard_map/ppermute | solution.py:303
  39.2 10.4 %collective-permute-start.19 = (bf16[576,128]{1,0:T(8,128)(2,1)S(1)}, bf16[576,128]{1,0:T(8,128)(2,1)S(1)}, u32[]{:S(2)}, u32[]{:S(2)}) collective-permute-start(bf16[576,128]{1,0:T(8,128)(2,1)S(1)} %add_convert_fusion), channel_id=1, source_target_pairs={{0,8},{1,9},{2,10},{3,11},{4,12},{5,13},{6,14},{7,15},{8,0},{9,1},... | collective-permute-start | bytes 442376 | tf_op jit(solution)/shard_map/ppermute | solution.py:303
  40.6 9.2 %collective-permute-start.22 = (bf16[2,576,128]{2,1,0:T(8,128)(2,1)S(1)}, bf16[2,576,128]{2,1,0:T(8,128)(2,1)S(1)}, u32[]{:S(2)}, u32[]{:S(2)}) collective-permute-start(bf16[2,576,128]{2,1,0:T(8,128)(2,1)S(1)} %join.1), channel_id=1, source_target_pairs={{0,2},{1,3},{2,0},{3,1},{4,6},{5,7},{6,4},{7,5},{8,10},{9,11},{10,... | collective-permute-start | bytes 884744 | tf_op jit(solution)/shard_map/ppermute | solution.py:303
  42.1 7.6 %collective-permute-start.21 = (bf16[2,576,128]{2,1,0:T(8,128)(2,1)S(1)}, bf16[2,576,128]{2,1,0:T(8,128)(2,1)S(1)}, u32[]{:S(2)}, u32[]{:S(2)}) collective-permute-start(bf16[2,576,128]{2,1,0:T(8,128)(2,1)S(1)} %get-tuple-element.92), channel_id=1, source_target_pairs={{0,1},{1,0},{2,3},{3,2},{4,5},{5,4},{6,7},{7,6},{8,9},{9,8},{10,11... | collective-permute-start | bytes 884744 | tf_op jit(solution)/shard_map/ppermute | solution.py:303

commit v18 on v17

--- a/solution.py
+++ b/solution.py
@@ -173,7 +173,7 @@
 
 def context_kernel(width, heads, *refs):
     q_refs = refs[:GROUP]
-    wuv_ref, near_k_ref, last_k_ref, g_ref, near_gp_ref, last_gp_ref = refs[GROUP:]
+    wuv_ref, k_ref, g_ref, gp_ref = refs[GROUP:]
     lat, all_rows = g_ref.shape
     tok = q_refs[0].shape[1]
     rows = heads * tok
@@ -184,8 +184,15 @@
             col = j * rows + h * tok
             g_ref[:, col : col + tok] = mm(wuv_ref[h], og).astype(BF16)
         cols = slice(j * rows, (j + 1) * rows)
-        near_gp_ref[:, cols] = mm(near_k_ref[:, :lat], g_ref[:, cols])
-        last_gp_ref[:, cols] = mm(last_k_ref[:, :lat], g_ref[:, cols])
+        gp_ref[:, cols] = mm(k_ref[:, :lat], g_ref[:, cols])
+
+
+def prob_kernel(k_ref, g_ref, gp_ref):
+    lat, all_rows = g_ref.shape
+    rows = all_rows // GROUP
+    for j in range(GROUP):
+        cols = slice(j * rows, (j + 1) * rows)
+        gp_ref[:, cols] = mm(k_ref[:, :lat], g_ref[:, cols])
 
 
 def pair_kernel(heads, keys, *refs):
@@ -394,22 +401,29 @@
         flops=most * score_flops,
         share=0,
     )
-    mine = add(pair[:heads], after(got_own, near_stat))
+    g, near_gp = call(
+        functools.partial(context_kernel, width, heads),
+        "near_context",
+        [((lat, all_rows), BF16), ((keys, all_rows), F32)],
+        qs + [wuv, near_k],
+        share=0,
+    )
+    mine = add(pair[:heads], after(got_own, near_gp))
     near = swap(mine, *line_hops[0])
     last_s, last_k, stat = call(
         functools.partial(score_kernel, factor, 1, width, heads, True),
         "last_scores",
         [((tok, all_rows), F32), ((tok, wide), BF16), ((EXTRA, tok), F32)],
-        [lats[most], q_all, near_stat, delta],
+        [lats[most], q_all, after(near_stat, near_gp), delta],
         [((wide, tok), BF16)],
         flops=score_flops,
     )
     stats = [stat] + [swap(stat, k) for k in range(1, GROUP)]
-    g, near_gp, last_gp = call(
-        functools.partial(context_kernel, width, heads),
-        "context",
-        [((lat, all_rows), BF16), ((keys, all_rows), F32), ((tok, all_rows), F32)],
-        qs + [wuv, near_k, last_k],
+    (last_gp,) = call(
+        prob_kernel,
+        "last_context",
+        [((tok, all_rows), F32)],
+        [last_k, g],
         flops=2 * lines * tok * all_rows * lat + 2 * all_rows * lat * HEAD_DIM,
         share=3,
     )

time: 50.9 us -> 50.7 us (level)
    pallas_call x14 -> x15, Pallas kernels: 12.2 us -> 12 us  [call(): pl.pallas_call(kernel, out_shape=[jax.ShapeDtypeStruct(s, d) for s, d in...]
  transfers between devices with their start and end apart: 23 -> 23, of which waited for: 7 -> 9; matrix products, arithmetic and copies ran while one was open for 2% -> 2% of each run, Pallas kernels for 17% -> 17%
where the time goes in v18:
time: 50.7 us; the launch traced here: 50.4 us
  starting transfers between devices  24.8 us (49%)
  Pallas kernels  12 us (24%)
  waiting for transfers between devices  9.06 us (18%)
  local copies, waits for them, and re-layouts  2.6 us (5%)
  other arithmetic  1.1 us (2%)
  between operations  0.85 us (2%)
    ppermute x23, starting transfers between devices, swap(): return lax.ppermute(x, axis, [(i, i ^ mask) for i in range(size)])  24.8 us
    pallas_call x15, Pallas kernels, call(): pl.pallas_call(kernel, out_shape=[jax.ShapeDtypeStruct(s, d) for s, d in...  12 us
    ppermute x23, waiting for transfers between devices, swap(): return lax.ppermute(x, axis, [(i, i ^ mask) for i in range(size)])  9.06 us
    unnamed x8, local copies, waits for them, and re-layouts  2.58 us
    convert_element_type x6, other arithmetic, add(): return (a.astype(F32) + b.astype(F32)).astype(BF16)  1.09 us
  transfers between devices with their start and end apart: 23, of which 9 were waited for; matrix products, arithmetic and copies ran while one was open for 2% of the time, Pallas kernels for 17%

profile of v18, /device:TPU:0, one launch (start us, length us, event | category | flops | bytes accessed | tf_op | source)
XLA Modules:
  0.0 50.4 jit_solution(14864740586711720894)
XLA Ops:
  0.6 2.8 %pack.1 = (bf16[592,128]{1,0:T(8,128)(2,1)}, bf16[1424,128]{1,0:T(8,128)(2,1)}, f32[8,128]{1,0:T(8,128)}, bf16[4,128,128]{2,1,0:T(8,128)(2,1)}, bf16[4,128,128]{2,1,0:T(8,128)(2,1)}) custom-call(s32[1]{0:T(128)} %bitcast.idx_ref, s32[1,128]{1,0:T(1,128)} %pos_hbm.1, bf16[2,576,128]{2,1,0:T(8,128)(2,1)} %bitcast.15, bf16[128,2,128]{2,1,0:T(2,128)(2,1)} %bitcast.18, ...), custom_call_target="tpu_custom_call" | custom-call | bytes 1815044 | tf_op jit(solution)/shard_map/pack/pallas_call | solution.py:40
  3.5 0.5 %collective-permute-start = (bf16[1424,128]{1,0:T(8,128)(2,1)}, bf16[1424,128]{1,0:T(8,128)(2,1)S(1)}, u32[]{:S(2)}, u32[]{:S(2)}) collective-permute-start(bf16[1424,128]{1,0:T(8,128)(2,1)} %get-tuple-element.49.refs_1_), channel_id=1, source_target_pairs={{0,1},{1,0},{2,3},{3,2},{4,5},{5,4},{6,7},{7,6},{8,9},{9,8},{10,11... | collective-permute-start | bytes 1093640 | tf_op jit(solution)/shard_map/ppermute | solution.py:310
  4.0 0.1 collective-permute-start.4
  4.1 2.9 %collective-permute-start.1 = (bf16[1424,128]{1,0:T(8,128)(2,1)}, bf16[1424,128]{1,0:T(8,128)(2,1)S(1)}, u32[]{:S(2)}, u32[]{:S(2)}) collective-permute-start(bf16[1424,128]{1,0:T(8,128)(2,1)} %get-tuple-element.49.refs_1_), channel_id=1, source_target_pairs={{0,2},{1,3},{2,0},{3,1},{4,6},{5,7},{6,4},{7,5},{8,10},{9,11},{10,... | collective-permute-start | bytes 1093640 | tf_op jit(solution)/shard_map/ppermute | solution.py:310
  7.0 2.6 %collective-permute-start.3 = (bf16[592,128]{1,0:T(8,128)(2,1)}, bf16[592,128]{1,0:T(8,128)(2,1)S(1)}, u32[]{:S(2)}, u32[]{:S(2)}) collective-permute-start(bf16[592,128]{1,0:T(8,128)(2,1)} %get-tuple-element.51.refs_0_), channel_id=1, source_target_pairs={{0,8},{1,9},{2,10},{3,11},{4,12},{5,13},{6,14},{7,15},{8,0},{9,1},... | collective-permute-start | bytes 454664 | tf_op jit(solution)/shard_map/ppermute | solution.py:310
  9.6 0.0 collective-permute-done.refs_4_.refs_1_
  9.6 1.6 %collective-permute-start.2 = (bf16[592,128]{1,0:T(8,128)(2,1)}, bf16[592,128]{1,0:T(8,128)(2,1)S(1)}, u32[]{:S(2)}, u32[]{:S(2)}) collective-permute-start(bf16[592,128]{1,0:T(8,128)(2,1)} %get-tuple-element.51.refs_0_), channel_id=1, source_target_pairs={{0,4},{1,5},{2,6},{3,7},{4,0},{5,1},{6,2},{7,3},{8,12},{9,13},{10,... | collective-permute-start | bytes 454664 | tf_op jit(solution)/shard_map/ppermute | solution.py:310
  11.2 0.0 collective-permute-done.4
  11.2 0.9 %add_convert_fusion.2 = bf16[4,128,128]{2,1,0:T(8,128)(2,1)S(1)} fusion(bf16[4,128,128]{2,1,0:T(8,128)(2,1)S(1)} %collective-permute-done.4, bf16[4,128,128]{2,1,0:T(8,128)(2,1)} %get-tuple-element.52), kind=kLoop, calls=%fused_computation.2 | loop fusion | flops 262144 | bytes 393216 | tf_op jit(solution)/shard_map/convert_element_type | solution.py:358
  12.1 0.0 copy-start
  12.1 1.6 %collective-permute-start.5 = (bf16[4,128,128]{2,1,0:T(8,128)(2,1)S(1)}, bf16[4,128,128]{2,1,0:T(8,128)(2,1)S(1)}, u32[]{:S(2)}, u32[]{:S(2)}) collective-permute-start(bf16[4,128,128]{2,1,0:T(8,128)(2,1)S(1)} %add_convert_fusion.2), channel_id=1, source_target_pairs={{0,16},{16,0},{1,17},{17,1},{2,18},{18,2},{3,19},{19,3},{4,20},{20... | collective-permute-start | bytes 393224 | tf_op jit(solution)/shard_map/ppermute | solution.py:310
  13.7 1.0 %copy-done.1 = bf16[1424,128]{1,0:T(8,128)(2,1)S(1)} copy-done((bf16[1424,128]{1,0:T(8,128)(2,1)S(1)}, bf16[1424,128]{1,0:T(8,128)(2,1)}, u32[]{:S(2)}) %copy-start.1) | copy-done | bytes 364568
  14.7 0.9 %copy-done.2 = bf16[592,128]{1,0:T(8,128)(2,1)S(1)} copy-done((bf16[592,128]{1,0:T(8,128)(2,1)S(1)}, bf16[592,128]{1,0:T(8,128)(2,1)}, u32[]{:S(2)}) %copy-start.2) | copy-done | bytes 151576
  15.6 0.7 %copy-done.3 = f32[8,128]{1,0:T(8,128)S(1)} copy-done((f32[8,128]{1,0:T(8,128)S(1)}, f32[8,128]{1,0:T(8,128)}, u32[]{:S(2)}) %copy-start.3) | copy-done | bytes 4120
  16.3 0.8 %collective-permute-done.3.refs_2_.refs_9_ = bf16[592,128]{1,0:T(8,128)(2,1)S(1)} collective-permute-done((bf16[592,128]{1,0:T(8,128)(2,1)}, bf16[592,128]{1,0:T(8,128)(2,1)S(1)}, u32[]{:S(2)}, u32[]{:S(2)}) %collective-permute-start.3) | collective-permute-done | bytes 151584 | tf_op jit(solution)/shard_map/ppermute | solution.py:310
  17.1 0.1 collective-permute-done.5
  17.2 0.0 collective-permute-done.1.refs_5_.refs_2_
  17.2 0.1 collective-permute-done.2.refs_1_.refs_8_
  17.3 0.0 collective-permute-start.6
  17.4 0.5 %collective-permute-start.11 = (bf16[2,128,128]{2,1,0:T(8,128)(2,1)S(1)}, bf16[2,128,128]{2,1,0:T(8,128)(2,1)S(1)}, u32[]{:S(2)}, u32[]{:S(2)}) collective-permute-start(bf16[2,128,128]{2,1,0:T(8,128)(2,1)S(1)} %slice.17), channel_id=1, source_target_pairs={{0,2},{1,3},{2,0},{3,1},{4,6},{5,7},{6,4},{7,5},{8,10},{9,11},{10,... | collective-permute-start | bytes 196616 | tf_op jit(solution)/shard_map/ppermute | solution.py:310
  17.9 1.5 %collective-permute-start.7 = (bf16[592,128]{1,0:T(8,128)(2,1)S(1)}, bf16[592,128]{1,0:T(8,128)(2,1)S(1)}, u32[]{:S(2)}, u32[]{:S(2)}) collective-permute-start(bf16[592,128]{1,0:T(8,128)(2,1)S(1)} %collective-permute-done.3.refs_2_.refs_9_), channel_id=1, source_target_pairs={{0,4},{1,5},{2,6},{3,7},{4,0},{5,1},{6,2},{7,3},{8,12},{9,13},{10,... | collective-permute-start | bytes 454664 | tf_op jit(solution)/shard_map/ppermute | solution.py:310
  19.4 0.0 collective-permute-done.6.refs_6_.refs_3_
  19.4 1.2 %near_scores.1 = (f32[384,1024]{1,0:T(8,128)S(1)}, bf16[384,640]{1,0:T(8,128)(2,1)S(1)}, f32[16,128]{1,0:T(8,128)S(1)}, bf16[640,1024]{1,0:T(8,128)(2,1)S(1)}) custom-call(bf16[592,128]{1,0:T(8,128)(2,1)S(1)} %get-tuple-element.61.refs_0_.refs_7_, bf16[592,128]{1,0:T(8,128)(2,1)S(1)} %collective-permute-done.2.refs_1_.refs_8_, ...), custom_call_target="tpu_custom_call" | custom-call | tf_op jit(solution)/shard_map/near_scores/pallas_call | solution.py:40
  20.6 1.1 %near_context.1 = (bf16[512,1024]{1,0:T(8,128)(2,1)S(1)}, f32[384,1024]{1,0:T(8,128)S(1)}) custom-call(bf16[1424,128]{1,0:T(8,128)(2,1)S(1)} %get-tuple-element.58.refs_3_.refs_0_, bf16[1424,128]{1,0:T(8,128)(2,1)S(1)} %collective-permute-done.refs_4_.refs_1_, bf16[1424,128]{1,0:T(8,128)(2,1)S(1)} %collective-permute-done.1.refs_5_.refs_2_, ...), custom_call_target="tpu_custom_call" | custom-call | tf_op jit(solution)/shard_map/near_context/pallas_call | solution.py:40
  21.7 0.2 collective-permute-done.11
  22.0 1.5 %collective-permute-start.12 = (bf16[2,128,128]{2,1,0:T(8,128)(2,1)S(1)}, bf16[2,128,128]{2,1,0:T(8,128)(2,1)S(1)}, u32[]{:S(2)}, u32[]{:S(2)}) collective-permute-start(bf16[2,128,128]{2,1,0:T(8,128)(2,1)S(1)} %add_convert_fusion.5), channel_id=1, source_target_pairs={{0,4},{1,5},{2,6},{3,7},{4,0},{5,1},{6,2},{7,3},{8,12},{9,13},{10,... | collective-permute-start | bytes 196616 | tf_op jit(solution)/shard_map/ppermute | solution.py:310
  23.4 0.5 collective-permute-done.7.refs_0_.refs_10_
  23.9 0.5 last_scores.1
  24.4 0.7 %collective-permute-start.10 = (f32[16,128]{1,0:T(8,128)S(1)}, f32[16,128]{1,0:T(8,128)S(1)}, u32[]{:S(2)}, u32[]{:S(2)}) collective-permute-start(f32[16,128]{1,0:T(8,128)S(1)} %get-tuple-element.71.refs_0_), channel_id=1, source_target_pairs={{0,3},{1,2},{2,1},{3,0},{4,7},{5,6},{6,5},{7,4},{8,11},{9,10},{10,... | collective-permute-start | bytes 24584 | tf_op jit(solution)/shard_map/ppermute | solution.py:310
  25.1 1.1 %collective-permute-start.8 = (f32[16,128]{1,0:T(8,128)S(1)}, f32[16,128]{1,0:T(8,128)S(1)}, u32[]{:S(2)}, u32[]{:S(2)}) collective-permute-start(f32[16,128]{1,0:T(8,128)S(1)} %get-tuple-element.71.refs_0_), channel_id=1, source_target_pairs={{0,1},{1,0},{2,3},{3,2},{4,5},{5,4},{6,7},{7,6},{8,9},{9,8},{10,11... | collective-permute-start | bytes 24584 | tf_op jit(solution)/shard_map/ppermute | solution.py:310
  26.2 0.5 collective-permute-start.9
  26.7 0.0 collective-permute-done.12
  26.7 2.6 %collective-permute-start.13 = (bf16[2,128,128]{2,1,0:T(8,128)(2,1)S(1)}, bf16[2,128,128]{2,1,0:T(8,128)(2,1)S(1)}, u32[]{:S(2)}, u32[]{:S(2)}) collective-permute-start(bf16[2,128,128]{2,1,0:T(8,128)(2,1)S(1)} %add_convert_fusion.4), channel_id=1, source_target_pairs={{0,8},{1,9},{2,10},{3,11},{4,12},{5,13},{6,14},{7,15},{8,0},{9,1},... | collective-permute-start | bytes 196616 | tf_op jit(solution)/shard_map/ppermute | solution.py:310
  29.3 0.3 last_context.1.refs_5_
  29.6 0.0 collective-permute-done.10.refs_3_
  29.6 0.0 collective-permute-done.8.refs_1_
  29.6 0.2 collective-permute-done.9.refs_2_
  29.9 0.8 %last_gradients.1 = (bf16[576,128]{1,0:T(8,128)(2,1)S(1)}, bf16[128,1024]{1,0:T(8,128)(2,1)S(1)}) custom-call(f32[16,128]{1,0:T(8,128)S(1)} %get-tuple-element.71.refs_0_, f32[16,128]{1,0:T(8,128)S(1)} %collective-permute-done.8.refs_1_, f32[16,128]{1,0:T(8,128)S(1)} %collective-permute-done.9.refs_2_, f32[16,128]{1,0:T(8,128)S(1)} %collective-permute-done.10.refs_3_, ...), custom_call_target="tpu_custom_call" | custom-call | flops 285212672 | bytes 3850240 | tf_op jit(solution)/shard_map/last_gradients/pallas_call | solution.py:40
  30.7 1.9 %collective-permute-start.18 = (bf16[576,128]{1,0:T(8,128)(2,1)S(1)}, bf16[576,128]{1,0:T(8,128)(2,1)S(1)}, u32[]{:S(2)}, u32[]{:S(2)}) collective-permute-start(bf16[576,128]{1,0:T(8,128)(2,1)S(1)} %get-tuple-element.86), channel_id=1, source_target_pairs={{0,4},{1,5},{2,6},{3,7},{4,0},{5,1},{6,2},{7,3},{8,12},{9,13},{10,... | collective-permute-start | bytes 442376 | tf_op jit(solution)/shard_map/ppermute | solution.py:310
  32.6 0.8 %next_gradients.1 = bf16[576,128]{1,0:T(8,128)(2,1)S(1)} custom-call(f32[16,128]{1,0:T(8,128)S(1)} %get-tuple-element.71.refs_0_, f32[16,128]{1,0:T(8,128)S(1)} %collective-permute-done.8.refs_1_, f32[16,128]{1,0:T(8,128)S(1)} %collective-permute-done.9.refs_2_, f32[16,128]{1,0:T(8,128)S(1)} %collective-permute-done.10.refs_3_, ...), custom_call_target="tpu_custom_call" | custom-call | flops 285212672 | bytes 5685248 | tf_op jit(solution)/shard_map/next_gradients/pallas_call | solution.py:40
  33.4 0.2 collective-permute-start.20
  33.6 0.0 collective-permute-done.13
  33.6 1.3 %collective-permute-start.16 = (bf16[2,128,128]{2,1,0:T(8,128)(2,1)S(1)}, bf16[2,128,128]{2,1,0:T(8,128)(2,1)S(1)}, u32[]{:S(2)}, u32[]{:S(2)}) collective-permute-start(bf16[2,128,128]{2,1,0:T(8,128)(2,1)S(1)} %add_convert_fusion.3.refs_0_), channel_id=1, source_target_pairs={{0,2},{1,3},{2,0},{3,1},{4,6},{5,7},{6,4},{7,5},{8,10},{9,11},{10,... | collective-permute-start | bytes 196616 | tf_op jit(solution)/shard_map/ppermute | solution.py:310
  34.9 1.1 %query_gradients.1 = (bf16[2,576,128]{2,1,0:T(8,128)(2,1)S(1)}, bf16[2,576,128]{2,1,0:T(8,128)(2,1)S(1)}, bf16[2,576,128]{2,1,0:T(8,128)(2,1)S(1)}, bf16[576,128...) custom-call(f32[16,128]{1,0:T(8,128)S(1)} %get-tuple-element.71.refs, ...), custom_call_target="tpu_custom_call" | custom-call | tf_op jit(solution)/shard_map/query_gradients/pallas_call | solution.py:40
  36.1 0.1 collective-permute-start.14
  36.1 0.5 collective-permute-start.15
  36.6 0.7 %middle_gradients.1 = bf16[576,128]{1,0:T(8,128)(2,1)S(1)} custom-call(bf16[512,1024]{1,0:T(8,128)(2,1)S(1)} %get-tuple-element.65.g_ref.refs_6_, bf16[640,1024]{1,0:T(8,128)(2,1)S(1)} %get-tuple-element.66.refs_1_.refs_7_.q_all_ref, bf16[384,1024]{1,0:T(8,128)(2,1)S(1)} %get-tuple-element.80.gs_ref, bf16[384,1024]{1,0:T(8,128)(2,1)S(1)} %get-tuple-element.84.p_ref), custom_call_target="tpu_custom_call" | custom-call | flops 855638016 | bytes 12238848 | tf_op jit(solution)/shard_map/middle_gradients/pallas_call | solution.py:40
  37.4 0.6 %collective-permute-done.16.refs_2_ = bf16[2,128,128]{2,1,0:T(8,128)(2,1)S(1)} collective-permute-done((bf16[2,128,128]{2,1,0:T(8,128)(2,1)S(1)}, bf16[2,128,128]{2,1,0:T(8,128)(2,1)S(1)}, u32[]{:S(2)}, u32[]{:S(2)}) %collective-permute-start.16) | collective-permute-done | bytes 65568 | tf_op jit(solution)/shard_map/ppermute | solution.py:310
  38.0 0.1 collective-permute-start.17
  38.1 0.0 collective-permute-done.18
  38.1 2.2 %collective-permute-start.19 = (bf16[576,128]{1,0:T(8,128)(2,1)S(1)}, bf16[576,128]{1,0:T(8,128)(2,1)S(1)}, u32[]{:S(2)}, u32[]{:S(2)}) collective-permute-start(bf16[576,128]{1,0:T(8,128)(2,1)S(1)} %add_convert_fusion), channel_id=1, source_target_pairs={{0,8},{1,9},{2,10},{3,11},{4,12},{5,13},{6,14},{7,15},{8,0},{9,1},... | collective-permute-start | bytes 442376 | tf_op jit(solution)/shard_map/ppermute | solution.py:310
  40.3 0.0 collective-permute-done.14.refs_0_
  40.3 0.0 collective-permute-done.15.refs_1_
  40.3 0.1 join.1
  40.4 1.0 %collective-permute-start.22 = (bf16[2,576,128]{2,1,0:T(8,128)(2,1)S(1)}, bf16[2,576,128]{2,1,0:T(8,128)(2,1)S(1)}, u32[]{:S(2)}, u32[]{:S(2)}) collective-permute-start(bf16[2,576,128]{2,1,0:T(8,128)(2,1)S(1)} %join.1), channel_id=1, source_target_pairs={{0,2},{1,3},{2,0},{3,1},{4,6},{5,7},{6,4},{7,5},{8,10},{9,11},{10,... | collective-permute-start | bytes 884744 | tf_op jit(solution)/shard_map/ppermute | solution.py:310
  41.4 0.0 collective-permute-start.21
  41.4 0.7 %near_gradients.1.refs_0_ = bf16[576,128]{1,0:T(8,128)(2,1)S(1)} custom-call(bf16[512,1024]{1,0:T(8,128)(2,1)S(1)} %get-tuple-element.65.g_ref.refs_6_, bf16[640,1024]{1,0:T(8,128)(2,1)S(1)} %get-tuple-element.66.refs_1_.refs_7_.q_all_ref, bf16[384,1024]{1,0:T(8,128)(2,1)S(1)} %get-tuple-element.80.gs_ref, bf16[384,1024]{1,0:T(8,128)(2,1)S(1)} %get-tuple-element.84.p_ref), custom_call_target="tpu_custom_call" | custom-call | flops 285212672 | bytes 4079616 | tf_op jit(solution)/shard_map/near_gradients/pallas_call | solution.py:40
  42.1 0.0 collective-permute-done.17
  42.1 0.8 %spread.1 = f32[2,512,128]{2,1,0:T(8,128)} custom-call(s32[1]{0:T(128)} %bitcast.idx_ref, bf16[2,128,128]{2,1,0:T(8,128)(2,1)S(1)} %add_convert_fusion.3.refs_0_, bf16[2,128,128]{2,1,0:T(8,128)(2,1)S(1)} %get-tuple-element.96.refs_1_, bf16[2,128,128]{2,1,0:T(8,128)(2,1)S(1)} %collective-permute-done.16.refs_2_, ...), custom_call_target="tpu_custom_call" | custom-call | bytes 786436 | tf_op jit(solution)/shard_map/spread/pallas_call | solution.py:40
  43.0 0.0 collective-permute-done.20.refs_2_
  43.0 5.5 %collective-permute-done.19.refs_1_ = bf16[576,128]{1,0:T(8,128)(2,1)S(1)} collective-permute-done((bf16[576,128]{1,0:T(8,128)(2,1)S(1)}, bf16[576,128]{1,0:T(8,128)(2,1)S(1)}, u32[]{:S(2)}, u32[]{:S(2)}) %collective-permute-start.19) | collective-permute-done | bytes 147488 | tf_op jit(solution)/shard_map/ppermute | solution.py:310
  48.5 0.1 latent_sum.1.lat_sum_ref
  48.6 1.0 %collective-permute-done.22.refs_2_ = bf16[2,576,128]{2,1,0:T(8,128)(2,1)S(1)} collective-permute-done((bf16[2,576,128]{2,1,0:T(8,128)(2,1)S(1)}, bf16[2,576,128]{2,1,0:T(8,128)(2,1)S(1)}, u32[]{:S(2)}, u32[]{:S(2)}) %collective-permute-start.22) | collective-permute-done | bytes 294944 | tf_op jit(solution)/shard_map/ppermute | solution.py:310
  49.6 0.8 %finish.1 = (bf16[576,128]{1,0:T(8,128)(2,1)}, bf16[2,576,128]{2,1,0:T(8,128)(2,1)}) custom-call(f32[576,128]{1,0:T(8,128)S(1)} %latent_sum.1.lat_sum_ref, bf16[2,576,128]{2,1,0:T(8,128)(2,1)S(1)} %get-tuple-element.88.refs_0_, bf16[2,576,128]{2,1,0:T(8,128)(2,1)S(1)} %collective-permute-done.21.refs_1_, bf16[2,576,128]{2,1,0:T(8,128)(2,1)S(1)} %collective-permute-done.22.refs_2_), custom_call_target="tpu_custom_call" | custom-call | bytes 1622016 | tf_op jit(solution)/shard_map/finish/pallas_call | solution.py:40
  (14 shorter events, 0.2 us)
Async XLA Ops:
  3.5 6.1 %collective-permute-start = (bf16[1424,128]{1,0:T(8,128)(2,1)}, bf16[1424,128]{1,0:T(8,128)(2,1)S(1)}, u32[]{:S(2)}, u32[]{:S(2)}) collective-permute-start(bf16[1424,128]{1,0:T(8,128)(2,1)} %get-tuple-element.49.refs_1_), channel_id=1, source_target_pairs={{0,1},{1,0},{2,3},{3,2},{4,5},{5,4},{6,7},{7,6},{8,9},{9,8},{10,11... | collective-permute-start | bytes 1093640 | tf_op jit(solution)/shard_map/ppermute | solution.py:310
  4.0 7.2 %collective-permute-start.4 = (bf16[4,128,128]{2,1,0:T(8,128)(2,1)}, bf16[4,128,128]{2,1,0:T(8,128)(2,1)S(1)}, u32[]{:S(2)}, u32[]{:S(2)}) collective-permute-start(bf16[4,128,128]{2,1,0:T(8,128)(2,1)} %get-tuple-element.53), channel_id=1, source_target_pairs={{0,1},{1,0},{2,3},{3,2},{4,5},{5,4},{6,7},{7,6},{8,9},{9,8},{10,11... | collective-permute-start | bytes 393224 | tf_op jit(solution)/shard_map/ppermute | solution.py:310
  4.1 13.1 %collective-permute-start.1 = (bf16[1424,128]{1,0:T(8,128)(2,1)}, bf16[1424,128]{1,0:T(8,128)(2,1)S(1)}, u32[]{:S(2)}, u32[]{:S(2)}) collective-permute-start(bf16[1424,128]{1,0:T(8,128)(2,1)} %get-tuple-element.49.refs_1_), channel_id=1, source_target_pairs={{0,2},{1,3},{2,0},{3,1},{4,6},{5,7},{6,4},{7,5},{8,10},{9,11},{10,... | collective-permute-start | bytes 1093640 | tf_op jit(solution)/shard_map/ppermute | solution.py:310
  7.0 10.1 %collective-permute-start.3 = (bf16[592,128]{1,0:T(8,128)(2,1)}, bf16[592,128]{1,0:T(8,128)(2,1)S(1)}, u32[]{:S(2)}, u32[]{:S(2)}) collective-permute-start(bf16[592,128]{1,0:T(8,128)(2,1)} %get-tuple-element.51.refs_0_), channel_id=1, source_target_pairs={{0,8},{1,9},{2,10},{3,11},{4,12},{5,13},{6,14},{7,15},{8,0},{9,1},... | collective-permute-start | bytes 454664 | tf_op jit(solution)/shard_map/ppermute | solution.py:310
  9.6 7.7 %collective-permute-start.2 = (bf16[592,128]{1,0:T(8,128)(2,1)}, bf16[592,128]{1,0:T(8,128)(2,1)S(1)}, u32[]{:S(2)}, u32[]{:S(2)}) collective-permute-start(bf16[592,128]{1,0:T(8,128)(2,1)} %get-tuple-element.51.refs_0_), channel_id=1, source_target_pairs={{0,4},{1,5},{2,6},{3,7},{4,0},{5,1},{6,2},{7,3},{8,12},{9,13},{10,... | collective-permute-start | bytes 454664 | tf_op jit(solution)/shard_map/ppermute | solution.py:310
  12.1 8.5 %copy-start = (bf16[2,512,128]{2,1,0:T(8,128)(2,1)S(1)}, bf16[2,512,128]{2,1,0:T(8,128)(2,1)}, u32[]{:S(2)}) copy-start(bf16[2,512,128]{2,1,0:T(8,128)(2,1)} %refs_4_.1) | copy-start | bytes 786436
  12.1 5.0 %collective-permute-start.5 = (bf16[4,128,128]{2,1,0:T(8,128)(2,1)S(1)}, bf16[4,128,128]{2,1,0:T(8,128)(2,1)S(1)}, u32[]{:S(2)}, u32[]{:S(2)}) collective-permute-start(bf16[4,128,128]{2,1,0:T(8,128)(2,1)S(1)} %add_convert_fusion.2), channel_id=1, source_target_pairs={{0,16},{16,0},{1,17},{17,1},{2,18},{18,2},{3,19},{19,3},{4,20},{20... | collective-permute-start | bytes 393224 | tf_op jit(solution)/shard_map/ppermute | solution.py:310
  13.7 1.0 %copy-start.1 = (bf16[1424,128]{1,0:T(8,128)(2,1)S(1)}, bf16[1424,128]{1,0:T(8,128)(2,1)}, u32[]{:S(2)}) copy-start(bf16[1424,128]{1,0:T(8,128)(2,1)} %get-tuple-element.49.refs_1_) | copy-start | bytes 1093636
  14.7 0.9 %copy-start.2 = (bf16[592,128]{1,0:T(8,128)(2,1)S(1)}, bf16[592,128]{1,0:T(8,128)(2,1)}, u32[]{:S(2)}) copy-start(bf16[592,128]{1,0:T(8,128)(2,1)} %get-tuple-element.51.refs_0_) | copy-start | bytes 454660
  15.6 0.7 %copy-start.3 = (f32[8,128]{1,0:T(8,128)S(1)}, f32[8,128]{1,0:T(8,128)}, u32[]{:S(2)}) copy-start(f32[8,128]{1,0:T(8,128)} %get-tuple-element.54.refs_2_) | copy-start | bytes 12292
  17.3 2.1 %collective-permute-start.6 = (bf16[1424,128]{1,0:T(8,128)(2,1)S(1)}, bf16[1424,128]{1,0:T(8,128)(2,1)S(1)}, u32[]{:S(2)}, u32[]{:S(2)}) collective-permute-start(bf16[1424,128]{1,0:T(8,128)(2,1)S(1)} %collective-permute-done.1.refs_5_.refs_2_), channel_id=1, source_target_pairs={{0,1},{1,0},{2,3},{3,2},{4,5},{5,4},{6,7},{7,6},{8,9},{9,8},{10,11... | collective-permute-start | bytes 1093640 | tf_op jit(solution)/shard_map/ppermute | solution.py:310
  17.4 4.6 %collective-permute-start.11 = (bf16[2,128,128]{2,1,0:T(8,128)(2,1)S(1)}, bf16[2,128,128]{2,1,0:T(8,128)(2,1)S(1)}, u32[]{:S(2)}, u32[]{:S(2)}) collective-permute-start(bf16[2,128,128]{2,1,0:T(8,128)(2,1)S(1)} %slice.17), channel_id=1, source_target_pairs={{0,2},{1,3},{2,0},{3,1},{4,6},{5,7},{6,4},{7,5},{8,10},{9,11},{10,... | collective-permute-start | bytes 196616 | tf_op jit(solution)/shard_map/ppermute | solution.py:310
  17.9 6.1 %collective-permute-start.7 = (bf16[592,128]{1,0:T(8,128)(2,1)S(1)}, bf16[592,128]{1,0:T(8,128)(2,1)S(1)}, u32[]{:S(2)}, u32[]{:S(2)}) collective-permute-start(bf16[592,128]{1,0:T(8,128)(2,1)S(1)} %collective-permute-done.3.refs_2_.refs_9_), channel_id=1, source_target_pairs={{0,4},{1,5},{2,6},{3,7},{4,0},{5,1},{6,2},{7,3},{8,12},{9,13},{10,... | collective-permute-start | bytes 454664 | tf_op jit(solution)/shard_map/ppermute | solution.py:310
  22.0 4.7 %collective-permute-start.12 = (bf16[2,128,128]{2,1,0:T(8,128)(2,1)S(1)}, bf16[2,128,128]{2,1,0:T(8,128)(2,1)S(1)}, u32[]{:S(2)}, u32[]{:S(2)}) collective-permute-start(bf16[2,128,128]{2,1,0:T(8,128)(2,1)S(1)} %add_convert_fusion.5), channel_id=1, source_target_pairs={{0,4},{1,5},{2,6},{3,7},{4,0},{5,1},{6,2},{7,3},{8,12},{9,13},{10,... | collective-permute-start | bytes 196616 | tf_op jit(solution)/shard_map/ppermute | solution.py:310
  24.4 5.2 %collective-permute-start.10 = (f32[16,128]{1,0:T(8,128)S(1)}, f32[16,128]{1,0:T(8,128)S(1)}, u32[]{:S(2)}, u32[]{:S(2)}) collective-permute-start(f32[16,128]{1,0:T(8,128)S(1)} %get-tuple-element.71.refs_0_), channel_id=1, source_target_pairs={{0,3},{1,2},{2,1},{3,0},{4,7},{5,6},{6,5},{7,4},{8,11},{9,10},{10,... | collective-permute-start | bytes 24584 | tf_op jit(solution)/shard_map/ppermute | solution.py:310
  25.1 4.5 %collective-permute-start.8 = (f32[16,128]{1,0:T(8,128)S(1)}, f32[16,128]{1,0:T(8,128)S(1)}, u32[]{:S(2)}, u32[]{:S(2)}) collective-permute-start(f32[16,128]{1,0:T(8,128)S(1)} %get-tuple-element.71.refs_0_), channel_id=1, source_target_pairs={{0,1},{1,0},{2,3},{3,2},{4,5},{5,4},{6,7},{7,6},{8,9},{9,8},{10,11... | collective-permute-start | bytes 24584 | tf_op jit(solution)/shard_map/ppermute | solution.py:310
  26.2 3.7 %collective-permute-start.9 = (f32[16,128]{1,0:T(8,128)S(1)}, f32[16,128]{1,0:T(8,128)S(1)}, u32[]{:S(2)}, u32[]{:S(2)}) collective-permute-start(f32[16,128]{1,0:T(8,128)S(1)} %get-tuple-element.71.refs_0_), channel_id=1, source_target_pairs={{0,2},{1,3},{2,0},{3,1},{4,6},{5,7},{6,4},{7,5},{8,10},{9,11},{10,... | collective-permute-start | bytes 24584 | tf_op jit(solution)/shard_map/ppermute | solution.py:310
  26.7 6.9 %collective-permute-start.13 = (bf16[2,128,128]{2,1,0:T(8,128)(2,1)S(1)}, bf16[2,128,128]{2,1,0:T(8,128)(2,1)S(1)}, u32[]{:S(2)}, u32[]{:S(2)}) collective-permute-start(bf16[2,128,128]{2,1,0:T(8,128)(2,1)S(1)} %add_convert_fusion.4), channel_id=1, source_target_pairs={{0,8},{1,9},{2,10},{3,11},{4,12},{5,13},{6,14},{7,15},{8,0},{9,1},... | collective-permute-start | bytes 196616 | tf_op jit(solution)/shard_map/ppermute | solution.py:310
  30.7 7.4 %collective-permute-start.18 = (bf16[576,128]{1,0:T(8,128)(2,1)S(1)}, bf16[576,128]{1,0:T(8,128)(2,1)S(1)}, u32[]{:S(2)}, u32[]{:S(2)}) collective-permute-start(bf16[576,128]{1,0:T(8,128)(2,1)S(1)} %get-tuple-element.86), channel_id=1, source_target_pairs={{0,4},{1,5},{2,6},{3,7},{4,0},{5,1},{6,2},{7,3},{8,12},{9,13},{10,... | collective-permute-start | bytes 442376 | tf_op jit(solution)/shard_map/ppermute | solution.py:310
  33.4 9.6 %collective-permute-start.20 = (bf16[576,128]{1,0:T(8,128)(2,1)S(1)}, bf16[576,128]{1,0:T(8,128)(2,1)S(1)}, u32[]{:S(2)}, u32[]{:S(2)}) collective-permute-start(bf16[576,128]{1,0:T(8,128)(2,1)S(1)} %next_gradients.1), channel_id=1, source_target_pairs={{0,4},{1,5},{2,6},{3,7},{4,0},{5,1},{6,2},{7,3},{8,12},{9,13},{10,... | collective-permute-start | bytes 442376 | tf_op jit(solution)/shard_map/ppermute | solution.py:310
  33.6 4.3 %collective-permute-start.16 = (bf16[2,128,128]{2,1,0:T(8,128)(2,1)S(1)}, bf16[2,128,128]{2,1,0:T(8,128)(2,1)S(1)}, u32[]{:S(2)}, u32[]{:S(2)}) collective-permute-start(bf16[2,128,128]{2,1,0:T(8,128)(2,1)S(1)} %add_convert_fusion.3.refs_0_), channel_id=1, source_target_pairs={{0,2},{1,3},{2,0},{3,1},{4,6},{5,7},{6,4},{7,5},{8,10},{9,11},{10,... | collective-permute-start | bytes 196616 | tf_op jit(solution)/shard_map/ppermute | solution.py:310
  36.1 4.3 %collective-permute-start.14 = (bf16[576,128]{1,0:T(8,128)(2,1)S(1)}, bf16[576,128]{1,0:T(8,128)(2,1)S(1)}, u32[]{:S(2)}, u32[]{:S(2)}) collective-permute-start(bf16[576,128]{1,0:T(8,128)(2,1)S(1)} %get-tuple-element.82), channel_id=1, source_target_pairs={{0,1},{1,0},{2,3},{3,2},{4,5},{5,4},{6,7},{7,6},{8,9},{9,8},{10,11... | collective-permute-start | bytes 442376 | tf_op jit(solution)/shard_map/ppermute | solution.py:310
  36.1 4.2 %collective-permute-start.15 = (bf16[576,128]{1,0:T(8,128)(2,1)S(1)}, bf16[576,128]{1,0:T(8,128)(2,1)S(1)}, u32[]{:S(2)}, u32[]{:S(2)}) collective-permute-start(bf16[576,128]{1,0:T(8,128)(2,1)S(1)} %get-tuple-element.83), channel_id=1, source_target_pairs={{0,1},{1,0},{2,3},{3,2},{4,5},{5,4},{6,7},{7,6},{8,9},{9,8},{10,11... | collective-permute-start | bytes 442376 | tf_op jit(solution)/shard_map/ppermute | solution.py:310
  38.0 4.1 %collective-permute-start.17 = (bf16[4,128,128]{2,1,0:T(8,128)(2,1)S(1)}, bf16[4,128,128]{2,1,0:T(8,128)(2,1)S(1)}, u32[]{:S(2)}, u32[]{:S(2)}) collective-permute-start(bf16[4,128,128]{2,1,0:T(8,128)(2,1)S(1)} %pad_maximum_fusion), channel_id=1, source_target_pairs={{0,1},{1,0},{2,3},{3,2},{4,5},{5,4},{6,7},{7,6},{8,9},{9,8},{10,11... | collective-permute-start | bytes 393224 | tf_op jit(solution)/shard_map/ppermute | solution.py:310
  38.1 10.4 %collective-permute-start.19 = (bf16[576,128]{1,0:T(8,128)(2,1)S(1)}, bf16[576,128]{1,0:T(8,128)(2,1)S(1)}, u32[]{:S(2)}, u32[]{:S(2)}) collective-permute-start(bf16[576,128]{1,0:T(8,128)(2,1)S(1)} %add_convert_fusion), channel_id=1, source_target_pairs={{0,8},{1,9},{2,10},{3,11},{4,12},{5,13},{6,14},{7,15},{8,0},{9,1},... | collective-permute-start | bytes 442376 | tf_op jit(solution)/shard_map/ppermute | solution.py:310
  40.4 9.2 %collective-permute-start.22 = (bf16[2,576,128]{2,1,0:T(8,128)(2,1)S(1)}, bf16[2,576,128]{2,1,0:T(8,128)(2,1)S(1)}, u32[]{:S(2)}, u32[]{:S(2)}) collective-permute-start(bf16[2,576,128]{2,1,0:T(8,128)(2,1)S(1)} %join.1), channel_id=1, source_target_pairs={{0,2},{1,3},{2,0},{3,1},{4,6},{5,7},{6,4},{7,5},{8,10},{9,11},{10,... | collective-permute-start | bytes 884744 | tf_op jit(solution)/shard_map/ppermute | solution.py:310
  41.4 7.2 %collective-permute-start.21 = (bf16[2,576,128]{2,1,0:T(8,128)(2,1)S(1)}, bf16[2,576,128]{2,1,0:T(8,128)(2,1)S(1)}, u32[]{:S(2)}, u32[]{:S(2)}) collective-permute-start(bf16[2,576,128]{2,1,0:T(8,128)(2,1)S(1)} %get-tuple-element.92), channel_id=1, source_target_pairs={{0,1},{1,0},{2,3},{3,2},{4,5},{5,4},{6,7},{7,6},{8,9},{9,8},{10,11... | collective-permute-start | bytes 884744 | tf_op jit(solution)/shard_map/ppermute | solution.py:310

commit v19 on v18

--- a/solution.py
+++ b/solution.py
@@ -281,9 +281,16 @@
 
 
 def finish_kernel(lat_sum_ref, *refs):
-    pieces, lat_out_ref, q_out_ref = refs[:-2], refs[-2], refs[-1]
-    lat_out_ref[...] = lat_sum_ref[...].astype(BF16)
-    q_out_ref[...] = sum(piece[...].astype(F32) for piece in pieces).astype(BF16)
+    pieces, (lat_hbm, q_hbm, lat_ref, q_ref, sems) = refs[:-5], refs[-5:]
+    lat_ref[...] = lat_sum_ref[...].astype(BF16)
+    copies = [pltpu.make_async_copy(lat_ref, lat_hbm, sems.at[0])]
+    copies[0].start()
+    for h in range(q_ref.shape[0]):
+        q_ref[h] = sum(piece[h].astype(F32) for piece in pieces).astype(BF16)
+        copies.append(pltpu.make_async_copy(q_ref.at[h], q_hbm.at[h], sems.at[1 + h]))
+        copies[-1].start()
+    for copy in copies:
+        copy.wait()
 
 
 def spread_kernel(scale, idx_ref, *refs):
@@ -504,6 +511,9 @@
         "finish",
         [((width, tok), BF16), ((heads, width, tok), BF16)],
         [lat_sum, gq_own, gq_core, gq_last],
+        [((width, tok), BF16), ((heads, width, tok), BF16)],
+        copies=1 + heads,
+        out=pltpu.HBM,
     )
     return (jnp.transpose(grad_q, (2, 0, 1))[None], grad_lat.T[None], grad_w)
 

time: 50.7 us -> 50.6 us (level)
  no operation moved by 1% of the time
where the time goes in v19:
time: 50.6 us; the launch traced here: 50.4 us
  starting transfers between devices  24.8 us (49%)
  Pallas kernels  12 us (24%)
  waiting for transfers between devices  9.06 us (18%)
  local copies, waits for them, and re-layouts  2.6 us (5%)
  other arithmetic  1.1 us (2%)
  between operations  0.85 us (2%)
    ppermute x23, starting transfers between devices, swap(): return lax.ppermute(x, axis, [(i, i ^ mask) for i in range(size)])  24.8 us
    pallas_call x15, Pallas kernels, call(): pl.pallas_call(kernel, out_shape=[jax.ShapeDtypeStruct(s, d) for s, d in...  12 us
    ppermute x23, waiting for transfers between devices, swap(): return lax.ppermute(x, axis, [(i, i ^ mask) for i in range(size)])  9.06 us
    unnamed x8, local copies, waits for them, and re-layouts  2.58 us
    convert_element_type x6, other arithmetic, add(): return (a.astype(F32) + b.astype(F32)).astype(BF16)  1.09 us
  transfers between devices with their start and end apart: 23, of which 9 were waited for; matrix products, arithmetic and copies ran while one was open for 2% of the time, Pallas kernels for 17%

profile of v19, /device:TPU:0, one launch (start us, length us, event | category | flops | bytes accessed | tf_op | source)
XLA Modules:
  0.0 50.4 jit_solution(17536626629969171669)
XLA Ops:
  0.6 2.8 %pack.1 = (bf16[592,128]{1,0:T(8,128)(2,1)}, bf16[1424,128]{1,0:T(8,128)(2,1)}, f32[8,128]{1,0:T(8,128)}, bf16[4,128,128]{2,1,0:T(8,128)(2,1)}, bf16[4,128,128]{2,1,0:T(8,128)(2,1)}) custom-call(s32[1]{0:T(128)} %bitcast.idx_ref, s32[1,128]{1,0:T(1,128)} %pos_hbm.1, bf16[2,576,128]{2,1,0:T(8,128)(2,1)} %bitcast.15, bf16[128,2,128]{2,1,0:T(2,128)(2,1)} %bitcast.18, ...), custom_call_target="tpu_custom_call" | custom-call | bytes 1815044 | tf_op jit(solution)/shard_map/pack/pallas_call | solution.py:40
  3.5 0.5 %collective-permute-start = (bf16[1424,128]{1,0:T(8,128)(2,1)}, bf16[1424,128]{1,0:T(8,128)(2,1)S(1)}, u32[]{:S(2)}, u32[]{:S(2)}) collective-permute-start(bf16[1424,128]{1,0:T(8,128)(2,1)} %get-tuple-element.49.refs_1_), channel_id=1, source_target_pairs={{0,1},{1,0},{2,3},{3,2},{4,5},{5,4},{6,7},{7,6},{8,9},{9,8},{10,11... | collective-permute-start | bytes 1093640 | tf_op jit(solution)/shard_map/ppermute | solution.py:317
  4.0 0.1 collective-permute-start.4
  4.1 2.9 %collective-permute-start.1 = (bf16[1424,128]{1,0:T(8,128)(2,1)}, bf16[1424,128]{1,0:T(8,128)(2,1)S(1)}, u32[]{:S(2)}, u32[]{:S(2)}) collective-permute-start(bf16[1424,128]{1,0:T(8,128)(2,1)} %get-tuple-element.49.refs_1_), channel_id=1, source_target_pairs={{0,2},{1,3},{2,0},{3,1},{4,6},{5,7},{6,4},{7,5},{8,10},{9,11},{10,... | collective-permute-start | bytes 1093640 | tf_op jit(solution)/shard_map/ppermute | solution.py:317
  7.0 2.6 %collective-permute-start.3 = (bf16[592,128]{1,0:T(8,128)(2,1)}, bf16[592,128]{1,0:T(8,128)(2,1)S(1)}, u32[]{:S(2)}, u32[]{:S(2)}) collective-permute-start(bf16[592,128]{1,0:T(8,128)(2,1)} %get-tuple-element.51.refs_0_), channel_id=1, source_target_pairs={{0,8},{1,9},{2,10},{3,11},{4,12},{5,13},{6,14},{7,15},{8,0},{9,1},... | collective-permute-start | bytes 454664 | tf_op jit(solution)/shard_map/ppermute | solution.py:317
  9.6 0.0 collective-permute-done.refs_4_.refs_1_
  9.6 1.6 %collective-permute-start.2 = (bf16[592,128]{1,0:T(8,128)(2,1)}, bf16[592,128]{1,0:T(8,128)(2,1)S(1)}, u32[]{:S(2)}, u32[]{:S(2)}) collective-permute-start(bf16[592,128]{1,0:T(8,128)(2,1)} %get-tuple-element.51.refs_0_), channel_id=1, source_target_pairs={{0,4},{1,5},{2,6},{3,7},{4,0},{5,1},{6,2},{7,3},{8,12},{9,13},{10,... | collective-permute-start | bytes 454664 | tf_op jit(solution)/shard_map/ppermute | solution.py:317
  11.2 0.0 collective-permute-done.4
  11.2 0.9 %add_convert_fusion.2 = bf16[4,128,128]{2,1,0:T(8,128)(2,1)S(1)} fusion(bf16[4,128,128]{2,1,0:T(8,128)(2,1)S(1)} %collective-permute-done.4, bf16[4,128,128]{2,1,0:T(8,128)(2,1)} %get-tuple-element.52), kind=kLoop, calls=%fused_computation.2 | loop fusion | flops 262144 | bytes 393216 | tf_op jit(solution)/shard_map/convert_element_type | solution.py:365
  12.1 0.0 copy-start
  12.1 1.6 %collective-permute-start.5 = (bf16[4,128,128]{2,1,0:T(8,128)(2,1)S(1)}, bf16[4,128,128]{2,1,0:T(8,128)(2,1)S(1)}, u32[]{:S(2)}, u32[]{:S(2)}) collective-permute-start(bf16[4,128,128]{2,1,0:T(8,128)(2,1)S(1)} %add_convert_fusion.2), channel_id=1, source_target_pairs={{0,16},{16,0},{1,17},{17,1},{2,18},{18,2},{3,19},{19,3},{4,20},{20... | collective-permute-start | bytes 393224 | tf_op jit(solution)/shard_map/ppermute | solution.py:317
  13.7 1.0 %copy-done.1 = bf16[1424,128]{1,0:T(8,128)(2,1)S(1)} copy-done((bf16[1424,128]{1,0:T(8,128)(2,1)S(1)}, bf16[1424,128]{1,0:T(8,128)(2,1)}, u32[]{:S(2)}) %copy-start.1) | copy-done | bytes 364568
  14.7 0.9 %copy-done.2 = bf16[592,128]{1,0:T(8,128)(2,1)S(1)} copy-done((bf16[592,128]{1,0:T(8,128)(2,1)S(1)}, bf16[592,128]{1,0:T(8,128)(2,1)}, u32[]{:S(2)}) %copy-start.2) | copy-done | bytes 151576
  15.6 0.7 %copy-done.3 = f32[8,128]{1,0:T(8,128)S(1)} copy-done((f32[8,128]{1,0:T(8,128)S(1)}, f32[8,128]{1,0:T(8,128)}, u32[]{:S(2)}) %copy-start.3) | copy-done | bytes 4120
  16.3 0.8 %collective-permute-done.3.refs_2_.refs_9_ = bf16[592,128]{1,0:T(8,128)(2,1)S(1)} collective-permute-done((bf16[592,128]{1,0:T(8,128)(2,1)}, bf16[592,128]{1,0:T(8,128)(2,1)S(1)}, u32[]{:S(2)}, u32[]{:S(2)}) %collective-permute-start.3) | collective-permute-done | bytes 151584 | tf_op jit(solution)/shard_map/ppermute | solution.py:317
  17.1 0.1 collective-permute-done.5
  17.2 0.0 collective-permute-done.1.refs_5_.refs_2_
  17.2 0.1 collective-permute-done.2.refs_1_.refs_8_
  17.3 0.0 collective-permute-start.6
  17.4 0.5 %collective-permute-start.11 = (bf16[2,128,128]{2,1,0:T(8,128)(2,1)S(1)}, bf16[2,128,128]{2,1,0:T(8,128)(2,1)S(1)}, u32[]{:S(2)}, u32[]{:S(2)}) collective-permute-start(bf16[2,128,128]{2,1,0:T(8,128)(2,1)S(1)} %slice.17), channel_id=1, source_target_pairs={{0,2},{1,3},{2,0},{3,1},{4,6},{5,7},{6,4},{7,5},{8,10},{9,11},{10,... | collective-permute-start | bytes 196616 | tf_op jit(solution)/shard_map/ppermute | solution.py:317
  17.9 1.5 %collective-permute-start.7 = (bf16[592,128]{1,0:T(8,128)(2,1)S(1)}, bf16[592,128]{1,0:T(8,128)(2,1)S(1)}, u32[]{:S(2)}, u32[]{:S(2)}) collective-permute-start(bf16[592,128]{1,0:T(8,128)(2,1)S(1)} %collective-permute-done.3.refs_2_.refs_9_), channel_id=1, source_target_pairs={{0,4},{1,5},{2,6},{3,7},{4,0},{5,1},{6,2},{7,3},{8,12},{9,13},{10,... | collective-permute-start | bytes 454664 | tf_op jit(solution)/shard_map/ppermute | solution.py:317
  19.4 0.0 collective-permute-done.6.refs_6_.refs_3_
  19.4 1.2 %near_scores.1 = (f32[384,1024]{1,0:T(8,128)S(1)}, bf16[384,640]{1,0:T(8,128)(2,1)S(1)}, f32[16,128]{1,0:T(8,128)S(1)}, bf16[640,1024]{1,0:T(8,128)(2,1)S(1)}) custom-call(bf16[592,128]{1,0:T(8,128)(2,1)S(1)} %get-tuple-element.61.refs_0_.refs_7_, bf16[592,128]{1,0:T(8,128)(2,1)S(1)} %collective-permute-done.2.refs_1_.refs_8_, ...), custom_call_target="tpu_custom_call" | custom-call | tf_op jit(solution)/shard_map/near_scores/pallas_call | solution.py:40
  20.6 1.1 %near_context.1 = (bf16[512,1024]{1,0:T(8,128)(2,1)S(1)}, f32[384,1024]{1,0:T(8,128)S(1)}) custom-call(bf16[1424,128]{1,0:T(8,128)(2,1)S(1)} %get-tuple-element.58.refs_3_.refs_0_, bf16[1424,128]{1,0:T(8,128)(2,1)S(1)} %collective-permute-done.refs_4_.refs_1_, bf16[1424,128]{1,0:T(8,128)(2,1)S(1)} %collective-permute-done.1.refs_5_.refs_2_, ...), custom_call_target="tpu_custom_call" | custom-call | tf_op jit(solution)/shard_map/near_context/pallas_call | solution.py:40
  21.7 0.2 collective-permute-done.11
  22.0 1.5 %collective-permute-start.12 = (bf16[2,128,128]{2,1,0:T(8,128)(2,1)S(1)}, bf16[2,128,128]{2,1,0:T(8,128)(2,1)S(1)}, u32[]{:S(2)}, u32[]{:S(2)}) collective-permute-start(bf16[2,128,128]{2,1,0:T(8,128)(2,1)S(1)} %add_convert_fusion.5), channel_id=1, source_target_pairs={{0,4},{1,5},{2,6},{3,7},{4,0},{5,1},{6,2},{7,3},{8,12},{9,13},{10,... | collective-permute-start | bytes 196616 | tf_op jit(solution)/shard_map/ppermute | solution.py:317
  23.4 0.5 collective-permute-done.7.refs_0_.refs_10_
  23.9 0.5 last_scores.1
  24.4 0.7 %collective-permute-start.10 = (f32[16,128]{1,0:T(8,128)S(1)}, f32[16,128]{1,0:T(8,128)S(1)}, u32[]{:S(2)}, u32[]{:S(2)}) collective-permute-start(f32[16,128]{1,0:T(8,128)S(1)} %get-tuple-element.71.refs_0_), channel_id=1, source_target_pairs={{0,3},{1,2},{2,1},{3,0},{4,7},{5,6},{6,5},{7,4},{8,11},{9,10},{10,... | collective-permute-start | bytes 24584 | tf_op jit(solution)/shard_map/ppermute | solution.py:317
  25.1 1.1 %collective-permute-start.8 = (f32[16,128]{1,0:T(8,128)S(1)}, f32[16,128]{1,0:T(8,128)S(1)}, u32[]{:S(2)}, u32[]{:S(2)}) collective-permute-start(f32[16,128]{1,0:T(8,128)S(1)} %get-tuple-element.71.refs_0_), channel_id=1, source_target_pairs={{0,1},{1,0},{2,3},{3,2},{4,5},{5,4},{6,7},{7,6},{8,9},{9,8},{10,11... | collective-permute-start | bytes 24584 | tf_op jit(solution)/shard_map/ppermute | solution.py:317
  26.2 0.5 collective-permute-start.9
  26.7 0.0 collective-permute-done.12
  26.7 2.6 %collective-permute-start.13 = (bf16[2,128,128]{2,1,0:T(8,128)(2,1)S(1)}, bf16[2,128,128]{2,1,0:T(8,128)(2,1)S(1)}, u32[]{:S(2)}, u32[]{:S(2)}) collective-permute-start(bf16[2,128,128]{2,1,0:T(8,128)(2,1)S(1)} %add_convert_fusion.4), channel_id=1, source_target_pairs={{0,8},{1,9},{2,10},{3,11},{4,12},{5,13},{6,14},{7,15},{8,0},{9,1},... | collective-permute-start | bytes 196616 | tf_op jit(solution)/shard_map/ppermute | solution.py:317
  29.3 0.3 last_context.1.refs_5_
  29.6 0.0 collective-permute-done.10.refs_3_
  29.6 0.0 collective-permute-done.8.refs_1_
  29.6 0.2 collective-permute-done.9.refs_2_
  29.9 0.8 %last_gradients.1 = (bf16[576,128]{1,0:T(8,128)(2,1)S(1)}, bf16[128,1024]{1,0:T(8,128)(2,1)S(1)}) custom-call(f32[16,128]{1,0:T(8,128)S(1)} %get-tuple-element.71.refs_0_, f32[16,128]{1,0:T(8,128)S(1)} %collective-permute-done.8.refs_1_, f32[16,128]{1,0:T(8,128)S(1)} %collective-permute-done.9.refs_2_, f32[16,128]{1,0:T(8,128)S(1)} %collective-permute-done.10.refs_3_, ...), custom_call_target="tpu_custom_call" | custom-call | flops 285212672 | bytes 3850240 | tf_op jit(solution)/shard_map/last_gradients/pallas_call | solution.py:40
  30.7 1.9 %collective-permute-start.18 = (bf16[576,128]{1,0:T(8,128)(2,1)S(1)}, bf16[576,128]{1,0:T(8,128)(2,1)S(1)}, u32[]{:S(2)}, u32[]{:S(2)}) collective-permute-start(bf16[576,128]{1,0:T(8,128)(2,1)S(1)} %get-tuple-element.86), channel_id=1, source_target_pairs={{0,4},{1,5},{2,6},{3,7},{4,0},{5,1},{6,2},{7,3},{8,12},{9,13},{10,... | collective-permute-start | bytes 442376 | tf_op jit(solution)/shard_map/ppermute | solution.py:317
  32.6 0.8 %next_gradients.1 = bf16[576,128]{1,0:T(8,128)(2,1)S(1)} custom-call(f32[16,128]{1,0:T(8,128)S(1)} %get-tuple-element.71.refs_0_, f32[16,128]{1,0:T(8,128)S(1)} %collective-permute-done.8.refs_1_, f32[16,128]{1,0:T(8,128)S(1)} %collective-permute-done.9.refs_2_, f32[16,128]{1,0:T(8,128)S(1)} %collective-permute-done.10.refs_3_, ...), custom_call_target="tpu_custom_call" | custom-call | flops 285212672 | bytes 5685248 | tf_op jit(solution)/shard_map/next_gradients/pallas_call | solution.py:40
  33.4 0.2 collective-permute-start.20
  33.6 0.0 collective-permute-done.13
  33.6 1.3 %collective-permute-start.16 = (bf16[2,128,128]{2,1,0:T(8,128)(2,1)S(1)}, bf16[2,128,128]{2,1,0:T(8,128)(2,1)S(1)}, u32[]{:S(2)}, u32[]{:S(2)}) collective-permute-start(bf16[2,128,128]{2,1,0:T(8,128)(2,1)S(1)} %add_convert_fusion.3.refs_0_), channel_id=1, source_target_pairs={{0,2},{1,3},{2,0},{3,1},{4,6},{5,7},{6,4},{7,5},{8,10},{9,11},{10,... | collective-permute-start | bytes 196616 | tf_op jit(solution)/shard_map/ppermute | solution.py:317
  34.9 1.1 %query_gradients.1 = (bf16[2,576,128]{2,1,0:T(8,128)(2,1)S(1)}, bf16[2,576,128]{2,1,0:T(8,128)(2,1)S(1)}, bf16[2,576,128]{2,1,0:T(8,128)(2,1)S(1)}, bf16[576,128...) custom-call(f32[16,128]{1,0:T(8,128)S(1)} %get-tuple-element.71.refs, ...), custom_call_target="tpu_custom_call" | custom-call | tf_op jit(solution)/shard_map/query_gradients/pallas_call | solution.py:40
  36.1 0.1 collective-permute-start.14
  36.1 0.5 collective-permute-start.15
  36.6 0.7 %middle_gradients.1 = bf16[576,128]{1,0:T(8,128)(2,1)S(1)} custom-call(bf16[512,1024]{1,0:T(8,128)(2,1)S(1)} %get-tuple-element.65.g_ref.refs_6_, bf16[640,1024]{1,0:T(8,128)(2,1)S(1)} %get-tuple-element.66.refs_1_.refs_7_.q_all_ref, bf16[384,1024]{1,0:T(8,128)(2,1)S(1)} %get-tuple-element.80.gs_ref, bf16[384,1024]{1,0:T(8,128)(2,1)S(1)} %get-tuple-element.84.p_ref), custom_call_target="tpu_custom_call" | custom-call | flops 855638016 | bytes 12238848 | tf_op jit(solution)/shard_map/middle_gradients/pallas_call | solution.py:40
  37.4 0.6 %collective-permute-done.16.refs_2_ = bf16[2,128,128]{2,1,0:T(8,128)(2,1)S(1)} collective-permute-done((bf16[2,128,128]{2,1,0:T(8,128)(2,1)S(1)}, bf16[2,128,128]{2,1,0:T(8,128)(2,1)S(1)}, u32[]{:S(2)}, u32[]{:S(2)}) %collective-permute-start.16) | collective-permute-done | bytes 65568 | tf_op jit(solution)/shard_map/ppermute | solution.py:317
  38.0 0.1 collective-permute-start.17
  38.1 0.0 collective-permute-done.18
  38.1 2.2 %collective-permute-start.19 = (bf16[576,128]{1,0:T(8,128)(2,1)S(1)}, bf16[576,128]{1,0:T(8,128)(2,1)S(1)}, u32[]{:S(2)}, u32[]{:S(2)}) collective-permute-start(bf16[576,128]{1,0:T(8,128)(2,1)S(1)} %add_convert_fusion), channel_id=1, source_target_pairs={{0,8},{1,9},{2,10},{3,11},{4,12},{5,13},{6,14},{7,15},{8,0},{9,1},... | collective-permute-start | bytes 442376 | tf_op jit(solution)/shard_map/ppermute | solution.py:317
  40.3 0.0 collective-permute-done.14.refs_0_
  40.3 0.0 collective-permute-done.15.refs_1_
  40.3 0.1 join.1
  40.4 1.0 %collective-permute-start.22 = (bf16[2,576,128]{2,1,0:T(8,128)(2,1)S(1)}, bf16[2,576,128]{2,1,0:T(8,128)(2,1)S(1)}, u32[]{:S(2)}, u32[]{:S(2)}) collective-permute-start(bf16[2,576,128]{2,1,0:T(8,128)(2,1)S(1)} %join.1), channel_id=1, source_target_pairs={{0,2},{1,3},{2,0},{3,1},{4,6},{5,7},{6,4},{7,5},{8,10},{9,11},{10,... | collective-permute-start | bytes 884744 | tf_op jit(solution)/shard_map/ppermute | solution.py:317
  41.4 0.7 %near_gradients.1.refs_0_ = bf16[576,128]{1,0:T(8,128)(2,1)S(1)} custom-call(bf16[512,1024]{1,0:T(8,128)(2,1)S(1)} %get-tuple-element.65.g_ref.refs_6_, bf16[640,1024]{1,0:T(8,128)(2,1)S(1)} %get-tuple-element.66.refs_1_.refs_7_.q_all_ref, bf16[384,1024]{1,0:T(8,128)(2,1)S(1)} %get-tuple-element.80.gs_ref, bf16[384,1024]{1,0:T(8,128)(2,1)S(1)} %get-tuple-element.84.p_ref), custom_call_target="tpu_custom_call" | custom-call | flops 285212672 | bytes 4079616 | tf_op jit(solution)/shard_map/near_gradients/pallas_call | solution.py:40
  42.1 0.0 collective-permute-done.17
  42.1 0.8 %spread.1 = f32[2,512,128]{2,1,0:T(8,128)} custom-call(s32[1]{0:T(128)} %bitcast.idx_ref, bf16[2,128,128]{2,1,0:T(8,128)(2,1)S(1)} %add_convert_fusion.3.refs_0_, bf16[2,128,128]{2,1,0:T(8,128)(2,1)S(1)} %get-tuple-element.96.refs_1_, bf16[2,128,128]{2,1,0:T(8,128)(2,1)S(1)} %collective-permute-done.16.refs_2_, ...), custom_call_target="tpu_custom_call" | custom-call | bytes 786436 | tf_op jit(solution)/shard_map/spread/pallas_call | solution.py:40
  43.0 0.0 collective-permute-done.20.refs_2_
  43.0 5.5 %collective-permute-done.19.refs_1_ = bf16[576,128]{1,0:T(8,128)(2,1)S(1)} collective-permute-done((bf16[576,128]{1,0:T(8,128)(2,1)S(1)}, bf16[576,128]{1,0:T(8,128)(2,1)S(1)}, u32[]{:S(2)}, u32[]{:S(2)}) %collective-permute-start.19) | collective-permute-done | bytes 147488 | tf_op jit(solution)/shard_map/ppermute | solution.py:317
  48.5 0.1 latent_sum.1.lat_sum_ref
  48.6 0.0 collective-permute-done.21.refs_1_
  48.6 1.0 %collective-permute-done.22.refs_2_ = bf16[2,576,128]{2,1,0:T(8,128)(2,1)S(1)} collective-permute-done((bf16[2,576,128]{2,1,0:T(8,128)(2,1)S(1)}, bf16[2,576,128]{2,1,0:T(8,128)(2,1)S(1)}, u32[]{:S(2)}, u32[]{:S(2)}) %collective-permute-start.22) | collective-permute-done | bytes 294944 | tf_op jit(solution)/shard_map/ppermute | solution.py:317
  49.6 0.8 %finish.1 = (bf16[576,128]{1,0:T(8,128)(2,1)}, bf16[2,576,128]{2,1,0:T(8,128)(2,1)}) custom-call(f32[576,128]{1,0:T(8,128)S(1)} %latent_sum.1.lat_sum_ref, bf16[2,576,128]{2,1,0:T(8,128)(2,1)S(1)} %get-tuple-element.88.refs_0_, bf16[2,576,128]{2,1,0:T(8,128)(2,1)S(1)} %collective-permute-done.21.refs_1_, bf16[2,576,128]{2,1,0:T(8,128)(2,1)S(1)} %collective-permute-done.22.refs_2_), custom_call_target="tpu_custom_call" | custom-call | bytes 1622016 | tf_op jit(solution)/shard_map/finish/pallas_call | solution.py:40
  (14 shorter events, 0.2 us)
Async XLA Ops:
  3.5 6.1 %collective-permute-start = (bf16[1424,128]{1,0:T(8,128)(2,1)}, bf16[1424,128]{1,0:T(8,128)(2,1)S(1)}, u32[]{:S(2)}, u32[]{:S(2)}) collective-permute-start(bf16[1424,128]{1,0:T(8,128)(2,1)} %get-tuple-element.49.refs_1_), channel_id=1, source_target_pairs={{0,1},{1,0},{2,3},{3,2},{4,5},{5,4},{6,7},{7,6},{8,9},{9,8},{10,11... | collective-permute-start | bytes 1093640 | tf_op jit(solution)/shard_map/ppermute | solution.py:317
  4.0 7.2 %collective-permute-start.4 = (bf16[4,128,128]{2,1,0:T(8,128)(2,1)}, bf16[4,128,128]{2,1,0:T(8,128)(2,1)S(1)}, u32[]{:S(2)}, u32[]{:S(2)}) collective-permute-start(bf16[4,128,128]{2,1,0:T(8,128)(2,1)} %get-tuple-element.53), channel_id=1, source_target_pairs={{0,1},{1,0},{2,3},{3,2},{4,5},{5,4},{6,7},{7,6},{8,9},{9,8},{10,11... | collective-permute-start | bytes 393224 | tf_op jit(solution)/shard_map/ppermute | solution.py:317
  4.1 13.1 %collective-permute-start.1 = (bf16[1424,128]{1,0:T(8,128)(2,1)}, bf16[1424,128]{1,0:T(8,128)(2,1)S(1)}, u32[]{:S(2)}, u32[]{:S(2)}) collective-permute-start(bf16[1424,128]{1,0:T(8,128)(2,1)} %get-tuple-element.49.refs_1_), channel_id=1, source_target_pairs={{0,2},{1,3},{2,0},{3,1},{4,6},{5,7},{6,4},{7,5},{8,10},{9,11},{10,... | collective-permute-start | bytes 1093640 | tf_op jit(solution)/shard_map/ppermute | solution.py:317
  7.0 10.1 %collective-permute-start.3 = (bf16[592,128]{1,0:T(8,128)(2,1)}, bf16[592,128]{1,0:T(8,128)(2,1)S(1)}, u32[]{:S(2)}, u32[]{:S(2)}) collective-permute-start(bf16[592,128]{1,0:T(8,128)(2,1)} %get-tuple-element.51.refs_0_), channel_id=1, source_target_pairs={{0,8},{1,9},{2,10},{3,11},{4,12},{5,13},{6,14},{7,15},{8,0},{9,1},... | collective-permute-start | bytes 454664 | tf_op jit(solution)/shard_map/ppermute | solution.py:317
  9.6 7.7 %collective-permute-start.2 = (bf16[592,128]{1,0:T(8,128)(2,1)}, bf16[592,128]{1,0:T(8,128)(2,1)S(1)}, u32[]{:S(2)}, u32[]{:S(2)}) collective-permute-start(bf16[592,128]{1,0:T(8,128)(2,1)} %get-tuple-element.51.refs_0_), channel_id=1, source_target_pairs={{0,4},{1,5},{2,6},{3,7},{4,0},{5,1},{6,2},{7,3},{8,12},{9,13},{10,... | collective-permute-start | bytes 454664 | tf_op jit(solution)/shard_map/ppermute | solution.py:317
  12.1 8.5 %copy-start = (bf16[2,512,128]{2,1,0:T(8,128)(2,1)S(1)}, bf16[2,512,128]{2,1,0:T(8,128)(2,1)}, u32[]{:S(2)}) copy-start(bf16[2,512,128]{2,1,0:T(8,128)(2,1)} %refs_4_.1) | copy-start | bytes 786436
  12.1 5.0 %collective-permute-start.5 = (bf16[4,128,128]{2,1,0:T(8,128)(2,1)S(1)}, bf16[4,128,128]{2,1,0:T(8,128)(2,1)S(1)}, u32[]{:S(2)}, u32[]{:S(2)}) collective-permute-start(bf16[4,128,128]{2,1,0:T(8,128)(2,1)S(1)} %add_convert_fusion.2), channel_id=1, source_target_pairs={{0,16},{16,0},{1,17},{17,1},{2,18},{18,2},{3,19},{19,3},{4,20},{20... | collective-permute-start | bytes 393224 | tf_op jit(solution)/shard_map/ppermute | solution.py:317
  13.7 1.0 %copy-start.1 = (bf16[1424,128]{1,0:T(8,128)(2,1)S(1)}, bf16[1424,128]{1,0:T(8,128)(2,1)}, u32[]{:S(2)}) copy-start(bf16[1424,128]{1,0:T(8,128)(2,1)} %get-tuple-element.49.refs_1_) | copy-start | bytes 1093636
  14.7 0.9 %copy-start.2 = (bf16[592,128]{1,0:T(8,128)(2,1)S(1)}, bf16[592,128]{1,0:T(8,128)(2,1)}, u32[]{:S(2)}) copy-start(bf16[592,128]{1,0:T(8,128)(2,1)} %get-tuple-element.51.refs_0_) | copy-start | bytes 454660
  15.6 0.7 %copy-start.3 = (f32[8,128]{1,0:T(8,128)S(1)}, f32[8,128]{1,0:T(8,128)}, u32[]{:S(2)}) copy-start(f32[8,128]{1,0:T(8,128)} %get-tuple-element.54.refs_2_) | copy-start | bytes 12292
  17.3 2.1 %collective-permute-start.6 = (bf16[1424,128]{1,0:T(8,128)(2,1)S(1)}, bf16[1424,128]{1,0:T(8,128)(2,1)S(1)}, u32[]{:S(2)}, u32[]{:S(2)}) collective-permute-start(bf16[1424,128]{1,0:T(8,128)(2,1)S(1)} %collective-permute-done.1.refs_5_.refs_2_), channel_id=1, source_target_pairs={{0,1},{1,0},{2,3},{3,2},{4,5},{5,4},{6,7},{7,6},{8,9},{9,8},{10,11... | collective-permute-start | bytes 1093640 | tf_op jit(solution)/shard_map/ppermute | solution.py:317
  17.4 4.6 %collective-permute-start.11 = (bf16[2,128,128]{2,1,0:T(8,128)(2,1)S(1)}, bf16[2,128,128]{2,1,0:T(8,128)(2,1)S(1)}, u32[]{:S(2)}, u32[]{:S(2)}) collective-permute-start(bf16[2,128,128]{2,1,0:T(8,128)(2,1)S(1)} %slice.17), channel_id=1, source_target_pairs={{0,2},{1,3},{2,0},{3,1},{4,6},{5,7},{6,4},{7,5},{8,10},{9,11},{10,... | collective-permute-start | bytes 196616 | tf_op jit(solution)/shard_map/ppermute | solution.py:317
  17.9 6.1 %collective-permute-start.7 = (bf16[592,128]{1,0:T(8,128)(2,1)S(1)}, bf16[592,128]{1,0:T(8,128)(2,1)S(1)}, u32[]{:S(2)}, u32[]{:S(2)}) collective-permute-start(bf16[592,128]{1,0:T(8,128)(2,1)S(1)} %collective-permute-done.3.refs_2_.refs_9_), channel_id=1, source_target_pairs={{0,4},{1,5},{2,6},{3,7},{4,0},{5,1},{6,2},{7,3},{8,12},{9,13},{10,... | collective-permute-start | bytes 454664 | tf_op jit(solution)/shard_map/ppermute | solution.py:317
  22.0 4.7 %collective-permute-start.12 = (bf16[2,128,128]{2,1,0:T(8,128)(2,1)S(1)}, bf16[2,128,128]{2,1,0:T(8,128)(2,1)S(1)}, u32[]{:S(2)}, u32[]{:S(2)}) collective-permute-start(bf16[2,128,128]{2,1,0:T(8,128)(2,1)S(1)} %add_convert_fusion.5), channel_id=1, source_target_pairs={{0,4},{1,5},{2,6},{3,7},{4,0},{5,1},{6,2},{7,3},{8,12},{9,13},{10,... | collective-permute-start | bytes 196616 | tf_op jit(solution)/shard_map/ppermute | solution.py:317
  24.4 5.2 %collective-permute-start.10 = (f32[16,128]{1,0:T(8,128)S(1)}, f32[16,128]{1,0:T(8,128)S(1)}, u32[]{:S(2)}, u32[]{:S(2)}) collective-permute-start(f32[16,128]{1,0:T(8,128)S(1)} %get-tuple-element.71.refs_0_), channel_id=1, source_target_pairs={{0,3},{1,2},{2,1},{3,0},{4,7},{5,6},{6,5},{7,4},{8,11},{9,10},{10,... | collective-permute-start | bytes 24584 | tf_op jit(solution)/shard_map/ppermute | solution.py:317
  25.1 4.5 %collective-permute-start.8 = (f32[16,128]{1,0:T(8,128)S(1)}, f32[16,128]{1,0:T(8,128)S(1)}, u32[]{:S(2)}, u32[]{:S(2)}) collective-permute-start(f32[16,128]{1,0:T(8,128)S(1)} %get-tuple-element.71.refs_0_), channel_id=1, source_target_pairs={{0,1},{1,0},{2,3},{3,2},{4,5},{5,4},{6,7},{7,6},{8,9},{9,8},{10,11... | collective-permute-start | bytes 24584 | tf_op jit(solution)/shard_map/ppermute | solution.py:317
  26.2 3.7 %collective-permute-start.9 = (f32[16,128]{1,0:T(8,128)S(1)}, f32[16,128]{1,0:T(8,128)S(1)}, u32[]{:S(2)}, u32[]{:S(2)}) collective-permute-start(f32[16,128]{1,0:T(8,128)S(1)} %get-tuple-element.71.refs_0_), channel_id=1, source_target_pairs={{0,2},{1,3},{2,0},{3,1},{4,6},{5,7},{6,4},{7,5},{8,10},{9,11},{10,... | collective-permute-start | bytes 24584 | tf_op jit(solution)/shard_map/ppermute | solution.py:317
  26.7 6.9 %collective-permute-start.13 = (bf16[2,128,128]{2,1,0:T(8,128)(2,1)S(1)}, bf16[2,128,128]{2,1,0:T(8,128)(2,1)S(1)}, u32[]{:S(2)}, u32[]{:S(2)}) collective-permute-start(bf16[2,128,128]{2,1,0:T(8,128)(2,1)S(1)} %add_convert_fusion.4), channel_id=1, source_target_pairs={{0,8},{1,9},{2,10},{3,11},{4,12},{5,13},{6,14},{7,15},{8,0},{9,1},... | collective-permute-start | bytes 196616 | tf_op jit(solution)/shard_map/ppermute | solution.py:317
  30.7 7.4 %collective-permute-start.18 = (bf16[576,128]{1,0:T(8,128)(2,1)S(1)}, bf16[576,128]{1,0:T(8,128)(2,1)S(1)}, u32[]{:S(2)}, u32[]{:S(2)}) collective-permute-start(bf16[576,128]{1,0:T(8,128)(2,1)S(1)} %get-tuple-element.86), channel_id=1, source_target_pairs={{0,4},{1,5},{2,6},{3,7},{4,0},{5,1},{6,2},{7,3},{8,12},{9,13},{10,... | collective-permute-start | bytes 442376 | tf_op jit(solution)/shard_map/ppermute | solution.py:317
  33.4 9.6 %collective-permute-start.20 = (bf16[576,128]{1,0:T(8,128)(2,1)S(1)}, bf16[576,128]{1,0:T(8,128)(2,1)S(1)}, u32[]{:S(2)}, u32[]{:S(2)}) collective-permute-start(bf16[576,128]{1,0:T(8,128)(2,1)S(1)} %next_gradients.1), channel_id=1, source_target_pairs={{0,4},{1,5},{2,6},{3,7},{4,0},{5,1},{6,2},{7,3},{8,12},{9,13},{10,... | collective-permute-start | bytes 442376 | tf_op jit(solution)/shard_map/ppermute | solution.py:317
  33.6 4.3 %collective-permute-start.16 = (bf16[2,128,128]{2,1,0:T(8,128)(2,1)S(1)}, bf16[2,128,128]{2,1,0:T(8,128)(2,1)S(1)}, u32[]{:S(2)}, u32[]{:S(2)}) collective-permute-start(bf16[2,128,128]{2,1,0:T(8,128)(2,1)S(1)} %add_convert_fusion.3.refs_0_), channel_id=1, source_target_pairs={{0,2},{1,3},{2,0},{3,1},{4,6},{5,7},{6,4},{7,5},{8,10},{9,11},{10,... | collective-permute-start | bytes 196616 | tf_op jit(solution)/shard_map/ppermute | solution.py:317
  36.1 4.3 %collective-permute-start.14 = (bf16[576,128]{1,0:T(8,128)(2,1)S(1)}, bf16[576,128]{1,0:T(8,128)(2,1)S(1)}, u32[]{:S(2)}, u32[]{:S(2)}) collective-permute-start(bf16[576,128]{1,0:T(8,128)(2,1)S(1)} %get-tuple-element.82), channel_id=1, source_target_pairs={{0,1},{1,0},{2,3},{3,2},{4,5},{5,4},{6,7},{7,6},{8,9},{9,8},{10,11... | collective-permute-start | bytes 442376 | tf_op jit(solution)/shard_map/ppermute | solution.py:317
  36.1 4.2 %collective-permute-start.15 = (bf16[576,128]{1,0:T(8,128)(2,1)S(1)}, bf16[576,128]{1,0:T(8,128)(2,1)S(1)}, u32[]{:S(2)}, u32[]{:S(2)}) collective-permute-start(bf16[576,128]{1,0:T(8,128)(2,1)S(1)} %get-tuple-element.83), channel_id=1, source_target_pairs={{0,1},{1,0},{2,3},{3,2},{4,5},{5,4},{6,7},{7,6},{8,9},{9,8},{10,11... | collective-permute-start | bytes 442376 | tf_op jit(solution)/shard_map/ppermute | solution.py:317
  38.0 4.1 %collective-permute-start.17 = (bf16[4,128,128]{2,1,0:T(8,128)(2,1)S(1)}, bf16[4,128,128]{2,1,0:T(8,128)(2,1)S(1)}, u32[]{:S(2)}, u32[]{:S(2)}) collective-permute-start(bf16[4,128,128]{2,1,0:T(8,128)(2,1)S(1)} %pad_maximum_fusion), channel_id=1, source_target_pairs={{0,1},{1,0},{2,3},{3,2},{4,5},{5,4},{6,7},{7,6},{8,9},{9,8},{10,11... | collective-permute-start | bytes 393224 | tf_op jit(solution)/shard_map/ppermute | solution.py:317
  38.1 10.4 %collective-permute-start.19 = (bf16[576,128]{1,0:T(8,128)(2,1)S(1)}, bf16[576,128]{1,0:T(8,128)(2,1)S(1)}, u32[]{:S(2)}, u32[]{:S(2)}) collective-permute-start(bf16[576,128]{1,0:T(8,128)(2,1)S(1)} %add_convert_fusion), channel_id=1, source_target_pairs={{0,8},{1,9},{2,10},{3,11},{4,12},{5,13},{6,14},{7,15},{8,0},{9,1},... | collective-permute-start | bytes 442376 | tf_op jit(solution)/shard_map/ppermute | solution.py:317
  40.4 9.2 %collective-permute-start.22 = (bf16[2,576,128]{2,1,0:T(8,128)(2,1)S(1)}, bf16[2,576,128]{2,1,0:T(8,128)(2,1)S(1)}, u32[]{:S(2)}, u32[]{:S(2)}) collective-permute-start(bf16[2,576,128]{2,1,0:T(8,128)(2,1)S(1)} %join.1), channel_id=1, source_target_pairs={{0,2},{1,3},{2,0},{3,1},{4,6},{5,7},{6,4},{7,5},{8,10},{9,11},{10,... | collective-permute-start | bytes 884744 | tf_op jit(solution)/shard_map/ppermute | solution.py:317
  41.4 7.2 %collective-permute-start.21 = (bf16[2,576,128]{2,1,0:T(8,128)(2,1)S(1)}, bf16[2,576,128]{2,1,0:T(8,128)(2,1)S(1)}, u32[]{:S(2)}, u32[]{:S(2)}) collective-permute-start(bf16[2,576,128]{2,1,0:T(8,128)(2,1)S(1)} %get-tuple-element.92), channel_id=1, source_target_pairs={{0,1},{1,0},{2,3},{3,2},{4,5},{5,4},{6,7},{7,6},{8,9},{9,8},{10,11... | collective-permute-start | bytes 884744 | tf_op jit(solution)/shard_map/ppermute | solution.py:317
